TPU v7x, 32 devices: a whole 2x2x4 slice. The times are simulated.
32 devices in a mesh: groups: 2 (over y), adapter: 4 (over z), mp: 4 (over x, core).
Axes of the slice: x: 2, y: 2, z: 4, core: 2. Of those that a mesh axis runs over, the one named last changes fastest.
Arguments:
- tokens: bfloat16 [3072, 8192], P(('groups', 'adapter'), 'mp'), parts along dimension 0, may hold values from -6 to 6
- base_key_weight: bfloat16 [8192, 512], P('mp'), may hold values from -0.0625 to 0.0625
- stacked_down_weight: bfloat16 [8192, 1024], P('mp', 'adapter'), may hold values from -0.0625 to 0.0625
- stacked_up_weight: bfloat16 [1024, 512], P('adapter', 'mp'), may hold values from -1.5 to 1.5
- request_adapter_owner: int32 [3072, 1], P(('groups', 'adapter')), parts along dimension 0, may hold values from 0 to 3; in each aligned block of 384 rows (0 to 383, 384 to 767, ...) at most 144 rows name the same one
- request_adapter_slot: int32 [3072], P(('groups', 'adapter')), parts along dimension 0, may hold values from 0 to 15
Outputs:
- keys_out: bfloat16 [3072, 512], P(('groups', 'adapter'), 'mp'), parts along dimension 0
There are 2 independent parts, one for each index of `groups`. A program takes and returns all parts, laid end to end along the dimension named above; an argument that names none is the same for every part. Nothing has to cross between parts.
Inputs may be any that keep to these rules, and one draw needn't show every extreme that they name: `request_adapter_owner`: in each aligned block of 384 rows (the rows of one device) at most 144 rows name the same owner, a bound that some block reaches.
All inputs are finite; a program needn't handle non-finite values.
Results may differ from a plain program's by a relative error of at most 0.0054.
Values may be sent and summed in bfloat16 or wider, within the bound.
No kernel may reach another device: no remote copies, remote signals or barrier semaphores. Data moves between devices by JAX's collectives and lax.ppermute only.
A program may use at most 64 MiB of HBM per device.

v0:
```python
import jax
import jax.numpy as jnp
from jax import lax
from jax.sharding import PartitionSpec as P

ADAPTER_RANK = 16


ADAPTER_SCALE = 2.0


def local(
    tokens,
    base_key_weight,
    stacked_down_weight,
    stacked_up_weight,
    request_adapter_owner,
    request_adapter_slot,
):
    rows_here = tokens.shape[0]
    feature_share = tokens.shape[1]
    owner_count = lax.axis_size("adapter")
    capacity = max(2, 3 * rows_here // (2 * owner_count))
    local_adapters = stacked_down_weight.shape[1] // ADAPTER_RANK
    key_output_share = stacked_up_weight.shape[1]
    owners = request_adapter_owner.reshape(-1)
    onehot = (owners[:, None] == jnp.arange(owner_count, dtype=jnp.int32)[None, :]).astype(
        jnp.int32
    )
    before = jnp.sum((jnp.cumsum(onehot, axis=0) - onehot) * onehot, axis=1)
    places = owners * capacity + before
    send_rows = (
        jnp.zeros((owner_count * capacity, feature_share), jnp.bfloat16).at[places].set(tokens)
    )
    send_rows = send_rows.reshape(owner_count, capacity, feature_share)
    send_slots = (
        jnp.full((owner_count * capacity,), -1, jnp.int32).at[places].set(request_adapter_slot)
    )
    send_slots = send_slots.reshape(owner_count, capacity)
    input_rows = lax.all_to_all(send_rows, "adapter", split_axis=0, concat_axis=0, tiled=True)
    slots_in = lax.all_to_all(send_slots, "adapter", split_axis=0, concat_axis=0, tiled=True)
    key_projection_output = jnp.einsum(
        "rzq,qt->rzt", input_rows, stacked_down_weight, preferred_element_type=jnp.float32
    )
    key_projection_output = key_projection_output.reshape(
        input_rows.shape[0], input_rows.shape[1], local_adapters, ADAPTER_RANK
    )
    chosen = slots_in[:, :, None] == jnp.arange(local_adapters, dtype=jnp.int32)[None, None, :]
    partial_low = jnp.sum(jnp.where(chosen[:, :, :, None], key_projection_output, 0.0), axis=2)
    partial_low, slots_in = (partial_low, slots_in)
    shrunk = lax.psum(partial_low, "mp")
    shrunk_bf = shrunk.astype(jnp.bfloat16)
    returned = lax.all_to_all(shrunk_bf, "adapter", split_axis=0, concat_axis=0, tiled=True)
    low_rows = returned.reshape(owner_count * capacity, ADAPTER_RANK)[places]
    gathered_up_weight = lax.all_gather(stacked_up_weight, "adapter", axis=0, tiled=True)
    adapter_ids = owners * local_adapters + request_adapter_slot
    up_taken = gathered_up_weight.reshape(-1, ADAPTER_RANK, key_output_share)[adapter_ids]
    adapter_updates = jnp.einsum(
        "tr,trk->tk", low_rows, up_taken, preferred_element_type=jnp.float32
    ).astype(jnp.bfloat16)
    base_output_share = lax.psum_scatter(
        lax.dot_general(
            base_key_weight, tokens, (((0,), (1,)), ((), ())), preferred_element_type=jnp.float32
        ),
        "mp",
        scatter_dimension=0,
        tiled=True,
    )
    return (base_output_share.T + ADAPTER_SCALE * adapter_updates.astype(jnp.float32)).astype(
        jnp.bfloat16
    )


def solution(mesh):
    placed = (
        P(("groups", "adapter"), "mp"),
        P("mp", None),
        P("mp", "adapter"),
        P("adapter", "mp"),
        P(("groups", "adapter"), None),
        P(("groups", "adapter")),
    )
    return jax.shard_map(
        local, mesh=mesh, in_specs=placed, out_specs=P(("groups", "adapter"), "mp"), check_vma=False
    )
```

profile of v0, /device:TPU:0, one launch (start us, length us, event | category | flops | bytes accessed | tf_op | source)
XLA Modules:
  0.0 130.7 jit_solution(15153360889486542213)
XLA Ops:
  6.5 0.0 copy-start
  6.5 0.8 reduce
  7.4 1.2 reduce-window.6
  8.6 0.2 slice_reduce_fusion
  8.8 0.2 reduce-window.9
  9.0 0.1 add_bitcast_fusion
  9.1 0.7 fusion.13
  9.8 3.1 %scatter_custom_fusion = s32[576]{0:T(1024)S(1)} fusion(s32[384]{0:T(512)S(1)} %fusion.13, s32[384]{0:T(512)} %param.11, s32[]{:T(128)} %constant.9.clone.1), kind=kCustom, calls=%fused_computation.29 | custom fusion | bytes 2816 | tf_op jit(solution)/shard_map/scatter | solution.py:37
  12.9 0.7 all_to_all.12
  13.6 6.3 %all-to-all-start = ((s32[4,1,144]{2,1,0:T(1,128)}), s32[4,1,144]{2,1,0:T(1,128)S(1)}, u32[]{:S(2)}, u32[]{:S(2)}) async-start(s32[4,1,144]{2,1,0:T(1,128)} %all_to_all.12), calls=%async_computation.1 | async-start | bytes 8192 | tf_op jit(solution)/shard_map/all_to_all | solution.py:41
  19.9 5.4 %scatter_custom_fusion.1 = bf16[576,2048]{1,0:T(8,128)(2,1)} fusion(s32[384]{0:T(512)S(1)} %fusion.13, bf16[384,2048]{1,0:T(8,128)(2,1)} %param.6, bf16[]{:T(256)} %constant.5.clone.1), kind=kCustom, calls=%fused_computation.4 | custom fusion | bytes 2359808 | tf_op jit(solution)/shard_map/scatter | solution.py:33
  25.3 0.2 all-to-all-done
  25.5 4.9 %all-to-all-start.1 = ((bf16[4,144,2048]{2,1,0:T(8,128)(2,1)}), bf16[4,144,2048]{2,1,0:T(8,128)(2,1)}, u32[]{:S(2)}, u32[]{:S(2)}) async-start(bf16[4,144,2048]{2,1,0:T(8,128)(2,1)} %bitcast.44), calls=%async_computation.2 | async-start | bytes 4718592 | tf_op jit(solution)/shard_map/all_to_all | solution.py:40
  30.4 0.0 copy-start.2
  30.4 0.0 copy-start.3
  30.4 0.0 reduce-scatter.2.cloned.1.call-start
  30.4 0.0 copy-done
  30.4 3.7 %fusion.14 = f32[512,384]{1,0:T(8,128)} fusion(bf16[2048,512]{1,0:T(8,128)(2,1)S(1)} %copy-done, bf16[384,2048]{1,0:T(8,128)(2,1)} %param.6), kind=kOutput, calls=%fused_computation.32 | convolution fusion | flops 805306368 | bytes 4456448 | tf_op jit(solution)/shard_map/dot_general | solution.py:62
  34.1 0.0 reduce-scatter.2.cloned.1.call-update
  34.2 0.0 copy-done.2
  34.2 0.0 copy-start.1
  34.2 49.5 %all-to-all-done.1 = bf16[4,144,2048]{2,1,0:T(8,128)(2,1)} async-done(((bf16[4,144,2048]{2,1,0:T(8,128)(2,1)}), bf16[4,144,2048]{2,1,0:T(8,128)(2,1)}, u32[]{:S(2)}, u32[]{:S(2)}) %all-to-all-start.1) | async-done | bytes 2359328 | tf_op jit(solution)/shard_map/all_to_all | solution.py:40
  83.8 0.0 copy-done.3
  83.8 3.0 %fusion.2 = f32[4,144,256]{1,2,0:T(8,128)S(1)} fusion(bf16[4,144,2048]{2,1,0:T(8,128)(2,1)} %all-to-all-done.1, bf16[2048,256]{1,0:T(8,128)(2,1)S(1)} %copy-done.3), kind=kOutput, calls=%fused_computation.6 | convolution fusion | flops 603979776 | bytes 3997696 | tf_op jit(solution)/shard_map/rzq,qt->rzt/dot_general | solution.py:42
  86.7 0.2 select_reduce_fusion
  86.9 11.3 %psum.7 = bf16[4,144,16]{1,2,0:T(8,128)(2,1)} all-reduce(f32[4,144,16]{1,2,0:T(8,128)S(1)} %select_reduce_fusion), channel_id=1, replica_groups=mesh['groups'=2,'adapter'=4,'mp'=4] {'mp'}, use_global_device_ids=true, to_apply=%region_7.8 | all-reduce | flops 9216 | bytes 55296 | tf_op jit(solution)/shard_map/psum | solution.py:51
  98.2 3.3 %all-to-all-start.2 = ((bf16[4,144,16]{1,2,0:T(8,128)(2,1)}), bf16[4,144,16]{1,2,0:T(8,128)(2,1)S(1)}, u32[]{:S(2)}, u32[]{:S(2)}) async-start(bf16[4,144,16]{1,2,0:T(8,128)(2,1)} %psum.7), calls=%async_computation.3 | async-start | bytes 65536 | tf_op jit(solution)/shard_map/all_to_all | solution.py:53
  101.5 0.0 copy-done.1
  101.5 14.4 %all_gather.3 = bf16[1024,128]{1,0:T(8,128)(2,1)S(1)} all-gather(bf16[256,128]{1,0:T(8,128)(2,1)S(1)} %copy-done.1), channel_id=1, replica_groups=mesh['groups'=2,'adapter'=4,'mp'=4] {'adapter'}, dimensions={0}, use_global_device_ids=true | all-gather | bytes 327680 | tf_op jit(solution)/shard_map/all_gather | solution.py:55
  115.9 2.6 %gather_fusion.1 = bf16[384,16,128]{2,1,0:T(8,128)(2,1)} fusion(bf16[64,16,128]{2,1,0:T(8,128)(2,1)S(1)} %bitcast.43, s32[1024]{0:T(1024)S(1)} %pad_clamp_fusion), kind=kCustom, calls=%fused_computation.1 | custom fusion | bytes 3147264 | tf_op jit(solution)/shard_map/gather | solution.py:57
  118.4 0.0 all-to-all-done.2
  118.4 0.2 copy.11
  118.6 1.4 %gather_fusion = bf16[384,16]{1,0:T(8,128)(2,1)S(1)} fusion(bf16[576,16]{1,0:T(8,128)(2,1)S(1)} %bitcast.45, s32[1024]{0:T(1024)S(1)} %pad_clamp_fusion.1), kind=kCustom, calls=%fused_computation | custom fusion | bytes 26112 | tf_op jit(solution)/shard_map/gather | solution.py:54
  120.1 2.0 %fusion.5 = bf16[384,1,128]{2,1,0:T(2,128)(2,1)S(1)} fusion(bf16[384,16,128]{2,1,0:T(8,128)(2,1)} %gather_fusion.1, bf16[384,16,1]{1,0,2:T(8,128)(2,1)S(1)} %bitcast.47), kind=kOutput, calls=%fused_computation.12 | convolution fusion | flops 1572864 | bytes 1683456 | tf_op jit(solution)/shard_map/tr,trk->tk/dot_general | solution.py:58
  122.0 0.1 copy.15
  122.2 0.0 reduce-scatter.2.cloned.1.call-done
  122.2 1.0 fusion.4
  123.1 0.8 copy.12
  (7 shorter events, 0.1 us)
Async XLA Ops:
  6.5 23.9 %copy-start = (bf16[2048,512]{1,0:T(8,128)(2,1)S(1)}, bf16[2048,512]{1,0:T(8,128)(2,1)}, u32[]{:S(2)}) copy-start(bf16[2048,512]{1,0:T(8,128)(2,1)} %param.7) | copy-start | bytes 6291460
  13.6 11.9 %all-to-all-start = ((s32[4,1,144]{2,1,0:T(1,128)}), s32[4,1,144]{2,1,0:T(1,128)S(1)}, u32[]{:S(2)}, u32[]{:S(2)}) async-start(s32[4,1,144]{2,1,0:T(1,128)} %all_to_all.12), calls=%async_computation.1 | async-start | bytes 8192 | tf_op jit(solution)/shard_map/all_to_all | solution.py:41
  25.5 58.3 %all-to-all-start.1 = ((bf16[4,144,2048]{2,1,0:T(8,128)(2,1)}), bf16[4,144,2048]{2,1,0:T(8,128)(2,1)}, u32[]{:S(2)}, u32[]{:S(2)}) async-start(bf16[4,144,2048]{2,1,0:T(8,128)(2,1)} %bitcast.44), calls=%async_computation.2 | async-start | bytes 4718592 | tf_op jit(solution)/shard_map/all_to_all | solution.py:40
  30.4 3.8 %copy-start.2 = (s32[384]{0:T(512)S(1)}, s32[384]{0:T(512)}, u32[]{:S(2)}) copy-start(s32[384]{0:T(512)} %param.11) | copy-start | bytes 4612
  30.4 53.4 %copy-start.3 = (bf16[2048,256]{1,0:T(8,128)(2,1)S(1)}, bf16[2048,256]{1,0:T(8,128)(2,1)}, u32[]{:S(2)}) copy-start(bf16[2048,256]{1,0:T(8,128)(2,1)} %param.8) | copy-start | bytes 3145732
  30.4 91.8 %reduce-scatter.2.cloned.1.call-start = ((), (), s32[]{:S(2)}) async-start(), calls=%async_computation.4 | async-start | bytes 983040 | tf_op jit(solution)/shard_map/reduce_scatter | solution.py:61
  34.2 67.2 %copy-start.1 = (bf16[256,128]{1,0:T(8,128)(2,1)S(1)}, bf16[256,128]{1,0:T(8,128)(2,1)}, u32[]{:S(2)}) copy-start(bf16[256,128]{1,0:T(8,128)(2,1)} %param.9) | copy-start | bytes 196612
  98.2 20.2 %all-to-all-start.2 = ((bf16[4,144,16]{1,2,0:T(8,128)(2,1)}), bf16[4,144,16]{1,2,0:T(8,128)(2,1)S(1)}, u32[]{:S(2)}, u32[]{:S(2)}) async-start(bf16[4,144,16]{1,2,0:T(8,128)(2,1)} %psum.7), calls=%async_computation.3 | async-start | bytes 65536 | tf_op jit(solution)/shard_map/all_to_all | solution.py:53
Sparse Core Ops, SparseCore 0:
  34.3 24.6 reduce-scatter.1
where the time goes:
time: 131 us
  waiting for transfers between devices  49.7 us (38%)
  blocking collectives  25.7 us (20%)
  starting transfers between devices  14.5 us (11%)
  local copies, waits for them, and re-layouts  14.4 us (11%)
  between operations  13.5 us (10%)
  matrix products  8.59 us (7%)
  other arithmetic  4.22 us (3%)
    all_to_all x1, waiting for transfers between devices, local(): lax.all_to_all(send_rows, 'adapter', split_axis=0, concat_axis=0, tiled=T...  49.5 us
    all_gather x1, blocking collectives, local(): lax.all_gather(stacked_up_weight, 'adapter', axis=0, tiled=True)  14.4 us
    psum x1, blocking collectives, local(): shrunk = lax.psum(partial_low, 'mp')  11.3 us
    all_to_all x1, starting transfers between devices, local(): lax.all_to_all(send_slots, 'adapter', split_axis=0, concat_axis=0, tiled=...  6.32 us
    scatter x1, local copies, waits for them, and re-layouts, local(): jnp.zeros((owner_count * capacity, feature_share), jnp.bfloat16).at[places]  5.39 us
    all_to_all x1, starting transfers between devices, local(): lax.all_to_all(send_rows, 'adapter', split_axis=0, concat_axis=0, tiled=T...  4.91 us
    dot_general x1, matrix products, local(): lax.dot_general(base_key_weight, tokens, (((0,), (1,)), ((), ())), prefer...  3.68 us
    all_to_all x1, starting transfers between devices, local(): lax.all_to_all(shrunk_bf, 'adapter', split_axis=0, concat_axis=0, tiled=T...  3.26 us
  transfers between devices with their start and end apart: 4, of which 2 were waited for; matrix products, arithmetic and copies ran while one was open for 14% of the time, Pallas kernels for 0%

commit v1 on v0

--- a/solution.py
+++ b/solution.py
@@ -9,7 +9,7 @@
 ADAPTER_SCALE = 2.0
 
 
-def local(
+def dispatch(
     tokens,
     base_key_weight,
     stacked_down_weight,
@@ -47,7 +47,6 @@
     )
     chosen = slots_in[:, :, None] == jnp.arange(local_adapters, dtype=jnp.int32)[None, None, :]
     partial_low = jnp.sum(jnp.where(chosen[:, :, :, None], key_projection_output, 0.0), axis=2)
-    partial_low, slots_in = (partial_low, slots_in)
     shrunk = lax.psum(partial_low, "mp")
     shrunk_bf = shrunk.astype(jnp.bfloat16)
     returned = lax.all_to_all(shrunk_bf, "adapter", split_axis=0, concat_axis=0, tiled=True)
@@ -71,6 +70,126 @@
     )
 
 
+AXES = ("groups", "adapter", "mp")
+
+
+def mesh_shift(x, group_step, mp_step):
+    groups, owners, shares = (lax.axis_size(name) for name in AXES)
+
+    def number(g, a, m):
+        return (g * owners + a) * shares + m
+
+    pairs = [
+        (number(g, a, m), number((g + group_step) % groups, a, (m + mp_step) % shares))
+        for g in range(groups)
+        for a in range(owners)
+        for m in range(shares)
+    ]
+    return lax.ppermute(x, AXES, pairs)
+
+
+def gather(
+    tokens,
+    base_key_weight,
+    stacked_down_weight,
+    stacked_up_weight,
+    request_adapter_owner,
+    request_adapter_slot,
+):
+    rows, features = tokens.shape
+    groups, owner_count, shares = (lax.axis_size(name) for name in AXES)
+    g, a, m = (lax.axis_index(name) for name in AXES)
+    columns = stacked_down_weight.shape[1]
+    keys = stacked_up_weight.shape[1]
+    part = features // groups
+    owner = request_adapter_owner.reshape(1, rows)
+    slot = request_adapter_slot.reshape(1, rows)
+
+    half = columns // keys
+    up_rows = columns // half
+    up_wide = jnp.concatenate(
+        [stacked_up_weight[i * up_rows : (i + 1) * up_rows] for i in range(half)], axis=1
+    )
+    down_own = lax.dynamic_slice(stacked_down_weight, (g * part, 0), (part, columns))
+    cut = part // 2
+    pieces = [jnp.concatenate([up_wide, down_own[:cut]], axis=0), down_own[cut:]]
+
+    blocks = [(a, pieces)]
+    forward, backward = pieces, pieces
+    for d in range(1, owner_count):
+        ahead = [(i, i + 1) for i in range(d - 1, owner_count - 1)]
+        back = [(i + 1, i) for i in range(0, owner_count - d)]
+        forward = [lax.ppermute(piece, "adapter", ahead) for piece in forward]
+        backward = [lax.ppermute(piece, "adapter", back) for piece in backward]
+        blocks.append((a - d, forward))
+        blocks.append((a + d, backward))
+
+    token_parts, owner_parts, slot_parts = [], [], []
+    for step in range(groups):
+        wanted = (g + step) % groups
+        mine = lax.dynamic_slice(tokens, (0, wanted * part), (rows, part))
+        if step:
+            token_parts.append(mesh_shift(mine, step, 0))
+            ids = mesh_shift(jnp.concatenate([owner, slot], axis=0), step, 0)
+            owner_parts.append(ids[:1])
+            slot_parts.append(ids[1:])
+        else:
+            token_parts.append(mine)
+            owner_parts.append(owner)
+            slot_parts.append(slot)
+    all_tokens = jnp.concatenate(token_parts, axis=0)
+    all_owner = jnp.concatenate(owner_parts, axis=1)
+    all_slot = jnp.concatenate(slot_parts, axis=1)
+
+    base_part = jnp.dot(tokens, base_key_weight, preferred_element_type=jnp.float32)
+    base = lax.dynamic_slice(base_part, (0, m * keys), (rows, keys))
+    for step in range(1, shares):
+        block = lax.dynamic_slice(base_part, (0, (m + step) % shares * keys), (rows, keys))
+        base = base + mesh_shift(block, 0, step)
+
+    contract = (((0,), (1,)), ((), ()))
+    picked = jnp.zeros((columns, groups * rows), jnp.float32)
+    for number, (first, second) in blocks:
+        wide = lax.dot_general(
+            first[up_rows:], all_tokens[:, :cut], contract, preferred_element_type=jnp.float32
+        ) + lax.dot_general(
+            second, all_tokens[:, cut:], contract, preferred_element_type=jnp.float32
+        )
+        picked = jnp.where(all_owner == number, wide, picked)
+    adapter = lax.broadcasted_iota(jnp.int32, (columns, 1), 0) // ADAPTER_RANK
+    picked = jnp.where(adapter == all_slot, picked, 0.0)
+    low = jnp.sum(picked.reshape(-1, ADAPTER_RANK, groups * rows), axis=0)
+
+    shrunk = low[:, :rows]
+    for group_step in range(groups):
+        mine = low[:, group_step * rows : (group_step + 1) * rows]
+        for mp_step in range(shares):
+            if group_step or mp_step:
+                shrunk = shrunk + mesh_shift(mine, -group_step, mp_step)
+
+    shrunk_bf = shrunk.astype(jnp.bfloat16)
+    spread = jnp.concatenate([shrunk_bf] * (columns // ADAPTER_RANK), axis=0)
+    spread = jnp.where(adapter == slot, spread, jnp.bfloat16(0))
+    updates = jnp.zeros((rows, keys), jnp.float32)
+    for number, (first, _) in blocks:
+        up = jnp.concatenate(
+            [first[:up_rows, i * keys : (i + 1) * keys] for i in range(half)], axis=0
+        )
+        chosen = jnp.where(owner == number, spread, jnp.bfloat16(0))
+        updates = updates + lax.dot_general(
+            chosen, up, (((0,), (0,)), ((), ())), preferred_element_type=jnp.float32
+        )
+    updates = updates.astype(jnp.bfloat16).astype(jnp.float32)
+    return (base + ADAPTER_SCALE * updates).astype(jnp.bfloat16)
+
+
+def local(*args):
+    rows, columns = args[0].shape[0], args[2].shape[1]
+    capacity = max(2, 3 * rows // (2 * lax.axis_size("adapter")))
+    travels = columns <= lax.axis_size("groups") * capacity
+    return (gather if travels else dispatch)(*args)
+
+
 def solution(mesh):
     placed = (
         P(("groups", "adapter"), "mp"),

time: 131 us -> 83 us (0.63)
  waiting for transfers between devices: 49.7 us -> 17 us
  blocking collectives: 25.7 us -> 0 us
  starting transfers between devices: 14.5 us -> 33.9 us
  between operations: 13.5 us -> 0.63 us
  matrix products: 8.59 us -> 18.3 us
  local copies, waits for them, and re-layouts: 14.4 us -> 10.2 us
  other arithmetic: 4.22 us -> 1.62 us
    all_to_all x3 -> x0, waiting for transfers between devices: 49.7 us -> none  [the longest x1 49.5 us: local(): lax.all_to_all(send_rows, 'adapter', split_axis=0, concat_axis=0, tiled=T...]
    ppermute x0 -> x24, starting transfers between devices: none -> 33.9 us  [the longest x6 13.6 us: gather(): forward = [lax.ppermute(piece, 'adapter', ahead) for piece in forward]]
    ppermute x0 -> x24, waiting for transfers between devices: none -> 17 us  [the longest x6 12.9 us: gather(): backward = [lax.ppermute(piece, 'adapter', back) for piece in backward]]
    all_to_all x3 -> x0, starting transfers between devices: 14.5 us -> none  [the longest x1 6.32 us: local(): lax.all_to_all(send_slots, 'adapter', split_axis=0, concat_axis=0, tiled=...]
    all_gather x1 -> x0, blocking collectives: 14.4 us -> none  [local(): lax.all_gather(stacked_up_weight, 'adapter', axis=0, tiled=True)]
    psum x1 -> x0, blocking collectives: 11.3 us -> none  [local(): shrunk = lax.psum(partial_low, 'mp')]
    dot_general x3 -> x22, matrix products: 8.59 us -> 18.3 us  [the longest x7 5.25 us: gather(): lax.dot_general(chosen, up, (((0,), (0,)), ((), ())), preferred_element_t...]
    scatter x2 -> x0, local copies, waits for them, and re-layouts: 8.47 us -> none  [the longest x1 5.39 us: local(): jnp.zeros((owner_count * capacity, feature_share), jnp.bfloat16).at[places]]
  transfers between devices with their start and end apart: 4 -> 24, of which waited for: 2 -> 5; matrix products, arithmetic and copies ran while one was open for 14% -> 32% of each run, Pallas kernels for 0% -> 0%
where the time goes in v1:
time: 83 us; the launch traced here: 81.6 us
  starting transfers between devices  33.9 us (41%)
  matrix products  18.3 us (22%)
  waiting for transfers between devices  17 us (20%)
  local copies, waits for them, and re-layouts  10.2 us (12%)
  other arithmetic  1.62 us (2%)
    ppermute x6, starting transfers between devices, gather(): forward = [lax.ppermute(piece, 'adapter', ahead) for piece in forward]  13.6 us
    ppermute x6, waiting for transfers between devices, gather(): backward = [lax.ppermute(piece, 'adapter', back) for piece in backward]  12.9 us
    ppermute x12, starting transfers between devices, mesh_shift(): return lax.ppermute(x, AXES, pairs)  12.6 us
    ppermute x6, starting transfers between devices, gather(): backward = [lax.ppermute(piece, 'adapter', back) for piece in backward]  7.71 us
    dot_general x7, matrix products, gather(): lax.dot_general(chosen, up, (((0,), (0,)), ((), ())), preferred_element_t...  5.25 us
    dot_general x7, matrix products, gather(): lax.dot_general(first[up_rows:], all_tokens[:, :cut], contract, preferred...  4.85 us
    dot_general x7, matrix products, gather(): lax.dot_general(second, all_tokens[:, cut:], contract, preferred_element_...  4.77 us
    slice x6, local copies, waits for them, and re-layouts, gather(): first[:up_rows, i * keys:(i + 1) * keys]  4.37 us
  transfers between devices with their start and end apart: 24, of which 5 were waited for; matrix products, arithmetic and copies ran while one was open for 32% of the time, Pallas kernels for 0%

profile of v1, /device:TPU:0, one launch (start us, length us, event | category | flops | bytes accessed | tf_op | source)
XLA Modules:
  0.0 81.6 jit_solution(13771706731012681191)
XLA Ops:
  0.0 1.2 %constant_dynamic-slice_fusion.3 = (bf16[512,256]{1,0:T(8,128)(2,1)S(1)}, bf16[512,256]{1,0:T(8,128)(2,1)S(1)}) fusion(bf16[2048,256]{1,0:T(8,128)(2,1)} %param.8, s32[]{:T(128)S(6)} %add.188, s32[]{:T(128)S(6)} %select_n.116), kind=kLoop, calls=%fused_computation.113 | loop fusion | bytes 1048584 | tf_op jit(solution)/shard_map/slice | solution.py:115
  1.2 5.7 %collective-permute-start.14 = (bf16[512,256]{1,0:T(8,128)(2,1)S(1)}, bf16[512,256]{1,0:T(8,128)(2,1)}, u32[]{:S(2)}, u32[]{:S(2)}) collective-permute-start(bf16[512,256]{1,0:T(8,128)(2,1)S(1)} %get-tuple-element.11), channel_id=1, source_target_pairs={{0,4},{4,8},{8,12},{1,5},{5,9},{9,13},{2,6},{6,10},{10,14},{3,7},{... | collective-permute-start | bytes 786440 | tf_op jit(solution)/shard_map/ppermute | solution.py:122
  6.9 1.3 %collective-permute-start.8 = (bf16[512,256]{1,0:T(8,128)(2,1)S(1)}, bf16[512,256]{1,0:T(8,128)(2,1)}, u32[]{:S(2)}, u32[]{:S(2)}) collective-permute-start(bf16[512,256]{1,0:T(8,128)(2,1)S(1)} %get-tuple-element.11), channel_id=1, source_target_pairs={{4,0},{8,4},{12,8},{5,1},{9,5},{13,9},{6,2},{10,6},{14,10},{7,3},{... | collective-permute-start | bytes 786440 | tf_op jit(solution)/shard_map/ppermute | solution.py:123
  8.2 0.8 fusion.83
  8.9 0.8 pad_maximum_fusion.1
  9.7 5.3 %collective-permute-start.11 = (bf16[640,256]{1,0:T(8,128)(2,1)}, bf16[640,256]{1,0:T(8,128)(2,1)}, u32[]{:S(2)}, u32[]{:S(2)}) collective-permute-start(bf16[640,256]{1,0:T(8,128)(2,1)} %pad_maximum_fusion.1), channel_id=1, source_target_pairs={{0,4},{4,8},{8,12},{1,5},{5,9},{9,13},{2,6},{6,10},{10,14},{3,7},{... | collective-permute-start | bytes 983048 | tf_op jit(solution)/shard_map/ppermute | solution.py:122
  15.0 1.3 %collective-permute-start.4 = (bf16[640,256]{1,0:T(8,128)(2,1)}, bf16[640,256]{1,0:T(8,128)(2,1)}, u32[]{:S(2)}, u32[]{:S(2)}) collective-permute-start(bf16[640,256]{1,0:T(8,128)(2,1)} %pad_maximum_fusion.1), channel_id=1, source_target_pairs={{4,0},{8,4},{12,8},{5,1},{9,5},{13,9},{6,2},{10,6},{14,10},{7,3},{... | collective-permute-start | bytes 983048 | tf_op jit(solution)/shard_map/ppermute | solution.py:123
  16.3 1.6 %collective-permute-start.3 = (s32[2,384]{1,0:T(2,128)S(1)}, s32[2,384]{1,0:T(2,128)S(1)}, u32[]{:S(2)}, u32[]{:S(2)}) collective-permute-start(s32[2,384]{1,0:T(2,128)S(1)} %pad_add_fusion.1), channel_id=1, source_target_pairs={{0,16},{1,17},{2,18},{3,19},{4,20},{5,21},{6,22},{7,23},{8,24},{9,... | collective-permute-start | bytes 9224 | tf_op jit(solution)/shard_map/ppermute | solution.py:88
  18.0 3.4 %fusion.86 = f32[384,512]{1,0:T(8,128)} fusion(bf16[384,2048]{1,0:T(8,128)(2,1)} %param.6, bf16[2048,512]{1,0:T(8,128)(2,1)S(1)} %copy-done), kind=kOutput, calls=%fused_computation.148 | convolution fusion | flops 805306368 | bytes 4456448 | tf_op jit(solution)/shard_map/dot_general | solution.py:144
  21.4 1.0 %constant_dynamic-slice_fusion.2 = (bf16[384,1024]{1,0:T(8,128)(2,1)S(1)}, bf16[384,1024]{1,0:T(8,128)(2,1)}) fusion(bf16[384,2048]{1,0:T(8,128)(2,1)S(1)} %copy-done.1, s32[]{:T(128)S(6)} %select_n.118, s32[]{:T(128)S(6)} %select_n.120), kind=kLoop, calls=%fused_computation.112 | loop fusion | bytes 3145736 | tf_op jit(solution)/shard_map/dynamic_slice | solution.py:130
  22.4 1.9 %constant_dynamic-slice_fusion.6 = (f32[384,128]{1,0:T(8,128)}, f32[384,128]{1,0:T(8,128)}, f32[384,128]{1,0:T(8,128)}) fusion(f32[384,512]{1,0:T(8,128)} %fusion.86, s32[]{:T(128)S(6)} %select_n.110, s32[]{:T(128)S(6)} %select_n.114, s32[]{:T(128)S(6)} %select_n.112), kind=kLoop, calls=%fused_computation.116 | loop fusion | bytes 1179660 | tf_op jit(solution)/shard_map/dynamic_slice | solution.py:147
  24.4 0.6 broadcast_compare_fusion.8
  25.0 0.6 collective-permute-start.7
  25.6 0.7 collective-permute-start.15
  26.3 1.3 %collective-permute-start.9 = (bf16[512,256]{1,0:T(8,128)(2,1)}, bf16[512,256]{1,0:T(8,128)(2,1)S(1)}, u32[]{:S(2)}, u32[]{:S(2)}) collective-permute-start(bf16[512,256]{1,0:T(8,128)(2,1)} %collective-permute-done.8), channel_id=1, source_target_pairs={{4,0},{8,4},{5,1},{9,5},{6,2},{10,6},{7,3},{11,7},{20,16},{24,20},... | collective-permute-start | bytes 786440 | tf_op jit(solution)/shard_map/ppermute | solution.py:123
  27.6 0.7 collective-permute-start.12
  28.3 1.3 %collective-permute-start.5 = (bf16[640,256]{1,0:T(8,128)(2,1)}, bf16[640,256]{1,0:T(8,128)(2,1)S(1)}, u32[]{:S(2)}, u32[]{:S(2)}) collective-permute-start(bf16[640,256]{1,0:T(8,128)(2,1)} %collective-permute-done.4), channel_id=1, source_target_pairs={{4,0},{8,4},{5,1},{9,5},{6,2},{10,6},{7,3},{11,7},{20,16},{24,20},... | collective-permute-start | bytes 983048 | tf_op jit(solution)/shard_map/ppermute | solution.py:123
  29.6 1.4 %fusion.80 = (bf16[128,128]{1,0:T(8,128)(2,1)}, bf16[128,128]{1,0:T(8,128)(2,1)}) fusion(bf16[640,256]{1,0:T(8,128)(2,1)} %collective-permute-done.11), kind=kLoop, calls=%fused_computation.142 | loop fusion | bytes 131072 | tf_op jit(solution)/shard_map/slice | solution.py:176
  31.0 0.8 fusion.79
  31.8 0.7 collective-permute-start.16
  32.5 5.0 %collective-permute-done.9 = bf16[512,256]{1,0:T(8,128)(2,1)S(1)} collective-permute-done((bf16[512,256]{1,0:T(8,128)(2,1)}, bf16[512,256]{1,0:T(8,128)(2,1)S(1)}, u32[]{:S(2)}, u32[]{:S(2)}) %collective-permute-start.9) | collective-permute-done | bytes 262176 | tf_op jit(solution)/shard_map/ppermute | solution.py:123
  37.5 1.3 %collective-permute-start.10 = (bf16[512,256]{1,0:T(8,128)(2,1)S(1)}, bf16[512,256]{1,0:T(8,128)(2,1)S(1)}, u32[]{:S(2)}, u32[]{:S(2)}) collective-permute-start(bf16[512,256]{1,0:T(8,128)(2,1)S(1)} %collective-permute-done.9), channel_id=1, source_target_pairs={{4,0},{5,1},{6,2},{7,3},{20,16},{21,17},{22,18},{23,19}} | collective-permute-start | bytes 786440 | tf_op jit(solution)/shard_map/ppermute | solution.py:123
  38.8 0.7 collective-permute-start.13
  39.5 7.8 %collective-permute-done.5 = bf16[640,256]{1,0:T(8,128)(2,1)S(1)} collective-permute-done((bf16[640,256]{1,0:T(8,128)(2,1)}, bf16[640,256]{1,0:T(8,128)(2,1)S(1)}, u32[]{:S(2)}, u32[]{:S(2)}) %collective-permute-start.5) | collective-permute-done | bytes 327712 | tf_op jit(solution)/shard_map/ppermute | solution.py:123
  47.4 1.3 %collective-permute-start.6 = (bf16[640,256]{1,0:T(8,128)(2,1)S(1)}, bf16[640,256]{1,0:T(8,128)(2,1)S(1)}, u32[]{:S(2)}, u32[]{:S(2)}) collective-permute-start(bf16[640,256]{1,0:T(8,128)(2,1)S(1)} %collective-permute-done.5), channel_id=1, source_target_pairs={{4,0},{5,1},{6,2},{7,3},{20,16},{21,17},{22,18},{23,19}} | collective-permute-start | bytes 983048 | tf_op jit(solution)/shard_map/ppermute | solution.py:123
  48.6 0.6 fusion.81
  50.2 1.4 %fusion.92 = f32[256,768]{1,0:T(8,128)S(1)} fusion(bf16[512,256]{1,0:T(8,128)(2,1)} %collective-permute-done.14, bf16[768,512]{1,0:T(8,128)(2,1)S(1)} %get-tuple-element.8), kind=kOutput, calls=%fused_computation.154 | convolution fusion | flops 201326592 | bytes 1835008 | tf_op jit(solution)/shard_map/dot_general | solution.py:155
  51.6 1.4 %fusion.91 = f32[256,768]{1,0:T(8,128)S(1)} fusion(bf16[512,256]{1,0:T(8,128)(2,1)} %collective-permute-done.8, bf16[768,512]{1,0:T(8,128)(2,1)S(1)} %get-tuple-element.8), kind=kOutput, calls=%fused_computation.153 | convolution fusion | flops 201326592 | bytes 1835008 | tf_op jit(solution)/shard_map/dot_general | solution.py:155
  53.8 1.4 %fusion.1 = f32[256,768]{1,0:T(8,128)S(1)} fusion(f32[256,768]{1,0:T(8,128)S(1)} %fusion, f32[256,768]{1,0:T(8,128)S(1)} %fusion.92, bf16[768,512]{1,0:T(8,128)(2,1)S(1)} %get-tuple-element.7, pred[768]{0:T(1024)(128)(4,1)S(1)} %get-tuple-element.37, bf16[640,256]{1,0:T(8,128)(2,1)} %collective-permute-done.11), kind=kOutput, calls=%fused_computation.5 | convolution fusion | flops 201719808 | bytes 3408640 | tf_op jit(solution)/shard_map/dot_general | solution.py:153
  55.2 1.4 %fusion.2 = f32[256,768]{1,0:T(8,128)S(1)} fusion(f32[256,768]{1,0:T(8,128)S(1)} %fusion.1, f32[256,768]{1,0:T(8,128)S(1)} %fusion.91, bf16[768,512]{1,0:T(8,128)(2,1)S(1)} %get-tuple-element.7, pred[768]{0:T(1024)(128)(4,1)S(1)} %get-tuple-element.36, bf16[640,256]{1,0:T(8,128)(2,1)} %collective-permute-done.4), kind=kOutput, calls=%fused_computation.7 | convolution fusion | flops 201719808 | bytes 3408640 | tf_op jit(solution)/shard_map/dot_general | solution.py:153
  56.5 0.4 fusion.3
  57.0 0.4 fusion.4
  58.3 0.4 fusion.5
  59.0 0.4 fusion.7
  59.9 1.5 %collective-permute-start.18 = (f32[16,384]{1,0:T(8,128)S(1)}, f32[16,384]{1,0:T(8,128)S(1)}, u32[]{:S(2)}, u32[]{:S(2)}) collective-permute-start(f32[16,384]{1,0:T(8,128)S(1)} %get-tuple-element.30), channel_id=1, source_target_pairs={{0,2},{1,3},{2,0},{3,1},{4,6},{5,7},{6,4},{7,5},{8,10},{9,11},{10,... | collective-permute-start | bytes 73736 | tf_op jit(solution)/shard_map/ppermute | solution.py:88
  61.5 1.4 %collective-permute-start.19 = (f32[16,384]{1,0:T(8,128)S(1)}, f32[16,384]{1,0:T(8,128)S(1)}, u32[]{:S(2)}, u32[]{:S(2)}) collective-permute-start(f32[16,384]{1,0:T(8,128)S(1)} %get-tuple-element.30), channel_id=1, source_target_pairs={{0,3},{1,0},{2,1},{3,2},{4,7},{5,4},{6,5},{7,6},{8,11},{9,8},{10,9... | collective-permute-start | bytes 73736 | tf_op jit(solution)/shard_map/ppermute | solution.py:88
  62.9 1.5 %collective-permute-start.20 = (f32[16,384]{1,0:T(8,128)S(1)}, f32[16,384]{1,0:T(8,128)S(1)}, u32[]{:S(2)}, u32[]{:S(2)}) collective-permute-start(f32[16,384]{1,0:T(8,128)S(1)} %get-tuple-element.31), channel_id=1, source_target_pairs={{0,16},{1,17},{2,18},{3,19},{4,20},{5,21},{6,22},{7,23},{8,24},{9,... | collective-permute-start | bytes 73736 | tf_op jit(solution)/shard_map/ppermute | solution.py:88
  64.4 0.8 fusion.82
  65.2 1.2 %collective-permute-start.22 = (f32[16,384]{1,0:T(8,128)S(1)}, f32[16,384]{1,0:T(8,128)S(1)}, u32[]{:S(2)}, u32[]{:S(2)}) collective-permute-start(f32[16,384]{1,0:T(8,128)S(1)} %get-tuple-element.31), channel_id=1, source_target_pairs={{0,18},{1,19},{2,16},{3,17},{4,22},{5,23},{6,20},{7,21},{8,26},{9,... | collective-permute-start | bytes 73736 | tf_op jit(solution)/shard_map/ppermute | solution.py:88
  66.4 1.7 %collective-permute-start.23 = (f32[16,384]{1,0:T(8,128)S(1)}, f32[16,384]{1,0:T(8,128)S(1)}, u32[]{:S(2)}, u32[]{:S(2)}) collective-permute-start(f32[16,384]{1,0:T(8,128)S(1)} %get-tuple-element.31), channel_id=1, source_target_pairs={{0,19},{1,16},{2,17},{3,18},{4,23},{5,20},{6,21},{7,22},{8,27},{9,... | collective-permute-start | bytes 73736 | tf_op jit(solution)/shard_map/ppermute | solution.py:88
  68.1 0.8 fusion.77
  68.9 1.6 %collective-permute-start.1 = (f32[384,128]{1,0:T(8,128)}, f32[384,128]{1,0:T(8,128)S(1)}, u32[]{:S(2)}, u32[]{:S(2)}) collective-permute-start(f32[384,128]{1,0:T(8,128)} %get-tuple-element.15), channel_id=1, source_target_pairs={{0,2},{1,3},{2,0},{3,1},{4,6},{5,7},{6,4},{7,5},{8,10},{9,11},{10,... | collective-permute-start | bytes 589832 | tf_op jit(solution)/shard_map/ppermute | solution.py:88
  70.5 1.4 %collective-permute-start.2 = (f32[384,128]{1,0:T(8,128)}, f32[384,128]{1,0:T(8,128)S(1)}, u32[]{:S(2)}, u32[]{:S(2)}) collective-permute-start(f32[384,128]{1,0:T(8,128)} %get-tuple-element.14), channel_id=1, source_target_pairs={{0,3},{1,0},{2,1},{3,2},{4,7},{5,4},{6,5},{7,6},{8,11},{9,8},{10,9... | collective-permute-start | bytes 589832 | tf_op jit(solution)/shard_map/ppermute | solution.py:88
  72.1 0.9 %fusion.30 = f32[384,128]{1,0:T(8,128)S(1)} fusion(bf16[256,128]{1,0:T(8,128)(2,1)S(1)} %copy-done.4, pred[384]{0:T(512)(128)(4,1)} %get-tuple-element.46, bf16[256,384]{1,0:T(8,128)(2,1)S(1)} %constant_dynamic-update-slice_fusion, s32[384]{0:T(512)S(1)} %copy-done.9, s32[256]{0:T(256)S(1)} %and_select_fusion), kind=kOutput, calls=%fused_computation.46 | convolution fusion | flops 25460736 | bytes 461696 | tf_op jit(solution)/shard_map/dot_general | solution.py:179
  73.1 1.0 %fusion.25 = f32[384,128]{1,0:T(8,128)S(1)} fusion(pred[384]{0:T(512)(128)(4,1)} %get-tuple-element.42, bf16[128,128]{1,0:T(8,128)(2,1)S(1)} %copy-done.8, bf16[128,128]{1,0:T(8,128)(2,1)S(1)} %copy-done.7, bf16[256,384]{1,0:T(8,128)(2,1)S(1)} %constant_dynamic-update-slice_fusion, s32[384]{0:T(512)S(1)} %copy-done.9, s32[256]{0:T(256)S(1)} %and_select_fusion), kind=kOutput, calls=%fused_computation.41 | convolution fusion | flops 25591808 | bytes 461696 | tf_op jit(solution)/shard_map/dot_general | solution.py:179
  75.7 1.2 %collective-permute-done.1 = f32[384,128]{1,0:T(8,128)S(1)} collective-permute-done((f32[384,128]{1,0:T(8,128)}, f32[384,128]{1,0:T(8,128)S(1)}, u32[]{:S(2)}, u32[]{:S(2)}) %collective-permute-start.1) | collective-permute-done | bytes 196640 | tf_op jit(solution)/shard_map/ppermute | solution.py:88
  76.9 2.7 %collective-permute-done.2 = f32[384,128]{1,0:T(8,128)S(1)} collective-permute-done((f32[384,128]{1,0:T(8,128)}, f32[384,128]{1,0:T(8,128)S(1)}, u32[]{:S(2)}, u32[]{:S(2)}) %collective-permute-start.2) | collective-permute-done | bytes 196640 | tf_op jit(solution)/shard_map/ppermute | solution.py:88
  79.7 1.9 %fusion.14 = bf16[384,128]{1,0:T(8,128)(2,1)} fusion(f32[384,128]{1,0:T(8,128)S(1)} %fusion.22, f32[384,128]{1,0:T(8,128)S(1)} %fusion.9, f32[384,128]{1,0:T(8,128)S(1)} %collective-permute-done.2, f32[384,128]{1,0:T(8,128)S(1)} %collective-permute-done.1, f32[384,128]{1,0:T(8,128)S(1)} %collective-permute-done, f32[384,512]{1,0:T(8,128)} %fusion.86, ...), kind=kOutput, calls=%fused_computation.27 | convolution fusion | flops 26083328 | bytes 1543044 | tf_op jit(solution)/shard_map/dot_general | solution.py:179
  (89 shorter events, 5.3 us)
Async XLA Ops:
  0.0 18.0 %copy-start = (bf16[2048,512]{1,0:T(8,128)(2,1)S(1)}, bf16[2048,512]{1,0:T(8,128)(2,1)}, u32[]{:S(2)}) copy-start(bf16[2048,512]{1,0:T(8,128)(2,1)} %param.7) | copy-start | bytes 6291460
  0.0 16.3 %copy-start.9 = (s32[384]{0:T(512)S(1)}, s32[384]{0:T(512)}, u32[]{:S(2)}) copy-start(s32[384]{0:T(512)} %param.11) | copy-start | bytes 4612
  0.0 16.3 %copy-start.10 = (s32[384,1]{0,1:T(1,128)S(1)}, s32[384,1]{0,1:T(1,128)}, u32[]{:S(2)}) copy-start(s32[384,1]{0,1:T(1,128)} %param.10) | copy-start | bytes 4612
  1.2 24.4 %collective-permute-start.14 = (bf16[512,256]{1,0:T(8,128)(2,1)S(1)}, bf16[512,256]{1,0:T(8,128)(2,1)}, u32[]{:S(2)}, u32[]{:S(2)}) collective-permute-start(bf16[512,256]{1,0:T(8,128)(2,1)S(1)} %get-tuple-element.11), channel_id=1, source_target_pairs={{0,4},{4,8},{8,12},{1,5},{5,9},{9,13},{2,6},{6,10},{10,14},{3,7},{... | collective-permute-start | bytes 786440 | tf_op jit(solution)/shard_map/ppermute | solution.py:122
  6.9 19.5 %collective-permute-start.8 = (bf16[512,256]{1,0:T(8,128)(2,1)S(1)}, bf16[512,256]{1,0:T(8,128)(2,1)}, u32[]{:S(2)}, u32[]{:S(2)}) collective-permute-start(bf16[512,256]{1,0:T(8,128)(2,1)S(1)} %get-tuple-element.11), channel_id=1, source_target_pairs={{4,0},{8,4},{12,8},{5,1},{9,5},{13,9},{6,2},{10,6},{14,10},{7,3},{... | collective-permute-start | bytes 786440 | tf_op jit(solution)/shard_map/ppermute | solution.py:123
  9.7 17.9 %collective-permute-start.11 = (bf16[640,256]{1,0:T(8,128)(2,1)}, bf16[640,256]{1,0:T(8,128)(2,1)}, u32[]{:S(2)}, u32[]{:S(2)}) collective-permute-start(bf16[640,256]{1,0:T(8,128)(2,1)} %pad_maximum_fusion.1), channel_id=1, source_target_pairs={{0,4},{4,8},{8,12},{1,5},{5,9},{9,13},{2,6},{6,10},{10,14},{3,7},{... | collective-permute-start | bytes 983048 | tf_op jit(solution)/shard_map/ppermute | solution.py:122
  15.0 13.4 %collective-permute-start.4 = (bf16[640,256]{1,0:T(8,128)(2,1)}, bf16[640,256]{1,0:T(8,128)(2,1)}, u32[]{:S(2)}, u32[]{:S(2)}) collective-permute-start(bf16[640,256]{1,0:T(8,128)(2,1)} %pad_maximum_fusion.1), channel_id=1, source_target_pairs={{4,0},{8,4},{12,8},{5,1},{9,5},{13,9},{6,2},{10,6},{14,10},{7,3},{... | collective-permute-start | bytes 983048 | tf_op jit(solution)/shard_map/ppermute | solution.py:123
  16.3 8.7 %collective-permute-start.3 = (s32[2,384]{1,0:T(2,128)S(1)}, s32[2,384]{1,0:T(2,128)S(1)}, u32[]{:S(2)}, u32[]{:S(2)}) collective-permute-start(s32[2,384]{1,0:T(2,128)S(1)} %pad_add_fusion.1), channel_id=1, source_target_pairs={{0,16},{1,17},{2,18},{3,19},{4,20},{5,21},{6,22},{7,23},{8,24},{9,... | collective-permute-start | bytes 9224 | tf_op jit(solution)/shard_map/ppermute | solution.py:88
  18.0 3.4 %copy-start.1 = (bf16[384,2048]{1,0:T(8,128)(2,1)S(1)}, bf16[384,2048]{1,0:T(8,128)(2,1)}, u32[]{:S(2)}) copy-start(bf16[384,2048]{1,0:T(8,128)(2,1)} %param.6) | copy-start | bytes 4718596
  25.0 24.3 %collective-permute-start.7 = (bf16[384,1024]{1,0:T(8,128)(2,1)}, bf16[384,1024]{1,0:T(8,128)(2,1)S(1)}, u32[]{:S(2)}, u32[]{:S(2)}) collective-permute-start(bf16[384,1024]{1,0:T(8,128)(2,1)} %get-tuple-element.10), channel_id=1, source_target_pairs={{0,16},{1,17},{2,18},{3,19},{4,20},{5,21},{6,22},{7,23},{8,24},{9,... | collective-permute-start | bytes 2359304 | tf_op jit(solution)/shard_map/ppermute | solution.py:88
  25.6 6.2 %collective-permute-start.15 = (bf16[512,256]{1,0:T(8,128)(2,1)}, bf16[512,256]{1,0:T(8,128)(2,1)S(1)}, u32[]{:S(2)}, u32[]{:S(2)}) collective-permute-start(bf16[512,256]{1,0:T(8,128)(2,1)} %collective-permute-done.14), channel_id=1, source_target_pairs={{4,8},{8,12},{5,9},{9,13},{6,10},{10,14},{7,11},{11,15},{20,24},{2... | collective-permute-start | bytes 786440 | tf_op jit(solution)/shard_map/ppermute | solution.py:122
  26.3 11.2 %collective-permute-start.9 = (bf16[512,256]{1,0:T(8,128)(2,1)}, bf16[512,256]{1,0:T(8,128)(2,1)S(1)}, u32[]{:S(2)}, u32[]{:S(2)}) collective-permute-start(bf16[512,256]{1,0:T(8,128)(2,1)} %collective-permute-done.8), channel_id=1, source_target_pairs={{4,0},{8,4},{5,1},{9,5},{6,2},{10,6},{7,3},{11,7},{20,16},{24,20},... | collective-permute-start | bytes 786440 | tf_op jit(solution)/shard_map/ppermute | solution.py:123
  27.6 11.2 %collective-permute-start.12 = (bf16[640,256]{1,0:T(8,128)(2,1)}, bf16[640,256]{1,0:T(8,128)(2,1)S(1)}, u32[]{:S(2)}, u32[]{:S(2)}) collective-permute-start(bf16[640,256]{1,0:T(8,128)(2,1)} %collective-permute-done.11), channel_id=1, source_target_pairs={{4,8},{8,12},{5,9},{9,13},{6,10},{10,14},{7,11},{11,15},{20,24},{2... | collective-permute-start | bytes 983048 | tf_op jit(solution)/shard_map/ppermute | solution.py:122
  28.3 19.0 %collective-permute-start.5 = (bf16[640,256]{1,0:T(8,128)(2,1)}, bf16[640,256]{1,0:T(8,128)(2,1)S(1)}, u32[]{:S(2)}, u32[]{:S(2)}) collective-permute-start(bf16[640,256]{1,0:T(8,128)(2,1)} %collective-permute-done.4), channel_id=1, source_target_pairs={{4,0},{8,4},{5,1},{9,5},{6,2},{10,6},{7,3},{11,7},{20,16},{24,20},... | collective-permute-start | bytes 983048 | tf_op jit(solution)/shard_map/ppermute | solution.py:123
  31.8 25.6 %collective-permute-start.16 = (bf16[512,256]{1,0:T(8,128)(2,1)S(1)}, bf16[512,256]{1,0:T(8,128)(2,1)S(1)}, u32[]{:S(2)}, u32[]{:S(2)}) collective-permute-start(bf16[512,256]{1,0:T(8,128)(2,1)S(1)} %collective-permute-done.15), channel_id=1, source_target_pairs={{8,12},{9,13},{10,14},{11,15},{24,28},{25,29},{26,30},{27,31}} | collective-permute-start | bytes 786440 | tf_op jit(solution)/shard_map/ppermute | solution.py:122
  37.5 20.3 %collective-permute-start.10 = (bf16[512,256]{1,0:T(8,128)(2,1)S(1)}, bf16[512,256]{1,0:T(8,128)(2,1)S(1)}, u32[]{:S(2)}, u32[]{:S(2)}) collective-permute-start(bf16[512,256]{1,0:T(8,128)(2,1)S(1)} %collective-permute-done.9), channel_id=1, source_target_pairs={{4,0},{5,1},{6,2},{7,3},{20,16},{21,17},{22,18},{23,19}} | collective-permute-start | bytes 786440 | tf_op jit(solution)/shard_map/ppermute | solution.py:123
  38.8 19.5 %collective-permute-start.13 = (bf16[640,256]{1,0:T(8,128)(2,1)S(1)}, bf16[640,256]{1,0:T(8,128)(2,1)S(1)}, u32[]{:S(2)}, u32[]{:S(2)}) collective-permute-start(bf16[640,256]{1,0:T(8,128)(2,1)S(1)} %collective-permute-done.12), channel_id=1, source_target_pairs={{8,12},{9,13},{10,14},{11,15},{24,28},{25,29},{26,30},{27,31}} | collective-permute-start | bytes 983048 | tf_op jit(solution)/shard_map/ppermute | solution.py:122
  47.4 11.7 %collective-permute-start.6 = (bf16[640,256]{1,0:T(8,128)(2,1)S(1)}, bf16[640,256]{1,0:T(8,128)(2,1)S(1)}, u32[]{:S(2)}, u32[]{:S(2)}) collective-permute-start(bf16[640,256]{1,0:T(8,128)(2,1)S(1)} %collective-permute-done.5), channel_id=1, source_target_pairs={{4,0},{5,1},{6,2},{7,3},{20,16},{21,17},{22,18},{23,19}} | collective-permute-start | bytes 983048 | tf_op jit(solution)/shard_map/ppermute | solution.py:123
  58.3 0.7 copy-start.2
  59.0 0.7 copy-start.3
  59.8 12.4 %copy-start.4 = (bf16[256,128]{1,0:T(8,128)(2,1)S(1)}, bf16[256,128]{1,0:T(8,128)(2,1)}, u32[]{:S(2)}) copy-start(bf16[256,128]{1,0:T(8,128)(2,1)} %param.9) | copy-start | bytes 196612
  59.8 13.3 %copy-start.7 = (bf16[128,128]{1,0:T(8,128)(2,1)S(1)}, bf16[128,128]{1,0:T(8,128)(2,1)}, u32[]{:S(2)}) copy-start(bf16[128,128]{1,0:T(8,128)(2,1)} %get-tuple-element.24) | copy-start | bytes 98308
  59.8 13.3 %copy-start.8 = (bf16[128,128]{1,0:T(8,128)(2,1)S(1)}, bf16[128,128]{1,0:T(8,128)(2,1)}, u32[]{:S(2)}) copy-start(bf16[128,128]{1,0:T(8,128)(2,1)} %get-tuple-element.25) | copy-start | bytes 98308
  59.8 14.3 %copy-start.5 = (bf16[128,128]{1,0:T(8,128)(2,1)S(1)}, bf16[128,128]{1,0:T(8,128)(2,1)}, u32[]{:S(2)}) copy-start(bf16[128,128]{1,0:T(8,128)(2,1)} %get-tuple-element.22) | copy-start | bytes 98308
  59.8 14.3 %copy-start.6 = (bf16[128,128]{1,0:T(8,128)(2,1)S(1)}, bf16[128,128]{1,0:T(8,128)(2,1)}, u32[]{:S(2)}) copy-start(bf16[128,128]{1,0:T(8,128)(2,1)} %get-tuple-element.23) | copy-start | bytes 98308
  59.8 14.3 %copy-start.13 = (pred[384]{0:T(512)(128)(4,1)S(1)}, pred[384]{0:T(512)(128)(4,1)}, u32[]{:S(2)}) copy-start(pred[384]{0:T(512)(128)(4,1)} %get-tuple-element.45) | copy-start | bytes 1156
  59.9 5.3 %collective-permute-start.17 = (f32[16,384]{1,0:T(8,128)S(1)}, f32[16,384]{1,0:T(8,128)S(1)}, u32[]{:S(2)}, u32[]{:S(2)}) collective-permute-start(f32[16,384]{1,0:T(8,128)S(1)} %get-tuple-element.30), channel_id=1, source_target_pairs={{0,1},{1,2},{2,3},{3,0},{4,5},{5,6},{6,7},{7,4},{8,9},{9,10},{10,1... | collective-permute-start | bytes 73736 | tf_op jit(solution)/shard_map/ppermute | solution.py:88
  59.9 6.5 %collective-permute-start.18 = (f32[16,384]{1,0:T(8,128)S(1)}, f32[16,384]{1,0:T(8,128)S(1)}, u32[]{:S(2)}, u32[]{:S(2)}) collective-permute-start(f32[16,384]{1,0:T(8,128)S(1)} %get-tuple-element.30), channel_id=1, source_target_pairs={{0,2},{1,3},{2,0},{3,1},{4,6},{5,7},{6,4},{7,5},{8,10},{9,11},{10,... | collective-permute-start | bytes 73736 | tf_op jit(solution)/shard_map/ppermute | solution.py:88
  61.5 7.4 %collective-permute-start.19 = (f32[16,384]{1,0:T(8,128)S(1)}, f32[16,384]{1,0:T(8,128)S(1)}, u32[]{:S(2)}, u32[]{:S(2)}) collective-permute-start(f32[16,384]{1,0:T(8,128)S(1)} %get-tuple-element.30), channel_id=1, source_target_pairs={{0,3},{1,0},{2,1},{3,2},{4,7},{5,4},{6,5},{7,6},{8,11},{9,8},{10,9... | collective-permute-start | bytes 73736 | tf_op jit(solution)/shard_map/ppermute | solution.py:88
  62.9 11.6 %copy-start.12 = (pred[384]{0:T(512)(128)(4,1)S(1)}, pred[384]{0:T(512)(128)(4,1)}, u32[]{:S(2)}) copy-start(pred[384]{0:T(512)(128)(4,1)} %get-tuple-element.44) | copy-start | bytes 1156
  62.9 6.1 %collective-permute-start.20 = (f32[16,384]{1,0:T(8,128)S(1)}, f32[16,384]{1,0:T(8,128)S(1)}, u32[]{:S(2)}, u32[]{:S(2)}) collective-permute-start(f32[16,384]{1,0:T(8,128)S(1)} %get-tuple-element.31), channel_id=1, source_target_pairs={{0,16},{1,17},{2,18},{3,19},{4,20},{5,21},{6,22},{7,23},{8,24},{9,... | collective-permute-start | bytes 73736 | tf_op jit(solution)/shard_map/ppermute | solution.py:88
  64.4 6.1 %collective-permute-start.21 = (f32[16,384]{1,0:T(8,128)S(1)}, f32[16,384]{1,0:T(8,128)S(1)}, u32[]{:S(2)}, u32[]{:S(2)}) collective-permute-start(f32[16,384]{1,0:T(8,128)S(1)} %get-tuple-element.31), channel_id=1, source_target_pairs={{0,17},{1,18},{2,19},{3,16},{4,21},{5,22},{6,23},{7,20},{8,25},{9,... | collective-permute-start | bytes 73736 | tf_op jit(solution)/shard_map/ppermute | solution.py:88
  65.2 6.7 %collective-permute-start.22 = (f32[16,384]{1,0:T(8,128)S(1)}, f32[16,384]{1,0:T(8,128)S(1)}, u32[]{:S(2)}, u32[]{:S(2)}) collective-permute-start(f32[16,384]{1,0:T(8,128)S(1)} %get-tuple-element.31), channel_id=1, source_target_pairs={{0,18},{1,19},{2,16},{3,17},{4,22},{5,23},{6,20},{7,21},{8,26},{9,... | collective-permute-start | bytes 73736 | tf_op jit(solution)/shard_map/ppermute | solution.py:88
  66.4 5.5 %collective-permute-start.23 = (f32[16,384]{1,0:T(8,128)S(1)}, f32[16,384]{1,0:T(8,128)S(1)}, u32[]{:S(2)}, u32[]{:S(2)}) collective-permute-start(f32[16,384]{1,0:T(8,128)S(1)} %get-tuple-element.31), channel_id=1, source_target_pairs={{0,19},{1,16},{2,17},{3,18},{4,23},{5,20},{6,21},{7,22},{8,27},{9,... | collective-permute-start | bytes 73736 | tf_op jit(solution)/shard_map/ppermute | solution.py:88
  68.9 6.8 %collective-permute-start = (f32[384,128]{1,0:T(8,128)}, f32[384,128]{1,0:T(8,128)S(1)}, u32[]{:S(2)}, u32[]{:S(2)}) collective-permute-start(f32[384,128]{1,0:T(8,128)} %get-tuple-element.13), channel_id=1, source_target_pairs={{0,1},{1,2},{2,3},{3,0},{4,5},{5,6},{6,7},{7,4},{8,9},{9,10},{10,1... | collective-permute-start | bytes 589832 | tf_op jit(solution)/shard_map/ppermute | solution.py:88
  68.9 8.0 %collective-permute-start.1 = (f32[384,128]{1,0:T(8,128)}, f32[384,128]{1,0:T(8,128)S(1)}, u32[]{:S(2)}, u32[]{:S(2)}) collective-permute-start(f32[384,128]{1,0:T(8,128)} %get-tuple-element.15), channel_id=1, source_target_pairs={{0,2},{1,3},{2,0},{3,1},{4,6},{5,7},{6,4},{7,5},{8,10},{9,11},{10,... | collective-permute-start | bytes 589832 | tf_op jit(solution)/shard_map/ppermute | solution.py:88
  70.5 9.2 %collective-permute-start.2 = (f32[384,128]{1,0:T(8,128)}, f32[384,128]{1,0:T(8,128)S(1)}, u32[]{:S(2)}, u32[]{:S(2)}) collective-permute-start(f32[384,128]{1,0:T(8,128)} %get-tuple-element.14), channel_id=1, source_target_pairs={{0,3},{1,0},{2,1},{3,2},{4,7},{5,4},{6,5},{7,6},{8,11},{9,8},{10,9... | collective-permute-start | bytes 589832 | tf_op jit(solution)/shard_map/ppermute | solution.py:88
  73.1 2.1 %copy-start.11 = (pred[384]{0:T(512)(128)(4,1)S(1)}, pred[384]{0:T(512)(128)(4,1)}, u32[]{:S(2)}) copy-start(pred[384]{0:T(512)(128)(4,1)} %get-tuple-element.41) | copy-start | bytes 1156

commit v2 on v0

--- a/solution.py
+++ b/solution.py
@@ -1,6 +1,10 @@
+import functools
+
 import jax
 import jax.numpy as jnp
 from jax import lax
+from jax.experimental import pallas as pl
+from jax.experimental.pallas import tpu as pltpu
 from jax.sharding import PartitionSpec as P
 
 ADAPTER_RANK = 16
@@ -9,7 +13,7 @@
 ADAPTER_SCALE = 2.0
 
 
-def local(
+def dispatch(
     tokens,
     base_key_weight,
     stacked_down_weight,
@@ -47,7 +51,6 @@
     )
     chosen = slots_in[:, :, None] == jnp.arange(local_adapters, dtype=jnp.int32)[None, None, :]
     partial_low = jnp.sum(jnp.where(chosen[:, :, :, None], key_projection_output, 0.0), axis=2)
-    partial_low, slots_in = (partial_low, slots_in)
     shrunk = lax.psum(partial_low, "mp")
     shrunk_bf = shrunk.astype(jnp.bfloat16)
     returned = lax.all_to_all(shrunk_bf, "adapter", split_axis=0, concat_axis=0, tiled=True)
@@ -71,6 +74,233 @@
     )
 
 
+AXES = ("groups", "adapter", "mp")
+ID_ROWS = 16
+
+
+def mesh_shift(x, group_step, mp_step):
+    groups, owners, shares = (lax.axis_size(name) for name in AXES)
+
+    def number(g, a, m):
+        return (g * owners + a) * shares + m
+
+    pairs = [
+        (number(g, a, m), number((g + group_step) % groups, a, (m + mp_step) % shares))
+        for g in range(groups)
+        for a in range(owners)
+        for m in range(shares)
+    ]
+    return lax.ppermute(x, AXES, pairs)
+
+
+def whole(body, outs, *operands, **params):
+    spec = pl.BlockSpec(memory_space=pltpu.VMEM)
+    return pl.pallas_call(
+        body,
+        out_shape=outs,
+        in_specs=[spec] * len(operands),
+        out_specs=jax.tree.map(lambda _: spec, outs),
+        compiler_params=pltpu.CompilerParams(vmem_limit_bytes=40 * 1024 * 1024),
+        **params,
+    )(*operands)
+
+
+def base_body(keys, tokens, weights, out):
+    wide = jnp.dot(tokens[...], weights[...], preferred_element_type=jnp.float32)
+    for k in range(out.shape[0]):
+        out[k] = wide[:, k * keys : (k + 1) * keys]
+
+
+def shrink_body(distances, cuts, rows, first, last, *refs):
+    groups, shares = lax.axis_size("groups"), lax.axis_size("mp")
+    a, g = lax.axis_index("adapter"), lax.axis_index("groups")
+    token_refs, rest = refs[:groups], refs[groups:]
+    picked_in = None
+    if not first:
+        picked_in, rest = rest[0], rest[1:]
+    blocks, out = rest[:-1], rest[-1]
+    columns = blocks[0].shape[1]
+    eye = (
+        lax.broadcasted_iota(jnp.int32, (ID_ROWS, ID_ROWS), 0)
+        == lax.broadcasted_iota(jnp.int32, (ID_ROWS, ID_ROWS), 1)
+    ).astype(jnp.bfloat16)
+    for part, tokens in enumerate(token_refs):
+        ids = lax.dot_general(
+            tokens[rows : rows + ID_ROWS, :rows],
+            eye,
+            (((0,), (0,)), ((), ())),
+            preferred_element_type=jnp.float32,
+        )
+        owner, slot = ids[:, 0:1], ids[:, 1:2]
+        picked = jnp.zeros((rows, columns), jnp.float32) if first else picked_in[part]
+        for i, distance in enumerate(distances):
+            wide = None
+            for p, (start, stop) in enumerate(cuts):
+                term = jnp.dot(
+                    tokens[:rows, start:stop],
+                    blocks[i * len(cuts) + p][: stop - start],
+                    preferred_element_type=jnp.float32,
+                )
+                wide = term if wide is None else wide + term
+            picked = jnp.where(owner == (a + distance).astype(jnp.float32), wide, picked)
+        if not last:
+            out[part] = picked
+            continue
+        column = lax.broadcasted_iota(jnp.int32, (rows, columns), 1)
+        adapter = (column // ADAPTER_RANK).astype(jnp.float32)
+        picked = jnp.where(adapter == slot, picked, 0.0)
+        lanes = 128
+        folded = picked[:, :lanes]
+        for k in range(1, columns // lanes):
+            folded = folded + picked[:, k * lanes : (k + 1) * lanes]
+        turned = folded.T
+        low = turned[:ADAPTER_RANK]
+        for k in range(1, lanes // ADAPTER_RANK):
+            low = low + turned[k * ADAPTER_RANK : (k + 1) * ADAPTER_RANK]
+        target = lax.rem(g + part, groups) * shares
+        for m in range(shares):
+            out[target + m] = low
+
+
+def ups_body(distances, up_start, own, *refs):
+    a, owners = lax.axis_index("adapter"), lax.axis_size("adapter")
+    blocks, out = refs[:-1], refs[-1]
+    rows, keys = own.shape
+    out[pl.ds(pl.multiple_of(a * rows, rows), rows), :] = own[...]
+    for distance, block in zip(distances, blocks):
+        number = a + distance
+
+        @pl.when((number >= 0) & (number < owners))
+        def _():
+            taken = block[up_start:, :]
+            count = taken.shape[1] // keys
+            size = rows // count
+            for k in range(count):
+                start = pl.multiple_of(number * rows + k * size, size)
+                out[pl.ds(start, size), :] = taken[:, k * keys : (k + 1) * keys]
+
+
+def finish_body(parts, bases, ids, ups, out):
+    shrunk = parts[0]
+    for k in range(1, parts.shape[0]):
+        shrunk = shrunk + parts[k]
+    base = bases[0]
+    for k in range(1, bases.shape[0]):
+        base = base + bases[k]
+    rank_total = ups.shape[0]
+    column = lax.broadcasted_iota(jnp.int32, (ADAPTER_RANK, rank_total), 1)
+    row = lax.broadcasted_iota(jnp.int32, (ADAPTER_RANK, rank_total), 0)
+    repeat = (lax.rem(column, ADAPTER_RANK) == row).astype(jnp.bfloat16)
+    spread = lax.dot_general(
+        shrunk.astype(jnp.bfloat16),
+        repeat,
+        (((0,), (0,)), ((), ())),
+        preferred_element_type=jnp.float32,
+    )
+    adapter = lax.broadcasted_iota(jnp.int32, spread.shape, 1) // ADAPTER_RANK
+    spread = jnp.where(adapter == ids[...], spread, 0.0).astype(jnp.bfloat16)
+    updates = jnp.dot(spread, ups[...], preferred_element_type=jnp.float32)
+    updates = updates.astype(jnp.bfloat16).astype(jnp.float32)
+    out[...] = (base + ADAPTER_SCALE * updates).astype(jnp.bfloat16)
+
+
+def gather(
+    tokens,
+    base_key_weight,
+    stacked_down_weight,
+    stacked_up_weight,
+    request_adapter_owner,
+    request_adapter_slot,
+):
+    rows, features = tokens.shape
+    groups, owner_count, shares = (lax.axis_size(name) for name in AXES)
+    g = lax.axis_index("groups")
+    columns = stacked_down_weight.shape[1]
+    keys = stacked_up_weight.shape[1]
+    local_adapters = columns // ADAPTER_RANK
+    part = features // groups
+
+    half = columns // keys
+    up_rows = columns // half
+    up_wide = jnp.concatenate(
+        [stacked_up_weight[i * up_rows : (i + 1) * up_rows] for i in range(half)], axis=1
+    )
+    down_own = lax.dynamic_slice(stacked_down_weight, (g * part, 0), (part, columns))
+    cut = part // 2
+    cuts = ((0, cut), (cut, part))
+    pieces = [down_own[:cut], jnp.concatenate([down_own[cut:], up_wide], axis=0)]
+
+    steps = []
+    forward, backward = pieces, pieces
+    for d in range(1, owner_count):
+        ahead = [(i, i + 1) for i in range(d - 1, owner_count - 1)]
+        back = [(i + 1, i) for i in range(0, owner_count - d)]
+        nexts = [
+            (lax.ppermute(f, "adapter", ahead), lax.ppermute(b, "adapter", back))
+            for f, b in zip(forward, backward)
+        ]
+        forward, backward = [x[0] for x in nexts], [x[1] for x in nexts]
+        steps.append((forward, backward))
+
+    id_rows = jnp.concatenate(
+        [request_adapter_owner.reshape(1, rows), request_adapter_slot.reshape(1, rows)], axis=0
+    ).astype(jnp.bfloat16)
+    id_rows = jnp.pad(id_rows, ((0, ID_ROWS - 2), (0, part - rows)))
+    token_parts = []
+    for step in range(groups):
+        wanted = (g + step) % groups
+        taken = lax.dynamic_slice(tokens, (0, wanted * part), (rows, part))
+        taken = jnp.concatenate([taken, id_rows], axis=0)
+        token_parts.append(mesh_shift(taken, step, 0) if step else taken)
+
+    bases = whole(
+        functools.partial(base_body, keys),
+        jax.ShapeDtypeStruct((shares, rows, keys), jnp.float32),
+        tokens,
+        base_key_weight,
+    )
+    bases = lax.all_to_all(bases, "mp", 0, 0, tiled=True)
+
+    picked_shape = jax.ShapeDtypeStruct((groups, rows, columns), jnp.float32)
+    low_shape = jax.ShapeDtypeStruct((groups * shares, ADAPTER_RANK, rows), jnp.float32)
+    picked = whole(
+        functools.partial(shrink_body, (0,), cuts, rows, True, False),
+        picked_shape,
+        *token_parts,
+        *pieces,
+    )
+    for d, (forward, backward) in enumerate(steps, 1):
+        last = d == owner_count - 1
+        picked = whole(
+            functools.partial(shrink_body, (-d, d), cuts, rows, False, last),
+            low_shape if last else picked_shape,
+            *token_parts,
+            picked,
+            *forward,
+            *backward,
+        )
+    parts = lax.all_to_all(picked, ("groups", "mp"), 0, 0, tiled=True)
+
+    distances = [d for step in range(1, owner_count) for d in (-step, step)]
+    ups = whole(
+        functools.partial(ups_body, distances, part - cut),
+        jax.ShapeDtypeStruct((owner_count * columns, keys), jnp.bfloat16),
+        stacked_up_weight,
+        *[block[-1] for step in steps for block in step],
+    )
+    ids = request_adapter_owner * local_adapters + request_adapter_slot.reshape(rows, 1)
+    return whole(
+        finish_body, jax.ShapeDtypeStruct((rows, keys), jnp.bfloat16), parts, bases, ids, ups
+    )
+
+
+def local(*args):
+    rows, columns = args[0].shape[0], args[2].shape[1]
+    capacity = max(2, 3 * rows // (2 * lax.axis_size("adapter")))
+    travels = columns <= lax.axis_size("groups") * capacity
+    return (gather if travels else dispatch)(*args)
+
+
 def solution(mesh):
     placed = (
         P(("groups", "adapter"), "mp"),

time: 131 us -> 73.9 us (0.56)
  waiting for transfers between devices: 49.7 us -> 22.5 us
  blocking collectives: 25.7 us -> 0 us
  starting transfers between devices: 14.5 us -> 29.7 us
  between operations: 13.5 us -> 0.35 us
  Pallas kernels: 0 us -> 11.5 us
  matrix products: 8.59 us -> 0 us
  local copies, waits for them, and re-layouts: 14.4 us -> 7.27 us
  other arithmetic: 4.22 us -> 1.84 us
    all_to_all x3 -> x2, waiting for transfers between devices: 49.7 us -> 2.84 us  [the longest x1 2.83 us: gather(): parts = lax.all_to_all(picked, ('groups', 'mp'), 0, 0, tiled=True)]
    ppermute x0 -> x13, starting transfers between devices: none -> 22.8 us  [the longest x6 13.6 us: gather(): lax.ppermute(f, 'adapter', ahead)]
    ppermute x0 -> x13, waiting for transfers between devices: none -> 19.7 us  [the longest x6 19.7 us: gather(): lax.ppermute(b, 'adapter', back)]
    all_gather x1 -> x0, blocking collectives: 14.4 us -> none  [local(): lax.all_gather(stacked_up_weight, 'adapter', axis=0, tiled=True)]
    pallas_call x0 -> x7, Pallas kernels: none -> 11.5 us  [whole(): pl.pallas_call(body, out_shape=outs, in_specs=[spec] * len(operands), out...]
    psum x1 -> x0, blocking collectives: 11.3 us -> none  [local(): shrunk = lax.psum(partial_low, 'mp')]
    dot_general x3 -> x0, matrix products: 8.59 us -> none  [the longest x1 3.68 us: local(): lax.dot_general(base_key_weight, tokens, (((0,), (1,)), ((), ())), prefer...]
    scatter x2 -> x0, local copies, waits for them, and re-layouts: 8.47 us -> none  [the longest x1 5.39 us: local(): jnp.zeros((owner_count * capacity, feature_share), jnp.bfloat16).at[places]]
  transfers between devices with their start and end apart: 4 -> 15, of which waited for: 2 -> 4; matrix products, arithmetic and copies ran while one was open for 14% -> 2% of each run, Pallas kernels for 0% -> 14%
where the time goes in v2:
time: 73.9 us; the launch traced here: 73.2 us
  starting transfers between devices  29.7 us (40%)
  waiting for transfers between devices  22.5 us (30%)
  Pallas kernels  11.5 us (16%)
  local copies, waits for them, and re-layouts  7.27 us (10%)
  other arithmetic  1.84 us (2%)
    ppermute x6, waiting for transfers between devices, gather(): lax.ppermute(b, 'adapter', back)  19.7 us
    ppermute x6, starting transfers between devices, gather(): lax.ppermute(f, 'adapter', ahead)  13.6 us
    pallas_call x7, Pallas kernels, whole(): pl.pallas_call(body, out_shape=outs, in_specs=[spec] * len(operands), out...  11.5 us
    ppermute x6, starting transfers between devices, gather(): lax.ppermute(b, 'adapter', back)  7.71 us
    unnamed x20, local copies, waits for them, and re-layouts  4.32 us
    all_to_all x1, starting transfers between devices, gather(): bases = lax.all_to_all(bases, 'mp', 0, 0, tiled=True)  3.49 us
    all_to_all x1, starting transfers between devices, gather(): parts = lax.all_to_all(picked, ('groups', 'mp'), 0, 0, tiled=True)  3.39 us
    all_to_all x1, waiting for transfers between devices, gather(): parts = lax.all_to_all(picked, ('groups', 'mp'), 0, 0, tiled=True)  2.83 us
  transfers between devices with their start and end apart: 15, of which 4 were waited for; matrix products, arithmetic and copies ran while one was open for 2% of the time, Pallas kernels for 14%

profile of v2, /device:TPU:0, one launch (start us, length us, event | category | flops | bytes accessed | tf_op | source)
XLA Modules:
  0.0 73.2 jit_solution(6765525596412741771)
XLA Ops:
  0.0 0.9 %fusion.6 = (bf16[128,128]{1,0:T(8,128)(2,1)S(1)}, bf16[128,128]{1,0:T(8,128)(2,1)S(1)}) fusion(bf16[256,128]{1,0:T(8,128)(2,1)} %own.1), kind=kLoop, calls=%fused_computation.17 | loop fusion | bytes 131072 | tf_op jit(solution)/shard_map/slice | solution.py:226
  0.9 1.8 %constant_dynamic-slice_fusion.1 = (bf16[512,256]{1,0:T(8,128)(2,1)S(1)}, bf16[512,256]{1,0:T(8,128)(2,1)}) fusion(bf16[2048,256]{1,0:T(8,128)(2,1)} %param.8, s32[]{:T(128)S(6)} %add.31, s32[]{:T(128)S(6)} %select_n.24), kind=kLoop, calls=%fused_computation.14 | loop fusion | bytes 1048584 | tf_op jit(solution)/shard_map/slice | solution.py:231
  2.7 0.8 %maximum_maximum_fusion.refs_3_ = bf16[640,256]{1,0:T(8,128)(2,1)} fusion(bf16[128,128]{1,0:T(8,128)(2,1)S(1)} %get-tuple-element.10, bf16[128,128]{1,0:T(8,128)(2,1)S(1)} %get-tuple-element.9, bf16[512,256]{1,0:T(8,128)(2,1)S(1)} %get-tuple-element.7), kind=kLoop, calls=%fused_computation.2 | loop fusion | flops 983040 | bytes 655360 | tf_op jit(solution)/shard_map/concatenate | solution.py:231
  3.4 4.9 %collective-permute-start.2 = (bf16[640,256]{1,0:T(8,128)(2,1)}, bf16[640,256]{1,0:T(8,128)(2,1)S(1)}, u32[]{:S(2)}, u32[]{:S(2)}) collective-permute-start(bf16[640,256]{1,0:T(8,128)(2,1)} %maximum_maximum_fusion.refs_3_), channel_id=1, source_target_pairs={{0,4},{4,8},{8,12},{1,5},{5,9},{9,13},{2,6},{6,10},{10,14},{3,7},{... | collective-permute-start | bytes 983048 | tf_op jit(solution)/shard_map/ppermute | solution.py:239
  8.4 1.3 %collective-permute-start.4 = (bf16[640,256]{1,0:T(8,128)(2,1)}, bf16[640,256]{1,0:T(8,128)(2,1)}, u32[]{:S(2)}, u32[]{:S(2)}) collective-permute-start(bf16[640,256]{1,0:T(8,128)(2,1)} %maximum_maximum_fusion.refs_3_), channel_id=1, source_target_pairs={{4,0},{8,4},{12,8},{5,1},{9,5},{13,9},{6,2},{10,6},{14,10},{7,3},{... | collective-permute-start | bytes 983048 | tf_op jit(solution)/shard_map/ppermute | solution.py:239
  9.8 0.1 constant_dynamic-slice_fusion.2
  9.9 0.0 copy-start.2
  10.0 1.1 %pad_maximum_fusion = (bf16[400,1024]{1,0:T(8,128)(2,1)}, bf16[400,1024]{1,0:T(8,128)(2,1)S(1)}) fusion(bf16[16,1024]{1,0:T(8,128)(2,1)S(1)} %fusion.5, bf16[384,1024]{1,0:T(8,128)(2,1)S(1)} %get-tuple-element.5, bf16[384,1024]{1,0:T(8,128)(2,1)S(1)} %get-tuple-element.6), kind=kLoop, calls=%fused_computation | loop fusion | flops 2867200 | bytes 3244032 | tf_op jit(solution)/shard_map/concatenate | solution.py:253
  11.0 1.5 %collective-permute-start = (bf16[400,1024]{1,0:T(8,128)(2,1)}, bf16[400,1024]{1,0:T(8,128)(2,1)S(1)}, u32[]{:S(2)}, u32[]{:S(2)}) collective-permute-start(bf16[400,1024]{1,0:T(8,128)(2,1)} %get-tuple-element.11), channel_id=1, source_target_pairs={{0,16},{1,17},{2,18},{3,19},{4,20},{5,21},{6,22},{7,23},{8,24},{9,... | collective-permute-start | bytes 2457608 | tf_op jit(solution)/shard_map/ppermute | solution.py:93
  12.5 5.2 %collective-permute-start.1 = (bf16[512,256]{1,0:T(8,128)(2,1)}, bf16[512,256]{1,0:T(8,128)(2,1)}, u32[]{:S(2)}, u32[]{:S(2)}) collective-permute-start(bf16[512,256]{1,0:T(8,128)(2,1)} %get-tuple-element.8.refs_2_), channel_id=1, source_target_pairs={{0,4},{4,8},{8,12},{1,5},{5,9},{9,13},{2,6},{6,10},{10,14},{3,7},{... | collective-permute-start | bytes 786440 | tf_op jit(solution)/shard_map/ppermute | solution.py:239
  17.8 1.3 %collective-permute-start.3 = (bf16[512,256]{1,0:T(8,128)(2,1)}, bf16[512,256]{1,0:T(8,128)(2,1)}, u32[]{:S(2)}, u32[]{:S(2)}) collective-permute-start(bf16[512,256]{1,0:T(8,128)(2,1)} %get-tuple-element.8.refs_2_), channel_id=1, source_target_pairs={{4,0},{8,4},{12,8},{5,1},{9,5},{13,9},{6,2},{10,6},{14,10},{7,3},{... | collective-permute-start | bytes 786440 | tf_op jit(solution)/shard_map/ppermute | solution.py:239
  19.1 0.0 collective-permute-done.2.refs_4_.refs_0_
  19.1 1.4 %collective-permute-start.6 = (bf16[640,256]{1,0:T(8,128)(2,1)S(1)}, bf16[640,256]{1,0:T(8,128)(2,1)}, u32[]{:S(2)}, u32[]{:S(2)}) collective-permute-start(bf16[640,256]{1,0:T(8,128)(2,1)S(1)} %collective-permute-done.2.refs_4_.refs_0_), channel_id=1, source_target_pairs={{4,8},{8,12},{5,9},{9,13},{6,10},{10,14},{7,11},{11,15},{20,24},{2... | collective-permute-start | bytes 983048 | tf_op jit(solution)/shard_map/ppermute | solution.py:239
  20.5 0.0 collective-permute-done.4.refs_6_.refs_1_
  20.5 1.3 %collective-permute-start.8 = (bf16[640,256]{1,0:T(8,128)(2,1)}, bf16[640,256]{1,0:T(8,128)(2,1)}, u32[]{:S(2)}, u32[]{:S(2)}) collective-permute-start(bf16[640,256]{1,0:T(8,128)(2,1)} %collective-permute-done.4.refs_6_.refs_1_), channel_id=1, source_target_pairs={{4,0},{8,4},{5,1},{9,5},{6,2},{10,6},{7,3},{11,7},{20,16},{24,20},... | collective-permute-start | bytes 983048 | tf_op jit(solution)/shard_map/ppermute | solution.py:239
  21.8 1.0 %shard_map.68 = f32[4,384,128]{2,1,0:T(8,128)S(1)} custom-call(bf16[384,2048]{1,0:T(8,128)(2,1)S(1)} %copy-done, bf16[2048,512]{1,0:T(8,128)(2,1)S(1)} %copy-done.2), custom_call_target="tpu_custom_call" | custom-call | tf_op jit(solution)/shard_map/pallas_call | solution.py:98
  22.8 0.9 %copy-done.1 = f32[4,384,128]{2,1,0:T(8,128)} copy-done((f32[4,384,128]{2,1,0:T(8,128)}, f32[4,384,128]{2,1,0:T(8,128)S(1)}, u32[]{:S(2)}) %copy-start.1) | copy-done | bytes 786456
  23.7 3.5 %all-to-all-start.1 = ((f32[4,384,128]{2,1,0:T(8,128)}), f32[4,384,128]{2,1,0:T(8,128)S(1)}, u32[]{:S(2)}, u32[]{:S(2)}) async-start(f32[4,384,128]{2,1,0:T(8,128)} %copy-done.1), calls=%async_computation.1 | async-start | bytes 1572864 | tf_op jit(solution)/shard_map/all_to_all | solution.py:262
  27.2 0.0 collective-permute-done.1.refs_3_
  27.2 0.7 collective-permute-start.5
  27.9 0.0 collective-permute-done.3.refs_5_
  27.9 1.3 %collective-permute-start.7 = (bf16[512,256]{1,0:T(8,128)(2,1)}, bf16[512,256]{1,0:T(8,128)(2,1)S(1)}, u32[]{:S(2)}, u32[]{:S(2)}) collective-permute-start(bf16[512,256]{1,0:T(8,128)(2,1)} %collective-permute-done.3.refs_5_), channel_id=1, source_target_pairs={{4,0},{8,4},{5,1},{9,5},{6,2},{10,6},{7,3},{11,7},{20,16},{24,20},... | collective-permute-start | bytes 786440 | tf_op jit(solution)/shard_map/ppermute | solution.py:239
  29.2 0.0 collective-permute-done.6.refs_4_.refs_2_
  29.2 0.7 collective-permute-start.10
  29.9 4.1 %collective-permute-done.8.refs_6_.refs_3_ = bf16[640,256]{1,0:T(8,128)(2,1)} collective-permute-done((bf16[640,256]{1,0:T(8,128)(2,1)}, bf16[640,256]{1,0:T(8,128)(2,1)}, u32[]{:S(2)}, u32[]{:S(2)}) %collective-permute-start.8) | collective-permute-done | bytes 327712 | tf_op jit(solution)/shard_map/ppermute | solution.py:239
  34.0 1.3 %collective-permute-start.12 = (bf16[640,256]{1,0:T(8,128)(2,1)}, bf16[640,256]{1,0:T(8,128)(2,1)S(1)}, u32[]{:S(2)}, u32[]{:S(2)}) collective-permute-start(bf16[640,256]{1,0:T(8,128)(2,1)} %collective-permute-done.8.refs_6_.refs_3_), channel_id=1, source_target_pairs={{4,0},{5,1},{6,2},{7,3},{20,16},{21,17},{22,18},{23,19}} | collective-permute-start | bytes 983048 | tf_op jit(solution)/shard_map/ppermute | solution.py:239
  35.3 0.0 collective-permute-done.5.refs_3_
  35.3 0.7 collective-permute-start.9
  36.0 10.7 %collective-permute-done.7.refs_5_ = bf16[512,256]{1,0:T(8,128)(2,1)S(1)} collective-permute-done((bf16[512,256]{1,0:T(8,128)(2,1)}, bf16[512,256]{1,0:T(8,128)(2,1)S(1)}, u32[]{:S(2)}, u32[]{:S(2)}) %collective-permute-start.7) | collective-permute-done | bytes 262176 | tf_op jit(solution)/shard_map/ppermute | solution.py:239
  46.7 1.3 %collective-permute-start.11 = (bf16[512,256]{1,0:T(8,128)(2,1)S(1)}, bf16[512,256]{1,0:T(8,128)(2,1)S(1)}, u32[]{:S(2)}, u32[]{:S(2)}) collective-permute-start(bf16[512,256]{1,0:T(8,128)(2,1)S(1)} %collective-permute-done.7.refs_5_), channel_id=1, source_target_pairs={{4,0},{5,1},{6,2},{7,3},{20,16},{21,17},{22,18},{23,19}} | collective-permute-start | bytes 786440 | tf_op jit(solution)/shard_map/ppermute | solution.py:239
  48.0 0.0 collective-permute-done.refs_1_
  48.0 1.7 %shard_map.64.refs_2_ = f32[2,384,256]{2,1,0:T(8,128)S(1)} custom-call(bf16[400,1024]{1,0:T(8,128)(2,1)S(1)} %get-tuple-element.12.refs_0_, bf16[400,1024]{1,0:T(8,128)(2,1)S(1)} %collective-permute-done.refs_1_, bf16[512,256]{1,0:T(8,128)(2,1)} %get-tuple-element.8.refs_2_, bf16[640,256]{1,0:T(8,128)(2,1)} %maximum_maximum_fusion.refs_3_), custom_call_target="tpu_custom_call" | custom-call | tf_op jit(solution)/shard_map/pallas_call | solution.py:98
  49.7 2.2 %shard_map.65.refs_2_ = f32[2,384,256]{2,1,0:T(8,128)S(1)} custom-call(bf16[400,1024]{1,0:T(8,128)(2,1)S(1)} %get-tuple-element.12.refs_0_, bf16[400,1024]{1,0:T(8,128)(2,1)S(1)} %collective-permute-done.refs_1_, f32[2,384,256]{2,1,0:T(8,128)S(1)} %shard_map.64.refs_2_, bf16[512,256]{1,0:T(8,128)(2,1)} %collective-permute-done.1.refs_3_, ...), custom_call_target="tpu_custom_call" | custom-call | tf_op jit(solution)/shard_map/pallas_call | solution.py:98
  51.9 2.1 %shard_map.66.refs_2_ = f32[2,384,256]{2,1,0:T(8,128)S(1)} custom-call(bf16[400,1024]{1,0:T(8,128)(2,1)S(1)} %get-tuple-element.12.refs_0_, bf16[400,1024]{1,0:T(8,128)(2,1)S(1)} %collective-permute-done.refs_1_, f32[2,384,256]{2,1,0:T(8,128)S(1)} %shard_map.65.refs_2_, bf16[512,256]{1,0:T(8,128)(2,1)S(1)} %collective-permute-done.5.refs_3_, ...), custom_call_target="tpu_custom_call" | custom-call | tf_op jit(solution)/shard_map/pallas_call | solution.py:98
  54.1 0.0 copy-start.7
  54.1 4.8 %collective-permute-done.11.refs_5_ = bf16[512,256]{1,0:T(8,128)(2,1)S(1)} collective-permute-done((bf16[512,256]{1,0:T(8,128)(2,1)S(1)}, bf16[512,256]{1,0:T(8,128)(2,1)S(1)}, u32[]{:S(2)}, u32[]{:S(2)}) %collective-permute-start.11) | collective-permute-done | bytes 262176 | tf_op jit(solution)/shard_map/ppermute | solution.py:239
  58.9 0.0 collective-permute-done.10.refs_4_
  58.9 1.9 %shard_map.67 = f32[8,16,384]{2,1,0:T(8,128)} custom-call(bf16[400,1024]{1,0:T(8,128)(2,1)S(1)} %get-tuple-element.12.refs_0_, bf16[400,1024]{1,0:T(8,128)(2,1)S(1)} %collective-permute-done.refs_1_, f32[2,384,256]{2,1,0:T(8,128)S(1)} %shard_map.66.refs_2_, bf16[512,256]{1,0:T(8,128)(2,1)S(1)} %collective-permute-done.9.refs_3_, ...), custom_call_target="tpu_custom_call" | custom-call | tf_op jit(solution)/shard_map/pallas_call | solution.py:98
  60.8 0.7 copy-done.3
  61.5 0.7 copy-done.5
  62.2 0.0 all-to-all-done.1.bases
  62.2 3.4 %all-to-all-start = ((f32[8,16,384]{2,1,0:T(8,128)}), f32[8,16,384]{2,1,0:T(8,128)S(1)}, u32[]{:S(2)}, u32[]{:S(2)}) async-start(f32[8,16,384]{2,1,0:T(8,128)} %shard_map.67), calls=%async_computation | async-start | bytes 393216 | tf_op jit(solution)/shard_map/all_to_all | solution.py:282
  65.6 0.1 copy.12.ids
  65.8 1.0 %copy-done.4 = bf16[640,256]{1,0:T(8,128)(2,1)S(1)} copy-done((bf16[640,256]{1,0:T(8,128)(2,1)S(1)}, bf16[640,256]{1,0:T(8,128)(2,1)}, u32[]{:S(2)}) %copy-start.4) | copy-done | bytes 327704
  66.8 1.0 %copy-done.6 = bf16[640,256]{1,0:T(8,128)(2,1)S(1)} copy-done((bf16[640,256]{1,0:T(8,128)(2,1)S(1)}, bf16[640,256]{1,0:T(8,128)(2,1)}, u32[]{:S(2)}) %copy-start.6) | copy-done | bytes 327704
  67.7 1.2 %shard_map.69.ups = bf16[1024,128]{1,0:T(8,128)(2,1)S(1)} custom-call(bf16[256,128]{1,0:T(8,128)(2,1)S(1)} %copy-done.7, bf16[640,256]{1,0:T(8,128)(2,1)S(1)} %collective-permute-done.2.refs_4_.refs_0_, bf16[640,256]{1,0:T(8,128)(2,1)} %collective-permute-done.4.refs_6_.refs_1_, bf16[640,256]{1,0:T(8,128)(2,1)} %collective-permute-done.6.refs_4_.refs_2_, ...), custom_call_target="tpu_custom_call" | custom-call | tf_op jit(solution)/shard_map/pallas_call | solution.py:98
  69.0 2.8 %all-to-all-done.parts = f32[8,16,384]{2,1,0:T(8,128)S(1)} async-done(((f32[8,16,384]{2,1,0:T(8,128)}), f32[8,16,384]{2,1,0:T(8,128)S(1)}, u32[]{:S(2)}, u32[]{:S(2)}) %all-to-all-start) | async-done | bytes 196640 | tf_op jit(solution)/shard_map/all_to_all | solution.py:282
  71.8 1.4 %shard_map.70 = bf16[384,128]{1,0:T(8,128)(2,1)} custom-call(f32[8,16,384]{2,1,0:T(8,128)S(1)} %all-to-all-done.parts, f32[4,384,128]{2,1,0:T(8,128)S(1)} %all-to-all-done.1.bases, s32[384,1]{1,0:T(8,128)S(1)} %copy.12.ids, bf16[1024,128]{1,0:T(8,128)(2,1)S(1)} %shard_map.69.ups), custom_call_target="tpu_custom_call" | custom-call | tf_op jit(solution)/shard_map/pallas_call | solution.py:98
  (19 shorter events, 0.1 us)
Async XLA Ops:
  0.0 9.7 %copy-start.8 = (s32[384]{0:T(512)S(1)}, s32[384]{0:T(512)}, u32[]{:S(2)}) copy-start(s32[384]{0:T(512)} %param.11) | copy-start | bytes 4612
  0.0 9.7 %copy-start.9 = (s32[384,1]{0,1:T(1,128)S(1)}, s32[384,1]{0,1:T(1,128)}, u32[]{:S(2)}) copy-start(s32[384,1]{0,1:T(1,128)} %param.10) | copy-start | bytes 4612
  0.0 9.8 %copy-start = (bf16[384,2048]{1,0:T(8,128)(2,1)S(1)}, bf16[384,2048]{1,0:T(8,128)(2,1)}, u32[]{:S(2)}) copy-start(bf16[384,2048]{1,0:T(8,128)(2,1)} %tokens.1) | copy-start | bytes 4718596
  3.4 15.6 %collective-permute-start.2 = (bf16[640,256]{1,0:T(8,128)(2,1)}, bf16[640,256]{1,0:T(8,128)(2,1)S(1)}, u32[]{:S(2)}, u32[]{:S(2)}) collective-permute-start(bf16[640,256]{1,0:T(8,128)(2,1)} %maximum_maximum_fusion.refs_3_), channel_id=1, source_target_pairs={{0,4},{4,8},{8,12},{1,5},{5,9},{9,13},{2,6},{6,10},{10,14},{3,7},{... | collective-permute-start | bytes 983048 | tf_op jit(solution)/shard_map/ppermute | solution.py:239
  8.4 12.1 %collective-permute-start.4 = (bf16[640,256]{1,0:T(8,128)(2,1)}, bf16[640,256]{1,0:T(8,128)(2,1)}, u32[]{:S(2)}, u32[]{:S(2)}) collective-permute-start(bf16[640,256]{1,0:T(8,128)(2,1)} %maximum_maximum_fusion.refs_3_), channel_id=1, source_target_pairs={{4,0},{8,4},{12,8},{5,1},{9,5},{13,9},{6,2},{10,6},{14,10},{7,3},{... | collective-permute-start | bytes 983048 | tf_op jit(solution)/shard_map/ppermute | solution.py:239
  9.9 11.8 %copy-start.2 = (bf16[2048,512]{1,0:T(8,128)(2,1)S(1)}, bf16[2048,512]{1,0:T(8,128)(2,1)}, u32[]{:S(2)}) copy-start(bf16[2048,512]{1,0:T(8,128)(2,1)} %weights.1) | copy-start | bytes 6291460
  11.0 37.0 %collective-permute-start = (bf16[400,1024]{1,0:T(8,128)(2,1)}, bf16[400,1024]{1,0:T(8,128)(2,1)S(1)}, u32[]{:S(2)}, u32[]{:S(2)}) collective-permute-start(bf16[400,1024]{1,0:T(8,128)(2,1)} %get-tuple-element.11), channel_id=1, source_target_pairs={{0,16},{1,17},{2,18},{3,19},{4,20},{5,21},{6,22},{7,23},{8,24},{9,... | collective-permute-start | bytes 2457608 | tf_op jit(solution)/shard_map/ppermute | solution.py:93
  12.5 14.6 %collective-permute-start.1 = (bf16[512,256]{1,0:T(8,128)(2,1)}, bf16[512,256]{1,0:T(8,128)(2,1)}, u32[]{:S(2)}, u32[]{:S(2)}) collective-permute-start(bf16[512,256]{1,0:T(8,128)(2,1)} %get-tuple-element.8.refs_2_), channel_id=1, source_target_pairs={{0,4},{4,8},{8,12},{1,5},{5,9},{9,13},{2,6},{6,10},{10,14},{3,7},{... | collective-permute-start | bytes 786440 | tf_op jit(solution)/shard_map/ppermute | solution.py:239
  17.8 10.1 %collective-permute-start.3 = (bf16[512,256]{1,0:T(8,128)(2,1)}, bf16[512,256]{1,0:T(8,128)(2,1)}, u32[]{:S(2)}, u32[]{:S(2)}) collective-permute-start(bf16[512,256]{1,0:T(8,128)(2,1)} %get-tuple-element.8.refs_2_), channel_id=1, source_target_pairs={{4,0},{8,4},{12,8},{5,1},{9,5},{13,9},{6,2},{10,6},{14,10},{7,3},{... | collective-permute-start | bytes 786440 | tf_op jit(solution)/shard_map/ppermute | solution.py:239
  19.1 10.1 %collective-permute-start.6 = (bf16[640,256]{1,0:T(8,128)(2,1)S(1)}, bf16[640,256]{1,0:T(8,128)(2,1)}, u32[]{:S(2)}, u32[]{:S(2)}) collective-permute-start(bf16[640,256]{1,0:T(8,128)(2,1)S(1)} %collective-permute-done.2.refs_4_.refs_0_), channel_id=1, source_target_pairs={{4,8},{8,12},{5,9},{9,13},{6,10},{10,14},{7,11},{11,15},{20,24},{2... | collective-permute-start | bytes 983048 | tf_op jit(solution)/shard_map/ppermute | solution.py:239
  20.5 13.6 %collective-permute-start.8 = (bf16[640,256]{1,0:T(8,128)(2,1)}, bf16[640,256]{1,0:T(8,128)(2,1)}, u32[]{:S(2)}, u32[]{:S(2)}) collective-permute-start(bf16[640,256]{1,0:T(8,128)(2,1)} %collective-permute-done.4.refs_6_.refs_1_), channel_id=1, source_target_pairs={{4,0},{8,4},{5,1},{9,5},{6,2},{10,6},{7,3},{11,7},{20,16},{24,20},... | collective-permute-start | bytes 983048 | tf_op jit(solution)/shard_map/ppermute | solution.py:239
  22.7 0.9 %copy-start.1 = (f32[4,384,128]{2,1,0:T(8,128)}, f32[4,384,128]{2,1,0:T(8,128)S(1)}, u32[]{:S(2)}) copy-start(f32[4,384,128]{2,1,0:T(8,128)S(1)} %shard_map.68) | copy-start | bytes 2359300
  23.7 38.6 %all-to-all-start.1 = ((f32[4,384,128]{2,1,0:T(8,128)}), f32[4,384,128]{2,1,0:T(8,128)S(1)}, u32[]{:S(2)}, u32[]{:S(2)}) async-start(f32[4,384,128]{2,1,0:T(8,128)} %copy-done.1), calls=%async_computation.1 | async-start | bytes 1572864 | tf_op jit(solution)/shard_map/all_to_all | solution.py:262
  27.2 8.1 %collective-permute-start.5 = (bf16[512,256]{1,0:T(8,128)(2,1)}, bf16[512,256]{1,0:T(8,128)(2,1)S(1)}, u32[]{:S(2)}, u32[]{:S(2)}) collective-permute-start(bf16[512,256]{1,0:T(8,128)(2,1)} %collective-permute-done.1.refs_3_), channel_id=1, source_target_pairs={{4,8},{8,12},{5,9},{9,13},{6,10},{10,14},{7,11},{11,15},{20,24},{2... | collective-permute-start | bytes 786440 | tf_op jit(solution)/shard_map/ppermute | solution.py:239
  27.9 18.8 %collective-permute-start.7 = (bf16[512,256]{1,0:T(8,128)(2,1)}, bf16[512,256]{1,0:T(8,128)(2,1)S(1)}, u32[]{:S(2)}, u32[]{:S(2)}) collective-permute-start(bf16[512,256]{1,0:T(8,128)(2,1)} %collective-permute-done.3.refs_5_), channel_id=1, source_target_pairs={{4,0},{8,4},{5,1},{9,5},{6,2},{10,6},{7,3},{11,7},{20,16},{24,20},... | collective-permute-start | bytes 786440 | tf_op jit(solution)/shard_map/ppermute | solution.py:239
  29.2 29.7 %collective-permute-start.10 = (bf16[640,256]{1,0:T(8,128)(2,1)}, bf16[640,256]{1,0:T(8,128)(2,1)S(1)}, u32[]{:S(2)}, u32[]{:S(2)}) collective-permute-start(bf16[640,256]{1,0:T(8,128)(2,1)} %collective-permute-done.6.refs_4_.refs_2_), channel_id=1, source_target_pairs={{8,12},{9,13},{10,14},{11,15},{24,28},{25,29},{26,30},{27,31}} | collective-permute-start | bytes 983048 | tf_op jit(solution)/shard_map/ppermute | solution.py:239
  34.0 24.9 %collective-permute-start.12 = (bf16[640,256]{1,0:T(8,128)(2,1)}, bf16[640,256]{1,0:T(8,128)(2,1)S(1)}, u32[]{:S(2)}, u32[]{:S(2)}) collective-permute-start(bf16[640,256]{1,0:T(8,128)(2,1)} %collective-permute-done.8.refs_6_.refs_3_), channel_id=1, source_target_pairs={{4,0},{5,1},{6,2},{7,3},{20,16},{21,17},{22,18},{23,19}} | collective-permute-start | bytes 983048 | tf_op jit(solution)/shard_map/ppermute | solution.py:239
  35.3 18.8 %collective-permute-start.9 = (bf16[512,256]{1,0:T(8,128)(2,1)S(1)}, bf16[512,256]{1,0:T(8,128)(2,1)S(1)}, u32[]{:S(2)}, u32[]{:S(2)}) collective-permute-start(bf16[512,256]{1,0:T(8,128)(2,1)S(1)} %collective-permute-done.5.refs_3_), channel_id=1, source_target_pairs={{8,12},{9,13},{10,14},{11,15},{24,28},{25,29},{26,30},{27,31}} | collective-permute-start | bytes 786440 | tf_op jit(solution)/shard_map/ppermute | solution.py:239
  46.7 12.2 %collective-permute-start.11 = (bf16[512,256]{1,0:T(8,128)(2,1)S(1)}, bf16[512,256]{1,0:T(8,128)(2,1)S(1)}, u32[]{:S(2)}, u32[]{:S(2)}) collective-permute-start(bf16[512,256]{1,0:T(8,128)(2,1)S(1)} %collective-permute-done.7.refs_5_), channel_id=1, source_target_pairs={{4,0},{5,1},{6,2},{7,3},{20,16},{21,17},{22,18},{23,19}} | collective-permute-start | bytes 786440 | tf_op jit(solution)/shard_map/ppermute | solution.py:239
  54.1 11.7 %copy-start.7 = (bf16[256,128]{1,0:T(8,128)(2,1)S(1)}, bf16[256,128]{1,0:T(8,128)(2,1)}, u32[]{:S(2)}) copy-start(bf16[256,128]{1,0:T(8,128)(2,1)} %own.1) | copy-start | bytes 196612
  60.8 0.7 copy-start.3
  61.5 0.7 copy-start.5
  62.2 9.6 %all-to-all-start = ((f32[8,16,384]{2,1,0:T(8,128)}), f32[8,16,384]{2,1,0:T(8,128)S(1)}, u32[]{:S(2)}, u32[]{:S(2)}) async-start(f32[8,16,384]{2,1,0:T(8,128)} %shard_map.67), calls=%async_computation | async-start | bytes 393216 | tf_op jit(solution)/shard_map/all_to_all | solution.py:282
  65.8 1.0 %copy-start.4 = (bf16[640,256]{1,0:T(8,128)(2,1)S(1)}, bf16[640,256]{1,0:T(8,128)(2,1)}, u32[]{:S(2)}) copy-start(bf16[640,256]{1,0:T(8,128)(2,1)} %copy-done.3) | copy-start | bytes 983044
  66.8 1.0 %copy-start.6 = (bf16[640,256]{1,0:T(8,128)(2,1)S(1)}, bf16[640,256]{1,0:T(8,128)(2,1)}, u32[]{:S(2)}) copy-start(bf16[640,256]{1,0:T(8,128)(2,1)} %copy-done.5) | copy-start | bytes 983044

commit v3 on v0

--- a/solution.py
+++ b/solution.py
@@ -1,6 +1,10 @@
+import functools
+
 import jax
 import jax.numpy as jnp
 from jax import lax
+from jax.experimental import pallas as pl
+from jax.experimental.pallas import tpu as pltpu
 from jax.sharding import PartitionSpec as P
 
 ADAPTER_RANK = 16
@@ -9,7 +13,7 @@
 ADAPTER_SCALE = 2.0
 
 
-def local(
+def dispatch(
     tokens,
     base_key_weight,
     stacked_down_weight,
@@ -47,7 +51,6 @@
     )
     chosen = slots_in[:, :, None] == jnp.arange(local_adapters, dtype=jnp.int32)[None, None, :]
     partial_low = jnp.sum(jnp.where(chosen[:, :, :, None], key_projection_output, 0.0), axis=2)
-    partial_low, slots_in = (partial_low, slots_in)
     shrunk = lax.psum(partial_low, "mp")
     shrunk_bf = shrunk.astype(jnp.bfloat16)
     returned = lax.all_to_all(shrunk_bf, "adapter", split_axis=0, concat_axis=0, tiled=True)
@@ -71,6 +74,231 @@
     )
 
 
+AXES = ("groups", "adapter", "mp")
+ID_ROWS = 16
+OWNERS = 4
+
+
+def swap(x, group_bits, owner_bits, share_bits):
+    groups, owners, shares = (lax.axis_size(name) for name in AXES)
+
+    def number(g, a, m):
+        return (g * owners + a) * shares + m
+
+    pairs = [
+        (number(g, a, m), number(g ^ group_bits, a ^ owner_bits, m ^ share_bits))
+        for g in range(groups)
+        for a in range(owners)
+        for m in range(shares)
+    ]
+    return lax.ppermute(x, AXES, pairs)
+
+
+def kernel(body, outs, operands, spaces=None, scratch=()):
+    inner = pl.BlockSpec(memory_space=pltpu.VMEM)
+    specs = [inner if s is None else pl.BlockSpec(memory_space=s) for s in spaces or ()]
+    return pl.pallas_call(
+        body,
+        out_shape=outs,
+        in_specs=specs or [inner] * len(operands),
+        out_specs=jax.tree.map(lambda _: inner, outs),
+        scratch_shapes=scratch,
+        compiler_params=pltpu.CompilerParams(vmem_limit_bytes=16 * 1024 * 1024),
+    )(*operands)
+
+
+def pack_body(down, up, out, sems):
+    g = lax.axis_index("groups")
+    columns, keys = down.shape[1], up.shape[1]
+    count = columns // keys
+    size = up.shape[0] // count
+    part = out.shape[0] - size
+    copies = [
+        pltpu.make_async_copy(
+            down.at[pl.ds(pl.multiple_of(g * part, part), part), :],
+            out.at[pl.ds(0, part), :],
+            sems.at[count],
+        )
+    ]
+    for k in range(count):
+        copies.append(
+            pltpu.make_async_copy(
+                up.at[pl.ds(k * size, size), :],
+                out.at[pl.ds(part, size), pl.ds(k * keys, keys)],
+                sems.at[k],
+            )
+        )
+    for copy in copies:
+        copy.start()
+    for copy in copies:
+        copy.wait()
+
+
+def base_body(keys, tokens, weights, out):
+    wide = jnp.dot(tokens[...], weights[...], preferred_element_type=jnp.float32)
+    for k in range(out.shape[0]):
+        out[k] = wide[:, k * keys : (k + 1) * keys]
+
+
+def shrink_body(bits, part, rows, first, last, *refs):
+    groups = lax.axis_size("groups")
+    a = lax.axis_index("adapter")
+    token_refs, rest = refs[:groups], refs[groups:]
+    picked_in = None
+    if not first:
+        picked_in, rest = rest[0], rest[1:]
+    blocks, outs = rest[: len(bits)], rest[len(bits) :]
+    if not first and not last:
+        bases, outs = outs[0], outs[1:]
+        base = bases[0]
+        for k in range(1, bases.shape[0]):
+            base = base + bases[k]
+        outs[1][...] = base
+    columns = blocks[0].shape[1]
+    eye = (
+        lax.broadcasted_iota(jnp.int32, (ID_ROWS, ID_ROWS), 0)
+        == lax.broadcasted_iota(jnp.int32, (ID_ROWS, ID_ROWS), 1)
+    ).astype(jnp.bfloat16)
+    for n, tokens in enumerate(token_refs):
+        ids = lax.dot_general(
+            tokens[rows : rows + ID_ROWS, :rows],
+            eye,
+            (((0,), (0,)), ((), ())),
+            preferred_element_type=jnp.float32,
+        )
+        owner, slot = ids[:, 0:1], ids[:, 1:2]
+        picked = jnp.zeros((rows, columns), jnp.float32) if first else picked_in[n]
+        for bit, block in zip(bits, blocks):
+            wide = jnp.dot(tokens[:rows, :], block[:part, :], preferred_element_type=jnp.float32)
+            picked = jnp.where(owner == (a ^ bit).astype(jnp.float32), wide, picked)
+        if not last:
+            outs[0][n] = picked
+            continue
+        column = lax.broadcasted_iota(jnp.int32, (rows, columns), 1)
+        adapter = (column // ADAPTER_RANK).astype(jnp.float32)
+        picked = jnp.where(adapter == slot, picked, 0.0)
+        lanes = 128
+        folded = picked[:, :lanes]
+        for k in range(1, columns // lanes):
+            folded = folded + picked[:, k * lanes : (k + 1) * lanes]
+        turned = folded.T
+        low = turned[:ADAPTER_RANK]
+        for k in range(1, lanes // ADAPTER_RANK):
+            low = low + turned[k * ADAPTER_RANK : (k + 1) * ADAPTER_RANK]
+        outs[n][...] = low
+
+
+def finish_body(bits, part, near, far, base, ids, *refs):
+    a = lax.axis_index("adapter")
+    blocks, out = refs[:-1], refs[-1]
+    rows, keys = out.shape
+    columns = blocks[0].shape[1]
+    column = lax.broadcasted_iota(jnp.int32, (ADAPTER_RANK, columns), 1)
+    row = lax.broadcasted_iota(jnp.int32, (ADAPTER_RANK, columns), 0)
+    repeat = (lax.rem(column, ADAPTER_RANK) == row).astype(jnp.bfloat16)
+    shrunk = (near[...] + far[...]).astype(jnp.bfloat16)
+    spread = lax.dot_general(
+        shrunk, repeat, (((0,), (0,)), ((), ())), preferred_element_type=jnp.float32
+    )
+    adapter = lax.broadcasted_iota(jnp.int32, (rows, columns), 1) // ADAPTER_RANK
+    updates = jnp.zeros((rows, keys), jnp.float32)
+    for bit, block in zip(bits, blocks):
+        wide = block[part:, :]
+        up = jnp.concatenate([wide[:, k * keys : (k + 1) * keys] for k in range(columns // keys)])
+        first = (a ^ bit) * (columns // ADAPTER_RANK)
+        chosen = jnp.where(adapter + first == ids[...], spread, 0.0).astype(jnp.bfloat16)
+        updates = updates + jnp.dot(chosen, up, preferred_element_type=jnp.float32)
+    updates = updates.astype(jnp.bfloat16).astype(jnp.float32)
+    out[...] = (base[...] + ADAPTER_SCALE * updates).astype(jnp.bfloat16)
+
+
+def gather(
+    tokens,
+    base_key_weight,
+    stacked_down_weight,
+    stacked_up_weight,
+    request_adapter_owner,
+    request_adapter_slot,
+):
+    rows, features = tokens.shape
+    groups, _, shares = (lax.axis_size(name) for name in AXES)
+    g = lax.axis_index("groups")
+    columns = stacked_down_weight.shape[1]
+    keys = stacked_up_weight.shape[1]
+    local_adapters = columns // ADAPTER_RANK
+    part = features // groups
+    half = columns // keys
+
+    own = kernel(
+        pack_body,
+        jax.ShapeDtypeStruct((part + columns // half, columns), jnp.bfloat16),
+        (stacked_down_weight, stacked_up_weight),
+        (pl.ANY, pl.ANY),
+        [pltpu.SemaphoreType.DMA((half + 1,))],
+    )
+    across = swap(own, 0, 3, 0)
+    beside = swap(own, 0, 1, 0)
+    behind = swap(across, 0, 1, 0)
+
+    id_rows = jnp.concatenate(
+        [request_adapter_owner.reshape(1, rows), request_adapter_slot.reshape(1, rows)], axis=0
+    ).astype(jnp.bfloat16)
+    id_rows = jnp.pad(id_rows, ((0, ID_ROWS - 2), (0, part - rows)))
+    token_parts = []
+    for step in range(groups):
+        taken = lax.dynamic_slice(tokens, (0, (g ^ step) * part), (rows, part))
+        taken = jnp.concatenate([taken, id_rows], axis=0)
+        token_parts.append(swap(taken, step, 0, 0) if step else taken)
+
+    bases = kernel(
+        functools.partial(base_body, keys),
+        jax.ShapeDtypeStruct((shares, rows, keys), jnp.float32),
+        (tokens, base_key_weight),
+    )
+    bases = lax.all_to_all(bases, "mp", 0, 0, tiled=True)
+
+    picked_shape = jax.ShapeDtypeStruct((groups, rows, columns), jnp.float32)
+    low_shape = jax.ShapeDtypeStruct((ADAPTER_RANK, rows), jnp.float32)
+    picked = kernel(
+        functools.partial(shrink_body, (0,), part, rows, True, False),
+        picked_shape,
+        (*token_parts, own),
+    )
+    picked, base = kernel(
+        functools.partial(shrink_body, (3, 1), part, rows, False, False),
+        [picked_shape, jax.ShapeDtypeStruct((rows, keys), jnp.float32)],
+        (*token_parts, picked, across, beside, bases),
+    )
+    low, low_away = kernel(
+        functools.partial(shrink_body, (2,), part, rows, False, True),
+        [low_shape] * groups,
+        (*token_parts, picked, behind),
+    )
+
+    low = low + swap(low_away, 1, 0, 0)
+    bit = shares // 2
+    while bit > 1:
+        low = low + swap(low, 0, 0, bit)
+        bit //= 2
+    low_far = swap(low, 0, 0, 1)
+
+    ids = request_adapter_owner * local_adapters + request_adapter_slot.reshape(rows, 1)
+    return kernel(
+        functools.partial(finish_body, (0, 3, 1, 2), part),
+        jax.ShapeDtypeStruct((rows, keys), jnp.bfloat16),
+        (low, low_far, base, ids, own, across, beside, behind),
+    )
+
+
+def local(*args):
+    rows, columns = args[0].shape[0], args[2].shape[1]
+    groups, owners, shares = (lax.axis_size(name) for name in AXES)
+    capacity = max(2, 3 * rows // (2 * owners))
+    fits = owners == OWNERS and groups == 2 and shares > 1 and shares & (shares - 1) == 0
+    travels = fits and columns <= groups * capacity
+    return (gather if travels else dispatch)(*args)
+
+
 def solution(mesh):
     placed = (
         P(("groups", "adapter"), "mp"),

time: 131 us -> 61.2 us (0.47)
  waiting for transfers between devices: 49.7 us -> 21 us
  blocking collectives: 25.7 us -> 0 us
  between operations: 13.5 us -> 0.15 us
  local copies, waits for them, and re-layouts: 14.4 us -> 3.37 us
  Pallas kernels: 0 us -> 10.6 us
  starting transfers between devices: 14.5 us -> 24.6 us
  matrix products: 8.59 us -> 0 us
  other arithmetic: 4.22 us -> 1.06 us
    all_to_all x3 -> x1, waiting for transfers between devices: 49.7 us -> 0.01 us  [gather(): bases = lax.all_to_all(bases, 'mp', 0, 0, tiled=True)]
    ppermute x0 -> x7, starting transfers between devices: none -> 21.2 us  [swap(): return lax.ppermute(x, AXES, pairs)]
    ppermute x0 -> x7, waiting for transfers between devices: none -> 21 us  [swap(): return lax.ppermute(x, AXES, pairs)]
    all_gather x1 -> x0, blocking collectives: 14.4 us -> none  [local(): lax.all_gather(stacked_up_weight, 'adapter', axis=0, tiled=True)]
    psum x1 -> x0, blocking collectives: 11.3 us -> none  [local(): shrunk = lax.psum(partial_low, 'mp')]
    all_to_all x3 -> x1, starting transfers between devices: 14.5 us -> 3.49 us  [gather(): bases = lax.all_to_all(bases, 'mp', 0, 0, tiled=True)]
    pallas_call x0 -> x6, Pallas kernels: none -> 10.6 us  [kernel(): pl.pallas_call(body, out_shape=outs, in_specs=specs or [inner] * len(oper...]
    dot_general x3 -> x0, matrix products: 8.59 us -> none  [the longest x1 3.68 us: local(): lax.dot_general(base_key_weight, tokens, (((0,), (1,)), ((), ())), prefer...]
  transfers between devices with their start and end apart: 4 -> 8, of which waited for: 2 -> 5; matrix products, arithmetic and copies ran while one was open for 14% -> 2% of each run, Pallas kernels for 0% -> 8%
where the time goes in v3:
time: 61.2 us; the launch traced here: 60.9 us
  starting transfers between devices  24.6 us (40%)
  waiting for transfers between devices  21 us (34%)
  Pallas kernels  10.6 us (17%)
  local copies, waits for them, and re-layouts  3.37 us (6%)
  other arithmetic  1.06 us (2%)
    ppermute x7, starting transfers between devices, swap(): return lax.ppermute(x, AXES, pairs)  21.2 us
    ppermute x7, waiting for transfers between devices, swap(): return lax.ppermute(x, AXES, pairs)  21 us
    pallas_call x6, Pallas kernels, kernel(): pl.pallas_call(body, out_shape=outs, in_specs=specs or [inner] * len(oper...  10.6 us
    all_to_all x1, starting transfers between devices, gather(): bases = lax.all_to_all(bases, 'mp', 0, 0, tiled=True)  3.49 us
    unnamed x14, local copies, waits for them, and re-layouts  3.11 us
  transfers between devices with their start and end apart: 8, of which 5 were waited for; matrix products, arithmetic and copies ran while one was open for 2% of the time, Pallas kernels for 8%

profile of v3, /device:TPU:0, one launch (start us, length us, event | category | flops | bytes accessed | tf_op | source)
XLA Modules:
  0.0 60.9 jit_solution(8324887217415712931)
XLA Ops:
  0.0 0.0 copy-start
  0.0 0.0 copy-start.3
  0.0 1.3 %copy-done.3 = bf16[2048,256]{1,0:T(8,128)(2,1)S(1)} copy-done((bf16[2048,256]{1,0:T(8,128)(2,1)S(1)}, bf16[2048,256]{1,0:T(8,128)(2,1)}, u32[]{:S(2)}) %copy-start.3) | copy-done | bytes 1048600
  1.3 0.0 copy-start.4
  1.3 0.8 %copy-done.4 = bf16[256,128]{1,0:T(8,128)(2,1)S(1)} copy-done((bf16[256,128]{1,0:T(8,128)(2,1)S(1)}, bf16[256,128]{1,0:T(8,128)(2,1)}, u32[]{:S(2)}) %copy-start.4) | copy-done | bytes 65560
  2.2 0.0 copy-start.5
  2.2 0.0 copy-start.6
  2.2 0.9 %shard_map.64.refs_2_.refs_0_ = bf16[1152,256]{1,0:T(8,128)(2,1)} custom-call(bf16[2048,256]{1,0:T(8,128)(2,1)S(1)} %copy-done.3, bf16[256,128]{1,0:T(8,128)(2,1)S(1)} %copy-done.4), custom_call_target="tpu_custom_call" | custom-call | tf_op jit(solution)/shard_map/pallas_call | solution.py:100
  3.1 5.1 %collective-permute-start.1 = (bf16[1152,256]{1,0:T(8,128)(2,1)}, bf16[1152,256]{1,0:T(8,128)(2,1)}, u32[]{:S(2)}, u32[]{:S(2)}) collective-permute-start(bf16[1152,256]{1,0:T(8,128)(2,1)} %shard_map.64.refs_2_.refs_0_), channel_id=1, source_target_pairs={{0,12},{1,13},{2,14},{3,15},{4,8},{5,9},{6,10},{7,11},{8,4},{9,5},... | collective-permute-start | bytes 1769480 | tf_op jit(solution)/shard_map/ppermute | solution.py:94
  8.2 0.0 copy-done.5
  8.2 0.0 copy-done.6
  8.3 0.0 copy-done
  8.3 0.1 constant_dynamic-slice_fusion
  8.4 0.0 copy-start.2
  8.4 1.0 %pad_maximum_fusion = (bf16[400,1024]{1,0:T(8,128)(2,1)}, bf16[400,1024]{1,0:T(8,128)(2,1)S(1)}) fusion(bf16[16,1024]{1,0:T(8,128)(2,1)S(1)} %fusion.5, bf16[384,1024]{1,0:T(8,128)(2,1)S(1)} %get-tuple-element.13, bf16[384,1024]{1,0:T(8,128)(2,1)S(1)} %get-tuple-element.14), kind=kLoop, calls=%fused_computation | loop fusion | flops 2867200 | bytes 3244032 | tf_op jit(solution)/shard_map/concatenate | solution.py:250
  9.5 1.5 %collective-permute-start = (bf16[400,1024]{1,0:T(8,128)(2,1)}, bf16[400,1024]{1,0:T(8,128)(2,1)S(1)}, u32[]{:S(2)}, u32[]{:S(2)}) collective-permute-start(bf16[400,1024]{1,0:T(8,128)(2,1)} %get-tuple-element.15), channel_id=1, source_target_pairs={{0,16},{1,17},{2,18},{3,19},{4,20},{5,21},{6,22},{7,23},{8,24},{9,... | collective-permute-start | bytes 2457608 | tf_op jit(solution)/shard_map/ppermute | solution.py:94
  11.0 0.0 collective-permute-start.2
  11.0 0.0 copy-done.2
  11.0 1.0 %shard_map.66 = f32[4,384,128]{2,1,0:T(8,128)S(1)} custom-call(bf16[384,2048]{1,0:T(8,128)(2,1)S(1)} %copy-done, bf16[2048,512]{1,0:T(8,128)(2,1)S(1)} %copy-done.2), custom_call_target="tpu_custom_call" | custom-call | tf_op jit(solution)/shard_map/pallas_call | solution.py:100
  12.0 0.0 copy-start.1
  12.0 0.9 %copy-done.1 = f32[4,384,128]{2,1,0:T(8,128)} copy-done((f32[4,384,128]{2,1,0:T(8,128)}, f32[4,384,128]{2,1,0:T(8,128)S(1)}, u32[]{:S(2)}) %copy-start.1) | copy-done | bytes 786456
  12.9 3.5 %all-to-all-start = ((f32[4,384,128]{2,1,0:T(8,128)}), f32[4,384,128]{2,1,0:T(8,128)S(1)}, u32[]{:S(2)}, u32[]{:S(2)}) async-start(f32[4,384,128]{2,1,0:T(8,128)} %copy-done.1), calls=%async_computation | async-start | bytes 1572864 | tf_op jit(solution)/shard_map/all_to_all | solution.py:258
  16.4 6.4 %collective-permute-done.1.refs_3_.refs_1_ = bf16[1152,256]{1,0:T(8,128)(2,1)} collective-permute-done((bf16[1152,256]{1,0:T(8,128)(2,1)}, bf16[1152,256]{1,0:T(8,128)(2,1)}, u32[]{:S(2)}, u32[]{:S(2)}) %collective-permute-start.1) | collective-permute-done | bytes 589856 | tf_op jit(solution)/shard_map/ppermute | solution.py:94
  22.8 11.4 %collective-permute-start.3 = (bf16[1152,256]{1,0:T(8,128)(2,1)}, bf16[1152,256]{1,0:T(8,128)(2,1)}, u32[]{:S(2)}, u32[]{:S(2)}) collective-permute-start(bf16[1152,256]{1,0:T(8,128)(2,1)} %collective-permute-done.1.refs_3_.refs_1_), channel_id=1, source_target_pairs={{0,4},{1,5},{2,6},{3,7},{4,0},{5,1},{6,2},{7,3},{8,12},{9,13},{10,... | collective-permute-start | bytes 1769480 | tf_op jit(solution)/shard_map/ppermute | solution.py:94
  34.2 0.0 collective-permute-done.refs_1_
  34.2 1.7 %shard_map.65.refs_2_ = f32[2,384,256]{2,1,0:T(8,128)S(1)} custom-call(bf16[400,1024]{1,0:T(8,128)(2,1)S(1)} %get-tuple-element.16.refs_0_, bf16[400,1024]{1,0:T(8,128)(2,1)S(1)} %collective-permute-done.refs_1_, bf16[1152,256]{1,0:T(8,128)(2,1)} %shard_map.64.refs_2_.refs_0_), custom_call_target="tpu_custom_call" | custom-call | tf_op jit(solution)/shard_map/pallas_call | solution.py:100
  35.9 0.0 collective-permute-done.2.refs_4_.refs_2_
  36.0 0.0 all-to-all-done.refs_5_
  36.0 2.3 %shard_map.67 = (f32[2,384,256]{2,1,0:T(8,128)S(1)}, f32[384,128]{1,0:T(8,128)S(1)}) custom-call(bf16[400,1024]{1,0:T(8,128)(2,1)S(1)} %get-tuple-element.16.refs_0_, bf16[400,1024]{1,0:T(8,128)(2,1)S(1)} %collective-permute-done.refs_1_, f32[2,384,256]{2,1,0:T(8,128)S(1)} %shard_map.65.refs_2_, bf16[1152,256]{1,0:T(8,128)(2,1)} %collective-permute-done.1.refs_3_.refs_1_, ...), custom_call_target="tpu_custom_call" | custom-call | tf_op jit(solution)/shard_map/pallas_call | solution.py:100
  38.3 8.9 %collective-permute-done.3.refs_3_ = bf16[1152,256]{1,0:T(8,128)(2,1)} collective-permute-done((bf16[1152,256]{1,0:T(8,128)(2,1)}, bf16[1152,256]{1,0:T(8,128)(2,1)}, u32[]{:S(2)}, u32[]{:S(2)}) %collective-permute-start.3) | collective-permute-done | bytes 589856 | tf_op jit(solution)/shard_map/ppermute | solution.py:94
  47.2 1.8 %shard_map.68 = (f32[16,384]{1,0:T(8,128)S(1)}, f32[16,384]{1,0:T(8,128)S(1)}) custom-call(bf16[400,1024]{1,0:T(8,128)(2,1)S(1)} %get-tuple-element.16.refs_0_, bf16[400,1024]{1,0:T(8,128)(2,1)S(1)} %collective-permute-done.refs_1_, f32[2,384,256]{2,1,0:T(8,128)S(1)} %get-tuple-element.9.refs_2_, bf16[1152,256]{1,0:T(8,128)(2,1)} %collective-permute-done.3.refs_3_), custom_call_target="tpu_custom_call" | custom-call | tf_op jit(solution)/shard_map/pallas_call | solution.py:100
  49.1 1.6 %collective-permute-start.4 = (f32[16,384]{1,0:T(8,128)S(1)}, f32[16,384]{1,0:T(8,128)S(1)}, u32[]{:S(2)}, u32[]{:S(2)}) collective-permute-start(f32[16,384]{1,0:T(8,128)S(1)} %get-tuple-element.11), channel_id=1, source_target_pairs={{0,16},{1,17},{2,18},{3,19},{4,20},{5,21},{6,22},{7,23},{8,24},{9,... | collective-permute-start | bytes 73736 | tf_op jit(solution)/shard_map/ppermute | solution.py:94
  50.7 2.3 %collective-permute-done.4 = f32[16,384]{1,0:T(8,128)S(1)} collective-permute-done((f32[16,384]{1,0:T(8,128)S(1)}, f32[16,384]{1,0:T(8,128)S(1)}, u32[]{:S(2)}, u32[]{:S(2)}) %collective-permute-start.4) | collective-permute-done | bytes 24608 | tf_op jit(solution)/shard_map/ppermute | solution.py:94
  53.0 1.5 %collective-permute-start.5 = (f32[16,384]{1,0:T(8,128)S(1)}, f32[16,384]{1,0:T(8,128)S(1)}, u32[]{:S(2)}, u32[]{:S(2)}) collective-permute-start(f32[16,384]{1,0:T(8,128)S(1)} %add.19), channel_id=1, source_target_pairs={{0,2},{1,3},{2,0},{3,1},{4,6},{5,7},{6,4},{7,5},{8,10},{9,11},{10,... | collective-permute-start | bytes 73736 | tf_op jit(solution)/shard_map/ppermute | solution.py:94
  54.5 2.3 %collective-permute-done.5 = f32[16,384]{1,0:T(8,128)S(1)} collective-permute-done((f32[16,384]{1,0:T(8,128)S(1)}, f32[16,384]{1,0:T(8,128)S(1)}, u32[]{:S(2)}, u32[]{:S(2)}) %collective-permute-start.5) | collective-permute-done | bytes 24608 | tf_op jit(solution)/shard_map/ppermute | solution.py:94
  56.8 0.0 collective-permute-start.6
  56.8 0.1 copy.12.ids
  56.9 1.0 %collective-permute-done.6.far = f32[16,384]{1,0:T(8,128)S(1)} collective-permute-done((f32[16,384]{1,0:T(8,128)S(1)}, f32[16,384]{1,0:T(8,128)S(1)}, u32[]{:S(2)}, u32[]{:S(2)}) %collective-permute-start.6) | collective-permute-done | bytes 24608 | tf_op jit(solution)/shard_map/ppermute | solution.py:94
  58.0 2.9 %shard_map.69 = bf16[384,128]{1,0:T(8,128)(2,1)} custom-call(f32[16,384]{1,0:T(8,128)S(1)} %add.20.near, f32[16,384]{1,0:T(8,128)S(1)} %collective-permute-done.6.far, f32[384,128]{1,0:T(8,128)S(1)} %get-tuple-element.12.base, s32[384,1]{1,0:T(8,128)S(1)} %copy.12.ids, bf16[1152,256]{1,0:T(8,128)(2,1)} %shard_map.64.refs_2_.refs_0_, ...), custom_call_target="tpu_custom_call" | custom-call | tf_op jit(solution)/shard_map/pallas_call | solution.py:100
  (6 shorter events, 0.0 us)
Async XLA Ops:
  0.0 8.3 %copy-start = (bf16[384,2048]{1,0:T(8,128)(2,1)S(1)}, bf16[384,2048]{1,0:T(8,128)(2,1)}, u32[]{:S(2)}) copy-start(bf16[384,2048]{1,0:T(8,128)(2,1)} %tokens.1) | copy-start | bytes 4718596
  0.0 1.3 %copy-start.3 = (bf16[2048,256]{1,0:T(8,128)(2,1)S(1)}, bf16[2048,256]{1,0:T(8,128)(2,1)}, u32[]{:S(2)}) copy-start(bf16[2048,256]{1,0:T(8,128)(2,1)} %down.1) | copy-start | bytes 3145732
  1.3 0.8 %copy-start.4 = (bf16[256,128]{1,0:T(8,128)(2,1)S(1)}, bf16[256,128]{1,0:T(8,128)(2,1)}, u32[]{:S(2)}) copy-start(bf16[256,128]{1,0:T(8,128)(2,1)} %up.1) | copy-start | bytes 196612
  2.2 6.0 %copy-start.5 = (s32[384]{0:T(512)S(1)}, s32[384]{0:T(512)}, u32[]{:S(2)}) copy-start(s32[384]{0:T(512)} %param.11) | copy-start | bytes 4612
  2.2 6.0 %copy-start.6 = (s32[384,1]{0,1:T(1,128)S(1)}, s32[384,1]{0,1:T(1,128)}, u32[]{:S(2)}) copy-start(s32[384,1]{0,1:T(1,128)} %param.10) | copy-start | bytes 4612
  3.1 19.7 %collective-permute-start.1 = (bf16[1152,256]{1,0:T(8,128)(2,1)}, bf16[1152,256]{1,0:T(8,128)(2,1)}, u32[]{:S(2)}, u32[]{:S(2)}) collective-permute-start(bf16[1152,256]{1,0:T(8,128)(2,1)} %shard_map.64.refs_2_.refs_0_), channel_id=1, source_target_pairs={{0,12},{1,13},{2,14},{3,15},{4,8},{5,9},{6,10},{7,11},{8,4},{9,5},... | collective-permute-start | bytes 1769480 | tf_op jit(solution)/shard_map/ppermute | solution.py:94
  8.4 2.6 %copy-start.2 = (bf16[2048,512]{1,0:T(8,128)(2,1)S(1)}, bf16[2048,512]{1,0:T(8,128)(2,1)}, u32[]{:S(2)}) copy-start(bf16[2048,512]{1,0:T(8,128)(2,1)} %weights.1) | copy-start | bytes 6291460
  9.5 24.7 %collective-permute-start = (bf16[400,1024]{1,0:T(8,128)(2,1)}, bf16[400,1024]{1,0:T(8,128)(2,1)S(1)}, u32[]{:S(2)}, u32[]{:S(2)}) collective-permute-start(bf16[400,1024]{1,0:T(8,128)(2,1)} %get-tuple-element.15), channel_id=1, source_target_pairs={{0,16},{1,17},{2,18},{3,19},{4,20},{5,21},{6,22},{7,23},{8,24},{9,... | collective-permute-start | bytes 2457608 | tf_op jit(solution)/shard_map/ppermute | solution.py:94
  11.0 25.0 %collective-permute-start.2 = (bf16[1152,256]{1,0:T(8,128)(2,1)}, bf16[1152,256]{1,0:T(8,128)(2,1)}, u32[]{:S(2)}, u32[]{:S(2)}) collective-permute-start(bf16[1152,256]{1,0:T(8,128)(2,1)} %shard_map.64.refs_2_.refs_0_), channel_id=1, source_target_pairs={{0,4},{1,5},{2,6},{3,7},{4,0},{5,1},{6,2},{7,3},{8,12},{9,13},{10,... | collective-permute-start | bytes 1769480 | tf_op jit(solution)/shard_map/ppermute | solution.py:94
  12.0 0.9 %copy-start.1 = (f32[4,384,128]{2,1,0:T(8,128)}, f32[4,384,128]{2,1,0:T(8,128)S(1)}, u32[]{:S(2)}) copy-start(f32[4,384,128]{2,1,0:T(8,128)S(1)} %shard_map.66) | copy-start | bytes 2359300
  12.9 23.1 %all-to-all-start = ((f32[4,384,128]{2,1,0:T(8,128)}), f32[4,384,128]{2,1,0:T(8,128)S(1)}, u32[]{:S(2)}, u32[]{:S(2)}) async-start(f32[4,384,128]{2,1,0:T(8,128)} %copy-done.1), calls=%async_computation | async-start | bytes 1572864 | tf_op jit(solution)/shard_map/all_to_all | solution.py:258
  22.8 24.5 %collective-permute-start.3 = (bf16[1152,256]{1,0:T(8,128)(2,1)}, bf16[1152,256]{1,0:T(8,128)(2,1)}, u32[]{:S(2)}, u32[]{:S(2)}) collective-permute-start(bf16[1152,256]{1,0:T(8,128)(2,1)} %collective-permute-done.1.refs_3_.refs_1_), channel_id=1, source_target_pairs={{0,4},{1,5},{2,6},{3,7},{4,0},{5,1},{6,2},{7,3},{8,12},{9,13},{10,... | collective-permute-start | bytes 1769480 | tf_op jit(solution)/shard_map/ppermute | solution.py:94
  49.1 3.9 %collective-permute-start.4 = (f32[16,384]{1,0:T(8,128)S(1)}, f32[16,384]{1,0:T(8,128)S(1)}, u32[]{:S(2)}, u32[]{:S(2)}) collective-permute-start(f32[16,384]{1,0:T(8,128)S(1)} %get-tuple-element.11), channel_id=1, source_target_pairs={{0,16},{1,17},{2,18},{3,19},{4,20},{5,21},{6,22},{7,23},{8,24},{9,... | collective-permute-start | bytes 73736 | tf_op jit(solution)/shard_map/ppermute | solution.py:94
  53.0 3.8 %collective-permute-start.5 = (f32[16,384]{1,0:T(8,128)S(1)}, f32[16,384]{1,0:T(8,128)S(1)}, u32[]{:S(2)}, u32[]{:S(2)}) collective-permute-start(f32[16,384]{1,0:T(8,128)S(1)} %add.19), channel_id=1, source_target_pairs={{0,2},{1,3},{2,0},{3,1},{4,6},{5,7},{6,4},{7,5},{8,10},{9,11},{10,... | collective-permute-start | bytes 73736 | tf_op jit(solution)/shard_map/ppermute | solution.py:94
  56.8 1.2 %collective-permute-start.6 = (f32[16,384]{1,0:T(8,128)S(1)}, f32[16,384]{1,0:T(8,128)S(1)}, u32[]{:S(2)}, u32[]{:S(2)}) collective-permute-start(f32[16,384]{1,0:T(8,128)S(1)} %add.20.near), channel_id=1, source_target_pairs={{0,1},{1,0},{2,3},{3,2},{4,5},{5,4},{6,7},{7,6},{8,9},{9,8},{10,11... | collective-permute-start | bytes 73736 | tf_op jit(solution)/shard_map/ppermute | solution.py:94

commit v4 on v0

--- a/solution.py
+++ b/solution.py
@@ -1,6 +1,10 @@
+import functools
+
 import jax
 import jax.numpy as jnp
 from jax import lax
+from jax.experimental import pallas as pl
+from jax.experimental.pallas import tpu as pltpu
 from jax.sharding import PartitionSpec as P
 
 ADAPTER_RANK = 16
@@ -9,7 +13,7 @@
 ADAPTER_SCALE = 2.0
 
 
-def local(
+def dispatch(
     tokens,
     base_key_weight,
     stacked_down_weight,
@@ -47,7 +51,6 @@
     )
     chosen = slots_in[:, :, None] == jnp.arange(local_adapters, dtype=jnp.int32)[None, None, :]
     partial_low = jnp.sum(jnp.where(chosen[:, :, :, None], key_projection_output, 0.0), axis=2)
-    partial_low, slots_in = (partial_low, slots_in)
     shrunk = lax.psum(partial_low, "mp")
     shrunk_bf = shrunk.astype(jnp.bfloat16)
     returned = lax.all_to_all(shrunk_bf, "adapter", split_axis=0, concat_axis=0, tiled=True)
@@ -71,6 +74,356 @@
     )
 
 
+AXES = ("groups", "adapter", "mp")
+ID_ROWS = 16
+OWNERS = 4
+LANES = 128
+
+
+def exchange(x, group_bits, share_bits, owners):
+    groups, count, shares = (lax.axis_size(name) for name in AXES)
+
+    def number(g, a, m):
+        return (g * count + a) * shares + m
+
+    pairs = [
+        (number(g, a, m), number(g ^ group_bits, b, m ^ share_bits))
+        for g in range(groups)
+        for a, b in owners
+        for m in range(shares)
+    ]
+    return lax.ppermute(x, AXES, pairs)
+
+
+SAME = tuple((a, a) for a in range(OWNERS))
+BESIDE = ((0, 1), (1, 0), (2, 3), (3, 2))
+ACROSS = ((0, 2), (1, 3), (2, 0), (3, 1))
+MIRROR = ((0, 3), (1, 2), (2, 1), (3, 0))
+MIDDLE = ((1, 2), (2, 1))
+OUTWARD = ((1, 0), (2, 3))
+INWARD = ((0, 1), (3, 2))
+
+
+def after(x, *others):
+    return lax.optimization_barrier((x, *others))[0]
+
+
+def kernel(body, outs, operands, spaces=None, scratch=()):
+    inner = pl.BlockSpec(memory_space=pltpu.VMEM)
+    specs = [inner if s is None else pl.BlockSpec(memory_space=s) for s in spaces or ()]
+    return pl.pallas_call(
+        body,
+        out_shape=outs,
+        in_specs=specs or [inner] * len(operands),
+        out_specs=jax.tree.map(lambda _: inner, outs),
+        scratch_shapes=scratch,
+        compiler_params=pltpu.CompilerParams(vmem_limit_bytes=16 * 1024 * 1024),
+    )(*operands)
+
+
+def pack_body(down, up, out, up_out, sems):
+    g = lax.axis_index("groups")
+    keys = up.shape[1]
+    part, size = out.shape[0], up_out.shape[0]
+    count = down.shape[1] // keys
+    copies = [
+        pltpu.make_async_copy(
+            down.at[pl.ds(pl.multiple_of(g * part, part), part), :], out, sems.at[count]
+        )
+    ]
+    for k in range(count):
+        start = pl.multiple_of((g * count + k) * size, size)
+        copies.append(
+            pltpu.make_async_copy(
+                up.at[pl.ds(start, size), :], up_out.at[:, pl.ds(k * keys, keys)], sems.at[k]
+            )
+        )
+    for copy in copies:
+        copy.start()
+    for copy in copies:
+        copy.wait()
+
+
+def hop_body(capacity, tokens, id_rows, own, away, places):
+    a, g = lax.axis_index("adapter"), lax.axis_index("groups")
+    rows = tokens.shape[0]
+    part = own.shape[1]
+    ids = id_rows[:, :rows]
+    match = (ids.astype(jnp.float32) == (OWNERS - 1 - a).astype(jnp.float32)).astype(jnp.bfloat16)
+    earlier = lax.broadcasted_iota(jnp.int32, (rows, rows), 0) < lax.broadcasted_iota(
+        jnp.int32, (rows, rows), 1
+    )
+    rank = jnp.dot(match, earlier.astype(jnp.bfloat16), preferred_element_type=jnp.float32)
+    place = lax.broadcasted_iota(jnp.int32, (capacity, rows), 0).astype(jnp.float32)
+    taken = (place == rank[0:1]) & (match[0:1].astype(jnp.float32) > 0)
+    chosen = taken.astype(jnp.bfloat16)
+    places[...] = chosen
+    kept = lax.dot_general(ids, chosen, NT, preferred_element_type=jnp.float32)
+    for out, half in ((own, g), (away, 1 - g)):
+        block = tokens[:, pl.ds(pl.multiple_of(half * part, part), part)]
+        packed = jnp.dot(chosen, block, preferred_element_type=jnp.float32)
+        out[:capacity, :] = packed.astype(jnp.bfloat16)
+        out[capacity:, :] = jnp.zeros((ID_ROWS, part), jnp.bfloat16)
+        out[capacity:, :capacity] = kept.astype(jnp.bfloat16)
+
+
+NT = (((1,), (1,)), ((), ()))
+TN = (((0,), (0,)), ((), ()))
+
+
+def base_body(keys, tokens, weights, out):
+    wide = jnp.dot(tokens[...], weights[...], preferred_element_type=jnp.float32)
+    for k in range(out.shape[0]):
+        out[k] = wide[:, k * keys : (k + 1) * keys]
+
+
+def id_columns(rows_ref, start, count):
+    eye = (
+        lax.broadcasted_iota(jnp.int32, (ID_ROWS, ID_ROWS), 0)
+        == lax.broadcasted_iota(jnp.int32, (ID_ROWS, ID_ROWS), 1)
+    ).astype(jnp.bfloat16)
+    ids = lax.dot_general(
+        rows_ref[start : start + ID_ROWS, :count], eye, TN, preferred_element_type=jnp.float32
+    )
+    return ids[:, 0:1], ids[:, 1:2]
+
+
+def adapters(rows, columns):
+    column = lax.broadcasted_iota(jnp.int32, (rows, columns), 1)
+    return (column // ADAPTER_RANK).astype(jnp.float32)
+
+
+def fold(wide):
+    folded = wide[:, :LANES]
+    for k in range(1, wide.shape[1] // LANES):
+        folded = folded + wide[:, k * LANES : (k + 1) * LANES]
+    return folded
+
+
+def low_rank(folded):
+    turned = folded.T
+    low = turned[:ADAPTER_RANK]
+    for k in range(1, LANES // ADAPTER_RANK):
+        low = low + turned[k * ADAPTER_RANK : (k + 1) * ADAPTER_RANK]
+    return low
+
+
+def early_body(bits, part, rows, *refs):
+    groups = lax.axis_size("groups")
+    a = lax.axis_index("adapter")
+    token_refs, rest = refs[:groups], refs[groups:]
+    blocks, (bases, folded, mask, base) = rest[: len(bits)], rest[len(bits) :]
+    columns = blocks[0].shape[1]
+    total = bases[0]
+    for k in range(1, bases.shape[0]):
+        total = total + bases[k]
+    base[...] = total
+    adapter = adapters(rows, columns)
+    for n, tokens in enumerate(token_refs):
+        owner, slot = id_columns(tokens, rows, rows)
+        right = adapter == slot
+        picked = jnp.zeros((rows, columns), jnp.float32)
+        for bit, block in zip(bits, blocks):
+            wide = jnp.dot(tokens[:rows, :], block[...], preferred_element_type=jnp.float32)
+            picked = jnp.where(owner == (a ^ bit).astype(jnp.float32), wide, picked)
+        folded[n] = fold(jnp.where(right, picked, 0.0))
+        mask[n] = jnp.where(owner == (a ^ 2).astype(jnp.float32), right.astype(jnp.float32), 0.0)
+
+
+def last_body(part, rows, capacity, *refs):
+    groups = lax.axis_size("groups")
+    a = lax.axis_index("adapter")
+    token_refs, rest = refs[:groups], refs[groups:]
+    hops, rest = rest[:groups], rest[groups:]
+    folded, mask, inside, outside = rest[:4]
+    lows, hop_lows = rest[4 : 4 + groups], rest[4 + groups :]
+    columns = inside.shape[1]
+
+    def finish(block):
+        for n, tokens in enumerate(token_refs):
+            wide = jnp.dot(tokens[:rows, :], block[...], preferred_element_type=jnp.float32)
+            kept = fold(jnp.where(mask[n] > 0, wide, 0.0))
+            lows[n][...] = low_rank(folded[n] + kept)
+
+    middle = (a == 1) | (a == 2)
+
+    @pl.when(middle)
+    def _():
+        finish(inside)
+        adapter = adapters(capacity, columns)
+        for hop, out in zip(hops, hop_lows):
+            _, slot = id_columns(hop, capacity, capacity)
+            wide = jnp.dot(hop[:capacity, :], inside[...], preferred_element_type=jnp.float32)
+            kept = fold(jnp.where(adapter == slot, wide, 0.0))
+            rest_rows = -capacity % LANES
+            kept = jnp.concatenate([kept, jnp.zeros((rest_rows, LANES), jnp.float32)], axis=0)
+            out[...] = low_rank(kept)[:, :capacity]
+
+    @pl.when(jnp.logical_not(middle))
+    def _():
+        finish(outside)
+        for out in hop_lows:
+            out[...] = jnp.zeros(out.shape, jnp.float32)
+
+
+def merge_body(low, near, places, *refs):
+    hops, out = refs[:-1], refs[-1]
+    back = hops[0][...]
+    for hop in hops[1:]:
+        back = back + hop[...]
+    spread = jnp.zeros(low.shape, jnp.float32)
+    for _ in range(3):
+        piece = back.astype(jnp.bfloat16)
+        back = back - piece.astype(jnp.float32)
+        spread = spread + jnp.dot(piece, places[...], preferred_element_type=jnp.float32)
+    out[...] = low[...] + near[...] + spread
+
+
+def ups_body(own, *refs):
+    g = lax.axis_index("groups")
+    blocks, out = refs[:-1], refs[-1]
+    columns, keys = own.shape
+    out[:columns, :] = own[...]
+    size = columns // len(blocks)
+    count = blocks[0].shape[1] // keys
+    for n, block in enumerate(blocks):
+        half = g if n == 0 else 1 - g
+        height = block.shape[0] // (OWNERS - 1)
+        for i in range(OWNERS - 1):
+            for k in range(count):
+                start = (i + 1) * columns + half * size + k * height
+                start = pl.multiple_of(start, height)
+                out[pl.ds(start, height), :] = block[
+                    i * height : (i + 1) * height, k * keys : (k + 1) * keys
+                ]
+
+
+def finish_body(near, far, base, ids, ups, out):
+    a = lax.axis_index("adapter")
+    rows = out.shape[0]
+    columns = ups.shape[0] // OWNERS
+    column = lax.broadcasted_iota(jnp.int32, (ADAPTER_RANK, columns), 1)
+    row = lax.broadcasted_iota(jnp.int32, (ADAPTER_RANK, columns), 0)
+    repeat = (lax.rem(column, ADAPTER_RANK) == row).astype(jnp.bfloat16)
+    shrunk = (near[...] + far[...]).astype(jnp.bfloat16)
+    spread = lax.dot_general(shrunk, repeat, TN, preferred_element_type=jnp.float32)
+    adapter = lax.broadcasted_iota(jnp.int32, (rows, columns), 1) // ADAPTER_RANK
+    updates = jnp.zeros(out.shape, jnp.float32)
+    for bit in range(OWNERS):
+        wanted = ids[...] - (a ^ bit) * (columns // ADAPTER_RANK)
+        chosen = jnp.where(adapter == wanted, spread, 0.0).astype(jnp.bfloat16)
+        up = ups[bit * columns : (bit + 1) * columns, :]
+        updates = updates + jnp.dot(chosen, up, preferred_element_type=jnp.float32)
+    updates = updates.astype(jnp.bfloat16).astype(jnp.float32)
+    out[...] = (base[...] + ADAPTER_SCALE * updates).astype(jnp.bfloat16)
+
+
+def gather(
+    tokens,
+    base_key_weight,
+    stacked_down_weight,
+    stacked_up_weight,
+    request_adapter_owner,
+    request_adapter_slot,
+):
+    rows, features = tokens.shape
+    groups, _, shares = (lax.axis_size(name) for name in AXES)
+    g = lax.axis_index("groups")
+    columns = stacked_down_weight.shape[1]
+    keys = stacked_up_weight.shape[1]
+    local_adapters = columns // ADAPTER_RANK
+    part = features // groups
+    half = columns // keys
+    capacity = -(-row_limit(rows) // ID_ROWS) * ID_ROWS
+    up_rows = columns // half // groups
+
+    def shape(*dims, dtype=jnp.float32):
+        return jax.ShapeDtypeStruct(dims, dtype)
+
+    own, up_own = kernel(
+        pack_body,
+        [shape(part, columns, dtype=jnp.bfloat16), shape(up_rows, columns, dtype=jnp.bfloat16)],
+        (stacked_down_weight, stacked_up_weight),
+        (pl.ANY, pl.ANY),
+        [pltpu.SemaphoreType.DMA((half + 1,))],
+    )
+    beside = exchange(own, 0, 0, BESIDE)
+    mirror = exchange(own, 0, 0, MIDDLE)
+
+    id_rows = jnp.concatenate(
+        [request_adapter_owner.reshape(1, rows), request_adapter_slot.reshape(1, rows)], axis=0
+    ).astype(jnp.bfloat16)
+    id_rows = jnp.pad(id_rows, ((0, ID_ROWS - 2), (0, part - rows)))
+    hop_shape = shape(capacity + ID_ROWS, part, dtype=jnp.bfloat16)
+    hop_own, hop_away, places = kernel(
+        functools.partial(hop_body, capacity),
+        [hop_shape, hop_shape, shape(capacity, rows, dtype=jnp.bfloat16)],
+        (tokens, id_rows),
+    )
+    hop_parts = [hop_own, exchange(hop_away, 1, 0, SAME)]
+    token_parts = []
+    for step in range(groups):
+        taken = lax.dynamic_slice(tokens, (0, (g ^ step) * part), (rows, part))
+        taken = after(jnp.concatenate([taken, id_rows], axis=0), hop_away)
+        token_parts.append(exchange(taken, step, 0, SAME) if step else taken)
+
+    up_parts = [exchange(up_own, 0, 0, to) for to in (BESIDE, ACROSS, MIRROR)]
+    up_parts = jnp.concatenate(up_parts, axis=0)
+    ups = kernel(
+        ups_body,
+        shape(OWNERS * columns, keys, dtype=jnp.bfloat16),
+        (stacked_up_weight, up_parts, exchange(up_parts, 1, 0, SAME)),
+    )
+
+    bases = kernel(
+        functools.partial(base_body, keys),
+        shape(shares, rows, keys),
+        (tokens, base_key_weight),
+    )
+    bases = lax.all_to_all(bases, "mp", 0, 0, tiled=True)
+
+    inside = exchange(beside, 0, 0, MIDDLE)
+    outside = exchange(mirror, 0, 0, OUTWARD)
+    hops = [exchange(after(x, beside), 0, 0, INWARD) for x in hop_parts]
+
+    folded, mask, base = kernel(
+        functools.partial(early_body, (0, 1, 3), part, rows),
+        [shape(groups, rows, LANES), shape(groups, rows, columns), shape(rows, keys)],
+        (*token_parts, own, beside, mirror, bases),
+    )
+    low_shape, hop_low_shape = shape(ADAPTER_RANK, rows), shape(ADAPTER_RANK, capacity)
+    low, low_away, back, back_away = kernel(
+        functools.partial(last_body, part, rows, capacity),
+        [low_shape] * groups + [hop_low_shape] * groups,
+        (*token_parts, *hops, folded, mask, inside, outside),
+    )
+
+    near = exchange(low_away, 1, 0, SAME)
+    back = exchange(back, 0, 0, OUTWARD)
+    back_away = exchange(back_away, 1, 0, OUTWARD)
+    low = kernel(merge_body, low_shape, (low, near, places, back, back_away))
+    bit = shares // 2
+    while bit > 1:
+        low = low + exchange(low, 0, bit, SAME)
+        bit //= 2
+    low_far = exchange(low, 0, 1, SAME)
+
+    ids = request_adapter_owner * local_adapters + request_adapter_slot.reshape(rows, 1)
+    return kernel(finish_body, shape(rows, keys, dtype=jnp.bfloat16), (low, low_far, base, ids, ups))
+
+
+def row_limit(rows):
+    return max(2, 3 * rows // (2 * lax.axis_size("adapter")))
+
+
+def local(*args):
+    rows, columns = args[0].shape[0], args[2].shape[1]
+    groups, owners, shares = (lax.axis_size(name) for name in AXES)
+    fits = owners == OWNERS and groups == 2 and shares > 1 and shares & (shares - 1) == 0
+    travels = fits and columns <= groups * row_limit(rows)
+    return (gather if travels else dispatch)(*args)
+
+
 def solution(mesh):
     placed = (
         P(("groups", "adapter"), "mp"),

time: 131 us -> 78.3 us (0.60)
  blocking collectives: 25.7 us -> 0 us
  waiting for transfers between devices: 49.7 us -> 26.6 us
  starting transfers between devices: 14.5 us -> 31 us
  between operations: 13.5 us -> 0.2 us
  Pallas kernels: 0 us -> 10.3 us
  matrix products: 8.59 us -> 0 us
  local copies, waits for them, and re-layouts: 14.4 us -> 7.16 us
  other arithmetic: 4.22 us -> 2.49 us
    all_to_all x3 -> x1, waiting for transfers between devices: 49.7 us -> 0.01 us  [gather(): bases = lax.all_to_all(bases, 'mp', 0, 0, tiled=True)]
    ppermute x0 -> x17, starting transfers between devices: none -> 27.5 us  [exchange(): return lax.ppermute(x, AXES, pairs)]
    ppermute x0 -> x17, waiting for transfers between devices: none -> 26.6 us  [exchange(): return lax.ppermute(x, AXES, pairs)]
    all_gather x1 -> x0, blocking collectives: 14.4 us -> none  [local(): lax.all_gather(stacked_up_weight, 'adapter', axis=0, tiled=True)]
    psum x1 -> x0, blocking collectives: 11.3 us -> none  [local(): shrunk = lax.psum(partial_low, 'mp')]
    all_to_all x3 -> x1, starting transfers between devices: 14.5 us -> 3.49 us  [gather(): bases = lax.all_to_all(bases, 'mp', 0, 0, tiled=True)]
    pallas_call x0 -> x8, Pallas kernels: none -> 10.3 us  [kernel(): pl.pallas_call(body, out_shape=outs, in_specs=specs or [inner] * len(oper...]
    dot_general x3 -> x0, matrix products: 8.59 us -> none  [the longest x1 3.68 us: local(): lax.dot_general(base_key_weight, tokens, (((0,), (1,)), ((), ())), prefer...]
  transfers between devices with their start and end apart: 4 -> 18, of which waited for: 2 -> 6; matrix products, arithmetic and copies ran while one was open for 14% -> 8% of each run, Pallas kernels for 0% -> 11%
where the time goes in v4:
time: 78.3 us; the launch traced here: 77.8 us
  starting transfers between devices  31 us (40%)
  waiting for transfers between devices  26.6 us (34%)
  Pallas kernels  10.3 us (13%)
  local copies, waits for them, and re-layouts  7.16 us (9%)
  other arithmetic  2.49 us (3%)
    ppermute x17, starting transfers between devices, exchange(): return lax.ppermute(x, AXES, pairs)  27.5 us
    ppermute x17, waiting for transfers between devices, exchange(): return lax.ppermute(x, AXES, pairs)  26.6 us
    pallas_call x8, Pallas kernels, kernel(): pl.pallas_call(body, out_shape=outs, in_specs=specs or [inner] * len(oper...  10.3 us
    unnamed x24, local copies, waits for them, and re-layouts  4.9 us
    all_to_all x1, starting transfers between devices, gather(): bases = lax.all_to_all(bases, 'mp', 0, 0, tiled=True)  3.49 us
  transfers between devices with their start and end apart: 18, of which 6 were waited for; matrix products, arithmetic and copies ran while one was open for 8% of the time, Pallas kernels for 11%

profile of v4, /device:TPU:0, one launch (start us, length us, event | category | flops | bytes accessed | tf_op | source)
XLA Modules:
  0.0 77.8 jit_solution(11171593032311261699)
XLA Ops:
  0.0 1.2 %copy-done.3 = bf16[2048,256]{1,0:T(8,128)(2,1)S(1)} copy-done((bf16[2048,256]{1,0:T(8,128)(2,1)S(1)}, bf16[2048,256]{1,0:T(8,128)(2,1)}, u32[]{:S(2)}) %copy-start.3) | copy-done | bytes 1048600
  1.2 0.8 %copy-done.4 = bf16[256,128]{1,0:T(8,128)(2,1)S(1)} copy-done((bf16[256,128]{1,0:T(8,128)(2,1)S(1)}, bf16[256,128]{1,0:T(8,128)(2,1)}, u32[]{:S(2)}) %copy-start.4) | copy-done | bytes 65560
  2.1 0.9 %shard_map.65 = (bf16[1024,256]{1,0:T(8,128)(2,1)}, bf16[64,256]{1,0:T(8,128)(2,1)S(1)}) custom-call(bf16[2048,256]{1,0:T(8,128)(2,1)S(1)} %copy-done.3, bf16[256,128]{1,0:T(8,128)(2,1)S(1)} %copy-done.4), custom_call_target="tpu_custom_call" | custom-call | tf_op jit(solution)/shard_map/pallas_call | solution.py:114
  2.9 0.0 copy-start
  3.0 3.1 %collective-permute-start.1 = (bf16[1024,256]{1,0:T(8,128)(2,1)}, bf16[1024,256]{1,0:T(8,128)(2,1)}, u32[]{:S(2)}, u32[]{:S(2)}) collective-permute-start(bf16[1024,256]{1,0:T(8,128)(2,1)} %get-tuple-element.25.refs_2_), channel_id=1, source_target_pairs={{0,4},{1,5},{2,6},{3,7},{4,0},{5,1},{6,2},{7,3},{8,12},{9,13},{10,... | collective-permute-start | bytes 1572872 | tf_op jit(solution)/shard_map/ppermute | solution.py:95
  6.0 1.5 %collective-permute-start.5 = (bf16[1024,256]{1,0:T(8,128)(2,1)}, bf16[1024,256]{1,0:T(8,128)(2,1)}, u32[]{:S(2)}, u32[]{:S(2)}) collective-permute-start(bf16[1024,256]{1,0:T(8,128)(2,1)} %get-tuple-element.25.refs_2_), channel_id=1, source_target_pairs={{4,8},{5,9},{6,10},{7,11},{8,4},{9,5},{10,6},{11,7},{20,24},{21,25... | collective-permute-start | bytes 1572872 | tf_op jit(solution)/shard_map/ppermute | solution.py:95
  7.5 0.7 convert.9
  8.2 0.8 reshape_add_fusion
  9.0 1.5 %constant_dynamic-slice_fusion = (bf16[384,1024]{1,0:T(8,128)(2,1)S(1)}, bf16[384,1024]{1,0:T(8,128)(2,1)S(1)}) fusion(bf16[384,2048]{1,0:T(8,128)(2,1)} %tokens.3, s32[]{:T(128)S(6)} %select_n.7, s32[]{:T(128)S(6)} %select_n.6), kind=kLoop, calls=%fused_computation.15 | loop fusion | bytes 3145736 | tf_op jit(solution)/shard_map/dynamic_slice | solution.py:366
  10.5 1.4 %shard_map.64 = (bf16[160,1024]{1,0:T(8,128)(2,1)S(1)}, bf16[160,1024]{1,0:T(8,128)(2,1)}, bf16[144,384]{1,0:T(8,128)(2,1)S(1)}) custom-call(bf16[384,2048]{1,0:T(8,128)(2,1)S(1)} %copy-done, bf16[16,1024]{1,0:T(8,128)(2,1)S(1)} %fusion.5.id_rows), custom_call_target="tpu_custom_call" | custom-call | tf_op jit(solution)/shard_map/pallas_call | solution.py:114
  11.9 1.0 %pad_maximum_fusion = (bf16[400,1024]{1,0:T(8,128)(2,1)}, bf16[400,1024]{1,0:T(8,128)(2,1)S(1)}) fusion(bf16[16,1024]{1,0:T(8,128)(2,1)S(1)} %fusion.5.id_rows, bf16[384,1024]{1,0:T(8,128)(2,1)S(1)} %get-tuple-element.37, bf16[384,1024]{1,0:T(8,128)(2,1)S(1)} %get-tuple-element.38), kind=kLoop, calls=%fused_computation | loop fusion | flops 2867200 | bytes 3244032 | tf_op jit(solution)/shard_map/concatenate | solution.py:367
  12.9 0.0 copy-done.10
  12.9 1.5 %collective-permute-start = (bf16[400,1024]{1,0:T(8,128)(2,1)}, bf16[400,1024]{1,0:T(8,128)(2,1)S(1)}, u32[]{:S(2)}, u32[]{:S(2)}) collective-permute-start(bf16[400,1024]{1,0:T(8,128)(2,1)} %get-tuple-element.23), channel_id=1, source_target_pairs={{0,16},{1,17},{2,18},{3,19},{4,20},{5,21},{6,22},{7,23},{8,24},{9,... | collective-permute-start | bytes 2457608 | tf_op jit(solution)/shard_map/ppermute | solution.py:95
  14.4 0.5 collective-permute-start.3
  15.0 1.0 %shard_map.66 = f32[4,384,128]{2,1,0:T(8,128)S(1)} custom-call(bf16[384,2048]{1,0:T(8,128)(2,1)S(1)} %copy-done, bf16[2048,512]{1,0:T(8,128)(2,1)S(1)} %copy-done.2), custom_call_target="tpu_custom_call" | custom-call | tf_op jit(solution)/shard_map/pallas_call | solution.py:114
  15.9 0.9 %copy-done.1 = f32[4,384,128]{2,1,0:T(8,128)} copy-done((f32[4,384,128]{2,1,0:T(8,128)}, f32[4,384,128]{2,1,0:T(8,128)S(1)}, u32[]{:S(2)}) %copy-start.1) | copy-done | bytes 786456
  16.8 3.5 %all-to-all-start = ((f32[4,384,128]{2,1,0:T(8,128)}), f32[4,384,128]{2,1,0:T(8,128)S(1)}, u32[]{:S(2)}, u32[]{:S(2)}) async-start(f32[4,384,128]{2,1,0:T(8,128)} %copy-done.1), calls=%async_computation | async-start | bytes 1572864 | tf_op jit(solution)/shard_map/all_to_all | solution.py:383
  20.3 0.0 collective-permute-done.1.refs_3_
  20.4 0.7 collective-permute-start.6
  21.1 1.3 %collective-permute-start.7 = (bf16[1024,256]{1,0:T(8,128)(2,1)}, bf16[1024,256]{1,0:T(8,128)(2,1)S(1)}, u32[]{:S(2)}, u32[]{:S(2)}) collective-permute-start(bf16[1024,256]{1,0:T(8,128)(2,1)} %collective-permute-done.5.refs_4_), channel_id=1, source_target_pairs={{4,0},{5,1},{6,2},{7,3},{8,12},{9,13},{10,14},{11,15},{20,16},{21,... | collective-permute-start | bytes 1572872 | tf_op jit(solution)/shard_map/ppermute | solution.py:95
  22.4 4.9 %collective-permute-start.13 = (bf16[64,256]{1,0:T(8,128)(2,1)S(1)}, bf16[64,256]{1,0:T(8,128)(2,1)S(1)}, u32[]{:S(2)}, u32[]{:S(2)}) collective-permute-start(bf16[64,256]{1,0:T(8,128)(2,1)S(1)} %get-tuple-element.36), channel_id=1, source_target_pairs={{0,4},{1,5},{2,6},{3,7},{4,0},{5,1},{6,2},{7,3},{8,12},{9,13},{10,... | collective-permute-start | bytes 98312 | tf_op jit(solution)/shard_map/ppermute | solution.py:95
  27.3 13.3 %collective-permute-done.13 = bf16[64,256]{1,0:T(8,128)(2,1)S(1)} collective-permute-done((bf16[64,256]{1,0:T(8,128)(2,1)S(1)}, bf16[64,256]{1,0:T(8,128)(2,1)S(1)}, u32[]{:S(2)}, u32[]{:S(2)}) %collective-permute-start.13) | collective-permute-done | bytes 32800 | tf_op jit(solution)/shard_map/ppermute | solution.py:95
  40.6 0.7 collective-permute-start.14
  41.3 1.9 %collective-permute-start.15 = (bf16[64,256]{1,0:T(8,128)(2,1)S(1)}, bf16[64,256]{1,0:T(8,128)(2,1)S(1)}, u32[]{:S(2)}, u32[]{:S(2)}) collective-permute-start(bf16[64,256]{1,0:T(8,128)(2,1)S(1)} %get-tuple-element.36), channel_id=1, source_target_pairs={{0,12},{1,13},{2,14},{3,15},{4,8},{5,9},{6,10},{7,11},{8,4},{9,5},... | collective-permute-start | bytes 98312 | tf_op jit(solution)/shard_map/ppermute | solution.py:95
  43.3 2.9 %collective-permute-done.14 = bf16[64,256]{1,0:T(8,128)(2,1)S(1)} collective-permute-done((bf16[64,256]{1,0:T(8,128)(2,1)S(1)}, bf16[64,256]{1,0:T(8,128)(2,1)S(1)}, u32[]{:S(2)}, u32[]{:S(2)}) %collective-permute-start.14) | collective-permute-done | bytes 32800 | tf_op jit(solution)/shard_map/ppermute | solution.py:95
  46.2 2.2 %collective-permute-start.4 = (bf16[160,1024]{1,0:T(8,128)(2,1)}, bf16[160,1024]{1,0:T(8,128)(2,1)}, u32[]{:S(2)}, u32[]{:S(2)}) collective-permute-start(bf16[160,1024]{1,0:T(8,128)(2,1)} %collective-permute-done.3), channel_id=1, source_target_pairs={{0,4},{1,5},{2,6},{3,7},{12,8},{13,9},{14,10},{15,11},{16,20},{17,... | collective-permute-start | bytes 983048 | tf_op jit(solution)/shard_map/ppermute | solution.py:95
  48.4 2.2 %collective-permute-start.2 = (bf16[160,1024]{1,0:T(8,128)(2,1)}, bf16[160,1024]{1,0:T(8,128)(2,1)}, u32[]{:S(2)}, u32[]{:S(2)}) collective-permute-start(bf16[160,1024]{1,0:T(8,128)(2,1)} %copy-done.10), channel_id=1, source_target_pairs={{0,4},{1,5},{2,6},{3,7},{12,8},{13,9},{14,10},{15,11},{16,20},{17,... | collective-permute-start | bytes 983048 | tf_op jit(solution)/shard_map/ppermute | solution.py:95
  50.6 0.6 constant_dynamic-update-slice_fusion.2
  51.2 0.6 constant_dynamic-update-slice_fusion.1
  51.8 0.6 constant_dynamic-update-slice_fusion.refs_0_
  52.4 1.5 %collective-permute-start.16 = (bf16[192,256]{1,0:T(8,128)(2,1)}, bf16[192,256]{1,0:T(8,128)(2,1)}, u32[]{:S(2)}, u32[]{:S(2)}) collective-permute-start(bf16[192,256]{1,0:T(8,128)(2,1)} %constant_dynamic-update-slice_fusion.refs_0_), channel_id=1, source_target_pairs={{0,16},{1,17},{2,18},{3,19},{4,20},{5,21},{6,22},{7,23},{8,24},{9,... | collective-permute-start | bytes 294920 | tf_op jit(solution)/shard_map/ppermute | solution.py:95
  53.9 0.0 all-to-all-done.refs_5_
  53.9 2.9 %shard_map.67 = (f32[2,384,128]{2,1,0:T(8,128)S(1)}, f32[2,384,256]{2,1,0:T(8,128)S(1)}, f32[384,128]{1,0:T(8,128)S(1)}) custom-call(bf16[400,1024]{1,0:T(8,128)(2,1)S(1)} %get-tuple-element.22.refs_0_, bf16[400,1024]{1,0:T(8,128)(2,1)S(1)} %collective-permute-done.refs_1_, bf16[1024,256]{1,0:T(8,128)(2,1)} %get-tuple-element.25.refs_2_, ...), custom_call_target="tpu_custom_call" | custom-call | tf_op jit(solution)/shard_map/pallas_call | solution.py:114
  56.9 0.7 copy-done.6
  57.5 3.3 %collective-permute-done.2.refs_2_ = bf16[160,1024]{1,0:T(8,128)(2,1)} collective-permute-done((bf16[160,1024]{1,0:T(8,128)(2,1)}, bf16[160,1024]{1,0:T(8,128)(2,1)}, u32[]{:S(2)}, u32[]{:S(2)}) %collective-permute-start.2) | collective-permute-done | bytes 327712 | tf_op jit(solution)/shard_map/ppermute | solution.py:95
  60.9 1.8 %shard_map.68 = (f32[16,384]{1,0:T(8,128)S(1)}, f32[16,384]{1,0:T(8,128)S(1)}, f32[16,144]{1,0:T(8,128)S(1)}, f32[16,144]{1,0:T(8,128)S(1)}) custom-call(bf16[400,1024]{1,0:T(8,128)(2,1)S(1)} %get-tuple-element.22.refs_0_, bf16[400,1024]{1,0:T(8,128)(2,1)S(1)} %collective-permute-done.refs_1_, bf16[160,1024]{1,0:T(8,128)(2,1)} %collective-permute-done.2.refs_2_, ...), custom_call_target="tpu_custom_call" | custom-call | tf_op jit(solution)/shard_map/pallas_call | solution.py:114
  62.7 1.6 %collective-permute-start.8 = (f32[16,384]{1,0:T(8,128)S(1)}, f32[16,384]{1,0:T(8,128)S(1)}, u32[]{:S(2)}, u32[]{:S(2)}) collective-permute-start(f32[16,384]{1,0:T(8,128)S(1)} %get-tuple-element.31), channel_id=1, source_target_pairs={{0,16},{1,17},{2,18},{3,19},{4,20},{5,21},{6,22},{7,23},{8,24},{9,... | collective-permute-start | bytes 73736 | tf_op jit(solution)/shard_map/ppermute | solution.py:95
  64.3 1.3 %collective-permute-start.10 = (f32[16,144]{1,0:T(8,128)S(1)}, f32[16,144]{1,0:T(8,128)S(1)}, u32[]{:S(2)}, u32[]{:S(2)}) collective-permute-start(f32[16,144]{1,0:T(8,128)S(1)} %get-tuple-element.34), channel_id=1, source_target_pairs={{4,16},{5,17},{6,18},{7,19},{8,28},{9,29},{10,30},{11,31},{20,0},{... | collective-permute-start | bytes 27656 | tf_op jit(solution)/shard_map/ppermute | solution.py:95
  65.6 1.3 %collective-permute-start.9 = (f32[16,144]{1,0:T(8,128)S(1)}, f32[16,144]{1,0:T(8,128)S(1)}, u32[]{:S(2)}, u32[]{:S(2)}) collective-permute-start(f32[16,144]{1,0:T(8,128)S(1)} %get-tuple-element.33), channel_id=1, source_target_pairs={{4,0},{5,1},{6,2},{7,3},{8,12},{9,13},{10,14},{11,15},{20,16},{21,... | collective-permute-start | bytes 27656 | tf_op jit(solution)/shard_map/ppermute | solution.py:95
  66.9 3.9 %collective-permute-done.10.refs_1_ = f32[16,144]{1,0:T(8,128)S(1)} collective-permute-done((f32[16,144]{1,0:T(8,128)S(1)}, f32[16,144]{1,0:T(8,128)S(1)}, u32[]{:S(2)}, u32[]{:S(2)}) %collective-permute-start.10) | collective-permute-done | bytes 9248 | tf_op jit(solution)/shard_map/ppermute | solution.py:95
  70.8 0.5 collective-permute-done.9.refs_0_
  71.3 0.2 shard_map.69
  71.5 1.3 %collective-permute-start.11 = (f32[16,384]{1,0:T(8,128)S(1)}, f32[16,384]{1,0:T(8,128)S(1)}, u32[]{:S(2)}, u32[]{:S(2)}) collective-permute-start(f32[16,384]{1,0:T(8,128)S(1)} %shard_map.69), channel_id=1, source_target_pairs={{0,2},{1,3},{2,0},{3,1},{4,6},{5,7},{6,4},{7,5},{8,10},{9,11},{10,... | collective-permute-start | bytes 73736 | tf_op jit(solution)/shard_map/ppermute | solution.py:95
  72.8 2.5 %collective-permute-done.11 = f32[16,384]{1,0:T(8,128)S(1)} collective-permute-done((f32[16,384]{1,0:T(8,128)S(1)}, f32[16,384]{1,0:T(8,128)S(1)}, u32[]{:S(2)}, u32[]{:S(2)}) %collective-permute-start.11) | collective-permute-done | bytes 24608 | tf_op jit(solution)/shard_map/ppermute | solution.py:95
  75.3 0.1 copy.12.ids
  75.5 1.0 %shard_map.70.ups = bf16[1024,128]{1,0:T(8,128)(2,1)S(1)} custom-call(bf16[256,128]{1,0:T(8,128)(2,1)S(1)} %copy-done.5, bf16[192,256]{1,0:T(8,128)(2,1)} %constant_dynamic-update-slice_fusion.refs_0_, bf16[192,256]{1,0:T(8,128)(2,1)} %collective-permute-done.16.refs_1_), custom_call_target="tpu_custom_call" | custom-call | tf_op jit(solution)/shard_map/pallas_call | solution.py:114
  76.5 0.0 collective-permute-done.12.far
  76.5 1.3 %shard_map.71 = bf16[384,128]{1,0:T(8,128)(2,1)} custom-call(f32[16,384]{1,0:T(8,128)S(1)} %add.16.near, f32[16,384]{1,0:T(8,128)S(1)} %collective-permute-done.12.far, f32[384,128]{1,0:T(8,128)S(1)} %copy-done.7, s32[384,1]{1,0:T(8,128)S(1)} %copy.12.ids, bf16[1024,128]{1,0:T(8,128)(2,1)S(1)} %shard_map.70.ups), custom_call_target="tpu_custom_call" | custom-call | tf_op jit(solution)/shard_map/pallas_call | solution.py:114
  (29 shorter events, 0.1 us)
Async XLA Ops:
  0.0 1.2 %copy-start.3 = (bf16[2048,256]{1,0:T(8,128)(2,1)S(1)}, bf16[2048,256]{1,0:T(8,128)(2,1)}, u32[]{:S(2)}) copy-start(bf16[2048,256]{1,0:T(8,128)(2,1)} %down.1) | copy-start | bytes 3145732
  1.2 0.8 %copy-start.4 = (bf16[256,128]{1,0:T(8,128)(2,1)S(1)}, bf16[256,128]{1,0:T(8,128)(2,1)}, u32[]{:S(2)}) copy-start(bf16[256,128]{1,0:T(8,128)(2,1)} %own.1) | copy-start | bytes 196612
  2.9 7.5 %copy-start = (bf16[384,2048]{1,0:T(8,128)(2,1)S(1)}, bf16[384,2048]{1,0:T(8,128)(2,1)}, u32[]{:S(2)}) copy-start(bf16[384,2048]{1,0:T(8,128)(2,1)} %tokens.3) | copy-start | bytes 4718596
  3.0 17.4 %collective-permute-start.1 = (bf16[1024,256]{1,0:T(8,128)(2,1)}, bf16[1024,256]{1,0:T(8,128)(2,1)}, u32[]{:S(2)}, u32[]{:S(2)}) collective-permute-start(bf16[1024,256]{1,0:T(8,128)(2,1)} %get-tuple-element.25.refs_2_), channel_id=1, source_target_pairs={{0,4},{1,5},{2,6},{3,7},{4,0},{5,1},{6,2},{7,3},{8,12},{9,13},{10,... | collective-permute-start | bytes 1572872 | tf_op jit(solution)/shard_map/ppermute | solution.py:95
  6.0 15.0 %collective-permute-start.5 = (bf16[1024,256]{1,0:T(8,128)(2,1)}, bf16[1024,256]{1,0:T(8,128)(2,1)}, u32[]{:S(2)}, u32[]{:S(2)}) collective-permute-start(bf16[1024,256]{1,0:T(8,128)(2,1)} %get-tuple-element.25.refs_2_), channel_id=1, source_target_pairs={{4,8},{5,9},{6,10},{7,11},{8,4},{9,5},{10,6},{11,7},{20,24},{21,25... | collective-permute-start | bytes 1572872 | tf_op jit(solution)/shard_map/ppermute | solution.py:95
  11.9 1.0 %copy-start.8 = (bf16[144,384]{1,0:T(8,128)(2,1)}, bf16[144,384]{1,0:T(8,128)(2,1)S(1)}, u32[]{:S(2)}) copy-start(bf16[144,384]{1,0:T(8,128)(2,1)S(1)} %get-tuple-element.32.places) | copy-start | bytes 331780
  11.9 1.0 %copy-start.10 = (bf16[160,1024]{1,0:T(8,128)(2,1)}, bf16[160,1024]{1,0:T(8,128)(2,1)S(1)}, u32[]{:S(2)}) copy-start(bf16[160,1024]{1,0:T(8,128)(2,1)S(1)} %get-tuple-element.26) | copy-start | bytes 983044
  11.9 3.1 %copy-start.2 = (bf16[2048,512]{1,0:T(8,128)(2,1)S(1)}, bf16[2048,512]{1,0:T(8,128)(2,1)}, u32[]{:S(2)}) copy-start(bf16[2048,512]{1,0:T(8,128)(2,1)} %weights.1) | copy-start | bytes 6291460
  12.9 39.5 %collective-permute-start = (bf16[400,1024]{1,0:T(8,128)(2,1)}, bf16[400,1024]{1,0:T(8,128)(2,1)S(1)}, u32[]{:S(2)}, u32[]{:S(2)}) collective-permute-start(bf16[400,1024]{1,0:T(8,128)(2,1)} %get-tuple-element.23), channel_id=1, source_target_pairs={{0,16},{1,17},{2,18},{3,19},{4,20},{5,21},{6,22},{7,23},{8,24},{9,... | collective-permute-start | bytes 2457608 | tf_op jit(solution)/shard_map/ppermute | solution.py:95
  14.4 26.9 %collective-permute-start.3 = (bf16[160,1024]{1,0:T(8,128)(2,1)}, bf16[160,1024]{1,0:T(8,128)(2,1)}, u32[]{:S(2)}, u32[]{:S(2)}) collective-permute-start(bf16[160,1024]{1,0:T(8,128)(2,1)} %get-tuple-element.21), channel_id=1, source_target_pairs={{0,16},{1,17},{2,18},{3,19},{4,20},{5,21},{6,22},{7,23},{8,24},{9,... | collective-permute-start | bytes 983048 | tf_op jit(solution)/shard_map/ppermute | solution.py:95
  15.9 0.9 %copy-start.1 = (f32[4,384,128]{2,1,0:T(8,128)}, f32[4,384,128]{2,1,0:T(8,128)S(1)}, u32[]{:S(2)}) copy-start(f32[4,384,128]{2,1,0:T(8,128)S(1)} %shard_map.66) | copy-start | bytes 2359300
  16.8 37.1 %all-to-all-start = ((f32[4,384,128]{2,1,0:T(8,128)}), f32[4,384,128]{2,1,0:T(8,128)S(1)}, u32[]{:S(2)}, u32[]{:S(2)}) async-start(f32[4,384,128]{2,1,0:T(8,128)} %copy-done.1), calls=%async_computation | async-start | bytes 1572864 | tf_op jit(solution)/shard_map/all_to_all | solution.py:383
  20.4 40.5 %collective-permute-start.6 = (bf16[1024,256]{1,0:T(8,128)(2,1)}, bf16[1024,256]{1,0:T(8,128)(2,1)S(1)}, u32[]{:S(2)}, u32[]{:S(2)}) collective-permute-start(bf16[1024,256]{1,0:T(8,128)(2,1)} %collective-permute-done.1.refs_3_), channel_id=1, source_target_pairs={{4,8},{5,9},{6,10},{7,11},{8,4},{9,5},{10,6},{11,7},{20,24},{21,25... | collective-permute-start | bytes 1572872 | tf_op jit(solution)/shard_map/ppermute | solution.py:95
  21.1 39.8 %collective-permute-start.7 = (bf16[1024,256]{1,0:T(8,128)(2,1)}, bf16[1024,256]{1,0:T(8,128)(2,1)S(1)}, u32[]{:S(2)}, u32[]{:S(2)}) collective-permute-start(bf16[1024,256]{1,0:T(8,128)(2,1)} %collective-permute-done.5.refs_4_), channel_id=1, source_target_pairs={{4,0},{5,1},{6,2},{7,3},{8,12},{9,13},{10,14},{11,15},{20,16},{21,... | collective-permute-start | bytes 1572872 | tf_op jit(solution)/shard_map/ppermute | solution.py:95
  22.4 18.2 %collective-permute-start.13 = (bf16[64,256]{1,0:T(8,128)(2,1)S(1)}, bf16[64,256]{1,0:T(8,128)(2,1)S(1)}, u32[]{:S(2)}, u32[]{:S(2)}) collective-permute-start(bf16[64,256]{1,0:T(8,128)(2,1)S(1)} %get-tuple-element.36), channel_id=1, source_target_pairs={{0,4},{1,5},{2,6},{3,7},{4,0},{5,1},{6,2},{7,3},{8,12},{9,13},{10,... | collective-permute-start | bytes 98312 | tf_op jit(solution)/shard_map/ppermute | solution.py:95
  40.6 5.6 %collective-permute-start.14 = (bf16[64,256]{1,0:T(8,128)(2,1)S(1)}, bf16[64,256]{1,0:T(8,128)(2,1)S(1)}, u32[]{:S(2)}, u32[]{:S(2)}) collective-permute-start(bf16[64,256]{1,0:T(8,128)(2,1)S(1)} %get-tuple-element.36), channel_id=1, source_target_pairs={{0,8},{1,9},{2,10},{3,11},{4,12},{5,13},{6,14},{7,15},{8,0},{9,1},... | collective-permute-start | bytes 98312 | tf_op jit(solution)/shard_map/ppermute | solution.py:95
  41.3 7.0 %collective-permute-start.15 = (bf16[64,256]{1,0:T(8,128)(2,1)S(1)}, bf16[64,256]{1,0:T(8,128)(2,1)S(1)}, u32[]{:S(2)}, u32[]{:S(2)}) collective-permute-start(bf16[64,256]{1,0:T(8,128)(2,1)S(1)} %get-tuple-element.36), channel_id=1, source_target_pairs={{0,12},{1,13},{2,14},{3,15},{4,8},{5,9},{6,10},{7,11},{8,4},{9,5},... | collective-permute-start | bytes 98312 | tf_op jit(solution)/shard_map/ppermute | solution.py:95
  46.2 11.3 %collective-permute-start.4 = (bf16[160,1024]{1,0:T(8,128)(2,1)}, bf16[160,1024]{1,0:T(8,128)(2,1)}, u32[]{:S(2)}, u32[]{:S(2)}) collective-permute-start(bf16[160,1024]{1,0:T(8,128)(2,1)} %collective-permute-done.3), channel_id=1, source_target_pairs={{0,4},{1,5},{2,6},{3,7},{12,8},{13,9},{14,10},{15,11},{16,20},{17,... | collective-permute-start | bytes 983048 | tf_op jit(solution)/shard_map/ppermute | solution.py:95
  48.4 12.5 %collective-permute-start.2 = (bf16[160,1024]{1,0:T(8,128)(2,1)}, bf16[160,1024]{1,0:T(8,128)(2,1)}, u32[]{:S(2)}, u32[]{:S(2)}) collective-permute-start(bf16[160,1024]{1,0:T(8,128)(2,1)} %copy-done.10), channel_id=1, source_target_pairs={{0,4},{1,5},{2,6},{3,7},{12,8},{13,9},{14,10},{15,11},{16,20},{17,... | collective-permute-start | bytes 983048 | tf_op jit(solution)/shard_map/ppermute | solution.py:95
  52.4 23.0 %collective-permute-start.16 = (bf16[192,256]{1,0:T(8,128)(2,1)}, bf16[192,256]{1,0:T(8,128)(2,1)}, u32[]{:S(2)}, u32[]{:S(2)}) collective-permute-start(bf16[192,256]{1,0:T(8,128)(2,1)} %constant_dynamic-update-slice_fusion.refs_0_), channel_id=1, source_target_pairs={{0,16},{1,17},{2,18},{3,19},{4,20},{5,21},{6,22},{7,23},{8,24},{9,... | collective-permute-start | bytes 294920 | tf_op jit(solution)/shard_map/ppermute | solution.py:95
  56.8 0.7 copy-start.6
  60.9 10.4 %copy-start.9 = (bf16[144,384]{1,0:T(8,128)(2,1)S(1)}, bf16[144,384]{1,0:T(8,128)(2,1)}, u32[]{:S(2)}) copy-start(bf16[144,384]{1,0:T(8,128)(2,1)} %copy-done.8) | copy-start | bytes 331780
  60.9 14.6 %copy-start.5 = (bf16[256,128]{1,0:T(8,128)(2,1)S(1)}, bf16[256,128]{1,0:T(8,128)(2,1)}, u32[]{:S(2)}) copy-start(bf16[256,128]{1,0:T(8,128)(2,1)} %own.1) | copy-start | bytes 196612
  60.9 15.6 %copy-start.7 = (f32[384,128]{1,0:T(8,128)S(1)}, f32[384,128]{1,0:T(8,128)}, u32[]{:S(2)}) copy-start(f32[384,128]{1,0:T(8,128)} %copy-done.6) | copy-start | bytes 589828
  62.7 8.6 %collective-permute-start.8 = (f32[16,384]{1,0:T(8,128)S(1)}, f32[16,384]{1,0:T(8,128)S(1)}, u32[]{:S(2)}, u32[]{:S(2)}) collective-permute-start(f32[16,384]{1,0:T(8,128)S(1)} %get-tuple-element.31), channel_id=1, source_target_pairs={{0,16},{1,17},{2,18},{3,19},{4,20},{5,21},{6,22},{7,23},{8,24},{9,... | collective-permute-start | bytes 73736 | tf_op jit(solution)/shard_map/ppermute | solution.py:95
  64.3 6.5 %collective-permute-start.10 = (f32[16,144]{1,0:T(8,128)S(1)}, f32[16,144]{1,0:T(8,128)S(1)}, u32[]{:S(2)}, u32[]{:S(2)}) collective-permute-start(f32[16,144]{1,0:T(8,128)S(1)} %get-tuple-element.34), channel_id=1, source_target_pairs={{4,16},{5,17},{6,18},{7,19},{8,28},{9,29},{10,30},{11,31},{20,0},{... | collective-permute-start | bytes 27656 | tf_op jit(solution)/shard_map/ppermute | solution.py:95
  65.6 5.7 %collective-permute-start.9 = (f32[16,144]{1,0:T(8,128)S(1)}, f32[16,144]{1,0:T(8,128)S(1)}, u32[]{:S(2)}, u32[]{:S(2)}) collective-permute-start(f32[16,144]{1,0:T(8,128)S(1)} %get-tuple-element.33), channel_id=1, source_target_pairs={{4,0},{5,1},{6,2},{7,3},{8,12},{9,13},{10,14},{11,15},{20,16},{21,... | collective-permute-start | bytes 27656 | tf_op jit(solution)/shard_map/ppermute | solution.py:95
  71.5 3.9 %collective-permute-start.11 = (f32[16,384]{1,0:T(8,128)S(1)}, f32[16,384]{1,0:T(8,128)S(1)}, u32[]{:S(2)}, u32[]{:S(2)}) collective-permute-start(f32[16,384]{1,0:T(8,128)S(1)} %shard_map.69), channel_id=1, source_target_pairs={{0,2},{1,3},{2,0},{3,1},{4,6},{5,7},{6,4},{7,5},{8,10},{9,11},{10,... | collective-permute-start | bytes 73736 | tf_op jit(solution)/shard_map/ppermute | solution.py:95
  75.3 1.2 %collective-permute-start.12 = (f32[16,384]{1,0:T(8,128)S(1)}, f32[16,384]{1,0:T(8,128)S(1)}, u32[]{:S(2)}, u32[]{:S(2)}) collective-permute-start(f32[16,384]{1,0:T(8,128)S(1)} %add.16.near), channel_id=1, source_target_pairs={{0,1},{1,0},{2,3},{3,2},{4,5},{5,4},{6,7},{7,6},{8,9},{9,8},{10,11... | collective-permute-start | bytes 73736 | tf_op jit(solution)/shard_map/ppermute | solution.py:95

commit v5 on v4

--- a/solution.py
+++ b/solution.py
@@ -121,34 +121,56 @@
     )(*operands)
 
 
-def pack_body(down, up, out, up_out, sems):
-    g = lax.axis_index("groups")
-    keys = up.shape[1]
-    part, size = out.shape[0], up_out.shape[0]
-    count = down.shape[1] // keys
-    copies = [
-        pltpu.make_async_copy(
-            down.at[pl.ds(pl.multiple_of(g * part, part), part), :], out, sems.at[count]
-        )
-    ]
-    for k in range(count):
-        start = pl.multiple_of((g * count + k) * size, size)
-        copies.append(
-            pltpu.make_async_copy(
-                up.at[pl.ds(start, size), :], up_out.at[:, pl.ds(k * keys, keys)], sems.at[k]
-            )
-        )
+def copy_all(copies):
     for copy in copies:
         copy.start()
     for copy in copies:
         copy.wait()
 
 
-def hop_body(capacity, tokens, id_rows, own, away, places):
-    a, g = lax.axis_index("adapter"), lax.axis_index("groups")
-    rows = tokens.shape[0]
+def pack_body(down, up, out, ups_out, sems):
+    g = lax.axis_index("groups")
+    keys = up.shape[1]
+    part, size = out.shape[0], ups_out.shape[1]
+    count = down.shape[1] // keys
+    mine = down.at[pl.ds(pl.multiple_of(g * part, part), part), :]
+    copies = [pltpu.make_async_copy(mine, out, sems.at[0])]
+    for i in range(ups_out.shape[0]):
+        for k in range(count):
+            start = pl.multiple_of((g * count + k) * size, size)
+            copies.append(
+                pltpu.make_async_copy(
+                    up.at[pl.ds(start, size), :],
+                    ups_out.at[i, :, pl.ds(k * keys, keys)],
+                    sems.at[1 + i * count + k],
+                )
+            )
+    copy_all(copies)
+
+
+def split_body(tokens, owner, slot, own, away, sems):
+    g = lax.axis_index("groups")
+    rows, part = tokens.shape[0], own.shape[1]
+    copies = []
+    for n, (out, half) in enumerate(((own, g), (away, 1 - g))):
+        taken = tokens.at[:, pl.ds(pl.multiple_of(half * part, part), part)]
+        copies.append(pltpu.make_async_copy(taken, out.at[pl.ds(0, rows), :], sems.at[n]))
+    for copy in copies:
+        copy.start()
+    row = lax.broadcasted_iota(jnp.int32, (ID_ROWS, rows), 0)
+    ids = jnp.where(row == 0, owner[...], jnp.where(row == 1, slot[...], 0))
+    ids = ids.astype(jnp.float32).astype(jnp.bfloat16)
+    for out in (own, away):
+        out[rows:, :rows] = ids
+        out[rows:, rows:] = jnp.zeros((ID_ROWS, part - rows), jnp.bfloat16)
+    for copy in copies:
+        copy.wait()
+
+
+def hop_body(rows, capacity, own, away, own_out, away_out, places):
+    a = lax.axis_index("adapter")
     part = own.shape[1]
-    ids = id_rows[:, :rows]
+    ids = own[rows:, :rows]
     match = (ids.astype(jnp.float32) == (OWNERS - 1 - a).astype(jnp.float32)).astype(jnp.bfloat16)
     earlier = lax.broadcasted_iota(jnp.int32, (rows, rows), 0) < lax.broadcasted_iota(
         jnp.int32, (rows, rows), 1
@@ -159,9 +181,8 @@
     chosen = taken.astype(jnp.bfloat16)
     places[...] = chosen
     kept = lax.dot_general(ids, chosen, NT, preferred_element_type=jnp.float32)
-    for out, half in ((own, g), (away, 1 - g)):
-        block = tokens[:, pl.ds(pl.multiple_of(half * part, part), part)]
-        packed = jnp.dot(chosen, block, preferred_element_type=jnp.float32)
+    for tokens, out in ((own, own_out), (away, away_out)):
+        packed = jnp.dot(chosen, tokens[:rows, :], preferred_element_type=jnp.float32)
         out[:capacity, :] = packed.astype(jnp.bfloat16)
         out[capacity:, :] = jnp.zeros((ID_ROWS, part), jnp.bfloat16)
         out[capacity:, :capacity] = kept.astype(jnp.bfloat16)
@@ -212,7 +233,7 @@
     groups = lax.axis_size("groups")
     a = lax.axis_index("adapter")
     token_refs, rest = refs[:groups], refs[groups:]
-    blocks, (bases, folded, mask, base) = rest[: len(bits)], rest[len(bits) :]
+    blocks, (bases, folded, mask, numbers, base) = rest[: len(bits)], rest[len(bits) :]
     columns = blocks[0].shape[1]
     total = bases[0]
     for k in range(1, bases.shape[0]):
@@ -221,6 +242,8 @@
     adapter = adapters(rows, columns)
     for n, tokens in enumerate(token_refs):
         owner, slot = id_columns(tokens, rows, rows)
+        if n == 0:
+            numbers[...] = owner * (columns // ADAPTER_RANK) + slot
         right = adapter == slot
         picked = jnp.zeros((rows, columns), jnp.float32)
         for bit, block in zip(bits, blocks):
@@ -279,27 +302,19 @@
     out[...] = low[...] + near[...] + spread
 
 
-def ups_body(own, *refs):
+def ups_body(mine, other, out):
     g = lax.axis_index("groups")
-    blocks, out = refs[:-1], refs[-1]
-    columns, keys = own.shape
-    out[:columns, :] = own[...]
-    size = columns // len(blocks)
-    count = blocks[0].shape[1] // keys
-    for n, block in enumerate(blocks):
-        half = g if n == 0 else 1 - g
-        height = block.shape[0] // (OWNERS - 1)
-        for i in range(OWNERS - 1):
+    owners, height, wide = mine.shape
+    keys = out.shape[1]
+    count = wide // keys
+    for block, half in ((mine, g), (other, 1 - g)):
+        for i in range(owners):
             for k in range(count):
-                start = (i + 1) * columns + half * size + k * height
-                start = pl.multiple_of(start, height)
-                out[pl.ds(start, height), :] = block[
-                    i * height : (i + 1) * height, k * keys : (k + 1) * keys
-                ]
-
-
-def finish_body(near, far, base, ids, ups, out):
-    a = lax.axis_index("adapter")
+                start = pl.multiple_of(((2 * i + half) * count + k) * height, height)
+                out[pl.ds(start, height), :] = block[i][:, k * keys : (k + 1) * keys]
+
+
+def finish_body(near, far, base, numbers, ups, out):
     rows = out.shape[0]
     columns = ups.shape[0] // OWNERS
     column = lax.broadcasted_iota(jnp.int32, (ADAPTER_RANK, columns), 1)
@@ -307,12 +322,12 @@
     repeat = (lax.rem(column, ADAPTER_RANK) == row).astype(jnp.bfloat16)
     shrunk = (near[...] + far[...]).astype(jnp.bfloat16)
     spread = lax.dot_general(shrunk, repeat, TN, preferred_element_type=jnp.float32)
-    adapter = lax.broadcasted_iota(jnp.int32, (rows, columns), 1) // ADAPTER_RANK
+    adapter = adapters(rows, columns)
     updates = jnp.zeros(out.shape, jnp.float32)
-    for bit in range(OWNERS):
-        wanted = ids[...] - (a ^ bit) * (columns // ADAPTER_RANK)
+    for i in range(OWNERS):
+        wanted = numbers[...] - float(i * (columns // ADAPTER_RANK))
         chosen = jnp.where(adapter == wanted, spread, 0.0).astype(jnp.bfloat16)
-        up = ups[bit * columns : (bit + 1) * columns, :]
+        up = ups[i * columns : (i + 1) * columns, :]
         updates = updates + jnp.dot(chosen, up, preferred_element_type=jnp.float32)
     updates = updates.astype(jnp.bfloat16).astype(jnp.float32)
     out[...] = (base[...] + ADAPTER_SCALE * updates).astype(jnp.bfloat16)
@@ -327,89 +342,82 @@
     request_adapter_slot,
 ):
     rows, features = tokens.shape
-    groups, _, shares = (lax.axis_size(name) for name in AXES)
-    g = lax.axis_index("groups")
+    groups, owners, shares = (lax.axis_size(name) for name in AXES)
     columns = stacked_down_weight.shape[1]
     keys = stacked_up_weight.shape[1]
-    local_adapters = columns // ADAPTER_RANK
     part = features // groups
     half = columns // keys
     capacity = -(-row_limit(rows) // ID_ROWS) * ID_ROWS
     up_rows = columns // half // groups
 
-    def shape(*dims, dtype=jnp.float32):
-        return jax.ShapeDtypeStruct(dims, dtype)
+    def narrow(*dims):
+        return jax.ShapeDtypeStruct(dims, jnp.bfloat16)
+
+    def wide(*dims):
+        return jax.ShapeDtypeStruct(dims, jnp.float32)
 
     own, up_own = kernel(
         pack_body,
-        [shape(part, columns, dtype=jnp.bfloat16), shape(up_rows, columns, dtype=jnp.bfloat16)],
+        [narrow(part, columns), narrow(owners, up_rows, columns)],
         (stacked_down_weight, stacked_up_weight),
-        (pl.ANY, pl.ANY),
-        [pltpu.SemaphoreType.DMA((half + 1,))],
+        (pltpu.HBM, pltpu.HBM),
+        [pltpu.SemaphoreType.DMA((1 + half * owners,))],
     )
     beside = exchange(own, 0, 0, BESIDE)
     mirror = exchange(own, 0, 0, MIDDLE)
 
-    id_rows = jnp.concatenate(
-        [request_adapter_owner.reshape(1, rows), request_adapter_slot.reshape(1, rows)], axis=0
-    ).astype(jnp.bfloat16)
-    id_rows = jnp.pad(id_rows, ((0, ID_ROWS - 2), (0, part - rows)))
-    hop_shape = shape(capacity + ID_ROWS, part, dtype=jnp.bfloat16)
+    slot = request_adapter_slot.reshape(1, rows)
+    tok_own, tok_away = kernel(
+        split_body,
+        [narrow(rows + ID_ROWS, part)] * groups,
+        (tokens, request_adapter_owner.reshape(1, rows), after(slot, own)),
+        (pltpu.HBM, None, None),
+        [pltpu.SemaphoreType.DMA((groups,))],
+    )
+    token_parts = [tok_own, exchange(tok_away, 1, 0, SAME)]
     hop_own, hop_away, places = kernel(
-        functools.partial(hop_body, capacity),
-        [hop_shape, hop_shape, shape(capacity, rows, dtype=jnp.bfloat16)],
-        (tokens, id_rows),
-    )
-    hop_parts = [hop_own, exchange(hop_away, 1, 0, SAME)]
-    token_parts = []
-    for step in range(groups):
-        taken = lax.dynamic_slice(tokens, (0, (g ^ step) * part), (rows, part))
-        taken = after(jnp.concatenate([taken, id_rows], axis=0), hop_away)
-        token_parts.append(exchange(taken, step, 0, SAME) if step else taken)
-
-    up_parts = [exchange(up_own, 0, 0, to) for to in (BESIDE, ACROSS, MIRROR)]
-    up_parts = jnp.concatenate(up_parts, axis=0)
-    ups = kernel(
-        ups_body,
-        shape(OWNERS * columns, keys, dtype=jnp.bfloat16),
-        (stacked_up_weight, up_parts, exchange(up_parts, 1, 0, SAME)),
-    )
+        functools.partial(hop_body, rows, capacity),
+        [narrow(capacity + ID_ROWS, part)] * groups + [narrow(capacity, rows)],
+        (tok_own, tok_away),
+    )
+
+    up_half = lax.all_to_all(up_own, "adapter", 0, 0, tiled=True)
+    up_other = exchange(after(up_half, token_parts[1]), 1, 0, SAME)
+    ups = kernel(ups_body, narrow(owners * columns, keys), (up_half, up_other))
 
     bases = kernel(
-        functools.partial(base_body, keys),
-        shape(shares, rows, keys),
-        (tokens, base_key_weight),
+        functools.partial(base_body, keys), wide(shares, rows, keys), (tokens, base_key_weight)
     )
     bases = lax.all_to_all(bases, "mp", 0, 0, tiled=True)
 
-    inside = exchange(beside, 0, 0, MIDDLE)
+    inside = exchange(after(beside, places), 0, 0, MIDDLE)
     outside = exchange(mirror, 0, 0, OUTWARD)
-    hops = [exchange(after(x, beside), 0, 0, INWARD) for x in hop_parts]
-
-    folded, mask, base = kernel(
+    hops = [
+        exchange(hop_own, 0, 0, INWARD),
+        exchange(hop_away, 1, 0, INWARD),
+    ]
+
+    folded, mask, numbers, base = kernel(
         functools.partial(early_body, (0, 1, 3), part, rows),
-        [shape(groups, rows, LANES), shape(groups, rows, columns), shape(rows, keys)],
-        (*token_parts, own, beside, mirror, bases),
-    )
-    low_shape, hop_low_shape = shape(ADAPTER_RANK, rows), shape(ADAPTER_RANK, capacity)
+        [wide(groups, rows, LANES), wide(groups, rows, columns), wide(rows, 1), wide(rows, keys)],
+        (*token_parts, after(own, up_half), beside, mirror, bases),
+    )
     low, low_away, back, back_away = kernel(
         functools.partial(last_body, part, rows, capacity),
-        [low_shape] * groups + [hop_low_shape] * groups,
-        (*token_parts, *hops, folded, mask, inside, outside),
+        [wide(ADAPTER_RANK, rows)] * groups + [wide(ADAPTER_RANK, capacity)] * groups,
+        (*token_parts, *hops, after(folded, ups), mask, inside, outside),
     )
 
     near = exchange(low_away, 1, 0, SAME)
     back = exchange(back, 0, 0, OUTWARD)
     back_away = exchange(back_away, 1, 0, OUTWARD)
-    low = kernel(merge_body, low_shape, (low, near, places, back, back_away))
+    low = kernel(merge_body, wide(ADAPTER_RANK, rows), (low, near, places, back, back_away))
     bit = shares // 2
     while bit > 1:
         low = low + exchange(low, 0, bit, SAME)
         bit //= 2
     low_far = exchange(low, 0, 1, SAME)
-
-    ids = request_adapter_owner * local_adapters + request_adapter_slot.reshape(rows, 1)
-    return kernel(finish_body, shape(rows, keys, dtype=jnp.bfloat16), (low, low_far, base, ids, ups))
+    return kernel(finish_body, narrow(rows, keys), (low, low_far, base, numbers, ups))
 
 
 def row_limit(rows):

time: 78.3 us -> 72.8 us (0.930)
  waiting for transfers between devices: 26.6 us -> 19 us
  other arithmetic: 2.49 us -> 0.01 us
  Pallas kernels: 10.3 us -> 12.7 us
  local copies, waits for them, and re-layouts: 7.16 us -> 8.64 us
    ppermute x17 -> x13, waiting for transfers between devices: 26.6 us -> 15.2 us  [exchange(): return lax.ppermute(x, AXES, pairs)]
    all_to_all x0 -> x1, starting transfers between devices: none -> 4.87 us  [gather(): up_half = lax.all_to_all(up_own, 'adapter', 0, 0, tiled=True)]
    ppermute x17 -> x13, starting transfers between devices: 27.5 us -> 23.3 us  [exchange(): return lax.ppermute(x, AXES, pairs)]
    all_to_all x0 -> x1, waiting for transfers between devices: none -> 3.86 us  [gather(): up_half = lax.all_to_all(up_own, 'adapter', 0, 0, tiled=True)]
    unnamed x24 -> x22, local copies, waits for them, and re-layouts: 4.9 us -> 7.96 us
    pallas_call x8 -> x9, Pallas kernels: 10.3 us -> 12.7 us  [kernel(): pl.pallas_call(body, out_shape=outs, in_specs=specs or [inner] * len(oper...]
    dynamic_slice x1 -> x0, local copies, waits for them, and re-layouts: 1.5 us -> none  [gather(): taken = lax.dynamic_slice(tokens, (0, (g ^ step) * part), (rows, part))]
    concatenate x2 -> x0, other arithmetic: 1.04 us -> none  [the longest x1 1.03 us: gather(): taken = after(jnp.concatenate([taken, id_rows], axis=0), hop_away)]
  transfers between devices with their start and end apart: 18 -> 15, of which waited for: 6 -> 7; matrix products, arithmetic and copies ran while one was open for 8% -> 1% of each run, Pallas kernels for 11% -> 12%
where the time goes in v5:
time: 72.8 us; the launch traced here: 72.1 us
  starting transfers between devices  31.7 us (44%)
  waiting for transfers between devices  19 us (26%)
  Pallas kernels  12.7 us (17%)
  local copies, waits for them, and re-layouts  8.64 us (12%)
    ppermute x13, starting transfers between devices, exchange(): return lax.ppermute(x, AXES, pairs)  23.3 us
    ppermute x13, waiting for transfers between devices, exchange(): return lax.ppermute(x, AXES, pairs)  15.2 us
    pallas_call x9, Pallas kernels, kernel(): pl.pallas_call(body, out_shape=outs, in_specs=specs or [inner] * len(oper...  12.7 us
    unnamed x22, local copies, waits for them, and re-layouts  7.96 us
    all_to_all x1, starting transfers between devices, gather(): up_half = lax.all_to_all(up_own, 'adapter', 0, 0, tiled=True)  4.87 us
    all_to_all x1, waiting for transfers between devices, gather(): up_half = lax.all_to_all(up_own, 'adapter', 0, 0, tiled=True)  3.86 us
    all_to_all x1, starting transfers between devices, gather(): bases = lax.all_to_all(bases, 'mp', 0, 0, tiled=True)  3.49 us
  transfers between devices with their start and end apart: 15, of which 7 were waited for; matrix products, arithmetic and copies ran while one was open for 1% of the time, Pallas kernels for 12%

profile of v5, /device:TPU:0, one launch (start us, length us, event | category | flops | bytes accessed | tf_op | source)
XLA Modules:
  0.0 72.1 jit_solution(1375185603138202863)
XLA Ops:
  0.0 1.2 %copy-done.4 = bf16[2048,256]{1,0:T(8,128)(2,1)S(1)} copy-done((bf16[2048,256]{1,0:T(8,128)(2,1)S(1)}, bf16[2048,256]{1,0:T(8,128)(2,1)}, u32[]{:S(2)}) %copy-start.4) | copy-done | bytes 1048600
  1.2 0.8 %copy-done.9 = bf16[256,128]{1,0:T(8,128)(2,1)S(1)} copy-done((bf16[256,128]{1,0:T(8,128)(2,1)S(1)}, bf16[256,128]{1,0:T(8,128)(2,1)}, u32[]{:S(2)}) %copy-start.9) | copy-done | bytes 65560
  2.1 1.0 %shard_map.64 = (bf16[1024,256]{1,0:T(8,128)(2,1)}, bf16[4,64,256]{2,1,0:T(8,128)(2,1)}) custom-call(bf16[2048,256]{1,0:T(8,128)(2,1)S(1)} %copy-done.4, bf16[256,128]{1,0:T(8,128)(2,1)S(1)} %copy-done.9), custom_call_target="tpu_custom_call" | custom-call | tf_op jit(solution)/shard_map/pallas_call | solution.py:114
  3.1 3.1 %collective-permute-start.3 = (bf16[1024,256]{1,0:T(8,128)(2,1)}, bf16[1024,256]{1,0:T(8,128)(2,1)}, u32[]{:S(2)}, u32[]{:S(2)}) collective-permute-start(bf16[1024,256]{1,0:T(8,128)(2,1)} %get-tuple-element.32.refs_2_), channel_id=1, source_target_pairs={{0,4},{1,5},{2,6},{3,7},{4,0},{5,1},{6,2},{7,3},{8,12},{9,13},{10,... | collective-permute-start | bytes 1572872 | tf_op jit(solution)/shard_map/ppermute | solution.py:95
  6.2 1.5 %collective-permute-start.4 = (bf16[1024,256]{1,0:T(8,128)(2,1)}, bf16[1024,256]{1,0:T(8,128)(2,1)}, u32[]{:S(2)}, u32[]{:S(2)}) collective-permute-start(bf16[1024,256]{1,0:T(8,128)(2,1)} %get-tuple-element.32.refs_2_), channel_id=1, source_target_pairs={{4,8},{5,9},{6,10},{7,11},{8,4},{9,5},{10,6},{11,7},{20,24},{21,25... | collective-permute-start | bytes 1572872 | tf_op jit(solution)/shard_map/ppermute | solution.py:95
  7.6 0.7 reshape.7.slot
  8.3 1.4 %copy-done = bf16[384,2048]{1,0:T(8,128)(2,1)S(1)} copy-done((bf16[384,2048]{1,0:T(8,128)(2,1)S(1)}, bf16[384,2048]{1,0:T(8,128)(2,1)}, u32[]{:S(2)}) %copy-start) | copy-done | bytes 1572888
  9.7 0.7 copy-done.10
  10.4 1.1 %shard_map.65 = (bf16[400,1024]{1,0:T(8,128)(2,1)S(1)}, bf16[400,1024]{1,0:T(8,128)(2,1)}) custom-call(bf16[384,2048]{1,0:T(8,128)(2,1)S(1)} %copy-done, s32[1,384]{1,0:T(1,128)S(1)} %bitcast.1, s32[1,384]{1,0:T(1,128)S(1)} %reshape.7.slot), custom_call_target="tpu_custom_call" | custom-call | tf_op jit(solution)/shard_map/pallas_call | solution.py:114
  11.5 1.6 %collective-permute-start = (bf16[400,1024]{1,0:T(8,128)(2,1)}, bf16[400,1024]{1,0:T(8,128)(2,1)S(1)}, u32[]{:S(2)}, u32[]{:S(2)}) collective-permute-start(bf16[400,1024]{1,0:T(8,128)(2,1)} %get-tuple-element.28.away), channel_id=1, source_target_pairs={{0,16},{1,17},{2,18},{3,19},{4,20},{5,21},{6,22},{7,23},{8,24},{9,... | collective-permute-start | bytes 2457608 | tf_op jit(solution)/shard_map/ppermute | solution.py:95
  13.1 4.9 %all-to-all-start = ((bf16[4,64,256]{2,1,0:T(8,128)(2,1)}), bf16[4,64,256]{2,1,0:T(8,128)(2,1)S(1)}, u32[]{:S(2)}, u32[]{:S(2)}) async-start(bf16[4,64,256]{2,1,0:T(8,128)(2,1)} %get-tuple-element.31), calls=%async_computation | async-start | bytes 262144 | tf_op jit(solution)/shard_map/all_to_all | solution.py:384
  18.0 1.6 %copy-done.3 = bf16[2048,512]{1,0:T(8,128)(2,1)S(1)} copy-done((bf16[2048,512]{1,0:T(8,128)(2,1)S(1)}, bf16[2048,512]{1,0:T(8,128)(2,1)}, u32[]{:S(2)}) %copy-start.3) | copy-done | bytes 2097176
  19.5 1.0 %shard_map.67 = f32[4,384,128]{2,1,0:T(8,128)S(1)} custom-call(bf16[384,2048]{1,0:T(8,128)(2,1)S(1)} %copy-done.1, bf16[2048,512]{1,0:T(8,128)(2,1)S(1)} %copy-done.3), custom_call_target="tpu_custom_call" | custom-call | tf_op jit(solution)/shard_map/pallas_call | solution.py:114
  20.5 0.9 %copy-done.2 = f32[4,384,128]{2,1,0:T(8,128)} copy-done((f32[4,384,128]{2,1,0:T(8,128)}, f32[4,384,128]{2,1,0:T(8,128)S(1)}, u32[]{:S(2)}) %copy-start.2) | copy-done | bytes 786456
  21.4 3.9 %all-to-all-done.mine = bf16[4,64,256]{2,1,0:T(8,128)(2,1)S(1)} async-done(((bf16[4,64,256]{2,1,0:T(8,128)(2,1)}), bf16[4,64,256]{2,1,0:T(8,128)(2,1)S(1)}, u32[]{:S(2)}, u32[]{:S(2)}) %all-to-all-start) | async-done | bytes 131104 | tf_op jit(solution)/shard_map/all_to_all | solution.py:384
  25.3 0.7 copy-done.5
  26.0 3.5 %all-to-all-start.1 = ((f32[4,384,128]{2,1,0:T(8,128)}), f32[4,384,128]{2,1,0:T(8,128)S(1)}, u32[]{:S(2)}, u32[]{:S(2)}) async-start(f32[4,384,128]{2,1,0:T(8,128)} %copy-done.2), calls=%async_computation.1 | async-start | bytes 1572864 | tf_op jit(solution)/shard_map/all_to_all | solution.py:391
  29.5 2.5 %shard_map.66 = (bf16[160,1024]{1,0:T(8,128)(2,1)}, bf16[160,1024]{1,0:T(8,128)(2,1)}, bf16[144,384]{1,0:T(8,128)(2,1)S(1)}) custom-call(bf16[400,1024]{1,0:T(8,128)(2,1)S(1)} %get-tuple-element.27.own.refs_0_, bf16[400,1024]{1,0:T(8,128)(2,1)} %get-tuple-element.28.away), custom_call_target="tpu_custom_call" | custom-call | tf_op jit(solution)/shard_map/pallas_call | solution.py:114
  32.0 0.6 copy-done.7
  32.6 0.0 collective-permute-done.3.refs_3_
  32.6 0.7 collective-permute-start.6
  33.3 0.0 collective-permute-done.4.refs_4_
  33.3 1.3 %collective-permute-start.7 = (bf16[1024,256]{1,0:T(8,128)(2,1)}, bf16[1024,256]{1,0:T(8,128)(2,1)S(1)}, u32[]{:S(2)}, u32[]{:S(2)}) collective-permute-start(bf16[1024,256]{1,0:T(8,128)(2,1)} %collective-permute-done.4.refs_4_), channel_id=1, source_target_pairs={{4,0},{5,1},{6,2},{7,3},{8,12},{9,13},{10,14},{11,15},{20,16},{21,... | collective-permute-start | bytes 1572872 | tf_op jit(solution)/shard_map/ppermute | solution.py:95
  34.6 5.8 %collective-permute-start.1 = (bf16[160,1024]{1,0:T(8,128)(2,1)}, bf16[160,1024]{1,0:T(8,128)(2,1)}, u32[]{:S(2)}, u32[]{:S(2)}) collective-permute-start(bf16[160,1024]{1,0:T(8,128)(2,1)} %get-tuple-element.29), channel_id=1, source_target_pairs={{0,4},{1,5},{2,6},{3,7},{12,8},{13,9},{14,10},{15,11},{16,20},{17,... | collective-permute-start | bytes 983048 | tf_op jit(solution)/shard_map/ppermute | solution.py:95
  40.5 2.3 %collective-permute-start.2 = (bf16[160,1024]{1,0:T(8,128)(2,1)}, bf16[160,1024]{1,0:T(8,128)(2,1)}, u32[]{:S(2)}, u32[]{:S(2)}) collective-permute-start(bf16[160,1024]{1,0:T(8,128)(2,1)} %get-tuple-element.30), channel_id=1, source_target_pairs={{0,20},{1,21},{2,22},{3,23},{12,24},{13,25},{14,26},{15,27},{16,4}... | collective-permute-start | bytes 983048 | tf_op jit(solution)/shard_map/ppermute | solution.py:95
  42.7 0.0 collective-permute-done.refs_1_
  42.7 1.3 %collective-permute-start.5 = (bf16[4,64,256]{2,1,0:T(8,128)(2,1)}, bf16[4,64,256]{2,1,0:T(8,128)(2,1)}, u32[]{:S(2)}, u32[]{:S(2)}) collective-permute-start(bf16[4,64,256]{2,1,0:T(8,128)(2,1)} %copy-done.5), channel_id=1, source_target_pairs={{0,16},{1,17},{2,18},{3,19},{4,20},{5,21},{6,22},{7,23},{8,24},{9,... | collective-permute-start | bytes 393224 | tf_op jit(solution)/shard_map/ppermute | solution.py:95
  44.0 0.0 all-to-all-done.1.refs_5_
  44.0 2.9 %shard_map.68 = (f32[2,384,128]{2,1,0:T(8,128)S(1)}, f32[2,384,256]{2,1,0:T(8,128)S(1)}, f32[384,1]{1,0:T(8,128)S(1)}, f32[384,128]{1,0:T(8,128)S(1)}) custom-call(bf16[400,1024]{1,0:T(8,128)(2,1)S(1)} %get-tuple-element.27.own.refs_0_, bf16[400,1024]{1,0:T(8,128)(2,1)S(1)} %collective-permute-done.refs_1_, bf16[1024,256]{1,0:T(8,128)(2,1)} %get-tuple-element.32.refs_2_, ...), custom_call_target="tpu_custom_call" | custom-call | tf_op jit(solution)/shard_map/pallas_call | solution.py:114
  46.9 1.4 %collective-permute-done.5.other = bf16[4,64,256]{2,1,0:T(8,128)(2,1)} collective-permute-done((bf16[4,64,256]{2,1,0:T(8,128)(2,1)}, bf16[4,64,256]{2,1,0:T(8,128)(2,1)}, u32[]{:S(2)}, u32[]{:S(2)}) %collective-permute-start.5) | collective-permute-done | bytes 131104 | tf_op jit(solution)/shard_map/ppermute | solution.py:95
  48.3 0.9 %shard_map.69.ups = bf16[1024,128]{1,0:T(8,128)(2,1)S(1)} custom-call(bf16[4,64,256]{2,1,0:T(8,128)(2,1)S(1)} %copy-done.6, bf16[4,64,256]{2,1,0:T(8,128)(2,1)} %collective-permute-done.5.other), custom_call_target="tpu_custom_call" | custom-call | tf_op jit(solution)/shard_map/pallas_call | solution.py:114
  49.3 0.0 collective-permute-done.1.refs_2_
  49.3 5.1 %collective-permute-done.2.refs_3_ = bf16[160,1024]{1,0:T(8,128)(2,1)} collective-permute-done((bf16[160,1024]{1,0:T(8,128)(2,1)}, bf16[160,1024]{1,0:T(8,128)(2,1)}, u32[]{:S(2)}, u32[]{:S(2)}) %collective-permute-start.2) | collective-permute-done | bytes 327712 | tf_op jit(solution)/shard_map/ppermute | solution.py:95
  54.4 0.0 collective-permute-done.6.refs_6_
  54.4 0.0 collective-permute-done.7.refs_7_
  54.4 1.8 %shard_map.70 = (f32[16,384]{1,0:T(8,128)S(1)}, f32[16,384]{1,0:T(8,128)S(1)}, f32[16,144]{1,0:T(8,128)S(1)}, f32[16,144]{1,0:T(8,128)S(1)}) custom-call(bf16[400,1024]{1,0:T(8,128)(2,1)S(1)} %get-tuple-element.27.own.refs_0_, bf16[400,1024]{1,0:T(8,128)(2,1)S(1)} %collective-permute-done.refs_1_, bf16[160,1024]{1,0:T(8,128)(2,1)} %collective-permute-done.1.refs_2_, ...), custom_call_target="tpu_custom_call" | custom-call | tf_op jit(solution)/shard_map/pallas_call | solution.py:114
  56.2 1.6 %collective-permute-start.8 = (f32[16,384]{1,0:T(8,128)S(1)}, f32[16,384]{1,0:T(8,128)S(1)}, u32[]{:S(2)}, u32[]{:S(2)}) collective-permute-start(f32[16,384]{1,0:T(8,128)S(1)} %get-tuple-element.40), channel_id=1, source_target_pairs={{0,16},{1,17},{2,18},{3,19},{4,20},{5,21},{6,22},{7,23},{8,24},{9,... | collective-permute-start | bytes 73736 | tf_op jit(solution)/shard_map/ppermute | solution.py:95
  57.8 1.3 %collective-permute-start.9 = (f32[16,144]{1,0:T(8,128)S(1)}, f32[16,144]{1,0:T(8,128)S(1)}, u32[]{:S(2)}, u32[]{:S(2)}) collective-permute-start(f32[16,144]{1,0:T(8,128)S(1)} %get-tuple-element.41), channel_id=1, source_target_pairs={{4,0},{5,1},{6,2},{7,3},{8,12},{9,13},{10,14},{11,15},{20,16},{21,... | collective-permute-start | bytes 27656 | tf_op jit(solution)/shard_map/ppermute | solution.py:95
  59.0 1.3 %collective-permute-start.10 = (f32[16,144]{1,0:T(8,128)S(1)}, f32[16,144]{1,0:T(8,128)S(1)}, u32[]{:S(2)}, u32[]{:S(2)}) collective-permute-start(f32[16,144]{1,0:T(8,128)S(1)} %get-tuple-element.42), channel_id=1, source_target_pairs={{4,16},{5,17},{6,18},{7,19},{8,28},{9,29},{10,30},{11,31},{20,0},{... | collective-permute-start | bytes 27656 | tf_op jit(solution)/shard_map/ppermute | solution.py:95
  60.3 3.1 %collective-permute-done.9.refs_0_ = f32[16,144]{1,0:T(8,128)S(1)} collective-permute-done((f32[16,144]{1,0:T(8,128)S(1)}, f32[16,144]{1,0:T(8,128)S(1)}, u32[]{:S(2)}, u32[]{:S(2)}) %collective-permute-start.9) | collective-permute-done | bytes 9248 | tf_op jit(solution)/shard_map/ppermute | solution.py:95
  63.4 2.3 %collective-permute-done.10.refs_1_ = f32[16,144]{1,0:T(8,128)S(1)} collective-permute-done((f32[16,144]{1,0:T(8,128)S(1)}, f32[16,144]{1,0:T(8,128)S(1)}, u32[]{:S(2)}, u32[]{:S(2)}) %collective-permute-start.10) | collective-permute-done | bytes 9248 | tf_op jit(solution)/shard_map/ppermute | solution.py:95
  65.7 0.0 collective-permute-done.8.near
  65.7 0.2 shard_map.71
  65.8 1.7 %collective-permute-start.11 = (f32[16,384]{1,0:T(8,128)S(1)}, f32[16,384]{1,0:T(8,128)S(1)}, u32[]{:S(2)}, u32[]{:S(2)}) collective-permute-start(f32[16,384]{1,0:T(8,128)S(1)} %shard_map.71), channel_id=1, source_target_pairs={{0,2},{1,3},{2,0},{3,1},{4,6},{5,7},{6,4},{7,5},{8,10},{9,11},{10,... | collective-permute-start | bytes 73736 | tf_op jit(solution)/shard_map/ppermute | solution.py:95
  67.5 2.2 %collective-permute-done.11 = f32[16,384]{1,0:T(8,128)S(1)} collective-permute-done((f32[16,384]{1,0:T(8,128)S(1)}, f32[16,384]{1,0:T(8,128)S(1)}, u32[]{:S(2)}, u32[]{:S(2)}) %collective-permute-start.11) | collective-permute-done | bytes 24608 | tf_op jit(solution)/shard_map/ppermute | solution.py:95
  69.7 0.0 collective-permute-start.12
  69.7 1.2 %collective-permute-done.12.far = f32[16,384]{1,0:T(8,128)S(1)} collective-permute-done((f32[16,384]{1,0:T(8,128)S(1)}, f32[16,384]{1,0:T(8,128)S(1)}, u32[]{:S(2)}, u32[]{:S(2)}) %collective-permute-start.12) | collective-permute-done | bytes 24608 | tf_op jit(solution)/shard_map/ppermute | solution.py:95
  70.9 1.3 %shard_map.72 = bf16[384,128]{1,0:T(8,128)(2,1)} custom-call(f32[16,384]{1,0:T(8,128)S(1)} %add.3.near, f32[16,384]{1,0:T(8,128)S(1)} %collective-permute-done.12.far, f32[384,128]{1,0:T(8,128)S(1)} %get-tuple-element.43.base, f32[384,1]{1,0:T(8,128)S(1)} %get-tuple-element.44.numbers, bf16[1024,128]{1,0:T(8,128)(2,1)S(1)} %shard_map.69.ups), custom_call_target="tpu_custom_call" | custom-call | tf_op jit(solution)/shard_map/pallas_call | solution.py:114
  (15 shorter events, 0.0 us)
Async XLA Ops:
  0.0 1.2 %copy-start.4 = (bf16[2048,256]{1,0:T(8,128)(2,1)S(1)}, bf16[2048,256]{1,0:T(8,128)(2,1)}, u32[]{:S(2)}) copy-start(bf16[2048,256]{1,0:T(8,128)(2,1)} %down.1) | copy-start | bytes 3145732
  1.2 0.8 %copy-start.9 = (bf16[256,128]{1,0:T(8,128)(2,1)S(1)}, bf16[256,128]{1,0:T(8,128)(2,1)}, u32[]{:S(2)}) copy-start(bf16[256,128]{1,0:T(8,128)(2,1)} %up.1) | copy-start | bytes 196612
  3.1 29.6 %collective-permute-start.3 = (bf16[1024,256]{1,0:T(8,128)(2,1)}, bf16[1024,256]{1,0:T(8,128)(2,1)}, u32[]{:S(2)}, u32[]{:S(2)}) collective-permute-start(bf16[1024,256]{1,0:T(8,128)(2,1)} %get-tuple-element.32.refs_2_), channel_id=1, source_target_pairs={{0,4},{1,5},{2,6},{3,7},{4,0},{5,1},{6,2},{7,3},{8,12},{9,13},{10,... | collective-permute-start | bytes 1572872 | tf_op jit(solution)/shard_map/ppermute | solution.py:95
  6.2 27.2 %collective-permute-start.4 = (bf16[1024,256]{1,0:T(8,128)(2,1)}, bf16[1024,256]{1,0:T(8,128)(2,1)}, u32[]{:S(2)}, u32[]{:S(2)}) collective-permute-start(bf16[1024,256]{1,0:T(8,128)(2,1)} %get-tuple-element.32.refs_2_), channel_id=1, source_target_pairs={{4,8},{5,9},{6,10},{7,11},{8,4},{9,5},{10,6},{11,7},{20,24},{21,25... | collective-permute-start | bytes 1572872 | tf_op jit(solution)/shard_map/ppermute | solution.py:95
  8.3 1.4 %copy-start = (bf16[384,2048]{1,0:T(8,128)(2,1)S(1)}, bf16[384,2048]{1,0:T(8,128)(2,1)}, u32[]{:S(2)}) copy-start(bf16[384,2048]{1,0:T(8,128)(2,1)} %tokens.3) | copy-start | bytes 4718596
  9.7 0.7 copy-start.10
  10.4 7.6 %copy-start.1 = (bf16[384,2048]{1,0:T(8,128)(2,1)S(1)}, bf16[384,2048]{1,0:T(8,128)(2,1)}, u32[]{:S(2)}) copy-start(bf16[384,2048]{1,0:T(8,128)(2,1)} %tokens.3) | copy-start | bytes 4718596
  11.5 31.2 %collective-permute-start = (bf16[400,1024]{1,0:T(8,128)(2,1)}, bf16[400,1024]{1,0:T(8,128)(2,1)S(1)}, u32[]{:S(2)}, u32[]{:S(2)}) collective-permute-start(bf16[400,1024]{1,0:T(8,128)(2,1)} %get-tuple-element.28.away), channel_id=1, source_target_pairs={{0,16},{1,17},{2,18},{3,19},{4,20},{5,21},{6,22},{7,23},{8,24},{9,... | collective-permute-start | bytes 2457608 | tf_op jit(solution)/shard_map/ppermute | solution.py:95
  13.1 12.2 %all-to-all-start = ((bf16[4,64,256]{2,1,0:T(8,128)(2,1)}), bf16[4,64,256]{2,1,0:T(8,128)(2,1)S(1)}, u32[]{:S(2)}, u32[]{:S(2)}) async-start(bf16[4,64,256]{2,1,0:T(8,128)(2,1)} %get-tuple-element.31), calls=%async_computation | async-start | bytes 262144 | tf_op jit(solution)/shard_map/all_to_all | solution.py:384
  18.0 1.6 %copy-start.3 = (bf16[2048,512]{1,0:T(8,128)(2,1)S(1)}, bf16[2048,512]{1,0:T(8,128)(2,1)}, u32[]{:S(2)}) copy-start(bf16[2048,512]{1,0:T(8,128)(2,1)} %weights.1) | copy-start | bytes 6291460
  20.5 0.9 %copy-start.2 = (f32[4,384,128]{2,1,0:T(8,128)}, f32[4,384,128]{2,1,0:T(8,128)S(1)}, u32[]{:S(2)}) copy-start(f32[4,384,128]{2,1,0:T(8,128)S(1)} %shard_map.67) | copy-start | bytes 2359300
  25.3 0.7 copy-start.5
  26.0 18.0 %all-to-all-start.1 = ((f32[4,384,128]{2,1,0:T(8,128)}), f32[4,384,128]{2,1,0:T(8,128)S(1)}, u32[]{:S(2)}, u32[]{:S(2)}) async-start(f32[4,384,128]{2,1,0:T(8,128)} %copy-done.2), calls=%async_computation.1 | async-start | bytes 1572864 | tf_op jit(solution)/shard_map/all_to_all | solution.py:391
  32.0 0.6 copy-start.7
  32.6 21.7 %collective-permute-start.6 = (bf16[1024,256]{1,0:T(8,128)(2,1)}, bf16[1024,256]{1,0:T(8,128)(2,1)S(1)}, u32[]{:S(2)}, u32[]{:S(2)}) collective-permute-start(bf16[1024,256]{1,0:T(8,128)(2,1)} %collective-permute-done.3.refs_3_), channel_id=1, source_target_pairs={{4,8},{5,9},{6,10},{7,11},{8,4},{9,5},{10,6},{11,7},{20,24},{21,25... | collective-permute-start | bytes 1572872 | tf_op jit(solution)/shard_map/ppermute | solution.py:95
  33.3 21.1 %collective-permute-start.7 = (bf16[1024,256]{1,0:T(8,128)(2,1)}, bf16[1024,256]{1,0:T(8,128)(2,1)S(1)}, u32[]{:S(2)}, u32[]{:S(2)}) collective-permute-start(bf16[1024,256]{1,0:T(8,128)(2,1)} %collective-permute-done.4.refs_4_), channel_id=1, source_target_pairs={{4,0},{5,1},{6,2},{7,3},{8,12},{9,13},{10,14},{11,15},{20,16},{21,... | collective-permute-start | bytes 1572872 | tf_op jit(solution)/shard_map/ppermute | solution.py:95
  34.6 14.7 %collective-permute-start.1 = (bf16[160,1024]{1,0:T(8,128)(2,1)}, bf16[160,1024]{1,0:T(8,128)(2,1)}, u32[]{:S(2)}, u32[]{:S(2)}) collective-permute-start(bf16[160,1024]{1,0:T(8,128)(2,1)} %get-tuple-element.29), channel_id=1, source_target_pairs={{0,4},{1,5},{2,6},{3,7},{12,8},{13,9},{14,10},{15,11},{16,20},{17,... | collective-permute-start | bytes 983048 | tf_op jit(solution)/shard_map/ppermute | solution.py:95
  40.5 13.9 %collective-permute-start.2 = (bf16[160,1024]{1,0:T(8,128)(2,1)}, bf16[160,1024]{1,0:T(8,128)(2,1)}, u32[]{:S(2)}, u32[]{:S(2)}) collective-permute-start(bf16[160,1024]{1,0:T(8,128)(2,1)} %get-tuple-element.30), channel_id=1, source_target_pairs={{0,20},{1,21},{2,22},{3,23},{12,24},{13,25},{14,26},{15,27},{16,4}... | collective-permute-start | bytes 983048 | tf_op jit(solution)/shard_map/ppermute | solution.py:95
  42.7 5.6 %collective-permute-start.5 = (bf16[4,64,256]{2,1,0:T(8,128)(2,1)}, bf16[4,64,256]{2,1,0:T(8,128)(2,1)}, u32[]{:S(2)}, u32[]{:S(2)}) collective-permute-start(bf16[4,64,256]{2,1,0:T(8,128)(2,1)} %copy-done.5), channel_id=1, source_target_pairs={{0,16},{1,17},{2,18},{3,19},{4,20},{5,21},{6,22},{7,23},{8,24},{9,... | collective-permute-start | bytes 393224 | tf_op jit(solution)/shard_map/ppermute | solution.py:95
  44.0 4.4 %copy-start.6 = (bf16[4,64,256]{2,1,0:T(8,128)(2,1)S(1)}, bf16[4,64,256]{2,1,0:T(8,128)(2,1)}, u32[]{:S(2)}) copy-start(bf16[4,64,256]{2,1,0:T(8,128)(2,1)} %copy-done.5) | copy-start | bytes 393220
  54.4 11.3 %copy-start.8 = (bf16[144,384]{1,0:T(8,128)(2,1)S(1)}, bf16[144,384]{1,0:T(8,128)(2,1)}, u32[]{:S(2)}) copy-start(bf16[144,384]{1,0:T(8,128)(2,1)} %copy-done.7) | copy-start | bytes 331780
  56.2 9.5 %collective-permute-start.8 = (f32[16,384]{1,0:T(8,128)S(1)}, f32[16,384]{1,0:T(8,128)S(1)}, u32[]{:S(2)}, u32[]{:S(2)}) collective-permute-start(f32[16,384]{1,0:T(8,128)S(1)} %get-tuple-element.40), channel_id=1, source_target_pairs={{0,16},{1,17},{2,18},{3,19},{4,20},{5,21},{6,22},{7,23},{8,24},{9,... | collective-permute-start | bytes 73736 | tf_op jit(solution)/shard_map/ppermute | solution.py:95
  57.8 5.6 %collective-permute-start.9 = (f32[16,144]{1,0:T(8,128)S(1)}, f32[16,144]{1,0:T(8,128)S(1)}, u32[]{:S(2)}, u32[]{:S(2)}) collective-permute-start(f32[16,144]{1,0:T(8,128)S(1)} %get-tuple-element.41), channel_id=1, source_target_pairs={{4,0},{5,1},{6,2},{7,3},{8,12},{9,13},{10,14},{11,15},{20,16},{21,... | collective-permute-start | bytes 27656 | tf_op jit(solution)/shard_map/ppermute | solution.py:95
  59.0 6.6 %collective-permute-start.10 = (f32[16,144]{1,0:T(8,128)S(1)}, f32[16,144]{1,0:T(8,128)S(1)}, u32[]{:S(2)}, u32[]{:S(2)}) collective-permute-start(f32[16,144]{1,0:T(8,128)S(1)} %get-tuple-element.42), channel_id=1, source_target_pairs={{4,16},{5,17},{6,18},{7,19},{8,28},{9,29},{10,30},{11,31},{20,0},{... | collective-permute-start | bytes 27656 | tf_op jit(solution)/shard_map/ppermute | solution.py:95
  65.8 3.9 %collective-permute-start.11 = (f32[16,384]{1,0:T(8,128)S(1)}, f32[16,384]{1,0:T(8,128)S(1)}, u32[]{:S(2)}, u32[]{:S(2)}) collective-permute-start(f32[16,384]{1,0:T(8,128)S(1)} %shard_map.71), channel_id=1, source_target_pairs={{0,2},{1,3},{2,0},{3,1},{4,6},{5,7},{6,4},{7,5},{8,10},{9,11},{10,... | collective-permute-start | bytes 73736 | tf_op jit(solution)/shard_map/ppermute | solution.py:95
  69.7 1.2 %collective-permute-start.12 = (f32[16,384]{1,0:T(8,128)S(1)}, f32[16,384]{1,0:T(8,128)S(1)}, u32[]{:S(2)}, u32[]{:S(2)}) collective-permute-start(f32[16,384]{1,0:T(8,128)S(1)} %add.3.near), channel_id=1, source_target_pairs={{0,1},{1,0},{2,3},{3,2},{4,5},{5,4},{6,7},{7,6},{8,9},{9,8},{10,11... | collective-permute-start | bytes 73736 | tf_op jit(solution)/shard_map/ppermute | solution.py:95

commit v6 on v5

--- a/solution.py
+++ b/solution.py
@@ -97,9 +97,8 @@
 
 SAME = tuple((a, a) for a in range(OWNERS))
 BESIDE = ((0, 1), (1, 0), (2, 3), (3, 2))
-ACROSS = ((0, 2), (1, 3), (2, 0), (3, 1))
-MIRROR = ((0, 3), (1, 2), (2, 1), (3, 0))
 MIDDLE = ((1, 2), (2, 1))
+ENDS = ((0, 3), (3, 0))
 OUTWARD = ((1, 0), (2, 3))
 INWARD = ((0, 1), (3, 2))
 
@@ -108,9 +107,10 @@
     return lax.optimization_barrier((x, *others))[0]
 
 
-def kernel(body, outs, operands, spaces=None, scratch=()):
+def kernel(body, outs, operands, flops=0, spaces=None, scratch=()):
     inner = pl.BlockSpec(memory_space=pltpu.VMEM)
     specs = [inner if s is None else pl.BlockSpec(memory_space=s) for s in spaces or ()]
+    touched = sum(x.size * x.dtype.itemsize for x in jax.tree.leaves((operands, outs)))
     return pl.pallas_call(
         body,
         out_shape=outs,
@@ -118,6 +118,7 @@
         out_specs=jax.tree.map(lambda _: inner, outs),
         scratch_shapes=scratch,
         compiler_params=pltpu.CompilerParams(vmem_limit_bytes=16 * 1024 * 1024),
+        cost_estimate=pl.CostEstimate(flops=flops, bytes_accessed=touched, transcendentals=0),
     )(*operands)
 
 
@@ -128,23 +129,22 @@
         copy.wait()
 
 
-def pack_body(down, up, out, ups_out, sems):
+def pack_body(down, up, out, sems):
     g = lax.axis_index("groups")
-    keys = up.shape[1]
-    part, size = out.shape[0], ups_out.shape[1]
-    count = down.shape[1] // keys
+    columns, keys = down.shape[1], up.shape[1]
+    count = columns // keys
+    size = up.shape[0] // count
+    part = out.shape[0] - size
     mine = down.at[pl.ds(pl.multiple_of(g * part, part), part), :]
-    copies = [pltpu.make_async_copy(mine, out, sems.at[0])]
-    for i in range(ups_out.shape[0]):
-        for k in range(count):
-            start = pl.multiple_of((g * count + k) * size, size)
-            copies.append(
-                pltpu.make_async_copy(
-                    up.at[pl.ds(start, size), :],
-                    ups_out.at[i, :, pl.ds(k * keys, keys)],
-                    sems.at[1 + i * count + k],
-                )
+    copies = [pltpu.make_async_copy(mine, out.at[pl.ds(0, part), :], sems.at[count])]
+    for k in range(count):
+        copies.append(
+            pltpu.make_async_copy(
+                up.at[pl.ds(k * size, size), :],
+                out.at[pl.ds(part, size), pl.ds(k * keys, keys)],
+                sems.at[k],
             )
+        )
     copy_all(copies)
 
 
@@ -247,7 +247,7 @@
         right = adapter == slot
         picked = jnp.zeros((rows, columns), jnp.float32)
         for bit, block in zip(bits, blocks):
-            wide = jnp.dot(tokens[:rows, :], block[...], preferred_element_type=jnp.float32)
+            wide = jnp.dot(tokens[:rows, :], block[:part, :], preferred_element_type=jnp.float32)
             picked = jnp.where(owner == (a ^ bit).astype(jnp.float32), wide, picked)
         folded[n] = fold(jnp.where(right, picked, 0.0))
         mask[n] = jnp.where(owner == (a ^ 2).astype(jnp.float32), right.astype(jnp.float32), 0.0)
@@ -264,7 +264,7 @@
 
     def finish(block):
         for n, tokens in enumerate(token_refs):
-            wide = jnp.dot(tokens[:rows, :], block[...], preferred_element_type=jnp.float32)
+            wide = jnp.dot(tokens[:rows, :], block[:part, :], preferred_element_type=jnp.float32)
             kept = fold(jnp.where(mask[n] > 0, wide, 0.0))
             lows[n][...] = low_rank(folded[n] + kept)
 
@@ -276,7 +276,7 @@
         adapter = adapters(capacity, columns)
         for hop, out in zip(hops, hop_lows):
             _, slot = id_columns(hop, capacity, capacity)
-            wide = jnp.dot(hop[:capacity, :], inside[...], preferred_element_type=jnp.float32)
+            wide = jnp.dot(hop[:capacity, :], inside[:part, :], preferred_element_type=jnp.float32)
             kept = fold(jnp.where(adapter == slot, wide, 0.0))
             rest_rows = -capacity % LANES
             kept = jnp.concatenate([kept, jnp.zeros((rest_rows, LANES), jnp.float32)], axis=0)
@@ -302,19 +302,34 @@
     out[...] = low[...] + near[...] + spread
 
 
-def ups_body(mine, other, out):
-    g = lax.axis_index("groups")
-    owners, height, wide = mine.shape
-    keys = out.shape[1]
-    count = wide // keys
-    for block, half in ((mine, g), (other, 1 - g)):
-        for i in range(owners):
-            for k in range(count):
-                start = pl.multiple_of(((2 * i + half) * count + k) * height, height)
-                out[pl.ds(start, height), :] = block[i][:, k * keys : (k + 1) * keys]
+def ups_body(part, own, beside, mirror, inside, outside, distant, out):
+    a = lax.axis_index("adapter")
+    columns, keys = distant.shape
+    count = columns // keys
+    size = columns // count
+
+    def place(number, block):
+        for k in range(count):
+            start = number * columns + k * size
+            out[start : start + size, :] = block[part:, k * keys : (k + 1) * keys]
+
+    place(0, own)
+    place(1, beside)
+    middle = (a == 1) | (a == 2)
+
+    @pl.when(middle)
+    def _():
+        place(2, inside)
+        place(3, mirror)
+
+    @pl.when(jnp.logical_not(middle))
+    def _():
+        place(2, outside)
+        out[3 * columns :, :] = distant[...]
 
 
 def finish_body(near, far, base, numbers, ups, out):
+    a = lax.axis_index("adapter")
     rows = out.shape[0]
     columns = ups.shape[0] // OWNERS
     column = lax.broadcasted_iota(jnp.int32, (ADAPTER_RANK, columns), 1)
@@ -325,7 +340,7 @@
     adapter = adapters(rows, columns)
     updates = jnp.zeros(out.shape, jnp.float32)
     for i in range(OWNERS):
-        wanted = numbers[...] - float(i * (columns // ADAPTER_RANK))
+        wanted = numbers[...] - ((a ^ i) * (columns // ADAPTER_RANK)).astype(jnp.float32)
         chosen = jnp.where(adapter == wanted, spread, 0.0).astype(jnp.bfloat16)
         up = ups[i * columns : (i + 1) * columns, :]
         updates = updates + jnp.dot(chosen, up, preferred_element_type=jnp.float32)
@@ -348,7 +363,6 @@
     part = features // groups
     half = columns // keys
     capacity = -(-row_limit(rows) // ID_ROWS) * ID_ROWS
-    up_rows = columns // half // groups
 
     def narrow(*dims):
         return jax.ShapeDtypeStruct(dims, jnp.bfloat16)
@@ -356,21 +370,24 @@
     def wide(*dims):
         return jax.ShapeDtypeStruct(dims, jnp.float32)
 
-    own, up_own = kernel(
+    own = kernel(
         pack_body,
-        [narrow(part, columns), narrow(owners, up_rows, columns)],
+        narrow(part + columns // half, columns),
         (stacked_down_weight, stacked_up_weight),
+        0,
         (pltpu.HBM, pltpu.HBM),
-        [pltpu.SemaphoreType.DMA((1 + half * owners,))],
+        [pltpu.SemaphoreType.DMA((1 + half,))],
     )
     beside = exchange(own, 0, 0, BESIDE)
     mirror = exchange(own, 0, 0, MIDDLE)
+    distant = exchange(after(stacked_up_weight, own), 0, 0, ENDS)
 
     slot = request_adapter_slot.reshape(1, rows)
     tok_own, tok_away = kernel(
         split_body,
         [narrow(rows + ID_ROWS, part)] * groups,
         (tokens, request_adapter_owner.reshape(1, rows), after(slot, own)),
+        0,
         (pltpu.HBM, None, None),
         [pltpu.SemaphoreType.DMA((groups,))],
     )
@@ -379,14 +396,12 @@
         functools.partial(hop_body, rows, capacity),
         [narrow(capacity + ID_ROWS, part)] * groups + [narrow(capacity, rows)],
         (tok_own, tok_away),
-    )
-
-    up_half = lax.all_to_all(up_own, "adapter", 0, 0, tiled=True)
-    up_other = exchange(after(up_half, token_parts[1]), 1, 0, SAME)
-    ups = kernel(ups_body, narrow(owners * columns, keys), (up_half, up_other))
+        2 * capacity * rows * features,
+    )
 
     bases = kernel(
-        functools.partial(base_body, keys), wide(shares, rows, keys), (tokens, base_key_weight)
+        functools.partial(base_body, keys), wide(shares, rows, keys), (tokens, base_key_weight),
+        2 * rows * features * shares * keys,
     )
     bases = lax.all_to_all(bases, "mp", 0, 0, tiled=True)
 
@@ -400,12 +415,14 @@
     folded, mask, numbers, base = kernel(
         functools.partial(early_body, (0, 1, 3), part, rows),
         [wide(groups, rows, LANES), wide(groups, rows, columns), wide(rows, 1), wide(rows, keys)],
-        (*token_parts, after(own, up_half), beside, mirror, bases),
+        (*token_parts, own, beside, mirror, after(bases, distant)),
+        6 * groups * rows * part * columns,
     )
     low, low_away, back, back_away = kernel(
         functools.partial(last_body, part, rows, capacity),
         [wide(ADAPTER_RANK, rows)] * groups + [wide(ADAPTER_RANK, capacity)] * groups,
-        (*token_parts, *hops, after(folded, ups), mask, inside, outside),
+        (*token_parts, *hops, folded, mask, inside, outside),
+        2 * groups * (rows + capacity) * part * columns,
     )
 
     near = exchange(low_away, 1, 0, SAME)
@@ -417,6 +434,11 @@
         low = low + exchange(low, 0, bit, SAME)
         bit //= 2
     low_far = exchange(low, 0, 1, SAME)
+    ups = kernel(
+        functools.partial(ups_body, part),
+        narrow(owners * columns, keys),
+        (own, beside, mirror, inside, outside, distant),
+    )
     return kernel(finish_body, narrow(rows, keys), (low, low_far, base, numbers, ups))
 
 

time: 72.8 us -> 63 us (0.87)
  starting transfers between devices: 31.7 us -> 27.3 us
  waiting for transfers between devices: 19 us -> 16 us
  local copies, waits for them, and re-layouts: 8.64 us -> 5.77 us
    all_to_all x1 -> x0, starting transfers between devices: 4.87 us -> none  [gather(): up_half = lax.all_to_all(up_own, 'adapter', 0, 0, tiled=True)]
    all_to_all x1 -> x0, waiting for transfers between devices: 3.86 us -> none  [gather(): up_half = lax.all_to_all(up_own, 'adapter', 0, 0, tiled=True)]
    unnamed x22 -> x14, local copies, waits for them, and re-layouts: 7.96 us -> 5.09 us
    ppermute x13, waiting for transfers between devices: 15.2 us -> 16 us  [exchange(): return lax.ppermute(x, AXES, pairs)]
  transfers between devices with their start and end apart: 15 -> 14, of which waited for: 7 -> 6; matrix products, arithmetic and copies ran while one was open for 1% -> 1% of each run, Pallas kernels for 12% -> 16%
where the time goes in v6:
time: 63 us; the launch traced here: 62.4 us
  starting transfers between devices  27.3 us (43%)
  waiting for transfers between devices  16 us (25%)
  Pallas kernels  13.1 us (21%)
  local copies, waits for them, and re-layouts  5.77 us (9%)
    ppermute x13, starting transfers between devices, exchange(): return lax.ppermute(x, AXES, pairs)  23.1 us
    ppermute x13, waiting for transfers between devices, exchange(): return lax.ppermute(x, AXES, pairs)  16 us
    pallas_call x9, Pallas kernels, kernel(): pl.pallas_call(body, out_shape=outs, in_specs=specs or [inner] * len(oper...  13.1 us
    unnamed x14, local copies, waits for them, and re-layouts  5.09 us
    all_to_all x1, starting transfers between devices, gather(): bases = lax.all_to_all(bases, 'mp', 0, 0, tiled=True)  4.18 us
  transfers between devices with their start and end apart: 14, of which 6 were waited for; matrix products, arithmetic and copies ran while one was open for 1% of the time, Pallas kernels for 16%

profile of v6, /device:TPU:0, one launch (start us, length us, event | category | flops | bytes accessed | tf_op | source)
XLA Modules:
  0.0 62.4 jit_solution(6566876293609465989)
XLA Ops:
  0.0 0.0 copy-start
  0.0 0.0 copy-start.2
  0.0 1.3 %copy-done.2 = bf16[2048,256]{1,0:T(8,128)(2,1)S(1)} copy-done((bf16[2048,256]{1,0:T(8,128)(2,1)S(1)}, bf16[2048,256]{1,0:T(8,128)(2,1)}, u32[]{:S(2)}) %copy-start.2) | copy-done | bytes 1048600
  1.3 0.0 copy-start.5
  1.3 0.8 %copy-done.5 = bf16[256,128]{1,0:T(8,128)(2,1)S(1)} copy-done((bf16[256,128]{1,0:T(8,128)(2,1)S(1)}, bf16[256,128]{1,0:T(8,128)(2,1)}, u32[]{:S(2)}) %copy-start.5) | copy-done | bytes 65560
  2.2 0.1 shard_map.64.refs_2_.own
  2.3 3.1 %collective-permute-start.3 = (bf16[1152,256]{1,0:T(8,128)(2,1)S(1)}, bf16[1152,256]{1,0:T(8,128)(2,1)}, u32[]{:S(2)}, u32[]{:S(2)}) collective-permute-start(bf16[1152,256]{1,0:T(8,128)(2,1)S(1)} %shard_map.64.refs_2_.own), channel_id=1, source_target_pairs={{0,4},{1,5},{2,6},{3,7},{4,0},{5,1},{6,2},{7,3},{8,12},{9,13},{10,... | collective-permute-start | bytes 1769480 | tf_op jit(solution)/shard_map/ppermute | solution.py:95
  5.4 1.5 %collective-permute-start.4 = (bf16[1152,256]{1,0:T(8,128)(2,1)S(1)}, bf16[1152,256]{1,0:T(8,128)(2,1)}, u32[]{:S(2)}, u32[]{:S(2)}) collective-permute-start(bf16[1152,256]{1,0:T(8,128)(2,1)S(1)} %shard_map.64.refs_2_.own), channel_id=1, source_target_pairs={{4,8},{5,9},{6,10},{7,11},{8,4},{9,5},{10,6},{11,7},{20,24},{21,25... | collective-permute-start | bytes 1769480 | tf_op jit(solution)/shard_map/ppermute | solution.py:95
  6.8 0.7 %reshape.7.slot = s32[1,384]{1,0:T(1,128)S(1)} reshape(s32[384]{0:T(512)} %param.11) | data formatting | bytes 3072 | tf_op jit(solution)/shard_map/reshape | solution.py:385
  7.5 0.0 copy-done
  7.5 0.7 %copy-done.6 = s32[384,1]{0,1:T(1,128)S(1)} copy-done((s32[384,1]{0,1:T(1,128)S(1)}, s32[384,1]{0,1:T(1,128)}, u32[]{:S(2)}) %copy-start.6) | copy-done | bytes 1560
  8.2 1.1 %shard_map.65 = (bf16[400,1024]{1,0:T(8,128)(2,1)S(1)}, bf16[400,1024]{1,0:T(8,128)(2,1)}) custom-call(bf16[384,2048]{1,0:T(8,128)(2,1)S(1)} %copy-done, s32[1,384]{1,0:T(1,128)S(1)} %bitcast.1, s32[1,384]{1,0:T(1,128)S(1)} %reshape.7.slot), custom_call_target="tpu_custom_call" | custom-call | bytes 3214336 | tf_op jit(solution)/shard_map/pallas_call | solution.py:114
  9.3 1.6 %collective-permute-start = (bf16[400,1024]{1,0:T(8,128)(2,1)}, bf16[400,1024]{1,0:T(8,128)(2,1)S(1)}, u32[]{:S(2)}, u32[]{:S(2)}) collective-permute-start(bf16[400,1024]{1,0:T(8,128)(2,1)} %get-tuple-element.24.away), channel_id=1, source_target_pairs={{0,16},{1,17},{2,18},{3,19},{4,20},{5,21},{6,22},{7,23},{8,24},{9,... | collective-permute-start | bytes 2457608 | tf_op jit(solution)/shard_map/ppermute | solution.py:95
  10.9 1.6 %copy-done.1 = bf16[2048,512]{1,0:T(8,128)(2,1)S(1)} copy-done((bf16[2048,512]{1,0:T(8,128)(2,1)S(1)}, bf16[2048,512]{1,0:T(8,128)(2,1)}, u32[]{:S(2)}) %copy-start.1) | copy-done | bytes 2097176
  12.5 1.9 %shard_map.67 = f32[4,384,128]{2,1,0:T(8,128)} custom-call(bf16[384,2048]{1,0:T(8,128)(2,1)S(1)} %copy-done, bf16[2048,512]{1,0:T(8,128)(2,1)S(1)} %copy-done.1), custom_call_target="tpu_custom_call" | custom-call | flops 805306368 | bytes 4456448 | tf_op jit(solution)/shard_map/pallas_call | solution.py:114
  14.3 4.2 %all-to-all-start = ((f32[4,384,128]{2,1,0:T(8,128)}), f32[4,384,128]{2,1,0:T(8,128)}, u32[]{:S(2)}, u32[]{:S(2)}) async-start(f32[4,384,128]{2,1,0:T(8,128)} %shard_map.67), calls=%async_computation | async-start | bytes 1572864 | tf_op jit(solution)/shard_map/all_to_all | solution.py:406
  18.5 2.5 %shard_map.66 = (bf16[160,1024]{1,0:T(8,128)(2,1)}, bf16[160,1024]{1,0:T(8,128)(2,1)}, bf16[144,384]{1,0:T(8,128)(2,1)S(1)}) custom-call(bf16[400,1024]{1,0:T(8,128)(2,1)S(1)} %get-tuple-element.23.own.refs_0_, bf16[400,1024]{1,0:T(8,128)(2,1)} %get-tuple-element.24.away), custom_call_target="tpu_custom_call" | custom-call | flops 226492416 | bytes 2404352 | tf_op jit(solution)/shard_map/pallas_call | solution.py:114
  21.1 0.0 collective-permute-done.3.refs_3_.beside
  21.1 0.7 %collective-permute-start.6 = (bf16[1152,256]{1,0:T(8,128)(2,1)}, bf16[1152,256]{1,0:T(8,128)(2,1)S(1)}, u32[]{:S(2)}, u32[]{:S(2)}) collective-permute-start(bf16[1152,256]{1,0:T(8,128)(2,1)} %collective-permute-done.3.refs_3_.beside), channel_id=1, source_target_pairs={{4,8},{5,9},{6,10},{7,11},{8,4},{9,5},{10,6},{11,7},{20,24},{21,25... | collective-permute-start | bytes 1769480 | tf_op jit(solution)/shard_map/ppermute | solution.py:95
  21.8 0.0 collective-permute-done.4.refs_4_.mirror
  21.8 1.3 %collective-permute-start.7 = (bf16[1152,256]{1,0:T(8,128)(2,1)}, bf16[1152,256]{1,0:T(8,128)(2,1)S(1)}, u32[]{:S(2)}, u32[]{:S(2)}) collective-permute-start(bf16[1152,256]{1,0:T(8,128)(2,1)} %collective-permute-done.4.refs_4_.mirror), channel_id=1, source_target_pairs={{4,0},{5,1},{6,2},{7,3},{8,12},{9,13},{10,14},{11,15},{20,16},{21,... | collective-permute-start | bytes 1769480 | tf_op jit(solution)/shard_map/ppermute | solution.py:95
  23.1 4.4 %collective-permute-start.5 = (bf16[256,128]{1,0:T(8,128)(2,1)}, bf16[256,128]{1,0:T(8,128)(2,1)S(1)}, u32[]{:S(2)}, u32[]{:S(2)}) collective-permute-start(bf16[256,128]{1,0:T(8,128)(2,1)} %up.1), channel_id=1, source_target_pairs={{0,12},{1,13},{2,14},{3,15},{12,0},{13,1},{14,2},{15,3},{16,28},{1... | collective-permute-start | bytes 196616 | tf_op jit(solution)/shard_map/ppermute | solution.py:95
  27.5 3.8 %collective-permute-start.1 = (bf16[160,1024]{1,0:T(8,128)(2,1)}, bf16[160,1024]{1,0:T(8,128)(2,1)}, u32[]{:S(2)}, u32[]{:S(2)}) collective-permute-start(bf16[160,1024]{1,0:T(8,128)(2,1)} %get-tuple-element.25), channel_id=1, source_target_pairs={{0,4},{1,5},{2,6},{3,7},{12,8},{13,9},{14,10},{15,11},{16,20},{17,... | collective-permute-start | bytes 983048 | tf_op jit(solution)/shard_map/ppermute | solution.py:95
  31.2 0.4 collective-permute-done.5.distant
  31.6 0.6 %copy-done.3 = bf16[256,128]{1,0:T(8,128)(2,1)} copy-done((bf16[256,128]{1,0:T(8,128)(2,1)}, bf16[256,128]{1,0:T(8,128)(2,1)S(1)}, u32[]{:S(2)}) %copy-start.3) | copy-done | bytes 65560
  32.2 2.0 %collective-permute-start.2 = (bf16[160,1024]{1,0:T(8,128)(2,1)}, bf16[160,1024]{1,0:T(8,128)(2,1)}, u32[]{:S(2)}, u32[]{:S(2)}) collective-permute-start(bf16[160,1024]{1,0:T(8,128)(2,1)} %get-tuple-element.26), channel_id=1, source_target_pairs={{0,20},{1,21},{2,22},{3,23},{12,24},{13,25},{14,26},{15,27},{16,4}... | collective-permute-start | bytes 983048 | tf_op jit(solution)/shard_map/ppermute | solution.py:95
  34.2 0.0 all-to-all-done.refs_5_
  34.2 0.0 collective-permute-done.refs_1_
  34.2 3.1 %shard_map.68 = (f32[2,384,128]{2,1,0:T(8,128)S(1)}, f32[2,384,256]{2,1,0:T(8,128)S(1)}, f32[384,1]{1,0:T(8,128)S(1)}, f32[384,128]{1,0:T(8,128)S(1)}) custom-call(bf16[400,1024]{1,0:T(8,128)(2,1)S(1)} %get-tuple-element.23.own.refs_0_, bf16[400,1024]{1,0:T(8,128)(2,1)S(1)} %collective-permute-done.refs_1_, bf16[1152,256]{1,0:T(8,128)(2,1)S(1)} %shard_map.64.refs_2_.own, ...), custom_call_target="tpu_custom_call" | custom-call | flops 1207959552 | bytes 5572096 | tf_op jit(solution)/shard_map/pallas_call | solution.py:114
  37.3 1.5 %collective-permute-done.1.refs_2_ = bf16[160,1024]{1,0:T(8,128)(2,1)} collective-permute-done((bf16[160,1024]{1,0:T(8,128)(2,1)}, bf16[160,1024]{1,0:T(8,128)(2,1)}, u32[]{:S(2)}, u32[]{:S(2)}) %collective-permute-start.1) | collective-permute-done | bytes 327712 | tf_op jit(solution)/shard_map/ppermute | solution.py:95
  38.8 6.6 %collective-permute-done.2.refs_3_ = bf16[160,1024]{1,0:T(8,128)(2,1)} collective-permute-done((bf16[160,1024]{1,0:T(8,128)(2,1)}, bf16[160,1024]{1,0:T(8,128)(2,1)}, u32[]{:S(2)}, u32[]{:S(2)}) %collective-permute-start.2) | collective-permute-done | bytes 327712 | tf_op jit(solution)/shard_map/ppermute | solution.py:95
  45.4 0.0 collective-permute-done.6.refs_6_.inside
  45.4 0.0 collective-permute-done.7.refs_7_.outside
  45.4 1.8 %shard_map.69 = (f32[16,384]{1,0:T(8,128)S(1)}, f32[16,384]{1,0:T(8,128)S(1)}, f32[16,144]{1,0:T(8,128)S(1)}, f32[16,144]{1,0:T(8,128)S(1)}) custom-call(bf16[400,1024]{1,0:T(8,128)(2,1)S(1)} %get-tuple-element.23.own.refs_0_, bf16[400,1024]{1,0:T(8,128)(2,1)S(1)} %collective-permute-done.refs_1_, bf16[160,1024]{1,0:T(8,128)(2,1)} %collective-permute-done.1.refs_2_, ...), custom_call_target="tpu_custom_call" | custom-call | flops 553648128 | bytes 4720640 | tf_op jit(solution)/shard_map/pallas_call | solution.py:114
  47.2 0.6 collective-permute-start.8
  47.8 1.3 %collective-permute-start.10 = (f32[16,144]{1,0:T(8,128)S(1)}, f32[16,144]{1,0:T(8,128)S(1)}, u32[]{:S(2)}, u32[]{:S(2)}) collective-permute-start(f32[16,144]{1,0:T(8,128)S(1)} %get-tuple-element.36), channel_id=1, source_target_pairs={{4,16},{5,17},{6,18},{7,19},{8,28},{9,29},{10,30},{11,31},{20,0},{... | collective-permute-start | bytes 27656 | tf_op jit(solution)/shard_map/ppermute | solution.py:95
  49.1 1.3 %collective-permute-start.9 = (f32[16,144]{1,0:T(8,128)S(1)}, f32[16,144]{1,0:T(8,128)S(1)}, u32[]{:S(2)}, u32[]{:S(2)}) collective-permute-start(f32[16,144]{1,0:T(8,128)S(1)} %get-tuple-element.35), channel_id=1, source_target_pairs={{4,0},{5,1},{6,2},{7,3},{8,12},{9,13},{10,14},{11,15},{20,16},{21,... | collective-permute-start | bytes 27656 | tf_op jit(solution)/shard_map/ppermute | solution.py:95
  50.4 4.2 %collective-permute-done.10.refs_1_ = f32[16,144]{1,0:T(8,128)S(1)} collective-permute-done((f32[16,144]{1,0:T(8,128)S(1)}, f32[16,144]{1,0:T(8,128)S(1)}, u32[]{:S(2)}, u32[]{:S(2)}) %collective-permute-start.10) | collective-permute-done | bytes 9248 | tf_op jit(solution)/shard_map/ppermute | solution.py:95
  54.6 1.2 %collective-permute-done.9.refs_0_ = f32[16,144]{1,0:T(8,128)S(1)} collective-permute-done((f32[16,144]{1,0:T(8,128)S(1)}, f32[16,144]{1,0:T(8,128)S(1)}, u32[]{:S(2)}, u32[]{:S(2)}) %collective-permute-start.9) | collective-permute-done | bytes 9248 | tf_op jit(solution)/shard_map/ppermute | solution.py:95
  55.7 0.0 collective-permute-done.8.near
  55.7 0.2 shard_map.70
  55.9 1.7 %collective-permute-start.11 = (f32[16,384]{1,0:T(8,128)S(1)}, f32[16,384]{1,0:T(8,128)S(1)}, u32[]{:S(2)}, u32[]{:S(2)}) collective-permute-start(f32[16,384]{1,0:T(8,128)S(1)} %shard_map.70), channel_id=1, source_target_pairs={{0,2},{1,3},{2,0},{3,1},{4,6},{5,7},{6,4},{7,5},{8,10},{9,11},{10,... | collective-permute-start | bytes 73736 | tf_op jit(solution)/shard_map/ppermute | solution.py:95
  57.6 2.2 %collective-permute-done.11 = f32[16,384]{1,0:T(8,128)S(1)} collective-permute-done((f32[16,384]{1,0:T(8,128)S(1)}, f32[16,384]{1,0:T(8,128)S(1)}, u32[]{:S(2)}, u32[]{:S(2)}) %collective-permute-start.11) | collective-permute-done | bytes 24608 | tf_op jit(solution)/shard_map/ppermute | solution.py:95
  59.8 0.0 collective-permute-start.12
  59.8 0.0 copy-done.4
  59.8 1.3 %shard_map.71.ups = bf16[1024,128]{1,0:T(8,128)(2,1)S(1)} custom-call(bf16[1152,256]{1,0:T(8,128)(2,1)S(1)} %shard_map.64.refs_2_.own, bf16[1152,256]{1,0:T(8,128)(2,1)} %collective-permute-done.3.refs_3_.beside, bf16[1152,256]{1,0:T(8,128)(2,1)} %collective-permute-done.4.refs_4_.mirror, bf16[1152,256]{1,0:T(8,128)(2,1)S(1)} %collective-permute-done.6.refs_6_.inside, ...), custom_call_target="tpu_custom_call" | custom-call | bytes 3276800 | tf_op jit(solution)/shard_map/pallas_call | solution.py:114
  61.1 0.0 collective-permute-done.12.far
  61.1 1.3 %shard_map.72 = bf16[384,128]{1,0:T(8,128)(2,1)} custom-call(f32[16,384]{1,0:T(8,128)S(1)} %add.3.near, f32[16,384]{1,0:T(8,128)S(1)} %collective-permute-done.12.far, f32[384,128]{1,0:T(8,128)S(1)} %get-tuple-element.37.base, f32[384,1]{1,0:T(8,128)S(1)} %get-tuple-element.38.numbers, bf16[1024,128]{1,0:T(8,128)(2,1)S(1)} %shard_map.71.ups), custom_call_target="tpu_custom_call" | custom-call | bytes 607744 | tf_op jit(solution)/shard_map/pallas_call | solution.py:114
  (5 shorter events, 0.0 us)
Async XLA Ops:
  0.0 7.5 %copy-start = (bf16[384,2048]{1,0:T(8,128)(2,1)S(1)}, bf16[384,2048]{1,0:T(8,128)(2,1)}, u32[]{:S(2)}) copy-start(bf16[384,2048]{1,0:T(8,128)(2,1)} %tokens.3) | copy-start | bytes 4718596
  0.0 1.3 %copy-start.2 = (bf16[2048,256]{1,0:T(8,128)(2,1)S(1)}, bf16[2048,256]{1,0:T(8,128)(2,1)}, u32[]{:S(2)}) copy-start(bf16[2048,256]{1,0:T(8,128)(2,1)} %down.1) | copy-start | bytes 3145732
  1.3 0.8 %copy-start.5 = (bf16[256,128]{1,0:T(8,128)(2,1)S(1)}, bf16[256,128]{1,0:T(8,128)(2,1)}, u32[]{:S(2)}) copy-start(bf16[256,128]{1,0:T(8,128)(2,1)} %up.1) | copy-start | bytes 196612
  2.3 18.8 %collective-permute-start.3 = (bf16[1152,256]{1,0:T(8,128)(2,1)S(1)}, bf16[1152,256]{1,0:T(8,128)(2,1)}, u32[]{:S(2)}, u32[]{:S(2)}) collective-permute-start(bf16[1152,256]{1,0:T(8,128)(2,1)S(1)} %shard_map.64.refs_2_.own), channel_id=1, source_target_pairs={{0,4},{1,5},{2,6},{3,7},{4,0},{5,1},{6,2},{7,3},{8,12},{9,13},{10,... | collective-permute-start | bytes 1769480 | tf_op jit(solution)/shard_map/ppermute | solution.py:95
  5.4 16.4 %collective-permute-start.4 = (bf16[1152,256]{1,0:T(8,128)(2,1)S(1)}, bf16[1152,256]{1,0:T(8,128)(2,1)}, u32[]{:S(2)}, u32[]{:S(2)}) collective-permute-start(bf16[1152,256]{1,0:T(8,128)(2,1)S(1)} %shard_map.64.refs_2_.own), channel_id=1, source_target_pairs={{4,8},{5,9},{6,10},{7,11},{8,4},{9,5},{10,6},{11,7},{20,24},{21,25... | collective-permute-start | bytes 1769480 | tf_op jit(solution)/shard_map/ppermute | solution.py:95
  7.5 0.7 %copy-start.6 = (s32[384,1]{0,1:T(1,128)S(1)}, s32[384,1]{0,1:T(1,128)}, u32[]{:S(2)}) copy-start(s32[384,1]{0,1:T(1,128)} %param.10) | copy-start | bytes 4612
  9.3 25.0 %collective-permute-start = (bf16[400,1024]{1,0:T(8,128)(2,1)}, bf16[400,1024]{1,0:T(8,128)(2,1)S(1)}, u32[]{:S(2)}, u32[]{:S(2)}) collective-permute-start(bf16[400,1024]{1,0:T(8,128)(2,1)} %get-tuple-element.24.away), channel_id=1, source_target_pairs={{0,16},{1,17},{2,18},{3,19},{4,20},{5,21},{6,22},{7,23},{8,24},{9,... | collective-permute-start | bytes 2457608 | tf_op jit(solution)/shard_map/ppermute | solution.py:95
  10.9 1.6 %copy-start.1 = (bf16[2048,512]{1,0:T(8,128)(2,1)S(1)}, bf16[2048,512]{1,0:T(8,128)(2,1)}, u32[]{:S(2)}) copy-start(bf16[2048,512]{1,0:T(8,128)(2,1)} %weights.1) | copy-start | bytes 6291460
  14.3 19.9 %all-to-all-start = ((f32[4,384,128]{2,1,0:T(8,128)}), f32[4,384,128]{2,1,0:T(8,128)}, u32[]{:S(2)}, u32[]{:S(2)}) async-start(f32[4,384,128]{2,1,0:T(8,128)} %shard_map.67), calls=%async_computation | async-start | bytes 1572864 | tf_op jit(solution)/shard_map/all_to_all | solution.py:406
  21.1 24.3 %collective-permute-start.6 = (bf16[1152,256]{1,0:T(8,128)(2,1)}, bf16[1152,256]{1,0:T(8,128)(2,1)S(1)}, u32[]{:S(2)}, u32[]{:S(2)}) collective-permute-start(bf16[1152,256]{1,0:T(8,128)(2,1)} %collective-permute-done.3.refs_3_.beside), channel_id=1, source_target_pairs={{4,8},{5,9},{6,10},{7,11},{8,4},{9,5},{10,6},{11,7},{20,24},{21,25... | collective-permute-start | bytes 1769480 | tf_op jit(solution)/shard_map/ppermute | solution.py:95
  21.8 23.6 %collective-permute-start.7 = (bf16[1152,256]{1,0:T(8,128)(2,1)}, bf16[1152,256]{1,0:T(8,128)(2,1)S(1)}, u32[]{:S(2)}, u32[]{:S(2)}) collective-permute-start(bf16[1152,256]{1,0:T(8,128)(2,1)} %collective-permute-done.4.refs_4_.mirror), channel_id=1, source_target_pairs={{4,0},{5,1},{6,2},{7,3},{8,12},{9,13},{10,14},{11,15},{20,16},{21,... | collective-permute-start | bytes 1769480 | tf_op jit(solution)/shard_map/ppermute | solution.py:95
  23.1 8.5 %collective-permute-start.5 = (bf16[256,128]{1,0:T(8,128)(2,1)}, bf16[256,128]{1,0:T(8,128)(2,1)S(1)}, u32[]{:S(2)}, u32[]{:S(2)}) collective-permute-start(bf16[256,128]{1,0:T(8,128)(2,1)} %up.1), channel_id=1, source_target_pairs={{0,12},{1,13},{2,14},{3,15},{12,0},{13,1},{14,2},{15,3},{16,28},{1... | collective-permute-start | bytes 196616 | tf_op jit(solution)/shard_map/ppermute | solution.py:95
  27.5 11.4 %collective-permute-start.1 = (bf16[160,1024]{1,0:T(8,128)(2,1)}, bf16[160,1024]{1,0:T(8,128)(2,1)}, u32[]{:S(2)}, u32[]{:S(2)}) collective-permute-start(bf16[160,1024]{1,0:T(8,128)(2,1)} %get-tuple-element.25), channel_id=1, source_target_pairs={{0,4},{1,5},{2,6},{3,7},{12,8},{13,9},{14,10},{15,11},{16,20},{17,... | collective-permute-start | bytes 983048 | tf_op jit(solution)/shard_map/ppermute | solution.py:95
  31.6 0.6 %copy-start.3 = (bf16[256,128]{1,0:T(8,128)(2,1)}, bf16[256,128]{1,0:T(8,128)(2,1)S(1)}, u32[]{:S(2)}) copy-start(bf16[256,128]{1,0:T(8,128)(2,1)S(1)} %collective-permute-done.5.distant) | copy-start | bytes 196612
  32.2 13.2 %collective-permute-start.2 = (bf16[160,1024]{1,0:T(8,128)(2,1)}, bf16[160,1024]{1,0:T(8,128)(2,1)}, u32[]{:S(2)}, u32[]{:S(2)}) collective-permute-start(bf16[160,1024]{1,0:T(8,128)(2,1)} %get-tuple-element.26), channel_id=1, source_target_pairs={{0,20},{1,21},{2,22},{3,23},{12,24},{13,25},{14,26},{15,27},{16,4}... | collective-permute-start | bytes 983048 | tf_op jit(solution)/shard_map/ppermute | solution.py:95
  45.4 14.4 %copy-start.4 = (bf16[256,128]{1,0:T(8,128)(2,1)S(1)}, bf16[256,128]{1,0:T(8,128)(2,1)}, u32[]{:S(2)}) copy-start(bf16[256,128]{1,0:T(8,128)(2,1)} %copy-done.3) | copy-start | bytes 196612
  47.2 8.6 %collective-permute-start.8 = (f32[16,384]{1,0:T(8,128)S(1)}, f32[16,384]{1,0:T(8,128)S(1)}, u32[]{:S(2)}, u32[]{:S(2)}) collective-permute-start(f32[16,384]{1,0:T(8,128)S(1)} %get-tuple-element.34), channel_id=1, source_target_pairs={{0,16},{1,17},{2,18},{3,19},{4,20},{5,21},{6,22},{7,23},{8,24},{9,... | collective-permute-start | bytes 73736 | tf_op jit(solution)/shard_map/ppermute | solution.py:95
  47.8 6.8 %collective-permute-start.10 = (f32[16,144]{1,0:T(8,128)S(1)}, f32[16,144]{1,0:T(8,128)S(1)}, u32[]{:S(2)}, u32[]{:S(2)}) collective-permute-start(f32[16,144]{1,0:T(8,128)S(1)} %get-tuple-element.36), channel_id=1, source_target_pairs={{4,16},{5,17},{6,18},{7,19},{8,28},{9,29},{10,30},{11,31},{20,0},{... | collective-permute-start | bytes 27656 | tf_op jit(solution)/shard_map/ppermute | solution.py:95
  49.1 6.7 %collective-permute-start.9 = (f32[16,144]{1,0:T(8,128)S(1)}, f32[16,144]{1,0:T(8,128)S(1)}, u32[]{:S(2)}, u32[]{:S(2)}) collective-permute-start(f32[16,144]{1,0:T(8,128)S(1)} %get-tuple-element.35), channel_id=1, source_target_pairs={{4,0},{5,1},{6,2},{7,3},{8,12},{9,13},{10,14},{11,15},{20,16},{21,... | collective-permute-start | bytes 27656 | tf_op jit(solution)/shard_map/ppermute | solution.py:95
  55.9 3.9 %collective-permute-start.11 = (f32[16,384]{1,0:T(8,128)S(1)}, f32[16,384]{1,0:T(8,128)S(1)}, u32[]{:S(2)}, u32[]{:S(2)}) collective-permute-start(f32[16,384]{1,0:T(8,128)S(1)} %shard_map.70), channel_id=1, source_target_pairs={{0,2},{1,3},{2,0},{3,1},{4,6},{5,7},{6,4},{7,5},{8,10},{9,11},{10,... | collective-permute-start | bytes 73736 | tf_op jit(solution)/shard_map/ppermute | solution.py:95
  59.8 1.3 %collective-permute-start.12 = (f32[16,384]{1,0:T(8,128)S(1)}, f32[16,384]{1,0:T(8,128)S(1)}, u32[]{:S(2)}, u32[]{:S(2)}) collective-permute-start(f32[16,384]{1,0:T(8,128)S(1)} %add.3.near), channel_id=1, source_target_pairs={{0,1},{1,0},{2,3},{3,2},{4,5},{5,4},{6,7},{7,6},{8,9},{9,8},{10,11... | collective-permute-start | bytes 73736 | tf_op jit(solution)/shard_map/ppermute | solution.py:95

commit v7 on v6

--- a/solution.py
+++ b/solution.py
@@ -98,7 +98,6 @@
 SAME = tuple((a, a) for a in range(OWNERS))
 BESIDE = ((0, 1), (1, 0), (2, 3), (3, 2))
 MIDDLE = ((1, 2), (2, 1))
-ENDS = ((0, 3), (3, 0))
 OUTWARD = ((1, 0), (2, 3))
 INWARD = ((0, 1), (3, 2))
 
@@ -158,7 +157,7 @@
     for copy in copies:
         copy.start()
     row = lax.broadcasted_iota(jnp.int32, (ID_ROWS, rows), 0)
-    ids = jnp.where(row == 0, owner[...], jnp.where(row == 1, slot[...], 0))
+    ids = jnp.where(row == 0, owner[...], jnp.where(row == 1, slot[...].reshape(1, rows), 0))
     ids = ids.astype(jnp.float32).astype(jnp.bfloat16)
     for out in (own, away):
         out[rows:, :rows] = ids
@@ -167,8 +166,8 @@
         copy.wait()
 
 
-def hop_body(rows, capacity, own, away, own_out, away_out, places):
-    a = lax.axis_index("adapter")
+def hop_body(rows, capacity, own, away, weights, own_out, away_out, places, bases):
+    a, g = lax.axis_index("adapter"), lax.axis_index("groups")
     part = own.shape[1]
     ids = own[rows:, :rows]
     match = (ids.astype(jnp.float32) == (OWNERS - 1 - a).astype(jnp.float32)).astype(jnp.bfloat16)
@@ -186,16 +185,17 @@
         out[:capacity, :] = packed.astype(jnp.bfloat16)
         out[capacity:, :] = jnp.zeros((ID_ROWS, part), jnp.bfloat16)
         out[capacity:, :capacity] = kept.astype(jnp.bfloat16)
+    base = jnp.zeros((rows, weights.shape[1]), jnp.float32)
+    for tokens, half in ((own, g), (away, 1 - g)):
+        part_weights = weights[pl.ds(pl.multiple_of(half * part, part), part), :]
+        base = base + jnp.dot(tokens[:rows, :], part_weights, preferred_element_type=jnp.float32)
+    keys = bases.shape[2]
+    for k in range(bases.shape[0]):
+        bases[k] = base[:, k * keys : (k + 1) * keys]
 
 
 NT = (((1,), (1,)), ((), ()))
 TN = (((0,), (0,)), ((), ()))
-
-
-def base_body(keys, tokens, weights, out):
-    wide = jnp.dot(tokens[...], weights[...], preferred_element_type=jnp.float32)
-    for k in range(out.shape[0]):
-        out[k] = wide[:, k * keys : (k + 1) * keys]
 
 
 def id_columns(rows_ref, start, count):
@@ -253,13 +253,21 @@
         mask[n] = jnp.where(owner == (a ^ 2).astype(jnp.float32), right.astype(jnp.float32), 0.0)
 
 
+def hop_mask_body(capacity, *refs):
+    hops, out = refs[:-1], refs[-1]
+    adapter = adapters(capacity, out.shape[2])
+    for n, hop in enumerate(hops):
+        _, slot = id_columns(hop, capacity, capacity)
+        out[n] = (adapter == slot).astype(jnp.float32)
+
+
 def last_body(part, rows, capacity, *refs):
     groups = lax.axis_size("groups")
     a = lax.axis_index("adapter")
     token_refs, rest = refs[:groups], refs[groups:]
     hops, rest = rest[:groups], rest[groups:]
-    folded, mask, inside, outside = rest[:4]
-    lows, hop_lows = rest[4 : 4 + groups], rest[4 + groups :]
+    hop_mask, folded, mask, inside, outside = rest[:5]
+    lows, hop_lows, far_ups = rest[5 : 5 + groups], rest[5 + groups : -1], rest[-1]
     columns = inside.shape[1]
 
     def finish(block):
@@ -273,11 +281,10 @@
     @pl.when(middle)
     def _():
         finish(inside)
-        adapter = adapters(capacity, columns)
-        for hop, out in zip(hops, hop_lows):
-            _, slot = id_columns(hop, capacity, capacity)
+        far_ups[...] = inside[part:, :]
+        for n, (hop, out) in enumerate(zip(hops, hop_lows)):
             wide = jnp.dot(hop[:capacity, :], inside[:part, :], preferred_element_type=jnp.float32)
-            kept = fold(jnp.where(adapter == slot, wide, 0.0))
+            kept = fold(jnp.where(hop_mask[n] > 0, wide, 0.0))
             rest_rows = -capacity % LANES
             kept = jnp.concatenate([kept, jnp.zeros((rest_rows, LANES), jnp.float32)], axis=0)
             out[...] = low_rank(kept)[:, :capacity]
@@ -285,6 +292,7 @@
     @pl.when(jnp.logical_not(middle))
     def _():
         finish(outside)
+        far_ups[...] = outside[part:, :]
         for out in hop_lows:
             out[...] = jnp.zeros(out.shape, jnp.float32)
 
@@ -302,16 +310,16 @@
     out[...] = low[...] + near[...] + spread
 
 
-def ups_body(part, own, beside, mirror, inside, outside, distant, out):
+def ups_body(keys, part, own, beside, mirror, inside, outside, distant, out):
     a = lax.axis_index("adapter")
-    columns, keys = distant.shape
+    columns = own.shape[1]
     count = columns // keys
     size = columns // count
 
-    def place(number, block):
+    def place(number, block, first=part):
         for k in range(count):
             start = number * columns + k * size
-            out[start : start + size, :] = block[part:, k * keys : (k + 1) * keys]
+            out[start : start + size, :] = block[first:, k * keys : (k + 1) * keys]
 
     place(0, own)
     place(1, beside)
@@ -325,7 +333,7 @@
     @pl.when(jnp.logical_not(middle))
     def _():
         place(2, outside)
-        out[3 * columns :, :] = distant[...]
+        place(3, distant, 0)
 
 
 def finish_body(near, far, base, numbers, ups, out):
@@ -378,30 +386,24 @@
         (pltpu.HBM, pltpu.HBM),
         [pltpu.SemaphoreType.DMA((1 + half,))],
     )
+    mirror = exchange(own, 0, 0, MIDDLE)
     beside = exchange(own, 0, 0, BESIDE)
-    mirror = exchange(own, 0, 0, MIDDLE)
-    distant = exchange(after(stacked_up_weight, own), 0, 0, ENDS)
-
-    slot = request_adapter_slot.reshape(1, rows)
+
     tok_own, tok_away = kernel(
         split_body,
         [narrow(rows + ID_ROWS, part)] * groups,
-        (tokens, request_adapter_owner.reshape(1, rows), after(slot, own)),
+        (tokens, request_adapter_owner.reshape(1, rows), after(request_adapter_slot, own)),
         0,
         (pltpu.HBM, None, None),
         [pltpu.SemaphoreType.DMA((groups,))],
     )
     token_parts = [tok_own, exchange(tok_away, 1, 0, SAME)]
-    hop_own, hop_away, places = kernel(
+    hop_own, hop_away, places, bases = kernel(
         functools.partial(hop_body, rows, capacity),
-        [narrow(capacity + ID_ROWS, part)] * groups + [narrow(capacity, rows)],
-        (tok_own, tok_away),
-        2 * capacity * rows * features,
-    )
-
-    bases = kernel(
-        functools.partial(base_body, keys), wide(shares, rows, keys), (tokens, base_key_weight),
-        2 * rows * features * shares * keys,
+        [narrow(capacity + ID_ROWS, part)] * groups
+        + [narrow(capacity, rows), wide(shares, rows, keys)],
+        (tok_own, tok_away, base_key_weight),
+        2 * rows * features * (capacity + shares * keys),
     )
     bases = lax.all_to_all(bases, "mp", 0, 0, tiled=True)
 
@@ -415,19 +417,25 @@
     folded, mask, numbers, base = kernel(
         functools.partial(early_body, (0, 1, 3), part, rows),
         [wide(groups, rows, LANES), wide(groups, rows, columns), wide(rows, 1), wide(rows, keys)],
-        (*token_parts, own, beside, mirror, after(bases, distant)),
+        (*token_parts, own, beside, mirror, bases),
         6 * groups * rows * part * columns,
     )
-    low, low_away, back, back_away = kernel(
+    hop_mask = kernel(
+        functools.partial(hop_mask_body, capacity), wide(groups, capacity, columns), (hops[0], after(hops[1], folded))
+    )
+    low, low_away, back, back_away, far_ups = kernel(
         functools.partial(last_body, part, rows, capacity),
-        [wide(ADAPTER_RANK, rows)] * groups + [wide(ADAPTER_RANK, capacity)] * groups,
-        (*token_parts, *hops, folded, mask, inside, outside),
+        [wide(ADAPTER_RANK, rows)] * groups
+        + [wide(ADAPTER_RANK, capacity)] * groups
+        + [narrow(columns // half, columns)],
+        (*token_parts, *hops, hop_mask, folded, mask, inside, outside),
         2 * groups * (rows + capacity) * part * columns,
     )
 
     near = exchange(low_away, 1, 0, SAME)
     back = exchange(back, 0, 0, OUTWARD)
     back_away = exchange(back_away, 1, 0, OUTWARD)
+    distant = exchange(far_ups, 0, 0, OUTWARD)
     low = kernel(merge_body, wide(ADAPTER_RANK, rows), (low, near, places, back, back_away))
     bit = shares // 2
     while bit > 1:
@@ -435,7 +443,7 @@
         bit //= 2
     low_far = exchange(low, 0, 1, SAME)
     ups = kernel(
-        functools.partial(ups_body, part),
+        functools.partial(ups_body, keys, part),
         narrow(owners * columns, keys),
         (own, beside, mirror, inside, outside, distant),
     )

time: 63 us -> 64.6 us (1.025)
  waiting for transfers between devices: 16 us -> 17.6 us
    all_to_all x1, waiting for transfers between devices: 0.01 us -> 1.62 us  [gather(): bases = lax.all_to_all(bases, 'mp', 0, 0, tiled=True)]
    unnamed x14, local copies, waits for them, and re-layouts: 5.09 us -> 5.86 us
    reshape x1 -> x0, local copies, waits for them, and re-layouts: 0.68 us -> none  [gather(): slot = request_adapter_slot.reshape(1, rows)]
  transfers between devices with their start and end apart: 14 -> 14, of which waited for: 6 -> 6; matrix products, arithmetic and copies ran while one was open for 1% -> 0% of each run, Pallas kernels for 16% -> 15%
where the time goes in v7:
time: 64.6 us; the launch traced here: 64 us
  starting transfers between devices  27.5 us (43%)
  waiting for transfers between devices  17.6 us (27%)
  Pallas kernels  12.8 us (20%)
  local copies, waits for them, and re-layouts  5.86 us (9%)
    ppermute x13, starting transfers between devices, exchange(): return lax.ppermute(x, AXES, pairs)  23.3 us
    ppermute x13, waiting for transfers between devices, exchange(): return lax.ppermute(x, AXES, pairs)  16 us
    pallas_call x9, Pallas kernels, kernel(): pl.pallas_call(body, out_shape=outs, in_specs=specs or [inner] * len(oper...  12.8 us
    unnamed x14, local copies, waits for them, and re-layouts  5.86 us
    all_to_all x1, starting transfers between devices, gather(): bases = lax.all_to_all(bases, 'mp', 0, 0, tiled=True)  4.19 us
    all_to_all x1, waiting for transfers between devices, gather(): bases = lax.all_to_all(bases, 'mp', 0, 0, tiled=True)  1.62 us
  transfers between devices with their start and end apart: 14, of which 6 were waited for; matrix products, arithmetic and copies ran while one was open for 0% of the time, Pallas kernels for 15%

profile of v7, /device:TPU:0, one launch (start us, length us, event | category | flops | bytes accessed | tf_op | source)
XLA Modules:
  0.0 64.0 jit_solution(372015053803415552)
XLA Ops:
  0.0 0.0 copy-start
  0.0 0.0 copy-start.1
  0.0 1.3 %copy-done.1 = bf16[2048,256]{1,0:T(8,128)(2,1)S(1)} copy-done((bf16[2048,256]{1,0:T(8,128)(2,1)S(1)}, bf16[2048,256]{1,0:T(8,128)(2,1)}, u32[]{:S(2)}) %copy-start.1) | copy-done | bytes 1048600
  1.3 0.0 copy-start.2
  1.3 0.8 %copy-done.2 = bf16[256,128]{1,0:T(8,128)(2,1)S(1)} copy-done((bf16[256,128]{1,0:T(8,128)(2,1)S(1)}, bf16[256,128]{1,0:T(8,128)(2,1)}, u32[]{:S(2)}) %copy-start.2) | copy-done | bytes 65560
  2.2 0.1 shard_map.64.refs_2_.own
  2.3 3.1 %collective-permute-start.3 = (bf16[1152,256]{1,0:T(8,128)(2,1)S(1)}, bf16[1152,256]{1,0:T(8,128)(2,1)}, u32[]{:S(2)}, u32[]{:S(2)}) collective-permute-start(bf16[1152,256]{1,0:T(8,128)(2,1)S(1)} %shard_map.64.refs_2_.own), channel_id=1, source_target_pairs={{0,4},{1,5},{2,6},{3,7},{4,0},{5,1},{6,2},{7,3},{8,12},{9,13},{10,... | collective-permute-start | bytes 1769480 | tf_op jit(solution)/shard_map/ppermute | solution.py:95
  5.4 1.5 %collective-permute-start.4 = (bf16[1152,256]{1,0:T(8,128)(2,1)S(1)}, bf16[1152,256]{1,0:T(8,128)(2,1)}, u32[]{:S(2)}, u32[]{:S(2)}) collective-permute-start(bf16[1152,256]{1,0:T(8,128)(2,1)S(1)} %shard_map.64.refs_2_.own), channel_id=1, source_target_pairs={{4,8},{5,9},{6,10},{7,11},{8,4},{9,5},{10,6},{11,7},{20,24},{21,25... | collective-permute-start | bytes 1769480 | tf_op jit(solution)/shard_map/ppermute | solution.py:95
  6.9 0.0 copy-done
  6.9 0.0 copy-start.3
  6.9 0.7 %copy-done.3 = s32[384]{0:T(512)S(1)} copy-done((s32[384]{0:T(512)S(1)}, s32[384]{0:T(512)}, u32[]{:S(2)}) %copy-start.3) | copy-done | bytes 1560
  7.5 0.7 %copy-done.4 = s32[384,1]{0,1:T(1,128)S(1)} copy-done((s32[384,1]{0,1:T(1,128)S(1)}, s32[384,1]{0,1:T(1,128)}, u32[]{:S(2)}) %copy-start.4) | copy-done | bytes 1560
  8.2 1.1 %shard_map.65 = (bf16[400,1024]{1,0:T(8,128)(2,1)S(1)}, bf16[400,1024]{1,0:T(8,128)(2,1)}) custom-call(bf16[384,2048]{1,0:T(8,128)(2,1)S(1)} %copy-done, s32[1,384]{1,0:T(1,128)S(1)} %bitcast.1, s32[384]{0:T(512)S(1)} %copy-done.3), custom_call_target="tpu_custom_call" | custom-call | bytes 3214336 | tf_op jit(solution)/shard_map/pallas_call | solution.py:113
  9.3 1.6 %collective-permute-start = (bf16[400,1024]{1,0:T(8,128)(2,1)}, bf16[400,1024]{1,0:T(8,128)(2,1)}, u32[]{:S(2)}, u32[]{:S(2)}) collective-permute-start(bf16[400,1024]{1,0:T(8,128)(2,1)} %get-tuple-element.25.away), channel_id=1, source_target_pairs={{0,16},{1,17},{2,18},{3,19},{4,20},{5,21},{6,22},{7,23},{8,24},{9,... | collective-permute-start | bytes 2457608 | tf_op jit(solution)/shard_map/ppermute | solution.py:95
  10.9 1.6 %copy-done.5 = bf16[2048,512]{1,0:T(8,128)(2,1)S(1)} copy-done((bf16[2048,512]{1,0:T(8,128)(2,1)S(1)}, bf16[2048,512]{1,0:T(8,128)(2,1)}, u32[]{:S(2)}) %copy-start.5) | copy-done | bytes 2097176
  12.5 3.5 %shard_map.66 = (bf16[160,1024]{1,0:T(8,128)(2,1)S(1)}, bf16[160,1024]{1,0:T(8,128)(2,1)}, bf16[144,384]{1,0:T(8,128)(2,1)S(1)}, f32[4,384,128]{2,1,0:T(8,128)}) custom-call(bf16[400,1024]{1,0:T(8,128)(2,1)S(1)} %get-tuple-element.24.own.refs_0_, bf16[400,1024]{1,0:T(8,128)(2,1)} %get-tuple-element.25.away, bf16[2048,512]{1,0:T(8,128)(2,1)S(1)} %copy-done.5), custom_call_target="tpu_custom_call" | custom-call | flops 1031798784 | bytes 5287936 | tf_op jit(solution)/shard_map/pallas_call | solution.py:113
  16.0 0.7 %copy-done.6 = bf16[160,1024]{1,0:T(8,128)(2,1)} copy-done((bf16[160,1024]{1,0:T(8,128)(2,1)}, bf16[160,1024]{1,0:T(8,128)(2,1)S(1)}, u32[]{:S(2)}) %copy-start.6) | copy-done | bytes 327704
  16.7 4.2 %all-to-all-start = ((f32[4,384,128]{2,1,0:T(8,128)}), f32[4,384,128]{2,1,0:T(8,128)}, u32[]{:S(2)}, u32[]{:S(2)}) async-start(f32[4,384,128]{2,1,0:T(8,128)} %get-tuple-element.28), calls=%async_computation | async-start | bytes 1572864 | tf_op jit(solution)/shard_map/all_to_all | solution.py:408
  20.9 0.0 collective-permute-done.3.refs_3_.beside
  20.9 0.7 %collective-permute-start.5 = (bf16[1152,256]{1,0:T(8,128)(2,1)}, bf16[1152,256]{1,0:T(8,128)(2,1)S(1)}, u32[]{:S(2)}, u32[]{:S(2)}) collective-permute-start(bf16[1152,256]{1,0:T(8,128)(2,1)} %collective-permute-done.3.refs_3_.beside), channel_id=1, source_target_pairs={{4,8},{5,9},{6,10},{7,11},{8,4},{9,5},{10,6},{11,7},{20,24},{21,25... | collective-permute-start | bytes 1769480 | tf_op jit(solution)/shard_map/ppermute | solution.py:95
  21.7 0.0 collective-permute-done.4.refs_4_.mirror
  21.7 1.3 %collective-permute-start.6 = (bf16[1152,256]{1,0:T(8,128)(2,1)}, bf16[1152,256]{1,0:T(8,128)(2,1)S(1)}, u32[]{:S(2)}, u32[]{:S(2)}) collective-permute-start(bf16[1152,256]{1,0:T(8,128)(2,1)} %collective-permute-done.4.refs_4_.mirror), channel_id=1, source_target_pairs={{4,0},{5,1},{6,2},{7,3},{8,12},{9,13},{10,14},{11,15},{20,16},{21,... | collective-permute-start | bytes 1769480 | tf_op jit(solution)/shard_map/ppermute | solution.py:95
  23.0 6.7 %collective-permute-start.2 = (bf16[160,1024]{1,0:T(8,128)(2,1)}, bf16[160,1024]{1,0:T(8,128)(2,1)S(1)}, u32[]{:S(2)}, u32[]{:S(2)}) collective-permute-start(bf16[160,1024]{1,0:T(8,128)(2,1)} %get-tuple-element.27), channel_id=1, source_target_pairs={{0,20},{1,21},{2,22},{3,23},{12,24},{13,25},{14,26},{15,27},{16,4}... | collective-permute-start | bytes 983048 | tf_op jit(solution)/shard_map/ppermute | solution.py:95
  29.7 1.4 %collective-permute-start.1 = (bf16[160,1024]{1,0:T(8,128)(2,1)}, bf16[160,1024]{1,0:T(8,128)(2,1)S(1)}, u32[]{:S(2)}, u32[]{:S(2)}) collective-permute-start(bf16[160,1024]{1,0:T(8,128)(2,1)} %copy-done.6), channel_id=1, source_target_pairs={{0,4},{1,5},{2,6},{3,7},{12,8},{13,9},{14,10},{15,11},{16,20},{17,... | collective-permute-start | bytes 983048 | tf_op jit(solution)/shard_map/ppermute | solution.py:95
  31.0 1.6 %all-to-all-done.refs_5_ = f32[4,384,128]{2,1,0:T(8,128)} async-done(((f32[4,384,128]{2,1,0:T(8,128)}), f32[4,384,128]{2,1,0:T(8,128)}, u32[]{:S(2)}, u32[]{:S(2)}) %all-to-all-start) | async-done | bytes 786464 | tf_op jit(solution)/shard_map/all_to_all | solution.py:408
  32.7 0.0 collective-permute-done.refs_1_
  32.7 3.3 %shard_map.67 = (f32[2,384,128]{2,1,0:T(8,128)S(1)}, f32[2,384,256]{2,1,0:T(8,128)S(1)}, f32[384,1]{1,0:T(8,128)S(1)}, f32[384,128]{1,0:T(8,128)S(1)}) custom-call(bf16[400,1024]{1,0:T(8,128)(2,1)S(1)} %get-tuple-element.24.own.refs_0_, bf16[400,1024]{1,0:T(8,128)(2,1)} %collective-permute-done.refs_1_, bf16[1152,256]{1,0:T(8,128)(2,1)S(1)} %shard_map.64.refs_2_.own, ...), custom_call_target="tpu_custom_call" | custom-call | flops 1207959552 | bytes 5572096 | tf_op jit(solution)/shard_map/pallas_call | solution.py:113
  36.0 2.0 %collective-permute-done.2.refs_1_.refs_3_ = bf16[160,1024]{1,0:T(8,128)(2,1)S(1)} collective-permute-done((bf16[160,1024]{1,0:T(8,128)(2,1)}, bf16[160,1024]{1,0:T(8,128)(2,1)S(1)}, u32[]{:S(2)}, u32[]{:S(2)}) %collective-permute-start.2) | collective-permute-done | bytes 327712 | tf_op jit(solution)/shard_map/ppermute | solution.py:95
  38.0 6.6 %collective-permute-done.1.refs_0_.refs_2_ = bf16[160,1024]{1,0:T(8,128)(2,1)S(1)} collective-permute-done((bf16[160,1024]{1,0:T(8,128)(2,1)}, bf16[160,1024]{1,0:T(8,128)(2,1)S(1)}, u32[]{:S(2)}, u32[]{:S(2)}) %collective-permute-start.1) | collective-permute-done | bytes 327712 | tf_op jit(solution)/shard_map/ppermute | solution.py:95
  44.5 0.3 shard_map.68.refs_4_
  44.9 0.0 collective-permute-done.5.refs_7_.inside
  44.9 0.0 collective-permute-done.6.refs_8_.outside
  44.9 1.8 %shard_map.69 = (f32[16,384]{1,0:T(8,128)S(1)}, f32[16,384]{1,0:T(8,128)S(1)}, f32[16,144]{1,0:T(8,128)S(1)}, f32[16,144]{1,0:T(8,128)S(1)}, bf16[128,256]{1,0:T(8,128)(2,1)S(1)}) custom-call(bf16[400,1024]{1,0:T(8,128)(2,1)S(1)} %get-tuple-element.24.own.refs_0_, bf16[400,1024]{1,0:T(8,128)(2,1)} %collective-permute-done.refs_1_, ...), custom_call_target="tpu_custom_call" | custom-call | flops 553648128 | bytes 5081088 | tf_op jit(solution)/shard_map/pallas_call | solution.py:113
  46.7 1.6 %collective-permute-start.7 = (f32[16,384]{1,0:T(8,128)S(1)}, f32[16,384]{1,0:T(8,128)S(1)}, u32[]{:S(2)}, u32[]{:S(2)}) collective-permute-start(f32[16,384]{1,0:T(8,128)S(1)} %get-tuple-element.35), channel_id=1, source_target_pairs={{0,16},{1,17},{2,18},{3,19},{4,20},{5,21},{6,22},{7,23},{8,24},{9,... | collective-permute-start | bytes 73736 | tf_op jit(solution)/shard_map/ppermute | solution.py:95
  48.3 1.3 %collective-permute-start.12 = (bf16[128,256]{1,0:T(8,128)(2,1)S(1)}, bf16[128,256]{1,0:T(8,128)(2,1)S(1)}, u32[]{:S(2)}, u32[]{:S(2)}) collective-permute-start(bf16[128,256]{1,0:T(8,128)(2,1)S(1)} %get-tuple-element.40), channel_id=1, source_target_pairs={{4,0},{5,1},{6,2},{7,3},{8,12},{9,13},{10,14},{11,15},{20,16},{21,... | collective-permute-start | bytes 196616 | tf_op jit(solution)/shard_map/ppermute | solution.py:95
  49.6 1.3 %collective-permute-start.8 = (f32[16,144]{1,0:T(8,128)S(1)}, f32[16,144]{1,0:T(8,128)S(1)}, u32[]{:S(2)}, u32[]{:S(2)}) collective-permute-start(f32[16,144]{1,0:T(8,128)S(1)} %get-tuple-element.36), channel_id=1, source_target_pairs={{4,0},{5,1},{6,2},{7,3},{8,12},{9,13},{10,14},{11,15},{20,16},{21,... | collective-permute-start | bytes 27656 | tf_op jit(solution)/shard_map/ppermute | solution.py:95
  50.9 1.3 %collective-permute-start.9 = (f32[16,144]{1,0:T(8,128)S(1)}, f32[16,144]{1,0:T(8,128)S(1)}, u32[]{:S(2)}, u32[]{:S(2)}) collective-permute-start(f32[16,144]{1,0:T(8,128)S(1)} %get-tuple-element.37), channel_id=1, source_target_pairs={{4,16},{5,17},{6,18},{7,19},{8,28},{9,29},{10,30},{11,31},{20,0},{... | collective-permute-start | bytes 27656 | tf_op jit(solution)/shard_map/ppermute | solution.py:95
  52.2 3.1 %collective-permute-done.8.refs_0_ = f32[16,144]{1,0:T(8,128)S(1)} collective-permute-done((f32[16,144]{1,0:T(8,128)S(1)}, f32[16,144]{1,0:T(8,128)S(1)}, u32[]{:S(2)}, u32[]{:S(2)}) %collective-permute-start.8) | collective-permute-done | bytes 9248 | tf_op jit(solution)/shard_map/ppermute | solution.py:95
  55.3 2.1 %collective-permute-done.9.refs_1_ = f32[16,144]{1,0:T(8,128)S(1)} collective-permute-done((f32[16,144]{1,0:T(8,128)S(1)}, f32[16,144]{1,0:T(8,128)S(1)}, u32[]{:S(2)}, u32[]{:S(2)}) %collective-permute-start.9) | collective-permute-done | bytes 9248 | tf_op jit(solution)/shard_map/ppermute | solution.py:95
  57.4 0.0 collective-permute-done.7.near
  57.4 0.2 shard_map.70
  57.6 1.7 %collective-permute-start.10 = (f32[16,384]{1,0:T(8,128)S(1)}, f32[16,384]{1,0:T(8,128)S(1)}, u32[]{:S(2)}, u32[]{:S(2)}) collective-permute-start(f32[16,384]{1,0:T(8,128)S(1)} %shard_map.70), channel_id=1, source_target_pairs={{0,2},{1,3},{2,0},{3,1},{4,6},{5,7},{6,4},{7,5},{8,10},{9,11},{10,... | collective-permute-start | bytes 73736 | tf_op jit(solution)/shard_map/ppermute | solution.py:95
  59.3 2.2 %collective-permute-done.10 = f32[16,384]{1,0:T(8,128)S(1)} collective-permute-done((f32[16,384]{1,0:T(8,128)S(1)}, f32[16,384]{1,0:T(8,128)S(1)}, u32[]{:S(2)}, u32[]{:S(2)}) %collective-permute-start.10) | collective-permute-done | bytes 24608 | tf_op jit(solution)/shard_map/ppermute | solution.py:95
  61.4 0.0 collective-permute-start.11
  61.4 0.0 collective-permute-done.12.distant
  61.4 1.3 %shard_map.71.ups = bf16[1024,128]{1,0:T(8,128)(2,1)S(1)} custom-call(bf16[1152,256]{1,0:T(8,128)(2,1)S(1)} %shard_map.64.refs_2_.own, bf16[1152,256]{1,0:T(8,128)(2,1)} %collective-permute-done.3.refs_3_.beside, bf16[1152,256]{1,0:T(8,128)(2,1)} %collective-permute-done.4.refs_4_.mirror, bf16[1152,256]{1,0:T(8,128)(2,1)S(1)} %collective-permute-done.5.refs_7_.inside, ...), custom_call_target="tpu_custom_call" | custom-call | bytes 3276800 | tf_op jit(solution)/shard_map/pallas_call | solution.py:113
  62.7 0.0 collective-permute-done.11.far
  62.8 1.3 %shard_map.72 = bf16[384,128]{1,0:T(8,128)(2,1)} custom-call(f32[16,384]{1,0:T(8,128)S(1)} %add.3.near, f32[16,384]{1,0:T(8,128)S(1)} %collective-permute-done.11.far, f32[384,128]{1,0:T(8,128)S(1)} %get-tuple-element.38.base, f32[384,1]{1,0:T(8,128)S(1)} %get-tuple-element.39.numbers, bf16[1024,128]{1,0:T(8,128)(2,1)S(1)} %shard_map.71.ups), custom_call_target="tpu_custom_call" | custom-call | bytes 607744 | tf_op jit(solution)/shard_map/pallas_call | solution.py:113
  (4 shorter events, 0.0 us)
Async XLA Ops:
  0.0 6.9 %copy-start = (bf16[384,2048]{1,0:T(8,128)(2,1)S(1)}, bf16[384,2048]{1,0:T(8,128)(2,1)}, u32[]{:S(2)}) copy-start(bf16[384,2048]{1,0:T(8,128)(2,1)} %tokens.1) | copy-start | bytes 4718596
  0.0 1.3 %copy-start.1 = (bf16[2048,256]{1,0:T(8,128)(2,1)S(1)}, bf16[2048,256]{1,0:T(8,128)(2,1)}, u32[]{:S(2)}) copy-start(bf16[2048,256]{1,0:T(8,128)(2,1)} %down.1) | copy-start | bytes 3145732
  1.3 0.8 %copy-start.2 = (bf16[256,128]{1,0:T(8,128)(2,1)S(1)}, bf16[256,128]{1,0:T(8,128)(2,1)}, u32[]{:S(2)}) copy-start(bf16[256,128]{1,0:T(8,128)(2,1)} %up.1) | copy-start | bytes 196612
  2.3 18.7 %collective-permute-start.3 = (bf16[1152,256]{1,0:T(8,128)(2,1)S(1)}, bf16[1152,256]{1,0:T(8,128)(2,1)}, u32[]{:S(2)}, u32[]{:S(2)}) collective-permute-start(bf16[1152,256]{1,0:T(8,128)(2,1)S(1)} %shard_map.64.refs_2_.own), channel_id=1, source_target_pairs={{0,4},{1,5},{2,6},{3,7},{4,0},{5,1},{6,2},{7,3},{8,12},{9,13},{10,... | collective-permute-start | bytes 1769480 | tf_op jit(solution)/shard_map/ppermute | solution.py:95
  5.4 16.3 %collective-permute-start.4 = (bf16[1152,256]{1,0:T(8,128)(2,1)S(1)}, bf16[1152,256]{1,0:T(8,128)(2,1)}, u32[]{:S(2)}, u32[]{:S(2)}) collective-permute-start(bf16[1152,256]{1,0:T(8,128)(2,1)S(1)} %shard_map.64.refs_2_.own), channel_id=1, source_target_pairs={{4,8},{5,9},{6,10},{7,11},{8,4},{9,5},{10,6},{11,7},{20,24},{21,25... | collective-permute-start | bytes 1769480 | tf_op jit(solution)/shard_map/ppermute | solution.py:95
  6.9 0.7 %copy-start.3 = (s32[384]{0:T(512)S(1)}, s32[384]{0:T(512)}, u32[]{:S(2)}) copy-start(s32[384]{0:T(512)} %slot) | copy-start | bytes 4612
  7.5 0.7 %copy-start.4 = (s32[384,1]{0,1:T(1,128)S(1)}, s32[384,1]{0,1:T(1,128)}, u32[]{:S(2)}) copy-start(s32[384,1]{0,1:T(1,128)} %param.10) | copy-start | bytes 4612
  9.3 23.3 %collective-permute-start = (bf16[400,1024]{1,0:T(8,128)(2,1)}, bf16[400,1024]{1,0:T(8,128)(2,1)}, u32[]{:S(2)}, u32[]{:S(2)}) collective-permute-start(bf16[400,1024]{1,0:T(8,128)(2,1)} %get-tuple-element.25.away), channel_id=1, source_target_pairs={{0,16},{1,17},{2,18},{3,19},{4,20},{5,21},{6,22},{7,23},{8,24},{9,... | collective-permute-start | bytes 2457608 | tf_op jit(solution)/shard_map/ppermute | solution.py:95
  10.9 1.6 %copy-start.5 = (bf16[2048,512]{1,0:T(8,128)(2,1)S(1)}, bf16[2048,512]{1,0:T(8,128)(2,1)}, u32[]{:S(2)}) copy-start(bf16[2048,512]{1,0:T(8,128)(2,1)} %weights.1) | copy-start | bytes 6291460
  16.0 0.7 %copy-start.6 = (bf16[160,1024]{1,0:T(8,128)(2,1)}, bf16[160,1024]{1,0:T(8,128)(2,1)S(1)}, u32[]{:S(2)}) copy-start(bf16[160,1024]{1,0:T(8,128)(2,1)S(1)} %get-tuple-element.26) | copy-start | bytes 983044
  16.7 15.9 %all-to-all-start = ((f32[4,384,128]{2,1,0:T(8,128)}), f32[4,384,128]{2,1,0:T(8,128)}, u32[]{:S(2)}, u32[]{:S(2)}) async-start(f32[4,384,128]{2,1,0:T(8,128)} %get-tuple-element.28), calls=%async_computation | async-start | bytes 1572864 | tf_op jit(solution)/shard_map/all_to_all | solution.py:408
  20.9 23.9 %collective-permute-start.5 = (bf16[1152,256]{1,0:T(8,128)(2,1)}, bf16[1152,256]{1,0:T(8,128)(2,1)S(1)}, u32[]{:S(2)}, u32[]{:S(2)}) collective-permute-start(bf16[1152,256]{1,0:T(8,128)(2,1)} %collective-permute-done.3.refs_3_.beside), channel_id=1, source_target_pairs={{4,8},{5,9},{6,10},{7,11},{8,4},{9,5},{10,6},{11,7},{20,24},{21,25... | collective-permute-start | bytes 1769480 | tf_op jit(solution)/shard_map/ppermute | solution.py:95
  21.7 23.2 %collective-permute-start.6 = (bf16[1152,256]{1,0:T(8,128)(2,1)}, bf16[1152,256]{1,0:T(8,128)(2,1)S(1)}, u32[]{:S(2)}, u32[]{:S(2)}) collective-permute-start(bf16[1152,256]{1,0:T(8,128)(2,1)} %collective-permute-done.4.refs_4_.mirror), channel_id=1, source_target_pairs={{4,0},{5,1},{6,2},{7,3},{8,12},{9,13},{10,14},{11,15},{20,16},{21,... | collective-permute-start | bytes 1769480 | tf_op jit(solution)/shard_map/ppermute | solution.py:95
  23.0 15.0 %collective-permute-start.2 = (bf16[160,1024]{1,0:T(8,128)(2,1)}, bf16[160,1024]{1,0:T(8,128)(2,1)S(1)}, u32[]{:S(2)}, u32[]{:S(2)}) collective-permute-start(bf16[160,1024]{1,0:T(8,128)(2,1)} %get-tuple-element.27), channel_id=1, source_target_pairs={{0,20},{1,21},{2,22},{3,23},{12,24},{13,25},{14,26},{15,27},{16,4}... | collective-permute-start | bytes 983048 | tf_op jit(solution)/shard_map/ppermute | solution.py:95
  29.7 14.9 %collective-permute-start.1 = (bf16[160,1024]{1,0:T(8,128)(2,1)}, bf16[160,1024]{1,0:T(8,128)(2,1)S(1)}, u32[]{:S(2)}, u32[]{:S(2)}) collective-permute-start(bf16[160,1024]{1,0:T(8,128)(2,1)} %copy-done.6), channel_id=1, source_target_pairs={{0,4},{1,5},{2,6},{3,7},{12,8},{13,9},{14,10},{15,11},{16,20},{17,... | collective-permute-start | bytes 983048 | tf_op jit(solution)/shard_map/ppermute | solution.py:95
  46.7 10.7 %collective-permute-start.7 = (f32[16,384]{1,0:T(8,128)S(1)}, f32[16,384]{1,0:T(8,128)S(1)}, u32[]{:S(2)}, u32[]{:S(2)}) collective-permute-start(f32[16,384]{1,0:T(8,128)S(1)} %get-tuple-element.35), channel_id=1, source_target_pairs={{0,16},{1,17},{2,18},{3,19},{4,20},{5,21},{6,22},{7,23},{8,24},{9,... | collective-permute-start | bytes 73736 | tf_op jit(solution)/shard_map/ppermute | solution.py:95
  48.3 13.1 %collective-permute-start.12 = (bf16[128,256]{1,0:T(8,128)(2,1)S(1)}, bf16[128,256]{1,0:T(8,128)(2,1)S(1)}, u32[]{:S(2)}, u32[]{:S(2)}) collective-permute-start(bf16[128,256]{1,0:T(8,128)(2,1)S(1)} %get-tuple-element.40), channel_id=1, source_target_pairs={{4,0},{5,1},{6,2},{7,3},{8,12},{9,13},{10,14},{11,15},{20,16},{21,... | collective-permute-start | bytes 196616 | tf_op jit(solution)/shard_map/ppermute | solution.py:95
  49.6 5.7 %collective-permute-start.8 = (f32[16,144]{1,0:T(8,128)S(1)}, f32[16,144]{1,0:T(8,128)S(1)}, u32[]{:S(2)}, u32[]{:S(2)}) collective-permute-start(f32[16,144]{1,0:T(8,128)S(1)} %get-tuple-element.36), channel_id=1, source_target_pairs={{4,0},{5,1},{6,2},{7,3},{8,12},{9,13},{10,14},{11,15},{20,16},{21,... | collective-permute-start | bytes 27656 | tf_op jit(solution)/shard_map/ppermute | solution.py:95
  50.9 6.5 %collective-permute-start.9 = (f32[16,144]{1,0:T(8,128)S(1)}, f32[16,144]{1,0:T(8,128)S(1)}, u32[]{:S(2)}, u32[]{:S(2)}) collective-permute-start(f32[16,144]{1,0:T(8,128)S(1)} %get-tuple-element.37), channel_id=1, source_target_pairs={{4,16},{5,17},{6,18},{7,19},{8,28},{9,29},{10,30},{11,31},{20,0},{... | collective-permute-start | bytes 27656 | tf_op jit(solution)/shard_map/ppermute | solution.py:95
  57.6 3.9 %collective-permute-start.10 = (f32[16,384]{1,0:T(8,128)S(1)}, f32[16,384]{1,0:T(8,128)S(1)}, u32[]{:S(2)}, u32[]{:S(2)}) collective-permute-start(f32[16,384]{1,0:T(8,128)S(1)} %shard_map.70), channel_id=1, source_target_pairs={{0,2},{1,3},{2,0},{3,1},{4,6},{5,7},{6,4},{7,5},{8,10},{9,11},{10,... | collective-permute-start | bytes 73736 | tf_op jit(solution)/shard_map/ppermute | solution.py:95
  61.4 1.3 %collective-permute-start.11 = (f32[16,384]{1,0:T(8,128)S(1)}, f32[16,384]{1,0:T(8,128)S(1)}, u32[]{:S(2)}, u32[]{:S(2)}) collective-permute-start(f32[16,384]{1,0:T(8,128)S(1)} %add.3.near), channel_id=1, source_target_pairs={{0,1},{1,0},{2,3},{3,2},{4,5},{5,4},{6,7},{7,6},{8,9},{9,8},{10,11... | collective-permute-start | bytes 73736 | tf_op jit(solution)/shard_map/ppermute | solution.py:95

commit v8 on v7

--- a/solution.py
+++ b/solution.py
@@ -76,6 +76,7 @@
 
 AXES = ("groups", "adapter", "mp")
 ID_ROWS = 16
+HOP_URGENCY = 12 * 10**9
 OWNERS = 4
 LANES = 128
 
@@ -98,6 +99,7 @@
 SAME = tuple((a, a) for a in range(OWNERS))
 BESIDE = ((0, 1), (1, 0), (2, 3), (3, 2))
 MIDDLE = ((1, 2), (2, 1))
+ENDS = ((0, 3), (3, 0))
 OUTWARD = ((1, 0), (2, 3))
 INWARD = ((0, 1), (3, 2))
 
@@ -229,12 +231,18 @@
     return low
 
 
+def stacked(wide, keys):
+    return jnp.concatenate([wide[:, k : k + keys] for k in range(0, wide.shape[1], keys)], axis=0)
+
+
 def early_body(bits, part, rows, *refs):
     groups = lax.axis_size("groups")
     a = lax.axis_index("adapter")
     token_refs, rest = refs[:groups], refs[groups:]
-    blocks, (bases, folded, mask, numbers, base) = rest[: len(bits)], rest[len(bits) :]
+    blocks, (bases, folded, mask, numbers, base, ups) = rest[: len(bits)], rest[len(bits) :]
     columns = blocks[0].shape[1]
+    for n, block in enumerate(blocks):
+        ups[n] = stacked(block[part:, :], ups.shape[2])
     total = bases[0]
     for k in range(1, bases.shape[0]):
         total = total + bases[k]
@@ -266,8 +274,8 @@
     a = lax.axis_index("adapter")
     token_refs, rest = refs[:groups], refs[groups:]
     hops, rest = rest[:groups], rest[groups:]
-    hop_mask, folded, mask, inside, outside = rest[:5]
-    lows, hop_lows, far_ups = rest[5 : 5 + groups], rest[5 + groups : -1], rest[-1]
+    hop_mask, folded, mask, outside, inside = rest[:5]
+    lows, hop_lows, last_up = rest[5 : 5 + groups], rest[5 + groups : -1], rest[-1]
     columns = inside.shape[1]
 
     def finish(block):
@@ -281,7 +289,7 @@
     @pl.when(middle)
     def _():
         finish(inside)
-        far_ups[...] = inside[part:, :]
+        last_up[...] = stacked(inside[part:, :], last_up.shape[1])
         for n, (hop, out) in enumerate(zip(hops, hop_lows)):
             wide = jnp.dot(hop[:capacity, :], inside[:part, :], preferred_element_type=jnp.float32)
             kept = fold(jnp.where(hop_mask[n] > 0, wide, 0.0))
@@ -292,7 +300,7 @@
     @pl.when(jnp.logical_not(middle))
     def _():
         finish(outside)
-        far_ups[...] = outside[part:, :]
+        last_up[...] = stacked(outside[part:, :], last_up.shape[1])
         for out in hop_lows:
             out[...] = jnp.zeros(out.shape, jnp.float32)
 
@@ -310,47 +318,23 @@
     out[...] = low[...] + near[...] + spread
 
 
-def ups_body(keys, part, own, beside, mirror, inside, outside, distant, out):
-    a = lax.axis_index("adapter")
-    columns = own.shape[1]
-    count = columns // keys
-    size = columns // count
-
-    def place(number, block, first=part):
-        for k in range(count):
-            start = number * columns + k * size
-            out[start : start + size, :] = block[first:, k * keys : (k + 1) * keys]
-
-    place(0, own)
-    place(1, beside)
-    middle = (a == 1) | (a == 2)
-
-    @pl.when(middle)
-    def _():
-        place(2, inside)
-        place(3, mirror)
-
-    @pl.when(jnp.logical_not(middle))
-    def _():
-        place(2, outside)
-        place(3, distant, 0)
-
-
-def finish_body(near, far, base, numbers, ups, out):
+def finish_body(near, far, base, numbers, ups, last_up, distant, out):
     a = lax.axis_index("adapter")
     rows = out.shape[0]
-    columns = ups.shape[0] // OWNERS
+    columns = last_up.shape[0]
     column = lax.broadcasted_iota(jnp.int32, (ADAPTER_RANK, columns), 1)
     row = lax.broadcasted_iota(jnp.int32, (ADAPTER_RANK, columns), 0)
     repeat = (lax.rem(column, ADAPTER_RANK) == row).astype(jnp.bfloat16)
     shrunk = (near[...] + far[...]).astype(jnp.bfloat16)
     spread = lax.dot_general(shrunk, repeat, TN, preferred_element_type=jnp.float32)
     adapter = adapters(rows, columns)
+    middle = (a == 1) | (a == 2)
+    mirrored = jnp.where(middle, ups[1].astype(jnp.float32), distant[...].astype(jnp.float32))
+    blocks = ((0, ups[0]), (1, ups[2]), (2, last_up[...]), (3, mirrored.astype(jnp.bfloat16)))
     updates = jnp.zeros(out.shape, jnp.float32)
-    for i in range(OWNERS):
-        wanted = numbers[...] - ((a ^ i) * (columns // ADAPTER_RANK)).astype(jnp.float32)
+    for bit, up in blocks:
+        wanted = numbers[...] - ((a ^ bit) * (columns // ADAPTER_RANK)).astype(jnp.float32)
         chosen = jnp.where(adapter == wanted, spread, 0.0).astype(jnp.bfloat16)
-        up = ups[i * columns : (i + 1) * columns, :]
         updates = updates + jnp.dot(chosen, up, preferred_element_type=jnp.float32)
     updates = updates.astype(jnp.bfloat16).astype(jnp.float32)
     out[...] = (base[...] + ADAPTER_SCALE * updates).astype(jnp.bfloat16)
@@ -414,40 +398,40 @@
         exchange(hop_away, 1, 0, INWARD),
     ]
 
-    folded, mask, numbers, base = kernel(
-        functools.partial(early_body, (0, 1, 3), part, rows),
-        [wide(groups, rows, LANES), wide(groups, rows, columns), wide(rows, 1), wide(rows, keys)],
-        (*token_parts, own, beside, mirror, bases),
+    folded, mask, numbers, base, ups = kernel(
+        functools.partial(early_body, (0, 3, 1), part, rows),
+        [wide(groups, rows, LANES), wide(groups, rows, columns), wide(rows, 1), wide(rows, keys), narrow(3, columns, keys)],
+        (*token_parts, own, mirror, beside, bases),
         6 * groups * rows * part * columns,
     )
+    distant = exchange(after(stacked_up_weight, folded), 0, 0, ENDS)
     hop_mask = kernel(
-        functools.partial(hop_mask_body, capacity), wide(groups, capacity, columns), (hops[0], after(hops[1], folded))
-    )
-    low, low_away, back, back_away, far_ups = kernel(
+        functools.partial(hop_mask_body, capacity),
+        wide(groups, capacity, columns),
+        (hops[0], after(hops[1], folded)),
+        HOP_URGENCY,
+    )
+    low, low_away, back, back_away, last_up = kernel(
         functools.partial(last_body, part, rows, capacity),
         [wide(ADAPTER_RANK, rows)] * groups
         + [wide(ADAPTER_RANK, capacity)] * groups
-        + [narrow(columns // half, columns)],
-        (*token_parts, *hops, hop_mask, folded, mask, inside, outside),
+        + [narrow(columns, keys)],
+        (*token_parts, *hops, hop_mask, after(folded, distant), mask, outside, inside),
         2 * groups * (rows + capacity) * part * columns,
     )
 
     near = exchange(low_away, 1, 0, SAME)
     back = exchange(back, 0, 0, OUTWARD)
     back_away = exchange(back_away, 1, 0, OUTWARD)
-    distant = exchange(far_ups, 0, 0, OUTWARD)
     low = kernel(merge_body, wide(ADAPTER_RANK, rows), (low, near, places, back, back_away))
     bit = shares // 2
     while bit > 1:
         low = low + exchange(low, 0, bit, SAME)
         bit //= 2
     low_far = exchange(low, 0, 1, SAME)
-    ups = kernel(
-        functools.partial(ups_body, keys, part),
-        narrow(owners * columns, keys),
-        (own, beside, mirror, inside, outside, distant),
-    )
-    return kernel(finish_body, narrow(rows, keys), (low, low_far, base, numbers, ups))
+    return kernel(
+        finish_body, narrow(rows, keys), (low, low_far, base, numbers, ups, last_up, distant)
+    )
 
 
 def row_limit(rows):

time: 64.6 us -> 63.5 us (0.983)
  local copies, waits for them, and re-layouts: 5.86 us -> 5.14 us
  starting transfers between devices: 27.5 us -> 26.8 us
    all_to_all x1, waiting for transfers between devices: 1.62 us -> 4.89 us  [gather(): bases = lax.all_to_all(bases, 'mp', 0, 0, tiled=True)]
    ppermute x13, waiting for transfers between devices: 16 us -> 12.9 us  [exchange(): return lax.ppermute(x, AXES, pairs)]
    unnamed x14, local copies, waits for them, and re-layouts: 5.86 us -> 5.14 us
    all_to_all x1, starting transfers between devices: 4.19 us -> 3.49 us  [gather(): bases = lax.all_to_all(bases, 'mp', 0, 0, tiled=True)]
    pallas_call x9 -> x8, Pallas kernels: 12.8 us -> 13 us  [kernel(): pl.pallas_call(body, out_shape=outs, in_specs=specs or [inner] * len(oper...]
  transfers between devices with their start and end apart: 14 -> 14, of which waited for: 6 -> 8; matrix products, arithmetic and copies ran while one was open for 0% -> 0% of each run, Pallas kernels for 15% -> 12%
where the time goes in v8:
time: 63.5 us; the launch traced here: 62.9 us
  starting transfers between devices  26.8 us (42%)
  waiting for transfers between devices  17.8 us (28%)
  Pallas kernels  13 us (20%)
  local copies, waits for them, and re-layouts  5.14 us (8%)
    ppermute x13, starting transfers between devices, exchange(): return lax.ppermute(x, AXES, pairs)  23.3 us
    pallas_call x8, Pallas kernels, kernel(): pl.pallas_call(body, out_shape=outs, in_specs=specs or [inner] * len(oper...  13 us
    ppermute x13, waiting for transfers between devices, exchange(): return lax.ppermute(x, AXES, pairs)  12.9 us
    unnamed x14, local copies, waits for them, and re-layouts  5.14 us
    all_to_all x1, waiting for transfers between devices, gather(): bases = lax.all_to_all(bases, 'mp', 0, 0, tiled=True)  4.89 us
    all_to_all x1, starting transfers between devices, gather(): bases = lax.all_to_all(bases, 'mp', 0, 0, tiled=True)  3.49 us
  transfers between devices with their start and end apart: 14, of which 8 were waited for; matrix products, arithmetic and copies ran while one was open for 0% of the time, Pallas kernels for 12%

profile of v8, /device:TPU:0, one launch (start us, length us, event | category | flops | bytes accessed | tf_op | source)
XLA Modules:
  0.0 62.9 jit_solution(14130683869302062794)
XLA Ops:
  0.0 0.0 copy-start
  0.0 0.0 copy-start.1
  0.0 1.3 %copy-done.1 = bf16[2048,256]{1,0:T(8,128)(2,1)S(1)} copy-done((bf16[2048,256]{1,0:T(8,128)(2,1)S(1)}, bf16[2048,256]{1,0:T(8,128)(2,1)}, u32[]{:S(2)}) %copy-start.1) | copy-done | bytes 1048600
  1.3 0.0 copy-start.2
  1.3 0.8 %copy-done.2 = bf16[256,128]{1,0:T(8,128)(2,1)S(1)} copy-done((bf16[256,128]{1,0:T(8,128)(2,1)S(1)}, bf16[256,128]{1,0:T(8,128)(2,1)}, u32[]{:S(2)}) %copy-start.2) | copy-done | bytes 65560
  2.2 0.9 %shard_map.64.refs_2_ = bf16[1152,256]{1,0:T(8,128)(2,1)} custom-call(bf16[2048,256]{1,0:T(8,128)(2,1)S(1)} %copy-done.1, bf16[256,128]{1,0:T(8,128)(2,1)S(1)} %copy-done.2), custom_call_target="tpu_custom_call" | custom-call | bytes 1703936 | tf_op jit(solution)/shard_map/pallas_call | solution.py:115
  3.1 0.0 copy-done
  3.1 0.0 copy-start.4
  3.1 0.7 %copy-done.4 = s32[384]{0:T(512)S(1)} copy-done((s32[384]{0:T(512)S(1)}, s32[384]{0:T(512)}, u32[]{:S(2)}) %copy-start.4) | copy-done | bytes 1560
  3.8 0.0 copy-start.5
  3.8 0.7 %copy-done.5 = s32[384,1]{0,1:T(1,128)S(1)} copy-done((s32[384,1]{0,1:T(1,128)S(1)}, s32[384,1]{0,1:T(1,128)}, u32[]{:S(2)}) %copy-start.5) | copy-done | bytes 1560
  4.5 1.0 %shard_map.65 = (bf16[400,1024]{1,0:T(8,128)(2,1)S(1)}, bf16[400,1024]{1,0:T(8,128)(2,1)}) custom-call(bf16[384,2048]{1,0:T(8,128)(2,1)S(1)} %copy-done, s32[1,384]{1,0:T(1,128)S(1)} %bitcast.1, s32[384]{0:T(512)S(1)} %copy-done.4), custom_call_target="tpu_custom_call" | custom-call | bytes 3214336 | tf_op jit(solution)/shard_map/pallas_call | solution.py:115
  5.5 3.0 %collective-permute-start = (bf16[400,1024]{1,0:T(8,128)(2,1)}, bf16[400,1024]{1,0:T(8,128)(2,1)S(1)}, u32[]{:S(2)}, u32[]{:S(2)}) collective-permute-start(bf16[400,1024]{1,0:T(8,128)(2,1)} %get-tuple-element.28.away), channel_id=1, source_target_pairs={{0,16},{1,17},{2,18},{3,19},{4,20},{5,21},{6,22},{7,23},{8,24},{9,... | collective-permute-start | bytes 2457608 | tf_op jit(solution)/shard_map/ppermute | solution.py:96
  8.5 1.5 %collective-permute-start.3 = (bf16[1152,256]{1,0:T(8,128)(2,1)}, bf16[1152,256]{1,0:T(8,128)(2,1)}, u32[]{:S(2)}, u32[]{:S(2)}) collective-permute-start(bf16[1152,256]{1,0:T(8,128)(2,1)} %shard_map.64.refs_2_), channel_id=1, source_target_pairs={{4,8},{5,9},{6,10},{7,11},{8,4},{9,5},{10,6},{11,7},{20,24},{21,25... | collective-permute-start | bytes 1769480 | tf_op jit(solution)/shard_map/ppermute | solution.py:96
  10.0 3.6 %collective-permute-start.4 = (bf16[1152,256]{1,0:T(8,128)(2,1)}, bf16[1152,256]{1,0:T(8,128)(2,1)}, u32[]{:S(2)}, u32[]{:S(2)}) collective-permute-start(bf16[1152,256]{1,0:T(8,128)(2,1)} %shard_map.64.refs_2_), channel_id=1, source_target_pairs={{0,4},{1,5},{2,6},{3,7},{4,0},{5,1},{6,2},{7,3},{8,12},{9,13},{10,... | collective-permute-start | bytes 1769480 | tf_op jit(solution)/shard_map/ppermute | solution.py:96
  13.7 1.6 %copy-done.6 = bf16[2048,512]{1,0:T(8,128)(2,1)S(1)} copy-done((bf16[2048,512]{1,0:T(8,128)(2,1)S(1)}, bf16[2048,512]{1,0:T(8,128)(2,1)}, u32[]{:S(2)}) %copy-start.6) | copy-done | bytes 2097176
  15.3 3.6 %shard_map.66 = (bf16[160,1024]{1,0:T(8,128)(2,1)}, bf16[160,1024]{1,0:T(8,128)(2,1)}, bf16[144,384]{1,0:T(8,128)(2,1)S(1)}, f32[4,384,128]{2,1,0:T(8,128)}) custom-call(bf16[400,1024]{1,0:T(8,128)(2,1)S(1)} %get-tuple-element.27.own.refs_0_, bf16[400,1024]{1,0:T(8,128)(2,1)} %get-tuple-element.28.away, bf16[2048,512]{1,0:T(8,128)(2,1)S(1)} %copy-done.6), custom_call_target="tpu_custom_call" | custom-call | flops 1031798784 | bytes 5287936 | tf_op jit(solution)/shard_map/pallas_call | solution.py:115
  18.8 3.5 %all-to-all-start = ((f32[4,384,128]{2,1,0:T(8,128)}), f32[4,384,128]{2,1,0:T(8,128)S(1)}, u32[]{:S(2)}, u32[]{:S(2)}) async-start(f32[4,384,128]{2,1,0:T(8,128)} %get-tuple-element.31), calls=%async_computation | async-start | bytes 1572864 | tf_op jit(solution)/shard_map/all_to_all | solution.py:392
  22.3 1.9 %collective-permute-start.2 = (bf16[160,1024]{1,0:T(8,128)(2,1)}, bf16[160,1024]{1,0:T(8,128)(2,1)S(1)}, u32[]{:S(2)}, u32[]{:S(2)}) collective-permute-start(bf16[160,1024]{1,0:T(8,128)(2,1)} %get-tuple-element.30), channel_id=1, source_target_pairs={{0,20},{1,21},{2,22},{3,23},{12,24},{13,25},{14,26},{15,27},{16,4}... | collective-permute-start | bytes 983048 | tf_op jit(solution)/shard_map/ppermute | solution.py:96
  24.2 2.1 %collective-permute-start.1 = (bf16[160,1024]{1,0:T(8,128)(2,1)}, bf16[160,1024]{1,0:T(8,128)(2,1)}, u32[]{:S(2)}, u32[]{:S(2)}) collective-permute-start(bf16[160,1024]{1,0:T(8,128)(2,1)} %get-tuple-element.29), channel_id=1, source_target_pairs={{0,4},{1,5},{2,6},{3,7},{12,8},{13,9},{14,10},{15,11},{16,20},{17,... | collective-permute-start | bytes 983048 | tf_op jit(solution)/shard_map/ppermute | solution.py:96
  26.3 0.6 %collective-permute-done.4.refs_4_ = bf16[1152,256]{1,0:T(8,128)(2,1)} collective-permute-done((bf16[1152,256]{1,0:T(8,128)(2,1)}, bf16[1152,256]{1,0:T(8,128)(2,1)}, u32[]{:S(2)}, u32[]{:S(2)}) %collective-permute-start.4) | collective-permute-done | bytes 589856 | tf_op jit(solution)/shard_map/ppermute | solution.py:96
  26.9 0.8 %collective-permute-start.7 = (bf16[1152,256]{1,0:T(8,128)(2,1)}, bf16[1152,256]{1,0:T(8,128)(2,1)S(1)}, u32[]{:S(2)}, u32[]{:S(2)}) collective-permute-start(bf16[1152,256]{1,0:T(8,128)(2,1)} %collective-permute-done.4.refs_4_), channel_id=1, source_target_pairs={{4,8},{5,9},{6,10},{7,11},{8,4},{9,5},{10,6},{11,7},{20,24},{21,25... | collective-permute-start | bytes 1769480 | tf_op jit(solution)/shard_map/ppermute | solution.py:96
  27.7 0.0 collective-permute-done.3.refs_3_
  27.7 1.3 %collective-permute-start.6 = (bf16[1152,256]{1,0:T(8,128)(2,1)}, bf16[1152,256]{1,0:T(8,128)(2,1)}, u32[]{:S(2)}, u32[]{:S(2)}) collective-permute-start(bf16[1152,256]{1,0:T(8,128)(2,1)} %collective-permute-done.3.refs_3_), channel_id=1, source_target_pairs={{4,0},{5,1},{6,2},{7,3},{8,12},{9,13},{10,14},{11,15},{20,16},{21,... | collective-permute-start | bytes 1769480 | tf_op jit(solution)/shard_map/ppermute | solution.py:96
  29.0 4.9 %all-to-all-done.refs_5_ = f32[4,384,128]{2,1,0:T(8,128)S(1)} async-done(((f32[4,384,128]{2,1,0:T(8,128)}), f32[4,384,128]{2,1,0:T(8,128)S(1)}, u32[]{:S(2)}, u32[]{:S(2)}) %all-to-all-start) | async-done | bytes 786464 | tf_op jit(solution)/shard_map/all_to_all | solution.py:392
  33.9 0.0 collective-permute-done.refs_1_
  33.9 3.0 %shard_map.67 = (f32[2,384,128]{2,1,0:T(8,128)S(1)}, f32[2,384,256]{2,1,0:T(8,128)S(1)}, f32[384,1]{1,0:T(8,128)S(1)}, f32[384,128]{1,0:T(8,128)S(1)}, bf16[3,256,128]{2,1,0:T(8,128)(2,1)S(1)}) custom-call(bf16[400,1024]{1,0:T(8,128)(2,1)S(1)} %get-tuple-element.27.own.refs_0_, bf16[400,1024]{1,0:T(8,128)(2,1)S(1)} %collective-permute-done.refs_1_, ...), custom_call_target="tpu_custom_call" | custom-call | flops 1207959552 | bytes 5768704 | tf_op jit(solution)/shard_map/pallas_call | solution.py:115
  36.9 0.0 copy-done.3
  36.9 3.3 %collective-permute-start.5 = (bf16[256,128]{1,0:T(8,128)(2,1)S(1)}, bf16[256,128]{1,0:T(8,128)(2,1)S(1)}, u32[]{:S(2)}, u32[]{:S(2)}) collective-permute-start(bf16[256,128]{1,0:T(8,128)(2,1)S(1)} %copy-done.3), channel_id=1, source_target_pairs={{0,12},{1,13},{2,14},{3,15},{12,0},{13,1},{14,2},{15,3},{16,28},{1... | collective-permute-start | bytes 196616 | tf_op jit(solution)/shard_map/ppermute | solution.py:96
  40.2 0.0 collective-permute-done.2.refs_1_.refs_3_
  40.2 0.0 collective-permute-done.1.refs_0_.refs_2_
  40.2 1.3 %shard_map.68.refs_4_ = f32[2,144,256]{2,1,0:T(8,128)S(1)} custom-call(bf16[160,1024]{1,0:T(8,128)(2,1)} %collective-permute-done.1.refs_0_.refs_2_, bf16[160,1024]{1,0:T(8,128)(2,1)S(1)} %collective-permute-done.2.refs_1_.refs_3_), custom_call_target="tpu_custom_call" | custom-call | flops 12000000000 | bytes 950272 | tf_op jit(solution)/shard_map/pallas_call | solution.py:115
  41.5 3.5 %collective-permute-done.5.distant = bf16[256,128]{1,0:T(8,128)(2,1)S(1)} collective-permute-done((bf16[256,128]{1,0:T(8,128)(2,1)S(1)}, bf16[256,128]{1,0:T(8,128)(2,1)S(1)}, u32[]{:S(2)}, u32[]{:S(2)}) %collective-permute-start.5) | collective-permute-done | bytes 65568 | tf_op jit(solution)/shard_map/ppermute | solution.py:96
  45.1 0.0 collective-permute-done.7.refs_8_
  45.1 1.1 %collective-permute-done.6.refs_7_ = bf16[1152,256]{1,0:T(8,128)(2,1)} collective-permute-done((bf16[1152,256]{1,0:T(8,128)(2,1)}, bf16[1152,256]{1,0:T(8,128)(2,1)}, u32[]{:S(2)}, u32[]{:S(2)}) %collective-permute-start.6) | collective-permute-done | bytes 589856 | tf_op jit(solution)/shard_map/ppermute | solution.py:96
  46.1 1.8 %shard_map.69 = (f32[16,384]{1,0:T(8,128)S(1)}, f32[16,384]{1,0:T(8,128)S(1)}, f32[16,144]{1,0:T(8,128)S(1)}, f32[16,144]{1,0:T(8,128)S(1)}, bf16[256,128]{1,0:T(8,128)(2,1)S(1)}) custom-call(bf16[400,1024]{1,0:T(8,128)(2,1)S(1)} %get-tuple-element.27.own.refs_0_, bf16[400,1024]{1,0:T(8,128)(2,1)S(1)} %collective-permute-done.refs_1_, ...), custom_call_target="tpu_custom_call" | custom-call | flops 553648128 | bytes 5081088 | tf_op jit(solution)/shard_map/pallas_call | solution.py:115
  48.0 1.5 %collective-permute-start.8 = (f32[16,384]{1,0:T(8,128)S(1)}, f32[16,384]{1,0:T(8,128)S(1)}, u32[]{:S(2)}, u32[]{:S(2)}) collective-permute-start(f32[16,384]{1,0:T(8,128)S(1)} %get-tuple-element.40), channel_id=1, source_target_pairs={{0,16},{1,17},{2,18},{3,19},{4,20},{5,21},{6,22},{7,23},{8,24},{9,... | collective-permute-start | bytes 73736 | tf_op jit(solution)/shard_map/ppermute | solution.py:96
  49.5 1.3 %collective-permute-start.10 = (f32[16,144]{1,0:T(8,128)S(1)}, f32[16,144]{1,0:T(8,128)S(1)}, u32[]{:S(2)}, u32[]{:S(2)}) collective-permute-start(f32[16,144]{1,0:T(8,128)S(1)} %get-tuple-element.42), channel_id=1, source_target_pairs={{4,16},{5,17},{6,18},{7,19},{8,28},{9,29},{10,30},{11,31},{20,0},{... | collective-permute-start | bytes 27656 | tf_op jit(solution)/shard_map/ppermute | solution.py:96
  50.8 1.3 %collective-permute-start.9 = (f32[16,144]{1,0:T(8,128)S(1)}, f32[16,144]{1,0:T(8,128)S(1)}, u32[]{:S(2)}, u32[]{:S(2)}) collective-permute-start(f32[16,144]{1,0:T(8,128)S(1)} %get-tuple-element.41), channel_id=1, source_target_pairs={{4,0},{5,1},{6,2},{7,3},{8,12},{9,13},{10,14},{11,15},{20,16},{21,... | collective-permute-start | bytes 27656 | tf_op jit(solution)/shard_map/ppermute | solution.py:96
  52.1 3.9 %collective-permute-done.10.refs_1_ = f32[16,144]{1,0:T(8,128)S(1)} collective-permute-done((f32[16,144]{1,0:T(8,128)S(1)}, f32[16,144]{1,0:T(8,128)S(1)}, u32[]{:S(2)}, u32[]{:S(2)}) %collective-permute-start.10) | collective-permute-done | bytes 9248 | tf_op jit(solution)/shard_map/ppermute | solution.py:96
  56.0 0.4 collective-permute-done.9.refs_0_
  56.5 0.0 collective-permute-done.8.near
  56.5 0.2 shard_map.70
  56.6 1.7 %collective-permute-start.11 = (f32[16,384]{1,0:T(8,128)S(1)}, f32[16,384]{1,0:T(8,128)S(1)}, u32[]{:S(2)}, u32[]{:S(2)}) collective-permute-start(f32[16,384]{1,0:T(8,128)S(1)} %shard_map.70), channel_id=1, source_target_pairs={{0,2},{1,3},{2,0},{3,1},{4,6},{5,7},{6,4},{7,5},{8,10},{9,11},{10,... | collective-permute-start | bytes 73736 | tf_op jit(solution)/shard_map/ppermute | solution.py:96
  58.3 2.2 %collective-permute-done.11 = f32[16,384]{1,0:T(8,128)S(1)} collective-permute-done((f32[16,384]{1,0:T(8,128)S(1)}, f32[16,384]{1,0:T(8,128)S(1)}, u32[]{:S(2)}, u32[]{:S(2)}) %collective-permute-start.11) | collective-permute-done | bytes 24608 | tf_op jit(solution)/shard_map/ppermute | solution.py:96
  60.5 0.0 collective-permute-start.12
  60.5 1.2 %collective-permute-done.12.far = f32[16,384]{1,0:T(8,128)S(1)} collective-permute-done((f32[16,384]{1,0:T(8,128)S(1)}, f32[16,384]{1,0:T(8,128)S(1)}, u32[]{:S(2)}, u32[]{:S(2)}) %collective-permute-start.12) | collective-permute-done | bytes 24608 | tf_op jit(solution)/shard_map/ppermute | solution.py:96
  61.7 1.3 %shard_map.71 = bf16[384,128]{1,0:T(8,128)(2,1)} custom-call(f32[16,384]{1,0:T(8,128)S(1)} %add.3.near, f32[16,384]{1,0:T(8,128)S(1)} %collective-permute-done.12.far, f32[384,128]{1,0:T(8,128)S(1)} %get-tuple-element.43.base, f32[384,1]{1,0:T(8,128)S(1)} %get-tuple-element.44.numbers, bf16[3,256,128]{2,1,0:T(8,128)(2,1)S(1)} %get-tuple-element.45.ups, ...), custom_call_target="tpu_custom_call" | custom-call | bytes 673280 | tf_op jit(solution)/shard_map/pallas_call | solution.py:115
  (3 shorter events, 0.0 us)
Async XLA Ops:
  0.0 3.1 %copy-start = (bf16[384,2048]{1,0:T(8,128)(2,1)S(1)}, bf16[384,2048]{1,0:T(8,128)(2,1)}, u32[]{:S(2)}) copy-start(bf16[384,2048]{1,0:T(8,128)(2,1)} %tokens.1) | copy-start | bytes 4718596
  0.0 1.3 %copy-start.1 = (bf16[2048,256]{1,0:T(8,128)(2,1)S(1)}, bf16[2048,256]{1,0:T(8,128)(2,1)}, u32[]{:S(2)}) copy-start(bf16[2048,256]{1,0:T(8,128)(2,1)} %down.1) | copy-start | bytes 3145732
  1.3 0.8 %copy-start.2 = (bf16[256,128]{1,0:T(8,128)(2,1)S(1)}, bf16[256,128]{1,0:T(8,128)(2,1)}, u32[]{:S(2)}) copy-start(bf16[256,128]{1,0:T(8,128)(2,1)} %up.1) | copy-start | bytes 196612
  3.1 0.7 %copy-start.4 = (s32[384]{0:T(512)S(1)}, s32[384]{0:T(512)}, u32[]{:S(2)}) copy-start(s32[384]{0:T(512)} %slot) | copy-start | bytes 4612
  3.8 0.7 %copy-start.5 = (s32[384,1]{0,1:T(1,128)S(1)}, s32[384,1]{0,1:T(1,128)}, u32[]{:S(2)}) copy-start(s32[384,1]{0,1:T(1,128)} %param.10) | copy-start | bytes 4612
  5.5 28.4 %collective-permute-start = (bf16[400,1024]{1,0:T(8,128)(2,1)}, bf16[400,1024]{1,0:T(8,128)(2,1)S(1)}, u32[]{:S(2)}, u32[]{:S(2)}) collective-permute-start(bf16[400,1024]{1,0:T(8,128)(2,1)} %get-tuple-element.28.away), channel_id=1, source_target_pairs={{0,16},{1,17},{2,18},{3,19},{4,20},{5,21},{6,22},{7,23},{8,24},{9,... | collective-permute-start | bytes 2457608 | tf_op jit(solution)/shard_map/ppermute | solution.py:96
  8.5 19.2 %collective-permute-start.3 = (bf16[1152,256]{1,0:T(8,128)(2,1)}, bf16[1152,256]{1,0:T(8,128)(2,1)}, u32[]{:S(2)}, u32[]{:S(2)}) collective-permute-start(bf16[1152,256]{1,0:T(8,128)(2,1)} %shard_map.64.refs_2_), channel_id=1, source_target_pairs={{4,8},{5,9},{6,10},{7,11},{8,4},{9,5},{10,6},{11,7},{20,24},{21,25... | collective-permute-start | bytes 1769480 | tf_op jit(solution)/shard_map/ppermute | solution.py:96
  10.0 16.9 %collective-permute-start.4 = (bf16[1152,256]{1,0:T(8,128)(2,1)}, bf16[1152,256]{1,0:T(8,128)(2,1)}, u32[]{:S(2)}, u32[]{:S(2)}) collective-permute-start(bf16[1152,256]{1,0:T(8,128)(2,1)} %shard_map.64.refs_2_), channel_id=1, source_target_pairs={{0,4},{1,5},{2,6},{3,7},{4,0},{5,1},{6,2},{7,3},{8,12},{9,13},{10,... | collective-permute-start | bytes 1769480 | tf_op jit(solution)/shard_map/ppermute | solution.py:96
  13.7 1.6 %copy-start.6 = (bf16[2048,512]{1,0:T(8,128)(2,1)S(1)}, bf16[2048,512]{1,0:T(8,128)(2,1)}, u32[]{:S(2)}) copy-start(bf16[2048,512]{1,0:T(8,128)(2,1)} %weights.1) | copy-start | bytes 6291460
  18.8 15.1 %all-to-all-start = ((f32[4,384,128]{2,1,0:T(8,128)}), f32[4,384,128]{2,1,0:T(8,128)S(1)}, u32[]{:S(2)}, u32[]{:S(2)}) async-start(f32[4,384,128]{2,1,0:T(8,128)} %get-tuple-element.31), calls=%async_computation | async-start | bytes 1572864 | tf_op jit(solution)/shard_map/all_to_all | solution.py:392
  22.3 17.9 %collective-permute-start.2 = (bf16[160,1024]{1,0:T(8,128)(2,1)}, bf16[160,1024]{1,0:T(8,128)(2,1)S(1)}, u32[]{:S(2)}, u32[]{:S(2)}) collective-permute-start(bf16[160,1024]{1,0:T(8,128)(2,1)} %get-tuple-element.30), channel_id=1, source_target_pairs={{0,20},{1,21},{2,22},{3,23},{12,24},{13,25},{14,26},{15,27},{16,4}... | collective-permute-start | bytes 983048 | tf_op jit(solution)/shard_map/ppermute | solution.py:96
  24.2 16.0 %collective-permute-start.1 = (bf16[160,1024]{1,0:T(8,128)(2,1)}, bf16[160,1024]{1,0:T(8,128)(2,1)}, u32[]{:S(2)}, u32[]{:S(2)}) collective-permute-start(bf16[160,1024]{1,0:T(8,128)(2,1)} %get-tuple-element.29), channel_id=1, source_target_pairs={{0,4},{1,5},{2,6},{3,7},{12,8},{13,9},{14,10},{15,11},{16,20},{17,... | collective-permute-start | bytes 983048 | tf_op jit(solution)/shard_map/ppermute | solution.py:96
  26.9 10.0 %copy-start.3 = (bf16[256,128]{1,0:T(8,128)(2,1)S(1)}, bf16[256,128]{1,0:T(8,128)(2,1)}, u32[]{:S(2)}) copy-start(bf16[256,128]{1,0:T(8,128)(2,1)} %up.1) | copy-start | bytes 196612
  26.9 18.2 %collective-permute-start.7 = (bf16[1152,256]{1,0:T(8,128)(2,1)}, bf16[1152,256]{1,0:T(8,128)(2,1)S(1)}, u32[]{:S(2)}, u32[]{:S(2)}) collective-permute-start(bf16[1152,256]{1,0:T(8,128)(2,1)} %collective-permute-done.4.refs_4_), channel_id=1, source_target_pairs={{4,8},{5,9},{6,10},{7,11},{8,4},{9,5},{10,6},{11,7},{20,24},{21,25... | collective-permute-start | bytes 1769480 | tf_op jit(solution)/shard_map/ppermute | solution.py:96
  27.7 18.4 %collective-permute-start.6 = (bf16[1152,256]{1,0:T(8,128)(2,1)}, bf16[1152,256]{1,0:T(8,128)(2,1)}, u32[]{:S(2)}, u32[]{:S(2)}) collective-permute-start(bf16[1152,256]{1,0:T(8,128)(2,1)} %collective-permute-done.3.refs_3_), channel_id=1, source_target_pairs={{4,0},{5,1},{6,2},{7,3},{8,12},{9,13},{10,14},{11,15},{20,16},{21,... | collective-permute-start | bytes 1769480 | tf_op jit(solution)/shard_map/ppermute | solution.py:96
  36.9 8.1 %collective-permute-start.5 = (bf16[256,128]{1,0:T(8,128)(2,1)S(1)}, bf16[256,128]{1,0:T(8,128)(2,1)S(1)}, u32[]{:S(2)}, u32[]{:S(2)}) collective-permute-start(bf16[256,128]{1,0:T(8,128)(2,1)S(1)} %copy-done.3), channel_id=1, source_target_pairs={{0,12},{1,13},{2,14},{3,15},{12,0},{13,1},{14,2},{15,3},{16,28},{1... | collective-permute-start | bytes 196616 | tf_op jit(solution)/shard_map/ppermute | solution.py:96
  48.0 8.5 %collective-permute-start.8 = (f32[16,384]{1,0:T(8,128)S(1)}, f32[16,384]{1,0:T(8,128)S(1)}, u32[]{:S(2)}, u32[]{:S(2)}) collective-permute-start(f32[16,384]{1,0:T(8,128)S(1)} %get-tuple-element.40), channel_id=1, source_target_pairs={{0,16},{1,17},{2,18},{3,19},{4,20},{5,21},{6,22},{7,23},{8,24},{9,... | collective-permute-start | bytes 73736 | tf_op jit(solution)/shard_map/ppermute | solution.py:96
  49.5 6.5 %collective-permute-start.10 = (f32[16,144]{1,0:T(8,128)S(1)}, f32[16,144]{1,0:T(8,128)S(1)}, u32[]{:S(2)}, u32[]{:S(2)}) collective-permute-start(f32[16,144]{1,0:T(8,128)S(1)} %get-tuple-element.42), channel_id=1, source_target_pairs={{4,16},{5,17},{6,18},{7,19},{8,28},{9,29},{10,30},{11,31},{20,0},{... | collective-permute-start | bytes 27656 | tf_op jit(solution)/shard_map/ppermute | solution.py:96
  50.8 5.6 %collective-permute-start.9 = (f32[16,144]{1,0:T(8,128)S(1)}, f32[16,144]{1,0:T(8,128)S(1)}, u32[]{:S(2)}, u32[]{:S(2)}) collective-permute-start(f32[16,144]{1,0:T(8,128)S(1)} %get-tuple-element.41), channel_id=1, source_target_pairs={{4,0},{5,1},{6,2},{7,3},{8,12},{9,13},{10,14},{11,15},{20,16},{21,... | collective-permute-start | bytes 27656 | tf_op jit(solution)/shard_map/ppermute | solution.py:96
  56.6 3.9 %collective-permute-start.11 = (f32[16,384]{1,0:T(8,128)S(1)}, f32[16,384]{1,0:T(8,128)S(1)}, u32[]{:S(2)}, u32[]{:S(2)}) collective-permute-start(f32[16,384]{1,0:T(8,128)S(1)} %shard_map.70), channel_id=1, source_target_pairs={{0,2},{1,3},{2,0},{3,1},{4,6},{5,7},{6,4},{7,5},{8,10},{9,11},{10,... | collective-permute-start | bytes 73736 | tf_op jit(solution)/shard_map/ppermute | solution.py:96
  60.5 1.2 %collective-permute-start.12 = (f32[16,384]{1,0:T(8,128)S(1)}, f32[16,384]{1,0:T(8,128)S(1)}, u32[]{:S(2)}, u32[]{:S(2)}) collective-permute-start(f32[16,384]{1,0:T(8,128)S(1)} %add.3.near), channel_id=1, source_target_pairs={{0,1},{1,0},{2,3},{3,2},{4,5},{5,4},{6,7},{7,6},{8,9},{9,8},{10,11... | collective-permute-start | bytes 73736 | tf_op jit(solution)/shard_map/ppermute | solution.py:96

commit v9 on v8

--- a/solution.py
+++ b/solution.py
@@ -76,7 +76,7 @@
 
 AXES = ("groups", "adapter", "mp")
 ID_ROWS = 16
-HOP_URGENCY = 12 * 10**9
+HOP_URGENCY = 4 * 10**9
 OWNERS = 4
 LANES = 128
 
@@ -239,14 +239,10 @@
     groups = lax.axis_size("groups")
     a = lax.axis_index("adapter")
     token_refs, rest = refs[:groups], refs[groups:]
-    blocks, (bases, folded, mask, numbers, base, ups) = rest[: len(bits)], rest[len(bits) :]
+    blocks, (folded, mask, numbers, ups) = rest[: len(bits)], rest[len(bits) :]
     columns = blocks[0].shape[1]
     for n, block in enumerate(blocks):
         ups[n] = stacked(block[part:, :], ups.shape[2])
-    total = bases[0]
-    for k in range(1, bases.shape[0]):
-        total = total + bases[k]
-    base[...] = total
     adapter = adapters(rows, columns)
     for n, tokens in enumerate(token_refs):
         owner, slot = id_columns(tokens, rows, rows)
@@ -316,6 +312,13 @@
         back = back - piece.astype(jnp.float32)
         spread = spread + jnp.dot(piece, places[...], preferred_element_type=jnp.float32)
     out[...] = low[...] + near[...] + spread
+
+
+def sum_body(parts, out):
+    total = parts[0]
+    for k in range(1, parts.shape[0]):
+        total = total + parts[k]
+    out[...] = total
 
 
 def finish_body(near, far, base, numbers, ups, last_up, distant, out):
@@ -398,10 +401,10 @@
         exchange(hop_away, 1, 0, INWARD),
     ]
 
-    folded, mask, numbers, base, ups = kernel(
+    folded, mask, numbers, ups = kernel(
         functools.partial(early_body, (0, 3, 1), part, rows),
-        [wide(groups, rows, LANES), wide(groups, rows, columns), wide(rows, 1), wide(rows, keys), narrow(3, columns, keys)],
-        (*token_parts, own, mirror, beside, bases),
+        [wide(groups, rows, LANES), wide(groups, rows, columns), wide(rows, 1), narrow(3, columns, keys)],
+        (*token_parts, own, mirror, beside),
         6 * groups * rows * part * columns,
     )
     distant = exchange(after(stacked_up_weight, folded), 0, 0, ENDS)
@@ -424,6 +427,7 @@
     back = exchange(back, 0, 0, OUTWARD)
     back_away = exchange(back_away, 1, 0, OUTWARD)
     low = kernel(merge_body, wide(ADAPTER_RANK, rows), (low, near, places, back, back_away))
+    base = kernel(sum_body, wide(rows, keys), (after(bases, low),))
     bit = shares // 2
     while bit > 1:
         low = low + exchange(low, 0, bit, SAME)

time: 63.5 us -> 64.4 us (1.014)
  waiting for transfers between devices: 17.8 us -> 11.4 us
  local copies, waits for them, and re-layouts: 5.14 us -> 10.2 us
  starting transfers between devices: 26.8 us -> 29.8 us
  Pallas kernels: 13 us -> 12 us
    unnamed x14 -> x34, local copies, waits for them, and re-layouts: 5.14 us -> 10.2 us
    all_to_all x1, waiting for transfers between devices: 4.89 us -> 0.01 us  [gather(): bases = lax.all_to_all(bases, 'mp', 0, 0, tiled=True)]
    ppermute x13, starting transfers between devices: 23.3 us -> 26.3 us  [exchange(): return lax.ppermute(x, AXES, pairs)]
    ppermute x13, waiting for transfers between devices: 12.9 us -> 11.4 us  [exchange(): return lax.ppermute(x, AXES, pairs)]
    pallas_call x8 -> x9, Pallas kernels: 13 us -> 12 us  [kernel(): pl.pallas_call(body, out_shape=outs, in_specs=specs or [inner] * len(oper...]
  transfers between devices with their start and end apart: 14 -> 14, of which waited for: 8 -> 5; matrix products, arithmetic and copies ran while one was open for 0% -> 0% of each run, Pallas kernels for 12% -> 15%
where the time goes in v9:
time: 64.4 us; the launch traced here: 63.6 us
  starting transfers between devices  29.8 us (46%)
  Pallas kernels  12 us (19%)
  waiting for transfers between devices  11.4 us (18%)
  local copies, waits for them, and re-layouts  10.2 us (16%)
    ppermute x13, starting transfers between devices, exchange(): return lax.ppermute(x, AXES, pairs)  26.3 us
    pallas_call x9, Pallas kernels, kernel(): pl.pallas_call(body, out_shape=outs, in_specs=specs or [inner] * len(oper...  12 us
    ppermute x13, waiting for transfers between devices, exchange(): return lax.ppermute(x, AXES, pairs)  11.4 us
    unnamed x34, local copies, waits for them, and re-layouts  10.2 us
    all_to_all x1, starting transfers between devices, gather(): bases = lax.all_to_all(bases, 'mp', 0, 0, tiled=True)  3.49 us
  transfers between devices with their start and end apart: 14, of which 5 were waited for; matrix products, arithmetic and copies ran while one was open for 0% of the time, Pallas kernels for 15%

profile of v9, /device:TPU:0, one launch (start us, length us, event | category | flops | bytes accessed | tf_op | source)
XLA Modules:
  0.0 63.6 jit_solution(11769989527546798753)
XLA Ops:
  0.0 1.3 %copy-done.1 = bf16[2048,256]{1,0:T(8,128)(2,1)S(1)} copy-done((bf16[2048,256]{1,0:T(8,128)(2,1)S(1)}, bf16[2048,256]{1,0:T(8,128)(2,1)}, u32[]{:S(2)}) %copy-start.1) | copy-done | bytes 1048600
  1.3 0.8 %copy-done.12 = bf16[256,128]{1,0:T(8,128)(2,1)S(1)} copy-done((bf16[256,128]{1,0:T(8,128)(2,1)S(1)}, bf16[256,128]{1,0:T(8,128)(2,1)}, u32[]{:S(2)}) %copy-start.12) | copy-done | bytes 65560
  2.2 0.1 shard_map.64.refs_2_
  2.3 0.0 copy-start.14
  2.3 0.7 %copy-done.14 = s32[384]{0:T(512)S(1)} copy-done((s32[384]{0:T(512)S(1)}, s32[384]{0:T(512)}, u32[]{:S(2)}) %copy-start.14) | copy-done | bytes 1560
  3.0 0.7 %copy-done.15 = s32[384,1]{0,1:T(1,128)S(1)} copy-done((s32[384,1]{0,1:T(1,128)S(1)}, s32[384,1]{0,1:T(1,128)}, u32[]{:S(2)}) %copy-start.15) | copy-done | bytes 1560
  3.7 1.0 %shard_map.65 = (bf16[400,1024]{1,0:T(8,128)(2,1)S(1)}, bf16[400,1024]{1,0:T(8,128)(2,1)}) custom-call(bf16[384,2048]{1,0:T(8,128)(2,1)S(1)} %copy-done, s32[1,384]{1,0:T(1,128)S(1)} %bitcast.1, s32[384]{0:T(512)S(1)} %copy-done.14), custom_call_target="tpu_custom_call" | custom-call | bytes 3214336 | tf_op jit(solution)/shard_map/pallas_call | solution.py:115
  4.7 3.0 %collective-permute-start = (bf16[400,1024]{1,0:T(8,128)(2,1)}, bf16[400,1024]{1,0:T(8,128)(2,1)S(1)}, u32[]{:S(2)}, u32[]{:S(2)}) collective-permute-start(bf16[400,1024]{1,0:T(8,128)(2,1)} %get-tuple-element.28.away), channel_id=1, source_target_pairs={{0,16},{1,17},{2,18},{3,19},{4,20},{5,21},{6,22},{7,23},{8,24},{9,... | collective-permute-start | bytes 2457608 | tf_op jit(solution)/shard_map/ppermute | solution.py:96
  7.8 1.6 %collective-permute-start.4 = (bf16[1152,256]{1,0:T(8,128)(2,1)S(1)}, bf16[1152,256]{1,0:T(8,128)(2,1)}, u32[]{:S(2)}, u32[]{:S(2)}) collective-permute-start(bf16[1152,256]{1,0:T(8,128)(2,1)S(1)} %shard_map.64.refs_2_), channel_id=1, source_target_pairs={{0,4},{1,5},{2,6},{3,7},{4,0},{5,1},{6,2},{7,3},{8,12},{9,13},{10,... | collective-permute-start | bytes 1769480 | tf_op jit(solution)/shard_map/ppermute | solution.py:96
  9.3 1.5 %collective-permute-start.3 = (bf16[1152,256]{1,0:T(8,128)(2,1)S(1)}, bf16[1152,256]{1,0:T(8,128)(2,1)}, u32[]{:S(2)}, u32[]{:S(2)}) collective-permute-start(bf16[1152,256]{1,0:T(8,128)(2,1)S(1)} %shard_map.64.refs_2_), channel_id=1, source_target_pairs={{4,8},{5,9},{6,10},{7,11},{8,4},{9,5},{10,6},{11,7},{20,24},{21,25... | collective-permute-start | bytes 1769480 | tf_op jit(solution)/shard_map/ppermute | solution.py:96
  10.8 1.6 %copy-done.16 = bf16[2048,512]{1,0:T(8,128)(2,1)S(1)} copy-done((bf16[2048,512]{1,0:T(8,128)(2,1)S(1)}, bf16[2048,512]{1,0:T(8,128)(2,1)}, u32[]{:S(2)}) %copy-start.16) | copy-done | bytes 2097176
  12.4 3.5 %shard_map.66 = (bf16[160,1024]{1,0:T(8,128)(2,1)}, bf16[160,1024]{1,0:T(8,128)(2,1)}, bf16[144,384]{1,0:T(8,128)(2,1)S(1)}, f32[4,384,128]{2,1,0:T(8,128)}) custom-call(bf16[400,1024]{1,0:T(8,128)(2,1)S(1)} %get-tuple-element.27.own.refs_0_, bf16[400,1024]{1,0:T(8,128)(2,1)} %get-tuple-element.28.away, bf16[2048,512]{1,0:T(8,128)(2,1)S(1)} %copy-done.16), custom_call_target="tpu_custom_call" | custom-call | flops 1031798784 | bytes 5287936 | tf_op jit(solution)/shard_map/pallas_call | solution.py:115
  16.0 0.7 %copy-done.6 = bf16[144,384]{1,0:T(8,128)(2,1)} copy-done((bf16[144,384]{1,0:T(8,128)(2,1)}, bf16[144,384]{1,0:T(8,128)(2,1)S(1)}, u32[]{:S(2)}) %copy-start.6) | copy-done | bytes 110616
  16.6 5.4 %collective-permute-start.2 = (bf16[160,1024]{1,0:T(8,128)(2,1)}, bf16[160,1024]{1,0:T(8,128)(2,1)S(1)}, u32[]{:S(2)}, u32[]{:S(2)}) collective-permute-start(bf16[160,1024]{1,0:T(8,128)(2,1)} %get-tuple-element.30), channel_id=1, source_target_pairs={{0,20},{1,21},{2,22},{3,23},{12,24},{13,25},{14,26},{15,27},{16,4}... | collective-permute-start | bytes 983048 | tf_op jit(solution)/shard_map/ppermute | solution.py:96
  22.1 2.1 %collective-permute-start.1 = (bf16[160,1024]{1,0:T(8,128)(2,1)}, bf16[160,1024]{1,0:T(8,128)(2,1)}, u32[]{:S(2)}, u32[]{:S(2)}) collective-permute-start(bf16[160,1024]{1,0:T(8,128)(2,1)} %get-tuple-element.29), channel_id=1, source_target_pairs={{0,4},{1,5},{2,6},{3,7},{12,8},{13,9},{14,10},{15,11},{16,20},{17,... | collective-permute-start | bytes 983048 | tf_op jit(solution)/shard_map/ppermute | solution.py:96
  24.2 0.0 collective-permute-done.4.refs_4_
  24.2 0.0 collective-permute-done.3.refs_3_
  24.2 1.3 %collective-permute-start.6 = (bf16[1152,256]{1,0:T(8,128)(2,1)}, bf16[1152,256]{1,0:T(8,128)(2,1)S(1)}, u32[]{:S(2)}, u32[]{:S(2)}) collective-permute-start(bf16[1152,256]{1,0:T(8,128)(2,1)} %collective-permute-done.3.refs_3_), channel_id=1, source_target_pairs={{4,0},{5,1},{6,2},{7,3},{8,12},{9,13},{10,14},{11,15},{20,16},{21,... | collective-permute-start | bytes 1769480 | tf_op jit(solution)/shard_map/ppermute | solution.py:96
  25.5 1.5 %collective-permute-start.7 = (bf16[1152,256]{1,0:T(8,128)(2,1)}, bf16[1152,256]{1,0:T(8,128)(2,1)}, u32[]{:S(2)}, u32[]{:S(2)}) collective-permute-start(bf16[1152,256]{1,0:T(8,128)(2,1)} %collective-permute-done.4.refs_4_), channel_id=1, source_target_pairs={{4,8},{5,9},{6,10},{7,11},{8,4},{9,5},{10,6},{11,7},{20,24},{21,25... | collective-permute-start | bytes 1769480 | tf_op jit(solution)/shard_map/ppermute | solution.py:96
  26.9 3.5 %all-to-all-start = ((f32[4,384,128]{2,1,0:T(8,128)}), f32[4,384,128]{2,1,0:T(8,128)S(1)}, u32[]{:S(2)}, u32[]{:S(2)}) async-start(f32[4,384,128]{2,1,0:T(8,128)} %get-tuple-element.42), calls=%async_computation | async-start | bytes 1572864 | tf_op jit(solution)/shard_map/all_to_all | solution.py:395
  30.4 0.0 collective-permute-done.refs_1_
  30.4 1.1 %copy-done.3 = bf16[1152,256]{1,0:T(8,128)(2,1)S(1)} copy-done((bf16[1152,256]{1,0:T(8,128)(2,1)S(1)}, bf16[1152,256]{1,0:T(8,128)(2,1)}, u32[]{:S(2)}) %copy-start.3) | copy-done | bytes 589848
  31.5 2.8 %shard_map.67 = (f32[2,384,128]{2,1,0:T(8,128)S(1)}, f32[2,384,256]{2,1,0:T(8,128)S(1)}, f32[384,1]{1,0:T(8,128)S(1)}, bf16[3,256,128]{2,1,0:T(8,128)(2,1)S(1)}) custom-call(bf16[400,1024]{1,0:T(8,128)(2,1)S(1)} %get-tuple-element.27.own.refs_0_, bf16[400,1024]{1,0:T(8,128)(2,1)S(1)} %collective-permute-done.refs_1_, bf16[1152,256]{1,0:T(8,128)(2,1)S(1)} %copy-done.3, ...), custom_call_target="tpu_custom_call" | custom-call | flops 1207959552 | bytes 4785664 | tf_op jit(solution)/shard_map/pallas_call | solution.py:115
  34.3 4.0 %collective-permute-start.5 = (bf16[256,128]{1,0:T(8,128)(2,1)S(1)}, bf16[256,128]{1,0:T(8,128)(2,1)S(1)}, u32[]{:S(2)}, u32[]{:S(2)}) collective-permute-start(bf16[256,128]{1,0:T(8,128)(2,1)S(1)} %copy-done.13), channel_id=1, source_target_pairs={{0,12},{1,13},{2,14},{3,15},{12,0},{13,1},{14,2},{15,3},{16,28},{1... | collective-permute-start | bytes 196616 | tf_op jit(solution)/shard_map/ppermute | solution.py:96
  38.3 0.0 collective-permute-done.2.refs_1_.refs_3_
  38.4 1.3 %shard_map.68.refs_4_ = f32[2,144,256]{2,1,0:T(8,128)S(1)} custom-call(bf16[160,1024]{1,0:T(8,128)(2,1)} %collective-permute-done.1.refs_0_.refs_2_, bf16[160,1024]{1,0:T(8,128)(2,1)S(1)} %collective-permute-done.2.refs_1_.refs_3_), custom_call_target="tpu_custom_call" | custom-call | flops 4000000000 | bytes 950272 | tf_op jit(solution)/shard_map/pallas_call | solution.py:115
  39.7 2.9 %collective-permute-done.5.distant = bf16[256,128]{1,0:T(8,128)(2,1)S(1)} collective-permute-done((bf16[256,128]{1,0:T(8,128)(2,1)S(1)}, bf16[256,128]{1,0:T(8,128)(2,1)S(1)}, u32[]{:S(2)}, u32[]{:S(2)}) %collective-permute-start.5) | collective-permute-done | bytes 65568 | tf_op jit(solution)/shard_map/ppermute | solution.py:96
  42.6 0.6 copy-done.8
  43.2 0.0 collective-permute-done.6.refs_7_
  43.2 0.0 collective-permute-done.7.refs_8_
  43.2 1.9 %shard_map.69 = (f32[16,384]{1,0:T(8,128)S(1)}, f32[16,384]{1,0:T(8,128)S(1)}, f32[16,144]{1,0:T(8,128)S(1)}, f32[16,144]{1,0:T(8,128)S(1)}, bf16[256,128]{1,0:T(8,128)(2,1)S(1)}) custom-call(bf16[400,1024]{1,0:T(8,128)(2,1)S(1)} %get-tuple-element.27.own.refs_0_, bf16[400,1024]{1,0:T(8,128)(2,1)S(1)} %collective-permute-done.refs_1_, ...), custom_call_target="tpu_custom_call" | custom-call | flops 553648128 | bytes 5081088 | tf_op jit(solution)/shard_map/pallas_call | solution.py:115
  45.1 0.0 copy-start.10
  45.1 1.5 %collective-permute-start.8 = (f32[16,384]{1,0:T(8,128)S(1)}, f32[16,384]{1,0:T(8,128)S(1)}, u32[]{:S(2)}, u32[]{:S(2)}) collective-permute-start(f32[16,384]{1,0:T(8,128)S(1)} %get-tuple-element.39), channel_id=1, source_target_pairs={{0,16},{1,17},{2,18},{3,19},{4,20},{5,21},{6,22},{7,23},{8,24},{9,... | collective-permute-start | bytes 73736 | tf_op jit(solution)/shard_map/ppermute | solution.py:96
  46.6 1.3 %collective-permute-start.9 = (f32[16,144]{1,0:T(8,128)S(1)}, f32[16,144]{1,0:T(8,128)S(1)}, u32[]{:S(2)}, u32[]{:S(2)}) collective-permute-start(f32[16,144]{1,0:T(8,128)S(1)} %get-tuple-element.40), channel_id=1, source_target_pairs={{4,0},{5,1},{6,2},{7,3},{8,12},{9,13},{10,14},{11,15},{20,16},{21,... | collective-permute-start | bytes 27656 | tf_op jit(solution)/shard_map/ppermute | solution.py:96
  47.9 1.3 %collective-permute-start.10 = (f32[16,144]{1,0:T(8,128)S(1)}, f32[16,144]{1,0:T(8,128)S(1)}, u32[]{:S(2)}, u32[]{:S(2)}) collective-permute-start(f32[16,144]{1,0:T(8,128)S(1)} %get-tuple-element.41), channel_id=1, source_target_pairs={{4,16},{5,17},{6,18},{7,19},{8,28},{9,29},{10,30},{11,31},{20,0},{... | collective-permute-start | bytes 27656 | tf_op jit(solution)/shard_map/ppermute | solution.py:96
  49.2 3.0 %collective-permute-done.9.refs_0_ = f32[16,144]{1,0:T(8,128)S(1)} collective-permute-done((f32[16,144]{1,0:T(8,128)S(1)}, f32[16,144]{1,0:T(8,128)S(1)}, u32[]{:S(2)}, u32[]{:S(2)}) %collective-permute-start.9) | collective-permute-done | bytes 9248 | tf_op jit(solution)/shard_map/ppermute | solution.py:96
  52.3 2.2 %collective-permute-done.10.refs_1_ = f32[16,144]{1,0:T(8,128)S(1)} collective-permute-done((f32[16,144]{1,0:T(8,128)S(1)}, f32[16,144]{1,0:T(8,128)S(1)}, u32[]{:S(2)}, u32[]{:S(2)}) %collective-permute-start.10) | collective-permute-done | bytes 9248 | tf_op jit(solution)/shard_map/ppermute | solution.py:96
  54.5 0.0 collective-permute-done.8.near
  54.5 0.2 shard_map.70
  54.6 1.8 %collective-permute-start.11 = (f32[16,384]{1,0:T(8,128)S(1)}, f32[16,384]{1,0:T(8,128)S(1)}, u32[]{:S(2)}, u32[]{:S(2)}) collective-permute-start(f32[16,384]{1,0:T(8,128)S(1)} %shard_map.70), channel_id=1, source_target_pairs={{0,2},{1,3},{2,0},{3,1},{4,6},{5,7},{6,4},{7,5},{8,10},{9,11},{10,... | collective-permute-start | bytes 73736 | tf_op jit(solution)/shard_map/ppermute | solution.py:96
  56.4 2.1 %collective-permute-done.11 = f32[16,384]{1,0:T(8,128)S(1)} collective-permute-done((f32[16,384]{1,0:T(8,128)S(1)}, f32[16,384]{1,0:T(8,128)S(1)}, u32[]{:S(2)}, u32[]{:S(2)}) %collective-permute-start.11) | collective-permute-done | bytes 24608 | tf_op jit(solution)/shard_map/ppermute | solution.py:96
  58.5 0.1 collective-permute-start.12
  58.6 0.0 all-to-all-done.parts
  58.6 1.1 %collective-permute-done.12.far = f32[16,384]{1,0:T(8,128)S(1)} collective-permute-done((f32[16,384]{1,0:T(8,128)S(1)}, f32[16,384]{1,0:T(8,128)S(1)}, u32[]{:S(2)}, u32[]{:S(2)}) %collective-permute-start.12) | collective-permute-done | bytes 24608 | tf_op jit(solution)/shard_map/ppermute | solution.py:96
  59.7 0.9 %copy-done.5 = bf16[3,256,128]{2,1,0:T(8,128)(2,1)S(1)} copy-done((bf16[3,256,128]{2,1,0:T(8,128)(2,1)S(1)}, bf16[3,256,128]{2,1,0:T(8,128)(2,1)}, u32[]{:S(2)}) %copy-start.5) | copy-done | bytes 196632
  60.7 0.8 %copy-done.9 = bf16[256,128]{1,0:T(8,128)(2,1)S(1)} copy-done((bf16[256,128]{1,0:T(8,128)(2,1)S(1)}, bf16[256,128]{1,0:T(8,128)(2,1)}, u32[]{:S(2)}) %copy-start.9) | copy-done | bytes 65560
  61.5 0.8 %copy-done.11 = bf16[256,128]{1,0:T(8,128)(2,1)S(1)} copy-done((bf16[256,128]{1,0:T(8,128)(2,1)S(1)}, bf16[256,128]{1,0:T(8,128)(2,1)}, u32[]{:S(2)}) %copy-start.11) | copy-done | bytes 65560
  62.4 1.3 %shard_map.72 = bf16[384,128]{1,0:T(8,128)(2,1)} custom-call(f32[16,384]{1,0:T(8,128)S(1)} %add.3.near, f32[16,384]{1,0:T(8,128)S(1)} %collective-permute-done.12.far, f32[384,128]{1,0:T(8,128)S(1)} %shard_map.71.base, f32[384,1]{1,0:T(8,128)S(1)} %get-tuple-element.44.numbers, bf16[3,256,128]{2,1,0:T(8,128)(2,1)S(1)} %copy-done.5, ...), custom_call_target="tpu_custom_call" | custom-call | bytes 673280 | tf_op jit(solution)/shard_map/pallas_call | solution.py:115
  (24 shorter events, 0.1 us)
Async XLA Ops:
  0.0 2.3 %copy-start = (bf16[384,2048]{1,0:T(8,128)(2,1)S(1)}, bf16[384,2048]{1,0:T(8,128)(2,1)}, u32[]{:S(2)}) copy-start(bf16[384,2048]{1,0:T(8,128)(2,1)} %tokens.1) | copy-start | bytes 4718596
  0.0 1.3 %copy-start.1 = (bf16[2048,256]{1,0:T(8,128)(2,1)S(1)}, bf16[2048,256]{1,0:T(8,128)(2,1)}, u32[]{:S(2)}) copy-start(bf16[2048,256]{1,0:T(8,128)(2,1)} %down.1) | copy-start | bytes 3145732
  1.3 0.8 %copy-start.12 = (bf16[256,128]{1,0:T(8,128)(2,1)S(1)}, bf16[256,128]{1,0:T(8,128)(2,1)}, u32[]{:S(2)}) copy-start(bf16[256,128]{1,0:T(8,128)(2,1)} %up.1) | copy-start | bytes 196612
  2.3 13.7 %copy-start.2 = (bf16[1152,256]{1,0:T(8,128)(2,1)}, bf16[1152,256]{1,0:T(8,128)(2,1)S(1)}, u32[]{:S(2)}) copy-start(bf16[1152,256]{1,0:T(8,128)(2,1)S(1)} %shard_map.64.refs_2_) | copy-start | bytes 1769476
  2.3 0.7 %copy-start.14 = (s32[384]{0:T(512)S(1)}, s32[384]{0:T(512)}, u32[]{:S(2)}) copy-start(s32[384]{0:T(512)} %slot) | copy-start | bytes 4612
  3.0 0.7 %copy-start.15 = (s32[384,1]{0,1:T(1,128)S(1)}, s32[384,1]{0,1:T(1,128)}, u32[]{:S(2)}) copy-start(s32[384,1]{0,1:T(1,128)} %param.10) | copy-start | bytes 4612
  4.7 25.7 %collective-permute-start = (bf16[400,1024]{1,0:T(8,128)(2,1)}, bf16[400,1024]{1,0:T(8,128)(2,1)S(1)}, u32[]{:S(2)}, u32[]{:S(2)}) collective-permute-start(bf16[400,1024]{1,0:T(8,128)(2,1)} %get-tuple-element.28.away), channel_id=1, source_target_pairs={{0,16},{1,17},{2,18},{3,19},{4,20},{5,21},{6,22},{7,23},{8,24},{9,... | collective-permute-start | bytes 2457608 | tf_op jit(solution)/shard_map/ppermute | solution.py:96
  7.8 16.4 %collective-permute-start.4 = (bf16[1152,256]{1,0:T(8,128)(2,1)S(1)}, bf16[1152,256]{1,0:T(8,128)(2,1)}, u32[]{:S(2)}, u32[]{:S(2)}) collective-permute-start(bf16[1152,256]{1,0:T(8,128)(2,1)S(1)} %shard_map.64.refs_2_), channel_id=1, source_target_pairs={{0,4},{1,5},{2,6},{3,7},{4,0},{5,1},{6,2},{7,3},{8,12},{9,13},{10,... | collective-permute-start | bytes 1769480 | tf_op jit(solution)/shard_map/ppermute | solution.py:96
  9.3 14.8 %collective-permute-start.3 = (bf16[1152,256]{1,0:T(8,128)(2,1)S(1)}, bf16[1152,256]{1,0:T(8,128)(2,1)}, u32[]{:S(2)}, u32[]{:S(2)}) collective-permute-start(bf16[1152,256]{1,0:T(8,128)(2,1)S(1)} %shard_map.64.refs_2_), channel_id=1, source_target_pairs={{4,8},{5,9},{6,10},{7,11},{8,4},{9,5},{10,6},{11,7},{20,24},{21,25... | collective-permute-start | bytes 1769480 | tf_op jit(solution)/shard_map/ppermute | solution.py:96
  10.8 1.6 %copy-start.16 = (bf16[2048,512]{1,0:T(8,128)(2,1)S(1)}, bf16[2048,512]{1,0:T(8,128)(2,1)}, u32[]{:S(2)}) copy-start(bf16[2048,512]{1,0:T(8,128)(2,1)} %weights.1) | copy-start | bytes 6291460
  16.0 0.7 %copy-start.6 = (bf16[144,384]{1,0:T(8,128)(2,1)}, bf16[144,384]{1,0:T(8,128)(2,1)S(1)}, u32[]{:S(2)}) copy-start(bf16[144,384]{1,0:T(8,128)(2,1)S(1)} %get-tuple-element.36.places) | copy-start | bytes 331780
  16.6 21.7 %collective-permute-start.2 = (bf16[160,1024]{1,0:T(8,128)(2,1)}, bf16[160,1024]{1,0:T(8,128)(2,1)S(1)}, u32[]{:S(2)}, u32[]{:S(2)}) collective-permute-start(bf16[160,1024]{1,0:T(8,128)(2,1)} %get-tuple-element.30), channel_id=1, source_target_pairs={{0,20},{1,21},{2,22},{3,23},{12,24},{13,25},{14,26},{15,27},{16,4}... | collective-permute-start | bytes 983048 | tf_op jit(solution)/shard_map/ppermute | solution.py:96
  22.1 16.3 %collective-permute-start.1 = (bf16[160,1024]{1,0:T(8,128)(2,1)}, bf16[160,1024]{1,0:T(8,128)(2,1)}, u32[]{:S(2)}, u32[]{:S(2)}) collective-permute-start(bf16[160,1024]{1,0:T(8,128)(2,1)} %get-tuple-element.29), channel_id=1, source_target_pairs={{0,4},{1,5},{2,6},{3,7},{12,8},{13,9},{14,10},{15,11},{16,20},{17,... | collective-permute-start | bytes 983048 | tf_op jit(solution)/shard_map/ppermute | solution.py:96
  24.2 19.0 %collective-permute-start.6 = (bf16[1152,256]{1,0:T(8,128)(2,1)}, bf16[1152,256]{1,0:T(8,128)(2,1)S(1)}, u32[]{:S(2)}, u32[]{:S(2)}) collective-permute-start(bf16[1152,256]{1,0:T(8,128)(2,1)} %collective-permute-done.3.refs_3_), channel_id=1, source_target_pairs={{4,0},{5,1},{6,2},{7,3},{8,12},{9,13},{10,14},{11,15},{20,16},{21,... | collective-permute-start | bytes 1769480 | tf_op jit(solution)/shard_map/ppermute | solution.py:96
  25.5 17.7 %collective-permute-start.7 = (bf16[1152,256]{1,0:T(8,128)(2,1)}, bf16[1152,256]{1,0:T(8,128)(2,1)}, u32[]{:S(2)}, u32[]{:S(2)}) collective-permute-start(bf16[1152,256]{1,0:T(8,128)(2,1)} %collective-permute-done.4.refs_4_), channel_id=1, source_target_pairs={{4,8},{5,9},{6,10},{7,11},{8,4},{9,5},{10,6},{11,7},{20,24},{21,25... | collective-permute-start | bytes 1769480 | tf_op jit(solution)/shard_map/ppermute | solution.py:96
  26.9 31.6 %all-to-all-start = ((f32[4,384,128]{2,1,0:T(8,128)}), f32[4,384,128]{2,1,0:T(8,128)S(1)}, u32[]{:S(2)}, u32[]{:S(2)}) async-start(f32[4,384,128]{2,1,0:T(8,128)} %get-tuple-element.42), calls=%async_computation | async-start | bytes 1572864 | tf_op jit(solution)/shard_map/all_to_all | solution.py:395
  30.4 1.1 %copy-start.3 = (bf16[1152,256]{1,0:T(8,128)(2,1)S(1)}, bf16[1152,256]{1,0:T(8,128)(2,1)}, u32[]{:S(2)}) copy-start(bf16[1152,256]{1,0:T(8,128)(2,1)} %copy-done.2) | copy-start | bytes 1769476
  31.5 2.8 %copy-start.13 = (bf16[256,128]{1,0:T(8,128)(2,1)S(1)}, bf16[256,128]{1,0:T(8,128)(2,1)}, u32[]{:S(2)}) copy-start(bf16[256,128]{1,0:T(8,128)(2,1)} %up.1) | copy-start | bytes 196612
  34.3 5.4 %copy-start.4 = (bf16[3,256,128]{2,1,0:T(8,128)(2,1)}, bf16[3,256,128]{2,1,0:T(8,128)(2,1)S(1)}, u32[]{:S(2)}) copy-start(bf16[3,256,128]{2,1,0:T(8,128)(2,1)S(1)} %get-tuple-element.45.ups) | copy-start | bytes 589828
  34.3 8.3 %collective-permute-start.5 = (bf16[256,128]{1,0:T(8,128)(2,1)S(1)}, bf16[256,128]{1,0:T(8,128)(2,1)S(1)}, u32[]{:S(2)}, u32[]{:S(2)}) collective-permute-start(bf16[256,128]{1,0:T(8,128)(2,1)S(1)} %copy-done.13), channel_id=1, source_target_pairs={{0,12},{1,13},{2,14},{3,15},{12,0},{13,1},{14,2},{15,3},{16,28},{1... | collective-permute-start | bytes 196616 | tf_op jit(solution)/shard_map/ppermute | solution.py:96
  42.6 0.6 copy-start.8
  43.2 11.3 %copy-start.7 = (bf16[144,384]{1,0:T(8,128)(2,1)S(1)}, bf16[144,384]{1,0:T(8,128)(2,1)}, u32[]{:S(2)}) copy-start(bf16[144,384]{1,0:T(8,128)(2,1)} %copy-done.6) | copy-start | bytes 331780
  45.1 13.4 %copy-start.10 = (bf16[256,128]{1,0:T(8,128)(2,1)}, bf16[256,128]{1,0:T(8,128)(2,1)S(1)}, u32[]{:S(2)}) copy-start(bf16[256,128]{1,0:T(8,128)(2,1)S(1)} %get-tuple-element.46.last_up) | copy-start | bytes 196612
  45.1 9.4 %collective-permute-start.8 = (f32[16,384]{1,0:T(8,128)S(1)}, f32[16,384]{1,0:T(8,128)S(1)}, u32[]{:S(2)}, u32[]{:S(2)}) collective-permute-start(f32[16,384]{1,0:T(8,128)S(1)} %get-tuple-element.39), channel_id=1, source_target_pairs={{0,16},{1,17},{2,18},{3,19},{4,20},{5,21},{6,22},{7,23},{8,24},{9,... | collective-permute-start | bytes 73736 | tf_op jit(solution)/shard_map/ppermute | solution.py:96
  46.6 5.6 %collective-permute-start.9 = (f32[16,144]{1,0:T(8,128)S(1)}, f32[16,144]{1,0:T(8,128)S(1)}, u32[]{:S(2)}, u32[]{:S(2)}) collective-permute-start(f32[16,144]{1,0:T(8,128)S(1)} %get-tuple-element.40), channel_id=1, source_target_pairs={{4,0},{5,1},{6,2},{7,3},{8,12},{9,13},{10,14},{11,15},{20,16},{21,... | collective-permute-start | bytes 27656 | tf_op jit(solution)/shard_map/ppermute | solution.py:96
  47.9 6.5 %collective-permute-start.10 = (f32[16,144]{1,0:T(8,128)S(1)}, f32[16,144]{1,0:T(8,128)S(1)}, u32[]{:S(2)}, u32[]{:S(2)}) collective-permute-start(f32[16,144]{1,0:T(8,128)S(1)} %get-tuple-element.41), channel_id=1, source_target_pairs={{4,16},{5,17},{6,18},{7,19},{8,28},{9,29},{10,30},{11,31},{20,0},{... | collective-permute-start | bytes 27656 | tf_op jit(solution)/shard_map/ppermute | solution.py:96
  54.6 3.9 %collective-permute-start.11 = (f32[16,384]{1,0:T(8,128)S(1)}, f32[16,384]{1,0:T(8,128)S(1)}, u32[]{:S(2)}, u32[]{:S(2)}) collective-permute-start(f32[16,384]{1,0:T(8,128)S(1)} %shard_map.70), channel_id=1, source_target_pairs={{0,2},{1,3},{2,0},{3,1},{4,6},{5,7},{6,4},{7,5},{8,10},{9,11},{10,... | collective-permute-start | bytes 73736 | tf_op jit(solution)/shard_map/ppermute | solution.py:96
  58.5 1.3 %collective-permute-start.12 = (f32[16,384]{1,0:T(8,128)S(1)}, f32[16,384]{1,0:T(8,128)S(1)}, u32[]{:S(2)}, u32[]{:S(2)}) collective-permute-start(f32[16,384]{1,0:T(8,128)S(1)} %add.3.near), channel_id=1, source_target_pairs={{0,1},{1,0},{2,3},{3,2},{4,5},{5,4},{6,7},{7,6},{8,9},{9,8},{10,11... | collective-permute-start | bytes 73736 | tf_op jit(solution)/shard_map/ppermute | solution.py:96
  59.7 0.9 %copy-start.5 = (bf16[3,256,128]{2,1,0:T(8,128)(2,1)S(1)}, bf16[3,256,128]{2,1,0:T(8,128)(2,1)}, u32[]{:S(2)}) copy-start(bf16[3,256,128]{2,1,0:T(8,128)(2,1)} %copy-done.4) | copy-start | bytes 589828
  60.7 0.8 %copy-start.9 = (bf16[256,128]{1,0:T(8,128)(2,1)S(1)}, bf16[256,128]{1,0:T(8,128)(2,1)}, u32[]{:S(2)}) copy-start(bf16[256,128]{1,0:T(8,128)(2,1)} %copy-done.8) | copy-start | bytes 196612
  61.5 0.8 %copy-start.11 = (bf16[256,128]{1,0:T(8,128)(2,1)S(1)}, bf16[256,128]{1,0:T(8,128)(2,1)}, u32[]{:S(2)}) copy-start(bf16[256,128]{1,0:T(8,128)(2,1)} %copy-done.10) | copy-start | bytes 196612

commit v10 on v9

--- a/solution.py
+++ b/solution.py
@@ -76,9 +76,10 @@
 
 AXES = ("groups", "adapter", "mp")
 ID_ROWS = 16
-HOP_URGENCY = 4 * 10**9
 OWNERS = 4
 LANES = 128
+NT = (((1,), (1,)), ((), ()))
+TN = (((0,), (0,)), ((), ()))
 
 
 def exchange(x, group_bits, share_bits, owners):
@@ -108,7 +109,7 @@
     return lax.optimization_barrier((x, *others))[0]
 
 
-def kernel(body, outs, operands, flops=0, spaces=None, scratch=()):
+def kernel(body, outs, operands, flops=0, spaces=None, scratch=(), light=False):
     inner = pl.BlockSpec(memory_space=pltpu.VMEM)
     specs = [inner if s is None else pl.BlockSpec(memory_space=s) for s in spaces or ()]
     touched = sum(x.size * x.dtype.itemsize for x in jax.tree.leaves((operands, outs)))
@@ -119,7 +120,9 @@
         out_specs=jax.tree.map(lambda _: inner, outs),
         scratch_shapes=scratch,
         compiler_params=pltpu.CompilerParams(vmem_limit_bytes=16 * 1024 * 1024),
-        cost_estimate=pl.CostEstimate(flops=flops, bytes_accessed=touched, transcendentals=0),
+        cost_estimate=pl.CostEstimate(
+            flops=flops, bytes_accessed=0 if light else touched, transcendentals=0
+        ),
     )(*operands)
 
 
@@ -168,7 +171,7 @@
         copy.wait()
 
 
-def hop_body(rows, capacity, own, away, weights, own_out, away_out, places, bases):
+def hop_body(rows, capacity, own, away, weights, own_out, away_out, places, keep, give, base):
     a, g = lax.axis_index("adapter"), lax.axis_index("groups")
     part = own.shape[1]
     ids = own[rows:, :rows]
@@ -187,17 +190,20 @@
         out[:capacity, :] = packed.astype(jnp.bfloat16)
         out[capacity:, :] = jnp.zeros((ID_ROWS, part), jnp.bfloat16)
         out[capacity:, :capacity] = kept.astype(jnp.bfloat16)
-    base = jnp.zeros((rows, weights.shape[1]), jnp.float32)
+    total = jnp.zeros(base.shape, jnp.float32)
     for tokens, half in ((own, g), (away, 1 - g)):
         part_weights = weights[pl.ds(pl.multiple_of(half * part, part), part), :]
-        base = base + jnp.dot(tokens[:rows, :], part_weights, preferred_element_type=jnp.float32)
-    keys = bases.shape[2]
-    for k in range(bases.shape[0]):
-        bases[k] = base[:, k * keys : (k + 1) * keys]
-
-
-NT = (((1,), (1,)), ((), ()))
-TN = (((0,), (0,)), ((), ()))
+        total = total + jnp.dot(tokens[:rows, :], part_weights, preferred_element_type=jnp.float32)
+    base[...] = total
+    halves(base, lax.axis_size("mp") // 2, keep, give)
+
+
+def halves(base, bit, keep, give):
+    m = lax.axis_index("mp")
+    width = keep.shape[1]
+    side = (m // bit) % 2
+    keep[...] = base[:, pl.ds(pl.multiple_of(side * width, width), width)]
+    give[...] = base[:, pl.ds(pl.multiple_of((1 - side) * width, width), width)]
 
 
 def id_columns(rows_ref, start, count):
@@ -301,8 +307,8 @@
             out[...] = jnp.zeros(out.shape, jnp.float32)
 
 
-def merge_body(low, near, places, *refs):
-    hops, out = refs[:-1], refs[-1]
+def merge_body(bit, low, near, places, kept, got, *refs):
+    hops, (out, keep, give, base) = refs[:-4], refs[-4:]
     back = hops[0][...]
     for hop in hops[1:]:
         back = back + hop[...]
@@ -312,16 +318,11 @@
         back = back - piece.astype(jnp.float32)
         spread = spread + jnp.dot(piece, places[...], preferred_element_type=jnp.float32)
     out[...] = low[...] + near[...] + spread
-
-
-def sum_body(parts, out):
-    total = parts[0]
-    for k in range(1, parts.shape[0]):
-        total = total + parts[k]
-    out[...] = total
-
-
-def finish_body(near, far, base, numbers, ups, last_up, distant, out):
+    base[...] = kept[...] + got[...]
+    halves(base, bit, keep, give)
+
+
+def finish_body(near, far, keep, got, numbers, ups, last_up, distant, out):
     a = lax.axis_index("adapter")
     rows = out.shape[0]
     columns = last_up.shape[0]
@@ -340,7 +341,8 @@
         chosen = jnp.where(adapter == wanted, spread, 0.0).astype(jnp.bfloat16)
         updates = updates + jnp.dot(chosen, up, preferred_element_type=jnp.float32)
     updates = updates.astype(jnp.bfloat16).astype(jnp.float32)
-    out[...] = (base[...] + ADAPTER_SCALE * updates).astype(jnp.bfloat16)
+    base = keep[...] + got[...]
+    out[...] = (base + ADAPTER_SCALE * updates).astype(jnp.bfloat16)
 
 
 def gather(
@@ -385,14 +387,15 @@
         [pltpu.SemaphoreType.DMA((groups,))],
     )
     token_parts = [tok_own, exchange(tok_away, 1, 0, SAME)]
-    hop_own, hop_away, places, bases = kernel(
+    hop_own, hop_away, places, keep, give = kernel(
         functools.partial(hop_body, rows, capacity),
         [narrow(capacity + ID_ROWS, part)] * groups
-        + [narrow(capacity, rows), wide(shares, rows, keys)],
+        + [narrow(capacity, rows)]
+        + [wide(rows, shares * keys // 2)] * 2,
         (tok_own, tok_away, base_key_weight),
         2 * rows * features * (capacity + shares * keys),
-    )
-    bases = lax.all_to_all(bases, "mp", 0, 0, tiled=True)
+        scratch=[pltpu.VMEM((rows, shares * keys), jnp.float32)],
+    )
 
     inside = exchange(after(beside, places), 0, 0, MIDDLE)
     outside = exchange(mirror, 0, 0, OUTWARD)
@@ -405,15 +408,17 @@
         functools.partial(early_body, (0, 3, 1), part, rows),
         [wide(groups, rows, LANES), wide(groups, rows, columns), wide(rows, 1), narrow(3, columns, keys)],
         (*token_parts, own, mirror, beside),
-        6 * groups * rows * part * columns,
+        light=True,
     )
     distant = exchange(after(stacked_up_weight, folded), 0, 0, ENDS)
     hop_mask = kernel(
         functools.partial(hop_mask_body, capacity),
         wide(groups, capacity, columns),
         (hops[0], after(hops[1], folded)),
-        HOP_URGENCY,
-    )
+    )
+    bits = (2, 1)
+    got = exchange(after(give, hop_mask), 0, bits[0], SAME)
+
     low, low_away, back, back_away, last_up = kernel(
         functools.partial(last_body, part, rows, capacity),
         [wide(ADAPTER_RANK, rows)] * groups
@@ -426,15 +431,17 @@
     near = exchange(low_away, 1, 0, SAME)
     back = exchange(back, 0, 0, OUTWARD)
     back_away = exchange(back_away, 1, 0, OUTWARD)
-    low = kernel(merge_body, wide(ADAPTER_RANK, rows), (low, near, places, back, back_away))
-    base = kernel(sum_body, wide(rows, keys), (after(bases, low),))
-    bit = shares // 2
-    while bit > 1:
-        low = low + exchange(low, 0, bit, SAME)
-        bit //= 2
-    low_far = exchange(low, 0, 1, SAME)
+    low, keep, give = kernel(
+        functools.partial(merge_body, bits[1]),
+        [wide(ADAPTER_RANK, rows)] + [wide(rows, bits[1] * keys)] * 2,
+        (low, near, places, keep, got, back, back_away),
+        scratch=[pltpu.VMEM((rows, bits[0] * keys), jnp.float32)],
+    )
+    got = exchange(give, 0, bits[1], SAME)
+    low = low + exchange(low, 0, bits[0], SAME)
+    low_far = exchange(low, 0, bits[1], SAME)
     return kernel(
-        finish_body, narrow(rows, keys), (low, low_far, base, numbers, ups, last_up, distant)
+        finish_body, narrow(rows, keys), (low, low_far, keep, got, numbers, ups, last_up, distant)
     )
 
 
@@ -445,7 +452,7 @@
 def local(*args):
     rows, columns = args[0].shape[0], args[2].shape[1]
     groups, owners, shares = (lax.axis_size(name) for name in AXES)
-    fits = owners == OWNERS and groups == 2 and shares > 1 and shares & (shares - 1) == 0
+    fits = owners == OWNERS and groups == 2 and shares == 4
     travels = fits and columns <= groups * row_limit(rows)
     return (gather if travels else dispatch)(*args)
 

time: 64.4 us -> 58.9 us (0.915)
  waiting for transfers between devices: 11.4 us -> 21.6 us
  Pallas kernels: 12 us -> 5.81 us
  local copies, waits for them, and re-layouts: 10.2 us -> 5.13 us
  starting transfers between devices: 29.8 us -> 25.8 us
    ppermute x13 -> x15, waiting for transfers between devices: 11.4 us -> 21.6 us  [exchange(): return lax.ppermute(x, AXES, pairs)]
    pallas_call x9 -> x8, Pallas kernels: 12 us -> 5.81 us  [kernel(): pl.pallas_call(body, out_shape=outs, in_specs=specs or [inner] * len(oper...]
    unnamed x34 -> x12, local copies, waits for them, and re-layouts: 10.2 us -> 5.13 us
    all_to_all x1 -> x0, starting transfers between devices: 3.49 us -> none  [gather(): bases = lax.all_to_all(bases, 'mp', 0, 0, tiled=True)]
    ppermute x13 -> x15, starting transfers between devices: 26.3 us -> 25.8 us  [exchange(): return lax.ppermute(x, AXES, pairs)]
  transfers between devices with their start and end apart: 14 -> 15, of which waited for: 5 -> 7; matrix products, arithmetic and copies ran while one was open for 0% -> 0% of each run, Pallas kernels for 15% -> 7%
where the time goes in v10:
time: 58.9 us; the launch traced here: 58.6 us
  starting transfers between devices  25.8 us (44%)
  waiting for transfers between devices  21.6 us (37%)
  Pallas kernels  5.81 us (10%)
  local copies, waits for them, and re-layouts  5.13 us (9%)
    ppermute x15, starting transfers between devices, exchange(): return lax.ppermute(x, AXES, pairs)  25.8 us
    ppermute x15, waiting for transfers between devices, exchange(): return lax.ppermute(x, AXES, pairs)  21.6 us
    pallas_call x8, Pallas kernels, kernel(): pl.pallas_call(body, out_shape=outs, in_specs=specs or [inner] * len(oper...  5.81 us
    unnamed x12, local copies, waits for them, and re-layouts  5.13 us
  transfers between devices with their start and end apart: 15, of which 7 were waited for; matrix products, arithmetic and copies ran while one was open for 0% of the time, Pallas kernels for 7%

profile of v10, /device:TPU:0, one launch (start us, length us, event | category | flops | bytes accessed | tf_op | source)
XLA Modules:
  0.0 58.6 jit_solution(2070975316465006943)
XLA Ops:
  0.0 0.0 copy-start
  0.0 0.0 copy-start.1
  0.0 1.3 %copy-done.1 = bf16[2048,256]{1,0:T(8,128)(2,1)S(1)} copy-done((bf16[2048,256]{1,0:T(8,128)(2,1)S(1)}, bf16[2048,256]{1,0:T(8,128)(2,1)}, u32[]{:S(2)}) %copy-start.1) | copy-done | bytes 1048600
  1.3 0.0 copy-start.2
  1.3 0.8 %copy-done.2 = bf16[256,128]{1,0:T(8,128)(2,1)S(1)} copy-done((bf16[256,128]{1,0:T(8,128)(2,1)S(1)}, bf16[256,128]{1,0:T(8,128)(2,1)}, u32[]{:S(2)}) %copy-start.2) | copy-done | bytes 65560
  2.2 0.1 shard_map.64.refs_2_
  2.3 3.1 %collective-permute-start.4 = (bf16[1152,256]{1,0:T(8,128)(2,1)S(1)}, bf16[1152,256]{1,0:T(8,128)(2,1)S(1)}, u32[]{:S(2)}, u32[]{:S(2)}) collective-permute-start(bf16[1152,256]{1,0:T(8,128)(2,1)S(1)} %shard_map.64.refs_2_), channel_id=1, source_target_pairs={{0,4},{1,5},{2,6},{3,7},{4,0},{5,1},{6,2},{7,3},{8,12},{9,13},{10,... | collective-permute-start | bytes 1769480 | tf_op jit(solution)/shard_map/ppermute | solution.py:97
  5.4 0.7 %collective-permute-start.3 = (bf16[1152,256]{1,0:T(8,128)(2,1)S(1)}, bf16[1152,256]{1,0:T(8,128)(2,1)S(1)}, u32[]{:S(2)}, u32[]{:S(2)}) collective-permute-start(bf16[1152,256]{1,0:T(8,128)(2,1)S(1)} %shard_map.64.refs_2_), channel_id=1, source_target_pairs={{4,8},{5,9},{6,10},{7,11},{8,4},{9,5},{10,6},{11,7},{20,24},{21,25... | collective-permute-start | bytes 1769480 | tf_op jit(solution)/shard_map/ppermute | solution.py:97
  6.1 0.0 copy-done
  6.1 0.0 copy-start.3
  6.1 0.7 %copy-done.3 = s32[384]{0:T(512)S(1)} copy-done((s32[384]{0:T(512)S(1)}, s32[384]{0:T(512)}, u32[]{:S(2)}) %copy-start.3) | copy-done | bytes 1560
  6.8 0.7 %copy-done.4 = s32[384,1]{0,1:T(1,128)S(1)} copy-done((s32[384,1]{0,1:T(1,128)S(1)}, s32[384,1]{0,1:T(1,128)}, u32[]{:S(2)}) %copy-start.4) | copy-done | bytes 1560
  7.4 0.2 shard_map.65
  7.6 1.6 %collective-permute-start = (bf16[400,1024]{1,0:T(8,128)(2,1)S(1)}, bf16[400,1024]{1,0:T(8,128)(2,1)S(1)}, u32[]{:S(2)}, u32[]{:S(2)}) collective-permute-start(bf16[400,1024]{1,0:T(8,128)(2,1)S(1)} %get-tuple-element.32.away), channel_id=1, source_target_pairs={{0,16},{1,17},{2,18},{3,19},{4,20},{5,21},{6,22},{7,23},{8,24},{9,... | collective-permute-start | bytes 2457608 | tf_op jit(solution)/shard_map/ppermute | solution.py:97
  9.2 1.6 %copy-done.5 = bf16[2048,512]{1,0:T(8,128)(2,1)S(1)} copy-done((bf16[2048,512]{1,0:T(8,128)(2,1)S(1)}, bf16[2048,512]{1,0:T(8,128)(2,1)}, u32[]{:S(2)}) %copy-start.5) | copy-done | bytes 2097176
  10.8 1.6 %shard_map.66 = (bf16[160,1024]{1,0:T(8,128)(2,1)S(1)}, bf16[160,1024]{1,0:T(8,128)(2,1)S(1)}, bf16[144,384]{1,0:T(8,128)(2,1)S(1)}, f32[384,256]{1,0:T(8,128)S(1)}, f32[384,256]{1,0:T(8,128)S(1)}) custom-call(bf16[400,1024]{1,0:T(8,128)(2,1)S(1)} %get-tuple-element.31.own.refs_0_, bf16[400,1024]{1,0:T(8,128)(2,1)S(1)} %get-tuple-element.32.away, ...), custom_call_target="tpu_custom_call" | custom-call | flops 1031798784 | bytes 5287936 | tf_op jit(solution)/shard_map/pallas_call | solution.py:116
  12.4 6.2 %collective-permute-start.2 = (bf16[160,1024]{1,0:T(8,128)(2,1)S(1)}, bf16[160,1024]{1,0:T(8,128)(2,1)S(1)}, u32[]{:S(2)}, u32[]{:S(2)}) collective-permute-start(bf16[160,1024]{1,0:T(8,128)(2,1)S(1)} %get-tuple-element.34), channel_id=1, source_target_pairs={{0,20},{1,21},{2,22},{3,23},{12,24},{13,25},{14,26},{15,27},{16,4}... | collective-permute-start | bytes 983048 | tf_op jit(solution)/shard_map/ppermute | solution.py:97
  18.6 1.3 %collective-permute-start.1 = (bf16[160,1024]{1,0:T(8,128)(2,1)S(1)}, bf16[160,1024]{1,0:T(8,128)(2,1)S(1)}, u32[]{:S(2)}, u32[]{:S(2)}) collective-permute-start(bf16[160,1024]{1,0:T(8,128)(2,1)S(1)} %get-tuple-element.33), channel_id=1, source_target_pairs={{0,4},{1,5},{2,6},{3,7},{12,8},{13,9},{14,10},{15,11},{16,20},{17,... | collective-permute-start | bytes 983048 | tf_op jit(solution)/shard_map/ppermute | solution.py:97
  20.0 0.0 collective-permute-done.4.refs_4_
  20.0 0.0 collective-permute-done.3.refs_3_
  20.0 1.3 %collective-permute-start.6 = (bf16[1152,256]{1,0:T(8,128)(2,1)S(1)}, bf16[1152,256]{1,0:T(8,128)(2,1)S(1)}, u32[]{:S(2)}, u32[]{:S(2)}) collective-permute-start(bf16[1152,256]{1,0:T(8,128)(2,1)S(1)} %collective-permute-done.3.refs_3_), channel_id=1, source_target_pairs={{4,0},{5,1},{6,2},{7,3},{8,12},{9,13},{10,14},{11,15},{20,16},{21,... | collective-permute-start | bytes 1769480 | tf_op jit(solution)/shard_map/ppermute | solution.py:97
  21.3 0.7 %collective-permute-start.7 = (bf16[1152,256]{1,0:T(8,128)(2,1)S(1)}, bf16[1152,256]{1,0:T(8,128)(2,1)S(1)}, u32[]{:S(2)}, u32[]{:S(2)}) collective-permute-start(bf16[1152,256]{1,0:T(8,128)(2,1)S(1)} %collective-permute-done.4.refs_4_), channel_id=1, source_target_pairs={{4,8},{5,9},{6,10},{7,11},{8,4},{9,5},{10,6},{11,7},{20,24},{21,25... | collective-permute-start | bytes 1769480 | tf_op jit(solution)/shard_map/ppermute | solution.py:97
  22.0 5.4 %collective-permute-done.refs_1_ = bf16[400,1024]{1,0:T(8,128)(2,1)S(1)} collective-permute-done((bf16[400,1024]{1,0:T(8,128)(2,1)S(1)}, bf16[400,1024]{1,0:T(8,128)(2,1)S(1)}, u32[]{:S(2)}, u32[]{:S(2)}) %collective-permute-start) | collective-permute-done | bytes 819232 | tf_op jit(solution)/shard_map/ppermute | solution.py:97
  27.4 1.6 %shard_map.67 = (f32[2,384,128]{2,1,0:T(8,128)S(1)}, f32[2,384,256]{2,1,0:T(8,128)S(1)}, f32[384,1]{1,0:T(8,128)S(1)}, bf16[3,256,128]{2,1,0:T(8,128)(2,1)S(1)}) custom-call(bf16[400,1024]{1,0:T(8,128)(2,1)S(1)} %get-tuple-element.31.own.refs_0_, bf16[400,1024]{1,0:T(8,128)(2,1)S(1)} %collective-permute-done.refs_1_, ...), custom_call_target="tpu_custom_call" | custom-call | tf_op jit(solution)/shard_map/pallas_call | solution.py:116
  28.9 0.0 collective-permute-done.2.refs_1_.refs_3_
  29.0 3.1 %collective-permute-done.1.refs_0_.refs_2_ = bf16[160,1024]{1,0:T(8,128)(2,1)S(1)} collective-permute-done((bf16[160,1024]{1,0:T(8,128)(2,1)S(1)}, bf16[160,1024]{1,0:T(8,128)(2,1)S(1)}, u32[]{:S(2)}, u32[]{:S(2)}) %collective-permute-start.1) | collective-permute-done | bytes 327712 | tf_op jit(solution)/shard_map/ppermute | solution.py:97
  32.0 0.3 shard_map.68.refs_4_
  32.4 1.6 %collective-permute-start.9 = (f32[384,256]{1,0:T(8,128)S(1)}, f32[384,256]{1,0:T(8,128)S(1)}, u32[]{:S(2)}, u32[]{:S(2)}) collective-permute-start(f32[384,256]{1,0:T(8,128)S(1)} %get-tuple-element.46), channel_id=1, source_target_pairs={{0,2},{1,3},{2,0},{3,1},{4,6},{5,7},{6,4},{7,5},{8,10},{9,11},{10,... | collective-permute-start | bytes 1179656 | tf_op jit(solution)/shard_map/ppermute | solution.py:97
  33.9 4.4 %collective-permute-start.5 = (bf16[256,128]{1,0:T(8,128)(2,1)S(1)}, bf16[256,128]{1,0:T(8,128)(2,1)S(1)}, u32[]{:S(2)}, u32[]{:S(2)}) collective-permute-start(bf16[256,128]{1,0:T(8,128)(2,1)S(1)} %copy-done.2), channel_id=1, source_target_pairs={{0,12},{1,13},{2,14},{3,15},{12,0},{13,1},{14,2},{15,3},{16,28},{1... | collective-permute-start | bytes 196616 | tf_op jit(solution)/shard_map/ppermute | solution.py:97
  38.3 3.6 %collective-permute-done.5.distant = bf16[256,128]{1,0:T(8,128)(2,1)S(1)} collective-permute-done((bf16[256,128]{1,0:T(8,128)(2,1)S(1)}, bf16[256,128]{1,0:T(8,128)(2,1)S(1)}, u32[]{:S(2)}, u32[]{:S(2)}) %collective-permute-start.5) | collective-permute-done | bytes 65568 | tf_op jit(solution)/shard_map/ppermute | solution.py:97
  41.9 0.0 collective-permute-done.6.refs_7_
  41.9 0.0 collective-permute-done.7.refs_8_
  41.9 0.7 %shard_map.69 = (f32[16,384]{1,0:T(8,128)S(1)}, f32[16,384]{1,0:T(8,128)S(1)}, f32[16,144]{1,0:T(8,128)S(1)}, f32[16,144]{1,0:T(8,128)S(1)}, bf16[256,128]{1,0:T(8,128)(2,1)S(1)}) custom-call(bf16[400,1024]{1,0:T(8,128)(2,1)S(1)} %get-tuple-element.31.own.refs_0_, bf16[400,1024]{1,0:T(8,128)(2,1)S(1)} %collective-permute-done.refs_1_, ...), custom_call_target="tpu_custom_call" | custom-call | flops 553648128 | bytes 5081088 | tf_op jit(solution)/shard_map/pallas_call | solution.py:116
  42.5 1.6 %collective-permute-start.8 = (f32[16,384]{1,0:T(8,128)S(1)}, f32[16,384]{1,0:T(8,128)S(1)}, u32[]{:S(2)}, u32[]{:S(2)}) collective-permute-start(f32[16,384]{1,0:T(8,128)S(1)} %get-tuple-element.43), channel_id=1, source_target_pairs={{0,16},{1,17},{2,18},{3,19},{4,20},{5,21},{6,22},{7,23},{8,24},{9,... | collective-permute-start | bytes 73736 | tf_op jit(solution)/shard_map/ppermute | solution.py:97
  44.1 1.3 %collective-permute-start.10 = (f32[16,144]{1,0:T(8,128)S(1)}, f32[16,144]{1,0:T(8,128)S(1)}, u32[]{:S(2)}, u32[]{:S(2)}) collective-permute-start(f32[16,144]{1,0:T(8,128)S(1)} %get-tuple-element.47), channel_id=1, source_target_pairs={{4,0},{5,1},{6,2},{7,3},{8,12},{9,13},{10,14},{11,15},{20,16},{21,... | collective-permute-start | bytes 27656 | tf_op jit(solution)/shard_map/ppermute | solution.py:97
  45.4 1.3 %collective-permute-start.11 = (f32[16,144]{1,0:T(8,128)S(1)}, f32[16,144]{1,0:T(8,128)S(1)}, u32[]{:S(2)}, u32[]{:S(2)}) collective-permute-start(f32[16,144]{1,0:T(8,128)S(1)} %get-tuple-element.48), channel_id=1, source_target_pairs={{4,16},{5,17},{6,18},{7,19},{8,28},{9,29},{10,30},{11,31},{20,0},{... | collective-permute-start | bytes 27656 | tf_op jit(solution)/shard_map/ppermute | solution.py:97
  46.7 3.0 %collective-permute-done.10.refs_0_ = f32[16,144]{1,0:T(8,128)S(1)} collective-permute-done((f32[16,144]{1,0:T(8,128)S(1)}, f32[16,144]{1,0:T(8,128)S(1)}, u32[]{:S(2)}, u32[]{:S(2)}) %collective-permute-start.10) | collective-permute-done | bytes 9248 | tf_op jit(solution)/shard_map/ppermute | solution.py:97
  49.8 2.2 %collective-permute-done.11.refs_1_ = f32[16,144]{1,0:T(8,128)S(1)} collective-permute-done((f32[16,144]{1,0:T(8,128)S(1)}, f32[16,144]{1,0:T(8,128)S(1)}, u32[]{:S(2)}, u32[]{:S(2)}) %collective-permute-start.11) | collective-permute-done | bytes 9248 | tf_op jit(solution)/shard_map/ppermute | solution.py:97
  52.0 0.0 collective-permute-done.8.near
  52.0 0.0 collective-permute-done.9.got
  52.0 0.2 shard_map.70
  52.1 0.1 collective-permute-start.14
  52.2 0.7 %collective-permute-start.12 = (f32[16,384]{1,0:T(8,128)S(1)}, f32[16,384]{1,0:T(8,128)S(1)}, u32[]{:S(2)}, u32[]{:S(2)}) collective-permute-start(f32[16,384]{1,0:T(8,128)S(1)} %get-tuple-element.49), channel_id=1, source_target_pairs={{0,2},{1,3},{2,0},{3,1},{4,6},{5,7},{6,4},{7,5},{8,10},{9,11},{10,... | collective-permute-start | bytes 73736 | tf_op jit(solution)/shard_map/ppermute | solution.py:97
  52.9 3.2 %collective-permute-done.12 = f32[16,384]{1,0:T(8,128)S(1)} collective-permute-done((f32[16,384]{1,0:T(8,128)S(1)}, f32[16,384]{1,0:T(8,128)S(1)}, u32[]{:S(2)}, u32[]{:S(2)}) %collective-permute-start.12) | collective-permute-done | bytes 24608 | tf_op jit(solution)/shard_map/ppermute | solution.py:97
  56.1 0.0 collective-permute-start.13
  56.1 1.2 %collective-permute-done.13.far = f32[16,384]{1,0:T(8,128)S(1)} collective-permute-done((f32[16,384]{1,0:T(8,128)S(1)}, f32[16,384]{1,0:T(8,128)S(1)}, u32[]{:S(2)}, u32[]{:S(2)}) %collective-permute-start.13) | collective-permute-done | bytes 24608 | tf_op jit(solution)/shard_map/ppermute | solution.py:97
  57.3 0.0 collective-permute-done.14.got
  57.3 1.3 %shard_map.71 = bf16[384,128]{1,0:T(8,128)(2,1)} custom-call(f32[16,384]{1,0:T(8,128)S(1)} %add.3.near, f32[16,384]{1,0:T(8,128)S(1)} %collective-permute-done.13.far, f32[384,128]{1,0:T(8,128)S(1)} %get-tuple-element.50.keep, f32[384,128]{1,0:T(8,128)S(1)} %collective-permute-done.14.got, f32[384,1]{1,0:T(8,128)S(1)} %get-tuple-element.52.numbers, ...), custom_call_target="tpu_custom_call" | custom-call | bytes 869888 | tf_op jit(solution)/shard_map/pallas_call | solution.py:116
  (3 shorter events, 0.0 us)
Async XLA Ops:
  0.0 6.1 %copy-start = (bf16[384,2048]{1,0:T(8,128)(2,1)S(1)}, bf16[384,2048]{1,0:T(8,128)(2,1)}, u32[]{:S(2)}) copy-start(bf16[384,2048]{1,0:T(8,128)(2,1)} %tokens.1) | copy-start | bytes 4718596
  0.0 1.3 %copy-start.1 = (bf16[2048,256]{1,0:T(8,128)(2,1)S(1)}, bf16[2048,256]{1,0:T(8,128)(2,1)}, u32[]{:S(2)}) copy-start(bf16[2048,256]{1,0:T(8,128)(2,1)} %down.1) | copy-start | bytes 3145732
  1.3 0.8 %copy-start.2 = (bf16[256,128]{1,0:T(8,128)(2,1)S(1)}, bf16[256,128]{1,0:T(8,128)(2,1)}, u32[]{:S(2)}) copy-start(bf16[256,128]{1,0:T(8,128)(2,1)} %up.1) | copy-start | bytes 196612
  2.3 17.7 %collective-permute-start.4 = (bf16[1152,256]{1,0:T(8,128)(2,1)S(1)}, bf16[1152,256]{1,0:T(8,128)(2,1)S(1)}, u32[]{:S(2)}, u32[]{:S(2)}) collective-permute-start(bf16[1152,256]{1,0:T(8,128)(2,1)S(1)} %shard_map.64.refs_2_), channel_id=1, source_target_pairs={{0,4},{1,5},{2,6},{3,7},{4,0},{5,1},{6,2},{7,3},{8,12},{9,13},{10,... | collective-permute-start | bytes 1769480 | tf_op jit(solution)/shard_map/ppermute | solution.py:97
  5.4 14.6 %collective-permute-start.3 = (bf16[1152,256]{1,0:T(8,128)(2,1)S(1)}, bf16[1152,256]{1,0:T(8,128)(2,1)S(1)}, u32[]{:S(2)}, u32[]{:S(2)}) collective-permute-start(bf16[1152,256]{1,0:T(8,128)(2,1)S(1)} %shard_map.64.refs_2_), channel_id=1, source_target_pairs={{4,8},{5,9},{6,10},{7,11},{8,4},{9,5},{10,6},{11,7},{20,24},{21,25... | collective-permute-start | bytes 1769480 | tf_op jit(solution)/shard_map/ppermute | solution.py:97
  6.1 0.7 %copy-start.3 = (s32[384]{0:T(512)S(1)}, s32[384]{0:T(512)}, u32[]{:S(2)}) copy-start(s32[384]{0:T(512)} %slot) | copy-start | bytes 4612
  6.8 0.7 %copy-start.4 = (s32[384,1]{0,1:T(1,128)S(1)}, s32[384,1]{0,1:T(1,128)}, u32[]{:S(2)}) copy-start(s32[384,1]{0,1:T(1,128)} %param.10) | copy-start | bytes 4612
  7.6 19.8 %collective-permute-start = (bf16[400,1024]{1,0:T(8,128)(2,1)S(1)}, bf16[400,1024]{1,0:T(8,128)(2,1)S(1)}, u32[]{:S(2)}, u32[]{:S(2)}) collective-permute-start(bf16[400,1024]{1,0:T(8,128)(2,1)S(1)} %get-tuple-element.32.away), channel_id=1, source_target_pairs={{0,16},{1,17},{2,18},{3,19},{4,20},{5,21},{6,22},{7,23},{8,24},{9,... | collective-permute-start | bytes 2457608 | tf_op jit(solution)/shard_map/ppermute | solution.py:97
  9.2 1.6 %copy-start.5 = (bf16[2048,512]{1,0:T(8,128)(2,1)S(1)}, bf16[2048,512]{1,0:T(8,128)(2,1)}, u32[]{:S(2)}) copy-start(bf16[2048,512]{1,0:T(8,128)(2,1)} %weights.1) | copy-start | bytes 6291460
  12.4 16.6 %collective-permute-start.2 = (bf16[160,1024]{1,0:T(8,128)(2,1)S(1)}, bf16[160,1024]{1,0:T(8,128)(2,1)S(1)}, u32[]{:S(2)}, u32[]{:S(2)}) collective-permute-start(bf16[160,1024]{1,0:T(8,128)(2,1)S(1)} %get-tuple-element.34), channel_id=1, source_target_pairs={{0,20},{1,21},{2,22},{3,23},{12,24},{13,25},{14,26},{15,27},{16,4}... | collective-permute-start | bytes 983048 | tf_op jit(solution)/shard_map/ppermute | solution.py:97
  18.6 13.4 %collective-permute-start.1 = (bf16[160,1024]{1,0:T(8,128)(2,1)S(1)}, bf16[160,1024]{1,0:T(8,128)(2,1)S(1)}, u32[]{:S(2)}, u32[]{:S(2)}) collective-permute-start(bf16[160,1024]{1,0:T(8,128)(2,1)S(1)} %get-tuple-element.33), channel_id=1, source_target_pairs={{0,4},{1,5},{2,6},{3,7},{12,8},{13,9},{14,10},{15,11},{16,20},{17,... | collective-permute-start | bytes 983048 | tf_op jit(solution)/shard_map/ppermute | solution.py:97
  20.0 21.9 %collective-permute-start.6 = (bf16[1152,256]{1,0:T(8,128)(2,1)S(1)}, bf16[1152,256]{1,0:T(8,128)(2,1)S(1)}, u32[]{:S(2)}, u32[]{:S(2)}) collective-permute-start(bf16[1152,256]{1,0:T(8,128)(2,1)S(1)} %collective-permute-done.3.refs_3_), channel_id=1, source_target_pairs={{4,0},{5,1},{6,2},{7,3},{8,12},{9,13},{10,14},{11,15},{20,16},{21,... | collective-permute-start | bytes 1769480 | tf_op jit(solution)/shard_map/ppermute | solution.py:97
  21.3 20.6 %collective-permute-start.7 = (bf16[1152,256]{1,0:T(8,128)(2,1)S(1)}, bf16[1152,256]{1,0:T(8,128)(2,1)S(1)}, u32[]{:S(2)}, u32[]{:S(2)}) collective-permute-start(bf16[1152,256]{1,0:T(8,128)(2,1)S(1)} %collective-permute-done.4.refs_4_), channel_id=1, source_target_pairs={{4,8},{5,9},{6,10},{7,11},{8,4},{9,5},{10,6},{11,7},{20,24},{21,25... | collective-permute-start | bytes 1769480 | tf_op jit(solution)/shard_map/ppermute | solution.py:97
  32.4 19.6 %collective-permute-start.9 = (f32[384,256]{1,0:T(8,128)S(1)}, f32[384,256]{1,0:T(8,128)S(1)}, u32[]{:S(2)}, u32[]{:S(2)}) collective-permute-start(f32[384,256]{1,0:T(8,128)S(1)} %get-tuple-element.46), channel_id=1, source_target_pairs={{0,2},{1,3},{2,0},{3,1},{4,6},{5,7},{6,4},{7,5},{8,10},{9,11},{10,... | collective-permute-start | bytes 1179656 | tf_op jit(solution)/shard_map/ppermute | solution.py:97
  33.9 7.9 %collective-permute-start.5 = (bf16[256,128]{1,0:T(8,128)(2,1)S(1)}, bf16[256,128]{1,0:T(8,128)(2,1)S(1)}, u32[]{:S(2)}, u32[]{:S(2)}) collective-permute-start(bf16[256,128]{1,0:T(8,128)(2,1)S(1)} %copy-done.2), channel_id=1, source_target_pairs={{0,12},{1,13},{2,14},{3,15},{12,0},{13,1},{14,2},{15,3},{16,28},{1... | collective-permute-start | bytes 196616 | tf_op jit(solution)/shard_map/ppermute | solution.py:97
  42.5 9.4 %collective-permute-start.8 = (f32[16,384]{1,0:T(8,128)S(1)}, f32[16,384]{1,0:T(8,128)S(1)}, u32[]{:S(2)}, u32[]{:S(2)}) collective-permute-start(f32[16,384]{1,0:T(8,128)S(1)} %get-tuple-element.43), channel_id=1, source_target_pairs={{0,16},{1,17},{2,18},{3,19},{4,20},{5,21},{6,22},{7,23},{8,24},{9,... | collective-permute-start | bytes 73736 | tf_op jit(solution)/shard_map/ppermute | solution.py:97
  44.1 5.6 %collective-permute-start.10 = (f32[16,144]{1,0:T(8,128)S(1)}, f32[16,144]{1,0:T(8,128)S(1)}, u32[]{:S(2)}, u32[]{:S(2)}) collective-permute-start(f32[16,144]{1,0:T(8,128)S(1)} %get-tuple-element.47), channel_id=1, source_target_pairs={{4,0},{5,1},{6,2},{7,3},{8,12},{9,13},{10,14},{11,15},{20,16},{21,... | collective-permute-start | bytes 27656 | tf_op jit(solution)/shard_map/ppermute | solution.py:97
  45.4 6.5 %collective-permute-start.11 = (f32[16,144]{1,0:T(8,128)S(1)}, f32[16,144]{1,0:T(8,128)S(1)}, u32[]{:S(2)}, u32[]{:S(2)}) collective-permute-start(f32[16,144]{1,0:T(8,128)S(1)} %get-tuple-element.48), channel_id=1, source_target_pairs={{4,16},{5,17},{6,18},{7,19},{8,28},{9,29},{10,30},{11,31},{20,0},{... | collective-permute-start | bytes 27656 | tf_op jit(solution)/shard_map/ppermute | solution.py:97
  52.1 5.2 %collective-permute-start.14 = (f32[384,128]{1,0:T(8,128)S(1)}, f32[384,128]{1,0:T(8,128)S(1)}, u32[]{:S(2)}, u32[]{:S(2)}) collective-permute-start(f32[384,128]{1,0:T(8,128)S(1)} %get-tuple-element.51), channel_id=1, source_target_pairs={{0,1},{1,0},{2,3},{3,2},{4,5},{5,4},{6,7},{7,6},{8,9},{9,8},{10,11... | collective-permute-start | bytes 589832 | tf_op jit(solution)/shard_map/ppermute | solution.py:97
  52.2 3.9 %collective-permute-start.12 = (f32[16,384]{1,0:T(8,128)S(1)}, f32[16,384]{1,0:T(8,128)S(1)}, u32[]{:S(2)}, u32[]{:S(2)}) collective-permute-start(f32[16,384]{1,0:T(8,128)S(1)} %get-tuple-element.49), channel_id=1, source_target_pairs={{0,2},{1,3},{2,0},{3,1},{4,6},{5,7},{6,4},{7,5},{8,10},{9,11},{10,... | collective-permute-start | bytes 73736 | tf_op jit(solution)/shard_map/ppermute | solution.py:97
  56.1 1.2 %collective-permute-start.13 = (f32[16,384]{1,0:T(8,128)S(1)}, f32[16,384]{1,0:T(8,128)S(1)}, u32[]{:S(2)}, u32[]{:S(2)}) collective-permute-start(f32[16,384]{1,0:T(8,128)S(1)} %add.3.near), channel_id=1, source_target_pairs={{0,1},{1,0},{2,3},{3,2},{4,5},{5,4},{6,7},{7,6},{8,9},{9,8},{10,11... | collective-permute-start | bytes 73736 | tf_op jit(solution)/shard_map/ppermute | solution.py:97

commit v11 on v10

--- a/solution.py
+++ b/solution.py
@@ -76,6 +76,7 @@
 
 AXES = ("groups", "adapter", "mp")
 ID_ROWS = 16
+HOP_URGENCY = 3 * 10**9
 OWNERS = 4
 LANES = 128
 NT = (((1,), (1,)), ((), ()))
@@ -152,7 +153,7 @@
     copy_all(copies)
 
 
-def split_body(tokens, owner, slot, own, away, sems):
+def split_body(tokens, owner, slot, _, own, away, sems):
     g = lax.axis_index("groups")
     rows, part = tokens.shape[0], own.shape[1]
     copies = []
@@ -171,8 +172,8 @@
         copy.wait()
 
 
-def hop_body(rows, capacity, own, away, weights, own_out, away_out, places, keep, give, base):
-    a, g = lax.axis_index("adapter"), lax.axis_index("groups")
+def hop_body(rows, capacity, own, away, own_out, away_out, places):
+    a = lax.axis_index("adapter")
     part = own.shape[1]
     ids = own[rows:, :rows]
     match = (ids.astype(jnp.float32) == (OWNERS - 1 - a).astype(jnp.float32)).astype(jnp.bfloat16)
@@ -190,12 +191,17 @@
         out[:capacity, :] = packed.astype(jnp.bfloat16)
         out[capacity:, :] = jnp.zeros((ID_ROWS, part), jnp.bfloat16)
         out[capacity:, :capacity] = kept.astype(jnp.bfloat16)
+
+
+def base_body(bit, rows, own, away, weights, _, keep, give, base):
+    g = lax.axis_index("groups")
+    part = own.shape[1]
     total = jnp.zeros(base.shape, jnp.float32)
     for tokens, half in ((own, g), (away, 1 - g)):
         part_weights = weights[pl.ds(pl.multiple_of(half * part, part), part), :]
         total = total + jnp.dot(tokens[:rows, :], part_weights, preferred_element_type=jnp.float32)
     base[...] = total
-    halves(base, lax.axis_size("mp") // 2, keep, give)
+    halves(base, bit, keep, give)
 
 
 def halves(base, bit, keep, give):
@@ -381,23 +387,21 @@
     tok_own, tok_away = kernel(
         split_body,
         [narrow(rows + ID_ROWS, part)] * groups,
-        (tokens, request_adapter_owner.reshape(1, rows), after(request_adapter_slot, own)),
+        (tokens, request_adapter_owner.reshape(1, rows), request_adapter_slot, own),
         0,
-        (pltpu.HBM, None, None),
+        (pltpu.HBM, None, None, pl.ANY),
         [pltpu.SemaphoreType.DMA((groups,))],
     )
     token_parts = [tok_own, exchange(tok_away, 1, 0, SAME)]
-    hop_own, hop_away, places, keep, give = kernel(
+    hop_own, hop_away, places = kernel(
         functools.partial(hop_body, rows, capacity),
         [narrow(capacity + ID_ROWS, part)] * groups
-        + [narrow(capacity, rows)]
-        + [wide(rows, shares * keys // 2)] * 2,
-        (tok_own, tok_away, base_key_weight),
-        2 * rows * features * (capacity + shares * keys),
-        scratch=[pltpu.VMEM((rows, shares * keys), jnp.float32)],
-    )
-
-    inside = exchange(after(beside, places), 0, 0, MIDDLE)
+        + [narrow(capacity, rows)],
+        (tok_own, tok_away),
+        2 * rows * features * capacity,
+    )
+
+    inside = exchange(beside, 0, 0, MIDDLE)
     outside = exchange(mirror, 0, 0, OUTWARD)
     hops = [
         exchange(hop_own, 0, 0, INWARD),
@@ -415,9 +419,18 @@
         functools.partial(hop_mask_body, capacity),
         wide(groups, capacity, columns),
         (hops[0], after(hops[1], folded)),
+        HOP_URGENCY,
     )
     bits = (2, 1)
-    got = exchange(after(give, hop_mask), 0, bits[0], SAME)
+    keep, give = kernel(
+        functools.partial(base_body, bits[0], rows),
+        [wide(rows, shares * keys // 2)] * 2,
+        (tok_own, tok_away, base_key_weight, places),
+        2 * rows * features * shares * keys,
+        (None, None, None, pl.ANY),
+        [pltpu.VMEM((rows, shares * keys), jnp.float32)],
+    )
+    got = exchange(give, 0, bits[0], SAME)
 
     low, low_away, back, back_away, last_up = kernel(
         functools.partial(last_body, part, rows, capacity),

time: 58.9 us -> 58 us (0.985)
  waiting for transfers between devices: 21.6 us -> 24.9 us
  starting transfers between devices: 25.8 us -> 23.2 us
  local copies, waits for them, and re-layouts: 5.13 us -> 3.56 us
    ppermute x15, waiting for transfers between devices: 21.6 us -> 24.9 us  [exchange(): return lax.ppermute(x, AXES, pairs)]
    ppermute x15, starting transfers between devices: 25.8 us -> 23.2 us  [exchange(): return lax.ppermute(x, AXES, pairs)]
    unnamed x12 -> x14, local copies, waits for them, and re-layouts: 5.13 us -> 3.56 us
    pallas_call x8 -> x9, Pallas kernels: 5.81 us -> 5.86 us  [kernel(): pl.pallas_call(body, out_shape=outs, in_specs=specs or [inner] * len(oper...]
  transfers between devices with their start and end apart: 15 -> 15, of which waited for: 7 -> 7; matrix products, arithmetic and copies ran while one was open for 0% -> 0% of each run, Pallas kernels for 7% -> 8%
where the time goes in v11:
time: 58 us; the launch traced here: 57.7 us
  waiting for transfers between devices  24.9 us (43%)
  starting transfers between devices  23.2 us (40%)
  Pallas kernels  5.86 us (10%)
  local copies, waits for them, and re-layouts  3.56 us (6%)
    ppermute x15, waiting for transfers between devices, exchange(): return lax.ppermute(x, AXES, pairs)  24.9 us
    ppermute x15, starting transfers between devices, exchange(): return lax.ppermute(x, AXES, pairs)  23.2 us
    pallas_call x9, Pallas kernels, kernel(): pl.pallas_call(body, out_shape=outs, in_specs=specs or [inner] * len(oper...  5.86 us
    unnamed x14, local copies, waits for them, and re-layouts  3.56 us
  transfers between devices with their start and end apart: 15, of which 7 were waited for; matrix products, arithmetic and copies ran while one was open for 0% of the time, Pallas kernels for 8%

profile of v11, /device:TPU:0, one launch (start us, length us, event | category | flops | bytes accessed | tf_op | source)
XLA Modules:
  0.0 57.7 jit_solution(5182526183461426875)
XLA Ops:
  0.0 1.3 %copy-done.2 = bf16[2048,256]{1,0:T(8,128)(2,1)S(1)} copy-done((bf16[2048,256]{1,0:T(8,128)(2,1)S(1)}, bf16[2048,256]{1,0:T(8,128)(2,1)}, u32[]{:S(2)}) %copy-start.2) | copy-done | bytes 1048600
  1.3 0.8 %copy-done.3 = bf16[256,128]{1,0:T(8,128)(2,1)S(1)} copy-done((bf16[256,128]{1,0:T(8,128)(2,1)S(1)}, bf16[256,128]{1,0:T(8,128)(2,1)}, u32[]{:S(2)}) %copy-start.3) | copy-done | bytes 65560
  2.2 0.1 shard_map.64._.refs_2_
  2.3 0.0 copy-start
  2.3 0.8 %collective-permute-start.3 = (bf16[1152,256]{1,0:T(8,128)(2,1)S(1)}, bf16[1152,256]{1,0:T(8,128)(2,1)S(1)}, u32[]{:S(2)}, u32[]{:S(2)}) collective-permute-start(bf16[1152,256]{1,0:T(8,128)(2,1)S(1)} %shard_map.64._.refs_2_), channel_id=1, source_target_pairs={{4,8},{5,9},{6,10},{7,11},{8,4},{9,5},{10,6},{11,7},{20,24},{21,25... | collective-permute-start | bytes 1769480 | tf_op jit(solution)/shard_map/ppermute | solution.py:98
  3.1 5.9 %collective-permute-start.4 = (bf16[1152,256]{1,0:T(8,128)(2,1)S(1)}, bf16[1152,256]{1,0:T(8,128)(2,1)S(1)}, u32[]{:S(2)}, u32[]{:S(2)}) collective-permute-start(bf16[1152,256]{1,0:T(8,128)(2,1)S(1)} %shard_map.64._.refs_2_), channel_id=1, source_target_pairs={{0,4},{1,5},{2,6},{3,7},{4,0},{5,1},{6,2},{7,3},{8,12},{9,13},{10,... | collective-permute-start | bytes 1769480 | tf_op jit(solution)/shard_map/ppermute | solution.py:98
  9.0 0.0 copy-done.1
  9.0 0.7 %copy-done.5 = s32[384]{0:T(512)S(1)} copy-done((s32[384]{0:T(512)S(1)}, s32[384]{0:T(512)}, u32[]{:S(2)}) %copy-start.5) | copy-done | bytes 1560
  9.7 0.7 %copy-done.6 = s32[384,1]{0,1:T(1,128)S(1)} copy-done((s32[384,1]{0,1:T(1,128)S(1)}, s32[384,1]{0,1:T(1,128)}, u32[]{:S(2)}) %copy-start.6) | copy-done | bytes 1560
  10.4 0.1 shard_map.65
  10.5 1.6 %collective-permute-start = (bf16[400,1024]{1,0:T(8,128)(2,1)S(1)}, bf16[400,1024]{1,0:T(8,128)(2,1)S(1)}, u32[]{:S(2)}, u32[]{:S(2)}) collective-permute-start(bf16[400,1024]{1,0:T(8,128)(2,1)S(1)} %get-tuple-element.28.away), channel_id=1, source_target_pairs={{0,16},{1,17},{2,18},{3,19},{4,20},{5,21},{6,22},{7,23},{8,24},{9,... | collective-permute-start | bytes 2457608 | tf_op jit(solution)/shard_map/ppermute | solution.py:98
  12.1 0.7 %shard_map.66 = (bf16[160,1024]{1,0:T(8,128)(2,1)S(1)}, bf16[160,1024]{1,0:T(8,128)(2,1)S(1)}, bf16[144,384]{1,0:T(8,128)(2,1)S(1)}) custom-call(bf16[400,1024]{1,0:T(8,128)(2,1)S(1)} %get-tuple-element.27.own.refs_0_, bf16[400,1024]{1,0:T(8,128)(2,1)S(1)} %get-tuple-element.28.away), custom_call_target="tpu_custom_call" | custom-call | flops 226492416 | bytes 2404352 | tf_op jit(solution)/shard_map/pallas_call | solution.py:117
  12.8 1.9 %collective-permute-start.2 = (bf16[160,1024]{1,0:T(8,128)(2,1)S(1)}, bf16[160,1024]{1,0:T(8,128)(2,1)S(1)}, u32[]{:S(2)}, u32[]{:S(2)}) collective-permute-start(bf16[160,1024]{1,0:T(8,128)(2,1)S(1)} %get-tuple-element.30), channel_id=1, source_target_pairs={{0,20},{1,21},{2,22},{3,23},{12,24},{13,25},{14,26},{15,27},{16,4}... | collective-permute-start | bytes 983048 | tf_op jit(solution)/shard_map/ppermute | solution.py:98
  14.7 1.4 %collective-permute-start.1 = (bf16[160,1024]{1,0:T(8,128)(2,1)S(1)}, bf16[160,1024]{1,0:T(8,128)(2,1)S(1)}, u32[]{:S(2)}, u32[]{:S(2)}) collective-permute-start(bf16[160,1024]{1,0:T(8,128)(2,1)S(1)} %get-tuple-element.29), channel_id=1, source_target_pairs={{0,4},{1,5},{2,6},{3,7},{12,8},{13,9},{14,10},{15,11},{16,20},{17,... | collective-permute-start | bytes 983048 | tf_op jit(solution)/shard_map/ppermute | solution.py:98
  16.0 0.0 collective-permute-done.3.refs_3_
  16.0 1.3 %collective-permute-start.6 = (bf16[1152,256]{1,0:T(8,128)(2,1)S(1)}, bf16[1152,256]{1,0:T(8,128)(2,1)S(1)}, u32[]{:S(2)}, u32[]{:S(2)}) collective-permute-start(bf16[1152,256]{1,0:T(8,128)(2,1)S(1)} %collective-permute-done.3.refs_3_), channel_id=1, source_target_pairs={{4,0},{5,1},{6,2},{7,3},{8,12},{9,13},{10,14},{11,15},{20,16},{21,... | collective-permute-start | bytes 1769480 | tf_op jit(solution)/shard_map/ppermute | solution.py:98
  17.3 5.4 %collective-permute-done.4.refs_4_ = bf16[1152,256]{1,0:T(8,128)(2,1)S(1)} collective-permute-done((bf16[1152,256]{1,0:T(8,128)(2,1)S(1)}, bf16[1152,256]{1,0:T(8,128)(2,1)S(1)}, u32[]{:S(2)}, u32[]{:S(2)}) %collective-permute-start.4) | collective-permute-done | bytes 589856 | tf_op jit(solution)/shard_map/ppermute | solution.py:98
  22.8 0.7 %collective-permute-start.7 = (bf16[1152,256]{1,0:T(8,128)(2,1)S(1)}, bf16[1152,256]{1,0:T(8,128)(2,1)S(1)}, u32[]{:S(2)}, u32[]{:S(2)}) collective-permute-start(bf16[1152,256]{1,0:T(8,128)(2,1)S(1)} %collective-permute-done.4.refs_4_), channel_id=1, source_target_pairs={{4,8},{5,9},{6,10},{7,11},{8,4},{9,5},{10,6},{11,7},{20,24},{21,25... | collective-permute-start | bytes 1769480 | tf_op jit(solution)/shard_map/ppermute | solution.py:98
  23.5 0.0 copy-done
  23.5 1.1 %shard_map.70 = (f32[384,256]{1,0:T(8,128)S(1)}, f32[384,256]{1,0:T(8,128)S(1)}) custom-call(bf16[400,1024]{1,0:T(8,128)(2,1)S(1)} %get-tuple-element.27.own.refs_0_, bf16[400,1024]{1,0:T(8,128)(2,1)S(1)} %get-tuple-element.28.away, bf16[2048,512]{1,0:T(8,128)(2,1)S(1)} %copy-done, bf16[144,384]{1,0:T(8,128)(2,1)S(1)} %get-tuple-element.38._.places), custom_call_target="tpu_custom_call" | custom-call | flops 805306368 | bytes 4632576 | tf_op jit(solution)/shard_map/pallas_call | solution.py:117
  24.5 0.0 copy-start.4
  24.6 5.4 %collective-permute-done.refs_1_ = bf16[400,1024]{1,0:T(8,128)(2,1)S(1)} collective-permute-done((bf16[400,1024]{1,0:T(8,128)(2,1)S(1)}, bf16[400,1024]{1,0:T(8,128)(2,1)S(1)}, u32[]{:S(2)}, u32[]{:S(2)}) %collective-permute-start) | collective-permute-done | bytes 819232 | tf_op jit(solution)/shard_map/ppermute | solution.py:98
  30.0 1.5 %collective-permute-start.9 = (f32[384,256]{1,0:T(8,128)S(1)}, f32[384,256]{1,0:T(8,128)S(1)}, u32[]{:S(2)}, u32[]{:S(2)}) collective-permute-start(f32[384,256]{1,0:T(8,128)S(1)} %get-tuple-element.40), channel_id=1, source_target_pairs={{0,2},{1,3},{2,0},{3,1},{4,6},{5,7},{6,4},{7,5},{8,10},{9,11},{10,... | collective-permute-start | bytes 1179656 | tf_op jit(solution)/shard_map/ppermute | solution.py:98
  31.5 1.5 %shard_map.67 = (f32[2,384,128]{2,1,0:T(8,128)S(1)}, f32[2,384,256]{2,1,0:T(8,128)S(1)}, f32[384,1]{1,0:T(8,128)S(1)}, bf16[3,256,128]{2,1,0:T(8,128)(2,1)S(1)}) custom-call(bf16[400,1024]{1,0:T(8,128)(2,1)S(1)} %get-tuple-element.27.own.refs_0_, bf16[400,1024]{1,0:T(8,128)(2,1)S(1)} %collective-permute-done.refs_1_, ...), custom_call_target="tpu_custom_call" | custom-call | tf_op jit(solution)/shard_map/pallas_call | solution.py:117
  33.0 0.0 collective-permute-done.2.refs_1_.refs_3_
  33.0 0.0 copy-done.4
  33.0 3.3 %collective-permute-start.5 = (bf16[256,128]{1,0:T(8,128)(2,1)S(1)}, bf16[256,128]{1,0:T(8,128)(2,1)S(1)}, u32[]{:S(2)}, u32[]{:S(2)}) collective-permute-start(bf16[256,128]{1,0:T(8,128)(2,1)S(1)} %copy-done.4), channel_id=1, source_target_pairs={{0,12},{1,13},{2,14},{3,15},{12,0},{13,1},{14,2},{15,3},{16,28},{1... | collective-permute-start | bytes 196616 | tf_op jit(solution)/shard_map/ppermute | solution.py:98
  36.3 0.0 collective-permute-done.1.refs_0_.refs_2_
  36.3 0.3 shard_map.68.refs_4_
  36.6 4.4 %collective-permute-done.5.distant = bf16[256,128]{1,0:T(8,128)(2,1)S(1)} collective-permute-done((bf16[256,128]{1,0:T(8,128)(2,1)S(1)}, bf16[256,128]{1,0:T(8,128)(2,1)S(1)}, u32[]{:S(2)}, u32[]{:S(2)}) %collective-permute-start.5) | collective-permute-done | bytes 65568 | tf_op jit(solution)/shard_map/ppermute | solution.py:98
  41.0 0.0 collective-permute-done.6.refs_7_
  41.0 0.0 collective-permute-done.7.refs_8_
  41.0 0.7 %shard_map.69 = (f32[16,384]{1,0:T(8,128)S(1)}, f32[16,384]{1,0:T(8,128)S(1)}, f32[16,144]{1,0:T(8,128)S(1)}, f32[16,144]{1,0:T(8,128)S(1)}, bf16[256,128]{1,0:T(8,128)(2,1)S(1)}) custom-call(bf16[400,1024]{1,0:T(8,128)(2,1)S(1)} %get-tuple-element.27.own.refs_0_, bf16[400,1024]{1,0:T(8,128)(2,1)S(1)} %collective-permute-done.refs_1_, ...), custom_call_target="tpu_custom_call" | custom-call | flops 553648128 | bytes 5081088 | tf_op jit(solution)/shard_map/pallas_call | solution.py:117
  41.7 1.6 %collective-permute-start.8 = (f32[16,384]{1,0:T(8,128)S(1)}, f32[16,384]{1,0:T(8,128)S(1)}, u32[]{:S(2)}, u32[]{:S(2)}) collective-permute-start(f32[16,384]{1,0:T(8,128)S(1)} %get-tuple-element.37), channel_id=1, source_target_pairs={{0,16},{1,17},{2,18},{3,19},{4,20},{5,21},{6,22},{7,23},{8,24},{9,... | collective-permute-start | bytes 73736 | tf_op jit(solution)/shard_map/ppermute | solution.py:98
  43.3 1.3 %collective-permute-start.10 = (f32[16,144]{1,0:T(8,128)S(1)}, f32[16,144]{1,0:T(8,128)S(1)}, u32[]{:S(2)}, u32[]{:S(2)}) collective-permute-start(f32[16,144]{1,0:T(8,128)S(1)} %get-tuple-element.41), channel_id=1, source_target_pairs={{4,0},{5,1},{6,2},{7,3},{8,12},{9,13},{10,14},{11,15},{20,16},{21,... | collective-permute-start | bytes 27656 | tf_op jit(solution)/shard_map/ppermute | solution.py:98
  44.5 1.3 %collective-permute-start.11 = (f32[16,144]{1,0:T(8,128)S(1)}, f32[16,144]{1,0:T(8,128)S(1)}, u32[]{:S(2)}, u32[]{:S(2)}) collective-permute-start(f32[16,144]{1,0:T(8,128)S(1)} %get-tuple-element.42), channel_id=1, source_target_pairs={{4,16},{5,17},{6,18},{7,19},{8,28},{9,29},{10,30},{11,31},{20,0},{... | collective-permute-start | bytes 27656 | tf_op jit(solution)/shard_map/ppermute | solution.py:98
  45.8 0.0 collective-permute-done.9.got
  45.9 3.0 %collective-permute-done.10.refs_0_ = f32[16,144]{1,0:T(8,128)S(1)} collective-permute-done((f32[16,144]{1,0:T(8,128)S(1)}, f32[16,144]{1,0:T(8,128)S(1)}, u32[]{:S(2)}, u32[]{:S(2)}) %collective-permute-start.10) | collective-permute-done | bytes 9248 | tf_op jit(solution)/shard_map/ppermute | solution.py:98
  48.9 2.2 %collective-permute-done.11.refs_1_ = f32[16,144]{1,0:T(8,128)S(1)} collective-permute-done((f32[16,144]{1,0:T(8,128)S(1)}, f32[16,144]{1,0:T(8,128)S(1)}, u32[]{:S(2)}, u32[]{:S(2)}) %collective-permute-start.11) | collective-permute-done | bytes 9248 | tf_op jit(solution)/shard_map/ppermute | solution.py:98
  51.1 0.0 collective-permute-done.8.near
  51.1 0.2 shard_map.71
  51.2 0.1 collective-permute-start.14
  51.3 0.7 %collective-permute-start.12 = (f32[16,384]{1,0:T(8,128)S(1)}, f32[16,384]{1,0:T(8,128)S(1)}, u32[]{:S(2)}, u32[]{:S(2)}) collective-permute-start(f32[16,384]{1,0:T(8,128)S(1)} %get-tuple-element.43), channel_id=1, source_target_pairs={{0,2},{1,3},{2,0},{3,1},{4,6},{5,7},{6,4},{7,5},{8,10},{9,11},{10,... | collective-permute-start | bytes 73736 | tf_op jit(solution)/shard_map/ppermute | solution.py:98
  52.0 3.2 %collective-permute-done.12 = f32[16,384]{1,0:T(8,128)S(1)} collective-permute-done((f32[16,384]{1,0:T(8,128)S(1)}, f32[16,384]{1,0:T(8,128)S(1)}, u32[]{:S(2)}, u32[]{:S(2)}) %collective-permute-start.12) | collective-permute-done | bytes 24608 | tf_op jit(solution)/shard_map/ppermute | solution.py:98
  55.2 0.0 collective-permute-start.13
  55.2 1.2 %collective-permute-done.13.far = f32[16,384]{1,0:T(8,128)S(1)} collective-permute-done((f32[16,384]{1,0:T(8,128)S(1)}, f32[16,384]{1,0:T(8,128)S(1)}, u32[]{:S(2)}, u32[]{:S(2)}) %collective-permute-start.13) | collective-permute-done | bytes 24608 | tf_op jit(solution)/shard_map/ppermute | solution.py:98
  56.4 0.0 collective-permute-done.14.got
  56.4 1.3 %shard_map.72 = bf16[384,128]{1,0:T(8,128)(2,1)} custom-call(f32[16,384]{1,0:T(8,128)S(1)} %add.3.near, f32[16,384]{1,0:T(8,128)S(1)} %collective-permute-done.13.far, f32[384,128]{1,0:T(8,128)S(1)} %get-tuple-element.44.keep, f32[384,128]{1,0:T(8,128)S(1)} %collective-permute-done.14.got, f32[384,1]{1,0:T(8,128)S(1)} %get-tuple-element.46.numbers, ...), custom_call_target="tpu_custom_call" | custom-call | bytes 869888 | tf_op jit(solution)/shard_map/pallas_call | solution.py:117
  (6 shorter events, 0.0 us)
Async XLA Ops:
  0.0 9.0 %copy-start.1 = (bf16[384,2048]{1,0:T(8,128)(2,1)S(1)}, bf16[384,2048]{1,0:T(8,128)(2,1)}, u32[]{:S(2)}) copy-start(bf16[384,2048]{1,0:T(8,128)(2,1)} %tokens.1) | copy-start | bytes 4718596
  0.0 1.3 %copy-start.2 = (bf16[2048,256]{1,0:T(8,128)(2,1)S(1)}, bf16[2048,256]{1,0:T(8,128)(2,1)}, u32[]{:S(2)}) copy-start(bf16[2048,256]{1,0:T(8,128)(2,1)} %down.1) | copy-start | bytes 3145732
  1.3 0.8 %copy-start.3 = (bf16[256,128]{1,0:T(8,128)(2,1)S(1)}, bf16[256,128]{1,0:T(8,128)(2,1)}, u32[]{:S(2)}) copy-start(bf16[256,128]{1,0:T(8,128)(2,1)} %up.1) | copy-start | bytes 196612
  2.3 21.2 %copy-start = (bf16[2048,512]{1,0:T(8,128)(2,1)S(1)}, bf16[2048,512]{1,0:T(8,128)(2,1)}, u32[]{:S(2)}) copy-start(bf16[2048,512]{1,0:T(8,128)(2,1)} %weights.1) | copy-start | bytes 6291460
  2.3 13.7 %collective-permute-start.3 = (bf16[1152,256]{1,0:T(8,128)(2,1)S(1)}, bf16[1152,256]{1,0:T(8,128)(2,1)S(1)}, u32[]{:S(2)}, u32[]{:S(2)}) collective-permute-start(bf16[1152,256]{1,0:T(8,128)(2,1)S(1)} %shard_map.64._.refs_2_), channel_id=1, source_target_pairs={{4,8},{5,9},{6,10},{7,11},{8,4},{9,5},{10,6},{11,7},{20,24},{21,25... | collective-permute-start | bytes 1769480 | tf_op jit(solution)/shard_map/ppermute | solution.py:98
  3.1 19.6 %collective-permute-start.4 = (bf16[1152,256]{1,0:T(8,128)(2,1)S(1)}, bf16[1152,256]{1,0:T(8,128)(2,1)S(1)}, u32[]{:S(2)}, u32[]{:S(2)}) collective-permute-start(bf16[1152,256]{1,0:T(8,128)(2,1)S(1)} %shard_map.64._.refs_2_), channel_id=1, source_target_pairs={{0,4},{1,5},{2,6},{3,7},{4,0},{5,1},{6,2},{7,3},{8,12},{9,13},{10,... | collective-permute-start | bytes 1769480 | tf_op jit(solution)/shard_map/ppermute | solution.py:98
  9.0 0.7 %copy-start.5 = (s32[384]{0:T(512)S(1)}, s32[384]{0:T(512)}, u32[]{:S(2)}) copy-start(s32[384]{0:T(512)} %slot.1) | copy-start | bytes 4612
  9.7 0.7 %copy-start.6 = (s32[384,1]{0,1:T(1,128)S(1)}, s32[384,1]{0,1:T(1,128)}, u32[]{:S(2)}) copy-start(s32[384,1]{0,1:T(1,128)} %param.10) | copy-start | bytes 4612
  10.5 19.5 %collective-permute-start = (bf16[400,1024]{1,0:T(8,128)(2,1)S(1)}, bf16[400,1024]{1,0:T(8,128)(2,1)S(1)}, u32[]{:S(2)}, u32[]{:S(2)}) collective-permute-start(bf16[400,1024]{1,0:T(8,128)(2,1)S(1)} %get-tuple-element.28.away), channel_id=1, source_target_pairs={{0,16},{1,17},{2,18},{3,19},{4,20},{5,21},{6,22},{7,23},{8,24},{9,... | collective-permute-start | bytes 2457608 | tf_op jit(solution)/shard_map/ppermute | solution.py:98
  12.8 20.2 %collective-permute-start.2 = (bf16[160,1024]{1,0:T(8,128)(2,1)S(1)}, bf16[160,1024]{1,0:T(8,128)(2,1)S(1)}, u32[]{:S(2)}, u32[]{:S(2)}) collective-permute-start(bf16[160,1024]{1,0:T(8,128)(2,1)S(1)} %get-tuple-element.30), channel_id=1, source_target_pairs={{0,20},{1,21},{2,22},{3,23},{12,24},{13,25},{14,26},{15,27},{16,4}... | collective-permute-start | bytes 983048 | tf_op jit(solution)/shard_map/ppermute | solution.py:98
  14.7 21.6 %collective-permute-start.1 = (bf16[160,1024]{1,0:T(8,128)(2,1)S(1)}, bf16[160,1024]{1,0:T(8,128)(2,1)S(1)}, u32[]{:S(2)}, u32[]{:S(2)}) collective-permute-start(bf16[160,1024]{1,0:T(8,128)(2,1)S(1)} %get-tuple-element.29), channel_id=1, source_target_pairs={{0,4},{1,5},{2,6},{3,7},{12,8},{13,9},{14,10},{15,11},{16,20},{17,... | collective-permute-start | bytes 983048 | tf_op jit(solution)/shard_map/ppermute | solution.py:98
  16.0 25.0 %collective-permute-start.6 = (bf16[1152,256]{1,0:T(8,128)(2,1)S(1)}, bf16[1152,256]{1,0:T(8,128)(2,1)S(1)}, u32[]{:S(2)}, u32[]{:S(2)}) collective-permute-start(bf16[1152,256]{1,0:T(8,128)(2,1)S(1)} %collective-permute-done.3.refs_3_), channel_id=1, source_target_pairs={{4,0},{5,1},{6,2},{7,3},{8,12},{9,13},{10,14},{11,15},{20,16},{21,... | collective-permute-start | bytes 1769480 | tf_op jit(solution)/shard_map/ppermute | solution.py:98
  22.8 18.2 %collective-permute-start.7 = (bf16[1152,256]{1,0:T(8,128)(2,1)S(1)}, bf16[1152,256]{1,0:T(8,128)(2,1)S(1)}, u32[]{:S(2)}, u32[]{:S(2)}) collective-permute-start(bf16[1152,256]{1,0:T(8,128)(2,1)S(1)} %collective-permute-done.4.refs_4_), channel_id=1, source_target_pairs={{4,8},{5,9},{6,10},{7,11},{8,4},{9,5},{10,6},{11,7},{20,24},{21,25... | collective-permute-start | bytes 1769480 | tf_op jit(solution)/shard_map/ppermute | solution.py:98
  24.5 8.5 %copy-start.4 = (bf16[256,128]{1,0:T(8,128)(2,1)S(1)}, bf16[256,128]{1,0:T(8,128)(2,1)}, u32[]{:S(2)}) copy-start(bf16[256,128]{1,0:T(8,128)(2,1)} %up.1) | copy-start | bytes 196612
  30.0 15.8 %collective-permute-start.9 = (f32[384,256]{1,0:T(8,128)S(1)}, f32[384,256]{1,0:T(8,128)S(1)}, u32[]{:S(2)}, u32[]{:S(2)}) collective-permute-start(f32[384,256]{1,0:T(8,128)S(1)} %get-tuple-element.40), channel_id=1, source_target_pairs={{0,2},{1,3},{2,0},{3,1},{4,6},{5,7},{6,4},{7,5},{8,10},{9,11},{10,... | collective-permute-start | bytes 1179656 | tf_op jit(solution)/shard_map/ppermute | solution.py:98
  33.0 8.0 %collective-permute-start.5 = (bf16[256,128]{1,0:T(8,128)(2,1)S(1)}, bf16[256,128]{1,0:T(8,128)(2,1)S(1)}, u32[]{:S(2)}, u32[]{:S(2)}) collective-permute-start(bf16[256,128]{1,0:T(8,128)(2,1)S(1)} %copy-done.4), channel_id=1, source_target_pairs={{0,12},{1,13},{2,14},{3,15},{12,0},{13,1},{14,2},{15,3},{16,28},{1... | collective-permute-start | bytes 196616 | tf_op jit(solution)/shard_map/ppermute | solution.py:98
  41.7 9.4 %collective-permute-start.8 = (f32[16,384]{1,0:T(8,128)S(1)}, f32[16,384]{1,0:T(8,128)S(1)}, u32[]{:S(2)}, u32[]{:S(2)}) collective-permute-start(f32[16,384]{1,0:T(8,128)S(1)} %get-tuple-element.37), channel_id=1, source_target_pairs={{0,16},{1,17},{2,18},{3,19},{4,20},{5,21},{6,22},{7,23},{8,24},{9,... | collective-permute-start | bytes 73736 | tf_op jit(solution)/shard_map/ppermute | solution.py:98
  43.3 5.6 %collective-permute-start.10 = (f32[16,144]{1,0:T(8,128)S(1)}, f32[16,144]{1,0:T(8,128)S(1)}, u32[]{:S(2)}, u32[]{:S(2)}) collective-permute-start(f32[16,144]{1,0:T(8,128)S(1)} %get-tuple-element.41), channel_id=1, source_target_pairs={{4,0},{5,1},{6,2},{7,3},{8,12},{9,13},{10,14},{11,15},{20,16},{21,... | collective-permute-start | bytes 27656 | tf_op jit(solution)/shard_map/ppermute | solution.py:98
  44.5 6.5 %collective-permute-start.11 = (f32[16,144]{1,0:T(8,128)S(1)}, f32[16,144]{1,0:T(8,128)S(1)}, u32[]{:S(2)}, u32[]{:S(2)}) collective-permute-start(f32[16,144]{1,0:T(8,128)S(1)} %get-tuple-element.42), channel_id=1, source_target_pairs={{4,16},{5,17},{6,18},{7,19},{8,28},{9,29},{10,30},{11,31},{20,0},{... | collective-permute-start | bytes 27656 | tf_op jit(solution)/shard_map/ppermute | solution.py:98
  51.2 5.2 %collective-permute-start.14 = (f32[384,128]{1,0:T(8,128)S(1)}, f32[384,128]{1,0:T(8,128)S(1)}, u32[]{:S(2)}, u32[]{:S(2)}) collective-permute-start(f32[384,128]{1,0:T(8,128)S(1)} %get-tuple-element.45), channel_id=1, source_target_pairs={{0,1},{1,0},{2,3},{3,2},{4,5},{5,4},{6,7},{7,6},{8,9},{9,8},{10,11... | collective-permute-start | bytes 589832 | tf_op jit(solution)/shard_map/ppermute | solution.py:98
  51.3 3.9 %collective-permute-start.12 = (f32[16,384]{1,0:T(8,128)S(1)}, f32[16,384]{1,0:T(8,128)S(1)}, u32[]{:S(2)}, u32[]{:S(2)}) collective-permute-start(f32[16,384]{1,0:T(8,128)S(1)} %get-tuple-element.43), channel_id=1, source_target_pairs={{0,2},{1,3},{2,0},{3,1},{4,6},{5,7},{6,4},{7,5},{8,10},{9,11},{10,... | collective-permute-start | bytes 73736 | tf_op jit(solution)/shard_map/ppermute | solution.py:98
  55.2 1.2 %collective-permute-start.13 = (f32[16,384]{1,0:T(8,128)S(1)}, f32[16,384]{1,0:T(8,128)S(1)}, u32[]{:S(2)}, u32[]{:S(2)}) collective-permute-start(f32[16,384]{1,0:T(8,128)S(1)} %add.3.near), channel_id=1, source_target_pairs={{0,1},{1,0},{2,3},{3,2},{4,5},{5,4},{6,7},{7,6},{8,9},{9,8},{10,11... | collective-permute-start | bytes 73736 | tf_op jit(solution)/shard_map/ppermute | solution.py:98

commit v12 on v11

--- a/solution.py
+++ b/solution.py
@@ -76,7 +76,7 @@
 
 AXES = ("groups", "adapter", "mp")
 ID_ROWS = 16
-HOP_URGENCY = 3 * 10**9
+HOP_URGENCY = (30 * 10**8, 0)
 OWNERS = 4
 LANES = 128
 NT = (((1,), (1,)), ((), ()))
@@ -127,14 +127,7 @@
     )(*operands)
 
 
-def copy_all(copies):
-    for copy in copies:
-        copy.start()
-    for copy in copies:
-        copy.wait()
-
-
-def pack_body(down, up, out, sems):
+def pack_body(down, up, owner, slot, out, ids, sems):
     g = lax.axis_index("groups")
     columns, keys = down.shape[1], up.shape[1]
     count = columns // keys
@@ -150,10 +143,16 @@
                 sems.at[k],
             )
         )
-    copy_all(copies)
-
-
-def split_body(tokens, owner, slot, _, own, away, sems):
+    for copy in copies:
+        copy.start()
+    row = lax.broadcasted_iota(jnp.int32, ids.shape, 0)
+    value = jnp.where(row == 0, owner[...], jnp.where(row == 1, slot[...].reshape(1, -1), 0))
+    ids[...] = value.astype(jnp.float32).astype(jnp.bfloat16)
+    for copy in copies:
+        copy.wait()
+
+
+def split_body(tokens, ids, own, away, sems):
     g = lax.axis_index("groups")
     rows, part = tokens.shape[0], own.shape[1]
     copies = []
@@ -162,11 +161,8 @@
         copies.append(pltpu.make_async_copy(taken, out.at[pl.ds(0, rows), :], sems.at[n]))
     for copy in copies:
         copy.start()
-    row = lax.broadcasted_iota(jnp.int32, (ID_ROWS, rows), 0)
-    ids = jnp.where(row == 0, owner[...], jnp.where(row == 1, slot[...].reshape(1, rows), 0))
-    ids = ids.astype(jnp.float32).astype(jnp.bfloat16)
     for out in (own, away):
-        out[rows:, :rows] = ids
+        out[rows:, :rows] = ids[...]
         out[rows:, rows:] = jnp.zeros((ID_ROWS, part - rows), jnp.bfloat16)
     for copy in copies:
         copy.wait()
@@ -269,12 +265,9 @@
         mask[n] = jnp.where(owner == (a ^ 2).astype(jnp.float32), right.astype(jnp.float32), 0.0)
 
 
-def hop_mask_body(capacity, *refs):
-    hops, out = refs[:-1], refs[-1]
-    adapter = adapters(capacity, out.shape[2])
-    for n, hop in enumerate(hops):
-        _, slot = id_columns(hop, capacity, capacity)
-        out[n] = (adapter == slot).astype(jnp.float32)
+def hop_mask_body(capacity, hop, _, out):
+    _, slot = id_columns(hop, capacity, capacity)
+    out[...] = (adapters(capacity, out.shape[1]) == slot).astype(jnp.float32)
 
 
 def last_body(part, rows, capacity, *refs):
@@ -282,15 +275,18 @@
     a = lax.axis_index("adapter")
     token_refs, rest = refs[:groups], refs[groups:]
     hops, rest = rest[:groups], rest[groups:]
-    hop_mask, folded, mask, outside, inside = rest[:5]
-    lows, hop_lows, last_up = rest[5 : 5 + groups], rest[5 + groups : -1], rest[-1]
+    hop_masks, rest = rest[:groups], rest[groups:]
+    folded, mask, outside, inside, low, hop_low, away, last_up = rest
     columns = inside.shape[1]
 
     def finish(block):
         for n, tokens in enumerate(token_refs):
             wide = jnp.dot(tokens[:rows, :], block[:part, :], preferred_element_type=jnp.float32)
             kept = fold(jnp.where(mask[n] > 0, wide, 0.0))
-            lows[n][...] = low_rank(folded[n] + kept)
+            if n:
+                away[:, :rows] = low_rank(folded[n] + kept)
+            else:
+                low[...] = low_rank(folded[n] + kept)
 
     middle = (a == 1) | (a == 2)
 
@@ -298,32 +294,38 @@
     def _():
         finish(inside)
         last_up[...] = stacked(inside[part:, :], last_up.shape[1])
-        for n, (hop, out) in enumerate(zip(hops, hop_lows)):
+        for n, (hop, hop_mask) in enumerate(zip(hops, hop_masks)):
             wide = jnp.dot(hop[:capacity, :], inside[:part, :], preferred_element_type=jnp.float32)
-            kept = fold(jnp.where(hop_mask[n] > 0, wide, 0.0))
+            kept = fold(jnp.where(hop_mask[...] > 0, wide, 0.0))
             rest_rows = -capacity % LANES
             kept = jnp.concatenate([kept, jnp.zeros((rest_rows, LANES), jnp.float32)], axis=0)
-            out[...] = low_rank(kept)[:, :capacity]
+            if n:
+                away[:, rows:] = low_rank(kept)[:, :capacity]
+            else:
+                hop_low[...] = low_rank(kept)[:, :capacity]
 
     @pl.when(jnp.logical_not(middle))
     def _():
         finish(outside)
         last_up[...] = stacked(outside[part:, :], last_up.shape[1])
-        for out in hop_lows:
-            out[...] = jnp.zeros(out.shape, jnp.float32)
-
-
-def merge_body(bit, low, near, places, kept, got, *refs):
-    hops, (out, keep, give, base) = refs[:-4], refs[-4:]
-    back = hops[0][...]
-    for hop in hops[1:]:
-        back = back + hop[...]
+        hop_low[...] = jnp.zeros(hop_low.shape, jnp.float32)
+        away[:, rows:] = jnp.zeros(hop_low.shape, jnp.float32)
+
+
+def near_body(low, hop_low, near, low_out, hop_out):
+    rows = low.shape[1]
+    low_out[...] = low[...] + near[:, :rows]
+    hop_out[...] = hop_low[...] + near[:, rows:]
+
+
+def merge_body(bit, low, places, kept, got, hop, out, keep, give, base):
+    back = hop[...]
     spread = jnp.zeros(low.shape, jnp.float32)
     for _ in range(3):
         piece = back.astype(jnp.bfloat16)
         back = back - piece.astype(jnp.float32)
         spread = spread + jnp.dot(piece, places[...], preferred_element_type=jnp.float32)
-    out[...] = low[...] + near[...] + spread
+    out[...] = low[...] + spread
     base[...] = kept[...] + got[...]
     halves(base, bit, keep, give)
 
@@ -373,12 +375,17 @@
     def wide(*dims):
         return jax.ShapeDtypeStruct(dims, jnp.float32)
 
-    own = kernel(
+    own, ids = kernel(
         pack_body,
-        narrow(part + columns // half, columns),
-        (stacked_down_weight, stacked_up_weight),
+        [narrow(part + columns // half, columns), narrow(ID_ROWS, rows)],
+        (
+            stacked_down_weight,
+            stacked_up_weight,
+            request_adapter_owner.reshape(1, rows),
+            request_adapter_slot,
+        ),
         0,
-        (pltpu.HBM, pltpu.HBM),
+        (pl.ANY, pl.ANY, None, None),
         [pltpu.SemaphoreType.DMA((1 + half,))],
     )
     mirror = exchange(own, 0, 0, MIDDLE)
@@ -387,9 +394,9 @@
     tok_own, tok_away = kernel(
         split_body,
         [narrow(rows + ID_ROWS, part)] * groups,
-        (tokens, request_adapter_owner.reshape(1, rows), request_adapter_slot, own),
+        (tokens, ids),
         0,
-        (pltpu.HBM, None, None, pl.ANY),
+        (pl.ANY, None),
         [pltpu.SemaphoreType.DMA((groups,))],
     )
     token_parts = [tok_own, exchange(tok_away, 1, 0, SAME)]
@@ -415,12 +422,16 @@
         light=True,
     )
     distant = exchange(after(stacked_up_weight, folded), 0, 0, ENDS)
-    hop_mask = kernel(
-        functools.partial(hop_mask_body, capacity),
-        wide(groups, capacity, columns),
-        (hops[0], after(hops[1], folded)),
-        HOP_URGENCY,
-    )
+    hop_masks, latest = [], folded
+    for hop, urgency in zip(hops, HOP_URGENCY):
+        latest = kernel(
+            functools.partial(hop_mask_body, capacity),
+            wide(capacity, columns),
+            (hop, latest),
+            urgency,
+            (None, pl.ANY),
+        )
+        hop_masks.append(latest)
     bits = (2, 1)
     keep, give = kernel(
         functools.partial(base_body, bits[0], rows),
@@ -430,24 +441,29 @@
         (None, None, None, pl.ANY),
         [pltpu.VMEM((rows, shares * keys), jnp.float32)],
     )
-    got = exchange(give, 0, bits[0], SAME)
-
-    low, low_away, back, back_away, last_up = kernel(
+    got = exchange(after(give, folded), 0, bits[0], SAME)
+
+    low, hop_low, away, last_up = kernel(
         functools.partial(last_body, part, rows, capacity),
-        [wide(ADAPTER_RANK, rows)] * groups
-        + [wide(ADAPTER_RANK, capacity)] * groups
-        + [narrow(columns, keys)],
-        (*token_parts, *hops, hop_mask, after(folded, distant), mask, outside, inside),
+        [
+            wide(ADAPTER_RANK, rows),
+            wide(ADAPTER_RANK, capacity),
+            wide(ADAPTER_RANK, rows + capacity),
+            narrow(columns, keys),
+        ],
+        (*token_parts, *hops, *hop_masks, after(folded, distant), mask, outside, inside),
         2 * groups * (rows + capacity) * part * columns,
     )
 
-    near = exchange(low_away, 1, 0, SAME)
-    back = exchange(back, 0, 0, OUTWARD)
-    back_away = exchange(back_away, 1, 0, OUTWARD)
+    near = exchange(away, 1, 0, SAME)
+    low, hop_low = kernel(
+        near_body, [wide(ADAPTER_RANK, rows), wide(ADAPTER_RANK, capacity)], (low, hop_low, near)
+    )
+    back = exchange(hop_low, 0, 0, OUTWARD)
     low, keep, give = kernel(
         functools.partial(merge_body, bits[1]),
         [wide(ADAPTER_RANK, rows)] + [wide(rows, bits[1] * keys)] * 2,
-        (low, near, places, keep, got, back, back_away),
+        (low, places, keep, got, back),
         scratch=[pltpu.VMEM((rows, bits[0] * keys), jnp.float32)],
     )
     got = exchange(give, 0, bits[1], SAME)

time: 58 us -> 61.2 us (1.055)
  starting transfers between devices: 23.2 us -> 27.7 us
  waiting for transfers between devices: 24.9 us -> 22 us
  local copies, waits for them, and re-layouts: 3.56 us -> 4.84 us
    ppermute x15 -> x14, starting transfers between devices: 23.2 us -> 27.7 us  [exchange(): return lax.ppermute(x, AXES, pairs)]
    ppermute x15 -> x14, waiting for transfers between devices: 24.9 us -> 22 us  [exchange(): return lax.ppermute(x, AXES, pairs)]
    unnamed x14, local copies, waits for them, and re-layouts: 3.56 us -> 4.84 us
    pallas_call x9 -> x11, Pallas kernels: 5.86 us -> 6.15 us  [kernel(): pl.pallas_call(body, out_shape=outs, in_specs=specs or [inner] * len(oper...]
  transfers between devices with their start and end apart: 15 -> 14, of which waited for: 7 -> 6; matrix products, arithmetic and copies ran while one was open for 0% -> 0% of each run, Pallas kernels for 8% -> 8%
where the time goes in v12:
time: 61.2 us; the launch traced here: 60.8 us
  starting transfers between devices  27.7 us (45%)
  waiting for transfers between devices  22 us (36%)
  Pallas kernels  6.15 us (10%)
  local copies, waits for them, and re-layouts  4.84 us (8%)
    ppermute x14, starting transfers between devices, exchange(): return lax.ppermute(x, AXES, pairs)  27.7 us
    ppermute x14, waiting for transfers between devices, exchange(): return lax.ppermute(x, AXES, pairs)  22 us
    pallas_call x11, Pallas kernels, kernel(): pl.pallas_call(body, out_shape=outs, in_specs=specs or [inner] * len(oper...  6.15 us
    unnamed x14, local copies, waits for them, and re-layouts  4.84 us
  transfers between devices with their start and end apart: 14, of which 6 were waited for; matrix products, arithmetic and copies ran while one was open for 0% of the time, Pallas kernels for 8%

profile of v12, /device:TPU:0, one launch (start us, length us, event | category | flops | bytes accessed | tf_op | source)
XLA Modules:
  0.0 60.8 jit_solution(259916105973998464)
XLA Ops:
  0.0 0.0 copy-start.2
  0.0 1.2 %copy-done.2 = bf16[2048,256]{1,0:T(8,128)(2,1)S(1)} copy-done((bf16[2048,256]{1,0:T(8,128)(2,1)S(1)}, bf16[2048,256]{1,0:T(8,128)(2,1)}, u32[]{:S(2)}) %copy-start.2) | copy-done | bytes 1048600
  1.2 0.0 copy-start.3
  1.2 0.8 %copy-done.3 = bf16[256,128]{1,0:T(8,128)(2,1)S(1)} copy-done((bf16[256,128]{1,0:T(8,128)(2,1)S(1)}, bf16[256,128]{1,0:T(8,128)(2,1)}, u32[]{:S(2)}) %copy-start.3) | copy-done | bytes 65560
  2.1 0.7 %copy-done.5 = s32[384]{0:T(512)S(1)} copy-done((s32[384]{0:T(512)S(1)}, s32[384]{0:T(512)}, u32[]{:S(2)}) %copy-start.5) | copy-done | bytes 1560
  2.8 0.7 %copy-done.6 = s32[384,1]{0,1:T(1,128)S(1)} copy-done((s32[384,1]{0,1:T(1,128)S(1)}, s32[384,1]{0,1:T(1,128)}, u32[]{:S(2)}) %copy-start.6) | copy-done | bytes 1560
  3.4 0.1 shard_map.64
  3.5 0.8 %collective-permute-start.3 = (bf16[1152,256]{1,0:T(8,128)(2,1)S(1)}, bf16[1152,256]{1,0:T(8,128)(2,1)S(1)}, u32[]{:S(2)}, u32[]{:S(2)}) collective-permute-start(bf16[1152,256]{1,0:T(8,128)(2,1)S(1)} %get-tuple-element.35.refs_2_), channel_id=1, source_target_pairs={{4,8},{5,9},{6,10},{7,11},{8,4},{9,5},{10,6},{11,7},{20,24},{21,25... | collective-permute-start | bytes 1769480 | tf_op jit(solution)/shard_map/ppermute | solution.py:98
  4.4 5.9 %collective-permute-start.4 = (bf16[1152,256]{1,0:T(8,128)(2,1)S(1)}, bf16[1152,256]{1,0:T(8,128)(2,1)S(1)}, u32[]{:S(2)}, u32[]{:S(2)}) collective-permute-start(bf16[1152,256]{1,0:T(8,128)(2,1)S(1)} %get-tuple-element.35.refs_2_), channel_id=1, source_target_pairs={{0,4},{1,5},{2,6},{3,7},{4,0},{5,1},{6,2},{7,3},{8,12},{9,13},{10,... | collective-permute-start | bytes 1769480 | tf_op jit(solution)/shard_map/ppermute | solution.py:98
  10.2 1.4 %copy-done.1 = bf16[384,2048]{1,0:T(8,128)(2,1)S(1)} copy-done((bf16[384,2048]{1,0:T(8,128)(2,1)S(1)}, bf16[384,2048]{1,0:T(8,128)(2,1)}, u32[]{:S(2)}) %copy-start.1) | copy-done | bytes 1572888
  11.6 0.2 shard_map.65
  11.8 1.6 %collective-permute-start = (bf16[400,1024]{1,0:T(8,128)(2,1)S(1)}, bf16[400,1024]{1,0:T(8,128)(2,1)S(1)}, u32[]{:S(2)}, u32[]{:S(2)}) collective-permute-start(bf16[400,1024]{1,0:T(8,128)(2,1)S(1)} %get-tuple-element.32.away), channel_id=1, source_target_pairs={{0,16},{1,17},{2,18},{3,19},{4,20},{5,21},{6,22},{7,23},{8,24},{9,... | collective-permute-start | bytes 2457608 | tf_op jit(solution)/shard_map/ppermute | solution.py:98
  13.4 0.7 %shard_map.66 = (bf16[160,1024]{1,0:T(8,128)(2,1)S(1)}, bf16[160,1024]{1,0:T(8,128)(2,1)S(1)}, bf16[144,384]{1,0:T(8,128)(2,1)S(1)}) custom-call(bf16[400,1024]{1,0:T(8,128)(2,1)S(1)} %get-tuple-element.31.own.refs_0_, bf16[400,1024]{1,0:T(8,128)(2,1)S(1)} %get-tuple-element.32.away), custom_call_target="tpu_custom_call" | custom-call | flops 226492416 | bytes 2404352 | tf_op jit(solution)/shard_map/pallas_call | solution.py:117
  14.1 1.9 %collective-permute-start.1 = (bf16[160,1024]{1,0:T(8,128)(2,1)S(1)}, bf16[160,1024]{1,0:T(8,128)(2,1)S(1)}, u32[]{:S(2)}, u32[]{:S(2)}) collective-permute-start(bf16[160,1024]{1,0:T(8,128)(2,1)S(1)} %get-tuple-element.33), channel_id=1, source_target_pairs={{0,4},{1,5},{2,6},{3,7},{12,8},{13,9},{14,10},{15,11},{16,20},{17,... | collective-permute-start | bytes 983048 | tf_op jit(solution)/shard_map/ppermute | solution.py:98
  16.0 0.0 collective-permute-done.3.refs_3_
  16.0 1.3 %collective-permute-start.6 = (bf16[1152,256]{1,0:T(8,128)(2,1)S(1)}, bf16[1152,256]{1,0:T(8,128)(2,1)S(1)}, u32[]{:S(2)}, u32[]{:S(2)}) collective-permute-start(bf16[1152,256]{1,0:T(8,128)(2,1)S(1)} %collective-permute-done.3.refs_3_), channel_id=1, source_target_pairs={{4,0},{5,1},{6,2},{7,3},{8,12},{9,13},{10,14},{11,15},{20,16},{21,... | collective-permute-start | bytes 1769480 | tf_op jit(solution)/shard_map/ppermute | solution.py:98
  17.3 6.7 %collective-permute-done.4.refs_4_ = bf16[1152,256]{1,0:T(8,128)(2,1)S(1)} collective-permute-done((bf16[1152,256]{1,0:T(8,128)(2,1)S(1)}, bf16[1152,256]{1,0:T(8,128)(2,1)S(1)}, u32[]{:S(2)}, u32[]{:S(2)}) %collective-permute-start.4) | collective-permute-done | bytes 589856 | tf_op jit(solution)/shard_map/ppermute | solution.py:98
  24.0 0.7 %collective-permute-start.7 = (bf16[1152,256]{1,0:T(8,128)(2,1)S(1)}, bf16[1152,256]{1,0:T(8,128)(2,1)S(1)}, u32[]{:S(2)}, u32[]{:S(2)}) collective-permute-start(bf16[1152,256]{1,0:T(8,128)(2,1)S(1)} %collective-permute-done.4.refs_4_), channel_id=1, source_target_pairs={{4,8},{5,9},{6,10},{7,11},{8,4},{9,5},{10,6},{11,7},{20,24},{21,25... | collective-permute-start | bytes 1769480 | tf_op jit(solution)/shard_map/ppermute | solution.py:98
  24.7 7.0 %collective-permute-start.2 = (bf16[160,1024]{1,0:T(8,128)(2,1)S(1)}, bf16[160,1024]{1,0:T(8,128)(2,1)S(1)}, u32[]{:S(2)}, u32[]{:S(2)}) collective-permute-start(bf16[160,1024]{1,0:T(8,128)(2,1)S(1)} %get-tuple-element.34), channel_id=1, source_target_pairs={{0,20},{1,21},{2,22},{3,23},{12,24},{13,25},{14,26},{15,27},{16,4}... | collective-permute-start | bytes 983048 | tf_op jit(solution)/shard_map/ppermute | solution.py:98
  31.7 0.0 copy-done
  31.7 1.1 %shard_map.72 = (f32[384,256]{1,0:T(8,128)S(1)}, f32[384,256]{1,0:T(8,128)S(1)}) custom-call(bf16[400,1024]{1,0:T(8,128)(2,1)S(1)} %get-tuple-element.31.own.refs_0_, bf16[400,1024]{1,0:T(8,128)(2,1)S(1)} %get-tuple-element.32.away, bf16[2048,512]{1,0:T(8,128)(2,1)S(1)} %copy-done, bf16[144,384]{1,0:T(8,128)(2,1)S(1)} %get-tuple-element.44._.places), custom_call_target="tpu_custom_call" | custom-call | flops 805306368 | bytes 4632576 | tf_op jit(solution)/shard_map/pallas_call | solution.py:117
  32.8 0.0 copy-start.4
  32.8 0.0 collective-permute-done.refs_1_
  32.8 1.5 %shard_map.67 = (f32[2,384,128]{2,1,0:T(8,128)S(1)}, f32[2,384,256]{2,1,0:T(8,128)S(1)}, f32[384,1]{1,0:T(8,128)S(1)}, bf16[3,256,128]{2,1,0:T(8,128)(2,1)S(1)}) custom-call(bf16[400,1024]{1,0:T(8,128)(2,1)S(1)} %get-tuple-element.31.own.refs_0_, bf16[400,1024]{1,0:T(8,128)(2,1)S(1)} %collective-permute-done.refs_1_, ...), custom_call_target="tpu_custom_call" | custom-call | tf_op jit(solution)/shard_map/pallas_call | solution.py:117
  34.4 1.6 %collective-permute-start.9 = (f32[384,256]{1,0:T(8,128)S(1)}, f32[384,256]{1,0:T(8,128)S(1)}, u32[]{:S(2)}, u32[]{:S(2)}) collective-permute-start(f32[384,256]{1,0:T(8,128)S(1)} %get-tuple-element.47), channel_id=1, source_target_pairs={{0,2},{1,3},{2,0},{3,1},{4,6},{5,7},{6,4},{7,5},{8,10},{9,11},{10,... | collective-permute-start | bytes 1179656 | tf_op jit(solution)/shard_map/ppermute | solution.py:98
  35.9 0.0 collective-permute-done.1.hop.refs_2_
  35.9 0.0 copy-done.4
  35.9 4.4 %collective-permute-start.5 = (bf16[256,128]{1,0:T(8,128)(2,1)S(1)}, bf16[256,128]{1,0:T(8,128)(2,1)S(1)}, u32[]{:S(2)}, u32[]{:S(2)}) collective-permute-start(bf16[256,128]{1,0:T(8,128)(2,1)S(1)} %copy-done.4), channel_id=1, source_target_pairs={{0,12},{1,13},{2,14},{3,15},{12,0},{13,1},{14,2},{15,3},{16,28},{1... | collective-permute-start | bytes 196616 | tf_op jit(solution)/shard_map/ppermute | solution.py:98
  40.3 0.3 shard_map.68._.refs_4_
  40.6 0.0 collective-permute-done.2.hop.refs_3_
  40.6 0.3 shard_map.69.refs_5_
  40.9 3.0 %collective-permute-done.5.distant = bf16[256,128]{1,0:T(8,128)(2,1)S(1)} collective-permute-done((bf16[256,128]{1,0:T(8,128)(2,1)S(1)}, bf16[256,128]{1,0:T(8,128)(2,1)S(1)}, u32[]{:S(2)}, u32[]{:S(2)}) %collective-permute-start.5) | collective-permute-done | bytes 65568 | tf_op jit(solution)/shard_map/ppermute | solution.py:98
  43.9 0.0 collective-permute-done.6.refs_8_
  43.9 0.0 collective-permute-done.7.refs_9_
  43.9 0.7 %shard_map.70 = (f32[16,384]{1,0:T(8,128)S(1)}, f32[16,144]{1,0:T(8,128)S(1)}, f32[16,528]{1,0:T(8,128)S(1)}, bf16[256,128]{1,0:T(8,128)(2,1)S(1)}) custom-call(bf16[400,1024]{1,0:T(8,128)(2,1)S(1)} %get-tuple-element.31.own.refs_0_, bf16[400,1024]{1,0:T(8,128)(2,1)S(1)} %collective-permute-done.refs_1_, ...), custom_call_target="tpu_custom_call" | custom-call | flops 553648128 | bytes 5081088 | tf_op jit(solution)/shard_map/pallas_call | solution.py:117
  44.6 0.6 collective-permute-start.8
  45.1 3.5 %collective-permute-done.8.near = f32[16,528]{1,0:T(8,128)S(1)} collective-permute-done((f32[16,528]{1,0:T(8,128)S(1)}, f32[16,528]{1,0:T(8,128)S(1)}, u32[]{:S(2)}, u32[]{:S(2)}) %collective-permute-start.8) | collective-permute-done | bytes 33824 | tf_op jit(solution)/shard_map/ppermute | solution.py:98
  48.6 1.3 %collective-permute-start.10 = (f32[16,144]{1,0:T(8,128)S(1)}, f32[16,144]{1,0:T(8,128)S(1)}, u32[]{:S(2)}, u32[]{:S(2)}) collective-permute-start(f32[16,144]{1,0:T(8,128)S(1)} %get-tuple-element.48), channel_id=1, source_target_pairs={{4,0},{5,1},{6,2},{7,3},{8,12},{9,13},{10,14},{11,15},{20,16},{21,... | collective-permute-start | bytes 27656 | tf_op jit(solution)/shard_map/ppermute | solution.py:98
  49.9 0.0 collective-permute-done.9.got
  49.9 4.3 %collective-permute-done.10.hop = f32[16,144]{1,0:T(8,128)S(1)} collective-permute-done((f32[16,144]{1,0:T(8,128)S(1)}, f32[16,144]{1,0:T(8,128)S(1)}, u32[]{:S(2)}, u32[]{:S(2)}) %collective-permute-start.10) | collective-permute-done | bytes 9248 | tf_op jit(solution)/shard_map/ppermute | solution.py:98
  54.3 0.2 shard_map.73
  54.4 0.1 collective-permute-start.13
  54.5 0.6 collective-permute-start.11
  55.1 3.3 %collective-permute-done.11 = f32[16,384]{1,0:T(8,128)S(1)} collective-permute-done((f32[16,384]{1,0:T(8,128)S(1)}, f32[16,384]{1,0:T(8,128)S(1)}, u32[]{:S(2)}, u32[]{:S(2)}) %collective-permute-start.11) | collective-permute-done | bytes 24608 | tf_op jit(solution)/shard_map/ppermute | solution.py:98
  58.4 0.0 collective-permute-start.12
  58.4 1.2 %collective-permute-done.12.far = f32[16,384]{1,0:T(8,128)S(1)} collective-permute-done((f32[16,384]{1,0:T(8,128)S(1)}, f32[16,384]{1,0:T(8,128)S(1)}, u32[]{:S(2)}, u32[]{:S(2)}) %collective-permute-start.12) | collective-permute-done | bytes 24608 | tf_op jit(solution)/shard_map/ppermute | solution.py:98
  59.6 0.0 collective-permute-done.13.got
  59.6 1.3 %shard_map.74 = bf16[384,128]{1,0:T(8,128)(2,1)} custom-call(f32[16,384]{1,0:T(8,128)S(1)} %add.3.near, f32[16,384]{1,0:T(8,128)S(1)} %collective-permute-done.12.far, f32[384,128]{1,0:T(8,128)S(1)} %get-tuple-element.50.keep, f32[384,128]{1,0:T(8,128)S(1)} %collective-permute-done.13.got, f32[384,1]{1,0:T(8,128)S(1)} %get-tuple-element.52.numbers, ...), custom_call_target="tpu_custom_call" | custom-call | bytes 869888 | tf_op jit(solution)/shard_map/pallas_call | solution.py:117
  (6 shorter events, 0.0 us)
Async XLA Ops:
  0.0 1.2 %copy-start.2 = (bf16[2048,256]{1,0:T(8,128)(2,1)S(1)}, bf16[2048,256]{1,0:T(8,128)(2,1)}, u32[]{:S(2)}) copy-start(bf16[2048,256]{1,0:T(8,128)(2,1)} %down.1) | copy-start | bytes 3145732
  1.2 0.8 %copy-start.3 = (bf16[256,128]{1,0:T(8,128)(2,1)S(1)}, bf16[256,128]{1,0:T(8,128)(2,1)}, u32[]{:S(2)}) copy-start(bf16[256,128]{1,0:T(8,128)(2,1)} %up.1) | copy-start | bytes 196612
  2.1 0.7 %copy-start.5 = (s32[384]{0:T(512)S(1)}, s32[384]{0:T(512)}, u32[]{:S(2)}) copy-start(s32[384]{0:T(512)} %slot.1) | copy-start | bytes 4612
  2.7 0.7 %copy-start.6 = (s32[384,1]{0,1:T(1,128)S(1)}, s32[384,1]{0,1:T(1,128)}, u32[]{:S(2)}) copy-start(s32[384,1]{0,1:T(1,128)} %param.10) | copy-start | bytes 4612
  3.4 28.3 %copy-start = (bf16[2048,512]{1,0:T(8,128)(2,1)S(1)}, bf16[2048,512]{1,0:T(8,128)(2,1)}, u32[]{:S(2)}) copy-start(bf16[2048,512]{1,0:T(8,128)(2,1)} %weights.1) | copy-start | bytes 6291460
  3.5 12.5 %collective-permute-start.3 = (bf16[1152,256]{1,0:T(8,128)(2,1)S(1)}, bf16[1152,256]{1,0:T(8,128)(2,1)S(1)}, u32[]{:S(2)}, u32[]{:S(2)}) collective-permute-start(bf16[1152,256]{1,0:T(8,128)(2,1)S(1)} %get-tuple-element.35.refs_2_), channel_id=1, source_target_pairs={{4,8},{5,9},{6,10},{7,11},{8,4},{9,5},{10,6},{11,7},{20,24},{21,25... | collective-permute-start | bytes 1769480 | tf_op jit(solution)/shard_map/ppermute | solution.py:98
  4.4 19.6 %collective-permute-start.4 = (bf16[1152,256]{1,0:T(8,128)(2,1)S(1)}, bf16[1152,256]{1,0:T(8,128)(2,1)S(1)}, u32[]{:S(2)}, u32[]{:S(2)}) collective-permute-start(bf16[1152,256]{1,0:T(8,128)(2,1)S(1)} %get-tuple-element.35.refs_2_), channel_id=1, source_target_pairs={{0,4},{1,5},{2,6},{3,7},{4,0},{5,1},{6,2},{7,3},{8,12},{9,13},{10,... | collective-permute-start | bytes 1769480 | tf_op jit(solution)/shard_map/ppermute | solution.py:98
  10.2 1.4 %copy-start.1 = (bf16[384,2048]{1,0:T(8,128)(2,1)S(1)}, bf16[384,2048]{1,0:T(8,128)(2,1)}, u32[]{:S(2)}) copy-start(bf16[384,2048]{1,0:T(8,128)(2,1)} %tokens.1) | copy-start | bytes 4718596
  11.8 21.0 %collective-permute-start = (bf16[400,1024]{1,0:T(8,128)(2,1)S(1)}, bf16[400,1024]{1,0:T(8,128)(2,1)S(1)}, u32[]{:S(2)}, u32[]{:S(2)}) collective-permute-start(bf16[400,1024]{1,0:T(8,128)(2,1)S(1)} %get-tuple-element.32.away), channel_id=1, source_target_pairs={{0,16},{1,17},{2,18},{3,19},{4,20},{5,21},{6,22},{7,23},{8,24},{9,... | collective-permute-start | bytes 2457608 | tf_op jit(solution)/shard_map/ppermute | solution.py:98
  14.1 21.8 %collective-permute-start.1 = (bf16[160,1024]{1,0:T(8,128)(2,1)S(1)}, bf16[160,1024]{1,0:T(8,128)(2,1)S(1)}, u32[]{:S(2)}, u32[]{:S(2)}) collective-permute-start(bf16[160,1024]{1,0:T(8,128)(2,1)S(1)} %get-tuple-element.33), channel_id=1, source_target_pairs={{0,4},{1,5},{2,6},{3,7},{12,8},{13,9},{14,10},{15,11},{16,20},{17,... | collective-permute-start | bytes 983048 | tf_op jit(solution)/shard_map/ppermute | solution.py:98
  16.0 27.8 %collective-permute-start.6 = (bf16[1152,256]{1,0:T(8,128)(2,1)S(1)}, bf16[1152,256]{1,0:T(8,128)(2,1)S(1)}, u32[]{:S(2)}, u32[]{:S(2)}) collective-permute-start(bf16[1152,256]{1,0:T(8,128)(2,1)S(1)} %collective-permute-done.3.refs_3_), channel_id=1, source_target_pairs={{4,0},{5,1},{6,2},{7,3},{8,12},{9,13},{10,14},{11,15},{20,16},{21,... | collective-permute-start | bytes 1769480 | tf_op jit(solution)/shard_map/ppermute | solution.py:98
  24.0 19.9 %collective-permute-start.7 = (bf16[1152,256]{1,0:T(8,128)(2,1)S(1)}, bf16[1152,256]{1,0:T(8,128)(2,1)S(1)}, u32[]{:S(2)}, u32[]{:S(2)}) collective-permute-start(bf16[1152,256]{1,0:T(8,128)(2,1)S(1)} %collective-permute-done.4.refs_4_), channel_id=1, source_target_pairs={{4,8},{5,9},{6,10},{7,11},{8,4},{9,5},{10,6},{11,7},{20,24},{21,25... | collective-permute-start | bytes 1769480 | tf_op jit(solution)/shard_map/ppermute | solution.py:98
  24.7 15.9 %collective-permute-start.2 = (bf16[160,1024]{1,0:T(8,128)(2,1)S(1)}, bf16[160,1024]{1,0:T(8,128)(2,1)S(1)}, u32[]{:S(2)}, u32[]{:S(2)}) collective-permute-start(bf16[160,1024]{1,0:T(8,128)(2,1)S(1)} %get-tuple-element.34), channel_id=1, source_target_pairs={{0,20},{1,21},{2,22},{3,23},{12,24},{13,25},{14,26},{15,27},{16,4}... | collective-permute-start | bytes 983048 | tf_op jit(solution)/shard_map/ppermute | solution.py:98
  32.8 3.1 %copy-start.4 = (bf16[256,128]{1,0:T(8,128)(2,1)S(1)}, bf16[256,128]{1,0:T(8,128)(2,1)}, u32[]{:S(2)}) copy-start(bf16[256,128]{1,0:T(8,128)(2,1)} %up.1) | copy-start | bytes 196612
  34.4 15.6 %collective-permute-start.9 = (f32[384,256]{1,0:T(8,128)S(1)}, f32[384,256]{1,0:T(8,128)S(1)}, u32[]{:S(2)}, u32[]{:S(2)}) collective-permute-start(f32[384,256]{1,0:T(8,128)S(1)} %get-tuple-element.47), channel_id=1, source_target_pairs={{0,2},{1,3},{2,0},{3,1},{4,6},{5,7},{6,4},{7,5},{8,10},{9,11},{10,... | collective-permute-start | bytes 1179656 | tf_op jit(solution)/shard_map/ppermute | solution.py:98
  35.9 7.9 %collective-permute-start.5 = (bf16[256,128]{1,0:T(8,128)(2,1)S(1)}, bf16[256,128]{1,0:T(8,128)(2,1)S(1)}, u32[]{:S(2)}, u32[]{:S(2)}) collective-permute-start(bf16[256,128]{1,0:T(8,128)(2,1)S(1)} %copy-done.4), channel_id=1, source_target_pairs={{0,12},{1,13},{2,14},{3,15},{12,0},{13,1},{14,2},{15,3},{16,28},{1... | collective-permute-start | bytes 196616 | tf_op jit(solution)/shard_map/ppermute | solution.py:98
  44.6 4.1 %collective-permute-start.8 = (f32[16,528]{1,0:T(8,128)S(1)}, f32[16,528]{1,0:T(8,128)S(1)}, u32[]{:S(2)}, u32[]{:S(2)}) collective-permute-start(f32[16,528]{1,0:T(8,128)S(1)} %get-tuple-element.42), channel_id=1, source_target_pairs={{0,16},{1,17},{2,18},{3,19},{4,20},{5,21},{6,22},{7,23},{8,24},{9,... | collective-permute-start | bytes 101384 | tf_op jit(solution)/shard_map/ppermute | solution.py:98
  48.6 5.6 %collective-permute-start.10 = (f32[16,144]{1,0:T(8,128)S(1)}, f32[16,144]{1,0:T(8,128)S(1)}, u32[]{:S(2)}, u32[]{:S(2)}) collective-permute-start(f32[16,144]{1,0:T(8,128)S(1)} %get-tuple-element.48), channel_id=1, source_target_pairs={{4,0},{5,1},{6,2},{7,3},{8,12},{9,13},{10,14},{11,15},{20,16},{21,... | collective-permute-start | bytes 27656 | tf_op jit(solution)/shard_map/ppermute | solution.py:98
  54.4 5.2 %collective-permute-start.13 = (f32[384,128]{1,0:T(8,128)S(1)}, f32[384,128]{1,0:T(8,128)S(1)}, u32[]{:S(2)}, u32[]{:S(2)}) collective-permute-start(f32[384,128]{1,0:T(8,128)S(1)} %get-tuple-element.51), channel_id=1, source_target_pairs={{0,1},{1,0},{2,3},{3,2},{4,5},{5,4},{6,7},{7,6},{8,9},{9,8},{10,11... | collective-permute-start | bytes 589832 | tf_op jit(solution)/shard_map/ppermute | solution.py:98
  54.5 3.9 %collective-permute-start.11 = (f32[16,384]{1,0:T(8,128)S(1)}, f32[16,384]{1,0:T(8,128)S(1)}, u32[]{:S(2)}, u32[]{:S(2)}) collective-permute-start(f32[16,384]{1,0:T(8,128)S(1)} %get-tuple-element.49), channel_id=1, source_target_pairs={{0,2},{1,3},{2,0},{3,1},{4,6},{5,7},{6,4},{7,5},{8,10},{9,11},{10,... | collective-permute-start | bytes 73736 | tf_op jit(solution)/shard_map/ppermute | solution.py:98
  58.4 1.2 %collective-permute-start.12 = (f32[16,384]{1,0:T(8,128)S(1)}, f32[16,384]{1,0:T(8,128)S(1)}, u32[]{:S(2)}, u32[]{:S(2)}) collective-permute-start(f32[16,384]{1,0:T(8,128)S(1)} %add.3.near), channel_id=1, source_target_pairs={{0,1},{1,0},{2,3},{3,2},{4,5},{5,4},{6,7},{7,6},{8,9},{9,8},{10,11... | collective-permute-start | bytes 73736 | tf_op jit(solution)/shard_map/ppermute | solution.py:98

commit v13 on v12

--- a/solution.py
+++ b/solution.py
@@ -110,6 +110,10 @@
     return lax.optimization_barrier((x, *others))[0]
 
 
+def in_hbm(x):
+    return pltpu.with_memory_space_constraint(x, pltpu.HBM)
+
+
 def kernel(body, outs, operands, flops=0, spaces=None, scratch=(), light=False):
     inner = pl.BlockSpec(memory_space=pltpu.VMEM)
     specs = [inner if s is None else pl.BlockSpec(memory_space=s) for s in spaces or ()]
@@ -127,7 +131,7 @@
     )(*operands)
 
 
-def pack_body(down, up, owner, slot, out, ids, sems):
+def pack_body(down, up, out, sems):
     g = lax.axis_index("groups")
     columns, keys = down.shape[1], up.shape[1]
     count = columns // keys
@@ -145,14 +149,11 @@
         )
     for copy in copies:
         copy.start()
-    row = lax.broadcasted_iota(jnp.int32, ids.shape, 0)
-    value = jnp.where(row == 0, owner[...], jnp.where(row == 1, slot[...].reshape(1, -1), 0))
-    ids[...] = value.astype(jnp.float32).astype(jnp.bfloat16)
     for copy in copies:
         copy.wait()
 
 
-def split_body(tokens, ids, own, away, sems):
+def split_body(tokens, owner, slot, _, own, away, sems):
     g = lax.axis_index("groups")
     rows, part = tokens.shape[0], own.shape[1]
     copies = []
@@ -161,8 +162,11 @@
         copies.append(pltpu.make_async_copy(taken, out.at[pl.ds(0, rows), :], sems.at[n]))
     for copy in copies:
         copy.start()
+    row = lax.broadcasted_iota(jnp.int32, (ID_ROWS, rows), 0)
+    ids = jnp.where(row == 0, owner[...], jnp.where(row == 1, slot[...].reshape(1, rows), 0))
+    ids = ids.astype(jnp.float32).astype(jnp.bfloat16)
     for out in (own, away):
-        out[rows:, :rows] = ids[...]
+        out[rows:, :rows] = ids
         out[rows:, rows:] = jnp.zeros((ID_ROWS, part - rows), jnp.bfloat16)
     for copy in copies:
         copy.wait()
@@ -375,17 +379,12 @@
     def wide(*dims):
         return jax.ShapeDtypeStruct(dims, jnp.float32)
 
-    own, ids = kernel(
+    own = kernel(
         pack_body,
-        [narrow(part + columns // half, columns), narrow(ID_ROWS, rows)],
-        (
-            stacked_down_weight,
-            stacked_up_weight,
-            request_adapter_owner.reshape(1, rows),
-            request_adapter_slot,
-        ),
+        narrow(part + columns // half, columns),
+        (in_hbm(stacked_down_weight), in_hbm(stacked_up_weight)),
         0,
-        (pl.ANY, pl.ANY, None, None),
+        (pl.ANY, pl.ANY),
         [pltpu.SemaphoreType.DMA((1 + half,))],
     )
     mirror = exchange(own, 0, 0, MIDDLE)
@@ -394,9 +393,9 @@
     tok_own, tok_away = kernel(
         split_body,
         [narrow(rows + ID_ROWS, part)] * groups,
-        (tokens, ids),
+        (in_hbm(tokens), request_adapter_owner.reshape(1, rows), request_adapter_slot, own),
         0,
-        (pl.ANY, None),
+        (pl.ANY, None, None, pl.ANY),
         [pltpu.SemaphoreType.DMA((groups,))],
     )
     token_parts = [tok_own, exchange(tok_away, 1, 0, SAME)]
@@ -411,7 +410,7 @@
     inside = exchange(beside, 0, 0, MIDDLE)
     outside = exchange(mirror, 0, 0, OUTWARD)
     hops = [
-        exchange(hop_own, 0, 0, INWARD),
+        exchange(after(hop_own, beside), 0, 0, INWARD),
         exchange(hop_away, 1, 0, INWARD),
     ]
 
@@ -421,7 +420,6 @@
         (*token_parts, own, mirror, beside),
         light=True,
     )
-    distant = exchange(after(stacked_up_weight, folded), 0, 0, ENDS)
     hop_masks, latest = [], folded
     for hop, urgency in zip(hops, HOP_URGENCY):
         latest = kernel(
@@ -451,11 +449,12 @@
             wide(ADAPTER_RANK, rows + capacity),
             narrow(columns, keys),
         ],
-        (*token_parts, *hops, *hop_masks, after(folded, distant), mask, outside, inside),
+        (*token_parts, *hops, *hop_masks, folded, mask, outside, inside),
         2 * groups * (rows + capacity) * part * columns,
     )
 
     near = exchange(away, 1, 0, SAME)
+    distant = exchange(after(stacked_up_weight, folded), 0, 0, ENDS)
     low, hop_low = kernel(
         near_body, [wide(ADAPTER_RANK, rows), wide(ADAPTER_RANK, capacity)], (low, hop_low, near)
     )
@@ -463,7 +462,7 @@
     low, keep, give = kernel(
         functools.partial(merge_body, bits[1]),
         [wide(ADAPTER_RANK, rows)] + [wide(rows, bits[1] * keys)] * 2,
-        (low, places, keep, got, back),
+        (after(low, distant), places, keep, got, back),
         scratch=[pltpu.VMEM((rows, bits[0] * keys), jnp.float32)],
     )
     got = exchange(give, 0, bits[1], SAME)

time: 61.2 us -> 57.7 us (0.943)
  local copies, waits for them, and re-layouts: 4.84 us -> 1.37 us
  Pallas kernels: 6.15 us -> 8.35 us
  starting transfers between devices: 27.7 us -> 26 us
    unnamed x14 -> x8, local copies, waits for them, and re-layouts: 4.84 us -> 1.37 us
    pallas_call x11, Pallas kernels: 6.15 us -> 8.35 us  [kernel(): pl.pallas_call(body, out_shape=outs, in_specs=specs or [inner] * len(oper...]
    ppermute x14, starting transfers between devices: 27.7 us -> 26 us  [exchange(): return lax.ppermute(x, AXES, pairs)]
  transfers between devices with their start and end apart: 14 -> 14, of which waited for: 6 -> 6; matrix products, arithmetic and copies ran while one was open for 0% -> 0% of each run, Pallas kernels for 8% -> 10%
where the time goes in v13:
time: 57.7 us; the launch traced here: 57.4 us
  starting transfers between devices  26 us (45%)
  waiting for transfers between devices  21.4 us (37%)
  Pallas kernels  8.35 us (14%)
  local copies, waits for them, and re-layouts  1.37 us (2%)
    ppermute x14, starting transfers between devices, exchange(): return lax.ppermute(x, AXES, pairs)  26 us
    ppermute x14, waiting for transfers between devices, exchange(): return lax.ppermute(x, AXES, pairs)  21.4 us
    pallas_call x11, Pallas kernels, kernel(): pl.pallas_call(body, out_shape=outs, in_specs=specs or [inner] * len(oper...  8.35 us
    unnamed x8, local copies, waits for them, and re-layouts  1.37 us
  transfers between devices with their start and end apart: 14, of which 6 were waited for; matrix products, arithmetic and copies ran while one was open for 0% of the time, Pallas kernels for 10%

profile of v13, /device:TPU:0, one launch (start us, length us, event | category | flops | bytes accessed | tf_op | source)
XLA Modules:
  0.0 57.4 jit_solution(9004565531048163266)
XLA Ops:
  0.0 1.1 %shard_map.64._.refs_2_ = bf16[1152,256]{1,0:T(8,128)(2,1)S(1)} custom-call(bf16[2048,256]{1,0:T(8,128)(2,1)} %down.1, bf16[256,128]{1,0:T(8,128)(2,1)} %up.1), custom_call_target="tpu_custom_call" | custom-call | bytes 1703936 | tf_op jit(solution)/shard_map/pallas_call | solution.py:121
  1.1 0.0 copy-start
  1.1 3.1 %collective-permute-start.1 = (bf16[1152,256]{1,0:T(8,128)(2,1)S(1)}, bf16[1152,256]{1,0:T(8,128)(2,1)S(1)}, u32[]{:S(2)}, u32[]{:S(2)}) collective-permute-start(bf16[1152,256]{1,0:T(8,128)(2,1)S(1)} %shard_map.64._.refs_2_), channel_id=1, source_target_pairs={{0,4},{1,5},{2,6},{3,7},{4,0},{5,1},{6,2},{7,3},{8,12},{9,13},{10,... | collective-permute-start | bytes 1769480 | tf_op jit(solution)/shard_map/ppermute | solution.py:98
  4.2 0.7 %collective-permute-start.4 = (bf16[1152,256]{1,0:T(8,128)(2,1)S(1)}, bf16[1152,256]{1,0:T(8,128)(2,1)S(1)}, u32[]{:S(2)}, u32[]{:S(2)}) collective-permute-start(bf16[1152,256]{1,0:T(8,128)(2,1)S(1)} %shard_map.64._.refs_2_), channel_id=1, source_target_pairs={{4,8},{5,9},{6,10},{7,11},{8,4},{9,5},{10,6},{11,7},{20,24},{21,25... | collective-permute-start | bytes 1769480 | tf_op jit(solution)/shard_map/ppermute | solution.py:98
  4.9 0.0 copy-start.1
  4.9 0.7 %copy-done.1 = s32[384]{0:T(512)S(1)} copy-done((s32[384]{0:T(512)S(1)}, s32[384]{0:T(512)}, u32[]{:S(2)}) %copy-start.1) | copy-done | bytes 1560
  5.6 0.0 copy-start.2
  5.6 0.7 %copy-done.2 = s32[384,1]{0,1:T(1,128)S(1)} copy-done((s32[384,1]{0,1:T(1,128)S(1)}, s32[384,1]{0,1:T(1,128)}, u32[]{:S(2)}) %copy-start.2) | copy-done | bytes 1560
  6.2 1.4 %shard_map.65 = (bf16[400,1024]{1,0:T(8,128)(2,1)S(1)}, bf16[400,1024]{1,0:T(8,128)(2,1)S(1)}) custom-call(bf16[384,2048]{1,0:T(8,128)(2,1)} %tokens.1, s32[1,384]{1,0:T(1,128)S(1)} %bitcast.1, s32[384]{0:T(512)S(1)} %copy-done.1, bf16[1152,256]{1,0:T(8,128)(2,1)S(1)} %shard_map.64._.refs_2_), custom_call_target="tpu_custom_call" | custom-call | bytes 3804160 | tf_op jit(solution)/shard_map/pallas_call | solution.py:121
  7.6 1.6 %collective-permute-start = (bf16[400,1024]{1,0:T(8,128)(2,1)S(1)}, bf16[400,1024]{1,0:T(8,128)(2,1)S(1)}, u32[]{:S(2)}, u32[]{:S(2)}) collective-permute-start(bf16[400,1024]{1,0:T(8,128)(2,1)S(1)} %get-tuple-element.30.away), channel_id=1, source_target_pairs={{0,16},{1,17},{2,18},{3,19},{4,20},{5,21},{6,22},{7,23},{8,24},{9,... | collective-permute-start | bytes 2457608 | tf_op jit(solution)/shard_map/ppermute | solution.py:98
  9.2 0.7 %shard_map.66 = (bf16[160,1024]{1,0:T(8,128)(2,1)S(1)}, bf16[160,1024]{1,0:T(8,128)(2,1)S(1)}, bf16[144,384]{1,0:T(8,128)(2,1)S(1)}) custom-call(bf16[400,1024]{1,0:T(8,128)(2,1)S(1)} %get-tuple-element.29.own.refs_0_, bf16[400,1024]{1,0:T(8,128)(2,1)S(1)} %get-tuple-element.30.away), custom_call_target="tpu_custom_call" | custom-call | flops 226492416 | bytes 2404352 | tf_op jit(solution)/shard_map/pallas_call | solution.py:121
  9.9 7.6 %collective-permute-done.1.refs_4_ = bf16[1152,256]{1,0:T(8,128)(2,1)S(1)} collective-permute-done((bf16[1152,256]{1,0:T(8,128)(2,1)S(1)}, bf16[1152,256]{1,0:T(8,128)(2,1)S(1)}, u32[]{:S(2)}, u32[]{:S(2)}) %collective-permute-start.1) | collective-permute-done | bytes 589856 | tf_op jit(solution)/shard_map/ppermute | solution.py:98
  17.5 3.7 %collective-permute-start.2 = (bf16[160,1024]{1,0:T(8,128)(2,1)S(1)}, bf16[160,1024]{1,0:T(8,128)(2,1)S(1)}, u32[]{:S(2)}, u32[]{:S(2)}) collective-permute-start(bf16[160,1024]{1,0:T(8,128)(2,1)S(1)} %get-tuple-element.32), channel_id=1, source_target_pairs={{0,4},{1,5},{2,6},{3,7},{12,8},{13,9},{14,10},{15,11},{16,20},{17,... | collective-permute-start | bytes 983048 | tf_op jit(solution)/shard_map/ppermute | solution.py:98
  21.2 0.7 %collective-permute-start.6 = (bf16[1152,256]{1,0:T(8,128)(2,1)S(1)}, bf16[1152,256]{1,0:T(8,128)(2,1)S(1)}, u32[]{:S(2)}, u32[]{:S(2)}) collective-permute-start(bf16[1152,256]{1,0:T(8,128)(2,1)S(1)} %collective-permute-done.1.refs_4_), channel_id=1, source_target_pairs={{4,8},{5,9},{6,10},{7,11},{8,4},{9,5},{10,6},{11,7},{20,24},{21,25... | collective-permute-start | bytes 1769480 | tf_op jit(solution)/shard_map/ppermute | solution.py:98
  21.9 0.0 collective-permute-done.4.refs_3_
  21.9 1.3 %collective-permute-start.5 = (bf16[1152,256]{1,0:T(8,128)(2,1)S(1)}, bf16[1152,256]{1,0:T(8,128)(2,1)S(1)}, u32[]{:S(2)}, u32[]{:S(2)}) collective-permute-start(bf16[1152,256]{1,0:T(8,128)(2,1)S(1)} %collective-permute-done.4.refs_3_), channel_id=1, source_target_pairs={{4,0},{5,1},{6,2},{7,3},{8,12},{9,13},{10,14},{11,15},{20,16},{21,... | collective-permute-start | bytes 1769480 | tf_op jit(solution)/shard_map/ppermute | solution.py:98
  23.2 5.6 %collective-permute-start.3 = (bf16[160,1024]{1,0:T(8,128)(2,1)S(1)}, bf16[160,1024]{1,0:T(8,128)(2,1)S(1)}, u32[]{:S(2)}, u32[]{:S(2)}) collective-permute-start(bf16[160,1024]{1,0:T(8,128)(2,1)S(1)} %get-tuple-element.33), channel_id=1, source_target_pairs={{0,20},{1,21},{2,22},{3,23},{12,24},{13,25},{14,26},{15,27},{16,4}... | collective-permute-start | bytes 983048 | tf_op jit(solution)/shard_map/ppermute | solution.py:98
  28.7 0.0 copy-done
  28.8 1.1 %shard_map.72 = (f32[384,256]{1,0:T(8,128)S(1)}, f32[384,256]{1,0:T(8,128)S(1)}) custom-call(bf16[400,1024]{1,0:T(8,128)(2,1)S(1)} %get-tuple-element.29.own.refs_0_, bf16[400,1024]{1,0:T(8,128)(2,1)S(1)} %get-tuple-element.30.away, bf16[2048,512]{1,0:T(8,128)(2,1)S(1)} %copy-done, bf16[144,384]{1,0:T(8,128)(2,1)S(1)} %get-tuple-element.42._.places), custom_call_target="tpu_custom_call" | custom-call | flops 805306368 | bytes 4632576 | tf_op jit(solution)/shard_map/pallas_call | solution.py:121
  29.8 0.0 copy-start.3
  29.8 0.0 collective-permute-done.refs_1_
  29.8 1.5 %shard_map.67 = (f32[2,384,128]{2,1,0:T(8,128)S(1)}, f32[2,384,256]{2,1,0:T(8,128)S(1)}, f32[384,1]{1,0:T(8,128)S(1)}, bf16[3,256,128]{2,1,0:T(8,128)(2,1)S(1)}) custom-call(bf16[400,1024]{1,0:T(8,128)(2,1)S(1)} %get-tuple-element.29.own.refs_0_, bf16[400,1024]{1,0:T(8,128)(2,1)S(1)} %collective-permute-done.refs_1_, ...), custom_call_target="tpu_custom_call" | custom-call | tf_op jit(solution)/shard_map/pallas_call | solution.py:121
  31.4 1.6 %collective-permute-start.9 = (f32[384,256]{1,0:T(8,128)S(1)}, f32[384,256]{1,0:T(8,128)S(1)}, u32[]{:S(2)}, u32[]{:S(2)}) collective-permute-start(f32[384,256]{1,0:T(8,128)S(1)} %get-tuple-element.45), channel_id=1, source_target_pairs={{0,2},{1,3},{2,0},{3,1},{4,6},{5,7},{6,4},{7,5},{8,10},{9,11},{10,... | collective-permute-start | bytes 1179656 | tf_op jit(solution)/shard_map/ppermute | solution.py:98
  32.9 0.0 collective-permute-done.2.hop.refs_2_
  32.9 0.0 copy-done.3
  32.9 4.4 %collective-permute-start.8 = (bf16[256,128]{1,0:T(8,128)(2,1)S(1)}, bf16[256,128]{1,0:T(8,128)(2,1)S(1)}, u32[]{:S(2)}, u32[]{:S(2)}) collective-permute-start(bf16[256,128]{1,0:T(8,128)(2,1)S(1)} %copy-done.3), channel_id=1, source_target_pairs={{0,12},{1,13},{2,14},{3,15},{12,0},{13,1},{14,2},{15,3},{16,28},{1... | collective-permute-start | bytes 196616 | tf_op jit(solution)/shard_map/ppermute | solution.py:98
  37.3 0.3 shard_map.68._.refs_4_
  37.6 0.0 collective-permute-done.3.hop.refs_3_
  37.6 0.3 shard_map.69.refs_5_
  37.9 0.0 collective-permute-done.6.refs_9_
  37.9 0.5 collective-permute-done.5.refs_8_
  38.4 0.7 %shard_map.70 = (f32[16,384]{1,0:T(8,128)S(1)}, f32[16,144]{1,0:T(8,128)S(1)}, f32[16,528]{1,0:T(8,128)S(1)}, bf16[256,128]{1,0:T(8,128)(2,1)S(1)}) custom-call(bf16[400,1024]{1,0:T(8,128)(2,1)S(1)} %get-tuple-element.29.own.refs_0_, bf16[400,1024]{1,0:T(8,128)(2,1)S(1)} %collective-permute-done.refs_1_, ...), custom_call_target="tpu_custom_call" | custom-call | flops 553648128 | bytes 5081088 | tf_op jit(solution)/shard_map/pallas_call | solution.py:121
  39.1 1.6 %collective-permute-start.7 = (f32[16,528]{1,0:T(8,128)S(1)}, f32[16,528]{1,0:T(8,128)S(1)}, u32[]{:S(2)}, u32[]{:S(2)}) collective-permute-start(f32[16,528]{1,0:T(8,128)S(1)} %get-tuple-element.38), channel_id=1, source_target_pairs={{0,16},{1,17},{2,18},{3,19},{4,20},{5,21},{6,22},{7,23},{8,24},{9,... | collective-permute-start | bytes 101384 | tf_op jit(solution)/shard_map/ppermute | solution.py:98
  40.7 2.5 %collective-permute-done.7.near = f32[16,528]{1,0:T(8,128)S(1)} collective-permute-done((f32[16,528]{1,0:T(8,128)S(1)}, f32[16,528]{1,0:T(8,128)S(1)}, u32[]{:S(2)}, u32[]{:S(2)}) %collective-permute-start.7) | collective-permute-done | bytes 33824 | tf_op jit(solution)/shard_map/ppermute | solution.py:98
  43.2 1.3 %collective-permute-start.10 = (f32[16,144]{1,0:T(8,128)S(1)}, f32[16,144]{1,0:T(8,128)S(1)}, u32[]{:S(2)}, u32[]{:S(2)}) collective-permute-start(f32[16,144]{1,0:T(8,128)S(1)} %get-tuple-element.46), channel_id=1, source_target_pairs={{4,0},{5,1},{6,2},{7,3},{8,12},{9,13},{10,14},{11,15},{20,16},{21,... | collective-permute-start | bytes 27656 | tf_op jit(solution)/shard_map/ppermute | solution.py:98
  44.4 0.0 collective-permute-done.8.distant
  44.5 0.0 collective-permute-done.9.got
  44.5 6.3 %collective-permute-done.10.hop = f32[16,144]{1,0:T(8,128)S(1)} collective-permute-done((f32[16,144]{1,0:T(8,128)S(1)}, f32[16,144]{1,0:T(8,128)S(1)}, u32[]{:S(2)}, u32[]{:S(2)}) %collective-permute-start.10) | collective-permute-done | bytes 9248 | tf_op jit(solution)/shard_map/ppermute | solution.py:98
  50.8 0.2 shard_map.73
  50.9 0.1 collective-permute-start.13
  51.0 0.6 %collective-permute-start.11 = (f32[16,384]{1,0:T(8,128)S(1)}, f32[16,384]{1,0:T(8,128)S(1)}, u32[]{:S(2)}, u32[]{:S(2)}) collective-permute-start(f32[16,384]{1,0:T(8,128)S(1)} %get-tuple-element.47), channel_id=1, source_target_pairs={{0,2},{1,3},{2,0},{3,1},{4,6},{5,7},{6,4},{7,5},{8,10},{9,11},{10,... | collective-permute-start | bytes 73736 | tf_op jit(solution)/shard_map/ppermute | solution.py:98
  51.6 3.3 %collective-permute-done.11 = f32[16,384]{1,0:T(8,128)S(1)} collective-permute-done((f32[16,384]{1,0:T(8,128)S(1)}, f32[16,384]{1,0:T(8,128)S(1)}, u32[]{:S(2)}, u32[]{:S(2)}) %collective-permute-start.11) | collective-permute-done | bytes 24608 | tf_op jit(solution)/shard_map/ppermute | solution.py:98
  54.9 0.0 collective-permute-start.12
  54.9 1.2 %collective-permute-done.12.far = f32[16,384]{1,0:T(8,128)S(1)} collective-permute-done((f32[16,384]{1,0:T(8,128)S(1)}, f32[16,384]{1,0:T(8,128)S(1)}, u32[]{:S(2)}, u32[]{:S(2)}) %collective-permute-start.12) | collective-permute-done | bytes 24608 | tf_op jit(solution)/shard_map/ppermute | solution.py:98
  56.1 0.0 collective-permute-done.13.got
  56.1 1.3 %shard_map.74 = bf16[384,128]{1,0:T(8,128)(2,1)} custom-call(f32[16,384]{1,0:T(8,128)S(1)} %add.3.near, f32[16,384]{1,0:T(8,128)S(1)} %collective-permute-done.12.far, f32[384,128]{1,0:T(8,128)S(1)} %get-tuple-element.48.keep, f32[384,128]{1,0:T(8,128)S(1)} %collective-permute-done.13.got, f32[384,1]{1,0:T(8,128)S(1)} %get-tuple-element.50.numbers, ...), custom_call_target="tpu_custom_call" | custom-call | bytes 869888 | tf_op jit(solution)/shard_map/pallas_call | solution.py:121
  (2 shorter events, 0.0 us)
Async XLA Ops:
  1.1 27.7 %copy-start = (bf16[2048,512]{1,0:T(8,128)(2,1)S(1)}, bf16[2048,512]{1,0:T(8,128)(2,1)}, u32[]{:S(2)}) copy-start(bf16[2048,512]{1,0:T(8,128)(2,1)} %weights.1) | copy-start | bytes 6291460
  1.1 16.4 %collective-permute-start.1 = (bf16[1152,256]{1,0:T(8,128)(2,1)S(1)}, bf16[1152,256]{1,0:T(8,128)(2,1)S(1)}, u32[]{:S(2)}, u32[]{:S(2)}) collective-permute-start(bf16[1152,256]{1,0:T(8,128)(2,1)S(1)} %shard_map.64._.refs_2_), channel_id=1, source_target_pairs={{0,4},{1,5},{2,6},{3,7},{4,0},{5,1},{6,2},{7,3},{8,12},{9,13},{10,... | collective-permute-start | bytes 1769480 | tf_op jit(solution)/shard_map/ppermute | solution.py:98
  4.2 17.7 %collective-permute-start.4 = (bf16[1152,256]{1,0:T(8,128)(2,1)S(1)}, bf16[1152,256]{1,0:T(8,128)(2,1)S(1)}, u32[]{:S(2)}, u32[]{:S(2)}) collective-permute-start(bf16[1152,256]{1,0:T(8,128)(2,1)S(1)} %shard_map.64._.refs_2_), channel_id=1, source_target_pairs={{4,8},{5,9},{6,10},{7,11},{8,4},{9,5},{10,6},{11,7},{20,24},{21,25... | collective-permute-start | bytes 1769480 | tf_op jit(solution)/shard_map/ppermute | solution.py:98
  4.9 0.7 %copy-start.1 = (s32[384]{0:T(512)S(1)}, s32[384]{0:T(512)}, u32[]{:S(2)}) copy-start(s32[384]{0:T(512)} %slot.1) | copy-start | bytes 4612
  5.6 0.7 %copy-start.2 = (s32[384,1]{0,1:T(1,128)S(1)}, s32[384,1]{0,1:T(1,128)}, u32[]{:S(2)}) copy-start(s32[384,1]{0,1:T(1,128)} %param.10) | copy-start | bytes 4612
  7.6 22.2 %collective-permute-start = (bf16[400,1024]{1,0:T(8,128)(2,1)S(1)}, bf16[400,1024]{1,0:T(8,128)(2,1)S(1)}, u32[]{:S(2)}, u32[]{:S(2)}) collective-permute-start(bf16[400,1024]{1,0:T(8,128)(2,1)S(1)} %get-tuple-element.30.away), channel_id=1, source_target_pairs={{0,16},{1,17},{2,18},{3,19},{4,20},{5,21},{6,22},{7,23},{8,24},{9,... | collective-permute-start | bytes 2457608 | tf_op jit(solution)/shard_map/ppermute | solution.py:98
  17.5 15.4 %collective-permute-start.2 = (bf16[160,1024]{1,0:T(8,128)(2,1)S(1)}, bf16[160,1024]{1,0:T(8,128)(2,1)S(1)}, u32[]{:S(2)}, u32[]{:S(2)}) collective-permute-start(bf16[160,1024]{1,0:T(8,128)(2,1)S(1)} %get-tuple-element.32), channel_id=1, source_target_pairs={{0,4},{1,5},{2,6},{3,7},{12,8},{13,9},{14,10},{15,11},{16,20},{17,... | collective-permute-start | bytes 983048 | tf_op jit(solution)/shard_map/ppermute | solution.py:98
  21.2 16.7 %collective-permute-start.6 = (bf16[1152,256]{1,0:T(8,128)(2,1)S(1)}, bf16[1152,256]{1,0:T(8,128)(2,1)S(1)}, u32[]{:S(2)}, u32[]{:S(2)}) collective-permute-start(bf16[1152,256]{1,0:T(8,128)(2,1)S(1)} %collective-permute-done.1.refs_4_), channel_id=1, source_target_pairs={{4,8},{5,9},{6,10},{7,11},{8,4},{9,5},{10,6},{11,7},{20,24},{21,25... | collective-permute-start | bytes 1769480 | tf_op jit(solution)/shard_map/ppermute | solution.py:98
  21.9 16.5 %collective-permute-start.5 = (bf16[1152,256]{1,0:T(8,128)(2,1)S(1)}, bf16[1152,256]{1,0:T(8,128)(2,1)S(1)}, u32[]{:S(2)}, u32[]{:S(2)}) collective-permute-start(bf16[1152,256]{1,0:T(8,128)(2,1)S(1)} %collective-permute-done.4.refs_3_), channel_id=1, source_target_pairs={{4,0},{5,1},{6,2},{7,3},{8,12},{9,13},{10,14},{11,15},{20,16},{21,... | collective-permute-start | bytes 1769480 | tf_op jit(solution)/shard_map/ppermute | solution.py:98
  23.2 14.4 %collective-permute-start.3 = (bf16[160,1024]{1,0:T(8,128)(2,1)S(1)}, bf16[160,1024]{1,0:T(8,128)(2,1)S(1)}, u32[]{:S(2)}, u32[]{:S(2)}) collective-permute-start(bf16[160,1024]{1,0:T(8,128)(2,1)S(1)} %get-tuple-element.33), channel_id=1, source_target_pairs={{0,20},{1,21},{2,22},{3,23},{12,24},{13,25},{14,26},{15,27},{16,4}... | collective-permute-start | bytes 983048 | tf_op jit(solution)/shard_map/ppermute | solution.py:98
  29.8 3.1 %copy-start.3 = (bf16[256,128]{1,0:T(8,128)(2,1)S(1)}, bf16[256,128]{1,0:T(8,128)(2,1)}, u32[]{:S(2)}) copy-start(bf16[256,128]{1,0:T(8,128)(2,1)} %up.1) | copy-start | bytes 196612
  31.4 13.1 %collective-permute-start.9 = (f32[384,256]{1,0:T(8,128)S(1)}, f32[384,256]{1,0:T(8,128)S(1)}, u32[]{:S(2)}, u32[]{:S(2)}) collective-permute-start(f32[384,256]{1,0:T(8,128)S(1)} %get-tuple-element.45), channel_id=1, source_target_pairs={{0,2},{1,3},{2,0},{3,1},{4,6},{5,7},{6,4},{7,5},{8,10},{9,11},{10,... | collective-permute-start | bytes 1179656 | tf_op jit(solution)/shard_map/ppermute | solution.py:98
  32.9 11.5 %collective-permute-start.8 = (bf16[256,128]{1,0:T(8,128)(2,1)S(1)}, bf16[256,128]{1,0:T(8,128)(2,1)S(1)}, u32[]{:S(2)}, u32[]{:S(2)}) collective-permute-start(bf16[256,128]{1,0:T(8,128)(2,1)S(1)} %copy-done.3), channel_id=1, source_target_pairs={{0,12},{1,13},{2,14},{3,15},{12,0},{13,1},{14,2},{15,3},{16,28},{1... | collective-permute-start | bytes 196616 | tf_op jit(solution)/shard_map/ppermute | solution.py:98
  39.1 4.1 %collective-permute-start.7 = (f32[16,528]{1,0:T(8,128)S(1)}, f32[16,528]{1,0:T(8,128)S(1)}, u32[]{:S(2)}, u32[]{:S(2)}) collective-permute-start(f32[16,528]{1,0:T(8,128)S(1)} %get-tuple-element.38), channel_id=1, source_target_pairs={{0,16},{1,17},{2,18},{3,19},{4,20},{5,21},{6,22},{7,23},{8,24},{9,... | collective-permute-start | bytes 101384 | tf_op jit(solution)/shard_map/ppermute | solution.py:98
  43.2 7.6 %collective-permute-start.10 = (f32[16,144]{1,0:T(8,128)S(1)}, f32[16,144]{1,0:T(8,128)S(1)}, u32[]{:S(2)}, u32[]{:S(2)}) collective-permute-start(f32[16,144]{1,0:T(8,128)S(1)} %get-tuple-element.46), channel_id=1, source_target_pairs={{4,0},{5,1},{6,2},{7,3},{8,12},{9,13},{10,14},{11,15},{20,16},{21,... | collective-permute-start | bytes 27656 | tf_op jit(solution)/shard_map/ppermute | solution.py:98
  50.9 5.2 %collective-permute-start.13 = (f32[384,128]{1,0:T(8,128)S(1)}, f32[384,128]{1,0:T(8,128)S(1)}, u32[]{:S(2)}, u32[]{:S(2)}) collective-permute-start(f32[384,128]{1,0:T(8,128)S(1)} %get-tuple-element.49), channel_id=1, source_target_pairs={{0,1},{1,0},{2,3},{3,2},{4,5},{5,4},{6,7},{7,6},{8,9},{9,8},{10,11... | collective-permute-start | bytes 589832 | tf_op jit(solution)/shard_map/ppermute | solution.py:98
  51.0 3.9 %collective-permute-start.11 = (f32[16,384]{1,0:T(8,128)S(1)}, f32[16,384]{1,0:T(8,128)S(1)}, u32[]{:S(2)}, u32[]{:S(2)}) collective-permute-start(f32[16,384]{1,0:T(8,128)S(1)} %get-tuple-element.47), channel_id=1, source_target_pairs={{0,2},{1,3},{2,0},{3,1},{4,6},{5,7},{6,4},{7,5},{8,10},{9,11},{10,... | collective-permute-start | bytes 73736 | tf_op jit(solution)/shard_map/ppermute | solution.py:98
  54.9 1.2 %collective-permute-start.12 = (f32[16,384]{1,0:T(8,128)S(1)}, f32[16,384]{1,0:T(8,128)S(1)}, u32[]{:S(2)}, u32[]{:S(2)}) collective-permute-start(f32[16,384]{1,0:T(8,128)S(1)} %add.3.near), channel_id=1, source_target_pairs={{0,1},{1,0},{2,3},{3,2},{4,5},{5,4},{6,7},{7,6},{8,9},{9,8},{10,11... | collective-permute-start | bytes 73736 | tf_op jit(solution)/shard_map/ppermute | solution.py:98

commit v14 on v13

--- a/solution.py
+++ b/solution.py
@@ -76,7 +76,7 @@
 
 AXES = ("groups", "adapter", "mp")
 ID_ROWS = 16
-HOP_URGENCY = (30 * 10**8, 0)
+HOP_URGENCY = (42 * 10**8, 0)
 OWNERS = 4
 LANES = 128
 NT = (((1,), (1,)), ((), ()))
@@ -153,15 +153,21 @@
         copy.wait()
 
 
-def split_body(tokens, owner, slot, _, own, away, sems):
+def split_body(tokens, owner_in, slot_in, _, own, away, owner, slot, sems):
     g = lax.axis_index("groups")
     rows, part = tokens.shape[0], own.shape[1]
     copies = []
     for n, (out, half) in enumerate(((own, g), (away, 1 - g))):
         taken = tokens.at[:, pl.ds(pl.multiple_of(half * part, part), part)]
         copies.append(pltpu.make_async_copy(taken, out.at[pl.ds(0, rows), :], sems.at[n]))
-    for copy in copies:
+    id_copies = [
+        pltpu.make_async_copy(owner_in, owner, sems.at[2]),
+        pltpu.make_async_copy(slot_in, slot, sems.at[3]),
+    ]
+    for copy in id_copies + copies:
         copy.start()
+    for copy in id_copies:
+        copy.wait()
     row = lax.broadcasted_iota(jnp.int32, (ID_ROWS, rows), 0)
     ids = jnp.where(row == 0, owner[...], jnp.where(row == 1, slot[...].reshape(1, rows), 0))
     ids = ids.astype(jnp.float32).astype(jnp.bfloat16)
@@ -393,10 +399,19 @@
     tok_own, tok_away = kernel(
         split_body,
         [narrow(rows + ID_ROWS, part)] * groups,
-        (in_hbm(tokens), request_adapter_owner.reshape(1, rows), request_adapter_slot, own),
+        (
+            in_hbm(tokens),
+            in_hbm(request_adapter_owner.reshape(1, rows)),
+            in_hbm(request_adapter_slot),
+            own,
+        ),
         0,
-        (pl.ANY, None, None, pl.ANY),
-        [pltpu.SemaphoreType.DMA((groups,))],
+        (pl.ANY, pl.ANY, pl.ANY, pl.ANY),
+        [
+            pltpu.VMEM((1, rows), jnp.int32),
+            pltpu.VMEM((rows,), jnp.int32),
+            pltpu.SemaphoreType.DMA((4,)),
+        ],
     )
     token_parts = [tok_own, exchange(tok_away, 1, 0, SAME)]
     hop_own, hop_away, places = kernel(

time: 57.7 us -> 57.1 us (0.990)
  local copies, waits for them, and re-layouts: 1.37 us -> 0.01 us
  waiting for transfers between devices: 21.4 us -> 22.3 us
    unnamed x8 -> x4, local copies, waits for them, and re-layouts: 1.37 us -> 0.01 us
    ppermute x14, waiting for transfers between devices: 21.4 us -> 22.3 us  [exchange(): return lax.ppermute(x, AXES, pairs)]
where the time goes in v14:
time: 57.1 us; the launch traced here: 56.8 us
  starting transfers between devices  25.8 us (45%)
  waiting for transfers between devices  22.3 us (39%)
  Pallas kernels  8.39 us (15%)
    ppermute x14, starting transfers between devices, exchange(): return lax.ppermute(x, AXES, pairs)  25.8 us
    ppermute x14, waiting for transfers between devices, exchange(): return lax.ppermute(x, AXES, pairs)  22.3 us
    pallas_call x11, Pallas kernels, kernel(): pl.pallas_call(body, out_shape=outs, in_specs=specs or [inner] * len(oper...  8.39 us
  transfers between devices with their start and end apart: 14, of which 6 were waited for; matrix products, arithmetic and copies ran while one was open for 0% of the time, Pallas kernels for 10%

profile of v14, /device:TPU:0, one launch (start us, length us, event | category | flops | bytes accessed | tf_op | source)
XLA Modules:
  0.0 56.8 jit_solution(2487212902881569)
XLA Ops:
  0.0 1.1 %shard_map.64._.refs_2_ = bf16[1152,256]{1,0:T(8,128)(2,1)S(1)} custom-call(bf16[2048,256]{1,0:T(8,128)(2,1)} %down.1, bf16[256,128]{1,0:T(8,128)(2,1)} %up.1), custom_call_target="tpu_custom_call" | custom-call | bytes 1703936 | tf_op jit(solution)/shard_map/pallas_call | solution.py:121
  1.1 0.0 copy-start
  1.1 3.1 %collective-permute-start.1 = (bf16[1152,256]{1,0:T(8,128)(2,1)S(1)}, bf16[1152,256]{1,0:T(8,128)(2,1)S(1)}, u32[]{:S(2)}, u32[]{:S(2)}) collective-permute-start(bf16[1152,256]{1,0:T(8,128)(2,1)S(1)} %shard_map.64._.refs_2_), channel_id=1, source_target_pairs={{0,4},{1,5},{2,6},{3,7},{4,0},{5,1},{6,2},{7,3},{8,12},{9,13},{10,... | collective-permute-start | bytes 1769480 | tf_op jit(solution)/shard_map/ppermute | solution.py:98
  4.2 1.4 %shard_map.65 = (bf16[400,1024]{1,0:T(8,128)(2,1)S(1)}, bf16[400,1024]{1,0:T(8,128)(2,1)S(1)}) custom-call(bf16[384,2048]{1,0:T(8,128)(2,1)} %tokens.1, s32[1,384]{1,0:T(1,128)} %bitcast.1, s32[384]{0:T(512)} %slot_in.1, bf16[1152,256]{1,0:T(8,128)(2,1)S(1)} %shard_map.64._.refs_2_), custom_call_target="tpu_custom_call" | custom-call | bytes 3804160 | tf_op jit(solution)/shard_map/pallas_call | solution.py:121
  5.6 1.6 %collective-permute-start = (bf16[400,1024]{1,0:T(8,128)(2,1)S(1)}, bf16[400,1024]{1,0:T(8,128)(2,1)S(1)}, u32[]{:S(2)}, u32[]{:S(2)}) collective-permute-start(bf16[400,1024]{1,0:T(8,128)(2,1)S(1)} %get-tuple-element.30.away), channel_id=1, source_target_pairs={{0,16},{1,17},{2,18},{3,19},{4,20},{5,21},{6,22},{7,23},{8,24},{9,... | collective-permute-start | bytes 2457608 | tf_op jit(solution)/shard_map/ppermute | solution.py:98
  7.2 0.7 %collective-permute-start.4 = (bf16[1152,256]{1,0:T(8,128)(2,1)S(1)}, bf16[1152,256]{1,0:T(8,128)(2,1)S(1)}, u32[]{:S(2)}, u32[]{:S(2)}) collective-permute-start(bf16[1152,256]{1,0:T(8,128)(2,1)S(1)} %shard_map.64._.refs_2_), channel_id=1, source_target_pairs={{4,8},{5,9},{6,10},{7,11},{8,4},{9,5},{10,6},{11,7},{20,24},{21,25... | collective-permute-start | bytes 1769480 | tf_op jit(solution)/shard_map/ppermute | solution.py:98
  7.9 0.7 %shard_map.66 = (bf16[160,1024]{1,0:T(8,128)(2,1)S(1)}, bf16[160,1024]{1,0:T(8,128)(2,1)S(1)}, bf16[144,384]{1,0:T(8,128)(2,1)S(1)}) custom-call(bf16[400,1024]{1,0:T(8,128)(2,1)S(1)} %get-tuple-element.29.own.refs_0_, bf16[400,1024]{1,0:T(8,128)(2,1)S(1)} %get-tuple-element.30.away), custom_call_target="tpu_custom_call" | custom-call | flops 226492416 | bytes 2404352 | tf_op jit(solution)/shard_map/pallas_call | solution.py:121
  8.6 8.9 %collective-permute-done.1.refs_4_ = bf16[1152,256]{1,0:T(8,128)(2,1)S(1)} collective-permute-done((bf16[1152,256]{1,0:T(8,128)(2,1)S(1)}, bf16[1152,256]{1,0:T(8,128)(2,1)S(1)}, u32[]{:S(2)}, u32[]{:S(2)}) %collective-permute-start.1) | collective-permute-done | bytes 589856 | tf_op jit(solution)/shard_map/ppermute | solution.py:98
  17.5 3.7 %collective-permute-start.2 = (bf16[160,1024]{1,0:T(8,128)(2,1)S(1)}, bf16[160,1024]{1,0:T(8,128)(2,1)S(1)}, u32[]{:S(2)}, u32[]{:S(2)}) collective-permute-start(bf16[160,1024]{1,0:T(8,128)(2,1)S(1)} %get-tuple-element.32), channel_id=1, source_target_pairs={{0,4},{1,5},{2,6},{3,7},{12,8},{13,9},{14,10},{15,11},{16,20},{17,... | collective-permute-start | bytes 983048 | tf_op jit(solution)/shard_map/ppermute | solution.py:98
  21.2 0.7 %collective-permute-start.6 = (bf16[1152,256]{1,0:T(8,128)(2,1)S(1)}, bf16[1152,256]{1,0:T(8,128)(2,1)S(1)}, u32[]{:S(2)}, u32[]{:S(2)}) collective-permute-start(bf16[1152,256]{1,0:T(8,128)(2,1)S(1)} %collective-permute-done.1.refs_4_), channel_id=1, source_target_pairs={{4,8},{5,9},{6,10},{7,11},{8,4},{9,5},{10,6},{11,7},{20,24},{21,25... | collective-permute-start | bytes 1769480 | tf_op jit(solution)/shard_map/ppermute | solution.py:98
  21.9 0.0 collective-permute-done.4.refs_3_
  21.9 1.3 %collective-permute-start.5 = (bf16[1152,256]{1,0:T(8,128)(2,1)S(1)}, bf16[1152,256]{1,0:T(8,128)(2,1)S(1)}, u32[]{:S(2)}, u32[]{:S(2)}) collective-permute-start(bf16[1152,256]{1,0:T(8,128)(2,1)S(1)} %collective-permute-done.4.refs_3_), channel_id=1, source_target_pairs={{4,0},{5,1},{6,2},{7,3},{8,12},{9,13},{10,14},{11,15},{20,16},{21,... | collective-permute-start | bytes 1769480 | tf_op jit(solution)/shard_map/ppermute | solution.py:98
  23.2 5.6 %collective-permute-start.3 = (bf16[160,1024]{1,0:T(8,128)(2,1)S(1)}, bf16[160,1024]{1,0:T(8,128)(2,1)S(1)}, u32[]{:S(2)}, u32[]{:S(2)}) collective-permute-start(bf16[160,1024]{1,0:T(8,128)(2,1)S(1)} %get-tuple-element.33), channel_id=1, source_target_pairs={{0,20},{1,21},{2,22},{3,23},{12,24},{13,25},{14,26},{15,27},{16,4}... | collective-permute-start | bytes 983048 | tf_op jit(solution)/shard_map/ppermute | solution.py:98
  28.7 0.0 copy-done
  28.8 1.1 %shard_map.72 = (f32[384,256]{1,0:T(8,128)S(1)}, f32[384,256]{1,0:T(8,128)S(1)}) custom-call(bf16[400,1024]{1,0:T(8,128)(2,1)S(1)} %get-tuple-element.29.own.refs_0_, bf16[400,1024]{1,0:T(8,128)(2,1)S(1)} %get-tuple-element.30.away, bf16[2048,512]{1,0:T(8,128)(2,1)S(1)} %copy-done, bf16[144,384]{1,0:T(8,128)(2,1)S(1)} %get-tuple-element.42._.places), custom_call_target="tpu_custom_call" | custom-call | flops 805306368 | bytes 4632576 | tf_op jit(solution)/shard_map/pallas_call | solution.py:121
  29.8 0.0 copy-start.1
  29.8 0.0 collective-permute-done.refs_1_
  29.8 1.5 %shard_map.67 = (f32[2,384,128]{2,1,0:T(8,128)S(1)}, f32[2,384,256]{2,1,0:T(8,128)S(1)}, f32[384,1]{1,0:T(8,128)S(1)}, bf16[3,256,128]{2,1,0:T(8,128)(2,1)S(1)}) custom-call(bf16[400,1024]{1,0:T(8,128)(2,1)S(1)} %get-tuple-element.29.own.refs_0_, bf16[400,1024]{1,0:T(8,128)(2,1)S(1)} %collective-permute-done.refs_1_, ...), custom_call_target="tpu_custom_call" | custom-call | tf_op jit(solution)/shard_map/pallas_call | solution.py:121
  31.4 0.0 copy-done.1
  31.4 4.4 %collective-permute-start.8 = (bf16[256,128]{1,0:T(8,128)(2,1)S(1)}, bf16[256,128]{1,0:T(8,128)(2,1)S(1)}, u32[]{:S(2)}, u32[]{:S(2)}) collective-permute-start(bf16[256,128]{1,0:T(8,128)(2,1)S(1)} %copy-done.1), channel_id=1, source_target_pairs={{0,12},{1,13},{2,14},{3,15},{12,0},{13,1},{14,2},{15,3},{16,28},{1... | collective-permute-start | bytes 196616 | tf_op jit(solution)/shard_map/ppermute | solution.py:98
  35.8 0.0 collective-permute-done.2.hop.refs_2_
  35.8 1.6 %collective-permute-start.9 = (f32[384,256]{1,0:T(8,128)S(1)}, f32[384,256]{1,0:T(8,128)S(1)}, u32[]{:S(2)}, u32[]{:S(2)}) collective-permute-start(f32[384,256]{1,0:T(8,128)S(1)} %get-tuple-element.45), channel_id=1, source_target_pairs={{0,2},{1,3},{2,0},{3,1},{4,6},{5,7},{6,4},{7,5},{8,10},{9,11},{10,... | collective-permute-start | bytes 1179656 | tf_op jit(solution)/shard_map/ppermute | solution.py:98
  37.3 0.3 shard_map.68._.refs_4_
  37.6 0.0 collective-permute-done.3.hop.refs_3_
  37.6 0.3 shard_map.69.refs_5_
  37.9 0.0 collective-permute-done.6.refs_9_
  37.9 1.9 %collective-permute-done.5.refs_8_ = bf16[1152,256]{1,0:T(8,128)(2,1)S(1)} collective-permute-done((bf16[1152,256]{1,0:T(8,128)(2,1)S(1)}, bf16[1152,256]{1,0:T(8,128)(2,1)S(1)}, u32[]{:S(2)}, u32[]{:S(2)}) %collective-permute-start.5) | collective-permute-done | bytes 589856 | tf_op jit(solution)/shard_map/ppermute | solution.py:98
  39.8 0.7 %shard_map.70 = (f32[16,384]{1,0:T(8,128)S(1)}, f32[16,144]{1,0:T(8,128)S(1)}, f32[16,528]{1,0:T(8,128)S(1)}, bf16[256,128]{1,0:T(8,128)(2,1)S(1)}) custom-call(bf16[400,1024]{1,0:T(8,128)(2,1)S(1)} %get-tuple-element.29.own.refs_0_, bf16[400,1024]{1,0:T(8,128)(2,1)S(1)} %collective-permute-done.refs_1_, ...), custom_call_target="tpu_custom_call" | custom-call | flops 553648128 | bytes 5081088 | tf_op jit(solution)/shard_map/pallas_call | solution.py:121
  40.5 0.4 collective-permute-start.7
  40.9 3.6 %collective-permute-done.7.near = f32[16,528]{1,0:T(8,128)S(1)} collective-permute-done((f32[16,528]{1,0:T(8,128)S(1)}, f32[16,528]{1,0:T(8,128)S(1)}, u32[]{:S(2)}, u32[]{:S(2)}) %collective-permute-start.7) | collective-permute-done | bytes 33824 | tf_op jit(solution)/shard_map/ppermute | solution.py:98
  44.6 1.3 %collective-permute-start.10 = (f32[16,144]{1,0:T(8,128)S(1)}, f32[16,144]{1,0:T(8,128)S(1)}, u32[]{:S(2)}, u32[]{:S(2)}) collective-permute-start(f32[16,144]{1,0:T(8,128)S(1)} %get-tuple-element.46), channel_id=1, source_target_pairs={{4,0},{5,1},{6,2},{7,3},{8,12},{9,13},{10,14},{11,15},{20,16},{21,... | collective-permute-start | bytes 27656 | tf_op jit(solution)/shard_map/ppermute | solution.py:98
  45.9 0.0 collective-permute-done.8.distant
  45.9 0.0 collective-permute-done.9.got
  45.9 4.3 %collective-permute-done.10.hop = f32[16,144]{1,0:T(8,128)S(1)} collective-permute-done((f32[16,144]{1,0:T(8,128)S(1)}, f32[16,144]{1,0:T(8,128)S(1)}, u32[]{:S(2)}, u32[]{:S(2)}) %collective-permute-start.10) | collective-permute-done | bytes 9248 | tf_op jit(solution)/shard_map/ppermute | solution.py:98
  50.2 0.2 shard_map.73
  50.4 0.1 collective-permute-start.13
  50.4 1.6 %collective-permute-start.11 = (f32[16,384]{1,0:T(8,128)S(1)}, f32[16,384]{1,0:T(8,128)S(1)}, u32[]{:S(2)}, u32[]{:S(2)}) collective-permute-start(f32[16,384]{1,0:T(8,128)S(1)} %get-tuple-element.47), channel_id=1, source_target_pairs={{0,2},{1,3},{2,0},{3,1},{4,6},{5,7},{6,4},{7,5},{8,10},{9,11},{10,... | collective-permute-start | bytes 73736 | tf_op jit(solution)/shard_map/ppermute | solution.py:98
  52.0 2.3 %collective-permute-done.11 = f32[16,384]{1,0:T(8,128)S(1)} collective-permute-done((f32[16,384]{1,0:T(8,128)S(1)}, f32[16,384]{1,0:T(8,128)S(1)}, u32[]{:S(2)}, u32[]{:S(2)}) %collective-permute-start.11) | collective-permute-done | bytes 24608 | tf_op jit(solution)/shard_map/ppermute | solution.py:98
  54.3 0.0 collective-permute-start.12
  54.3 1.2 %collective-permute-done.12.far = f32[16,384]{1,0:T(8,128)S(1)} collective-permute-done((f32[16,384]{1,0:T(8,128)S(1)}, f32[16,384]{1,0:T(8,128)S(1)}, u32[]{:S(2)}, u32[]{:S(2)}) %collective-permute-start.12) | collective-permute-done | bytes 24608 | tf_op jit(solution)/shard_map/ppermute | solution.py:98
  55.5 0.0 collective-permute-done.13.got
  55.5 1.3 %shard_map.74 = bf16[384,128]{1,0:T(8,128)(2,1)} custom-call(f32[16,384]{1,0:T(8,128)S(1)} %add.3.near, f32[16,384]{1,0:T(8,128)S(1)} %collective-permute-done.12.far, f32[384,128]{1,0:T(8,128)S(1)} %get-tuple-element.48.keep, f32[384,128]{1,0:T(8,128)S(1)} %collective-permute-done.13.got, f32[384,1]{1,0:T(8,128)S(1)} %get-tuple-element.50.numbers, ...), custom_call_target="tpu_custom_call" | custom-call | bytes 869888 | tf_op jit(solution)/shard_map/pallas_call | solution.py:121
  (2 shorter events, 0.0 us)
Async XLA Ops:
  1.1 27.7 %copy-start = (bf16[2048,512]{1,0:T(8,128)(2,1)S(1)}, bf16[2048,512]{1,0:T(8,128)(2,1)}, u32[]{:S(2)}) copy-start(bf16[2048,512]{1,0:T(8,128)(2,1)} %weights.1) | copy-start | bytes 6291460
  1.1 16.4 %collective-permute-start.1 = (bf16[1152,256]{1,0:T(8,128)(2,1)S(1)}, bf16[1152,256]{1,0:T(8,128)(2,1)S(1)}, u32[]{:S(2)}, u32[]{:S(2)}) collective-permute-start(bf16[1152,256]{1,0:T(8,128)(2,1)S(1)} %shard_map.64._.refs_2_), channel_id=1, source_target_pairs={{0,4},{1,5},{2,6},{3,7},{4,0},{5,1},{6,2},{7,3},{8,12},{9,13},{10,... | collective-permute-start | bytes 1769480 | tf_op jit(solution)/shard_map/ppermute | solution.py:98
  5.6 24.2 %collective-permute-start = (bf16[400,1024]{1,0:T(8,128)(2,1)S(1)}, bf16[400,1024]{1,0:T(8,128)(2,1)S(1)}, u32[]{:S(2)}, u32[]{:S(2)}) collective-permute-start(bf16[400,1024]{1,0:T(8,128)(2,1)S(1)} %get-tuple-element.30.away), channel_id=1, source_target_pairs={{0,16},{1,17},{2,18},{3,19},{4,20},{5,21},{6,22},{7,23},{8,24},{9,... | collective-permute-start | bytes 2457608 | tf_op jit(solution)/shard_map/ppermute | solution.py:98
  7.2 14.7 %collective-permute-start.4 = (bf16[1152,256]{1,0:T(8,128)(2,1)S(1)}, bf16[1152,256]{1,0:T(8,128)(2,1)S(1)}, u32[]{:S(2)}, u32[]{:S(2)}) collective-permute-start(bf16[1152,256]{1,0:T(8,128)(2,1)S(1)} %shard_map.64._.refs_2_), channel_id=1, source_target_pairs={{4,8},{5,9},{6,10},{7,11},{8,4},{9,5},{10,6},{11,7},{20,24},{21,25... | collective-permute-start | bytes 1769480 | tf_op jit(solution)/shard_map/ppermute | solution.py:98
  17.5 18.3 %collective-permute-start.2 = (bf16[160,1024]{1,0:T(8,128)(2,1)S(1)}, bf16[160,1024]{1,0:T(8,128)(2,1)S(1)}, u32[]{:S(2)}, u32[]{:S(2)}) collective-permute-start(bf16[160,1024]{1,0:T(8,128)(2,1)S(1)} %get-tuple-element.32), channel_id=1, source_target_pairs={{0,4},{1,5},{2,6},{3,7},{12,8},{13,9},{14,10},{15,11},{16,20},{17,... | collective-permute-start | bytes 983048 | tf_op jit(solution)/shard_map/ppermute | solution.py:98
  21.2 16.7 %collective-permute-start.6 = (bf16[1152,256]{1,0:T(8,128)(2,1)S(1)}, bf16[1152,256]{1,0:T(8,128)(2,1)S(1)}, u32[]{:S(2)}, u32[]{:S(2)}) collective-permute-start(bf16[1152,256]{1,0:T(8,128)(2,1)S(1)} %collective-permute-done.1.refs_4_), channel_id=1, source_target_pairs={{4,8},{5,9},{6,10},{7,11},{8,4},{9,5},{10,6},{11,7},{20,24},{21,25... | collective-permute-start | bytes 1769480 | tf_op jit(solution)/shard_map/ppermute | solution.py:98
  21.9 17.9 %collective-permute-start.5 = (bf16[1152,256]{1,0:T(8,128)(2,1)S(1)}, bf16[1152,256]{1,0:T(8,128)(2,1)S(1)}, u32[]{:S(2)}, u32[]{:S(2)}) collective-permute-start(bf16[1152,256]{1,0:T(8,128)(2,1)S(1)} %collective-permute-done.4.refs_3_), channel_id=1, source_target_pairs={{4,0},{5,1},{6,2},{7,3},{8,12},{9,13},{10,14},{11,15},{20,16},{21,... | collective-permute-start | bytes 1769480 | tf_op jit(solution)/shard_map/ppermute | solution.py:98
  23.2 14.4 %collective-permute-start.3 = (bf16[160,1024]{1,0:T(8,128)(2,1)S(1)}, bf16[160,1024]{1,0:T(8,128)(2,1)S(1)}, u32[]{:S(2)}, u32[]{:S(2)}) collective-permute-start(bf16[160,1024]{1,0:T(8,128)(2,1)S(1)} %get-tuple-element.33), channel_id=1, source_target_pairs={{0,20},{1,21},{2,22},{3,23},{12,24},{13,25},{14,26},{15,27},{16,4}... | collective-permute-start | bytes 983048 | tf_op jit(solution)/shard_map/ppermute | solution.py:98
  29.8 1.5 %copy-start.1 = (bf16[256,128]{1,0:T(8,128)(2,1)S(1)}, bf16[256,128]{1,0:T(8,128)(2,1)}, u32[]{:S(2)}) copy-start(bf16[256,128]{1,0:T(8,128)(2,1)} %up.1) | copy-start | bytes 196612
  31.4 14.5 %collective-permute-start.8 = (bf16[256,128]{1,0:T(8,128)(2,1)S(1)}, bf16[256,128]{1,0:T(8,128)(2,1)S(1)}, u32[]{:S(2)}, u32[]{:S(2)}) collective-permute-start(bf16[256,128]{1,0:T(8,128)(2,1)S(1)} %copy-done.1), channel_id=1, source_target_pairs={{0,12},{1,13},{2,14},{3,15},{12,0},{13,1},{14,2},{15,3},{16,28},{1... | collective-permute-start | bytes 196616 | tf_op jit(solution)/shard_map/ppermute | solution.py:98
  35.8 10.1 %collective-permute-start.9 = (f32[384,256]{1,0:T(8,128)S(1)}, f32[384,256]{1,0:T(8,128)S(1)}, u32[]{:S(2)}, u32[]{:S(2)}) collective-permute-start(f32[384,256]{1,0:T(8,128)S(1)} %get-tuple-element.45), channel_id=1, source_target_pairs={{0,2},{1,3},{2,0},{3,1},{4,6},{5,7},{6,4},{7,5},{8,10},{9,11},{10,... | collective-permute-start | bytes 1179656 | tf_op jit(solution)/shard_map/ppermute | solution.py:98
  40.5 4.1 %collective-permute-start.7 = (f32[16,528]{1,0:T(8,128)S(1)}, f32[16,528]{1,0:T(8,128)S(1)}, u32[]{:S(2)}, u32[]{:S(2)}) collective-permute-start(f32[16,528]{1,0:T(8,128)S(1)} %get-tuple-element.38), channel_id=1, source_target_pairs={{0,16},{1,17},{2,18},{3,19},{4,20},{5,21},{6,22},{7,23},{8,24},{9,... | collective-permute-start | bytes 101384 | tf_op jit(solution)/shard_map/ppermute | solution.py:98
  44.6 5.6 %collective-permute-start.10 = (f32[16,144]{1,0:T(8,128)S(1)}, f32[16,144]{1,0:T(8,128)S(1)}, u32[]{:S(2)}, u32[]{:S(2)}) collective-permute-start(f32[16,144]{1,0:T(8,128)S(1)} %get-tuple-element.46), channel_id=1, source_target_pairs={{4,0},{5,1},{6,2},{7,3},{8,12},{9,13},{10,14},{11,15},{20,16},{21,... | collective-permute-start | bytes 27656 | tf_op jit(solution)/shard_map/ppermute | solution.py:98
  50.4 5.2 %collective-permute-start.13 = (f32[384,128]{1,0:T(8,128)S(1)}, f32[384,128]{1,0:T(8,128)S(1)}, u32[]{:S(2)}, u32[]{:S(2)}) collective-permute-start(f32[384,128]{1,0:T(8,128)S(1)} %get-tuple-element.49), channel_id=1, source_target_pairs={{0,1},{1,0},{2,3},{3,2},{4,5},{5,4},{6,7},{7,6},{8,9},{9,8},{10,11... | collective-permute-start | bytes 589832 | tf_op jit(solution)/shard_map/ppermute | solution.py:98
  50.4 3.9 %collective-permute-start.11 = (f32[16,384]{1,0:T(8,128)S(1)}, f32[16,384]{1,0:T(8,128)S(1)}, u32[]{:S(2)}, u32[]{:S(2)}) collective-permute-start(f32[16,384]{1,0:T(8,128)S(1)} %get-tuple-element.47), channel_id=1, source_target_pairs={{0,2},{1,3},{2,0},{3,1},{4,6},{5,7},{6,4},{7,5},{8,10},{9,11},{10,... | collective-permute-start | bytes 73736 | tf_op jit(solution)/shard_map/ppermute | solution.py:98
  54.3 1.2 %collective-permute-start.12 = (f32[16,384]{1,0:T(8,128)S(1)}, f32[16,384]{1,0:T(8,128)S(1)}, u32[]{:S(2)}, u32[]{:S(2)}) collective-permute-start(f32[16,384]{1,0:T(8,128)S(1)} %add.3.near), channel_id=1, source_target_pairs={{0,1},{1,0},{2,3},{3,2},{4,5},{5,4},{6,7},{7,6},{8,9},{9,8},{10,11... | collective-permute-start | bytes 73736 | tf_op jit(solution)/shard_map/ppermute | solution.py:98

commit v15 on v14

--- a/solution.py
+++ b/solution.py
@@ -76,7 +76,7 @@
 
 AXES = ("groups", "adapter", "mp")
 ID_ROWS = 16
-HOP_URGENCY = (42 * 10**8, 0)
+HOP_URGENCY = (36 * 10**8, 0)
 OWNERS = 4
 LANES = 128
 NT = (((1,), (1,)), ((), ()))
@@ -100,8 +100,8 @@
 
 SAME = tuple((a, a) for a in range(OWNERS))
 BESIDE = ((0, 1), (1, 0), (2, 3), (3, 2))
-MIDDLE = ((1, 2), (2, 1))
-ENDS = ((0, 3), (3, 0))
+MIDDLE = ((0, 0), (1, 2), (2, 1), (3, 3))
+ENDS = ((0, 3), (1, 1), (2, 2), (3, 0))
 OUTWARD = ((1, 0), (2, 3))
 INWARD = ((0, 1), (3, 2))
 
@@ -270,7 +270,8 @@
         picked = jnp.zeros((rows, columns), jnp.float32)
         for bit, block in zip(bits, blocks):
             wide = jnp.dot(tokens[:rows, :], block[:part, :], preferred_element_type=jnp.float32)
-            picked = jnp.where(owner == (a ^ bit).astype(jnp.float32), wide, picked)
+            number = jnp.where((bit != 3) | (a == 1) | (a == 2), a ^ bit, -1)
+            picked = jnp.where(owner == number.astype(jnp.float32), wide, picked)
         folded[n] = fold(jnp.where(right, picked, 0.0))
         mask[n] = jnp.where(owner == (a ^ 2).astype(jnp.float32), right.astype(jnp.float32), 0.0)
 
@@ -393,7 +394,6 @@
         (pl.ANY, pl.ANY),
         [pltpu.SemaphoreType.DMA((1 + half,))],
     )
-    mirror = exchange(own, 0, 0, MIDDLE)
     beside = exchange(own, 0, 0, BESIDE)
 
     tok_own, tok_away = kernel(
@@ -414,6 +414,7 @@
         ],
     )
     token_parts = [tok_own, exchange(tok_away, 1, 0, SAME)]
+    mirror = exchange(after(own, tok_own), 0, 0, MIDDLE)
     hop_own, hop_away, places = kernel(
         functools.partial(hop_body, rows, capacity),
         [narrow(capacity + ID_ROWS, part)] * groups
@@ -422,7 +423,7 @@
         2 * rows * features * capacity,
     )
 
-    inside = exchange(beside, 0, 0, MIDDLE)
+    inside = exchange(after(beside, places), 0, 0, MIDDLE)
     outside = exchange(mirror, 0, 0, OUTWARD)
     hops = [
         exchange(after(hop_own, beside), 0, 0, INWARD),
@@ -473,7 +474,7 @@
     low, hop_low = kernel(
         near_body, [wide(ADAPTER_RANK, rows), wide(ADAPTER_RANK, capacity)], (low, hop_low, near)
     )
-    back = exchange(hop_low, 0, 0, OUTWARD)
+    back = exchange(hop_low, 0, 0, BESIDE)
     low, keep, give = kernel(
         functools.partial(merge_body, bits[1]),
         [wide(ADAPTER_RANK, rows)] + [wide(rows, bits[1] * keys)] * 2,

time: 57.1 us -> 54.6 us (0.956)
  waiting for transfers between devices: 22.3 us -> 17.3 us
  starting transfers between devices: 25.8 us -> 28.5 us
    ppermute x14, waiting for transfers between devices: 22.3 us -> 17.3 us  [exchange(): return lax.ppermute(x, AXES, pairs)]
    ppermute x14, starting transfers between devices: 25.8 us -> 28.5 us  [exchange(): return lax.ppermute(x, AXES, pairs)]
  transfers between devices with their start and end apart: 14 -> 14, of which waited for: 6 -> 6; matrix products, arithmetic and copies ran while one was open for 0% -> 0% of each run, Pallas kernels for 10% -> 11%
where the time goes in v15:
time: 54.6 us; the launch traced here: 54.4 us
  starting transfers between devices  28.5 us (52%)
  waiting for transfers between devices  17.3 us (32%)
  Pallas kernels  8.39 us (15%)
    ppermute x14, starting transfers between devices, exchange(): return lax.ppermute(x, AXES, pairs)  28.5 us
    ppermute x14, waiting for transfers between devices, exchange(): return lax.ppermute(x, AXES, pairs)  17.3 us
    pallas_call x11, Pallas kernels, kernel(): pl.pallas_call(body, out_shape=outs, in_specs=specs or [inner] * len(oper...  8.39 us
  transfers between devices with their start and end apart: 14, of which 6 were waited for; matrix products, arithmetic and copies ran while one was open for 0% of the time, Pallas kernels for 11%

profile of v15, /device:TPU:0, one launch (start us, length us, event | category | flops | bytes accessed | tf_op | source)
XLA Modules:
  0.0 54.4 jit_solution(9899948641854474768)
XLA Ops:
  0.0 1.1 %shard_map.64._.refs_2_ = bf16[1152,256]{1,0:T(8,128)(2,1)S(1)} custom-call(bf16[2048,256]{1,0:T(8,128)(2,1)} %down.1, bf16[256,128]{1,0:T(8,128)(2,1)} %up.1), custom_call_target="tpu_custom_call" | custom-call | bytes 1703936 | tf_op jit(solution)/shard_map/pallas_call | solution.py:121
  1.1 0.0 copy-start
  1.1 3.1 %collective-permute-start.1 = (bf16[1152,256]{1,0:T(8,128)(2,1)S(1)}, bf16[1152,256]{1,0:T(8,128)(2,1)S(1)}, u32[]{:S(2)}, u32[]{:S(2)}) collective-permute-start(bf16[1152,256]{1,0:T(8,128)(2,1)S(1)} %shard_map.64._.refs_2_), channel_id=1, source_target_pairs={{0,4},{1,5},{2,6},{3,7},{4,0},{5,1},{6,2},{7,3},{8,12},{9,13},{10,... | collective-permute-start | bytes 1769480 | tf_op jit(solution)/shard_map/ppermute | solution.py:98
  4.2 1.4 %shard_map.65 = (bf16[400,1024]{1,0:T(8,128)(2,1)S(1)}, bf16[400,1024]{1,0:T(8,128)(2,1)S(1)}) custom-call(bf16[384,2048]{1,0:T(8,128)(2,1)} %tokens.1, s32[1,384]{1,0:T(1,128)} %bitcast.1, s32[384]{0:T(512)} %slot_in.1, bf16[1152,256]{1,0:T(8,128)(2,1)S(1)} %shard_map.64._.refs_2_), custom_call_target="tpu_custom_call" | custom-call | bytes 3804160 | tf_op jit(solution)/shard_map/pallas_call | solution.py:121
  5.6 0.7 %collective-permute-start.4 = (bf16[1152,256]{1,0:T(8,128)(2,1)S(1)}, bf16[1152,256]{1,0:T(8,128)(2,1)S(1)}, u32[]{:S(2)}, u32[]{:S(2)}) collective-permute-start(bf16[1152,256]{1,0:T(8,128)(2,1)S(1)} %shard_map.64._.refs_2_), channel_id=1, source_target_pairs={{0,0},{1,1},{2,2},{3,3},{4,8},{5,9},{6,10},{7,11},{8,4},{9,5},{10,... | collective-permute-start | bytes 1769480 | tf_op jit(solution)/shard_map/ppermute | solution.py:98
  6.3 1.6 %collective-permute-start = (bf16[400,1024]{1,0:T(8,128)(2,1)S(1)}, bf16[400,1024]{1,0:T(8,128)(2,1)S(1)}, u32[]{:S(2)}, u32[]{:S(2)}) collective-permute-start(bf16[400,1024]{1,0:T(8,128)(2,1)S(1)} %get-tuple-element.32.away), channel_id=1, source_target_pairs={{0,16},{1,17},{2,18},{3,19},{4,20},{5,21},{6,22},{7,23},{8,24},{9,... | collective-permute-start | bytes 2457608 | tf_op jit(solution)/shard_map/ppermute | solution.py:98
  7.9 0.7 %shard_map.66 = (bf16[160,1024]{1,0:T(8,128)(2,1)S(1)}, bf16[160,1024]{1,0:T(8,128)(2,1)S(1)}, bf16[144,384]{1,0:T(8,128)(2,1)S(1)}) custom-call(bf16[400,1024]{1,0:T(8,128)(2,1)S(1)} %get-tuple-element.31.own.refs_0_, bf16[400,1024]{1,0:T(8,128)(2,1)S(1)} %get-tuple-element.32.away), custom_call_target="tpu_custom_call" | custom-call | flops 226492416 | bytes 2404352 | tf_op jit(solution)/shard_map/pallas_call | solution.py:121
  8.6 8.9 %collective-permute-done.1.refs_4_ = bf16[1152,256]{1,0:T(8,128)(2,1)S(1)} collective-permute-done((bf16[1152,256]{1,0:T(8,128)(2,1)S(1)}, bf16[1152,256]{1,0:T(8,128)(2,1)S(1)}, u32[]{:S(2)}, u32[]{:S(2)}) %collective-permute-start.1) | collective-permute-done | bytes 589856 | tf_op jit(solution)/shard_map/ppermute | solution.py:98
  17.5 3.7 %collective-permute-start.2 = (bf16[160,1024]{1,0:T(8,128)(2,1)S(1)}, bf16[160,1024]{1,0:T(8,128)(2,1)S(1)}, u32[]{:S(2)}, u32[]{:S(2)}) collective-permute-start(bf16[160,1024]{1,0:T(8,128)(2,1)S(1)} %get-tuple-element.34), channel_id=1, source_target_pairs={{0,4},{1,5},{2,6},{3,7},{12,8},{13,9},{14,10},{15,11},{16,20},{17,... | collective-permute-start | bytes 983048 | tf_op jit(solution)/shard_map/ppermute | solution.py:98
  21.2 0.7 %collective-permute-start.6 = (bf16[1152,256]{1,0:T(8,128)(2,1)S(1)}, bf16[1152,256]{1,0:T(8,128)(2,1)S(1)}, u32[]{:S(2)}, u32[]{:S(2)}) collective-permute-start(bf16[1152,256]{1,0:T(8,128)(2,1)S(1)} %collective-permute-done.1.refs_4_), channel_id=1, source_target_pairs={{0,0},{1,1},{2,2},{3,3},{4,8},{5,9},{6,10},{7,11},{8,4},{9,5},{10,... | collective-permute-start | bytes 1769480 | tf_op jit(solution)/shard_map/ppermute | solution.py:98
  21.9 0.0 collective-permute-done.4.refs_3_
  21.9 1.3 %collective-permute-start.5 = (bf16[1152,256]{1,0:T(8,128)(2,1)S(1)}, bf16[1152,256]{1,0:T(8,128)(2,1)S(1)}, u32[]{:S(2)}, u32[]{:S(2)}) collective-permute-start(bf16[1152,256]{1,0:T(8,128)(2,1)S(1)} %collective-permute-done.4.refs_3_), channel_id=1, source_target_pairs={{4,0},{5,1},{6,2},{7,3},{8,12},{9,13},{10,14},{11,15},{20,16},{21,... | collective-permute-start | bytes 1769480 | tf_op jit(solution)/shard_map/ppermute | solution.py:98
  23.2 5.6 %collective-permute-start.3 = (bf16[160,1024]{1,0:T(8,128)(2,1)S(1)}, bf16[160,1024]{1,0:T(8,128)(2,1)S(1)}, u32[]{:S(2)}, u32[]{:S(2)}) collective-permute-start(bf16[160,1024]{1,0:T(8,128)(2,1)S(1)} %get-tuple-element.35), channel_id=1, source_target_pairs={{0,20},{1,21},{2,22},{3,23},{12,24},{13,25},{14,26},{15,27},{16,4}... | collective-permute-start | bytes 983048 | tf_op jit(solution)/shard_map/ppermute | solution.py:98
  28.7 0.0 copy-done
  28.8 1.1 %shard_map.72 = (f32[384,256]{1,0:T(8,128)S(1)}, f32[384,256]{1,0:T(8,128)S(1)}) custom-call(bf16[400,1024]{1,0:T(8,128)(2,1)S(1)} %get-tuple-element.31.own.refs_0_, bf16[400,1024]{1,0:T(8,128)(2,1)S(1)} %get-tuple-element.32.away, bf16[2048,512]{1,0:T(8,128)(2,1)S(1)} %copy-done, bf16[144,384]{1,0:T(8,128)(2,1)S(1)} %get-tuple-element.39._.places), custom_call_target="tpu_custom_call" | custom-call | flops 805306368 | bytes 4632576 | tf_op jit(solution)/shard_map/pallas_call | solution.py:121
  29.8 0.0 copy-start.1
  29.8 0.0 collective-permute-done.refs_1_
  29.8 1.5 %shard_map.67 = (f32[2,384,128]{2,1,0:T(8,128)S(1)}, f32[2,384,256]{2,1,0:T(8,128)S(1)}, f32[384,1]{1,0:T(8,128)S(1)}, bf16[3,256,128]{2,1,0:T(8,128)(2,1)S(1)}) custom-call(bf16[400,1024]{1,0:T(8,128)(2,1)S(1)} %get-tuple-element.31.own.refs_0_, bf16[400,1024]{1,0:T(8,128)(2,1)S(1)} %collective-permute-done.refs_1_, ...), custom_call_target="tpu_custom_call" | custom-call | tf_op jit(solution)/shard_map/pallas_call | solution.py:121
  31.4 0.0 copy-done.1
  31.4 4.4 %collective-permute-start.8 = (bf16[256,128]{1,0:T(8,128)(2,1)S(1)}, bf16[256,128]{1,0:T(8,128)(2,1)S(1)}, u32[]{:S(2)}, u32[]{:S(2)}) collective-permute-start(bf16[256,128]{1,0:T(8,128)(2,1)S(1)} %copy-done.1), channel_id=1, source_target_pairs={{0,12},{1,13},{2,14},{3,15},{4,4},{5,5},{6,6},{7,7},{8,8},{9,9},{1... | collective-permute-start | bytes 196616 | tf_op jit(solution)/shard_map/ppermute | solution.py:98
  35.8 0.0 collective-permute-done.2.hop.refs_2_
  35.8 1.6 %collective-permute-start.9 = (f32[384,256]{1,0:T(8,128)S(1)}, f32[384,256]{1,0:T(8,128)S(1)}, u32[]{:S(2)}, u32[]{:S(2)}) collective-permute-start(f32[384,256]{1,0:T(8,128)S(1)} %get-tuple-element.49), channel_id=1, source_target_pairs={{0,2},{1,3},{2,0},{3,1},{4,6},{5,7},{6,4},{7,5},{8,10},{9,11},{10,... | collective-permute-start | bytes 1179656 | tf_op jit(solution)/shard_map/ppermute | solution.py:98
  37.3 0.3 shard_map.68._.refs_4_
  37.6 0.0 collective-permute-done.3.hop.refs_3_
  37.6 0.3 shard_map.69.refs_5_
  37.9 0.0 collective-permute-done.6.refs_9_
  37.9 0.5 collective-permute-done.5.refs_8_
  38.4 0.7 %shard_map.70 = (f32[16,384]{1,0:T(8,128)S(1)}, f32[16,144]{1,0:T(8,128)S(1)}, f32[16,528]{1,0:T(8,128)S(1)}, bf16[256,128]{1,0:T(8,128)(2,1)S(1)}) custom-call(bf16[400,1024]{1,0:T(8,128)(2,1)S(1)} %get-tuple-element.31.own.refs_0_, bf16[400,1024]{1,0:T(8,128)(2,1)S(1)} %collective-permute-done.refs_1_, ...), custom_call_target="tpu_custom_call" | custom-call | flops 553648128 | bytes 5081088 | tf_op jit(solution)/shard_map/pallas_call | solution.py:121
  39.1 2.3 %collective-permute-start.7 = (f32[16,528]{1,0:T(8,128)S(1)}, f32[16,528]{1,0:T(8,128)S(1)}, u32[]{:S(2)}, u32[]{:S(2)}) collective-permute-start(f32[16,528]{1,0:T(8,128)S(1)} %get-tuple-element.43), channel_id=1, source_target_pairs={{0,16},{1,17},{2,18},{3,19},{4,20},{5,21},{6,22},{7,23},{8,24},{9,... | collective-permute-start | bytes 101384 | tf_op jit(solution)/shard_map/ppermute | solution.py:98
  41.4 2.0 %collective-permute-done.7.near = f32[16,528]{1,0:T(8,128)S(1)} collective-permute-done((f32[16,528]{1,0:T(8,128)S(1)}, f32[16,528]{1,0:T(8,128)S(1)}, u32[]{:S(2)}, u32[]{:S(2)}) %collective-permute-start.7) | collective-permute-done | bytes 33824 | tf_op jit(solution)/shard_map/ppermute | solution.py:98
  43.4 2.7 %collective-permute-start.10 = (f32[16,144]{1,0:T(8,128)S(1)}, f32[16,144]{1,0:T(8,128)S(1)}, u32[]{:S(2)}, u32[]{:S(2)}) collective-permute-start(f32[16,144]{1,0:T(8,128)S(1)} %get-tuple-element.50), channel_id=1, source_target_pairs={{0,4},{1,5},{2,6},{3,7},{4,0},{5,1},{6,2},{7,3},{8,12},{9,13},{10,... | collective-permute-start | bytes 27656 | tf_op jit(solution)/shard_map/ppermute | solution.py:98
  46.1 0.0 collective-permute-done.8.distant
  46.1 0.0 collective-permute-done.9.got
  46.1 1.7 %collective-permute-done.10.hop = f32[16,144]{1,0:T(8,128)S(1)} collective-permute-done((f32[16,144]{1,0:T(8,128)S(1)}, f32[16,144]{1,0:T(8,128)S(1)}, u32[]{:S(2)}, u32[]{:S(2)}) %collective-permute-start.10) | collective-permute-done | bytes 9248 | tf_op jit(solution)/shard_map/ppermute | solution.py:98
  47.8 0.2 shard_map.73
  47.9 0.1 collective-permute-start.13
  48.0 0.9 %collective-permute-start.11 = (f32[16,384]{1,0:T(8,128)S(1)}, f32[16,384]{1,0:T(8,128)S(1)}, u32[]{:S(2)}, u32[]{:S(2)}) collective-permute-start(f32[16,384]{1,0:T(8,128)S(1)} %get-tuple-element.51), channel_id=1, source_target_pairs={{0,2},{1,3},{2,0},{3,1},{4,6},{5,7},{6,4},{7,5},{8,10},{9,11},{10,... | collective-permute-start | bytes 73736 | tf_op jit(solution)/shard_map/ppermute | solution.py:98
  48.9 3.0 %collective-permute-done.11 = f32[16,384]{1,0:T(8,128)S(1)} collective-permute-done((f32[16,384]{1,0:T(8,128)S(1)}, f32[16,384]{1,0:T(8,128)S(1)}, u32[]{:S(2)}, u32[]{:S(2)}) %collective-permute-start.11) | collective-permute-done | bytes 24608 | tf_op jit(solution)/shard_map/ppermute | solution.py:98
  51.9 0.0 collective-permute-start.12
  51.9 1.2 %collective-permute-done.12.far = f32[16,384]{1,0:T(8,128)S(1)} collective-permute-done((f32[16,384]{1,0:T(8,128)S(1)}, f32[16,384]{1,0:T(8,128)S(1)}, u32[]{:S(2)}, u32[]{:S(2)}) %collective-permute-start.12) | collective-permute-done | bytes 24608 | tf_op jit(solution)/shard_map/ppermute | solution.py:98
  53.1 0.0 collective-permute-done.13.got
  53.1 1.3 %shard_map.74 = bf16[384,128]{1,0:T(8,128)(2,1)} custom-call(f32[16,384]{1,0:T(8,128)S(1)} %add.3.near, f32[16,384]{1,0:T(8,128)S(1)} %collective-permute-done.12.far, f32[384,128]{1,0:T(8,128)S(1)} %get-tuple-element.52.keep, f32[384,128]{1,0:T(8,128)S(1)} %collective-permute-done.13.got, f32[384,1]{1,0:T(8,128)S(1)} %get-tuple-element.54.numbers, ...), custom_call_target="tpu_custom_call" | custom-call | bytes 869888 | tf_op jit(solution)/shard_map/pallas_call | solution.py:121
  (2 shorter events, 0.0 us)
Async XLA Ops:
  1.1 27.7 %copy-start = (bf16[2048,512]{1,0:T(8,128)(2,1)S(1)}, bf16[2048,512]{1,0:T(8,128)(2,1)}, u32[]{:S(2)}) copy-start(bf16[2048,512]{1,0:T(8,128)(2,1)} %weights.1) | copy-start | bytes 6291460
  1.1 16.4 %collective-permute-start.1 = (bf16[1152,256]{1,0:T(8,128)(2,1)S(1)}, bf16[1152,256]{1,0:T(8,128)(2,1)S(1)}, u32[]{:S(2)}, u32[]{:S(2)}) collective-permute-start(bf16[1152,256]{1,0:T(8,128)(2,1)S(1)} %shard_map.64._.refs_2_), channel_id=1, source_target_pairs={{0,4},{1,5},{2,6},{3,7},{4,0},{5,1},{6,2},{7,3},{8,12},{9,13},{10,... | collective-permute-start | bytes 1769480 | tf_op jit(solution)/shard_map/ppermute | solution.py:98
  5.6 16.3 %collective-permute-start.4 = (bf16[1152,256]{1,0:T(8,128)(2,1)S(1)}, bf16[1152,256]{1,0:T(8,128)(2,1)S(1)}, u32[]{:S(2)}, u32[]{:S(2)}) collective-permute-start(bf16[1152,256]{1,0:T(8,128)(2,1)S(1)} %shard_map.64._.refs_2_), channel_id=1, source_target_pairs={{0,0},{1,1},{2,2},{3,3},{4,8},{5,9},{6,10},{7,11},{8,4},{9,5},{10,... | collective-permute-start | bytes 1769480 | tf_op jit(solution)/shard_map/ppermute | solution.py:98
  6.3 23.5 %collective-permute-start = (bf16[400,1024]{1,0:T(8,128)(2,1)S(1)}, bf16[400,1024]{1,0:T(8,128)(2,1)S(1)}, u32[]{:S(2)}, u32[]{:S(2)}) collective-permute-start(bf16[400,1024]{1,0:T(8,128)(2,1)S(1)} %get-tuple-element.32.away), channel_id=1, source_target_pairs={{0,16},{1,17},{2,18},{3,19},{4,20},{5,21},{6,22},{7,23},{8,24},{9,... | collective-permute-start | bytes 2457608 | tf_op jit(solution)/shard_map/ppermute | solution.py:98
  17.5 18.3 %collective-permute-start.2 = (bf16[160,1024]{1,0:T(8,128)(2,1)S(1)}, bf16[160,1024]{1,0:T(8,128)(2,1)S(1)}, u32[]{:S(2)}, u32[]{:S(2)}) collective-permute-start(bf16[160,1024]{1,0:T(8,128)(2,1)S(1)} %get-tuple-element.34), channel_id=1, source_target_pairs={{0,4},{1,5},{2,6},{3,7},{12,8},{13,9},{14,10},{15,11},{16,20},{17,... | collective-permute-start | bytes 983048 | tf_op jit(solution)/shard_map/ppermute | solution.py:98
  21.2 16.7 %collective-permute-start.6 = (bf16[1152,256]{1,0:T(8,128)(2,1)S(1)}, bf16[1152,256]{1,0:T(8,128)(2,1)S(1)}, u32[]{:S(2)}, u32[]{:S(2)}) collective-permute-start(bf16[1152,256]{1,0:T(8,128)(2,1)S(1)} %collective-permute-done.1.refs_4_), channel_id=1, source_target_pairs={{0,0},{1,1},{2,2},{3,3},{4,8},{5,9},{6,10},{7,11},{8,4},{9,5},{10,... | collective-permute-start | bytes 1769480 | tf_op jit(solution)/shard_map/ppermute | solution.py:98
  21.9 16.5 %collective-permute-start.5 = (bf16[1152,256]{1,0:T(8,128)(2,1)S(1)}, bf16[1152,256]{1,0:T(8,128)(2,1)S(1)}, u32[]{:S(2)}, u32[]{:S(2)}) collective-permute-start(bf16[1152,256]{1,0:T(8,128)(2,1)S(1)} %collective-permute-done.4.refs_3_), channel_id=1, source_target_pairs={{4,0},{5,1},{6,2},{7,3},{8,12},{9,13},{10,14},{11,15},{20,16},{21,... | collective-permute-start | bytes 1769480 | tf_op jit(solution)/shard_map/ppermute | solution.py:98
  23.2 14.4 %collective-permute-start.3 = (bf16[160,1024]{1,0:T(8,128)(2,1)S(1)}, bf16[160,1024]{1,0:T(8,128)(2,1)S(1)}, u32[]{:S(2)}, u32[]{:S(2)}) collective-permute-start(bf16[160,1024]{1,0:T(8,128)(2,1)S(1)} %get-tuple-element.35), channel_id=1, source_target_pairs={{0,20},{1,21},{2,22},{3,23},{12,24},{13,25},{14,26},{15,27},{16,4}... | collective-permute-start | bytes 983048 | tf_op jit(solution)/shard_map/ppermute | solution.py:98
  29.8 1.5 %copy-start.1 = (bf16[256,128]{1,0:T(8,128)(2,1)S(1)}, bf16[256,128]{1,0:T(8,128)(2,1)}, u32[]{:S(2)}) copy-start(bf16[256,128]{1,0:T(8,128)(2,1)} %up.1) | copy-start | bytes 196612
  31.4 14.7 %collective-permute-start.8 = (bf16[256,128]{1,0:T(8,128)(2,1)S(1)}, bf16[256,128]{1,0:T(8,128)(2,1)S(1)}, u32[]{:S(2)}, u32[]{:S(2)}) collective-permute-start(bf16[256,128]{1,0:T(8,128)(2,1)S(1)} %copy-done.1), channel_id=1, source_target_pairs={{0,12},{1,13},{2,14},{3,15},{4,4},{5,5},{6,6},{7,7},{8,8},{9,9},{1... | collective-permute-start | bytes 196616 | tf_op jit(solution)/shard_map/ppermute | solution.py:98
  35.8 10.3 %collective-permute-start.9 = (f32[384,256]{1,0:T(8,128)S(1)}, f32[384,256]{1,0:T(8,128)S(1)}, u32[]{:S(2)}, u32[]{:S(2)}) collective-permute-start(f32[384,256]{1,0:T(8,128)S(1)} %get-tuple-element.49), channel_id=1, source_target_pairs={{0,2},{1,3},{2,0},{3,1},{4,6},{5,7},{6,4},{7,5},{8,10},{9,11},{10,... | collective-permute-start | bytes 1179656 | tf_op jit(solution)/shard_map/ppermute | solution.py:98
  39.1 4.3 %collective-permute-start.7 = (f32[16,528]{1,0:T(8,128)S(1)}, f32[16,528]{1,0:T(8,128)S(1)}, u32[]{:S(2)}, u32[]{:S(2)}) collective-permute-start(f32[16,528]{1,0:T(8,128)S(1)} %get-tuple-element.43), channel_id=1, source_target_pairs={{0,16},{1,17},{2,18},{3,19},{4,20},{5,21},{6,22},{7,23},{8,24},{9,... | collective-permute-start | bytes 101384 | tf_op jit(solution)/shard_map/ppermute | solution.py:98
  43.4 4.4 %collective-permute-start.10 = (f32[16,144]{1,0:T(8,128)S(1)}, f32[16,144]{1,0:T(8,128)S(1)}, u32[]{:S(2)}, u32[]{:S(2)}) collective-permute-start(f32[16,144]{1,0:T(8,128)S(1)} %get-tuple-element.50), channel_id=1, source_target_pairs={{0,4},{1,5},{2,6},{3,7},{4,0},{5,1},{6,2},{7,3},{8,12},{9,13},{10,... | collective-permute-start | bytes 27656 | tf_op jit(solution)/shard_map/ppermute | solution.py:98
  47.9 5.2 %collective-permute-start.13 = (f32[384,128]{1,0:T(8,128)S(1)}, f32[384,128]{1,0:T(8,128)S(1)}, u32[]{:S(2)}, u32[]{:S(2)}) collective-permute-start(f32[384,128]{1,0:T(8,128)S(1)} %get-tuple-element.53), channel_id=1, source_target_pairs={{0,1},{1,0},{2,3},{3,2},{4,5},{5,4},{6,7},{7,6},{8,9},{9,8},{10,11... | collective-permute-start | bytes 589832 | tf_op jit(solution)/shard_map/ppermute | solution.py:98
  48.0 3.9 %collective-permute-start.11 = (f32[16,384]{1,0:T(8,128)S(1)}, f32[16,384]{1,0:T(8,128)S(1)}, u32[]{:S(2)}, u32[]{:S(2)}) collective-permute-start(f32[16,384]{1,0:T(8,128)S(1)} %get-tuple-element.51), channel_id=1, source_target_pairs={{0,2},{1,3},{2,0},{3,1},{4,6},{5,7},{6,4},{7,5},{8,10},{9,11},{10,... | collective-permute-start | bytes 73736 | tf_op jit(solution)/shard_map/ppermute | solution.py:98
  51.9 1.2 %collective-permute-start.12 = (f32[16,384]{1,0:T(8,128)S(1)}, f32[16,384]{1,0:T(8,128)S(1)}, u32[]{:S(2)}, u32[]{:S(2)}) collective-permute-start(f32[16,384]{1,0:T(8,128)S(1)} %add.3.near), channel_id=1, source_target_pairs={{0,1},{1,0},{2,3},{3,2},{4,5},{5,4},{6,7},{7,6},{8,9},{9,8},{10,11... | collective-permute-start | bytes 73736 | tf_op jit(solution)/shard_map/ppermute | solution.py:98

commit v16 on v15

--- a/solution.py
+++ b/solution.py
@@ -76,7 +76,7 @@
 
 AXES = ("groups", "adapter", "mp")
 ID_ROWS = 16
-HOP_URGENCY = (36 * 10**8, 0)
+HOP_URGENCY = (30 * 10**8, 0)
 OWNERS = 4
 LANES = 128
 NT = (((1,), (1,)), ((), ()))
@@ -257,7 +257,10 @@
     groups = lax.axis_size("groups")
     a = lax.axis_index("adapter")
     token_refs, rest = refs[:groups], refs[groups:]
-    blocks, (folded, mask, numbers, ups) = rest[: len(bits)], rest[len(bits) :]
+    blocks, rest = rest[: len(bits)], rest[len(bits) :]
+    kept, got, folded, mask, numbers, ups, keep, give, base = rest
+    base[...] = kept[...] + got[...]
+    halves(base, 1, keep, give)
     columns = blocks[0].shape[1]
     for n, block in enumerate(blocks):
         ups[n] = stacked(block[part:, :], ups.shape[2])
@@ -287,7 +290,7 @@
     token_refs, rest = refs[:groups], refs[groups:]
     hops, rest = rest[:groups], rest[groups:]
     hop_masks, rest = rest[:groups], rest[groups:]
-    folded, mask, outside, inside, low, hop_low, away, last_up = rest
+    folded, mask, inside, outside, low, hop_low, away, last_up = rest
     columns = inside.shape[1]
 
     def finish(block):
@@ -329,16 +332,14 @@
     hop_out[...] = hop_low[...] + near[:, rows:]
 
 
-def merge_body(bit, low, places, kept, got, hop, out, keep, give, base):
-    back = hop[...]
+def merge_body(low, far, places, hop, hop_far, _, out):
+    back = hop[...] + hop_far[...]
     spread = jnp.zeros(low.shape, jnp.float32)
     for _ in range(3):
         piece = back.astype(jnp.bfloat16)
         back = back - piece.astype(jnp.float32)
         spread = spread + jnp.dot(piece, places[...], preferred_element_type=jnp.float32)
-    out[...] = low[...] + spread
-    base[...] = kept[...] + got[...]
-    halves(base, bit, keep, give)
+    out[...] = low[...] + far[...] + spread
 
 
 def finish_body(near, far, keep, got, numbers, ups, last_up, distant, out):
@@ -423,6 +424,16 @@
         2 * rows * features * capacity,
     )
 
+    keep, give = kernel(
+        functools.partial(base_body, 2, rows),
+        [wide(rows, shares * keys // 2)] * 2,
+        (tok_own, tok_away, base_key_weight, places),
+        2 * rows * features * shares * keys,
+        (None, None, None, pl.ANY),
+        [pltpu.VMEM((rows, shares * keys), jnp.float32)],
+    )
+    got = exchange(give, 0, 2, SAME)
+
     inside = exchange(after(beside, places), 0, 0, MIDDLE)
     outside = exchange(mirror, 0, 0, OUTWARD)
     hops = [
@@ -430,10 +441,18 @@
         exchange(hop_away, 1, 0, INWARD),
     ]
 
-    folded, mask, numbers, ups = kernel(
+    folded, mask, numbers, ups, keep, give = kernel(
         functools.partial(early_body, (0, 3, 1), part, rows),
-        [wide(groups, rows, LANES), wide(groups, rows, columns), wide(rows, 1), narrow(3, columns, keys)],
-        (*token_parts, own, mirror, beside),
+        [
+            wide(groups, rows, LANES),
+            wide(groups, rows, columns),
+            wide(rows, 1),
+            narrow(3, columns, keys),
+            wide(rows, keys),
+            wide(rows, keys),
+        ],
+        (*token_parts, own, mirror, beside, keep, got),
+        scratch=[pltpu.VMEM((rows, 2 * keys), jnp.float32)],
         light=True,
     )
     hop_masks, latest = [], folded
@@ -446,17 +465,6 @@
             (None, pl.ANY),
         )
         hop_masks.append(latest)
-    bits = (2, 1)
-    keep, give = kernel(
-        functools.partial(base_body, bits[0], rows),
-        [wide(rows, shares * keys // 2)] * 2,
-        (tok_own, tok_away, base_key_weight, places),
-        2 * rows * features * shares * keys,
-        (None, None, None, pl.ANY),
-        [pltpu.VMEM((rows, shares * keys), jnp.float32)],
-    )
-    got = exchange(after(give, folded), 0, bits[0], SAME)
-
     low, hop_low, away, last_up = kernel(
         functools.partial(last_body, part, rows, capacity),
         [
@@ -465,7 +473,7 @@
             wide(ADAPTER_RANK, rows + capacity),
             narrow(columns, keys),
         ],
-        (*token_parts, *hops, *hop_masks, folded, mask, outside, inside),
+        (*token_parts, *hops, *hop_masks, folded, mask, inside, outside),
         2 * groups * (rows + capacity) * part * columns,
     )
 
@@ -475,15 +483,17 @@
         near_body, [wide(ADAPTER_RANK, rows), wide(ADAPTER_RANK, capacity)], (low, hop_low, near)
     )
     back = exchange(hop_low, 0, 0, BESIDE)
-    low, keep, give = kernel(
-        functools.partial(merge_body, bits[1]),
-        [wide(ADAPTER_RANK, rows)] + [wide(rows, bits[1] * keys)] * 2,
-        (after(low, distant), places, keep, got, back),
-        scratch=[pltpu.VMEM((rows, bits[0] * keys), jnp.float32)],
-    )
-    got = exchange(give, 0, bits[1], SAME)
-    low = low + exchange(low, 0, bits[0], SAME)
-    low_far = exchange(low, 0, bits[1], SAME)
+    back_far = exchange(hop_low, 0, 2, BESIDE)
+    low_far = exchange(low, 0, 2, SAME)
+    low = kernel(
+        merge_body,
+        wide(ADAPTER_RANK, rows),
+        (low, low_far, places, back, back_far, distant),
+        0,
+        (None, None, None, None, None, pl.ANY),
+    )
+    got = exchange(give, 0, 1, SAME)
+    low_far = exchange(low, 0, 1, SAME)
     return kernel(
         finish_body, narrow(rows, keys), (low, low_far, keep, got, numbers, ups, last_up, distant)
     )

time: 54.6 us -> 53.1 us (0.973)
  starting transfers between devices: 28.5 us -> 27.7 us
  waiting for transfers between devices: 17.3 us -> 16.5 us
    ppermute x14 -> x15, waiting for transfers between devices: 17.3 us -> 16.5 us  [exchange(): return lax.ppermute(x, AXES, pairs)]
    ppermute x14 -> x15, starting transfers between devices: 28.5 us -> 27.7 us  [exchange(): return lax.ppermute(x, AXES, pairs)]
  transfers between devices with their start and end apart: 14 -> 15, of which waited for: 6 -> 6; matrix products, arithmetic and copies ran while one was open for 0% -> 0% of each run, Pallas kernels for 11% -> 12%
where the time goes in v16:
time: 53.1 us; the launch traced here: 52.9 us
  starting transfers between devices  27.7 us (52%)
  waiting for transfers between devices  16.5 us (31%)
  Pallas kernels  8.46 us (16%)
    ppermute x15, starting transfers between devices, exchange(): return lax.ppermute(x, AXES, pairs)  27.7 us
    ppermute x15, waiting for transfers between devices, exchange(): return lax.ppermute(x, AXES, pairs)  16.5 us
    pallas_call x11, Pallas kernels, kernel(): pl.pallas_call(body, out_shape=outs, in_specs=specs or [inner] * len(oper...  8.46 us
  transfers between devices with their start and end apart: 15, of which 6 were waited for; matrix products, arithmetic and copies ran while one was open for 0% of the time, Pallas kernels for 12%

profile of v16, /device:TPU:0, one launch (start us, length us, event | category | flops | bytes accessed | tf_op | source)
XLA Modules:
  0.0 52.9 jit_solution(11269341855082026651)
XLA Ops:
  0.0 1.1 %shard_map.64._.refs_2_ = bf16[1152,256]{1,0:T(8,128)(2,1)S(1)} custom-call(bf16[2048,256]{1,0:T(8,128)(2,1)} %down.1, bf16[256,128]{1,0:T(8,128)(2,1)} %up.1), custom_call_target="tpu_custom_call" | custom-call | bytes 1703936 | tf_op jit(solution)/shard_map/pallas_call | solution.py:121
  1.1 0.0 copy-start
  1.1 3.1 %collective-permute-start.1 = (bf16[1152,256]{1,0:T(8,128)(2,1)S(1)}, bf16[1152,256]{1,0:T(8,128)(2,1)S(1)}, u32[]{:S(2)}, u32[]{:S(2)}) collective-permute-start(bf16[1152,256]{1,0:T(8,128)(2,1)S(1)} %shard_map.64._.refs_2_), channel_id=1, source_target_pairs={{0,4},{1,5},{2,6},{3,7},{4,0},{5,1},{6,2},{7,3},{8,12},{9,13},{10,... | collective-permute-start | bytes 1769480 | tf_op jit(solution)/shard_map/ppermute | solution.py:98
  4.2 1.4 %shard_map.65 = (bf16[400,1024]{1,0:T(8,128)(2,1)S(1)}, bf16[400,1024]{1,0:T(8,128)(2,1)S(1)}) custom-call(bf16[384,2048]{1,0:T(8,128)(2,1)} %tokens.1, s32[1,384]{1,0:T(1,128)} %bitcast.1, s32[384]{0:T(512)} %slot_in.1, bf16[1152,256]{1,0:T(8,128)(2,1)S(1)} %shard_map.64._.refs_2_), custom_call_target="tpu_custom_call" | custom-call | bytes 3804160 | tf_op jit(solution)/shard_map/pallas_call | solution.py:121
  5.6 0.7 %collective-permute-start.4 = (bf16[1152,256]{1,0:T(8,128)(2,1)S(1)}, bf16[1152,256]{1,0:T(8,128)(2,1)S(1)}, u32[]{:S(2)}, u32[]{:S(2)}) collective-permute-start(bf16[1152,256]{1,0:T(8,128)(2,1)S(1)} %shard_map.64._.refs_2_), channel_id=1, source_target_pairs={{0,0},{1,1},{2,2},{3,3},{4,8},{5,9},{6,10},{7,11},{8,4},{9,5},{10,... | collective-permute-start | bytes 1769480 | tf_op jit(solution)/shard_map/ppermute | solution.py:98
  6.3 1.6 %collective-permute-start = (bf16[400,1024]{1,0:T(8,128)(2,1)S(1)}, bf16[400,1024]{1,0:T(8,128)(2,1)S(1)}, u32[]{:S(2)}, u32[]{:S(2)}) collective-permute-start(bf16[400,1024]{1,0:T(8,128)(2,1)S(1)} %get-tuple-element.29.away), channel_id=1, source_target_pairs={{0,16},{1,17},{2,18},{3,19},{4,20},{5,21},{6,22},{7,23},{8,24},{9,... | collective-permute-start | bytes 2457608 | tf_op jit(solution)/shard_map/ppermute | solution.py:98
  7.9 0.7 %shard_map.66 = (bf16[160,1024]{1,0:T(8,128)(2,1)S(1)}, bf16[160,1024]{1,0:T(8,128)(2,1)S(1)}, bf16[144,384]{1,0:T(8,128)(2,1)S(1)}) custom-call(bf16[400,1024]{1,0:T(8,128)(2,1)S(1)} %get-tuple-element.28.own.refs_0_, bf16[400,1024]{1,0:T(8,128)(2,1)S(1)} %get-tuple-element.29.away), custom_call_target="tpu_custom_call" | custom-call | flops 226492416 | bytes 2404352 | tf_op jit(solution)/shard_map/pallas_call | solution.py:121
  8.6 0.0 copy-done
  8.6 1.1 %shard_map.67 = (f32[384,256]{1,0:T(8,128)S(1)}, f32[384,256]{1,0:T(8,128)S(1)}) custom-call(bf16[400,1024]{1,0:T(8,128)(2,1)S(1)} %get-tuple-element.28.own.refs_0_, bf16[400,1024]{1,0:T(8,128)(2,1)S(1)} %get-tuple-element.29.away, bf16[2048,512]{1,0:T(8,128)(2,1)S(1)} %copy-done, bf16[144,384]{1,0:T(8,128)(2,1)S(1)} %get-tuple-element.34._.places), custom_call_target="tpu_custom_call" | custom-call | flops 805306368 | bytes 4632576 | tf_op jit(solution)/shard_map/pallas_call | solution.py:121
  9.7 1.6 %collective-permute-start.5 = (f32[384,256]{1,0:T(8,128)S(1)}, f32[384,256]{1,0:T(8,128)S(1)}, u32[]{:S(2)}, u32[]{:S(2)}) collective-permute-start(f32[384,256]{1,0:T(8,128)S(1)} %get-tuple-element.36), channel_id=1, source_target_pairs={{0,2},{1,3},{2,0},{3,1},{4,6},{5,7},{6,4},{7,5},{8,10},{9,11},{10,... | collective-permute-start | bytes 1179656 | tf_op jit(solution)/shard_map/ppermute | solution.py:98
  11.2 6.3 %collective-permute-done.1.refs_4_ = bf16[1152,256]{1,0:T(8,128)(2,1)S(1)} collective-permute-done((bf16[1152,256]{1,0:T(8,128)(2,1)S(1)}, bf16[1152,256]{1,0:T(8,128)(2,1)S(1)}, u32[]{:S(2)}, u32[]{:S(2)}) %collective-permute-start.1) | collective-permute-done | bytes 589856 | tf_op jit(solution)/shard_map/ppermute | solution.py:98
  17.5 3.7 %collective-permute-start.2 = (bf16[160,1024]{1,0:T(8,128)(2,1)S(1)}, bf16[160,1024]{1,0:T(8,128)(2,1)S(1)}, u32[]{:S(2)}, u32[]{:S(2)}) collective-permute-start(bf16[160,1024]{1,0:T(8,128)(2,1)S(1)} %get-tuple-element.31), channel_id=1, source_target_pairs={{0,4},{1,5},{2,6},{3,7},{12,8},{13,9},{14,10},{15,11},{16,20},{17,... | collective-permute-start | bytes 983048 | tf_op jit(solution)/shard_map/ppermute | solution.py:98
  21.2 0.7 %collective-permute-start.6 = (bf16[1152,256]{1,0:T(8,128)(2,1)S(1)}, bf16[1152,256]{1,0:T(8,128)(2,1)S(1)}, u32[]{:S(2)}, u32[]{:S(2)}) collective-permute-start(bf16[1152,256]{1,0:T(8,128)(2,1)S(1)} %collective-permute-done.1.refs_4_), channel_id=1, source_target_pairs={{0,0},{1,1},{2,2},{3,3},{4,8},{5,9},{6,10},{7,11},{8,4},{9,5},{10,... | collective-permute-start | bytes 1769480 | tf_op jit(solution)/shard_map/ppermute | solution.py:98
  21.9 0.0 collective-permute-done.4.refs_3_
  21.9 1.3 %collective-permute-start.7 = (bf16[1152,256]{1,0:T(8,128)(2,1)S(1)}, bf16[1152,256]{1,0:T(8,128)(2,1)S(1)}, u32[]{:S(2)}, u32[]{:S(2)}) collective-permute-start(bf16[1152,256]{1,0:T(8,128)(2,1)S(1)} %collective-permute-done.4.refs_3_), channel_id=1, source_target_pairs={{4,0},{5,1},{6,2},{7,3},{8,12},{9,13},{10,14},{11,15},{20,16},{21,... | collective-permute-start | bytes 1769480 | tf_op jit(solution)/shard_map/ppermute | solution.py:98
  23.2 0.0 collective-permute-done.5.refs_6_
  23.2 5.6 %collective-permute-start.3 = (bf16[160,1024]{1,0:T(8,128)(2,1)S(1)}, bf16[160,1024]{1,0:T(8,128)(2,1)S(1)}, u32[]{:S(2)}, u32[]{:S(2)}) collective-permute-start(bf16[160,1024]{1,0:T(8,128)(2,1)S(1)} %get-tuple-element.32), channel_id=1, source_target_pairs={{0,20},{1,21},{2,22},{3,23},{12,24},{13,25},{14,26},{15,27},{16,4}... | collective-permute-start | bytes 983048 | tf_op jit(solution)/shard_map/ppermute | solution.py:98
  28.8 0.0 collective-permute-done.refs_1_
  28.8 0.0 copy-start.1
  28.8 1.6 %shard_map.68 = (f32[2,384,128]{2,1,0:T(8,128)S(1)}, f32[2,384,256]{2,1,0:T(8,128)S(1)}, f32[384,1]{1,0:T(8,128)S(1)}, bf16[3,256,128]{2,1,0:T(8,128)(2,1)S(1)},...) custom-call(bf16[400,1024]{1,0:T(8,128)(2,1)S(1)} %get-tuple-element.28.own.refs_0_, ...), custom_call_target="tpu_custom_call" | custom-call | tf_op jit(solution)/shard_map/pallas_call | solution.py:121
  30.4 0.0 copy-done.1
  30.4 4.4 %collective-permute-start.12 = (bf16[256,128]{1,0:T(8,128)(2,1)S(1)}, bf16[256,128]{1,0:T(8,128)(2,1)S(1)}, u32[]{:S(2)}, u32[]{:S(2)}) collective-permute-start(bf16[256,128]{1,0:T(8,128)(2,1)S(1)} %copy-done.1), channel_id=1, source_target_pairs={{0,12},{1,13},{2,14},{3,15},{4,4},{5,5},{6,6},{7,7},{8,8},{9,9},{1... | collective-permute-start | bytes 196616 | tf_op jit(solution)/shard_map/ppermute | solution.py:98
  34.8 0.0 collective-permute-done.2.hop.refs_2_
  34.8 0.1 collective-permute-start.14
  34.9 0.3 shard_map.69._.refs_4_
  35.1 0.0 collective-permute-done.3.hop.refs_3_
  35.1 0.3 shard_map.70.refs_5_
  35.4 0.0 collective-permute-done.6.refs_8_
  35.4 3.7 %collective-permute-done.7.refs_9_ = bf16[1152,256]{1,0:T(8,128)(2,1)S(1)} collective-permute-done((bf16[1152,256]{1,0:T(8,128)(2,1)S(1)}, bf16[1152,256]{1,0:T(8,128)(2,1)S(1)}, u32[]{:S(2)}, u32[]{:S(2)}) %collective-permute-start.7) | collective-permute-done | bytes 589856 | tf_op jit(solution)/shard_map/ppermute | solution.py:98
  39.1 0.7 %shard_map.71 = (f32[16,384]{1,0:T(8,128)S(1)}, f32[16,144]{1,0:T(8,128)S(1)}, f32[16,528]{1,0:T(8,128)S(1)}, bf16[256,128]{1,0:T(8,128)(2,1)S(1)}) custom-call(bf16[400,1024]{1,0:T(8,128)(2,1)S(1)} %get-tuple-element.28.own.refs_0_, bf16[400,1024]{1,0:T(8,128)(2,1)S(1)} %collective-permute-done.refs_1_, ...), custom_call_target="tpu_custom_call" | custom-call | flops 553648128 | bytes 5081088 | tf_op jit(solution)/shard_map/pallas_call | solution.py:121
  39.8 1.6 %collective-permute-start.8 = (f32[16,528]{1,0:T(8,128)S(1)}, f32[16,528]{1,0:T(8,128)S(1)}, u32[]{:S(2)}, u32[]{:S(2)}) collective-permute-start(f32[16,528]{1,0:T(8,128)S(1)} %get-tuple-element.42), channel_id=1, source_target_pairs={{0,16},{1,17},{2,18},{3,19},{4,20},{5,21},{6,22},{7,23},{8,24},{9,... | collective-permute-start | bytes 101384 | tf_op jit(solution)/shard_map/ppermute | solution.py:98
  41.4 2.5 %collective-permute-done.8.near = f32[16,528]{1,0:T(8,128)S(1)} collective-permute-done((f32[16,528]{1,0:T(8,128)S(1)}, f32[16,528]{1,0:T(8,128)S(1)}, u32[]{:S(2)}, u32[]{:S(2)}) %collective-permute-start.8) | collective-permute-done | bytes 33824 | tf_op jit(solution)/shard_map/ppermute | solution.py:98
  43.9 1.5 %collective-permute-start.9 = (f32[16,384]{1,0:T(8,128)S(1)}, f32[16,384]{1,0:T(8,128)S(1)}, u32[]{:S(2)}, u32[]{:S(2)}) collective-permute-start(f32[16,384]{1,0:T(8,128)S(1)} %get-tuple-element.43.low), channel_id=1, source_target_pairs={{0,2},{1,3},{2,0},{3,1},{4,6},{5,7},{6,4},{7,5},{8,10},{9,11},{10,... | collective-permute-start | bytes 73736 | tf_op jit(solution)/shard_map/ppermute | solution.py:98
  45.4 0.2 collective-permute-start.10
  45.6 1.8 %collective-permute-start.11 = (f32[16,144]{1,0:T(8,128)S(1)}, f32[16,144]{1,0:T(8,128)S(1)}, u32[]{:S(2)}, u32[]{:S(2)}) collective-permute-start(f32[16,144]{1,0:T(8,128)S(1)} %get-tuple-element.44), channel_id=1, source_target_pairs={{0,6},{1,7},{2,4},{3,5},{4,2},{5,3},{6,0},{7,1},{8,14},{9,15},{10,... | collective-permute-start | bytes 27656 | tf_op jit(solution)/shard_map/ppermute | solution.py:98
  47.4 0.0 collective-permute-done.12._.distant
  47.4 1.7 %collective-permute-done.10.hop = f32[16,144]{1,0:T(8,128)S(1)} collective-permute-done((f32[16,144]{1,0:T(8,128)S(1)}, f32[16,144]{1,0:T(8,128)S(1)}, u32[]{:S(2)}, u32[]{:S(2)}) %collective-permute-start.10) | collective-permute-done | bytes 9248 | tf_op jit(solution)/shard_map/ppermute | solution.py:98
  49.1 1.1 %collective-permute-done.11.hop_far = f32[16,144]{1,0:T(8,128)S(1)} collective-permute-done((f32[16,144]{1,0:T(8,128)S(1)}, f32[16,144]{1,0:T(8,128)S(1)}, u32[]{:S(2)}, u32[]{:S(2)}) %collective-permute-start.11) | collective-permute-done | bytes 9248 | tf_op jit(solution)/shard_map/ppermute | solution.py:98
  50.3 0.0 collective-permute-done.9.far
  50.3 0.2 shard_map.73.near
  50.4 0.0 collective-permute-start.13
  50.4 0.0 collective-permute-done.14.got
  50.4 1.2 %collective-permute-done.13.far = f32[16,384]{1,0:T(8,128)S(1)} collective-permute-done((f32[16,384]{1,0:T(8,128)S(1)}, f32[16,384]{1,0:T(8,128)S(1)}, u32[]{:S(2)}, u32[]{:S(2)}) %collective-permute-start.13) | collective-permute-done | bytes 24608 | tf_op jit(solution)/shard_map/ppermute | solution.py:98
  51.6 1.3 %shard_map.74 = bf16[384,128]{1,0:T(8,128)(2,1)} custom-call(f32[16,384]{1,0:T(8,128)S(1)} %shard_map.73.near, f32[16,384]{1,0:T(8,128)S(1)} %collective-permute-done.13.far, f32[384,128]{1,0:T(8,128)S(1)} %get-tuple-element.46.keep, f32[384,128]{1,0:T(8,128)S(1)} %collective-permute-done.14.got, f32[384,1]{1,0:T(8,128)S(1)} %get-tuple-element.48.numbers, ...), custom_call_target="tpu_custom_call" | custom-call | bytes 869888 | tf_op jit(solution)/shard_map/pallas_call | solution.py:121
  (1 shorter events, 0.0 us)
Async XLA Ops:
  1.1 7.5 %copy-start = (bf16[2048,512]{1,0:T(8,128)(2,1)S(1)}, bf16[2048,512]{1,0:T(8,128)(2,1)}, u32[]{:S(2)}) copy-start(bf16[2048,512]{1,0:T(8,128)(2,1)} %weights.1) | copy-start | bytes 6291460
  1.1 16.4 %collective-permute-start.1 = (bf16[1152,256]{1,0:T(8,128)(2,1)S(1)}, bf16[1152,256]{1,0:T(8,128)(2,1)S(1)}, u32[]{:S(2)}, u32[]{:S(2)}) collective-permute-start(bf16[1152,256]{1,0:T(8,128)(2,1)S(1)} %shard_map.64._.refs_2_), channel_id=1, source_target_pairs={{0,4},{1,5},{2,6},{3,7},{4,0},{5,1},{6,2},{7,3},{8,12},{9,13},{10,... | collective-permute-start | bytes 1769480 | tf_op jit(solution)/shard_map/ppermute | solution.py:98
  5.6 16.3 %collective-permute-start.4 = (bf16[1152,256]{1,0:T(8,128)(2,1)S(1)}, bf16[1152,256]{1,0:T(8,128)(2,1)S(1)}, u32[]{:S(2)}, u32[]{:S(2)}) collective-permute-start(bf16[1152,256]{1,0:T(8,128)(2,1)S(1)} %shard_map.64._.refs_2_), channel_id=1, source_target_pairs={{0,0},{1,1},{2,2},{3,3},{4,8},{5,9},{6,10},{7,11},{8,4},{9,5},{10,... | collective-permute-start | bytes 1769480 | tf_op jit(solution)/shard_map/ppermute | solution.py:98
  6.3 22.4 %collective-permute-start = (bf16[400,1024]{1,0:T(8,128)(2,1)S(1)}, bf16[400,1024]{1,0:T(8,128)(2,1)S(1)}, u32[]{:S(2)}, u32[]{:S(2)}) collective-permute-start(bf16[400,1024]{1,0:T(8,128)(2,1)S(1)} %get-tuple-element.29.away), channel_id=1, source_target_pairs={{0,16},{1,17},{2,18},{3,19},{4,20},{5,21},{6,22},{7,23},{8,24},{9,... | collective-permute-start | bytes 2457608 | tf_op jit(solution)/shard_map/ppermute | solution.py:98
  9.7 13.5 %collective-permute-start.5 = (f32[384,256]{1,0:T(8,128)S(1)}, f32[384,256]{1,0:T(8,128)S(1)}, u32[]{:S(2)}, u32[]{:S(2)}) collective-permute-start(f32[384,256]{1,0:T(8,128)S(1)} %get-tuple-element.36), channel_id=1, source_target_pairs={{0,2},{1,3},{2,0},{3,1},{4,6},{5,7},{6,4},{7,5},{8,10},{9,11},{10,... | collective-permute-start | bytes 1179656 | tf_op jit(solution)/shard_map/ppermute | solution.py:98
  17.5 17.3 %collective-permute-start.2 = (bf16[160,1024]{1,0:T(8,128)(2,1)S(1)}, bf16[160,1024]{1,0:T(8,128)(2,1)S(1)}, u32[]{:S(2)}, u32[]{:S(2)}) collective-permute-start(bf16[160,1024]{1,0:T(8,128)(2,1)S(1)} %get-tuple-element.31), channel_id=1, source_target_pairs={{0,4},{1,5},{2,6},{3,7},{12,8},{13,9},{14,10},{15,11},{16,20},{17,... | collective-permute-start | bytes 983048 | tf_op jit(solution)/shard_map/ppermute | solution.py:98
  21.2 14.3 %collective-permute-start.6 = (bf16[1152,256]{1,0:T(8,128)(2,1)S(1)}, bf16[1152,256]{1,0:T(8,128)(2,1)S(1)}, u32[]{:S(2)}, u32[]{:S(2)}) collective-permute-start(bf16[1152,256]{1,0:T(8,128)(2,1)S(1)} %collective-permute-done.1.refs_4_), channel_id=1, source_target_pairs={{0,0},{1,1},{2,2},{3,3},{4,8},{5,9},{6,10},{7,11},{8,4},{9,5},{10,... | collective-permute-start | bytes 1769480 | tf_op jit(solution)/shard_map/ppermute | solution.py:98
  21.9 17.2 %collective-permute-start.7 = (bf16[1152,256]{1,0:T(8,128)(2,1)S(1)}, bf16[1152,256]{1,0:T(8,128)(2,1)S(1)}, u32[]{:S(2)}, u32[]{:S(2)}) collective-permute-start(bf16[1152,256]{1,0:T(8,128)(2,1)S(1)} %collective-permute-done.4.refs_3_), channel_id=1, source_target_pairs={{4,0},{5,1},{6,2},{7,3},{8,12},{9,13},{10,14},{11,15},{20,16},{21,... | collective-permute-start | bytes 1769480 | tf_op jit(solution)/shard_map/ppermute | solution.py:98
  23.2 11.9 %collective-permute-start.3 = (bf16[160,1024]{1,0:T(8,128)(2,1)S(1)}, bf16[160,1024]{1,0:T(8,128)(2,1)S(1)}, u32[]{:S(2)}, u32[]{:S(2)}) collective-permute-start(bf16[160,1024]{1,0:T(8,128)(2,1)S(1)} %get-tuple-element.32), channel_id=1, source_target_pairs={{0,20},{1,21},{2,22},{3,23},{12,24},{13,25},{14,26},{15,27},{16,4}... | collective-permute-start | bytes 983048 | tf_op jit(solution)/shard_map/ppermute | solution.py:98
  28.8 1.6 %copy-start.1 = (bf16[256,128]{1,0:T(8,128)(2,1)S(1)}, bf16[256,128]{1,0:T(8,128)(2,1)}, u32[]{:S(2)}) copy-start(bf16[256,128]{1,0:T(8,128)(2,1)} %up.1) | copy-start | bytes 196612
  30.4 17.0 %collective-permute-start.12 = (bf16[256,128]{1,0:T(8,128)(2,1)S(1)}, bf16[256,128]{1,0:T(8,128)(2,1)S(1)}, u32[]{:S(2)}, u32[]{:S(2)}) collective-permute-start(bf16[256,128]{1,0:T(8,128)(2,1)S(1)} %copy-done.1), channel_id=1, source_target_pairs={{0,12},{1,13},{2,14},{3,15},{4,4},{5,5},{6,6},{7,7},{8,8},{9,9},{1... | collective-permute-start | bytes 196616 | tf_op jit(solution)/shard_map/ppermute | solution.py:98
  34.8 15.7 %collective-permute-start.14 = (f32[384,128]{1,0:T(8,128)S(1)}, f32[384,128]{1,0:T(8,128)S(1)}, u32[]{:S(2)}, u32[]{:S(2)}) collective-permute-start(f32[384,128]{1,0:T(8,128)S(1)} %get-tuple-element.47), channel_id=1, source_target_pairs={{0,1},{1,0},{2,3},{3,2},{4,5},{5,4},{6,7},{7,6},{8,9},{9,8},{10,11... | collective-permute-start | bytes 589832 | tf_op jit(solution)/shard_map/ppermute | solution.py:98
  39.8 4.1 %collective-permute-start.8 = (f32[16,528]{1,0:T(8,128)S(1)}, f32[16,528]{1,0:T(8,128)S(1)}, u32[]{:S(2)}, u32[]{:S(2)}) collective-permute-start(f32[16,528]{1,0:T(8,128)S(1)} %get-tuple-element.42), channel_id=1, source_target_pairs={{0,16},{1,17},{2,18},{3,19},{4,20},{5,21},{6,22},{7,23},{8,24},{9,... | collective-permute-start | bytes 101384 | tf_op jit(solution)/shard_map/ppermute | solution.py:98
  43.9 6.4 %collective-permute-start.9 = (f32[16,384]{1,0:T(8,128)S(1)}, f32[16,384]{1,0:T(8,128)S(1)}, u32[]{:S(2)}, u32[]{:S(2)}) collective-permute-start(f32[16,384]{1,0:T(8,128)S(1)} %get-tuple-element.43.low), channel_id=1, source_target_pairs={{0,2},{1,3},{2,0},{3,1},{4,6},{5,7},{6,4},{7,5},{8,10},{9,11},{10,... | collective-permute-start | bytes 73736 | tf_op jit(solution)/shard_map/ppermute | solution.py:98
  45.4 3.7 %collective-permute-start.10 = (f32[16,144]{1,0:T(8,128)S(1)}, f32[16,144]{1,0:T(8,128)S(1)}, u32[]{:S(2)}, u32[]{:S(2)}) collective-permute-start(f32[16,144]{1,0:T(8,128)S(1)} %get-tuple-element.44), channel_id=1, source_target_pairs={{0,4},{1,5},{2,6},{3,7},{4,0},{5,1},{6,2},{7,3},{8,12},{9,13},{10,... | collective-permute-start | bytes 27656 | tf_op jit(solution)/shard_map/ppermute | solution.py:98
  45.6 4.6 %collective-permute-start.11 = (f32[16,144]{1,0:T(8,128)S(1)}, f32[16,144]{1,0:T(8,128)S(1)}, u32[]{:S(2)}, u32[]{:S(2)}) collective-permute-start(f32[16,144]{1,0:T(8,128)S(1)} %get-tuple-element.44), channel_id=1, source_target_pairs={{0,6},{1,7},{2,4},{3,5},{4,2},{5,3},{6,0},{7,1},{8,14},{9,15},{10,... | collective-permute-start | bytes 27656 | tf_op jit(solution)/shard_map/ppermute | solution.py:98
  50.4 1.2 %collective-permute-start.13 = (f32[16,384]{1,0:T(8,128)S(1)}, f32[16,384]{1,0:T(8,128)S(1)}, u32[]{:S(2)}, u32[]{:S(2)}) collective-permute-start(f32[16,384]{1,0:T(8,128)S(1)} %shard_map.73.near), channel_id=1, source_target_pairs={{0,1},{1,0},{2,3},{3,2},{4,5},{5,4},{6,7},{7,6},{8,9},{9,8},{10,11... | collective-permute-start | bytes 73736 | tf_op jit(solution)/shard_map/ppermute | solution.py:98

commit v17 on v16

--- a/solution.py
+++ b/solution.py
@@ -328,12 +328,15 @@
 
 def near_body(low, hop_low, near, low_out, hop_out):
     rows = low.shape[1]
+    capacity = hop_low.shape[1]
     low_out[...] = low[...] + near[:, :rows]
-    hop_out[...] = hop_low[...] + near[:, rows:]
-
-
-def merge_body(low, far, places, hop, hop_far, _, out):
-    back = hop[...] + hop_far[...]
+    hop_out[...] = jnp.zeros(hop_out.shape, jnp.float32)
+    hop_out[:, :capacity] = hop_low[...] + near[:, rows:]
+
+
+def merge_body(low, far, places, hop_far, hop, _, out):
+    capacity = places.shape[0]
+    back = hop[:, :capacity] + hop_far[:, :capacity]
     spread = jnp.zeros(low.shape, jnp.float32)
     for _ in range(3):
         piece = back.astype(jnp.bfloat16)
@@ -480,7 +483,9 @@
     near = exchange(away, 1, 0, SAME)
     distant = exchange(after(stacked_up_weight, folded), 0, 0, ENDS)
     low, hop_low = kernel(
-        near_body, [wide(ADAPTER_RANK, rows), wide(ADAPTER_RANK, capacity)], (low, hop_low, near)
+        near_body,
+        [wide(ADAPTER_RANK, rows), wide(ADAPTER_RANK, rows + LANES)],
+        (low, hop_low, near),
     )
     back = exchange(hop_low, 0, 0, BESIDE)
     back_far = exchange(hop_low, 0, 2, BESIDE)
@@ -488,7 +493,7 @@
     low = kernel(
         merge_body,
         wide(ADAPTER_RANK, rows),
-        (low, low_far, places, back, back_far, distant),
+        (low, low_far, places, back_far, back, distant),
         0,
         (None, None, None, None, None, pl.ANY),
     )

time: 53.1 us -> 54.1 us (1.019)
  waiting for transfers between devices: 16.5 us -> 17.5 us
    ppermute x15, waiting for transfers between devices: 16.5 us -> 17.5 us  [exchange(): return lax.ppermute(x, AXES, pairs)]
  transfers between devices with their start and end apart: 15 -> 15, of which waited for: 6 -> 5; matrix products, arithmetic and copies ran while one was open for 0% -> 0% of each run, Pallas kernels for 12% -> 11%
where the time goes in v17:
time: 54.1 us; the launch traced here: 53.9 us
  starting transfers between devices  27.7 us (51%)
  waiting for transfers between devices  17.5 us (32%)
  Pallas kernels  8.46 us (16%)
    ppermute x15, starting transfers between devices, exchange(): return lax.ppermute(x, AXES, pairs)  27.7 us
    ppermute x15, waiting for transfers between devices, exchange(): return lax.ppermute(x, AXES, pairs)  17.5 us
    pallas_call x11, Pallas kernels, kernel(): pl.pallas_call(body, out_shape=outs, in_specs=specs or [inner] * len(oper...  8.46 us
  transfers between devices with their start and end apart: 15, of which 5 were waited for; matrix products, arithmetic and copies ran while one was open for 0% of the time, Pallas kernels for 11%

profile of v17, /device:TPU:0, one launch (start us, length us, event | category | flops | bytes accessed | tf_op | source)
XLA Modules:
  0.0 53.9 jit_solution(17863973288305439273)
XLA Ops:
  0.0 1.1 %shard_map.64._.refs_2_ = bf16[1152,256]{1,0:T(8,128)(2,1)S(1)} custom-call(bf16[2048,256]{1,0:T(8,128)(2,1)} %down.1, bf16[256,128]{1,0:T(8,128)(2,1)} %up.1), custom_call_target="tpu_custom_call" | custom-call | bytes 1703936 | tf_op jit(solution)/shard_map/pallas_call | solution.py:121
  1.1 0.0 copy-start
  1.1 3.1 %collective-permute-start.1 = (bf16[1152,256]{1,0:T(8,128)(2,1)S(1)}, bf16[1152,256]{1,0:T(8,128)(2,1)S(1)}, u32[]{:S(2)}, u32[]{:S(2)}) collective-permute-start(bf16[1152,256]{1,0:T(8,128)(2,1)S(1)} %shard_map.64._.refs_2_), channel_id=1, source_target_pairs={{0,4},{1,5},{2,6},{3,7},{4,0},{5,1},{6,2},{7,3},{8,12},{9,13},{10,... | collective-permute-start | bytes 1769480 | tf_op jit(solution)/shard_map/ppermute | solution.py:98
  4.2 1.4 %shard_map.65 = (bf16[400,1024]{1,0:T(8,128)(2,1)S(1)}, bf16[400,1024]{1,0:T(8,128)(2,1)S(1)}) custom-call(bf16[384,2048]{1,0:T(8,128)(2,1)} %tokens.1, s32[1,384]{1,0:T(1,128)} %bitcast.1, s32[384]{0:T(512)} %slot_in.1, bf16[1152,256]{1,0:T(8,128)(2,1)S(1)} %shard_map.64._.refs_2_), custom_call_target="tpu_custom_call" | custom-call | bytes 3804160 | tf_op jit(solution)/shard_map/pallas_call | solution.py:121
  5.6 0.7 %collective-permute-start.4 = (bf16[1152,256]{1,0:T(8,128)(2,1)S(1)}, bf16[1152,256]{1,0:T(8,128)(2,1)S(1)}, u32[]{:S(2)}, u32[]{:S(2)}) collective-permute-start(bf16[1152,256]{1,0:T(8,128)(2,1)S(1)} %shard_map.64._.refs_2_), channel_id=1, source_target_pairs={{0,0},{1,1},{2,2},{3,3},{4,8},{5,9},{6,10},{7,11},{8,4},{9,5},{10,... | collective-permute-start | bytes 1769480 | tf_op jit(solution)/shard_map/ppermute | solution.py:98
  6.3 1.6 %collective-permute-start = (bf16[400,1024]{1,0:T(8,128)(2,1)S(1)}, bf16[400,1024]{1,0:T(8,128)(2,1)S(1)}, u32[]{:S(2)}, u32[]{:S(2)}) collective-permute-start(bf16[400,1024]{1,0:T(8,128)(2,1)S(1)} %get-tuple-element.29.away), channel_id=1, source_target_pairs={{0,16},{1,17},{2,18},{3,19},{4,20},{5,21},{6,22},{7,23},{8,24},{9,... | collective-permute-start | bytes 2457608 | tf_op jit(solution)/shard_map/ppermute | solution.py:98
  7.9 0.7 %shard_map.66 = (bf16[160,1024]{1,0:T(8,128)(2,1)S(1)}, bf16[160,1024]{1,0:T(8,128)(2,1)S(1)}, bf16[144,384]{1,0:T(8,128)(2,1)S(1)}) custom-call(bf16[400,1024]{1,0:T(8,128)(2,1)S(1)} %get-tuple-element.28.own.refs_0_, bf16[400,1024]{1,0:T(8,128)(2,1)S(1)} %get-tuple-element.29.away), custom_call_target="tpu_custom_call" | custom-call | flops 226492416 | bytes 2404352 | tf_op jit(solution)/shard_map/pallas_call | solution.py:121
  8.6 0.0 copy-done
  8.6 1.1 %shard_map.67 = (f32[384,256]{1,0:T(8,128)S(1)}, f32[384,256]{1,0:T(8,128)S(1)}) custom-call(bf16[400,1024]{1,0:T(8,128)(2,1)S(1)} %get-tuple-element.28.own.refs_0_, bf16[400,1024]{1,0:T(8,128)(2,1)S(1)} %get-tuple-element.29.away, bf16[2048,512]{1,0:T(8,128)(2,1)S(1)} %copy-done, bf16[144,384]{1,0:T(8,128)(2,1)S(1)} %get-tuple-element.34._.places), custom_call_target="tpu_custom_call" | custom-call | flops 805306368 | bytes 4632576 | tf_op jit(solution)/shard_map/pallas_call | solution.py:121
  9.7 1.6 %collective-permute-start.5 = (f32[384,256]{1,0:T(8,128)S(1)}, f32[384,256]{1,0:T(8,128)S(1)}, u32[]{:S(2)}, u32[]{:S(2)}) collective-permute-start(f32[384,256]{1,0:T(8,128)S(1)} %get-tuple-element.36), channel_id=1, source_target_pairs={{0,2},{1,3},{2,0},{3,1},{4,6},{5,7},{6,4},{7,5},{8,10},{9,11},{10,... | collective-permute-start | bytes 1179656 | tf_op jit(solution)/shard_map/ppermute | solution.py:98
  11.2 6.3 %collective-permute-done.1.refs_4_ = bf16[1152,256]{1,0:T(8,128)(2,1)S(1)} collective-permute-done((bf16[1152,256]{1,0:T(8,128)(2,1)S(1)}, bf16[1152,256]{1,0:T(8,128)(2,1)S(1)}, u32[]{:S(2)}, u32[]{:S(2)}) %collective-permute-start.1) | collective-permute-done | bytes 589856 | tf_op jit(solution)/shard_map/ppermute | solution.py:98
  17.5 3.7 %collective-permute-start.2 = (bf16[160,1024]{1,0:T(8,128)(2,1)S(1)}, bf16[160,1024]{1,0:T(8,128)(2,1)S(1)}, u32[]{:S(2)}, u32[]{:S(2)}) collective-permute-start(bf16[160,1024]{1,0:T(8,128)(2,1)S(1)} %get-tuple-element.31), channel_id=1, source_target_pairs={{0,4},{1,5},{2,6},{3,7},{12,8},{13,9},{14,10},{15,11},{16,20},{17,... | collective-permute-start | bytes 983048 | tf_op jit(solution)/shard_map/ppermute | solution.py:98
  21.2 0.7 %collective-permute-start.6 = (bf16[1152,256]{1,0:T(8,128)(2,1)S(1)}, bf16[1152,256]{1,0:T(8,128)(2,1)S(1)}, u32[]{:S(2)}, u32[]{:S(2)}) collective-permute-start(bf16[1152,256]{1,0:T(8,128)(2,1)S(1)} %collective-permute-done.1.refs_4_), channel_id=1, source_target_pairs={{0,0},{1,1},{2,2},{3,3},{4,8},{5,9},{6,10},{7,11},{8,4},{9,5},{10,... | collective-permute-start | bytes 1769480 | tf_op jit(solution)/shard_map/ppermute | solution.py:98
  21.9 0.0 collective-permute-done.4.refs_3_
  21.9 1.3 %collective-permute-start.7 = (bf16[1152,256]{1,0:T(8,128)(2,1)S(1)}, bf16[1152,256]{1,0:T(8,128)(2,1)S(1)}, u32[]{:S(2)}, u32[]{:S(2)}) collective-permute-start(bf16[1152,256]{1,0:T(8,128)(2,1)S(1)} %collective-permute-done.4.refs_3_), channel_id=1, source_target_pairs={{4,0},{5,1},{6,2},{7,3},{8,12},{9,13},{10,14},{11,15},{20,16},{21,... | collective-permute-start | bytes 1769480 | tf_op jit(solution)/shard_map/ppermute | solution.py:98
  23.2 0.0 collective-permute-done.5.refs_6_
  23.2 5.6 %collective-permute-start.3 = (bf16[160,1024]{1,0:T(8,128)(2,1)S(1)}, bf16[160,1024]{1,0:T(8,128)(2,1)S(1)}, u32[]{:S(2)}, u32[]{:S(2)}) collective-permute-start(bf16[160,1024]{1,0:T(8,128)(2,1)S(1)} %get-tuple-element.32), channel_id=1, source_target_pairs={{0,20},{1,21},{2,22},{3,23},{12,24},{13,25},{14,26},{15,27},{16,4}... | collective-permute-start | bytes 983048 | tf_op jit(solution)/shard_map/ppermute | solution.py:98
  28.8 0.0 collective-permute-done.refs_1_
  28.8 1.6 %shard_map.68 = (f32[2,384,128]{2,1,0:T(8,128)S(1)}, f32[2,384,256]{2,1,0:T(8,128)S(1)}, f32[384,1]{1,0:T(8,128)S(1)}, bf16[3,256,128]{2,1,0:T(8,128)(2,1)S(1)},...) custom-call(bf16[400,1024]{1,0:T(8,128)(2,1)S(1)} %get-tuple-element.28.own.refs_0_, ...), custom_call_target="tpu_custom_call" | custom-call | tf_op jit(solution)/shard_map/pallas_call | solution.py:121
  30.4 0.1 collective-permute-start.14
  30.4 0.0 collective-permute-done.2.hop.refs_2_
  30.4 0.3 shard_map.69._.refs_4_
  30.7 3.6 %collective-permute-done.3.hop.refs_3_ = bf16[160,1024]{1,0:T(8,128)(2,1)S(1)} collective-permute-done((bf16[160,1024]{1,0:T(8,128)(2,1)S(1)}, bf16[160,1024]{1,0:T(8,128)(2,1)S(1)}, u32[]{:S(2)}, u32[]{:S(2)}) %collective-permute-start.3) | collective-permute-done | bytes 327712 | tf_op jit(solution)/shard_map/ppermute | solution.py:98
  34.3 0.3 shard_map.70.refs_5_
  34.6 0.0 collective-permute-done.6.refs_8_
  34.6 3.1 %collective-permute-done.7.refs_9_ = bf16[1152,256]{1,0:T(8,128)(2,1)S(1)} collective-permute-done((bf16[1152,256]{1,0:T(8,128)(2,1)S(1)}, bf16[1152,256]{1,0:T(8,128)(2,1)S(1)}, u32[]{:S(2)}, u32[]{:S(2)}) %collective-permute-start.7) | collective-permute-done | bytes 589856 | tf_op jit(solution)/shard_map/ppermute | solution.py:98
  37.7 0.0 copy-start.1
  37.7 0.7 %shard_map.71 = (f32[16,384]{1,0:T(8,128)S(1)}, f32[16,144]{1,0:T(8,128)S(1)}, f32[16,528]{1,0:T(8,128)S(1)}, bf16[256,128]{1,0:T(8,128)(2,1)S(1)}) custom-call(bf16[400,1024]{1,0:T(8,128)(2,1)S(1)} %get-tuple-element.28.own.refs_0_, bf16[400,1024]{1,0:T(8,128)(2,1)S(1)} %collective-permute-done.refs_1_, ...), custom_call_target="tpu_custom_call" | custom-call | flops 553648128 | bytes 5081088 | tf_op jit(solution)/shard_map/pallas_call | solution.py:121
  38.4 1.6 %collective-permute-start.8 = (f32[16,528]{1,0:T(8,128)S(1)}, f32[16,528]{1,0:T(8,128)S(1)}, u32[]{:S(2)}, u32[]{:S(2)}) collective-permute-start(f32[16,528]{1,0:T(8,128)S(1)} %get-tuple-element.42), channel_id=1, source_target_pairs={{0,16},{1,17},{2,18},{3,19},{4,20},{5,21},{6,22},{7,23},{8,24},{9,... | collective-permute-start | bytes 101384 | tf_op jit(solution)/shard_map/ppermute | solution.py:98
  40.0 0.0 copy-done.1
  40.0 4.4 %collective-permute-start.12 = (bf16[256,128]{1,0:T(8,128)(2,1)S(1)}, bf16[256,128]{1,0:T(8,128)(2,1)S(1)}, u32[]{:S(2)}, u32[]{:S(2)}) collective-permute-start(bf16[256,128]{1,0:T(8,128)(2,1)S(1)} %copy-done.1), channel_id=1, source_target_pairs={{0,12},{1,13},{2,14},{3,15},{4,4},{5,5},{6,6},{7,7},{8,8},{9,9},{1... | collective-permute-start | bytes 196616 | tf_op jit(solution)/shard_map/ppermute | solution.py:98
  44.3 0.0 collective-permute-done.8.near
  44.4 0.8 %collective-permute-start.10 = (f32[16,512]{1,0:T(8,128)S(1)}, f32[16,512]{1,0:T(8,128)S(1)}, u32[]{:S(2)}, u32[]{:S(2)}) collective-permute-start(f32[16,512]{1,0:T(8,128)S(1)} %get-tuple-element.44), channel_id=1, source_target_pairs={{0,6},{1,7},{2,4},{3,5},{4,2},{5,3},{6,0},{7,1},{8,14},{9,15},{10,... | collective-permute-start | bytes 98312 | tf_op jit(solution)/shard_map/ppermute | solution.py:98
  45.2 2.2 %collective-permute-start.11 = (f32[16,512]{1,0:T(8,128)S(1)}, f32[16,512]{1,0:T(8,128)S(1)}, u32[]{:S(2)}, u32[]{:S(2)}) collective-permute-start(f32[16,512]{1,0:T(8,128)S(1)} %get-tuple-element.44), channel_id=1, source_target_pairs={{0,4},{1,5},{2,6},{3,7},{4,0},{5,1},{6,2},{7,3},{8,12},{9,13},{10,... | collective-permute-start | bytes 98312 | tf_op jit(solution)/shard_map/ppermute | solution.py:98
  47.4 0.5 collective-permute-start.9
  47.9 0.0 collective-permute-done.12._.distant
  48.0 3.3 %collective-permute-done.9.far = f32[16,384]{1,0:T(8,128)S(1)} collective-permute-done((f32[16,384]{1,0:T(8,128)S(1)}, f32[16,384]{1,0:T(8,128)S(1)}, u32[]{:S(2)}, u32[]{:S(2)}) %collective-permute-start.9) | collective-permute-done | bytes 24608 | tf_op jit(solution)/shard_map/ppermute | solution.py:98
  51.2 0.0 collective-permute-done.10.hop_far
  51.2 0.0 collective-permute-done.11.hop
  51.2 0.2 shard_map.73.near
  51.4 0.0 collective-permute-start.13
  51.4 0.0 collective-permute-done.14.got
  51.4 1.2 %collective-permute-done.13.far = f32[16,384]{1,0:T(8,128)S(1)} collective-permute-done((f32[16,384]{1,0:T(8,128)S(1)}, f32[16,384]{1,0:T(8,128)S(1)}, u32[]{:S(2)}, u32[]{:S(2)}) %collective-permute-start.13) | collective-permute-done | bytes 24608 | tf_op jit(solution)/shard_map/ppermute | solution.py:98
  52.6 1.3 %shard_map.74 = bf16[384,128]{1,0:T(8,128)(2,1)} custom-call(f32[16,384]{1,0:T(8,128)S(1)} %shard_map.73.near, f32[16,384]{1,0:T(8,128)S(1)} %collective-permute-done.13.far, f32[384,128]{1,0:T(8,128)S(1)} %get-tuple-element.46.keep, f32[384,128]{1,0:T(8,128)S(1)} %collective-permute-done.14.got, f32[384,1]{1,0:T(8,128)S(1)} %get-tuple-element.48.numbers, ...), custom_call_target="tpu_custom_call" | custom-call | bytes 869888 | tf_op jit(solution)/shard_map/pallas_call | solution.py:121
  (1 shorter events, 0.0 us)
Async XLA Ops:
  1.1 7.5 %copy-start = (bf16[2048,512]{1,0:T(8,128)(2,1)S(1)}, bf16[2048,512]{1,0:T(8,128)(2,1)}, u32[]{:S(2)}) copy-start(bf16[2048,512]{1,0:T(8,128)(2,1)} %weights.1) | copy-start | bytes 6291460
  1.1 16.4 %collective-permute-start.1 = (bf16[1152,256]{1,0:T(8,128)(2,1)S(1)}, bf16[1152,256]{1,0:T(8,128)(2,1)S(1)}, u32[]{:S(2)}, u32[]{:S(2)}) collective-permute-start(bf16[1152,256]{1,0:T(8,128)(2,1)S(1)} %shard_map.64._.refs_2_), channel_id=1, source_target_pairs={{0,4},{1,5},{2,6},{3,7},{4,0},{5,1},{6,2},{7,3},{8,12},{9,13},{10,... | collective-permute-start | bytes 1769480 | tf_op jit(solution)/shard_map/ppermute | solution.py:98
  5.6 16.3 %collective-permute-start.4 = (bf16[1152,256]{1,0:T(8,128)(2,1)S(1)}, bf16[1152,256]{1,0:T(8,128)(2,1)S(1)}, u32[]{:S(2)}, u32[]{:S(2)}) collective-permute-start(bf16[1152,256]{1,0:T(8,128)(2,1)S(1)} %shard_map.64._.refs_2_), channel_id=1, source_target_pairs={{0,0},{1,1},{2,2},{3,3},{4,8},{5,9},{6,10},{7,11},{8,4},{9,5},{10,... | collective-permute-start | bytes 1769480 | tf_op jit(solution)/shard_map/ppermute | solution.py:98
  6.3 22.4 %collective-permute-start = (bf16[400,1024]{1,0:T(8,128)(2,1)S(1)}, bf16[400,1024]{1,0:T(8,128)(2,1)S(1)}, u32[]{:S(2)}, u32[]{:S(2)}) collective-permute-start(bf16[400,1024]{1,0:T(8,128)(2,1)S(1)} %get-tuple-element.29.away), channel_id=1, source_target_pairs={{0,16},{1,17},{2,18},{3,19},{4,20},{5,21},{6,22},{7,23},{8,24},{9,... | collective-permute-start | bytes 2457608 | tf_op jit(solution)/shard_map/ppermute | solution.py:98
  9.7 13.5 %collective-permute-start.5 = (f32[384,256]{1,0:T(8,128)S(1)}, f32[384,256]{1,0:T(8,128)S(1)}, u32[]{:S(2)}, u32[]{:S(2)}) collective-permute-start(f32[384,256]{1,0:T(8,128)S(1)} %get-tuple-element.36), channel_id=1, source_target_pairs={{0,2},{1,3},{2,0},{3,1},{4,6},{5,7},{6,4},{7,5},{8,10},{9,11},{10,... | collective-permute-start | bytes 1179656 | tf_op jit(solution)/shard_map/ppermute | solution.py:98
  17.5 12.9 %collective-permute-start.2 = (bf16[160,1024]{1,0:T(8,128)(2,1)S(1)}, bf16[160,1024]{1,0:T(8,128)(2,1)S(1)}, u32[]{:S(2)}, u32[]{:S(2)}) collective-permute-start(bf16[160,1024]{1,0:T(8,128)(2,1)S(1)} %get-tuple-element.31), channel_id=1, source_target_pairs={{0,4},{1,5},{2,6},{3,7},{12,8},{13,9},{14,10},{15,11},{16,20},{17,... | collective-permute-start | bytes 983048 | tf_op jit(solution)/shard_map/ppermute | solution.py:98
  21.2 13.4 %collective-permute-start.6 = (bf16[1152,256]{1,0:T(8,128)(2,1)S(1)}, bf16[1152,256]{1,0:T(8,128)(2,1)S(1)}, u32[]{:S(2)}, u32[]{:S(2)}) collective-permute-start(bf16[1152,256]{1,0:T(8,128)(2,1)S(1)} %collective-permute-done.1.refs_4_), channel_id=1, source_target_pairs={{0,0},{1,1},{2,2},{3,3},{4,8},{5,9},{6,10},{7,11},{8,4},{9,5},{10,... | collective-permute-start | bytes 1769480 | tf_op jit(solution)/shard_map/ppermute | solution.py:98
  21.9 15.8 %collective-permute-start.7 = (bf16[1152,256]{1,0:T(8,128)(2,1)S(1)}, bf16[1152,256]{1,0:T(8,128)(2,1)S(1)}, u32[]{:S(2)}, u32[]{:S(2)}) collective-permute-start(bf16[1152,256]{1,0:T(8,128)(2,1)S(1)} %collective-permute-done.4.refs_3_), channel_id=1, source_target_pairs={{4,0},{5,1},{6,2},{7,3},{8,12},{9,13},{10,14},{11,15},{20,16},{21,... | collective-permute-start | bytes 1769480 | tf_op jit(solution)/shard_map/ppermute | solution.py:98
  23.2 11.1 %collective-permute-start.3 = (bf16[160,1024]{1,0:T(8,128)(2,1)S(1)}, bf16[160,1024]{1,0:T(8,128)(2,1)S(1)}, u32[]{:S(2)}, u32[]{:S(2)}) collective-permute-start(bf16[160,1024]{1,0:T(8,128)(2,1)S(1)} %get-tuple-element.32), channel_id=1, source_target_pairs={{0,20},{1,21},{2,22},{3,23},{12,24},{13,25},{14,26},{15,27},{16,4}... | collective-permute-start | bytes 983048 | tf_op jit(solution)/shard_map/ppermute | solution.py:98
  30.4 21.0 %collective-permute-start.14 = (f32[384,128]{1,0:T(8,128)S(1)}, f32[384,128]{1,0:T(8,128)S(1)}, u32[]{:S(2)}, u32[]{:S(2)}) collective-permute-start(f32[384,128]{1,0:T(8,128)S(1)} %get-tuple-element.47), channel_id=1, source_target_pairs={{0,1},{1,0},{2,3},{3,2},{4,5},{5,4},{6,7},{7,6},{8,9},{9,8},{10,11... | collective-permute-start | bytes 589832 | tf_op jit(solution)/shard_map/ppermute | solution.py:98
  37.7 2.3 %copy-start.1 = (bf16[256,128]{1,0:T(8,128)(2,1)S(1)}, bf16[256,128]{1,0:T(8,128)(2,1)}, u32[]{:S(2)}) copy-start(bf16[256,128]{1,0:T(8,128)(2,1)} %up.1) | copy-start | bytes 196612
  38.4 6.0 %collective-permute-start.8 = (f32[16,528]{1,0:T(8,128)S(1)}, f32[16,528]{1,0:T(8,128)S(1)}, u32[]{:S(2)}, u32[]{:S(2)}) collective-permute-start(f32[16,528]{1,0:T(8,128)S(1)} %get-tuple-element.42), channel_id=1, source_target_pairs={{0,16},{1,17},{2,18},{3,19},{4,20},{5,21},{6,22},{7,23},{8,24},{9,... | collective-permute-start | bytes 101384 | tf_op jit(solution)/shard_map/ppermute | solution.py:98
  40.0 8.0 %collective-permute-start.12 = (bf16[256,128]{1,0:T(8,128)(2,1)S(1)}, bf16[256,128]{1,0:T(8,128)(2,1)S(1)}, u32[]{:S(2)}, u32[]{:S(2)}) collective-permute-start(bf16[256,128]{1,0:T(8,128)(2,1)S(1)} %copy-done.1), channel_id=1, source_target_pairs={{0,12},{1,13},{2,14},{3,15},{4,4},{5,5},{6,6},{7,7},{8,8},{9,9},{1... | collective-permute-start | bytes 196616 | tf_op jit(solution)/shard_map/ppermute | solution.py:98
  44.4 6.8 %collective-permute-start.10 = (f32[16,512]{1,0:T(8,128)S(1)}, f32[16,512]{1,0:T(8,128)S(1)}, u32[]{:S(2)}, u32[]{:S(2)}) collective-permute-start(f32[16,512]{1,0:T(8,128)S(1)} %get-tuple-element.44), channel_id=1, source_target_pairs={{0,6},{1,7},{2,4},{3,5},{4,2},{5,3},{6,0},{7,1},{8,14},{9,15},{10,... | collective-permute-start | bytes 98312 | tf_op jit(solution)/shard_map/ppermute | solution.py:98
  45.2 6.1 %collective-permute-start.11 = (f32[16,512]{1,0:T(8,128)S(1)}, f32[16,512]{1,0:T(8,128)S(1)}, u32[]{:S(2)}, u32[]{:S(2)}) collective-permute-start(f32[16,512]{1,0:T(8,128)S(1)} %get-tuple-element.44), channel_id=1, source_target_pairs={{0,4},{1,5},{2,6},{3,7},{4,0},{5,1},{6,2},{7,3},{8,12},{9,13},{10,... | collective-permute-start | bytes 98312 | tf_op jit(solution)/shard_map/ppermute | solution.py:98
  47.4 3.8 %collective-permute-start.9 = (f32[16,384]{1,0:T(8,128)S(1)}, f32[16,384]{1,0:T(8,128)S(1)}, u32[]{:S(2)}, u32[]{:S(2)}) collective-permute-start(f32[16,384]{1,0:T(8,128)S(1)} %get-tuple-element.43.low), channel_id=1, source_target_pairs={{0,2},{1,3},{2,0},{3,1},{4,6},{5,7},{6,4},{7,5},{8,10},{9,11},{10,... | collective-permute-start | bytes 73736 | tf_op jit(solution)/shard_map/ppermute | solution.py:98
  51.4 1.2 %collective-permute-start.13 = (f32[16,384]{1,0:T(8,128)S(1)}, f32[16,384]{1,0:T(8,128)S(1)}, u32[]{:S(2)}, u32[]{:S(2)}) collective-permute-start(f32[16,384]{1,0:T(8,128)S(1)} %shard_map.73.near), channel_id=1, source_target_pairs={{0,1},{1,0},{2,3},{3,2},{4,5},{5,4},{6,7},{7,6},{8,9},{9,8},{10,11... | collective-permute-start | bytes 73736 | tf_op jit(solution)/shard_map/ppermute | solution.py:98

commit v18 on v17

--- a/solution.py
+++ b/solution.py
@@ -334,7 +334,7 @@
     hop_out[:, :capacity] = hop_low[...] + near[:, rows:]
 
 
-def merge_body(low, far, places, hop_far, hop, _, out):
+def merge_body(low, far, places, hop_far, hop, out):
     capacity = places.shape[0]
     back = hop[:, :capacity] + hop_far[:, :capacity]
     spread = jnp.zeros(low.shape, jnp.float32)
@@ -458,6 +458,7 @@
         scratch=[pltpu.VMEM((rows, 2 * keys), jnp.float32)],
         light=True,
     )
+    distant = exchange(after(stacked_up_weight, folded), 0, 0, ENDS)
     hop_masks, latest = [], folded
     for hop, urgency in zip(hops, HOP_URGENCY):
         latest = kernel(
@@ -481,11 +482,10 @@
     )
 
     near = exchange(away, 1, 0, SAME)
-    distant = exchange(after(stacked_up_weight, folded), 0, 0, ENDS)
     low, hop_low = kernel(
         near_body,
         [wide(ADAPTER_RANK, rows), wide(ADAPTER_RANK, rows + LANES)],
-        (low, hop_low, near),
+        (low, hop_low, after(near, distant)),
     )
     back = exchange(hop_low, 0, 0, BESIDE)
     back_far = exchange(hop_low, 0, 2, BESIDE)
@@ -493,9 +493,7 @@
     low = kernel(
         merge_body,
         wide(ADAPTER_RANK, rows),
-        (low, low_far, places, back_far, back, distant),
-        0,
-        (None, None, None, None, None, pl.ANY),
+        (low, low_far, places, back_far, back),
     )
     got = exchange(give, 0, 1, SAME)
     low_far = exchange(low, 0, 1, SAME)

time: 54.1 us -> 53.6 us (level)
  waiting for transfers between devices: 17.5 us -> 16.9 us
where the time goes in v18:
time: 53.6 us; the launch traced here: 53.3 us
  starting transfers between devices  27.7 us (52%)
  waiting for transfers between devices  16.9 us (32%)
  Pallas kernels  8.46 us (16%)
    ppermute x15, starting transfers between devices, exchange(): return lax.ppermute(x, AXES, pairs)  27.7 us
    ppermute x15, waiting for transfers between devices, exchange(): return lax.ppermute(x, AXES, pairs)  16.9 us
    pallas_call x11, Pallas kernels, kernel(): pl.pallas_call(body, out_shape=outs, in_specs=specs or [inner] * len(oper...  8.46 us
  transfers between devices with their start and end apart: 15, of which 5 were waited for; matrix products, arithmetic and copies ran while one was open for 0% of the time, Pallas kernels for 11%

profile of v18, /device:TPU:0, one launch (start us, length us, event | category | flops | bytes accessed | tf_op | source)
XLA Modules:
  0.0 53.3 jit_solution(12988713287312090547)
XLA Ops:
  0.0 1.1 %shard_map.64._.refs_2_ = bf16[1152,256]{1,0:T(8,128)(2,1)S(1)} custom-call(bf16[2048,256]{1,0:T(8,128)(2,1)} %down.1, bf16[256,128]{1,0:T(8,128)(2,1)} %up.1), custom_call_target="tpu_custom_call" | custom-call | bytes 1703936 | tf_op jit(solution)/shard_map/pallas_call | solution.py:121
  1.1 0.0 copy-start
  1.1 3.1 %collective-permute-start.1 = (bf16[1152,256]{1,0:T(8,128)(2,1)S(1)}, bf16[1152,256]{1,0:T(8,128)(2,1)S(1)}, u32[]{:S(2)}, u32[]{:S(2)}) collective-permute-start(bf16[1152,256]{1,0:T(8,128)(2,1)S(1)} %shard_map.64._.refs_2_), channel_id=1, source_target_pairs={{0,4},{1,5},{2,6},{3,7},{4,0},{5,1},{6,2},{7,3},{8,12},{9,13},{10,... | collective-permute-start | bytes 1769480 | tf_op jit(solution)/shard_map/ppermute | solution.py:98
  4.2 1.4 %shard_map.65 = (bf16[400,1024]{1,0:T(8,128)(2,1)S(1)}, bf16[400,1024]{1,0:T(8,128)(2,1)S(1)}) custom-call(bf16[384,2048]{1,0:T(8,128)(2,1)} %tokens.1, s32[1,384]{1,0:T(1,128)} %bitcast.1, s32[384]{0:T(512)} %slot_in.1, bf16[1152,256]{1,0:T(8,128)(2,1)S(1)} %shard_map.64._.refs_2_), custom_call_target="tpu_custom_call" | custom-call | bytes 3804160 | tf_op jit(solution)/shard_map/pallas_call | solution.py:121
  5.6 0.7 %collective-permute-start.4 = (bf16[1152,256]{1,0:T(8,128)(2,1)S(1)}, bf16[1152,256]{1,0:T(8,128)(2,1)S(1)}, u32[]{:S(2)}, u32[]{:S(2)}) collective-permute-start(bf16[1152,256]{1,0:T(8,128)(2,1)S(1)} %shard_map.64._.refs_2_), channel_id=1, source_target_pairs={{0,0},{1,1},{2,2},{3,3},{4,8},{5,9},{6,10},{7,11},{8,4},{9,5},{10,... | collective-permute-start | bytes 1769480 | tf_op jit(solution)/shard_map/ppermute | solution.py:98
  6.3 1.6 %collective-permute-start = (bf16[400,1024]{1,0:T(8,128)(2,1)S(1)}, bf16[400,1024]{1,0:T(8,128)(2,1)S(1)}, u32[]{:S(2)}, u32[]{:S(2)}) collective-permute-start(bf16[400,1024]{1,0:T(8,128)(2,1)S(1)} %get-tuple-element.30.away), channel_id=1, source_target_pairs={{0,16},{1,17},{2,18},{3,19},{4,20},{5,21},{6,22},{7,23},{8,24},{9,... | collective-permute-start | bytes 2457608 | tf_op jit(solution)/shard_map/ppermute | solution.py:98
  7.9 0.7 %shard_map.66 = (bf16[160,1024]{1,0:T(8,128)(2,1)S(1)}, bf16[160,1024]{1,0:T(8,128)(2,1)S(1)}, bf16[144,384]{1,0:T(8,128)(2,1)S(1)}) custom-call(bf16[400,1024]{1,0:T(8,128)(2,1)S(1)} %get-tuple-element.29.own.refs_0_, bf16[400,1024]{1,0:T(8,128)(2,1)S(1)} %get-tuple-element.30.away), custom_call_target="tpu_custom_call" | custom-call | flops 226492416 | bytes 2404352 | tf_op jit(solution)/shard_map/pallas_call | solution.py:121
  8.6 0.0 copy-done
  8.6 1.1 %shard_map.67 = (f32[384,256]{1,0:T(8,128)S(1)}, f32[384,256]{1,0:T(8,128)S(1)}) custom-call(bf16[400,1024]{1,0:T(8,128)(2,1)S(1)} %get-tuple-element.29.own.refs_0_, bf16[400,1024]{1,0:T(8,128)(2,1)S(1)} %get-tuple-element.30.away, bf16[2048,512]{1,0:T(8,128)(2,1)S(1)} %copy-done, bf16[144,384]{1,0:T(8,128)(2,1)S(1)} %get-tuple-element.35._.places), custom_call_target="tpu_custom_call" | custom-call | flops 805306368 | bytes 4632576 | tf_op jit(solution)/shard_map/pallas_call | solution.py:121
  9.7 1.6 %collective-permute-start.5 = (f32[384,256]{1,0:T(8,128)S(1)}, f32[384,256]{1,0:T(8,128)S(1)}, u32[]{:S(2)}, u32[]{:S(2)}) collective-permute-start(f32[384,256]{1,0:T(8,128)S(1)} %get-tuple-element.37), channel_id=1, source_target_pairs={{0,2},{1,3},{2,0},{3,1},{4,6},{5,7},{6,4},{7,5},{8,10},{9,11},{10,... | collective-permute-start | bytes 1179656 | tf_op jit(solution)/shard_map/ppermute | solution.py:98
  11.2 6.3 %collective-permute-done.1.refs_4_ = bf16[1152,256]{1,0:T(8,128)(2,1)S(1)} collective-permute-done((bf16[1152,256]{1,0:T(8,128)(2,1)S(1)}, bf16[1152,256]{1,0:T(8,128)(2,1)S(1)}, u32[]{:S(2)}, u32[]{:S(2)}) %collective-permute-start.1) | collective-permute-done | bytes 589856 | tf_op jit(solution)/shard_map/ppermute | solution.py:98
  17.5 3.7 %collective-permute-start.2 = (bf16[160,1024]{1,0:T(8,128)(2,1)S(1)}, bf16[160,1024]{1,0:T(8,128)(2,1)S(1)}, u32[]{:S(2)}, u32[]{:S(2)}) collective-permute-start(bf16[160,1024]{1,0:T(8,128)(2,1)S(1)} %get-tuple-element.32), channel_id=1, source_target_pairs={{0,4},{1,5},{2,6},{3,7},{12,8},{13,9},{14,10},{15,11},{16,20},{17,... | collective-permute-start | bytes 983048 | tf_op jit(solution)/shard_map/ppermute | solution.py:98
  21.2 0.7 %collective-permute-start.6 = (bf16[1152,256]{1,0:T(8,128)(2,1)S(1)}, bf16[1152,256]{1,0:T(8,128)(2,1)S(1)}, u32[]{:S(2)}, u32[]{:S(2)}) collective-permute-start(bf16[1152,256]{1,0:T(8,128)(2,1)S(1)} %collective-permute-done.1.refs_4_), channel_id=1, source_target_pairs={{0,0},{1,1},{2,2},{3,3},{4,8},{5,9},{6,10},{7,11},{8,4},{9,5},{10,... | collective-permute-start | bytes 1769480 | tf_op jit(solution)/shard_map/ppermute | solution.py:98
  21.9 0.0 collective-permute-done.4.refs_3_
  21.9 1.3 %collective-permute-start.7 = (bf16[1152,256]{1,0:T(8,128)(2,1)S(1)}, bf16[1152,256]{1,0:T(8,128)(2,1)S(1)}, u32[]{:S(2)}, u32[]{:S(2)}) collective-permute-start(bf16[1152,256]{1,0:T(8,128)(2,1)S(1)} %collective-permute-done.4.refs_3_), channel_id=1, source_target_pairs={{4,0},{5,1},{6,2},{7,3},{8,12},{9,13},{10,14},{11,15},{20,16},{21,... | collective-permute-start | bytes 1769480 | tf_op jit(solution)/shard_map/ppermute | solution.py:98
  23.2 0.0 collective-permute-done.5.refs_6_
  23.2 5.6 %collective-permute-start.3 = (bf16[160,1024]{1,0:T(8,128)(2,1)S(1)}, bf16[160,1024]{1,0:T(8,128)(2,1)S(1)}, u32[]{:S(2)}, u32[]{:S(2)}) collective-permute-start(bf16[160,1024]{1,0:T(8,128)(2,1)S(1)} %get-tuple-element.33), channel_id=1, source_target_pairs={{0,20},{1,21},{2,22},{3,23},{12,24},{13,25},{14,26},{15,27},{16,4}... | collective-permute-start | bytes 983048 | tf_op jit(solution)/shard_map/ppermute | solution.py:98
  28.8 0.0 collective-permute-done.refs_1_
  28.8 0.0 copy-start.1
  28.8 1.6 %shard_map.68 = (f32[2,384,128]{2,1,0:T(8,128)S(1)}, f32[2,384,256]{2,1,0:T(8,128)S(1)}, f32[384,1]{1,0:T(8,128)S(1)}, bf16[3,256,128]{2,1,0:T(8,128)(2,1)S(1)},...) custom-call(bf16[400,1024]{1,0:T(8,128)(2,1)S(1)} %get-tuple-element.29.own.refs_0_, ...), custom_call_target="tpu_custom_call" | custom-call | tf_op jit(solution)/shard_map/pallas_call | solution.py:121
  30.4 0.0 copy-done.1
  30.4 4.4 %collective-permute-start.9 = (bf16[256,128]{1,0:T(8,128)(2,1)S(1)}, bf16[256,128]{1,0:T(8,128)(2,1)S(1)}, u32[]{:S(2)}, u32[]{:S(2)}) collective-permute-start(bf16[256,128]{1,0:T(8,128)(2,1)S(1)} %copy-done.1), channel_id=1, source_target_pairs={{0,12},{1,13},{2,14},{3,15},{4,4},{5,5},{6,6},{7,7},{8,8},{9,9},{1... | collective-permute-start | bytes 196616 | tf_op jit(solution)/shard_map/ppermute | solution.py:98
  34.8 0.0 collective-permute-done.2.hop.refs_2_
  34.8 0.1 collective-permute-start.14
  34.9 0.3 shard_map.69._.refs_4_
  35.1 0.0 collective-permute-done.3.hop.refs_3_
  35.1 0.3 shard_map.70.refs_5_
  35.4 0.0 collective-permute-done.6.refs_8_
  35.4 3.7 %collective-permute-done.7.refs_9_ = bf16[1152,256]{1,0:T(8,128)(2,1)S(1)} collective-permute-done((bf16[1152,256]{1,0:T(8,128)(2,1)S(1)}, bf16[1152,256]{1,0:T(8,128)(2,1)S(1)}, u32[]{:S(2)}, u32[]{:S(2)}) %collective-permute-start.7) | collective-permute-done | bytes 589856 | tf_op jit(solution)/shard_map/ppermute | solution.py:98
  39.1 0.7 %shard_map.71 = (f32[16,384]{1,0:T(8,128)S(1)}, f32[16,144]{1,0:T(8,128)S(1)}, f32[16,528]{1,0:T(8,128)S(1)}, bf16[256,128]{1,0:T(8,128)(2,1)S(1)}) custom-call(bf16[400,1024]{1,0:T(8,128)(2,1)S(1)} %get-tuple-element.29.own.refs_0_, bf16[400,1024]{1,0:T(8,128)(2,1)S(1)} %collective-permute-done.refs_1_, ...), custom_call_target="tpu_custom_call" | custom-call | flops 553648128 | bytes 5081088 | tf_op jit(solution)/shard_map/pallas_call | solution.py:121
  39.8 1.6 %collective-permute-start.8 = (f32[16,528]{1,0:T(8,128)S(1)}, f32[16,528]{1,0:T(8,128)S(1)}, u32[]{:S(2)}, u32[]{:S(2)}) collective-permute-start(f32[16,528]{1,0:T(8,128)S(1)} %get-tuple-element.43), channel_id=1, source_target_pairs={{0,16},{1,17},{2,18},{3,19},{4,20},{5,21},{6,22},{7,23},{8,24},{9,... | collective-permute-start | bytes 101384 | tf_op jit(solution)/shard_map/ppermute | solution.py:98
  41.4 0.0 collective-permute-done.9.distant
  41.4 2.5 %collective-permute-done.8.near = f32[16,528]{1,0:T(8,128)S(1)} collective-permute-done((f32[16,528]{1,0:T(8,128)S(1)}, f32[16,528]{1,0:T(8,128)S(1)}, u32[]{:S(2)}, u32[]{:S(2)}) %collective-permute-start.8) | collective-permute-done | bytes 33824 | tf_op jit(solution)/shard_map/ppermute | solution.py:98
  43.9 1.2 %collective-permute-start.11 = (f32[16,512]{1,0:T(8,128)S(1)}, f32[16,512]{1,0:T(8,128)S(1)}, u32[]{:S(2)}, u32[]{:S(2)}) collective-permute-start(f32[16,512]{1,0:T(8,128)S(1)} %get-tuple-element.47), channel_id=1, source_target_pairs={{0,6},{1,7},{2,4},{3,5},{4,2},{5,3},{6,0},{7,1},{8,14},{9,15},{10,... | collective-permute-start | bytes 98312 | tf_op jit(solution)/shard_map/ppermute | solution.py:98
  45.1 1.8 %collective-permute-start.12 = (f32[16,512]{1,0:T(8,128)S(1)}, f32[16,512]{1,0:T(8,128)S(1)}, u32[]{:S(2)}, u32[]{:S(2)}) collective-permute-start(f32[16,512]{1,0:T(8,128)S(1)} %get-tuple-element.47), channel_id=1, source_target_pairs={{0,4},{1,5},{2,6},{3,7},{4,0},{5,1},{6,2},{7,3},{8,12},{9,13},{10,... | collective-permute-start | bytes 98312 | tf_op jit(solution)/shard_map/ppermute | solution.py:98
  46.9 0.5 %collective-permute-start.10 = (f32[16,384]{1,0:T(8,128)S(1)}, f32[16,384]{1,0:T(8,128)S(1)}, u32[]{:S(2)}, u32[]{:S(2)}) collective-permute-start(f32[16,384]{1,0:T(8,128)S(1)} %get-tuple-element.46.low), channel_id=1, source_target_pairs={{0,2},{1,3},{2,0},{3,1},{4,6},{5,7},{6,4},{7,5},{8,10},{9,11},{10,... | collective-permute-start | bytes 73736 | tf_op jit(solution)/shard_map/ppermute | solution.py:98
  47.4 3.3 %collective-permute-done.10.far = f32[16,384]{1,0:T(8,128)S(1)} collective-permute-done((f32[16,384]{1,0:T(8,128)S(1)}, f32[16,384]{1,0:T(8,128)S(1)}, u32[]{:S(2)}, u32[]{:S(2)}) %collective-permute-start.10) | collective-permute-done | bytes 24608 | tf_op jit(solution)/shard_map/ppermute | solution.py:98
  50.7 0.0 collective-permute-done.11.hop_far
  50.7 0.0 collective-permute-done.12.hop
  50.7 0.2 shard_map.73.near
  50.9 0.0 collective-permute-start.13
  50.9 0.0 collective-permute-done.14.got
  50.9 1.2 %collective-permute-done.13.far = f32[16,384]{1,0:T(8,128)S(1)} collective-permute-done((f32[16,384]{1,0:T(8,128)S(1)}, f32[16,384]{1,0:T(8,128)S(1)}, u32[]{:S(2)}, u32[]{:S(2)}) %collective-permute-start.13) | collective-permute-done | bytes 24608 | tf_op jit(solution)/shard_map/ppermute | solution.py:98
  52.1 1.3 %shard_map.74 = bf16[384,128]{1,0:T(8,128)(2,1)} custom-call(f32[16,384]{1,0:T(8,128)S(1)} %shard_map.73.near, f32[16,384]{1,0:T(8,128)S(1)} %collective-permute-done.13.far, f32[384,128]{1,0:T(8,128)S(1)} %get-tuple-element.48.keep, f32[384,128]{1,0:T(8,128)S(1)} %collective-permute-done.14.got, f32[384,1]{1,0:T(8,128)S(1)} %get-tuple-element.50.numbers, ...), custom_call_target="tpu_custom_call" | custom-call | bytes 869888 | tf_op jit(solution)/shard_map/pallas_call | solution.py:121
  (1 shorter events, 0.0 us)
Async XLA Ops:
  1.1 7.5 %copy-start = (bf16[2048,512]{1,0:T(8,128)(2,1)S(1)}, bf16[2048,512]{1,0:T(8,128)(2,1)}, u32[]{:S(2)}) copy-start(bf16[2048,512]{1,0:T(8,128)(2,1)} %weights.1) | copy-start | bytes 6291460
  1.1 16.4 %collective-permute-start.1 = (bf16[1152,256]{1,0:T(8,128)(2,1)S(1)}, bf16[1152,256]{1,0:T(8,128)(2,1)S(1)}, u32[]{:S(2)}, u32[]{:S(2)}) collective-permute-start(bf16[1152,256]{1,0:T(8,128)(2,1)S(1)} %shard_map.64._.refs_2_), channel_id=1, source_target_pairs={{0,4},{1,5},{2,6},{3,7},{4,0},{5,1},{6,2},{7,3},{8,12},{9,13},{10,... | collective-permute-start | bytes 1769480 | tf_op jit(solution)/shard_map/ppermute | solution.py:98
  5.6 16.3 %collective-permute-start.4 = (bf16[1152,256]{1,0:T(8,128)(2,1)S(1)}, bf16[1152,256]{1,0:T(8,128)(2,1)S(1)}, u32[]{:S(2)}, u32[]{:S(2)}) collective-permute-start(bf16[1152,256]{1,0:T(8,128)(2,1)S(1)} %shard_map.64._.refs_2_), channel_id=1, source_target_pairs={{0,0},{1,1},{2,2},{3,3},{4,8},{5,9},{6,10},{7,11},{8,4},{9,5},{10,... | collective-permute-start | bytes 1769480 | tf_op jit(solution)/shard_map/ppermute | solution.py:98
  6.3 22.4 %collective-permute-start = (bf16[400,1024]{1,0:T(8,128)(2,1)S(1)}, bf16[400,1024]{1,0:T(8,128)(2,1)S(1)}, u32[]{:S(2)}, u32[]{:S(2)}) collective-permute-start(bf16[400,1024]{1,0:T(8,128)(2,1)S(1)} %get-tuple-element.30.away), channel_id=1, source_target_pairs={{0,16},{1,17},{2,18},{3,19},{4,20},{5,21},{6,22},{7,23},{8,24},{9,... | collective-permute-start | bytes 2457608 | tf_op jit(solution)/shard_map/ppermute | solution.py:98
  9.7 13.5 %collective-permute-start.5 = (f32[384,256]{1,0:T(8,128)S(1)}, f32[384,256]{1,0:T(8,128)S(1)}, u32[]{:S(2)}, u32[]{:S(2)}) collective-permute-start(f32[384,256]{1,0:T(8,128)S(1)} %get-tuple-element.37), channel_id=1, source_target_pairs={{0,2},{1,3},{2,0},{3,1},{4,6},{5,7},{6,4},{7,5},{8,10},{9,11},{10,... | collective-permute-start | bytes 1179656 | tf_op jit(solution)/shard_map/ppermute | solution.py:98
  17.5 17.3 %collective-permute-start.2 = (bf16[160,1024]{1,0:T(8,128)(2,1)S(1)}, bf16[160,1024]{1,0:T(8,128)(2,1)S(1)}, u32[]{:S(2)}, u32[]{:S(2)}) collective-permute-start(bf16[160,1024]{1,0:T(8,128)(2,1)S(1)} %get-tuple-element.32), channel_id=1, source_target_pairs={{0,4},{1,5},{2,6},{3,7},{12,8},{13,9},{14,10},{15,11},{16,20},{17,... | collective-permute-start | bytes 983048 | tf_op jit(solution)/shard_map/ppermute | solution.py:98
  21.2 14.3 %collective-permute-start.6 = (bf16[1152,256]{1,0:T(8,128)(2,1)S(1)}, bf16[1152,256]{1,0:T(8,128)(2,1)S(1)}, u32[]{:S(2)}, u32[]{:S(2)}) collective-permute-start(bf16[1152,256]{1,0:T(8,128)(2,1)S(1)} %collective-permute-done.1.refs_4_), channel_id=1, source_target_pairs={{0,0},{1,1},{2,2},{3,3},{4,8},{5,9},{6,10},{7,11},{8,4},{9,5},{10,... | collective-permute-start | bytes 1769480 | tf_op jit(solution)/shard_map/ppermute | solution.py:98
  21.9 17.2 %collective-permute-start.7 = (bf16[1152,256]{1,0:T(8,128)(2,1)S(1)}, bf16[1152,256]{1,0:T(8,128)(2,1)S(1)}, u32[]{:S(2)}, u32[]{:S(2)}) collective-permute-start(bf16[1152,256]{1,0:T(8,128)(2,1)S(1)} %collective-permute-done.4.refs_3_), channel_id=1, source_target_pairs={{4,0},{5,1},{6,2},{7,3},{8,12},{9,13},{10,14},{11,15},{20,16},{21,... | collective-permute-start | bytes 1769480 | tf_op jit(solution)/shard_map/ppermute | solution.py:98
  23.2 11.9 %collective-permute-start.3 = (bf16[160,1024]{1,0:T(8,128)(2,1)S(1)}, bf16[160,1024]{1,0:T(8,128)(2,1)S(1)}, u32[]{:S(2)}, u32[]{:S(2)}) collective-permute-start(bf16[160,1024]{1,0:T(8,128)(2,1)S(1)} %get-tuple-element.33), channel_id=1, source_target_pairs={{0,20},{1,21},{2,22},{3,23},{12,24},{13,25},{14,26},{15,27},{16,4}... | collective-permute-start | bytes 983048 | tf_op jit(solution)/shard_map/ppermute | solution.py:98
  28.8 1.6 %copy-start.1 = (bf16[256,128]{1,0:T(8,128)(2,1)S(1)}, bf16[256,128]{1,0:T(8,128)(2,1)}, u32[]{:S(2)}) copy-start(bf16[256,128]{1,0:T(8,128)(2,1)} %up.1) | copy-start | bytes 196612
  30.4 11.0 %collective-permute-start.9 = (bf16[256,128]{1,0:T(8,128)(2,1)S(1)}, bf16[256,128]{1,0:T(8,128)(2,1)S(1)}, u32[]{:S(2)}, u32[]{:S(2)}) collective-permute-start(bf16[256,128]{1,0:T(8,128)(2,1)S(1)} %copy-done.1), channel_id=1, source_target_pairs={{0,12},{1,13},{2,14},{3,15},{4,4},{5,5},{6,6},{7,7},{8,8},{9,9},{1... | collective-permute-start | bytes 196616 | tf_op jit(solution)/shard_map/ppermute | solution.py:98
  34.8 16.1 %collective-permute-start.14 = (f32[384,128]{1,0:T(8,128)S(1)}, f32[384,128]{1,0:T(8,128)S(1)}, u32[]{:S(2)}, u32[]{:S(2)}) collective-permute-start(f32[384,128]{1,0:T(8,128)S(1)} %get-tuple-element.49), channel_id=1, source_target_pairs={{0,1},{1,0},{2,3},{3,2},{4,5},{5,4},{6,7},{7,6},{8,9},{9,8},{10,11... | collective-permute-start | bytes 589832 | tf_op jit(solution)/shard_map/ppermute | solution.py:98
  39.8 4.1 %collective-permute-start.8 = (f32[16,528]{1,0:T(8,128)S(1)}, f32[16,528]{1,0:T(8,128)S(1)}, u32[]{:S(2)}, u32[]{:S(2)}) collective-permute-start(f32[16,528]{1,0:T(8,128)S(1)} %get-tuple-element.43), channel_id=1, source_target_pairs={{0,16},{1,17},{2,18},{3,19},{4,20},{5,21},{6,22},{7,23},{8,24},{9,... | collective-permute-start | bytes 101384 | tf_op jit(solution)/shard_map/ppermute | solution.py:98
  43.9 6.8 %collective-permute-start.11 = (f32[16,512]{1,0:T(8,128)S(1)}, f32[16,512]{1,0:T(8,128)S(1)}, u32[]{:S(2)}, u32[]{:S(2)}) collective-permute-start(f32[16,512]{1,0:T(8,128)S(1)} %get-tuple-element.47), channel_id=1, source_target_pairs={{0,6},{1,7},{2,4},{3,5},{4,2},{5,3},{6,0},{7,1},{8,14},{9,15},{10,... | collective-permute-start | bytes 98312 | tf_op jit(solution)/shard_map/ppermute | solution.py:98
  45.1 5.7 %collective-permute-start.12 = (f32[16,512]{1,0:T(8,128)S(1)}, f32[16,512]{1,0:T(8,128)S(1)}, u32[]{:S(2)}, u32[]{:S(2)}) collective-permute-start(f32[16,512]{1,0:T(8,128)S(1)} %get-tuple-element.47), channel_id=1, source_target_pairs={{0,4},{1,5},{2,6},{3,7},{4,0},{5,1},{6,2},{7,3},{8,12},{9,13},{10,... | collective-permute-start | bytes 98312 | tf_op jit(solution)/shard_map/ppermute | solution.py:98
  46.9 3.8 %collective-permute-start.10 = (f32[16,384]{1,0:T(8,128)S(1)}, f32[16,384]{1,0:T(8,128)S(1)}, u32[]{:S(2)}, u32[]{:S(2)}) collective-permute-start(f32[16,384]{1,0:T(8,128)S(1)} %get-tuple-element.46.low), channel_id=1, source_target_pairs={{0,2},{1,3},{2,0},{3,1},{4,6},{5,7},{6,4},{7,5},{8,10},{9,11},{10,... | collective-permute-start | bytes 73736 | tf_op jit(solution)/shard_map/ppermute | solution.py:98
  50.9 1.2 %collective-permute-start.13 = (f32[16,384]{1,0:T(8,128)S(1)}, f32[16,384]{1,0:T(8,128)S(1)}, u32[]{:S(2)}, u32[]{:S(2)}) collective-permute-start(f32[16,384]{1,0:T(8,128)S(1)} %shard_map.73.near), channel_id=1, source_target_pairs={{0,1},{1,0},{2,3},{3,2},{4,5},{5,4},{6,7},{7,6},{8,9},{9,8},{10,11... | collective-permute-start | bytes 73736 | tf_op jit(solution)/shard_map/ppermute | solution.py:98

commit v19 on v18

--- a/solution.py
+++ b/solution.py
@@ -101,7 +101,6 @@
 SAME = tuple((a, a) for a in range(OWNERS))
 BESIDE = ((0, 1), (1, 0), (2, 3), (3, 2))
 MIDDLE = ((0, 0), (1, 2), (2, 1), (3, 3))
-ENDS = ((0, 3), (1, 1), (2, 2), (3, 0))
 OUTWARD = ((1, 0), (2, 3))
 INWARD = ((0, 1), (3, 2))
 
@@ -458,7 +457,6 @@
         scratch=[pltpu.VMEM((rows, 2 * keys), jnp.float32)],
         light=True,
     )
-    distant = exchange(after(stacked_up_weight, folded), 0, 0, ENDS)
     hop_masks, latest = [], folded
     for hop, urgency in zip(hops, HOP_URGENCY):
         latest = kernel(
@@ -482,10 +480,11 @@
     )
 
     near = exchange(away, 1, 0, SAME)
+    distant = exchange(last_up, 0, 0, BESIDE)
     low, hop_low = kernel(
         near_body,
         [wide(ADAPTER_RANK, rows), wide(ADAPTER_RANK, rows + LANES)],
-        (low, hop_low, after(near, distant)),
+        (low, hop_low, near),
     )
     back = exchange(hop_low, 0, 0, BESIDE)
     back_far = exchange(hop_low, 0, 2, BESIDE)

time: 53.6 us -> 52.2 us (0.974)
  starting transfers between devices: 27.7 us -> 25.3 us
  waiting for transfers between devices: 16.9 us -> 18 us
    ppermute x15, starting transfers between devices: 27.7 us -> 25.3 us  [exchange(): return lax.ppermute(x, AXES, pairs)]
    ppermute x15, waiting for transfers between devices: 16.9 us -> 18 us  [exchange(): return lax.ppermute(x, AXES, pairs)]
  transfers between devices with their start and end apart: 15 -> 15, of which waited for: 5 -> 6; matrix products, arithmetic and copies ran while one was open for 0% -> 0% of each run, Pallas kernels for 11% -> 12%
where the time goes in v19:
time: 52.2 us; the launch traced here: 51.9 us
  starting transfers between devices  25.3 us (48%)
  waiting for transfers between devices  18 us (34%)
  Pallas kernels  8.46 us (16%)
    ppermute x15, starting transfers between devices, exchange(): return lax.ppermute(x, AXES, pairs)  25.3 us
    ppermute x15, waiting for transfers between devices, exchange(): return lax.ppermute(x, AXES, pairs)  18 us
    pallas_call x11, Pallas kernels, kernel(): pl.pallas_call(body, out_shape=outs, in_specs=specs or [inner] * len(oper...  8.46 us
  transfers between devices with their start and end apart: 15, of which 6 were waited for; matrix products, arithmetic and copies ran while one was open for 0% of the time, Pallas kernels for 12%

profile of v19, /device:TPU:0, one launch (start us, length us, event | category | flops | bytes accessed | tf_op | source)
XLA Modules:
  0.0 51.9 jit_solution(6795383138303991840)
XLA Ops:
  0.0 1.1 %shard_map.64._.refs_2_ = bf16[1152,256]{1,0:T(8,128)(2,1)S(1)} custom-call(bf16[2048,256]{1,0:T(8,128)(2,1)} %down.1, bf16[256,128]{1,0:T(8,128)(2,1)} %up.1), custom_call_target="tpu_custom_call" | custom-call | bytes 1703936 | tf_op jit(solution)/shard_map/pallas_call | solution.py:120
  1.1 0.0 copy-start
  1.1 3.1 %collective-permute-start.1 = (bf16[1152,256]{1,0:T(8,128)(2,1)S(1)}, bf16[1152,256]{1,0:T(8,128)(2,1)S(1)}, u32[]{:S(2)}, u32[]{:S(2)}) collective-permute-start(bf16[1152,256]{1,0:T(8,128)(2,1)S(1)} %shard_map.64._.refs_2_), channel_id=1, source_target_pairs={{0,4},{1,5},{2,6},{3,7},{4,0},{5,1},{6,2},{7,3},{8,12},{9,13},{10,... | collective-permute-start | bytes 1769480 | tf_op jit(solution)/shard_map/ppermute | solution.py:98
  4.2 1.4 %shard_map.65 = (bf16[400,1024]{1,0:T(8,128)(2,1)S(1)}, bf16[400,1024]{1,0:T(8,128)(2,1)S(1)}) custom-call(bf16[384,2048]{1,0:T(8,128)(2,1)} %tokens.1, s32[1,384]{1,0:T(1,128)} %bitcast.1, s32[384]{0:T(512)} %slot_in.1, bf16[1152,256]{1,0:T(8,128)(2,1)S(1)} %shard_map.64._.refs_2_), custom_call_target="tpu_custom_call" | custom-call | bytes 3804160 | tf_op jit(solution)/shard_map/pallas_call | solution.py:120
  5.6 0.7 %collective-permute-start.4 = (bf16[1152,256]{1,0:T(8,128)(2,1)S(1)}, bf16[1152,256]{1,0:T(8,128)(2,1)S(1)}, u32[]{:S(2)}, u32[]{:S(2)}) collective-permute-start(bf16[1152,256]{1,0:T(8,128)(2,1)S(1)} %shard_map.64._.refs_2_), channel_id=1, source_target_pairs={{0,0},{1,1},{2,2},{3,3},{4,8},{5,9},{6,10},{7,11},{8,4},{9,5},{10,... | collective-permute-start | bytes 1769480 | tf_op jit(solution)/shard_map/ppermute | solution.py:98
  6.3 1.6 %collective-permute-start = (bf16[400,1024]{1,0:T(8,128)(2,1)S(1)}, bf16[400,1024]{1,0:T(8,128)(2,1)S(1)}, u32[]{:S(2)}, u32[]{:S(2)}) collective-permute-start(bf16[400,1024]{1,0:T(8,128)(2,1)S(1)} %get-tuple-element.28.away), channel_id=1, source_target_pairs={{0,16},{1,17},{2,18},{3,19},{4,20},{5,21},{6,22},{7,23},{8,24},{9,... | collective-permute-start | bytes 2457608 | tf_op jit(solution)/shard_map/ppermute | solution.py:98
  7.9 0.7 %shard_map.66 = (bf16[160,1024]{1,0:T(8,128)(2,1)S(1)}, bf16[160,1024]{1,0:T(8,128)(2,1)S(1)}, bf16[144,384]{1,0:T(8,128)(2,1)S(1)}) custom-call(bf16[400,1024]{1,0:T(8,128)(2,1)S(1)} %get-tuple-element.27.own.refs_0_, bf16[400,1024]{1,0:T(8,128)(2,1)S(1)} %get-tuple-element.28.away), custom_call_target="tpu_custom_call" | custom-call | flops 226492416 | bytes 2404352 | tf_op jit(solution)/shard_map/pallas_call | solution.py:120
  8.6 0.0 copy-done
  8.6 1.1 %shard_map.67 = (f32[384,256]{1,0:T(8,128)S(1)}, f32[384,256]{1,0:T(8,128)S(1)}) custom-call(bf16[400,1024]{1,0:T(8,128)(2,1)S(1)} %get-tuple-element.27.own.refs_0_, bf16[400,1024]{1,0:T(8,128)(2,1)S(1)} %get-tuple-element.28.away, bf16[2048,512]{1,0:T(8,128)(2,1)S(1)} %copy-done, bf16[144,384]{1,0:T(8,128)(2,1)S(1)} %get-tuple-element.33._.places), custom_call_target="tpu_custom_call" | custom-call | flops 805306368 | bytes 4632576 | tf_op jit(solution)/shard_map/pallas_call | solution.py:120
  9.7 1.6 %collective-permute-start.5 = (f32[384,256]{1,0:T(8,128)S(1)}, f32[384,256]{1,0:T(8,128)S(1)}, u32[]{:S(2)}, u32[]{:S(2)}) collective-permute-start(f32[384,256]{1,0:T(8,128)S(1)} %get-tuple-element.35), channel_id=1, source_target_pairs={{0,2},{1,3},{2,0},{3,1},{4,6},{5,7},{6,4},{7,5},{8,10},{9,11},{10,... | collective-permute-start | bytes 1179656 | tf_op jit(solution)/shard_map/ppermute | solution.py:98
  11.2 6.3 %collective-permute-done.1.refs_4_ = bf16[1152,256]{1,0:T(8,128)(2,1)S(1)} collective-permute-done((bf16[1152,256]{1,0:T(8,128)(2,1)S(1)}, bf16[1152,256]{1,0:T(8,128)(2,1)S(1)}, u32[]{:S(2)}, u32[]{:S(2)}) %collective-permute-start.1) | collective-permute-done | bytes 589856 | tf_op jit(solution)/shard_map/ppermute | solution.py:98
  17.5 3.7 %collective-permute-start.2 = (bf16[160,1024]{1,0:T(8,128)(2,1)S(1)}, bf16[160,1024]{1,0:T(8,128)(2,1)S(1)}, u32[]{:S(2)}, u32[]{:S(2)}) collective-permute-start(bf16[160,1024]{1,0:T(8,128)(2,1)S(1)} %get-tuple-element.30), channel_id=1, source_target_pairs={{0,4},{1,5},{2,6},{3,7},{12,8},{13,9},{14,10},{15,11},{16,20},{17,... | collective-permute-start | bytes 983048 | tf_op jit(solution)/shard_map/ppermute | solution.py:98
  21.2 0.7 %collective-permute-start.6 = (bf16[1152,256]{1,0:T(8,128)(2,1)S(1)}, bf16[1152,256]{1,0:T(8,128)(2,1)S(1)}, u32[]{:S(2)}, u32[]{:S(2)}) collective-permute-start(bf16[1152,256]{1,0:T(8,128)(2,1)S(1)} %collective-permute-done.1.refs_4_), channel_id=1, source_target_pairs={{0,0},{1,1},{2,2},{3,3},{4,8},{5,9},{6,10},{7,11},{8,4},{9,5},{10,... | collective-permute-start | bytes 1769480 | tf_op jit(solution)/shard_map/ppermute | solution.py:98
  21.9 0.0 collective-permute-done.4.refs_3_
  21.9 1.3 %collective-permute-start.7 = (bf16[1152,256]{1,0:T(8,128)(2,1)S(1)}, bf16[1152,256]{1,0:T(8,128)(2,1)S(1)}, u32[]{:S(2)}, u32[]{:S(2)}) collective-permute-start(bf16[1152,256]{1,0:T(8,128)(2,1)S(1)} %collective-permute-done.4.refs_3_), channel_id=1, source_target_pairs={{4,0},{5,1},{6,2},{7,3},{8,12},{9,13},{10,14},{11,15},{20,16},{21,... | collective-permute-start | bytes 1769480 | tf_op jit(solution)/shard_map/ppermute | solution.py:98
  23.2 0.0 collective-permute-done.5.refs_6_
  23.2 5.6 %collective-permute-start.3 = (bf16[160,1024]{1,0:T(8,128)(2,1)S(1)}, bf16[160,1024]{1,0:T(8,128)(2,1)S(1)}, u32[]{:S(2)}, u32[]{:S(2)}) collective-permute-start(bf16[160,1024]{1,0:T(8,128)(2,1)S(1)} %get-tuple-element.31), channel_id=1, source_target_pairs={{0,20},{1,21},{2,22},{3,23},{12,24},{13,25},{14,26},{15,27},{16,4}... | collective-permute-start | bytes 983048 | tf_op jit(solution)/shard_map/ppermute | solution.py:98
  28.8 0.0 collective-permute-done.refs_1_
  28.8 1.6 %shard_map.68 = (f32[2,384,128]{2,1,0:T(8,128)S(1)}, f32[2,384,256]{2,1,0:T(8,128)S(1)}, f32[384,1]{1,0:T(8,128)S(1)}, bf16[3,256,128]{2,1,0:T(8,128)(2,1)S(1)},...) custom-call(bf16[400,1024]{1,0:T(8,128)(2,1)S(1)} %get-tuple-element.27.own.refs_0_, ...), custom_call_target="tpu_custom_call" | custom-call | tf_op jit(solution)/shard_map/pallas_call | solution.py:120
  30.4 0.1 collective-permute-start.13
  30.4 0.0 collective-permute-done.2.hop.refs_2_
  30.4 0.3 shard_map.69._.refs_4_
  30.7 3.6 %collective-permute-done.3.hop.refs_3_ = bf16[160,1024]{1,0:T(8,128)(2,1)S(1)} collective-permute-done((bf16[160,1024]{1,0:T(8,128)(2,1)S(1)}, bf16[160,1024]{1,0:T(8,128)(2,1)S(1)}, u32[]{:S(2)}, u32[]{:S(2)}) %collective-permute-start.3) | collective-permute-done | bytes 327712 | tf_op jit(solution)/shard_map/ppermute | solution.py:98
  34.3 0.3 shard_map.70.refs_5_
  34.6 0.0 collective-permute-done.6.refs_8_
  34.6 3.1 %collective-permute-done.7.refs_9_ = bf16[1152,256]{1,0:T(8,128)(2,1)S(1)} collective-permute-done((bf16[1152,256]{1,0:T(8,128)(2,1)S(1)}, bf16[1152,256]{1,0:T(8,128)(2,1)S(1)}, u32[]{:S(2)}, u32[]{:S(2)}) %collective-permute-start.7) | collective-permute-done | bytes 589856 | tf_op jit(solution)/shard_map/ppermute | solution.py:98
  37.7 0.7 %shard_map.71 = (f32[16,384]{1,0:T(8,128)S(1)}, f32[16,144]{1,0:T(8,128)S(1)}, f32[16,528]{1,0:T(8,128)S(1)}, bf16[256,128]{1,0:T(8,128)(2,1)S(1)}) custom-call(bf16[400,1024]{1,0:T(8,128)(2,1)S(1)} %get-tuple-element.27.own.refs_0_, bf16[400,1024]{1,0:T(8,128)(2,1)S(1)} %collective-permute-done.refs_1_, ...), custom_call_target="tpu_custom_call" | custom-call | flops 553648128 | bytes 5081088 | tf_op jit(solution)/shard_map/pallas_call | solution.py:120
  38.4 1.6 %collective-permute-start.8 = (f32[16,528]{1,0:T(8,128)S(1)}, f32[16,528]{1,0:T(8,128)S(1)}, u32[]{:S(2)}, u32[]{:S(2)}) collective-permute-start(f32[16,528]{1,0:T(8,128)S(1)} %get-tuple-element.41), channel_id=1, source_target_pairs={{0,16},{1,17},{2,18},{3,19},{4,20},{5,21},{6,22},{7,23},{8,24},{9,... | collective-permute-start | bytes 101384 | tf_op jit(solution)/shard_map/ppermute | solution.py:98
  40.0 2.0 %collective-permute-start.14 = (bf16[256,128]{1,0:T(8,128)(2,1)S(1)}, bf16[256,128]{1,0:T(8,128)(2,1)S(1)}, u32[]{:S(2)}, u32[]{:S(2)}) collective-permute-start(bf16[256,128]{1,0:T(8,128)(2,1)S(1)} %get-tuple-element.48.last_up), channel_id=1, source_target_pairs={{0,4},{1,5},{2,6},{3,7},{4,0},{5,1},{6,2},{7,3},{8,12},{9,13},{10,... | collective-permute-start | bytes 196616 | tf_op jit(solution)/shard_map/ppermute | solution.py:98
  41.9 0.5 collective-permute-done.8.near
  42.5 2.7 %collective-permute-start.10 = (f32[16,512]{1,0:T(8,128)S(1)}, f32[16,512]{1,0:T(8,128)S(1)}, u32[]{:S(2)}, u32[]{:S(2)}) collective-permute-start(f32[16,512]{1,0:T(8,128)S(1)} %get-tuple-element.43), channel_id=1, source_target_pairs={{0,6},{1,7},{2,4},{3,5},{4,2},{5,3},{6,0},{7,1},{8,14},{9,15},{10,... | collective-permute-start | bytes 98312 | tf_op jit(solution)/shard_map/ppermute | solution.py:98
  45.1 0.3 collective-permute-start.11
  45.5 0.5 %collective-permute-start.9 = (f32[16,384]{1,0:T(8,128)S(1)}, f32[16,384]{1,0:T(8,128)S(1)}, u32[]{:S(2)}, u32[]{:S(2)}) collective-permute-start(f32[16,384]{1,0:T(8,128)S(1)} %get-tuple-element.42.low), channel_id=1, source_target_pairs={{0,2},{1,3},{2,0},{3,1},{4,6},{5,7},{6,4},{7,5},{8,10},{9,11},{10,... | collective-permute-start | bytes 73736 | tf_op jit(solution)/shard_map/ppermute | solution.py:98
  46.0 3.3 %collective-permute-done.9.far = f32[16,384]{1,0:T(8,128)S(1)} collective-permute-done((f32[16,384]{1,0:T(8,128)S(1)}, f32[16,384]{1,0:T(8,128)S(1)}, u32[]{:S(2)}, u32[]{:S(2)}) %collective-permute-start.9) | collective-permute-done | bytes 24608 | tf_op jit(solution)/shard_map/ppermute | solution.py:98
  49.3 0.0 collective-permute-done.10.hop_far
  49.3 0.0 collective-permute-done.11.hop
  49.3 0.2 shard_map.73.near
  49.5 0.0 collective-permute-start.12
  49.5 0.0 collective-permute-done.13.got
  49.5 0.0 collective-permute-done.14.distant
  49.5 1.2 %collective-permute-done.12.far = f32[16,384]{1,0:T(8,128)S(1)} collective-permute-done((f32[16,384]{1,0:T(8,128)S(1)}, f32[16,384]{1,0:T(8,128)S(1)}, u32[]{:S(2)}, u32[]{:S(2)}) %collective-permute-start.12) | collective-permute-done | bytes 24608 | tf_op jit(solution)/shard_map/ppermute | solution.py:98
  50.7 1.3 %shard_map.74 = bf16[384,128]{1,0:T(8,128)(2,1)} custom-call(f32[16,384]{1,0:T(8,128)S(1)} %shard_map.73.near, f32[16,384]{1,0:T(8,128)S(1)} %collective-permute-done.12.far, f32[384,128]{1,0:T(8,128)S(1)} %get-tuple-element.44.keep, f32[384,128]{1,0:T(8,128)S(1)} %collective-permute-done.13.got, f32[384,1]{1,0:T(8,128)S(1)} %get-tuple-element.46.numbers, ...), custom_call_target="tpu_custom_call" | custom-call | bytes 869888 | tf_op jit(solution)/shard_map/pallas_call | solution.py:120
  (1 shorter events, 0.0 us)
Async XLA Ops:
  1.1 7.5 %copy-start = (bf16[2048,512]{1,0:T(8,128)(2,1)S(1)}, bf16[2048,512]{1,0:T(8,128)(2,1)}, u32[]{:S(2)}) copy-start(bf16[2048,512]{1,0:T(8,128)(2,1)} %weights.1) | copy-start | bytes 6291460
  1.1 16.4 %collective-permute-start.1 = (bf16[1152,256]{1,0:T(8,128)(2,1)S(1)}, bf16[1152,256]{1,0:T(8,128)(2,1)S(1)}, u32[]{:S(2)}, u32[]{:S(2)}) collective-permute-start(bf16[1152,256]{1,0:T(8,128)(2,1)S(1)} %shard_map.64._.refs_2_), channel_id=1, source_target_pairs={{0,4},{1,5},{2,6},{3,7},{4,0},{5,1},{6,2},{7,3},{8,12},{9,13},{10,... | collective-permute-start | bytes 1769480 | tf_op jit(solution)/shard_map/ppermute | solution.py:98
  5.6 16.3 %collective-permute-start.4 = (bf16[1152,256]{1,0:T(8,128)(2,1)S(1)}, bf16[1152,256]{1,0:T(8,128)(2,1)S(1)}, u32[]{:S(2)}, u32[]{:S(2)}) collective-permute-start(bf16[1152,256]{1,0:T(8,128)(2,1)S(1)} %shard_map.64._.refs_2_), channel_id=1, source_target_pairs={{0,0},{1,1},{2,2},{3,3},{4,8},{5,9},{6,10},{7,11},{8,4},{9,5},{10,... | collective-permute-start | bytes 1769480 | tf_op jit(solution)/shard_map/ppermute | solution.py:98
  6.3 22.4 %collective-permute-start = (bf16[400,1024]{1,0:T(8,128)(2,1)S(1)}, bf16[400,1024]{1,0:T(8,128)(2,1)S(1)}, u32[]{:S(2)}, u32[]{:S(2)}) collective-permute-start(bf16[400,1024]{1,0:T(8,128)(2,1)S(1)} %get-tuple-element.28.away), channel_id=1, source_target_pairs={{0,16},{1,17},{2,18},{3,19},{4,20},{5,21},{6,22},{7,23},{8,24},{9,... | collective-permute-start | bytes 2457608 | tf_op jit(solution)/shard_map/ppermute | solution.py:98
  9.7 13.5 %collective-permute-start.5 = (f32[384,256]{1,0:T(8,128)S(1)}, f32[384,256]{1,0:T(8,128)S(1)}, u32[]{:S(2)}, u32[]{:S(2)}) collective-permute-start(f32[384,256]{1,0:T(8,128)S(1)} %get-tuple-element.35), channel_id=1, source_target_pairs={{0,2},{1,3},{2,0},{3,1},{4,6},{5,7},{6,4},{7,5},{8,10},{9,11},{10,... | collective-permute-start | bytes 1179656 | tf_op jit(solution)/shard_map/ppermute | solution.py:98
  17.5 12.9 %collective-permute-start.2 = (bf16[160,1024]{1,0:T(8,128)(2,1)S(1)}, bf16[160,1024]{1,0:T(8,128)(2,1)S(1)}, u32[]{:S(2)}, u32[]{:S(2)}) collective-permute-start(bf16[160,1024]{1,0:T(8,128)(2,1)S(1)} %get-tuple-element.30), channel_id=1, source_target_pairs={{0,4},{1,5},{2,6},{3,7},{12,8},{13,9},{14,10},{15,11},{16,20},{17,... | collective-permute-start | bytes 983048 | tf_op jit(solution)/shard_map/ppermute | solution.py:98
  21.2 13.4 %collective-permute-start.6 = (bf16[1152,256]{1,0:T(8,128)(2,1)S(1)}, bf16[1152,256]{1,0:T(8,128)(2,1)S(1)}, u32[]{:S(2)}, u32[]{:S(2)}) collective-permute-start(bf16[1152,256]{1,0:T(8,128)(2,1)S(1)} %collective-permute-done.1.refs_4_), channel_id=1, source_target_pairs={{0,0},{1,1},{2,2},{3,3},{4,8},{5,9},{6,10},{7,11},{8,4},{9,5},{10,... | collective-permute-start | bytes 1769480 | tf_op jit(solution)/shard_map/ppermute | solution.py:98
  21.9 15.8 %collective-permute-start.7 = (bf16[1152,256]{1,0:T(8,128)(2,1)S(1)}, bf16[1152,256]{1,0:T(8,128)(2,1)S(1)}, u32[]{:S(2)}, u32[]{:S(2)}) collective-permute-start(bf16[1152,256]{1,0:T(8,128)(2,1)S(1)} %collective-permute-done.4.refs_3_), channel_id=1, source_target_pairs={{4,0},{5,1},{6,2},{7,3},{8,12},{9,13},{10,14},{11,15},{20,16},{21,... | collective-permute-start | bytes 1769480 | tf_op jit(solution)/shard_map/ppermute | solution.py:98
  23.2 11.1 %collective-permute-start.3 = (bf16[160,1024]{1,0:T(8,128)(2,1)S(1)}, bf16[160,1024]{1,0:T(8,128)(2,1)S(1)}, u32[]{:S(2)}, u32[]{:S(2)}) collective-permute-start(bf16[160,1024]{1,0:T(8,128)(2,1)S(1)} %get-tuple-element.31), channel_id=1, source_target_pairs={{0,20},{1,21},{2,22},{3,23},{12,24},{13,25},{14,26},{15,27},{16,4}... | collective-permute-start | bytes 983048 | tf_op jit(solution)/shard_map/ppermute | solution.py:98
  30.4 19.1 %collective-permute-start.13 = (f32[384,128]{1,0:T(8,128)S(1)}, f32[384,128]{1,0:T(8,128)S(1)}, u32[]{:S(2)}, u32[]{:S(2)}) collective-permute-start(f32[384,128]{1,0:T(8,128)S(1)} %get-tuple-element.45), channel_id=1, source_target_pairs={{0,1},{1,0},{2,3},{3,2},{4,5},{5,4},{6,7},{7,6},{8,9},{9,8},{10,11... | collective-permute-start | bytes 589832 | tf_op jit(solution)/shard_map/ppermute | solution.py:98
  38.4 4.1 %collective-permute-start.8 = (f32[16,528]{1,0:T(8,128)S(1)}, f32[16,528]{1,0:T(8,128)S(1)}, u32[]{:S(2)}, u32[]{:S(2)}) collective-permute-start(f32[16,528]{1,0:T(8,128)S(1)} %get-tuple-element.41), channel_id=1, source_target_pairs={{0,16},{1,17},{2,18},{3,19},{4,20},{5,21},{6,22},{7,23},{8,24},{9,... | collective-permute-start | bytes 101384 | tf_op jit(solution)/shard_map/ppermute | solution.py:98
  40.0 9.5 %collective-permute-start.14 = (bf16[256,128]{1,0:T(8,128)(2,1)S(1)}, bf16[256,128]{1,0:T(8,128)(2,1)S(1)}, u32[]{:S(2)}, u32[]{:S(2)}) collective-permute-start(bf16[256,128]{1,0:T(8,128)(2,1)S(1)} %get-tuple-element.48.last_up), channel_id=1, source_target_pairs={{0,4},{1,5},{2,6},{3,7},{4,0},{5,1},{6,2},{7,3},{8,12},{9,13},{10,... | collective-permute-start | bytes 196616 | tf_op jit(solution)/shard_map/ppermute | solution.py:98
  42.5 6.8 %collective-permute-start.10 = (f32[16,512]{1,0:T(8,128)S(1)}, f32[16,512]{1,0:T(8,128)S(1)}, u32[]{:S(2)}, u32[]{:S(2)}) collective-permute-start(f32[16,512]{1,0:T(8,128)S(1)} %get-tuple-element.43), channel_id=1, source_target_pairs={{0,6},{1,7},{2,4},{3,5},{4,2},{5,3},{6,0},{7,1},{8,14},{9,15},{10,... | collective-permute-start | bytes 98312 | tf_op jit(solution)/shard_map/ppermute | solution.py:98
  45.1 4.2 %collective-permute-start.11 = (f32[16,512]{1,0:T(8,128)S(1)}, f32[16,512]{1,0:T(8,128)S(1)}, u32[]{:S(2)}, u32[]{:S(2)}) collective-permute-start(f32[16,512]{1,0:T(8,128)S(1)} %get-tuple-element.43), channel_id=1, source_target_pairs={{0,4},{1,5},{2,6},{3,7},{4,0},{5,1},{6,2},{7,3},{8,12},{9,13},{10,... | collective-permute-start | bytes 98312 | tf_op jit(solution)/shard_map/ppermute | solution.py:98
  45.5 3.8 %collective-permute-start.9 = (f32[16,384]{1,0:T(8,128)S(1)}, f32[16,384]{1,0:T(8,128)S(1)}, u32[]{:S(2)}, u32[]{:S(2)}) collective-permute-start(f32[16,384]{1,0:T(8,128)S(1)} %get-tuple-element.42.low), channel_id=1, source_target_pairs={{0,2},{1,3},{2,0},{3,1},{4,6},{5,7},{6,4},{7,5},{8,10},{9,11},{10,... | collective-permute-start | bytes 73736 | tf_op jit(solution)/shard_map/ppermute | solution.py:98
  49.5 1.2 %collective-permute-start.12 = (f32[16,384]{1,0:T(8,128)S(1)}, f32[16,384]{1,0:T(8,128)S(1)}, u32[]{:S(2)}, u32[]{:S(2)}) collective-permute-start(f32[16,384]{1,0:T(8,128)S(1)} %shard_map.73.near), channel_id=1, source_target_pairs={{0,1},{1,0},{2,3},{3,2},{4,5},{5,4},{6,7},{7,6},{8,9},{9,8},{10,11... | collective-permute-start | bytes 73736 | tf_op jit(solution)/shard_map/ppermute | solution.py:98

commit v20 on v19

--- a/solution.py
+++ b/solution.py
@@ -288,7 +288,7 @@
     a = lax.axis_index("adapter")
     token_refs, rest = refs[:groups], refs[groups:]
     hops, rest = rest[:groups], rest[groups:]
-    hop_masks, rest = rest[:groups], rest[groups:]
+    hop_mask, rest = rest[0], rest[1:]
     folded, mask, inside, outside, low, hop_low, away, last_up = rest
     columns = inside.shape[1]
 
@@ -307,9 +307,14 @@
     def _():
         finish(inside)
         last_up[...] = stacked(inside[part:, :], last_up.shape[1])
-        for n, (hop, hop_mask) in enumerate(zip(hops, hop_masks)):
+        for n, hop in enumerate(hops):
             wide = jnp.dot(hop[:capacity, :], inside[:part, :], preferred_element_type=jnp.float32)
-            kept = fold(jnp.where(hop_mask[...] > 0, wide, 0.0))
+            if n:
+                _, slot = id_columns(hop, capacity, capacity)
+                wanted = adapters(capacity, columns) == slot
+            else:
+                wanted = hop_mask[...] > 0
+            kept = fold(jnp.where(wanted, wide, 0.0))
             rest_rows = -capacity % LANES
             kept = jnp.concatenate([kept, jnp.zeros((rest_rows, LANES), jnp.float32)], axis=0)
             if n:
@@ -398,6 +403,7 @@
         [pltpu.SemaphoreType.DMA((1 + half,))],
     )
     beside = exchange(own, 0, 0, BESIDE)
+    mirror = exchange(own, 0, 0, MIDDLE)
 
     tok_own, tok_away = kernel(
         split_body,
@@ -417,7 +423,6 @@
         ],
     )
     token_parts = [tok_own, exchange(tok_away, 1, 0, SAME)]
-    mirror = exchange(after(own, tok_own), 0, 0, MIDDLE)
     hop_own, hop_away, places = kernel(
         functools.partial(hop_body, rows, capacity),
         [narrow(capacity + ID_ROWS, part)] * groups
@@ -458,7 +463,7 @@
         light=True,
     )
     hop_masks, latest = [], folded
-    for hop, urgency in zip(hops, HOP_URGENCY):
+    for hop, urgency in zip(hops[:1], HOP_URGENCY):
         latest = kernel(
             functools.partial(hop_mask_body, capacity),
             wide(capacity, columns),

time: 52.2 us -> 52.2 us (level)
    pallas_call x11 -> x10, Pallas kernels: 8.46 us -> 8.2 us  [kernel(): pl.pallas_call(body, out_shape=outs, in_specs=specs or [inner] * len(oper...]
  transfers between devices with their start and end apart: 15 -> 15, of which waited for: 6 -> 6; matrix products, arithmetic and copies ran while one was open for 0% -> 0% of each run, Pallas kernels for 12% -> 11%
where the time goes in v20:
time: 52.2 us; the launch traced here: 51.9 us
  starting transfers between devices  25.1 us (48%)
  waiting for transfers between devices  18.5 us (35%)
  Pallas kernels  8.2 us (16%)
    ppermute x15, starting transfers between devices, exchange(): return lax.ppermute(x, AXES, pairs)  25.1 us
    ppermute x15, waiting for transfers between devices, exchange(): return lax.ppermute(x, AXES, pairs)  18.5 us
    pallas_call x10, Pallas kernels, kernel(): pl.pallas_call(body, out_shape=outs, in_specs=specs or [inner] * len(oper...  8.2 us
  transfers between devices with their start and end apart: 15, of which 6 were waited for; matrix products, arithmetic and copies ran while one was open for 0% of the time, Pallas kernels for 11%

profile of v20, /device:TPU:0, one launch (start us, length us, event | category | flops | bytes accessed | tf_op | source)
XLA Modules:
  0.0 51.9 jit_solution(940819658278218773)
XLA Ops:
  0.0 1.1 %shard_map.64._.refs_2_ = bf16[1152,256]{1,0:T(8,128)(2,1)S(1)} custom-call(bf16[2048,256]{1,0:T(8,128)(2,1)} %down.1, bf16[256,128]{1,0:T(8,128)(2,1)} %up.1), custom_call_target="tpu_custom_call" | custom-call | bytes 1703936 | tf_op jit(solution)/shard_map/pallas_call | solution.py:120
  1.1 0.0 copy-start
  1.1 3.1 %collective-permute-start.1 = (bf16[1152,256]{1,0:T(8,128)(2,1)S(1)}, bf16[1152,256]{1,0:T(8,128)(2,1)S(1)}, u32[]{:S(2)}, u32[]{:S(2)}) collective-permute-start(bf16[1152,256]{1,0:T(8,128)(2,1)S(1)} %shard_map.64._.refs_2_), channel_id=1, source_target_pairs={{0,4},{1,5},{2,6},{3,7},{4,0},{5,1},{6,2},{7,3},{8,12},{9,13},{10,... | collective-permute-start | bytes 1769480 | tf_op jit(solution)/shard_map/ppermute | solution.py:98
  4.2 0.7 %collective-permute-start.4 = (bf16[1152,256]{1,0:T(8,128)(2,1)S(1)}, bf16[1152,256]{1,0:T(8,128)(2,1)S(1)}, u32[]{:S(2)}, u32[]{:S(2)}) collective-permute-start(bf16[1152,256]{1,0:T(8,128)(2,1)S(1)} %shard_map.64._.refs_2_), channel_id=1, source_target_pairs={{0,0},{1,1},{2,2},{3,3},{4,8},{5,9},{6,10},{7,11},{8,4},{9,5},{10,... | collective-permute-start | bytes 1769480 | tf_op jit(solution)/shard_map/ppermute | solution.py:98
  4.9 1.4 %shard_map.65 = (bf16[400,1024]{1,0:T(8,128)(2,1)S(1)}, bf16[400,1024]{1,0:T(8,128)(2,1)S(1)}) custom-call(bf16[384,2048]{1,0:T(8,128)(2,1)} %tokens.1, s32[1,384]{1,0:T(1,128)} %bitcast.1, s32[384]{0:T(512)} %slot_in.1, bf16[1152,256]{1,0:T(8,128)(2,1)S(1)} %shard_map.64._.refs_2_), custom_call_target="tpu_custom_call" | custom-call | bytes 3804160 | tf_op jit(solution)/shard_map/pallas_call | solution.py:120
  6.3 1.6 %collective-permute-start = (bf16[400,1024]{1,0:T(8,128)(2,1)S(1)}, bf16[400,1024]{1,0:T(8,128)(2,1)S(1)}, u32[]{:S(2)}, u32[]{:S(2)}) collective-permute-start(bf16[400,1024]{1,0:T(8,128)(2,1)S(1)} %get-tuple-element.27.away), channel_id=1, source_target_pairs={{0,16},{1,17},{2,18},{3,19},{4,20},{5,21},{6,22},{7,23},{8,24},{9,... | collective-permute-start | bytes 2457608 | tf_op jit(solution)/shard_map/ppermute | solution.py:98
  7.9 0.7 %shard_map.66 = (bf16[160,1024]{1,0:T(8,128)(2,1)S(1)}, bf16[160,1024]{1,0:T(8,128)(2,1)S(1)}, bf16[144,384]{1,0:T(8,128)(2,1)S(1)}) custom-call(bf16[400,1024]{1,0:T(8,128)(2,1)S(1)} %get-tuple-element.26.own.refs_0_, bf16[400,1024]{1,0:T(8,128)(2,1)S(1)} %get-tuple-element.27.away), custom_call_target="tpu_custom_call" | custom-call | flops 226492416 | bytes 2404352 | tf_op jit(solution)/shard_map/pallas_call | solution.py:120
  8.6 0.0 copy-done
  8.6 1.1 %shard_map.67 = (f32[384,256]{1,0:T(8,128)S(1)}, f32[384,256]{1,0:T(8,128)S(1)}) custom-call(bf16[400,1024]{1,0:T(8,128)(2,1)S(1)} %get-tuple-element.26.own.refs_0_, bf16[400,1024]{1,0:T(8,128)(2,1)S(1)} %get-tuple-element.27.away, bf16[2048,512]{1,0:T(8,128)(2,1)S(1)} %copy-done, bf16[144,384]{1,0:T(8,128)(2,1)S(1)} %get-tuple-element.31._.places), custom_call_target="tpu_custom_call" | custom-call | flops 805306368 | bytes 4632576 | tf_op jit(solution)/shard_map/pallas_call | solution.py:120
  9.7 1.6 %collective-permute-start.5 = (f32[384,256]{1,0:T(8,128)S(1)}, f32[384,256]{1,0:T(8,128)S(1)}, u32[]{:S(2)}, u32[]{:S(2)}) collective-permute-start(f32[384,256]{1,0:T(8,128)S(1)} %get-tuple-element.33), channel_id=1, source_target_pairs={{0,2},{1,3},{2,0},{3,1},{4,6},{5,7},{6,4},{7,5},{8,10},{9,11},{10,... | collective-permute-start | bytes 1179656 | tf_op jit(solution)/shard_map/ppermute | solution.py:98
  11.2 6.3 %collective-permute-done.1.refs_4_ = bf16[1152,256]{1,0:T(8,128)(2,1)S(1)} collective-permute-done((bf16[1152,256]{1,0:T(8,128)(2,1)S(1)}, bf16[1152,256]{1,0:T(8,128)(2,1)S(1)}, u32[]{:S(2)}, u32[]{:S(2)}) %collective-permute-start.1) | collective-permute-done | bytes 589856 | tf_op jit(solution)/shard_map/ppermute | solution.py:98
  17.5 3.7 %collective-permute-start.2 = (bf16[160,1024]{1,0:T(8,128)(2,1)S(1)}, bf16[160,1024]{1,0:T(8,128)(2,1)S(1)}, u32[]{:S(2)}, u32[]{:S(2)}) collective-permute-start(bf16[160,1024]{1,0:T(8,128)(2,1)S(1)} %get-tuple-element.29), channel_id=1, source_target_pairs={{0,4},{1,5},{2,6},{3,7},{12,8},{13,9},{14,10},{15,11},{16,20},{17,... | collective-permute-start | bytes 983048 | tf_op jit(solution)/shard_map/ppermute | solution.py:98
  21.2 0.7 %collective-permute-start.6 = (bf16[1152,256]{1,0:T(8,128)(2,1)S(1)}, bf16[1152,256]{1,0:T(8,128)(2,1)S(1)}, u32[]{:S(2)}, u32[]{:S(2)}) collective-permute-start(bf16[1152,256]{1,0:T(8,128)(2,1)S(1)} %collective-permute-done.1.refs_4_), channel_id=1, source_target_pairs={{0,0},{1,1},{2,2},{3,3},{4,8},{5,9},{6,10},{7,11},{8,4},{9,5},{10,... | collective-permute-start | bytes 1769480 | tf_op jit(solution)/shard_map/ppermute | solution.py:98
  21.9 0.0 collective-permute-done.4.refs_3_
  21.9 1.3 %collective-permute-start.7 = (bf16[1152,256]{1,0:T(8,128)(2,1)S(1)}, bf16[1152,256]{1,0:T(8,128)(2,1)S(1)}, u32[]{:S(2)}, u32[]{:S(2)}) collective-permute-start(bf16[1152,256]{1,0:T(8,128)(2,1)S(1)} %collective-permute-done.4.refs_3_), channel_id=1, source_target_pairs={{4,0},{5,1},{6,2},{7,3},{8,12},{9,13},{10,14},{11,15},{20,16},{21,... | collective-permute-start | bytes 1769480 | tf_op jit(solution)/shard_map/ppermute | solution.py:98
  23.2 0.0 collective-permute-done.5.refs_6_
  23.2 5.6 %collective-permute-start.3 = (bf16[160,1024]{1,0:T(8,128)(2,1)S(1)}, bf16[160,1024]{1,0:T(8,128)(2,1)S(1)}, u32[]{:S(2)}, u32[]{:S(2)}) collective-permute-start(bf16[160,1024]{1,0:T(8,128)(2,1)S(1)} %get-tuple-element.30), channel_id=1, source_target_pairs={{0,20},{1,21},{2,22},{3,23},{12,24},{13,25},{14,26},{15,27},{16,4}... | collective-permute-start | bytes 983048 | tf_op jit(solution)/shard_map/ppermute | solution.py:98
  28.8 0.0 collective-permute-done.refs_1_
  28.8 1.6 %shard_map.68 = (f32[2,384,128]{2,1,0:T(8,128)S(1)}, f32[2,384,256]{2,1,0:T(8,128)S(1)}, f32[384,1]{1,0:T(8,128)S(1)}, bf16[3,256,128]{2,1,0:T(8,128)(2,1)S(1)},...) custom-call(bf16[400,1024]{1,0:T(8,128)(2,1)S(1)} %get-tuple-element.26.own.refs_0_, ...), custom_call_target="tpu_custom_call" | custom-call | tf_op jit(solution)/shard_map/pallas_call | solution.py:120
  30.4 0.1 collective-permute-start.13
  30.4 0.0 collective-permute-done.2.hop.refs_2_
  30.4 0.3 shard_map.69.refs_4_
  30.7 3.6 %collective-permute-done.3.refs_3_ = bf16[160,1024]{1,0:T(8,128)(2,1)S(1)} collective-permute-done((bf16[160,1024]{1,0:T(8,128)(2,1)S(1)}, bf16[160,1024]{1,0:T(8,128)(2,1)S(1)}, u32[]{:S(2)}, u32[]{:S(2)}) %collective-permute-start.3) | collective-permute-done | bytes 327712 | tf_op jit(solution)/shard_map/ppermute | solution.py:98
  34.3 0.0 collective-permute-done.6.refs_7_
  34.3 3.4 %collective-permute-done.7.refs_8_ = bf16[1152,256]{1,0:T(8,128)(2,1)S(1)} collective-permute-done((bf16[1152,256]{1,0:T(8,128)(2,1)S(1)}, bf16[1152,256]{1,0:T(8,128)(2,1)S(1)}, u32[]{:S(2)}, u32[]{:S(2)}) %collective-permute-start.7) | collective-permute-done | bytes 589856 | tf_op jit(solution)/shard_map/ppermute | solution.py:98
  37.7 0.7 %shard_map.70 = (f32[16,384]{1,0:T(8,128)S(1)}, f32[16,144]{1,0:T(8,128)S(1)}, f32[16,528]{1,0:T(8,128)S(1)}, bf16[256,128]{1,0:T(8,128)(2,1)S(1)}) custom-call(bf16[400,1024]{1,0:T(8,128)(2,1)S(1)} %get-tuple-element.26.own.refs_0_, bf16[400,1024]{1,0:T(8,128)(2,1)S(1)} %collective-permute-done.refs_1_, ...), custom_call_target="tpu_custom_call" | custom-call | flops 553648128 | bytes 4933632 | tf_op jit(solution)/shard_map/pallas_call | solution.py:120
  38.4 1.6 %collective-permute-start.8 = (f32[16,528]{1,0:T(8,128)S(1)}, f32[16,528]{1,0:T(8,128)S(1)}, u32[]{:S(2)}, u32[]{:S(2)}) collective-permute-start(f32[16,528]{1,0:T(8,128)S(1)} %get-tuple-element.39), channel_id=1, source_target_pairs={{0,16},{1,17},{2,18},{3,19},{4,20},{5,21},{6,22},{7,23},{8,24},{9,... | collective-permute-start | bytes 101384 | tf_op jit(solution)/shard_map/ppermute | solution.py:98
  40.0 1.7 %collective-permute-start.14 = (bf16[256,128]{1,0:T(8,128)(2,1)S(1)}, bf16[256,128]{1,0:T(8,128)(2,1)S(1)}, u32[]{:S(2)}, u32[]{:S(2)}) collective-permute-start(bf16[256,128]{1,0:T(8,128)(2,1)S(1)} %get-tuple-element.46.last_up), channel_id=1, source_target_pairs={{0,4},{1,5},{2,6},{3,7},{4,0},{5,1},{6,2},{7,3},{8,12},{9,13},{10,... | collective-permute-start | bytes 196616 | tf_op jit(solution)/shard_map/ppermute | solution.py:98
  41.7 0.7 %collective-permute-done.8.near = f32[16,528]{1,0:T(8,128)S(1)} collective-permute-done((f32[16,528]{1,0:T(8,128)S(1)}, f32[16,528]{1,0:T(8,128)S(1)}, u32[]{:S(2)}, u32[]{:S(2)}) %collective-permute-start.8) | collective-permute-done | bytes 33824 | tf_op jit(solution)/shard_map/ppermute | solution.py:98
  42.5 2.5 %collective-permute-start.10 = (f32[16,512]{1,0:T(8,128)S(1)}, f32[16,512]{1,0:T(8,128)S(1)}, u32[]{:S(2)}, u32[]{:S(2)}) collective-permute-start(f32[16,512]{1,0:T(8,128)S(1)} %get-tuple-element.41), channel_id=1, source_target_pairs={{0,6},{1,7},{2,4},{3,5},{4,2},{5,3},{6,0},{7,1},{8,14},{9,15},{10,... | collective-permute-start | bytes 98312 | tf_op jit(solution)/shard_map/ppermute | solution.py:98
  44.9 0.5 %collective-permute-start.11 = (f32[16,512]{1,0:T(8,128)S(1)}, f32[16,512]{1,0:T(8,128)S(1)}, u32[]{:S(2)}, u32[]{:S(2)}) collective-permute-start(f32[16,512]{1,0:T(8,128)S(1)} %get-tuple-element.41), channel_id=1, source_target_pairs={{0,4},{1,5},{2,6},{3,7},{4,0},{5,1},{6,2},{7,3},{8,12},{9,13},{10,... | collective-permute-start | bytes 98312 | tf_op jit(solution)/shard_map/ppermute | solution.py:98
  45.5 0.5 %collective-permute-start.9 = (f32[16,384]{1,0:T(8,128)S(1)}, f32[16,384]{1,0:T(8,128)S(1)}, u32[]{:S(2)}, u32[]{:S(2)}) collective-permute-start(f32[16,384]{1,0:T(8,128)S(1)} %get-tuple-element.40.low), channel_id=1, source_target_pairs={{0,2},{1,3},{2,0},{3,1},{4,6},{5,7},{6,4},{7,5},{8,10},{9,11},{10,... | collective-permute-start | bytes 73736 | tf_op jit(solution)/shard_map/ppermute | solution.py:98
  46.0 3.3 %collective-permute-done.9.far = f32[16,384]{1,0:T(8,128)S(1)} collective-permute-done((f32[16,384]{1,0:T(8,128)S(1)}, f32[16,384]{1,0:T(8,128)S(1)}, u32[]{:S(2)}, u32[]{:S(2)}) %collective-permute-start.9) | collective-permute-done | bytes 24608 | tf_op jit(solution)/shard_map/ppermute | solution.py:98
  49.3 0.0 collective-permute-done.10.hop_far
  49.3 0.0 collective-permute-done.11.hop
  49.3 0.2 shard_map.72.near
  49.5 0.0 collective-permute-start.12
  49.5 0.0 collective-permute-done.13.got
  49.5 0.0 collective-permute-done.14.distant
  49.5 1.2 %collective-permute-done.12.far = f32[16,384]{1,0:T(8,128)S(1)} collective-permute-done((f32[16,384]{1,0:T(8,128)S(1)}, f32[16,384]{1,0:T(8,128)S(1)}, u32[]{:S(2)}, u32[]{:S(2)}) %collective-permute-start.12) | collective-permute-done | bytes 24608 | tf_op jit(solution)/shard_map/ppermute | solution.py:98
  50.7 1.3 %shard_map.73 = bf16[384,128]{1,0:T(8,128)(2,1)} custom-call(f32[16,384]{1,0:T(8,128)S(1)} %shard_map.72.near, f32[16,384]{1,0:T(8,128)S(1)} %collective-permute-done.12.far, f32[384,128]{1,0:T(8,128)S(1)} %get-tuple-element.42.keep, f32[384,128]{1,0:T(8,128)S(1)} %collective-permute-done.13.got, f32[384,1]{1,0:T(8,128)S(1)} %get-tuple-element.44.numbers, ...), custom_call_target="tpu_custom_call" | custom-call | bytes 869888 | tf_op jit(solution)/shard_map/pallas_call | solution.py:120
  (1 shorter events, 0.0 us)
Async XLA Ops:
  1.1 7.5 %copy-start = (bf16[2048,512]{1,0:T(8,128)(2,1)S(1)}, bf16[2048,512]{1,0:T(8,128)(2,1)}, u32[]{:S(2)}) copy-start(bf16[2048,512]{1,0:T(8,128)(2,1)} %weights.1) | copy-start | bytes 6291460
  1.1 16.4 %collective-permute-start.1 = (bf16[1152,256]{1,0:T(8,128)(2,1)S(1)}, bf16[1152,256]{1,0:T(8,128)(2,1)S(1)}, u32[]{:S(2)}, u32[]{:S(2)}) collective-permute-start(bf16[1152,256]{1,0:T(8,128)(2,1)S(1)} %shard_map.64._.refs_2_), channel_id=1, source_target_pairs={{0,4},{1,5},{2,6},{3,7},{4,0},{5,1},{6,2},{7,3},{8,12},{9,13},{10,... | collective-permute-start | bytes 1769480 | tf_op jit(solution)/shard_map/ppermute | solution.py:98
  4.2 17.7 %collective-permute-start.4 = (bf16[1152,256]{1,0:T(8,128)(2,1)S(1)}, bf16[1152,256]{1,0:T(8,128)(2,1)S(1)}, u32[]{:S(2)}, u32[]{:S(2)}) collective-permute-start(bf16[1152,256]{1,0:T(8,128)(2,1)S(1)} %shard_map.64._.refs_2_), channel_id=1, source_target_pairs={{0,0},{1,1},{2,2},{3,3},{4,8},{5,9},{6,10},{7,11},{8,4},{9,5},{10,... | collective-permute-start | bytes 1769480 | tf_op jit(solution)/shard_map/ppermute | solution.py:98
  6.3 22.4 %collective-permute-start = (bf16[400,1024]{1,0:T(8,128)(2,1)S(1)}, bf16[400,1024]{1,0:T(8,128)(2,1)S(1)}, u32[]{:S(2)}, u32[]{:S(2)}) collective-permute-start(bf16[400,1024]{1,0:T(8,128)(2,1)S(1)} %get-tuple-element.27.away), channel_id=1, source_target_pairs={{0,16},{1,17},{2,18},{3,19},{4,20},{5,21},{6,22},{7,23},{8,24},{9,... | collective-permute-start | bytes 2457608 | tf_op jit(solution)/shard_map/ppermute | solution.py:98
  9.7 13.5 %collective-permute-start.5 = (f32[384,256]{1,0:T(8,128)S(1)}, f32[384,256]{1,0:T(8,128)S(1)}, u32[]{:S(2)}, u32[]{:S(2)}) collective-permute-start(f32[384,256]{1,0:T(8,128)S(1)} %get-tuple-element.33), channel_id=1, source_target_pairs={{0,2},{1,3},{2,0},{3,1},{4,6},{5,7},{6,4},{7,5},{8,10},{9,11},{10,... | collective-permute-start | bytes 1179656 | tf_op jit(solution)/shard_map/ppermute | solution.py:98
  17.5 12.9 %collective-permute-start.2 = (bf16[160,1024]{1,0:T(8,128)(2,1)S(1)}, bf16[160,1024]{1,0:T(8,128)(2,1)S(1)}, u32[]{:S(2)}, u32[]{:S(2)}) collective-permute-start(bf16[160,1024]{1,0:T(8,128)(2,1)S(1)} %get-tuple-element.29), channel_id=1, source_target_pairs={{0,4},{1,5},{2,6},{3,7},{12,8},{13,9},{14,10},{15,11},{16,20},{17,... | collective-permute-start | bytes 983048 | tf_op jit(solution)/shard_map/ppermute | solution.py:98
  21.2 13.1 %collective-permute-start.6 = (bf16[1152,256]{1,0:T(8,128)(2,1)S(1)}, bf16[1152,256]{1,0:T(8,128)(2,1)S(1)}, u32[]{:S(2)}, u32[]{:S(2)}) collective-permute-start(bf16[1152,256]{1,0:T(8,128)(2,1)S(1)} %collective-permute-done.1.refs_4_), channel_id=1, source_target_pairs={{0,0},{1,1},{2,2},{3,3},{4,8},{5,9},{6,10},{7,11},{8,4},{9,5},{10,... | collective-permute-start | bytes 1769480 | tf_op jit(solution)/shard_map/ppermute | solution.py:98
  21.9 15.8 %collective-permute-start.7 = (bf16[1152,256]{1,0:T(8,128)(2,1)S(1)}, bf16[1152,256]{1,0:T(8,128)(2,1)S(1)}, u32[]{:S(2)}, u32[]{:S(2)}) collective-permute-start(bf16[1152,256]{1,0:T(8,128)(2,1)S(1)} %collective-permute-done.4.refs_3_), channel_id=1, source_target_pairs={{4,0},{5,1},{6,2},{7,3},{8,12},{9,13},{10,14},{11,15},{20,16},{21,... | collective-permute-start | bytes 1769480 | tf_op jit(solution)/shard_map/ppermute | solution.py:98
  23.2 11.1 %collective-permute-start.3 = (bf16[160,1024]{1,0:T(8,128)(2,1)S(1)}, bf16[160,1024]{1,0:T(8,128)(2,1)S(1)}, u32[]{:S(2)}, u32[]{:S(2)}) collective-permute-start(bf16[160,1024]{1,0:T(8,128)(2,1)S(1)} %get-tuple-element.30), channel_id=1, source_target_pairs={{0,20},{1,21},{2,22},{3,23},{12,24},{13,25},{14,26},{15,27},{16,4}... | collective-permute-start | bytes 983048 | tf_op jit(solution)/shard_map/ppermute | solution.py:98
  30.4 19.1 %collective-permute-start.13 = (f32[384,128]{1,0:T(8,128)S(1)}, f32[384,128]{1,0:T(8,128)S(1)}, u32[]{:S(2)}, u32[]{:S(2)}) collective-permute-start(f32[384,128]{1,0:T(8,128)S(1)} %get-tuple-element.43), channel_id=1, source_target_pairs={{0,1},{1,0},{2,3},{3,2},{4,5},{5,4},{6,7},{7,6},{8,9},{9,8},{10,11... | collective-permute-start | bytes 589832 | tf_op jit(solution)/shard_map/ppermute | solution.py:98
  38.4 4.1 %collective-permute-start.8 = (f32[16,528]{1,0:T(8,128)S(1)}, f32[16,528]{1,0:T(8,128)S(1)}, u32[]{:S(2)}, u32[]{:S(2)}) collective-permute-start(f32[16,528]{1,0:T(8,128)S(1)} %get-tuple-element.39), channel_id=1, source_target_pairs={{0,16},{1,17},{2,18},{3,19},{4,20},{5,21},{6,22},{7,23},{8,24},{9,... | collective-permute-start | bytes 101384 | tf_op jit(solution)/shard_map/ppermute | solution.py:98
  40.0 9.5 %collective-permute-start.14 = (bf16[256,128]{1,0:T(8,128)(2,1)S(1)}, bf16[256,128]{1,0:T(8,128)(2,1)S(1)}, u32[]{:S(2)}, u32[]{:S(2)}) collective-permute-start(bf16[256,128]{1,0:T(8,128)(2,1)S(1)} %get-tuple-element.46.last_up), channel_id=1, source_target_pairs={{0,4},{1,5},{2,6},{3,7},{4,0},{5,1},{6,2},{7,3},{8,12},{9,13},{10,... | collective-permute-start | bytes 196616 | tf_op jit(solution)/shard_map/ppermute | solution.py:98
  42.5 6.8 %collective-permute-start.10 = (f32[16,512]{1,0:T(8,128)S(1)}, f32[16,512]{1,0:T(8,128)S(1)}, u32[]{:S(2)}, u32[]{:S(2)}) collective-permute-start(f32[16,512]{1,0:T(8,128)S(1)} %get-tuple-element.41), channel_id=1, source_target_pairs={{0,6},{1,7},{2,4},{3,5},{4,2},{5,3},{6,0},{7,1},{8,14},{9,15},{10,... | collective-permute-start | bytes 98312 | tf_op jit(solution)/shard_map/ppermute | solution.py:98
  44.9 4.4 %collective-permute-start.11 = (f32[16,512]{1,0:T(8,128)S(1)}, f32[16,512]{1,0:T(8,128)S(1)}, u32[]{:S(2)}, u32[]{:S(2)}) collective-permute-start(f32[16,512]{1,0:T(8,128)S(1)} %get-tuple-element.41), channel_id=1, source_target_pairs={{0,4},{1,5},{2,6},{3,7},{4,0},{5,1},{6,2},{7,3},{8,12},{9,13},{10,... | collective-permute-start | bytes 98312 | tf_op jit(solution)/shard_map/ppermute | solution.py:98
  45.5 3.8 %collective-permute-start.9 = (f32[16,384]{1,0:T(8,128)S(1)}, f32[16,384]{1,0:T(8,128)S(1)}, u32[]{:S(2)}, u32[]{:S(2)}) collective-permute-start(f32[16,384]{1,0:T(8,128)S(1)} %get-tuple-element.40.low), channel_id=1, source_target_pairs={{0,2},{1,3},{2,0},{3,1},{4,6},{5,7},{6,4},{7,5},{8,10},{9,11},{10,... | collective-permute-start | bytes 73736 | tf_op jit(solution)/shard_map/ppermute | solution.py:98
  49.5 1.2 %collective-permute-start.12 = (f32[16,384]{1,0:T(8,128)S(1)}, f32[16,384]{1,0:T(8,128)S(1)}, u32[]{:S(2)}, u32[]{:S(2)}) collective-permute-start(f32[16,384]{1,0:T(8,128)S(1)} %shard_map.72.near), channel_id=1, source_target_pairs={{0,1},{1,0},{2,3},{3,2},{4,5},{5,4},{6,7},{7,6},{8,9},{9,8},{10,11... | collective-permute-start | bytes 73736 | tf_op jit(solution)/shard_map/ppermute | solution.py:98

commit v21 on v19

--- a/solution.py
+++ b/solution.py
@@ -289,17 +289,15 @@
     token_refs, rest = refs[:groups], refs[groups:]
     hops, rest = rest[:groups], rest[groups:]
     hop_masks, rest = rest[:groups], rest[groups:]
-    folded, mask, inside, outside, low, hop_low, away, last_up = rest
+    folded, mask, inside, outside, mine, away, last_up = rest
+    sums = (mine, away)
     columns = inside.shape[1]
 
     def finish(block):
         for n, tokens in enumerate(token_refs):
             wide = jnp.dot(tokens[:rows, :], block[:part, :], preferred_element_type=jnp.float32)
             kept = fold(jnp.where(mask[n] > 0, wide, 0.0))
-            if n:
-                away[:, :rows] = low_rank(folded[n] + kept)
-            else:
-                low[...] = low_rank(folded[n] + kept)
+            sums[n][:, :rows] = low_rank(folded[n] + kept)
 
     middle = (a == 1) | (a == 2)
 
@@ -312,36 +310,30 @@
             kept = fold(jnp.where(hop_mask[...] > 0, wide, 0.0))
             rest_rows = -capacity % LANES
             kept = jnp.concatenate([kept, jnp.zeros((rest_rows, LANES), jnp.float32)], axis=0)
-            if n:
-                away[:, rows:] = low_rank(kept)[:, :capacity]
-            else:
-                hop_low[...] = low_rank(kept)[:, :capacity]
+            sums[n][:, rows:] = low_rank(kept)[:, :capacity]
 
     @pl.when(jnp.logical_not(middle))
     def _():
         finish(outside)
         last_up[...] = stacked(outside[part:, :], last_up.shape[1])
-        hop_low[...] = jnp.zeros(hop_low.shape, jnp.float32)
-        away[:, rows:] = jnp.zeros(hop_low.shape, jnp.float32)
-
-
-def near_body(low, hop_low, near, low_out, hop_out):
+        for total in sums:
+            total[:, rows:] = jnp.zeros((ADAPTER_RANK, capacity), jnp.float32)
+
+
+def near_body(mine, near_far, near, far, low, hop):
     rows = low.shape[1]
-    capacity = hop_low.shape[1]
-    low_out[...] = low[...] + near[:, :rows]
-    hop_out[...] = jnp.zeros(hop_out.shape, jnp.float32)
-    hop_out[:, :capacity] = hop_low[...] + near[:, rows:]
-
-
-def merge_body(low, far, places, hop_far, hop, out):
-    capacity = places.shape[0]
-    back = hop[:, :capacity] + hop_far[:, :capacity]
+    low[...] = (mine[:, :rows] + far[:, :rows]) + (near[:, :rows] + near_far[:, :rows])
+    hop[...] = (mine[:, rows:] + far[:, rows:]) + (near[:, rows:] + near_far[:, rows:])
+
+
+def merge_body(low, places, hop, out):
+    back = hop[...]
     spread = jnp.zeros(low.shape, jnp.float32)
     for _ in range(3):
         piece = back.astype(jnp.bfloat16)
         back = back - piece.astype(jnp.float32)
         spread = spread + jnp.dot(piece, places[...], preferred_element_type=jnp.float32)
-    out[...] = low[...] + far[...] + spread
+    out[...] = low[...] + spread
 
 
 def finish_body(near, far, keep, got, numbers, ups, last_up, distant, out):
@@ -467,33 +459,24 @@
             (None, pl.ANY),
         )
         hop_masks.append(latest)
-    low, hop_low, away, last_up = kernel(
+    mine, away, last_up = kernel(
         functools.partial(last_body, part, rows, capacity),
-        [
-            wide(ADAPTER_RANK, rows),
-            wide(ADAPTER_RANK, capacity),
-            wide(ADAPTER_RANK, rows + capacity),
-            narrow(columns, keys),
-        ],
+        [wide(ADAPTER_RANK, rows + capacity)] * groups + [narrow(columns, keys)],
         (*token_parts, *hops, *hop_masks, folded, mask, inside, outside),
         2 * groups * (rows + capacity) * part * columns,
     )
 
+    near_far = exchange(away, 1, 2, SAME)
     near = exchange(away, 1, 0, SAME)
+    far = exchange(mine, 0, 2, SAME)
     distant = exchange(last_up, 0, 0, BESIDE)
     low, hop_low = kernel(
         near_body,
-        [wide(ADAPTER_RANK, rows), wide(ADAPTER_RANK, rows + LANES)],
-        (low, hop_low, near),
+        [wide(ADAPTER_RANK, rows), wide(ADAPTER_RANK, capacity)],
+        (mine, near_far, near, far),
     )
     back = exchange(hop_low, 0, 0, BESIDE)
-    back_far = exchange(hop_low, 0, 2, BESIDE)
-    low_far = exchange(low, 0, 2, SAME)
-    low = kernel(
-        merge_body,
-        wide(ADAPTER_RANK, rows),
-        (low, low_far, places, back_far, back),
-    )
+    low = kernel(merge_body, wide(ADAPTER_RANK, rows), (low, places, back))
     got = exchange(give, 0, 1, SAME)
     low_far = exchange(low, 0, 1, SAME)
     return kernel(

time: 52.2 us -> 52.1 us (level)
  transfers between devices with their start and end apart: 15 -> 15, of which waited for: 6 -> 7; matrix products, arithmetic and copies ran while one was open for 0% -> 0% of each run, Pallas kernels for 12% -> 12%
where the time goes in v21:
time: 52.1 us; the launch traced here: 51.9 us
  starting transfers between devices  24.9 us (48%)
  waiting for transfers between devices  18.3 us (35%)
  Pallas kernels  8.46 us (16%)
    ppermute x15, starting transfers between devices, exchange(): return lax.ppermute(x, AXES, pairs)  24.9 us
    ppermute x15, waiting for transfers between devices, exchange(): return lax.ppermute(x, AXES, pairs)  18.3 us
    pallas_call x11, Pallas kernels, kernel(): pl.pallas_call(body, out_shape=outs, in_specs=specs or [inner] * len(oper...  8.46 us
  transfers between devices with their start and end apart: 15, of which 7 were waited for; matrix products, arithmetic and copies ran while one was open for 0% of the time, Pallas kernels for 12%

profile of v21, /device:TPU:0, one launch (start us, length us, event | category | flops | bytes accessed | tf_op | source)
XLA Modules:
  0.0 51.9 jit_solution(5362742045995936923)
XLA Ops:
  0.0 1.1 %shard_map.64._.refs_2_ = bf16[1152,256]{1,0:T(8,128)(2,1)S(1)} custom-call(bf16[2048,256]{1,0:T(8,128)(2,1)} %down.1, bf16[256,128]{1,0:T(8,128)(2,1)} %up.1), custom_call_target="tpu_custom_call" | custom-call | bytes 1703936 | tf_op jit(solution)/shard_map/pallas_call | solution.py:120
  1.1 0.0 copy-start
  1.1 3.1 %collective-permute-start.1 = (bf16[1152,256]{1,0:T(8,128)(2,1)S(1)}, bf16[1152,256]{1,0:T(8,128)(2,1)S(1)}, u32[]{:S(2)}, u32[]{:S(2)}) collective-permute-start(bf16[1152,256]{1,0:T(8,128)(2,1)S(1)} %shard_map.64._.refs_2_), channel_id=1, source_target_pairs={{0,4},{1,5},{2,6},{3,7},{4,0},{5,1},{6,2},{7,3},{8,12},{9,13},{10,... | collective-permute-start | bytes 1769480 | tf_op jit(solution)/shard_map/ppermute | solution.py:98
  4.2 1.4 %shard_map.65 = (bf16[400,1024]{1,0:T(8,128)(2,1)S(1)}, bf16[400,1024]{1,0:T(8,128)(2,1)S(1)}) custom-call(bf16[384,2048]{1,0:T(8,128)(2,1)} %tokens.1, s32[1,384]{1,0:T(1,128)} %bitcast.1, s32[384]{0:T(512)} %slot_in.1, bf16[1152,256]{1,0:T(8,128)(2,1)S(1)} %shard_map.64._.refs_2_), custom_call_target="tpu_custom_call" | custom-call | bytes 3804160 | tf_op jit(solution)/shard_map/pallas_call | solution.py:120
  5.6 0.7 %collective-permute-start.4 = (bf16[1152,256]{1,0:T(8,128)(2,1)S(1)}, bf16[1152,256]{1,0:T(8,128)(2,1)S(1)}, u32[]{:S(2)}, u32[]{:S(2)}) collective-permute-start(bf16[1152,256]{1,0:T(8,128)(2,1)S(1)} %shard_map.64._.refs_2_), channel_id=1, source_target_pairs={{0,0},{1,1},{2,2},{3,3},{4,8},{5,9},{6,10},{7,11},{8,4},{9,5},{10,... | collective-permute-start | bytes 1769480 | tf_op jit(solution)/shard_map/ppermute | solution.py:98
  6.3 1.6 %collective-permute-start = (bf16[400,1024]{1,0:T(8,128)(2,1)S(1)}, bf16[400,1024]{1,0:T(8,128)(2,1)S(1)}, u32[]{:S(2)}, u32[]{:S(2)}) collective-permute-start(bf16[400,1024]{1,0:T(8,128)(2,1)S(1)} %get-tuple-element.27.away), channel_id=1, source_target_pairs={{0,16},{1,17},{2,18},{3,19},{4,20},{5,21},{6,22},{7,23},{8,24},{9,... | collective-permute-start | bytes 2457608 | tf_op jit(solution)/shard_map/ppermute | solution.py:98
  7.9 0.7 %shard_map.66 = (bf16[160,1024]{1,0:T(8,128)(2,1)S(1)}, bf16[160,1024]{1,0:T(8,128)(2,1)S(1)}, bf16[144,384]{1,0:T(8,128)(2,1)S(1)}) custom-call(bf16[400,1024]{1,0:T(8,128)(2,1)S(1)} %get-tuple-element.26.own.refs_0_, bf16[400,1024]{1,0:T(8,128)(2,1)S(1)} %get-tuple-element.27.away), custom_call_target="tpu_custom_call" | custom-call | flops 226492416 | bytes 2404352 | tf_op jit(solution)/shard_map/pallas_call | solution.py:120
  8.6 0.0 copy-done
  8.6 1.1 %shard_map.67 = (f32[384,256]{1,0:T(8,128)S(1)}, f32[384,256]{1,0:T(8,128)S(1)}) custom-call(bf16[400,1024]{1,0:T(8,128)(2,1)S(1)} %get-tuple-element.26.own.refs_0_, bf16[400,1024]{1,0:T(8,128)(2,1)S(1)} %get-tuple-element.27.away, bf16[2048,512]{1,0:T(8,128)(2,1)S(1)} %copy-done, bf16[144,384]{1,0:T(8,128)(2,1)S(1)} %get-tuple-element.32._.places), custom_call_target="tpu_custom_call" | custom-call | flops 805306368 | bytes 4632576 | tf_op jit(solution)/shard_map/pallas_call | solution.py:120
  9.7 1.6 %collective-permute-start.5 = (f32[384,256]{1,0:T(8,128)S(1)}, f32[384,256]{1,0:T(8,128)S(1)}, u32[]{:S(2)}, u32[]{:S(2)}) collective-permute-start(f32[384,256]{1,0:T(8,128)S(1)} %get-tuple-element.34), channel_id=1, source_target_pairs={{0,2},{1,3},{2,0},{3,1},{4,6},{5,7},{6,4},{7,5},{8,10},{9,11},{10,... | collective-permute-start | bytes 1179656 | tf_op jit(solution)/shard_map/ppermute | solution.py:98
  11.2 6.3 %collective-permute-done.1.refs_4_ = bf16[1152,256]{1,0:T(8,128)(2,1)S(1)} collective-permute-done((bf16[1152,256]{1,0:T(8,128)(2,1)S(1)}, bf16[1152,256]{1,0:T(8,128)(2,1)S(1)}, u32[]{:S(2)}, u32[]{:S(2)}) %collective-permute-start.1) | collective-permute-done | bytes 589856 | tf_op jit(solution)/shard_map/ppermute | solution.py:98
  17.5 3.7 %collective-permute-start.2 = (bf16[160,1024]{1,0:T(8,128)(2,1)S(1)}, bf16[160,1024]{1,0:T(8,128)(2,1)S(1)}, u32[]{:S(2)}, u32[]{:S(2)}) collective-permute-start(bf16[160,1024]{1,0:T(8,128)(2,1)S(1)} %get-tuple-element.29), channel_id=1, source_target_pairs={{0,4},{1,5},{2,6},{3,7},{12,8},{13,9},{14,10},{15,11},{16,20},{17,... | collective-permute-start | bytes 983048 | tf_op jit(solution)/shard_map/ppermute | solution.py:98
  21.2 0.7 %collective-permute-start.6 = (bf16[1152,256]{1,0:T(8,128)(2,1)S(1)}, bf16[1152,256]{1,0:T(8,128)(2,1)S(1)}, u32[]{:S(2)}, u32[]{:S(2)}) collective-permute-start(bf16[1152,256]{1,0:T(8,128)(2,1)S(1)} %collective-permute-done.1.refs_4_), channel_id=1, source_target_pairs={{0,0},{1,1},{2,2},{3,3},{4,8},{5,9},{6,10},{7,11},{8,4},{9,5},{10,... | collective-permute-start | bytes 1769480 | tf_op jit(solution)/shard_map/ppermute | solution.py:98
  21.9 0.0 collective-permute-done.4.refs_3_
  21.9 1.3 %collective-permute-start.7 = (bf16[1152,256]{1,0:T(8,128)(2,1)S(1)}, bf16[1152,256]{1,0:T(8,128)(2,1)S(1)}, u32[]{:S(2)}, u32[]{:S(2)}) collective-permute-start(bf16[1152,256]{1,0:T(8,128)(2,1)S(1)} %collective-permute-done.4.refs_3_), channel_id=1, source_target_pairs={{4,0},{5,1},{6,2},{7,3},{8,12},{9,13},{10,14},{11,15},{20,16},{21,... | collective-permute-start | bytes 1769480 | tf_op jit(solution)/shard_map/ppermute | solution.py:98
  23.2 0.0 collective-permute-done.5.refs_6_
  23.2 5.6 %collective-permute-start.3 = (bf16[160,1024]{1,0:T(8,128)(2,1)S(1)}, bf16[160,1024]{1,0:T(8,128)(2,1)S(1)}, u32[]{:S(2)}, u32[]{:S(2)}) collective-permute-start(bf16[160,1024]{1,0:T(8,128)(2,1)S(1)} %get-tuple-element.30), channel_id=1, source_target_pairs={{0,20},{1,21},{2,22},{3,23},{12,24},{13,25},{14,26},{15,27},{16,4}... | collective-permute-start | bytes 983048 | tf_op jit(solution)/shard_map/ppermute | solution.py:98
  28.8 0.0 collective-permute-done.refs_1_
  28.8 1.6 %shard_map.68 = (f32[2,384,128]{2,1,0:T(8,128)S(1)}, f32[2,384,256]{2,1,0:T(8,128)S(1)}, f32[384,1]{1,0:T(8,128)S(1)}, bf16[3,256,128]{2,1,0:T(8,128)(2,1)S(1)},...) custom-call(bf16[400,1024]{1,0:T(8,128)(2,1)S(1)} %get-tuple-element.26.own.refs_0_, ...), custom_call_target="tpu_custom_call" | custom-call | tf_op jit(solution)/shard_map/pallas_call | solution.py:120
  30.4 0.1 collective-permute-start.13
  30.4 0.0 collective-permute-done.2.hop.refs_2_
  30.4 0.3 shard_map.69._.refs_4_
  30.7 3.6 %collective-permute-done.3.hop.refs_3_ = bf16[160,1024]{1,0:T(8,128)(2,1)S(1)} collective-permute-done((bf16[160,1024]{1,0:T(8,128)(2,1)S(1)}, bf16[160,1024]{1,0:T(8,128)(2,1)S(1)}, u32[]{:S(2)}, u32[]{:S(2)}) %collective-permute-start.3) | collective-permute-done | bytes 327712 | tf_op jit(solution)/shard_map/ppermute | solution.py:98
  34.3 0.3 shard_map.70.refs_5_
  34.6 0.0 collective-permute-done.6.refs_8_
  34.6 3.1 %collective-permute-done.7.refs_9_ = bf16[1152,256]{1,0:T(8,128)(2,1)S(1)} collective-permute-done((bf16[1152,256]{1,0:T(8,128)(2,1)S(1)}, bf16[1152,256]{1,0:T(8,128)(2,1)S(1)}, u32[]{:S(2)}, u32[]{:S(2)}) %collective-permute-start.7) | collective-permute-done | bytes 589856 | tf_op jit(solution)/shard_map/ppermute | solution.py:98
  37.7 0.7 %shard_map.71 = (f32[16,528]{1,0:T(8,128)S(1)}, f32[16,528]{1,0:T(8,128)S(1)}, bf16[256,128]{1,0:T(8,128)(2,1)S(1)}) custom-call(bf16[400,1024]{1,0:T(8,128)(2,1)S(1)} %get-tuple-element.26.own.refs_0_, bf16[400,1024]{1,0:T(8,128)(2,1)S(1)} %collective-permute-done.refs_1_, bf16[160,1024]{1,0:T(8,128)(2,1)S(1)} %collective-permute-done.2.hop.refs_2_, ...), custom_call_target="tpu_custom_call" | custom-call | flops 553648128 | bytes 5081088 | tf_op jit(solution)/shard_map/pallas_call | solution.py:120
  38.4 2.5 %collective-permute-start.8 = (f32[16,528]{1,0:T(8,128)S(1)}, f32[16,528]{1,0:T(8,128)S(1)}, u32[]{:S(2)}, u32[]{:S(2)}) collective-permute-start(f32[16,528]{1,0:T(8,128)S(1)} %get-tuple-element.39), channel_id=1, source_target_pairs={{0,18},{1,19},{2,16},{3,17},{4,22},{5,23},{6,20},{7,21},{8,26},{9,... | collective-permute-start | bytes 101384 | tf_op jit(solution)/shard_map/ppermute | solution.py:98
  40.9 0.5 collective-permute-start.9
  41.4 0.5 %collective-permute-start.10 = (f32[16,528]{1,0:T(8,128)S(1)}, f32[16,528]{1,0:T(8,128)S(1)}, u32[]{:S(2)}, u32[]{:S(2)}) collective-permute-start(f32[16,528]{1,0:T(8,128)S(1)} %get-tuple-element.38.mine), channel_id=1, source_target_pairs={{0,2},{1,3},{2,0},{3,1},{4,6},{5,7},{6,4},{7,5},{8,10},{9,11},{10,... | collective-permute-start | bytes 101384 | tf_op jit(solution)/shard_map/ppermute | solution.py:98
  41.9 1.6 %collective-permute-start.14 = (bf16[256,128]{1,0:T(8,128)(2,1)S(1)}, bf16[256,128]{1,0:T(8,128)(2,1)S(1)}, u32[]{:S(2)}, u32[]{:S(2)}) collective-permute-start(bf16[256,128]{1,0:T(8,128)(2,1)S(1)} %get-tuple-element.46.last_up), channel_id=1, source_target_pairs={{0,4},{1,5},{2,6},{3,7},{4,0},{5,1},{6,2},{7,3},{8,12},{9,13},{10,... | collective-permute-start | bytes 196616 | tf_op jit(solution)/shard_map/ppermute | solution.py:98
  43.5 0.0 collective-permute-done.8.near_far
  43.5 1.4 %collective-permute-done.9.near = f32[16,528]{1,0:T(8,128)S(1)} collective-permute-done((f32[16,528]{1,0:T(8,128)S(1)}, f32[16,528]{1,0:T(8,128)S(1)}, u32[]{:S(2)}, u32[]{:S(2)}) %collective-permute-start.9) | collective-permute-done | bytes 33824 | tf_op jit(solution)/shard_map/ppermute | solution.py:98
  44.9 0.5 collective-permute-done.10.far
  45.4 1.5 %collective-permute-start.11 = (f32[16,144]{1,0:T(8,128)S(1)}, f32[16,144]{1,0:T(8,128)S(1)}, u32[]{:S(2)}, u32[]{:S(2)}) collective-permute-start(f32[16,144]{1,0:T(8,128)S(1)} %get-tuple-element.41), channel_id=1, source_target_pairs={{0,4},{1,5},{2,6},{3,7},{4,0},{5,1},{6,2},{7,3},{8,12},{9,13},{10,... | collective-permute-start | bytes 27656 | tf_op jit(solution)/shard_map/ppermute | solution.py:98
  46.9 2.3 %collective-permute-done.11.hop = f32[16,144]{1,0:T(8,128)S(1)} collective-permute-done((f32[16,144]{1,0:T(8,128)S(1)}, f32[16,144]{1,0:T(8,128)S(1)}, u32[]{:S(2)}, u32[]{:S(2)}) %collective-permute-start.11) | collective-permute-done | bytes 9248 | tf_op jit(solution)/shard_map/ppermute | solution.py:98
  49.2 0.1 shard_map.73.near
  49.4 0.0 collective-permute-start.12
  49.4 0.0 collective-permute-done.13.got
  49.4 0.0 collective-permute-done.14.distant
  49.4 1.2 %collective-permute-done.12.far = f32[16,384]{1,0:T(8,128)S(1)} collective-permute-done((f32[16,384]{1,0:T(8,128)S(1)}, f32[16,384]{1,0:T(8,128)S(1)}, u32[]{:S(2)}, u32[]{:S(2)}) %collective-permute-start.12) | collective-permute-done | bytes 24608 | tf_op jit(solution)/shard_map/ppermute | solution.py:98
  50.6 1.3 %shard_map.74 = bf16[384,128]{1,0:T(8,128)(2,1)} custom-call(f32[16,384]{1,0:T(8,128)S(1)} %shard_map.73.near, f32[16,384]{1,0:T(8,128)S(1)} %collective-permute-done.12.far, f32[384,128]{1,0:T(8,128)S(1)} %get-tuple-element.42.keep, f32[384,128]{1,0:T(8,128)S(1)} %collective-permute-done.13.got, f32[384,1]{1,0:T(8,128)S(1)} %get-tuple-element.44.numbers, ...), custom_call_target="tpu_custom_call" | custom-call | bytes 869888 | tf_op jit(solution)/shard_map/pallas_call | solution.py:120
  (1 shorter events, 0.0 us)
Async XLA Ops:
  1.1 7.5 %copy-start = (bf16[2048,512]{1,0:T(8,128)(2,1)S(1)}, bf16[2048,512]{1,0:T(8,128)(2,1)}, u32[]{:S(2)}) copy-start(bf16[2048,512]{1,0:T(8,128)(2,1)} %weights.1) | copy-start | bytes 6291460
  1.1 16.4 %collective-permute-start.1 = (bf16[1152,256]{1,0:T(8,128)(2,1)S(1)}, bf16[1152,256]{1,0:T(8,128)(2,1)S(1)}, u32[]{:S(2)}, u32[]{:S(2)}) collective-permute-start(bf16[1152,256]{1,0:T(8,128)(2,1)S(1)} %shard_map.64._.refs_2_), channel_id=1, source_target_pairs={{0,4},{1,5},{2,6},{3,7},{4,0},{5,1},{6,2},{7,3},{8,12},{9,13},{10,... | collective-permute-start | bytes 1769480 | tf_op jit(solution)/shard_map/ppermute | solution.py:98
  5.6 16.3 %collective-permute-start.4 = (bf16[1152,256]{1,0:T(8,128)(2,1)S(1)}, bf16[1152,256]{1,0:T(8,128)(2,1)S(1)}, u32[]{:S(2)}, u32[]{:S(2)}) collective-permute-start(bf16[1152,256]{1,0:T(8,128)(2,1)S(1)} %shard_map.64._.refs_2_), channel_id=1, source_target_pairs={{0,0},{1,1},{2,2},{3,3},{4,8},{5,9},{6,10},{7,11},{8,4},{9,5},{10,... | collective-permute-start | bytes 1769480 | tf_op jit(solution)/shard_map/ppermute | solution.py:98
  6.3 22.4 %collective-permute-start = (bf16[400,1024]{1,0:T(8,128)(2,1)S(1)}, bf16[400,1024]{1,0:T(8,128)(2,1)S(1)}, u32[]{:S(2)}, u32[]{:S(2)}) collective-permute-start(bf16[400,1024]{1,0:T(8,128)(2,1)S(1)} %get-tuple-element.27.away), channel_id=1, source_target_pairs={{0,16},{1,17},{2,18},{3,19},{4,20},{5,21},{6,22},{7,23},{8,24},{9,... | collective-permute-start | bytes 2457608 | tf_op jit(solution)/shard_map/ppermute | solution.py:98
  9.7 13.5 %collective-permute-start.5 = (f32[384,256]{1,0:T(8,128)S(1)}, f32[384,256]{1,0:T(8,128)S(1)}, u32[]{:S(2)}, u32[]{:S(2)}) collective-permute-start(f32[384,256]{1,0:T(8,128)S(1)} %get-tuple-element.34), channel_id=1, source_target_pairs={{0,2},{1,3},{2,0},{3,1},{4,6},{5,7},{6,4},{7,5},{8,10},{9,11},{10,... | collective-permute-start | bytes 1179656 | tf_op jit(solution)/shard_map/ppermute | solution.py:98
  17.5 12.9 %collective-permute-start.2 = (bf16[160,1024]{1,0:T(8,128)(2,1)S(1)}, bf16[160,1024]{1,0:T(8,128)(2,1)S(1)}, u32[]{:S(2)}, u32[]{:S(2)}) collective-permute-start(bf16[160,1024]{1,0:T(8,128)(2,1)S(1)} %get-tuple-element.29), channel_id=1, source_target_pairs={{0,4},{1,5},{2,6},{3,7},{12,8},{13,9},{14,10},{15,11},{16,20},{17,... | collective-permute-start | bytes 983048 | tf_op jit(solution)/shard_map/ppermute | solution.py:98
  21.2 13.4 %collective-permute-start.6 = (bf16[1152,256]{1,0:T(8,128)(2,1)S(1)}, bf16[1152,256]{1,0:T(8,128)(2,1)S(1)}, u32[]{:S(2)}, u32[]{:S(2)}) collective-permute-start(bf16[1152,256]{1,0:T(8,128)(2,1)S(1)} %collective-permute-done.1.refs_4_), channel_id=1, source_target_pairs={{0,0},{1,1},{2,2},{3,3},{4,8},{5,9},{6,10},{7,11},{8,4},{9,5},{10,... | collective-permute-start | bytes 1769480 | tf_op jit(solution)/shard_map/ppermute | solution.py:98
  21.9 15.8 %collective-permute-start.7 = (bf16[1152,256]{1,0:T(8,128)(2,1)S(1)}, bf16[1152,256]{1,0:T(8,128)(2,1)S(1)}, u32[]{:S(2)}, u32[]{:S(2)}) collective-permute-start(bf16[1152,256]{1,0:T(8,128)(2,1)S(1)} %collective-permute-done.4.refs_3_), channel_id=1, source_target_pairs={{4,0},{5,1},{6,2},{7,3},{8,12},{9,13},{10,14},{11,15},{20,16},{21,... | collective-permute-start | bytes 1769480 | tf_op jit(solution)/shard_map/ppermute | solution.py:98
  23.2 11.1 %collective-permute-start.3 = (bf16[160,1024]{1,0:T(8,128)(2,1)S(1)}, bf16[160,1024]{1,0:T(8,128)(2,1)S(1)}, u32[]{:S(2)}, u32[]{:S(2)}) collective-permute-start(bf16[160,1024]{1,0:T(8,128)(2,1)S(1)} %get-tuple-element.30), channel_id=1, source_target_pairs={{0,20},{1,21},{2,22},{3,23},{12,24},{13,25},{14,26},{15,27},{16,4}... | collective-permute-start | bytes 983048 | tf_op jit(solution)/shard_map/ppermute | solution.py:98
  30.4 19.0 %collective-permute-start.13 = (f32[384,128]{1,0:T(8,128)S(1)}, f32[384,128]{1,0:T(8,128)S(1)}, u32[]{:S(2)}, u32[]{:S(2)}) collective-permute-start(f32[384,128]{1,0:T(8,128)S(1)} %get-tuple-element.43), channel_id=1, source_target_pairs={{0,1},{1,0},{2,3},{3,2},{4,5},{5,4},{6,7},{7,6},{8,9},{9,8},{10,11... | collective-permute-start | bytes 589832 | tf_op jit(solution)/shard_map/ppermute | solution.py:98
  38.4 5.1 %collective-permute-start.8 = (f32[16,528]{1,0:T(8,128)S(1)}, f32[16,528]{1,0:T(8,128)S(1)}, u32[]{:S(2)}, u32[]{:S(2)}) collective-permute-start(f32[16,528]{1,0:T(8,128)S(1)} %get-tuple-element.39), channel_id=1, source_target_pairs={{0,18},{1,19},{2,16},{3,17},{4,22},{5,23},{6,20},{7,21},{8,26},{9,... | collective-permute-start | bytes 101384 | tf_op jit(solution)/shard_map/ppermute | solution.py:98
  40.9 4.0 %collective-permute-start.9 = (f32[16,528]{1,0:T(8,128)S(1)}, f32[16,528]{1,0:T(8,128)S(1)}, u32[]{:S(2)}, u32[]{:S(2)}) collective-permute-start(f32[16,528]{1,0:T(8,128)S(1)} %get-tuple-element.39), channel_id=1, source_target_pairs={{0,16},{1,17},{2,18},{3,19},{4,20},{5,21},{6,22},{7,23},{8,24},{9,... | collective-permute-start | bytes 101384 | tf_op jit(solution)/shard_map/ppermute | solution.py:98
  41.4 4.0 %collective-permute-start.10 = (f32[16,528]{1,0:T(8,128)S(1)}, f32[16,528]{1,0:T(8,128)S(1)}, u32[]{:S(2)}, u32[]{:S(2)}) collective-permute-start(f32[16,528]{1,0:T(8,128)S(1)} %get-tuple-element.38.mine), channel_id=1, source_target_pairs={{0,2},{1,3},{2,0},{3,1},{4,6},{5,7},{6,4},{7,5},{8,10},{9,11},{10,... | collective-permute-start | bytes 101384 | tf_op jit(solution)/shard_map/ppermute | solution.py:98
  41.9 7.5 %collective-permute-start.14 = (bf16[256,128]{1,0:T(8,128)(2,1)S(1)}, bf16[256,128]{1,0:T(8,128)(2,1)S(1)}, u32[]{:S(2)}, u32[]{:S(2)}) collective-permute-start(bf16[256,128]{1,0:T(8,128)(2,1)S(1)} %get-tuple-element.46.last_up), channel_id=1, source_target_pairs={{0,4},{1,5},{2,6},{3,7},{4,0},{5,1},{6,2},{7,3},{8,12},{9,13},{10,... | collective-permute-start | bytes 196616 | tf_op jit(solution)/shard_map/ppermute | solution.py:98
  45.4 3.8 %collective-permute-start.11 = (f32[16,144]{1,0:T(8,128)S(1)}, f32[16,144]{1,0:T(8,128)S(1)}, u32[]{:S(2)}, u32[]{:S(2)}) collective-permute-start(f32[16,144]{1,0:T(8,128)S(1)} %get-tuple-element.41), channel_id=1, source_target_pairs={{0,4},{1,5},{2,6},{3,7},{4,0},{5,1},{6,2},{7,3},{8,12},{9,13},{10,... | collective-permute-start | bytes 27656 | tf_op jit(solution)/shard_map/ppermute | solution.py:98
  49.4 1.2 %collective-permute-start.12 = (f32[16,384]{1,0:T(8,128)S(1)}, f32[16,384]{1,0:T(8,128)S(1)}, u32[]{:S(2)}, u32[]{:S(2)}) collective-permute-start(f32[16,384]{1,0:T(8,128)S(1)} %shard_map.73.near), channel_id=1, source_target_pairs={{0,1},{1,0},{2,3},{3,2},{4,5},{5,4},{6,7},{7,6},{8,9},{9,8},{10,11... | collective-permute-start | bytes 73736 | tf_op jit(solution)/shard_map/ppermute | solution.py:98

commit v22 on v20

--- a/solution.py
+++ b/solution.py
@@ -330,17 +330,19 @@
         away[:, rows:] = jnp.zeros(hop_low.shape, jnp.float32)
 
 
-def near_body(low, hop_low, near, low_out, hop_out):
+def near_body(low, hop_low, near, low_out, hop_out, hop_wide):
     rows = low.shape[1]
     capacity = hop_low.shape[1]
     low_out[...] = low[...] + near[:, :rows]
-    hop_out[...] = jnp.zeros(hop_out.shape, jnp.float32)
-    hop_out[:, :capacity] = hop_low[...] + near[:, rows:]
+    hop = hop_low[...] + near[:, rows:]
+    hop_out[...] = hop
+    hop_wide[...] = jnp.zeros(hop_wide.shape, jnp.float32)
+    hop_wide[:, :capacity] = hop
 
 
 def merge_body(low, far, places, hop_far, hop, out):
     capacity = places.shape[0]
-    back = hop[:, :capacity] + hop_far[:, :capacity]
+    back = hop[...] + hop_far[:, :capacity]
     spread = jnp.zeros(low.shape, jnp.float32)
     for _ in range(3):
         piece = back.astype(jnp.bfloat16)
@@ -486,13 +488,17 @@
 
     near = exchange(away, 1, 0, SAME)
     distant = exchange(last_up, 0, 0, BESIDE)
-    low, hop_low = kernel(
+    low, hop_low, hop_wide = kernel(
         near_body,
-        [wide(ADAPTER_RANK, rows), wide(ADAPTER_RANK, rows + LANES)],
+        [
+            wide(ADAPTER_RANK, rows),
+            wide(ADAPTER_RANK, capacity),
+            wide(ADAPTER_RANK, rows + LANES),
+        ],
         (low, hop_low, near),
     )
     back = exchange(hop_low, 0, 0, BESIDE)
-    back_far = exchange(hop_low, 0, 2, BESIDE)
+    back_far = exchange(hop_wide, 0, 2, BESIDE)
     low_far = exchange(low, 0, 2, SAME)
     low = kernel(
         merge_body,

time: 52.2 us -> 52.1 us (level)
  no operation moved by 1% of the time
where the time goes in v22:
time: 52.1 us; the launch traced here: 51.8 us
  starting transfers between devices  25.1 us (48%)
  waiting for transfers between devices  18.4 us (35%)
  Pallas kernels  8.2 us (16%)
    ppermute x15, starting transfers between devices, exchange(): return lax.ppermute(x, AXES, pairs)  25.1 us
    ppermute x15, waiting for transfers between devices, exchange(): return lax.ppermute(x, AXES, pairs)  18.4 us
    pallas_call x10, Pallas kernels, kernel(): pl.pallas_call(body, out_shape=outs, in_specs=specs or [inner] * len(oper...  8.2 us
  transfers between devices with their start and end apart: 15, of which 6 were waited for; matrix products, arithmetic and copies ran while one was open for 0% of the time, Pallas kernels for 11%

profile of v22, /device:TPU:0, one launch (start us, length us, event | category | flops | bytes accessed | tf_op | source)
XLA Modules:
  0.0 51.8 jit_solution(16825634202971238179)
XLA Ops:
  0.0 1.1 %shard_map.64._.refs_2_ = bf16[1152,256]{1,0:T(8,128)(2,1)S(1)} custom-call(bf16[2048,256]{1,0:T(8,128)(2,1)} %down.1, bf16[256,128]{1,0:T(8,128)(2,1)} %up.1), custom_call_target="tpu_custom_call" | custom-call | bytes 1703936 | tf_op jit(solution)/shard_map/pallas_call | solution.py:120
  1.1 0.0 copy-start
  1.1 3.1 %collective-permute-start.1 = (bf16[1152,256]{1,0:T(8,128)(2,1)S(1)}, bf16[1152,256]{1,0:T(8,128)(2,1)S(1)}, u32[]{:S(2)}, u32[]{:S(2)}) collective-permute-start(bf16[1152,256]{1,0:T(8,128)(2,1)S(1)} %shard_map.64._.refs_2_), channel_id=1, source_target_pairs={{0,4},{1,5},{2,6},{3,7},{4,0},{5,1},{6,2},{7,3},{8,12},{9,13},{10,... | collective-permute-start | bytes 1769480 | tf_op jit(solution)/shard_map/ppermute | solution.py:98
  4.2 0.7 %collective-permute-start.4 = (bf16[1152,256]{1,0:T(8,128)(2,1)S(1)}, bf16[1152,256]{1,0:T(8,128)(2,1)S(1)}, u32[]{:S(2)}, u32[]{:S(2)}) collective-permute-start(bf16[1152,256]{1,0:T(8,128)(2,1)S(1)} %shard_map.64._.refs_2_), channel_id=1, source_target_pairs={{0,0},{1,1},{2,2},{3,3},{4,8},{5,9},{6,10},{7,11},{8,4},{9,5},{10,... | collective-permute-start | bytes 1769480 | tf_op jit(solution)/shard_map/ppermute | solution.py:98
  4.9 1.4 %shard_map.65 = (bf16[400,1024]{1,0:T(8,128)(2,1)S(1)}, bf16[400,1024]{1,0:T(8,128)(2,1)S(1)}) custom-call(bf16[384,2048]{1,0:T(8,128)(2,1)} %tokens.1, s32[1,384]{1,0:T(1,128)} %bitcast.1, s32[384]{0:T(512)} %slot_in.1, bf16[1152,256]{1,0:T(8,128)(2,1)S(1)} %shard_map.64._.refs_2_), custom_call_target="tpu_custom_call" | custom-call | bytes 3804160 | tf_op jit(solution)/shard_map/pallas_call | solution.py:120
  6.3 1.6 %collective-permute-start = (bf16[400,1024]{1,0:T(8,128)(2,1)S(1)}, bf16[400,1024]{1,0:T(8,128)(2,1)S(1)}, u32[]{:S(2)}, u32[]{:S(2)}) collective-permute-start(bf16[400,1024]{1,0:T(8,128)(2,1)S(1)} %get-tuple-element.28.away), channel_id=1, source_target_pairs={{0,16},{1,17},{2,18},{3,19},{4,20},{5,21},{6,22},{7,23},{8,24},{9,... | collective-permute-start | bytes 2457608 | tf_op jit(solution)/shard_map/ppermute | solution.py:98
  7.9 0.7 %shard_map.66 = (bf16[160,1024]{1,0:T(8,128)(2,1)S(1)}, bf16[160,1024]{1,0:T(8,128)(2,1)S(1)}, bf16[144,384]{1,0:T(8,128)(2,1)S(1)}) custom-call(bf16[400,1024]{1,0:T(8,128)(2,1)S(1)} %get-tuple-element.27.own.refs_0_, bf16[400,1024]{1,0:T(8,128)(2,1)S(1)} %get-tuple-element.28.away), custom_call_target="tpu_custom_call" | custom-call | flops 226492416 | bytes 2404352 | tf_op jit(solution)/shard_map/pallas_call | solution.py:120
  8.6 0.0 copy-done
  8.6 1.1 %shard_map.67 = (f32[384,256]{1,0:T(8,128)S(1)}, f32[384,256]{1,0:T(8,128)S(1)}) custom-call(bf16[400,1024]{1,0:T(8,128)(2,1)S(1)} %get-tuple-element.27.own.refs_0_, bf16[400,1024]{1,0:T(8,128)(2,1)S(1)} %get-tuple-element.28.away, bf16[2048,512]{1,0:T(8,128)(2,1)S(1)} %copy-done, bf16[144,384]{1,0:T(8,128)(2,1)S(1)} %get-tuple-element.32._.places), custom_call_target="tpu_custom_call" | custom-call | flops 805306368 | bytes 4632576 | tf_op jit(solution)/shard_map/pallas_call | solution.py:120
  9.7 1.6 %collective-permute-start.5 = (f32[384,256]{1,0:T(8,128)S(1)}, f32[384,256]{1,0:T(8,128)S(1)}, u32[]{:S(2)}, u32[]{:S(2)}) collective-permute-start(f32[384,256]{1,0:T(8,128)S(1)} %get-tuple-element.34), channel_id=1, source_target_pairs={{0,2},{1,3},{2,0},{3,1},{4,6},{5,7},{6,4},{7,5},{8,10},{9,11},{10,... | collective-permute-start | bytes 1179656 | tf_op jit(solution)/shard_map/ppermute | solution.py:98
  11.2 6.3 %collective-permute-done.1.refs_4_ = bf16[1152,256]{1,0:T(8,128)(2,1)S(1)} collective-permute-done((bf16[1152,256]{1,0:T(8,128)(2,1)S(1)}, bf16[1152,256]{1,0:T(8,128)(2,1)S(1)}, u32[]{:S(2)}, u32[]{:S(2)}) %collective-permute-start.1) | collective-permute-done | bytes 589856 | tf_op jit(solution)/shard_map/ppermute | solution.py:98
  17.5 3.7 %collective-permute-start.2 = (bf16[160,1024]{1,0:T(8,128)(2,1)S(1)}, bf16[160,1024]{1,0:T(8,128)(2,1)S(1)}, u32[]{:S(2)}, u32[]{:S(2)}) collective-permute-start(bf16[160,1024]{1,0:T(8,128)(2,1)S(1)} %get-tuple-element.30), channel_id=1, source_target_pairs={{0,4},{1,5},{2,6},{3,7},{12,8},{13,9},{14,10},{15,11},{16,20},{17,... | collective-permute-start | bytes 983048 | tf_op jit(solution)/shard_map/ppermute | solution.py:98
  21.2 0.7 %collective-permute-start.6 = (bf16[1152,256]{1,0:T(8,128)(2,1)S(1)}, bf16[1152,256]{1,0:T(8,128)(2,1)S(1)}, u32[]{:S(2)}, u32[]{:S(2)}) collective-permute-start(bf16[1152,256]{1,0:T(8,128)(2,1)S(1)} %collective-permute-done.1.refs_4_), channel_id=1, source_target_pairs={{0,0},{1,1},{2,2},{3,3},{4,8},{5,9},{6,10},{7,11},{8,4},{9,5},{10,... | collective-permute-start | bytes 1769480 | tf_op jit(solution)/shard_map/ppermute | solution.py:98
  21.9 0.0 collective-permute-done.4.refs_3_
  21.9 1.3 %collective-permute-start.7 = (bf16[1152,256]{1,0:T(8,128)(2,1)S(1)}, bf16[1152,256]{1,0:T(8,128)(2,1)S(1)}, u32[]{:S(2)}, u32[]{:S(2)}) collective-permute-start(bf16[1152,256]{1,0:T(8,128)(2,1)S(1)} %collective-permute-done.4.refs_3_), channel_id=1, source_target_pairs={{4,0},{5,1},{6,2},{7,3},{8,12},{9,13},{10,14},{11,15},{20,16},{21,... | collective-permute-start | bytes 1769480 | tf_op jit(solution)/shard_map/ppermute | solution.py:98
  23.2 0.0 collective-permute-done.5.refs_6_
  23.2 5.6 %collective-permute-start.3 = (bf16[160,1024]{1,0:T(8,128)(2,1)S(1)}, bf16[160,1024]{1,0:T(8,128)(2,1)S(1)}, u32[]{:S(2)}, u32[]{:S(2)}) collective-permute-start(bf16[160,1024]{1,0:T(8,128)(2,1)S(1)} %get-tuple-element.31), channel_id=1, source_target_pairs={{0,20},{1,21},{2,22},{3,23},{12,24},{13,25},{14,26},{15,27},{16,4}... | collective-permute-start | bytes 983048 | tf_op jit(solution)/shard_map/ppermute | solution.py:98
  28.8 0.0 collective-permute-done.refs_1_
  28.8 1.6 %shard_map.68 = (f32[2,384,128]{2,1,0:T(8,128)S(1)}, f32[2,384,256]{2,1,0:T(8,128)S(1)}, f32[384,1]{1,0:T(8,128)S(1)}, bf16[3,256,128]{2,1,0:T(8,128)(2,1)S(1)},...) custom-call(bf16[400,1024]{1,0:T(8,128)(2,1)S(1)} %get-tuple-element.27.own.refs_0_, ...), custom_call_target="tpu_custom_call" | custom-call | tf_op jit(solution)/shard_map/pallas_call | solution.py:120
  30.4 0.1 collective-permute-start.13
  30.4 0.0 collective-permute-done.2.hop.refs_2_
  30.4 0.3 shard_map.69.refs_4_
  30.7 3.6 %collective-permute-done.3.refs_3_ = bf16[160,1024]{1,0:T(8,128)(2,1)S(1)} collective-permute-done((bf16[160,1024]{1,0:T(8,128)(2,1)S(1)}, bf16[160,1024]{1,0:T(8,128)(2,1)S(1)}, u32[]{:S(2)}, u32[]{:S(2)}) %collective-permute-start.3) | collective-permute-done | bytes 327712 | tf_op jit(solution)/shard_map/ppermute | solution.py:98
  34.3 0.0 collective-permute-done.6.refs_7_
  34.3 3.4 %collective-permute-done.7.refs_8_ = bf16[1152,256]{1,0:T(8,128)(2,1)S(1)} collective-permute-done((bf16[1152,256]{1,0:T(8,128)(2,1)S(1)}, bf16[1152,256]{1,0:T(8,128)(2,1)S(1)}, u32[]{:S(2)}, u32[]{:S(2)}) %collective-permute-start.7) | collective-permute-done | bytes 589856 | tf_op jit(solution)/shard_map/ppermute | solution.py:98
  37.7 0.7 %shard_map.70 = (f32[16,384]{1,0:T(8,128)S(1)}, f32[16,144]{1,0:T(8,128)S(1)}, f32[16,528]{1,0:T(8,128)S(1)}, bf16[256,128]{1,0:T(8,128)(2,1)S(1)}) custom-call(bf16[400,1024]{1,0:T(8,128)(2,1)S(1)} %get-tuple-element.27.own.refs_0_, bf16[400,1024]{1,0:T(8,128)(2,1)S(1)} %collective-permute-done.refs_1_, ...), custom_call_target="tpu_custom_call" | custom-call | flops 553648128 | bytes 4933632 | tf_op jit(solution)/shard_map/pallas_call | solution.py:120
  38.4 1.6 %collective-permute-start.8 = (f32[16,528]{1,0:T(8,128)S(1)}, f32[16,528]{1,0:T(8,128)S(1)}, u32[]{:S(2)}, u32[]{:S(2)}) collective-permute-start(f32[16,528]{1,0:T(8,128)S(1)} %get-tuple-element.40), channel_id=1, source_target_pairs={{0,16},{1,17},{2,18},{3,19},{4,20},{5,21},{6,22},{7,23},{8,24},{9,... | collective-permute-start | bytes 101384 | tf_op jit(solution)/shard_map/ppermute | solution.py:98
  40.0 1.7 %collective-permute-start.14 = (bf16[256,128]{1,0:T(8,128)(2,1)S(1)}, bf16[256,128]{1,0:T(8,128)(2,1)S(1)}, u32[]{:S(2)}, u32[]{:S(2)}) collective-permute-start(bf16[256,128]{1,0:T(8,128)(2,1)S(1)} %get-tuple-element.48.last_up), channel_id=1, source_target_pairs={{0,4},{1,5},{2,6},{3,7},{4,0},{5,1},{6,2},{7,3},{8,12},{9,13},{10,... | collective-permute-start | bytes 196616 | tf_op jit(solution)/shard_map/ppermute | solution.py:98
  41.7 0.7 %collective-permute-done.8.near = f32[16,528]{1,0:T(8,128)S(1)} collective-permute-done((f32[16,528]{1,0:T(8,128)S(1)}, f32[16,528]{1,0:T(8,128)S(1)}, u32[]{:S(2)}, u32[]{:S(2)}) %collective-permute-start.8) | collective-permute-done | bytes 33824 | tf_op jit(solution)/shard_map/ppermute | solution.py:98
  42.5 2.5 %collective-permute-start.10 = (f32[16,512]{1,0:T(8,128)S(1)}, f32[16,512]{1,0:T(8,128)S(1)}, u32[]{:S(2)}, u32[]{:S(2)}) collective-permute-start(f32[16,512]{1,0:T(8,128)S(1)} %get-tuple-element.42), channel_id=1, source_target_pairs={{0,6},{1,7},{2,4},{3,5},{4,2},{5,3},{6,0},{7,1},{8,14},{9,15},{10,... | collective-permute-start | bytes 98312 | tf_op jit(solution)/shard_map/ppermute | solution.py:98
  44.9 0.5 %collective-permute-start.9 = (f32[16,384]{1,0:T(8,128)S(1)}, f32[16,384]{1,0:T(8,128)S(1)}, u32[]{:S(2)}, u32[]{:S(2)}) collective-permute-start(f32[16,384]{1,0:T(8,128)S(1)} %get-tuple-element.41.low), channel_id=1, source_target_pairs={{0,2},{1,3},{2,0},{3,1},{4,6},{5,7},{6,4},{7,5},{8,10},{9,11},{10,... | collective-permute-start | bytes 73736 | tf_op jit(solution)/shard_map/ppermute | solution.py:98
  45.5 0.5 %collective-permute-start.11 = (f32[16,144]{1,0:T(8,128)S(1)}, f32[16,144]{1,0:T(8,128)S(1)}, u32[]{:S(2)}, u32[]{:S(2)}) collective-permute-start(f32[16,144]{1,0:T(8,128)S(1)} %get-tuple-element.43), channel_id=1, source_target_pairs={{0,4},{1,5},{2,6},{3,7},{4,0},{5,1},{6,2},{7,3},{8,12},{9,13},{10,... | collective-permute-start | bytes 27656 | tf_op jit(solution)/shard_map/ppermute | solution.py:98
  46.0 3.2 %collective-permute-done.11.hop = f32[16,144]{1,0:T(8,128)S(1)} collective-permute-done((f32[16,144]{1,0:T(8,128)S(1)}, f32[16,144]{1,0:T(8,128)S(1)}, u32[]{:S(2)}, u32[]{:S(2)}) %collective-permute-start.11) | collective-permute-done | bytes 9248 | tf_op jit(solution)/shard_map/ppermute | solution.py:98
  49.2 0.0 collective-permute-done.9.far
  49.2 0.0 collective-permute-done.10.hop_far
  49.2 0.2 shard_map.72.near
  49.4 0.0 collective-permute-start.12
  49.4 0.0 collective-permute-done.13.got
  49.4 0.0 collective-permute-done.14.distant
  49.4 1.2 %collective-permute-done.12.far = f32[16,384]{1,0:T(8,128)S(1)} collective-permute-done((f32[16,384]{1,0:T(8,128)S(1)}, f32[16,384]{1,0:T(8,128)S(1)}, u32[]{:S(2)}, u32[]{:S(2)}) %collective-permute-start.12) | collective-permute-done | bytes 24608 | tf_op jit(solution)/shard_map/ppermute | solution.py:98
  50.6 1.3 %shard_map.73 = bf16[384,128]{1,0:T(8,128)(2,1)} custom-call(f32[16,384]{1,0:T(8,128)S(1)} %shard_map.72.near, f32[16,384]{1,0:T(8,128)S(1)} %collective-permute-done.12.far, f32[384,128]{1,0:T(8,128)S(1)} %get-tuple-element.44.keep, f32[384,128]{1,0:T(8,128)S(1)} %collective-permute-done.13.got, f32[384,1]{1,0:T(8,128)S(1)} %get-tuple-element.46.numbers, ...), custom_call_target="tpu_custom_call" | custom-call | bytes 869888 | tf_op jit(solution)/shard_map/pallas_call | solution.py:120
  (1 shorter events, 0.0 us)
Async XLA Ops:
  1.1 7.5 %copy-start = (bf16[2048,512]{1,0:T(8,128)(2,1)S(1)}, bf16[2048,512]{1,0:T(8,128)(2,1)}, u32[]{:S(2)}) copy-start(bf16[2048,512]{1,0:T(8,128)(2,1)} %weights.1) | copy-start | bytes 6291460
  1.1 16.4 %collective-permute-start.1 = (bf16[1152,256]{1,0:T(8,128)(2,1)S(1)}, bf16[1152,256]{1,0:T(8,128)(2,1)S(1)}, u32[]{:S(2)}, u32[]{:S(2)}) collective-permute-start(bf16[1152,256]{1,0:T(8,128)(2,1)S(1)} %shard_map.64._.refs_2_), channel_id=1, source_target_pairs={{0,4},{1,5},{2,6},{3,7},{4,0},{5,1},{6,2},{7,3},{8,12},{9,13},{10,... | collective-permute-start | bytes 1769480 | tf_op jit(solution)/shard_map/ppermute | solution.py:98
  4.2 17.7 %collective-permute-start.4 = (bf16[1152,256]{1,0:T(8,128)(2,1)S(1)}, bf16[1152,256]{1,0:T(8,128)(2,1)S(1)}, u32[]{:S(2)}, u32[]{:S(2)}) collective-permute-start(bf16[1152,256]{1,0:T(8,128)(2,1)S(1)} %shard_map.64._.refs_2_), channel_id=1, source_target_pairs={{0,0},{1,1},{2,2},{3,3},{4,8},{5,9},{6,10},{7,11},{8,4},{9,5},{10,... | collective-permute-start | bytes 1769480 | tf_op jit(solution)/shard_map/ppermute | solution.py:98
  6.3 22.4 %collective-permute-start = (bf16[400,1024]{1,0:T(8,128)(2,1)S(1)}, bf16[400,1024]{1,0:T(8,128)(2,1)S(1)}, u32[]{:S(2)}, u32[]{:S(2)}) collective-permute-start(bf16[400,1024]{1,0:T(8,128)(2,1)S(1)} %get-tuple-element.28.away), channel_id=1, source_target_pairs={{0,16},{1,17},{2,18},{3,19},{4,20},{5,21},{6,22},{7,23},{8,24},{9,... | collective-permute-start | bytes 2457608 | tf_op jit(solution)/shard_map/ppermute | solution.py:98
  9.7 13.5 %collective-permute-start.5 = (f32[384,256]{1,0:T(8,128)S(1)}, f32[384,256]{1,0:T(8,128)S(1)}, u32[]{:S(2)}, u32[]{:S(2)}) collective-permute-start(f32[384,256]{1,0:T(8,128)S(1)} %get-tuple-element.34), channel_id=1, source_target_pairs={{0,2},{1,3},{2,0},{3,1},{4,6},{5,7},{6,4},{7,5},{8,10},{9,11},{10,... | collective-permute-start | bytes 1179656 | tf_op jit(solution)/shard_map/ppermute | solution.py:98
  17.5 12.9 %collective-permute-start.2 = (bf16[160,1024]{1,0:T(8,128)(2,1)S(1)}, bf16[160,1024]{1,0:T(8,128)(2,1)S(1)}, u32[]{:S(2)}, u32[]{:S(2)}) collective-permute-start(bf16[160,1024]{1,0:T(8,128)(2,1)S(1)} %get-tuple-element.30), channel_id=1, source_target_pairs={{0,4},{1,5},{2,6},{3,7},{12,8},{13,9},{14,10},{15,11},{16,20},{17,... | collective-permute-start | bytes 983048 | tf_op jit(solution)/shard_map/ppermute | solution.py:98
  21.2 13.1 %collective-permute-start.6 = (bf16[1152,256]{1,0:T(8,128)(2,1)S(1)}, bf16[1152,256]{1,0:T(8,128)(2,1)S(1)}, u32[]{:S(2)}, u32[]{:S(2)}) collective-permute-start(bf16[1152,256]{1,0:T(8,128)(2,1)S(1)} %collective-permute-done.1.refs_4_), channel_id=1, source_target_pairs={{0,0},{1,1},{2,2},{3,3},{4,8},{5,9},{6,10},{7,11},{8,4},{9,5},{10,... | collective-permute-start | bytes 1769480 | tf_op jit(solution)/shard_map/ppermute | solution.py:98
  21.9 15.8 %collective-permute-start.7 = (bf16[1152,256]{1,0:T(8,128)(2,1)S(1)}, bf16[1152,256]{1,0:T(8,128)(2,1)S(1)}, u32[]{:S(2)}, u32[]{:S(2)}) collective-permute-start(bf16[1152,256]{1,0:T(8,128)(2,1)S(1)} %collective-permute-done.4.refs_3_), channel_id=1, source_target_pairs={{4,0},{5,1},{6,2},{7,3},{8,12},{9,13},{10,14},{11,15},{20,16},{21,... | collective-permute-start | bytes 1769480 | tf_op jit(solution)/shard_map/ppermute | solution.py:98
  23.2 11.1 %collective-permute-start.3 = (bf16[160,1024]{1,0:T(8,128)(2,1)S(1)}, bf16[160,1024]{1,0:T(8,128)(2,1)S(1)}, u32[]{:S(2)}, u32[]{:S(2)}) collective-permute-start(bf16[160,1024]{1,0:T(8,128)(2,1)S(1)} %get-tuple-element.31), channel_id=1, source_target_pairs={{0,20},{1,21},{2,22},{3,23},{12,24},{13,25},{14,26},{15,27},{16,4}... | collective-permute-start | bytes 983048 | tf_op jit(solution)/shard_map/ppermute | solution.py:98
  30.4 19.0 %collective-permute-start.13 = (f32[384,128]{1,0:T(8,128)S(1)}, f32[384,128]{1,0:T(8,128)S(1)}, u32[]{:S(2)}, u32[]{:S(2)}) collective-permute-start(f32[384,128]{1,0:T(8,128)S(1)} %get-tuple-element.45), channel_id=1, source_target_pairs={{0,1},{1,0},{2,3},{3,2},{4,5},{5,4},{6,7},{7,6},{8,9},{9,8},{10,11... | collective-permute-start | bytes 589832 | tf_op jit(solution)/shard_map/ppermute | solution.py:98
  38.4 4.1 %collective-permute-start.8 = (f32[16,528]{1,0:T(8,128)S(1)}, f32[16,528]{1,0:T(8,128)S(1)}, u32[]{:S(2)}, u32[]{:S(2)}) collective-permute-start(f32[16,528]{1,0:T(8,128)S(1)} %get-tuple-element.40), channel_id=1, source_target_pairs={{0,16},{1,17},{2,18},{3,19},{4,20},{5,21},{6,22},{7,23},{8,24},{9,... | collective-permute-start | bytes 101384 | tf_op jit(solution)/shard_map/ppermute | solution.py:98
  40.0 9.4 %collective-permute-start.14 = (bf16[256,128]{1,0:T(8,128)(2,1)S(1)}, bf16[256,128]{1,0:T(8,128)(2,1)S(1)}, u32[]{:S(2)}, u32[]{:S(2)}) collective-permute-start(bf16[256,128]{1,0:T(8,128)(2,1)S(1)} %get-tuple-element.48.last_up), channel_id=1, source_target_pairs={{0,4},{1,5},{2,6},{3,7},{4,0},{5,1},{6,2},{7,3},{8,12},{9,13},{10,... | collective-permute-start | bytes 196616 | tf_op jit(solution)/shard_map/ppermute | solution.py:98
  42.5 6.8 %collective-permute-start.10 = (f32[16,512]{1,0:T(8,128)S(1)}, f32[16,512]{1,0:T(8,128)S(1)}, u32[]{:S(2)}, u32[]{:S(2)}) collective-permute-start(f32[16,512]{1,0:T(8,128)S(1)} %get-tuple-element.42), channel_id=1, source_target_pairs={{0,6},{1,7},{2,4},{3,5},{4,2},{5,3},{6,0},{7,1},{8,14},{9,15},{10,... | collective-permute-start | bytes 98312 | tf_op jit(solution)/shard_map/ppermute | solution.py:98
  44.9 4.3 %collective-permute-start.9 = (f32[16,384]{1,0:T(8,128)S(1)}, f32[16,384]{1,0:T(8,128)S(1)}, u32[]{:S(2)}, u32[]{:S(2)}) collective-permute-start(f32[16,384]{1,0:T(8,128)S(1)} %get-tuple-element.41.low), channel_id=1, source_target_pairs={{0,2},{1,3},{2,0},{3,1},{4,6},{5,7},{6,4},{7,5},{8,10},{9,11},{10,... | collective-permute-start | bytes 73736 | tf_op jit(solution)/shard_map/ppermute | solution.py:98
  45.5 3.7 %collective-permute-start.11 = (f32[16,144]{1,0:T(8,128)S(1)}, f32[16,144]{1,0:T(8,128)S(1)}, u32[]{:S(2)}, u32[]{:S(2)}) collective-permute-start(f32[16,144]{1,0:T(8,128)S(1)} %get-tuple-element.43), channel_id=1, source_target_pairs={{0,4},{1,5},{2,6},{3,7},{4,0},{5,1},{6,2},{7,3},{8,12},{9,13},{10,... | collective-permute-start | bytes 27656 | tf_op jit(solution)/shard_map/ppermute | solution.py:98
  49.4 1.2 %collective-permute-start.12 = (f32[16,384]{1,0:T(8,128)S(1)}, f32[16,384]{1,0:T(8,128)S(1)}, u32[]{:S(2)}, u32[]{:S(2)}) collective-permute-start(f32[16,384]{1,0:T(8,128)S(1)} %shard_map.72.near), channel_id=1, source_target_pairs={{0,1},{1,0},{2,3},{3,2},{4,5},{5,4},{6,7},{7,6},{8,9},{9,8},{10,11... | collective-permute-start | bytes 73736 | tf_op jit(solution)/shard_map/ppermute | solution.py:98

commit v23 on v21

--- a/solution.py
+++ b/solution.py
@@ -177,10 +177,9 @@
         copy.wait()
 
 
-def hop_body(rows, capacity, own, away, own_out, away_out, places):
+def packed_places(ids, capacity):
     a = lax.axis_index("adapter")
-    part = own.shape[1]
-    ids = own[rows:, :rows]
+    rows = ids.shape[1]
     match = (ids.astype(jnp.float32) == (OWNERS - 1 - a).astype(jnp.float32)).astype(jnp.bfloat16)
     earlier = lax.broadcasted_iota(jnp.int32, (rows, rows), 0) < lax.broadcasted_iota(
         jnp.int32, (rows, rows), 1
@@ -188,7 +187,13 @@
     rank = jnp.dot(match, earlier.astype(jnp.bfloat16), preferred_element_type=jnp.float32)
     place = lax.broadcasted_iota(jnp.int32, (capacity, rows), 0).astype(jnp.float32)
     taken = (place == rank[0:1]) & (match[0:1].astype(jnp.float32) > 0)
-    chosen = taken.astype(jnp.bfloat16)
+    return taken.astype(jnp.bfloat16)
+
+
+def hop_body(rows, capacity, own, away, own_out, away_out, places):
+    part = own.shape[1]
+    ids = own[rows:, :rows]
+    chosen = packed_places(ids, capacity)
     places[...] = chosen
     kept = lax.dot_general(ids, chosen, NT, preferred_element_type=jnp.float32)
     for tokens, out in ((own, own_out), (away, away_out)):
@@ -257,7 +262,8 @@
     a = lax.axis_index("adapter")
     token_refs, rest = refs[:groups], refs[groups:]
     blocks, rest = rest[: len(bits)], rest[len(bits) :]
-    kept, got, folded, mask, numbers, ups, keep, give, base = rest
+    kept, got, folded, mask, numbers, ups, keep, give, places, base = rest
+    places[...] = packed_places(token_refs[1][rows:, :rows], places.shape[0])
     base[...] = kept[...] + got[...]
     halves(base, 1, keep, give)
     columns = blocks[0].shape[1]
@@ -288,16 +294,15 @@
     a = lax.axis_index("adapter")
     token_refs, rest = refs[:groups], refs[groups:]
     hops, rest = rest[:groups], rest[groups:]
-    hop_masks, rest = rest[:groups], rest[groups:]
-    folded, mask, inside, outside, mine, away, last_up = rest
-    sums = (mine, away)
+    hop_mask, rest = rest[0], rest[1:]
+    folded, mask, inside, outside, low, low_away, hop_sums, last_up = rest
     columns = inside.shape[1]
 
     def finish(block):
         for n, tokens in enumerate(token_refs):
             wide = jnp.dot(tokens[:rows, :], block[:part, :], preferred_element_type=jnp.float32)
             kept = fold(jnp.where(mask[n] > 0, wide, 0.0))
-            sums[n][:, :rows] = low_rank(folded[n] + kept)
+            (low, low_away)[n][...] = low_rank(folded[n] + kept)
 
     middle = (a == 1) | (a == 2)
 
@@ -305,35 +310,40 @@
     def _():
         finish(inside)
         last_up[...] = stacked(inside[part:, :], last_up.shape[1])
-        for n, (hop, hop_mask) in enumerate(zip(hops, hop_masks)):
+        for n, hop in enumerate(hops):
             wide = jnp.dot(hop[:capacity, :], inside[:part, :], preferred_element_type=jnp.float32)
-            kept = fold(jnp.where(hop_mask[...] > 0, wide, 0.0))
+            if n:
+                _, slot = id_columns(hop, capacity, capacity)
+                wanted = adapters(capacity, columns) == slot
+            else:
+                wanted = hop_mask[...] > 0
+            kept = fold(jnp.where(wanted, wide, 0.0))
             rest_rows = -capacity % LANES
             kept = jnp.concatenate([kept, jnp.zeros((rest_rows, LANES), jnp.float32)], axis=0)
-            sums[n][:, rows:] = low_rank(kept)[:, :capacity]
+            hop_sums[n] = low_rank(kept)[:, :capacity]
 
     @pl.when(jnp.logical_not(middle))
     def _():
         finish(outside)
         last_up[...] = stacked(outside[part:, :], last_up.shape[1])
-        for total in sums:
-            total[:, rows:] = jnp.zeros((ADAPTER_RANK, capacity), jnp.float32)
-
-
-def near_body(mine, near_far, near, far, low, hop):
-    rows = low.shape[1]
-    low[...] = (mine[:, :rows] + far[:, :rows]) + (near[:, :rows] + near_far[:, :rows])
-    hop[...] = (mine[:, rows:] + far[:, rows:]) + (near[:, rows:] + near_far[:, rows:])
-
-
-def merge_body(low, places, hop, out):
-    back = hop[...]
-    spread = jnp.zeros(low.shape, jnp.float32)
-    for _ in range(3):
-        piece = back.astype(jnp.bfloat16)
-        back = back - piece.astype(jnp.float32)
-        spread = spread + jnp.dot(piece, places[...], preferred_element_type=jnp.float32)
-    out[...] = low[...] + spread
+        hop_sums[...] = jnp.zeros(hop_sums.shape, jnp.float32)
+
+
+def merge_body(low, low_away, places, places_away, hop_sums, out, out_away):
+    for n, (own, where, total) in enumerate(
+        ((low, places, out), (low_away, places_away, out_away))
+    ):
+        back = hop_sums[n]
+        spread = jnp.zeros(own.shape, jnp.float32)
+        for _ in range(3):
+            piece = back.astype(jnp.bfloat16)
+            back = back - piece.astype(jnp.float32)
+            spread = spread + jnp.dot(piece, where[...], preferred_element_type=jnp.float32)
+        total[...] = own[...] + spread
+
+
+def near_body(low, near_far, near, far, out):
+    out[...] = (low[...] + far[...]) + (near[...] + near_far[...])
 
 
 def finish_body(near, far, keep, got, numbers, ups, last_up, distant, out):
@@ -390,6 +400,7 @@
         [pltpu.SemaphoreType.DMA((1 + half,))],
     )
     beside = exchange(own, 0, 0, BESIDE)
+    mirror = exchange(own, 0, 0, MIDDLE)
 
     tok_own, tok_away = kernel(
         split_body,
@@ -409,7 +420,6 @@
         ],
     )
     token_parts = [tok_own, exchange(tok_away, 1, 0, SAME)]
-    mirror = exchange(after(own, tok_own), 0, 0, MIDDLE)
     hop_own, hop_away, places = kernel(
         functools.partial(hop_body, rows, capacity),
         [narrow(capacity + ID_ROWS, part)] * groups
@@ -435,7 +445,7 @@
         exchange(hop_away, 1, 0, INWARD),
     ]
 
-    folded, mask, numbers, ups, keep, give = kernel(
+    folded, mask, numbers, ups, keep, give, places_away = kernel(
         functools.partial(early_body, (0, 3, 1), part, rows),
         [
             wide(groups, rows, LANES),
@@ -444,13 +454,14 @@
             narrow(3, columns, keys),
             wide(rows, keys),
             wide(rows, keys),
+            narrow(capacity, rows),
         ],
         (*token_parts, own, mirror, beside, keep, got),
         scratch=[pltpu.VMEM((rows, 2 * keys), jnp.float32)],
         light=True,
     )
     hop_masks, latest = [], folded
-    for hop, urgency in zip(hops, HOP_URGENCY):
+    for hop, urgency in zip(hops[:1], HOP_URGENCY):
         latest = kernel(
             functools.partial(hop_mask_body, capacity),
             wide(capacity, columns),
@@ -459,24 +470,24 @@
             (None, pl.ANY),
         )
         hop_masks.append(latest)
-    mine, away, last_up = kernel(
+    low_shape = wide(ADAPTER_RANK, rows)
+    low, low_away, hop_sums, last_up = kernel(
         functools.partial(last_body, part, rows, capacity),
-        [wide(ADAPTER_RANK, rows + capacity)] * groups + [narrow(columns, keys)],
+        [low_shape, low_shape, wide(groups, ADAPTER_RANK, capacity), narrow(columns, keys)],
         (*token_parts, *hops, *hop_masks, folded, mask, inside, outside),
         2 * groups * (rows + capacity) * part * columns,
     )
 
-    near_far = exchange(away, 1, 2, SAME)
-    near = exchange(away, 1, 0, SAME)
-    far = exchange(mine, 0, 2, SAME)
+    back = exchange(hop_sums, 0, 0, BESIDE)
     distant = exchange(last_up, 0, 0, BESIDE)
-    low, hop_low = kernel(
-        near_body,
-        [wide(ADAPTER_RANK, rows), wide(ADAPTER_RANK, capacity)],
-        (mine, near_far, near, far),
-    )
-    back = exchange(hop_low, 0, 0, BESIDE)
-    low = kernel(merge_body, wide(ADAPTER_RANK, rows), (low, places, back))
+    low, low_away = kernel(
+        merge_body, [low_shape, low_shape], (low, low_away, places, places_away, back)
+    )
+
+    near_far = exchange(low_away, 1, 2, SAME)
+    near = exchange(low_away, 1, 0, SAME)
+    far = exchange(low, 0, 2, SAME)
+    low = kernel(near_body, low_shape, (low, near_far, near, far))
     got = exchange(give, 0, 1, SAME)
     low_far = exchange(low, 0, 1, SAME)
     return kernel(

time: 52.1 us -> 52.4 us (level)
  waiting for transfers between devices: 18.3 us -> 19.8 us
  starting transfers between devices: 24.9 us -> 23.9 us
    ppermute x15, waiting for transfers between devices: 18.3 us -> 19.8 us  [exchange(): return lax.ppermute(x, AXES, pairs)]
    ppermute x15, starting transfers between devices: 24.9 us -> 23.9 us  [exchange(): return lax.ppermute(x, AXES, pairs)]
    pallas_call x11 -> x10, Pallas kernels: 8.46 us -> 8.27 us  [kernel(): pl.pallas_call(body, out_shape=outs, in_specs=specs or [inner] * len(oper...]
  transfers between devices with their start and end apart: 15 -> 15, of which waited for: 7 -> 8; matrix products, arithmetic and copies ran while one was open for 0% -> 0% of each run, Pallas kernels for 12% -> 11%
where the time goes in v23:
time: 52.4 us; the launch traced here: 52.2 us
  starting transfers between devices  23.9 us (46%)
  waiting for transfers between devices  19.8 us (38%)
  Pallas kernels  8.27 us (16%)
    ppermute x15, starting transfers between devices, exchange(): return lax.ppermute(x, AXES, pairs)  23.9 us
    ppermute x15, waiting for transfers between devices, exchange(): return lax.ppermute(x, AXES, pairs)  19.8 us
    pallas_call x10, Pallas kernels, kernel(): pl.pallas_call(body, out_shape=outs, in_specs=specs or [inner] * len(oper...  8.27 us
  transfers between devices with their start and end apart: 15, of which 8 were waited for; matrix products, arithmetic and copies ran while one was open for 0% of the time, Pallas kernels for 11%

profile of v23, /device:TPU:0, one launch (start us, length us, event | category | flops | bytes accessed | tf_op | source)
XLA Modules:
  0.0 52.2 jit_solution(15166848406951790158)
XLA Ops:
  0.0 1.1 %shard_map.64._.refs_2_ = bf16[1152,256]{1,0:T(8,128)(2,1)S(1)} custom-call(bf16[2048,256]{1,0:T(8,128)(2,1)} %down.1, bf16[256,128]{1,0:T(8,128)(2,1)} %up.1), custom_call_target="tpu_custom_call" | custom-call | bytes 1703936 | tf_op jit(solution)/shard_map/pallas_call | solution.py:120
  1.1 0.0 copy-start
  1.1 3.1 %collective-permute-start.1 = (bf16[1152,256]{1,0:T(8,128)(2,1)S(1)}, bf16[1152,256]{1,0:T(8,128)(2,1)S(1)}, u32[]{:S(2)}, u32[]{:S(2)}) collective-permute-start(bf16[1152,256]{1,0:T(8,128)(2,1)S(1)} %shard_map.64._.refs_2_), channel_id=1, source_target_pairs={{0,4},{1,5},{2,6},{3,7},{4,0},{5,1},{6,2},{7,3},{8,12},{9,13},{10,... | collective-permute-start | bytes 1769480 | tf_op jit(solution)/shard_map/ppermute | solution.py:98
  4.2 0.7 %collective-permute-start.4 = (bf16[1152,256]{1,0:T(8,128)(2,1)S(1)}, bf16[1152,256]{1,0:T(8,128)(2,1)S(1)}, u32[]{:S(2)}, u32[]{:S(2)}) collective-permute-start(bf16[1152,256]{1,0:T(8,128)(2,1)S(1)} %shard_map.64._.refs_2_), channel_id=1, source_target_pairs={{0,0},{1,1},{2,2},{3,3},{4,8},{5,9},{6,10},{7,11},{8,4},{9,5},{10,... | collective-permute-start | bytes 1769480 | tf_op jit(solution)/shard_map/ppermute | solution.py:98
  4.9 1.4 %shard_map.65 = (bf16[400,1024]{1,0:T(8,128)(2,1)S(1)}, bf16[400,1024]{1,0:T(8,128)(2,1)S(1)}) custom-call(bf16[384,2048]{1,0:T(8,128)(2,1)} %tokens.1, s32[1,384]{1,0:T(1,128)} %bitcast.1, s32[384]{0:T(512)} %slot_in.1, bf16[1152,256]{1,0:T(8,128)(2,1)S(1)} %shard_map.64._.refs_2_), custom_call_target="tpu_custom_call" | custom-call | bytes 3804160 | tf_op jit(solution)/shard_map/pallas_call | solution.py:120
  6.3 1.6 %collective-permute-start = (bf16[400,1024]{1,0:T(8,128)(2,1)S(1)}, bf16[400,1024]{1,0:T(8,128)(2,1)S(1)}, u32[]{:S(2)}, u32[]{:S(2)}) collective-permute-start(bf16[400,1024]{1,0:T(8,128)(2,1)S(1)} %get-tuple-element.28.away), channel_id=1, source_target_pairs={{0,16},{1,17},{2,18},{3,19},{4,20},{5,21},{6,22},{7,23},{8,24},{9,... | collective-permute-start | bytes 2457608 | tf_op jit(solution)/shard_map/ppermute | solution.py:98
  7.9 0.7 %shard_map.66 = (bf16[160,1024]{1,0:T(8,128)(2,1)S(1)}, bf16[160,1024]{1,0:T(8,128)(2,1)S(1)}, bf16[144,384]{1,0:T(8,128)(2,1)S(1)}) custom-call(bf16[400,1024]{1,0:T(8,128)(2,1)S(1)} %get-tuple-element.27.own.refs_0_, bf16[400,1024]{1,0:T(8,128)(2,1)S(1)} %get-tuple-element.28.away), custom_call_target="tpu_custom_call" | custom-call | flops 226492416 | bytes 2404352 | tf_op jit(solution)/shard_map/pallas_call | solution.py:120
  8.6 0.0 copy-done
  8.6 1.1 %shard_map.67 = (f32[384,256]{1,0:T(8,128)S(1)}, f32[384,256]{1,0:T(8,128)S(1)}) custom-call(bf16[400,1024]{1,0:T(8,128)(2,1)S(1)} %get-tuple-element.27.own.refs_0_, bf16[400,1024]{1,0:T(8,128)(2,1)S(1)} %get-tuple-element.28.away, bf16[2048,512]{1,0:T(8,128)(2,1)S(1)} %copy-done, bf16[144,384]{1,0:T(8,128)(2,1)S(1)} %get-tuple-element.32._.places), custom_call_target="tpu_custom_call" | custom-call | flops 805306368 | bytes 4632576 | tf_op jit(solution)/shard_map/pallas_call | solution.py:120
  9.7 1.5 %collective-permute-start.5 = (f32[384,256]{1,0:T(8,128)S(1)}, f32[384,256]{1,0:T(8,128)S(1)}, u32[]{:S(2)}, u32[]{:S(2)}) collective-permute-start(f32[384,256]{1,0:T(8,128)S(1)} %get-tuple-element.34), channel_id=1, source_target_pairs={{0,2},{1,3},{2,0},{3,1},{4,6},{5,7},{6,4},{7,5},{8,10},{9,11},{10,... | collective-permute-start | bytes 1179656 | tf_op jit(solution)/shard_map/ppermute | solution.py:98
  11.2 6.3 %collective-permute-done.1.refs_4_ = bf16[1152,256]{1,0:T(8,128)(2,1)S(1)} collective-permute-done((bf16[1152,256]{1,0:T(8,128)(2,1)S(1)}, bf16[1152,256]{1,0:T(8,128)(2,1)S(1)}, u32[]{:S(2)}, u32[]{:S(2)}) %collective-permute-start.1) | collective-permute-done | bytes 589856 | tf_op jit(solution)/shard_map/ppermute | solution.py:98
  17.5 3.7 %collective-permute-start.2 = (bf16[160,1024]{1,0:T(8,128)(2,1)S(1)}, bf16[160,1024]{1,0:T(8,128)(2,1)S(1)}, u32[]{:S(2)}, u32[]{:S(2)}) collective-permute-start(bf16[160,1024]{1,0:T(8,128)(2,1)S(1)} %get-tuple-element.30), channel_id=1, source_target_pairs={{0,4},{1,5},{2,6},{3,7},{12,8},{13,9},{14,10},{15,11},{16,20},{17,... | collective-permute-start | bytes 983048 | tf_op jit(solution)/shard_map/ppermute | solution.py:98
  21.2 0.7 %collective-permute-start.6 = (bf16[1152,256]{1,0:T(8,128)(2,1)S(1)}, bf16[1152,256]{1,0:T(8,128)(2,1)S(1)}, u32[]{:S(2)}, u32[]{:S(2)}) collective-permute-start(bf16[1152,256]{1,0:T(8,128)(2,1)S(1)} %collective-permute-done.1.refs_4_), channel_id=1, source_target_pairs={{0,0},{1,1},{2,2},{3,3},{4,8},{5,9},{6,10},{7,11},{8,4},{9,5},{10,... | collective-permute-start | bytes 1769480 | tf_op jit(solution)/shard_map/ppermute | solution.py:98
  21.9 0.0 collective-permute-done.4.refs_3_
  21.9 1.3 %collective-permute-start.7 = (bf16[1152,256]{1,0:T(8,128)(2,1)S(1)}, bf16[1152,256]{1,0:T(8,128)(2,1)S(1)}, u32[]{:S(2)}, u32[]{:S(2)}) collective-permute-start(bf16[1152,256]{1,0:T(8,128)(2,1)S(1)} %collective-permute-done.4.refs_3_), channel_id=1, source_target_pairs={{4,0},{5,1},{6,2},{7,3},{8,12},{9,13},{10,14},{11,15},{20,16},{21,... | collective-permute-start | bytes 1769480 | tf_op jit(solution)/shard_map/ppermute | solution.py:98
  23.2 0.0 collective-permute-done.5.refs_6_
  23.2 5.6 %collective-permute-start.3 = (bf16[160,1024]{1,0:T(8,128)(2,1)S(1)}, bf16[160,1024]{1,0:T(8,128)(2,1)S(1)}, u32[]{:S(2)}, u32[]{:S(2)}) collective-permute-start(bf16[160,1024]{1,0:T(8,128)(2,1)S(1)} %get-tuple-element.31), channel_id=1, source_target_pairs={{0,20},{1,21},{2,22},{3,23},{12,24},{13,25},{14,26},{15,27},{16,4}... | collective-permute-start | bytes 983048 | tf_op jit(solution)/shard_map/ppermute | solution.py:98
  28.8 0.0 collective-permute-done.refs_1_
  28.8 1.6 %shard_map.68 = (f32[2,384,128]{2,1,0:T(8,128)S(1)}, f32[2,384,256]{2,1,0:T(8,128)S(1)}, f32[384,1]{1,0:T(8,128)S(1)}, bf16[3,256,128]{2,1,0:T(8,128)(2,1)S(1)},...) custom-call(bf16[400,1024]{1,0:T(8,128)(2,1)S(1)} %get-tuple-element.27.own.refs_0_, ...), custom_call_target="tpu_custom_call" | custom-call | tf_op jit(solution)/shard_map/pallas_call | solution.py:120
  30.4 0.1 collective-permute-start.13
  30.4 0.0 collective-permute-done.2.hop.refs_2_
  30.5 0.3 shard_map.69.refs_4_
  30.7 3.6 %collective-permute-done.3.refs_3_ = bf16[160,1024]{1,0:T(8,128)(2,1)S(1)} collective-permute-done((bf16[160,1024]{1,0:T(8,128)(2,1)S(1)}, bf16[160,1024]{1,0:T(8,128)(2,1)S(1)}, u32[]{:S(2)}, u32[]{:S(2)}) %collective-permute-start.3) | collective-permute-done | bytes 327712 | tf_op jit(solution)/shard_map/ppermute | solution.py:98
  34.3 0.0 collective-permute-done.6.refs_7_
  34.3 3.4 %collective-permute-done.7.refs_8_ = bf16[1152,256]{1,0:T(8,128)(2,1)S(1)} collective-permute-done((bf16[1152,256]{1,0:T(8,128)(2,1)S(1)}, bf16[1152,256]{1,0:T(8,128)(2,1)S(1)}, u32[]{:S(2)}, u32[]{:S(2)}) %collective-permute-start.7) | collective-permute-done | bytes 589856 | tf_op jit(solution)/shard_map/ppermute | solution.py:98
  37.7 0.7 %shard_map.70 = (f32[16,384]{1,0:T(8,128)S(1)}, f32[16,384]{1,0:T(8,128)S(1)}, f32[2,16,144]{2,1,0:T(8,128)S(1)}, bf16[256,128]{1,0:T(8,128)(2,1)S(1)}) custom-call(bf16[400,1024]{1,0:T(8,128)(2,1)S(1)} %get-tuple-element.27.own.refs_0_, bf16[400,1024]{1,0:T(8,128)(2,1)S(1)} %collective-permute-done.refs_1_, ...), custom_call_target="tpu_custom_call" | custom-call | flops 553648128 | bytes 4933632 | tf_op jit(solution)/shard_map/pallas_call | solution.py:120
  38.4 0.9 %collective-permute-start.8 = (f32[2,16,144]{2,1,0:T(8,128)S(1)}, f32[2,16,144]{2,1,0:T(8,128)S(1)}, u32[]{:S(2)}, u32[]{:S(2)}) collective-permute-start(f32[2,16,144]{2,1,0:T(8,128)S(1)} %get-tuple-element.41), channel_id=1, source_target_pairs={{0,4},{1,5},{2,6},{3,7},{4,0},{5,1},{6,2},{7,3},{8,12},{9,13},{10,... | collective-permute-start | bytes 55304 | tf_op jit(solution)/shard_map/ppermute | solution.py:98
  39.3 1.2 %collective-permute-start.14 = (bf16[256,128]{1,0:T(8,128)(2,1)S(1)}, bf16[256,128]{1,0:T(8,128)(2,1)S(1)}, u32[]{:S(2)}, u32[]{:S(2)}) collective-permute-start(bf16[256,128]{1,0:T(8,128)(2,1)S(1)} %get-tuple-element.48.last_up), channel_id=1, source_target_pairs={{0,4},{1,5},{2,6},{3,7},{4,0},{5,1},{6,2},{7,3},{8,12},{9,13},{10,... | collective-permute-start | bytes 196616 | tf_op jit(solution)/shard_map/ppermute | solution.py:98
  40.5 2.1 %collective-permute-done.8.hop_sums = f32[2,16,144]{2,1,0:T(8,128)S(1)} collective-permute-done((f32[2,16,144]{2,1,0:T(8,128)S(1)}, f32[2,16,144]{2,1,0:T(8,128)S(1)}, u32[]{:S(2)}, u32[]{:S(2)}) %collective-permute-start.8) | collective-permute-done | bytes 18464 | tf_op jit(solution)/shard_map/ppermute | solution.py:98
  42.6 0.2 shard_map.71
  42.8 2.3 %collective-permute-start.9 = (f32[16,384]{1,0:T(8,128)S(1)}, f32[16,384]{1,0:T(8,128)S(1)}, u32[]{:S(2)}, u32[]{:S(2)}) collective-permute-start(f32[16,384]{1,0:T(8,128)S(1)} %get-tuple-element.43), channel_id=1, source_target_pairs={{0,18},{1,19},{2,16},{3,17},{4,22},{5,23},{6,20},{7,21},{8,26},{9,... | collective-permute-start | bytes 73736 | tf_op jit(solution)/shard_map/ppermute | solution.py:98
  45.1 0.8 %collective-permute-start.10 = (f32[16,384]{1,0:T(8,128)S(1)}, f32[16,384]{1,0:T(8,128)S(1)}, u32[]{:S(2)}, u32[]{:S(2)}) collective-permute-start(f32[16,384]{1,0:T(8,128)S(1)} %get-tuple-element.43), channel_id=1, source_target_pairs={{0,16},{1,17},{2,18},{3,19},{4,20},{5,21},{6,22},{7,23},{8,24},{9,... | collective-permute-start | bytes 73736 | tf_op jit(solution)/shard_map/ppermute | solution.py:98
  45.8 0.5 %collective-permute-start.11 = (f32[16,384]{1,0:T(8,128)S(1)}, f32[16,384]{1,0:T(8,128)S(1)}, u32[]{:S(2)}, u32[]{:S(2)}) collective-permute-start(f32[16,384]{1,0:T(8,128)S(1)} %get-tuple-element.42.low), channel_id=1, source_target_pairs={{0,2},{1,3},{2,0},{3,1},{4,6},{5,7},{6,4},{7,5},{8,10},{9,11},{10,... | collective-permute-start | bytes 73736 | tf_op jit(solution)/shard_map/ppermute | solution.py:98
  46.4 1.2 %collective-permute-done.9.near_far = f32[16,384]{1,0:T(8,128)S(1)} collective-permute-done((f32[16,384]{1,0:T(8,128)S(1)}, f32[16,384]{1,0:T(8,128)S(1)}, u32[]{:S(2)}, u32[]{:S(2)}) %collective-permute-start.9) | collective-permute-done | bytes 24608 | tf_op jit(solution)/shard_map/ppermute | solution.py:98
  47.6 1.3 %collective-permute-done.10.near = f32[16,384]{1,0:T(8,128)S(1)} collective-permute-done((f32[16,384]{1,0:T(8,128)S(1)}, f32[16,384]{1,0:T(8,128)S(1)}, u32[]{:S(2)}, u32[]{:S(2)}) %collective-permute-start.10) | collective-permute-done | bytes 24608 | tf_op jit(solution)/shard_map/ppermute | solution.py:98
  48.9 0.8 %collective-permute-done.11.far = f32[16,384]{1,0:T(8,128)S(1)} collective-permute-done((f32[16,384]{1,0:T(8,128)S(1)}, f32[16,384]{1,0:T(8,128)S(1)}, u32[]{:S(2)}, u32[]{:S(2)}) %collective-permute-start.11) | collective-permute-done | bytes 24608 | tf_op jit(solution)/shard_map/ppermute | solution.py:98
  49.7 0.1 collective-permute-start.12
  49.7 0.0 collective-permute-done.13.got
  49.7 0.0 collective-permute-done.14.distant
  49.8 1.2 %collective-permute-done.12.far = f32[16,384]{1,0:T(8,128)S(1)} collective-permute-done((f32[16,384]{1,0:T(8,128)S(1)}, f32[16,384]{1,0:T(8,128)S(1)}, u32[]{:S(2)}, u32[]{:S(2)}) %collective-permute-start.12) | collective-permute-done | bytes 24608 | tf_op jit(solution)/shard_map/ppermute | solution.py:98
  50.9 1.3 %shard_map.73 = bf16[384,128]{1,0:T(8,128)(2,1)} custom-call(f32[16,384]{1,0:T(8,128)S(1)} %shard_map.72.near, f32[16,384]{1,0:T(8,128)S(1)} %collective-permute-done.12.far, f32[384,128]{1,0:T(8,128)S(1)} %get-tuple-element.44.keep, f32[384,128]{1,0:T(8,128)S(1)} %collective-permute-done.13.got, f32[384,1]{1,0:T(8,128)S(1)} %get-tuple-element.46.numbers, ...), custom_call_target="tpu_custom_call" | custom-call | bytes 869888 | tf_op jit(solution)/shard_map/pallas_call | solution.py:120
  (1 shorter events, 0.0 us)
Async XLA Ops:
  1.1 7.5 %copy-start = (bf16[2048,512]{1,0:T(8,128)(2,1)S(1)}, bf16[2048,512]{1,0:T(8,128)(2,1)}, u32[]{:S(2)}) copy-start(bf16[2048,512]{1,0:T(8,128)(2,1)} %weights.1) | copy-start | bytes 6291460
  1.1 16.4 %collective-permute-start.1 = (bf16[1152,256]{1,0:T(8,128)(2,1)S(1)}, bf16[1152,256]{1,0:T(8,128)(2,1)S(1)}, u32[]{:S(2)}, u32[]{:S(2)}) collective-permute-start(bf16[1152,256]{1,0:T(8,128)(2,1)S(1)} %shard_map.64._.refs_2_), channel_id=1, source_target_pairs={{0,4},{1,5},{2,6},{3,7},{4,0},{5,1},{6,2},{7,3},{8,12},{9,13},{10,... | collective-permute-start | bytes 1769480 | tf_op jit(solution)/shard_map/ppermute | solution.py:98
  4.2 17.7 %collective-permute-start.4 = (bf16[1152,256]{1,0:T(8,128)(2,1)S(1)}, bf16[1152,256]{1,0:T(8,128)(2,1)S(1)}, u32[]{:S(2)}, u32[]{:S(2)}) collective-permute-start(bf16[1152,256]{1,0:T(8,128)(2,1)S(1)} %shard_map.64._.refs_2_), channel_id=1, source_target_pairs={{0,0},{1,1},{2,2},{3,3},{4,8},{5,9},{6,10},{7,11},{8,4},{9,5},{10,... | collective-permute-start | bytes 1769480 | tf_op jit(solution)/shard_map/ppermute | solution.py:98
  6.3 22.4 %collective-permute-start = (bf16[400,1024]{1,0:T(8,128)(2,1)S(1)}, bf16[400,1024]{1,0:T(8,128)(2,1)S(1)}, u32[]{:S(2)}, u32[]{:S(2)}) collective-permute-start(bf16[400,1024]{1,0:T(8,128)(2,1)S(1)} %get-tuple-element.28.away), channel_id=1, source_target_pairs={{0,16},{1,17},{2,18},{3,19},{4,20},{5,21},{6,22},{7,23},{8,24},{9,... | collective-permute-start | bytes 2457608 | tf_op jit(solution)/shard_map/ppermute | solution.py:98
  9.7 13.5 %collective-permute-start.5 = (f32[384,256]{1,0:T(8,128)S(1)}, f32[384,256]{1,0:T(8,128)S(1)}, u32[]{:S(2)}, u32[]{:S(2)}) collective-permute-start(f32[384,256]{1,0:T(8,128)S(1)} %get-tuple-element.34), channel_id=1, source_target_pairs={{0,2},{1,3},{2,0},{3,1},{4,6},{5,7},{6,4},{7,5},{8,10},{9,11},{10,... | collective-permute-start | bytes 1179656 | tf_op jit(solution)/shard_map/ppermute | solution.py:98
  17.5 12.9 %collective-permute-start.2 = (bf16[160,1024]{1,0:T(8,128)(2,1)S(1)}, bf16[160,1024]{1,0:T(8,128)(2,1)S(1)}, u32[]{:S(2)}, u32[]{:S(2)}) collective-permute-start(bf16[160,1024]{1,0:T(8,128)(2,1)S(1)} %get-tuple-element.30), channel_id=1, source_target_pairs={{0,4},{1,5},{2,6},{3,7},{12,8},{13,9},{14,10},{15,11},{16,20},{17,... | collective-permute-start | bytes 983048 | tf_op jit(solution)/shard_map/ppermute | solution.py:98
  21.2 13.1 %collective-permute-start.6 = (bf16[1152,256]{1,0:T(8,128)(2,1)S(1)}, bf16[1152,256]{1,0:T(8,128)(2,1)S(1)}, u32[]{:S(2)}, u32[]{:S(2)}) collective-permute-start(bf16[1152,256]{1,0:T(8,128)(2,1)S(1)} %collective-permute-done.1.refs_4_), channel_id=1, source_target_pairs={{0,0},{1,1},{2,2},{3,3},{4,8},{5,9},{6,10},{7,11},{8,4},{9,5},{10,... | collective-permute-start | bytes 1769480 | tf_op jit(solution)/shard_map/ppermute | solution.py:98
  21.9 15.8 %collective-permute-start.7 = (bf16[1152,256]{1,0:T(8,128)(2,1)S(1)}, bf16[1152,256]{1,0:T(8,128)(2,1)S(1)}, u32[]{:S(2)}, u32[]{:S(2)}) collective-permute-start(bf16[1152,256]{1,0:T(8,128)(2,1)S(1)} %collective-permute-done.4.refs_3_), channel_id=1, source_target_pairs={{4,0},{5,1},{6,2},{7,3},{8,12},{9,13},{10,14},{11,15},{20,16},{21,... | collective-permute-start | bytes 1769480 | tf_op jit(solution)/shard_map/ppermute | solution.py:98
  23.2 11.1 %collective-permute-start.3 = (bf16[160,1024]{1,0:T(8,128)(2,1)S(1)}, bf16[160,1024]{1,0:T(8,128)(2,1)S(1)}, u32[]{:S(2)}, u32[]{:S(2)}) collective-permute-start(bf16[160,1024]{1,0:T(8,128)(2,1)S(1)} %get-tuple-element.31), channel_id=1, source_target_pairs={{0,20},{1,21},{2,22},{3,23},{12,24},{13,25},{14,26},{15,27},{16,4}... | collective-permute-start | bytes 983048 | tf_op jit(solution)/shard_map/ppermute | solution.py:98
  30.4 19.4 %collective-permute-start.13 = (f32[384,128]{1,0:T(8,128)S(1)}, f32[384,128]{1,0:T(8,128)S(1)}, u32[]{:S(2)}, u32[]{:S(2)}) collective-permute-start(f32[384,128]{1,0:T(8,128)S(1)} %get-tuple-element.45), channel_id=1, source_target_pairs={{0,1},{1,0},{2,3},{3,2},{4,5},{5,4},{6,7},{7,6},{8,9},{9,8},{10,11... | collective-permute-start | bytes 589832 | tf_op jit(solution)/shard_map/ppermute | solution.py:98
  38.4 4.2 %collective-permute-start.8 = (f32[2,16,144]{2,1,0:T(8,128)S(1)}, f32[2,16,144]{2,1,0:T(8,128)S(1)}, u32[]{:S(2)}, u32[]{:S(2)}) collective-permute-start(f32[2,16,144]{2,1,0:T(8,128)S(1)} %get-tuple-element.41), channel_id=1, source_target_pairs={{0,4},{1,5},{2,6},{3,7},{4,0},{5,1},{6,2},{7,3},{8,12},{9,13},{10,... | collective-permute-start | bytes 55304 | tf_op jit(solution)/shard_map/ppermute | solution.py:98
  39.3 10.5 %collective-permute-start.14 = (bf16[256,128]{1,0:T(8,128)(2,1)S(1)}, bf16[256,128]{1,0:T(8,128)(2,1)S(1)}, u32[]{:S(2)}, u32[]{:S(2)}) collective-permute-start(bf16[256,128]{1,0:T(8,128)(2,1)S(1)} %get-tuple-element.48.last_up), channel_id=1, source_target_pairs={{0,4},{1,5},{2,6},{3,7},{4,0},{5,1},{6,2},{7,3},{8,12},{9,13},{10,... | collective-permute-start | bytes 196616 | tf_op jit(solution)/shard_map/ppermute | solution.py:98
  42.8 4.8 %collective-permute-start.9 = (f32[16,384]{1,0:T(8,128)S(1)}, f32[16,384]{1,0:T(8,128)S(1)}, u32[]{:S(2)}, u32[]{:S(2)}) collective-permute-start(f32[16,384]{1,0:T(8,128)S(1)} %get-tuple-element.43), channel_id=1, source_target_pairs={{0,18},{1,19},{2,16},{3,17},{4,22},{5,23},{6,20},{7,21},{8,26},{9,... | collective-permute-start | bytes 73736 | tf_op jit(solution)/shard_map/ppermute | solution.py:98
  45.1 3.8 %collective-permute-start.10 = (f32[16,384]{1,0:T(8,128)S(1)}, f32[16,384]{1,0:T(8,128)S(1)}, u32[]{:S(2)}, u32[]{:S(2)}) collective-permute-start(f32[16,384]{1,0:T(8,128)S(1)} %get-tuple-element.43), channel_id=1, source_target_pairs={{0,16},{1,17},{2,18},{3,19},{4,20},{5,21},{6,22},{7,23},{8,24},{9,... | collective-permute-start | bytes 73736 | tf_op jit(solution)/shard_map/ppermute | solution.py:98
  45.8 3.8 %collective-permute-start.11 = (f32[16,384]{1,0:T(8,128)S(1)}, f32[16,384]{1,0:T(8,128)S(1)}, u32[]{:S(2)}, u32[]{:S(2)}) collective-permute-start(f32[16,384]{1,0:T(8,128)S(1)} %get-tuple-element.42.low), channel_id=1, source_target_pairs={{0,2},{1,3},{2,0},{3,1},{4,6},{5,7},{6,4},{7,5},{8,10},{9,11},{10,... | collective-permute-start | bytes 73736 | tf_op jit(solution)/shard_map/ppermute | solution.py:98
  49.7 1.3 %collective-permute-start.12 = (f32[16,384]{1,0:T(8,128)S(1)}, f32[16,384]{1,0:T(8,128)S(1)}, u32[]{:S(2)}, u32[]{:S(2)}) collective-permute-start(f32[16,384]{1,0:T(8,128)S(1)} %shard_map.72.near), channel_id=1, source_target_pairs={{0,1},{1,0},{2,3},{3,2},{4,5},{5,4},{6,7},{7,6},{8,9},{9,8},{10,11... | collective-permute-start | bytes 73736 | tf_op jit(solution)/shard_map/ppermute | solution.py:98

commit v24 on v22

--- a/solution.py
+++ b/solution.py
@@ -257,7 +257,7 @@
     a = lax.axis_index("adapter")
     token_refs, rest = refs[:groups], refs[groups:]
     blocks, rest = rest[: len(bits)], rest[len(bits) :]
-    kept, got, folded, mask, numbers, ups, keep, give, base = rest
+    kept, got, folded, mask, named_by, ups, keep, give, base = rest
     base[...] = kept[...] + got[...]
     halves(base, 1, keep, give)
     columns = blocks[0].shape[1]
@@ -267,7 +267,9 @@
     for n, tokens in enumerate(token_refs):
         owner, slot = id_columns(tokens, rows, rows)
         if n == 0:
-            numbers[...] = owner * (columns // ADAPTER_RANK) + slot
+            for bit in range(OWNERS):
+                named = (owner == (a ^ bit).astype(jnp.float32)) & (adapter == slot)
+                named_by[bit] = named.astype(jnp.float32).astype(jnp.bfloat16)
         right = adapter == slot
         picked = jnp.zeros((rows, columns), jnp.float32)
         for bit, block in zip(bits, blocks):
@@ -351,7 +353,7 @@
     out[...] = low[...] + far[...] + spread
 
 
-def finish_body(near, far, keep, got, numbers, ups, last_up, distant, out):
+def finish_body(near, far, keep, got, named_by, ups, last_up, distant, out):
     a = lax.axis_index("adapter")
     rows = out.shape[0]
     columns = last_up.shape[0]
@@ -360,14 +362,13 @@
     repeat = (lax.rem(column, ADAPTER_RANK) == row).astype(jnp.bfloat16)
     shrunk = (near[...] + far[...]).astype(jnp.bfloat16)
     spread = lax.dot_general(shrunk, repeat, TN, preferred_element_type=jnp.float32)
-    adapter = adapters(rows, columns)
+    spread = spread.astype(jnp.bfloat16)
     middle = (a == 1) | (a == 2)
     mirrored = jnp.where(middle, ups[1].astype(jnp.float32), distant[...].astype(jnp.float32))
     blocks = ((0, ups[0]), (1, ups[2]), (2, last_up[...]), (3, mirrored.astype(jnp.bfloat16)))
     updates = jnp.zeros(out.shape, jnp.float32)
     for bit, up in blocks:
-        wanted = numbers[...] - ((a ^ bit) * (columns // ADAPTER_RANK)).astype(jnp.float32)
-        chosen = jnp.where(adapter == wanted, spread, 0.0).astype(jnp.bfloat16)
+        chosen = spread * named_by[bit]
         updates = updates + jnp.dot(chosen, up, preferred_element_type=jnp.float32)
     updates = updates.astype(jnp.bfloat16).astype(jnp.float32)
     base = keep[...] + got[...]
@@ -450,12 +451,12 @@
         exchange(hop_away, 1, 0, INWARD),
     ]
 
-    folded, mask, numbers, ups, keep, give = kernel(
+    folded, mask, named_by, ups, keep, give = kernel(
         functools.partial(early_body, (0, 3, 1), part, rows),
         [
             wide(groups, rows, LANES),
             wide(groups, rows, columns),
-            wide(rows, 1),
+            narrow(owners, rows, columns),
             narrow(3, columns, keys),
             wide(rows, keys),
             wide(rows, keys),
@@ -508,7 +509,7 @@
     got = exchange(give, 0, 1, SAME)
     low_far = exchange(low, 0, 1, SAME)
     return kernel(
-        finish_body, narrow(rows, keys), (low, low_far, keep, got, numbers, ups, last_up, distant)
+        finish_body, narrow(rows, keys), (low, low_far, keep, got, named_by, ups, last_up, distant)
     )
 
 

time: 52.1 us -> 52.1 us (level)
  no operation moved by 1% of the time
where the time goes in v24:
time: 52.1 us; the launch traced here: 51.8 us
  starting transfers between devices  25.1 us (48%)
  waiting for transfers between devices  18.3 us (35%)
  Pallas kernels  8.22 us (16%)
    ppermute x15, starting transfers between devices, exchange(): return lax.ppermute(x, AXES, pairs)  25.1 us
    ppermute x15, waiting for transfers between devices, exchange(): return lax.ppermute(x, AXES, pairs)  18.3 us
    pallas_call x10, Pallas kernels, kernel(): pl.pallas_call(body, out_shape=outs, in_specs=specs or [inner] * len(oper...  8.22 us
  transfers between devices with their start and end apart: 15, of which 6 were waited for; matrix products, arithmetic and copies ran while one was open for 0% of the time, Pallas kernels for 11%

profile of v24, /device:TPU:0, one launch (start us, length us, event | category | flops | bytes accessed | tf_op | source)
XLA Modules:
  0.0 51.8 jit_solution(2402717438089368513)
XLA Ops:
  0.0 1.1 %shard_map.64._.refs_2_ = bf16[1152,256]{1,0:T(8,128)(2,1)S(1)} custom-call(bf16[2048,256]{1,0:T(8,128)(2,1)} %down.1, bf16[256,128]{1,0:T(8,128)(2,1)} %up.1), custom_call_target="tpu_custom_call" | custom-call | bytes 1703936 | tf_op jit(solution)/shard_map/pallas_call | solution.py:120
  1.1 0.0 copy-start
  1.1 3.1 %collective-permute-start.1 = (bf16[1152,256]{1,0:T(8,128)(2,1)S(1)}, bf16[1152,256]{1,0:T(8,128)(2,1)S(1)}, u32[]{:S(2)}, u32[]{:S(2)}) collective-permute-start(bf16[1152,256]{1,0:T(8,128)(2,1)S(1)} %shard_map.64._.refs_2_), channel_id=1, source_target_pairs={{0,4},{1,5},{2,6},{3,7},{4,0},{5,1},{6,2},{7,3},{8,12},{9,13},{10,... | collective-permute-start | bytes 1769480 | tf_op jit(solution)/shard_map/ppermute | solution.py:98
  4.2 0.7 %collective-permute-start.4 = (bf16[1152,256]{1,0:T(8,128)(2,1)S(1)}, bf16[1152,256]{1,0:T(8,128)(2,1)S(1)}, u32[]{:S(2)}, u32[]{:S(2)}) collective-permute-start(bf16[1152,256]{1,0:T(8,128)(2,1)S(1)} %shard_map.64._.refs_2_), channel_id=1, source_target_pairs={{0,0},{1,1},{2,2},{3,3},{4,8},{5,9},{6,10},{7,11},{8,4},{9,5},{10,... | collective-permute-start | bytes 1769480 | tf_op jit(solution)/shard_map/ppermute | solution.py:98
  4.9 1.4 %shard_map.65 = (bf16[400,1024]{1,0:T(8,128)(2,1)S(1)}, bf16[400,1024]{1,0:T(8,128)(2,1)S(1)}) custom-call(bf16[384,2048]{1,0:T(8,128)(2,1)} %tokens.1, s32[1,384]{1,0:T(1,128)} %bitcast.1, s32[384]{0:T(512)} %slot_in.1, bf16[1152,256]{1,0:T(8,128)(2,1)S(1)} %shard_map.64._.refs_2_), custom_call_target="tpu_custom_call" | custom-call | bytes 3804160 | tf_op jit(solution)/shard_map/pallas_call | solution.py:120
  6.3 1.6 %collective-permute-start = (bf16[400,1024]{1,0:T(8,128)(2,1)S(1)}, bf16[400,1024]{1,0:T(8,128)(2,1)S(1)}, u32[]{:S(2)}, u32[]{:S(2)}) collective-permute-start(bf16[400,1024]{1,0:T(8,128)(2,1)S(1)} %get-tuple-element.28.away), channel_id=1, source_target_pairs={{0,16},{1,17},{2,18},{3,19},{4,20},{5,21},{6,22},{7,23},{8,24},{9,... | collective-permute-start | bytes 2457608 | tf_op jit(solution)/shard_map/ppermute | solution.py:98
  7.9 0.7 %shard_map.66 = (bf16[160,1024]{1,0:T(8,128)(2,1)S(1)}, bf16[160,1024]{1,0:T(8,128)(2,1)S(1)}, bf16[144,384]{1,0:T(8,128)(2,1)S(1)}) custom-call(bf16[400,1024]{1,0:T(8,128)(2,1)S(1)} %get-tuple-element.27.own.refs_0_, bf16[400,1024]{1,0:T(8,128)(2,1)S(1)} %get-tuple-element.28.away), custom_call_target="tpu_custom_call" | custom-call | flops 226492416 | bytes 2404352 | tf_op jit(solution)/shard_map/pallas_call | solution.py:120
  8.6 0.0 copy-done
  8.6 1.1 %shard_map.67 = (f32[384,256]{1,0:T(8,128)S(1)}, f32[384,256]{1,0:T(8,128)S(1)}) custom-call(bf16[400,1024]{1,0:T(8,128)(2,1)S(1)} %get-tuple-element.27.own.refs_0_, bf16[400,1024]{1,0:T(8,128)(2,1)S(1)} %get-tuple-element.28.away, bf16[2048,512]{1,0:T(8,128)(2,1)S(1)} %copy-done, bf16[144,384]{1,0:T(8,128)(2,1)S(1)} %get-tuple-element.32._.places), custom_call_target="tpu_custom_call" | custom-call | flops 805306368 | bytes 4632576 | tf_op jit(solution)/shard_map/pallas_call | solution.py:120
  9.7 1.6 %collective-permute-start.5 = (f32[384,256]{1,0:T(8,128)S(1)}, f32[384,256]{1,0:T(8,128)S(1)}, u32[]{:S(2)}, u32[]{:S(2)}) collective-permute-start(f32[384,256]{1,0:T(8,128)S(1)} %get-tuple-element.34), channel_id=1, source_target_pairs={{0,2},{1,3},{2,0},{3,1},{4,6},{5,7},{6,4},{7,5},{8,10},{9,11},{10,... | collective-permute-start | bytes 1179656 | tf_op jit(solution)/shard_map/ppermute | solution.py:98
  11.2 6.3 %collective-permute-done.1.refs_4_ = bf16[1152,256]{1,0:T(8,128)(2,1)S(1)} collective-permute-done((bf16[1152,256]{1,0:T(8,128)(2,1)S(1)}, bf16[1152,256]{1,0:T(8,128)(2,1)S(1)}, u32[]{:S(2)}, u32[]{:S(2)}) %collective-permute-start.1) | collective-permute-done | bytes 589856 | tf_op jit(solution)/shard_map/ppermute | solution.py:98
  17.5 3.7 %collective-permute-start.2 = (bf16[160,1024]{1,0:T(8,128)(2,1)S(1)}, bf16[160,1024]{1,0:T(8,128)(2,1)S(1)}, u32[]{:S(2)}, u32[]{:S(2)}) collective-permute-start(bf16[160,1024]{1,0:T(8,128)(2,1)S(1)} %get-tuple-element.30), channel_id=1, source_target_pairs={{0,4},{1,5},{2,6},{3,7},{12,8},{13,9},{14,10},{15,11},{16,20},{17,... | collective-permute-start | bytes 983048 | tf_op jit(solution)/shard_map/ppermute | solution.py:98
  21.2 0.7 %collective-permute-start.6 = (bf16[1152,256]{1,0:T(8,128)(2,1)S(1)}, bf16[1152,256]{1,0:T(8,128)(2,1)S(1)}, u32[]{:S(2)}, u32[]{:S(2)}) collective-permute-start(bf16[1152,256]{1,0:T(8,128)(2,1)S(1)} %collective-permute-done.1.refs_4_), channel_id=1, source_target_pairs={{0,0},{1,1},{2,2},{3,3},{4,8},{5,9},{6,10},{7,11},{8,4},{9,5},{10,... | collective-permute-start | bytes 1769480 | tf_op jit(solution)/shard_map/ppermute | solution.py:98
  21.9 0.0 collective-permute-done.4.refs_3_
  21.9 1.3 %collective-permute-start.7 = (bf16[1152,256]{1,0:T(8,128)(2,1)S(1)}, bf16[1152,256]{1,0:T(8,128)(2,1)S(1)}, u32[]{:S(2)}, u32[]{:S(2)}) collective-permute-start(bf16[1152,256]{1,0:T(8,128)(2,1)S(1)} %collective-permute-done.4.refs_3_), channel_id=1, source_target_pairs={{4,0},{5,1},{6,2},{7,3},{8,12},{9,13},{10,14},{11,15},{20,16},{21,... | collective-permute-start | bytes 1769480 | tf_op jit(solution)/shard_map/ppermute | solution.py:98
  23.2 0.0 collective-permute-done.5.refs_6_
  23.2 5.6 %collective-permute-start.3 = (bf16[160,1024]{1,0:T(8,128)(2,1)S(1)}, bf16[160,1024]{1,0:T(8,128)(2,1)S(1)}, u32[]{:S(2)}, u32[]{:S(2)}) collective-permute-start(bf16[160,1024]{1,0:T(8,128)(2,1)S(1)} %get-tuple-element.31), channel_id=1, source_target_pairs={{0,20},{1,21},{2,22},{3,23},{12,24},{13,25},{14,26},{15,27},{16,4}... | collective-permute-start | bytes 983048 | tf_op jit(solution)/shard_map/ppermute | solution.py:98
  28.8 0.0 collective-permute-done.refs_1_
  28.8 1.6 %shard_map.68 = (f32[2,384,128]{2,1,0:T(8,128)S(1)}, f32[2,384,256]{2,1,0:T(8,128)S(1)}, bf16[4,384,256]{2,1,0:T(8,128)(2,1)S(1)}, bf16[3,256,128]{2,1,0:T(8,128...) custom-call(bf16[400,1024]{1,0:T(8,128)(2,1)S(1)} %get-tuple-element.27.own.refs_0_, ...), custom_call_target="tpu_custom_call" | custom-call | tf_op jit(solution)/shard_map/pallas_call | solution.py:120
  30.4 0.1 collective-permute-start.13
  30.5 0.0 collective-permute-done.2.hop.refs_2_
  30.5 0.3 shard_map.69.refs_4_
  30.7 3.6 %collective-permute-done.3.refs_3_ = bf16[160,1024]{1,0:T(8,128)(2,1)S(1)} collective-permute-done((bf16[160,1024]{1,0:T(8,128)(2,1)S(1)}, bf16[160,1024]{1,0:T(8,128)(2,1)S(1)}, u32[]{:S(2)}, u32[]{:S(2)}) %collective-permute-start.3) | collective-permute-done | bytes 327712 | tf_op jit(solution)/shard_map/ppermute | solution.py:98
  34.3 0.0 collective-permute-done.6.refs_7_
  34.3 3.4 %collective-permute-done.7.refs_8_ = bf16[1152,256]{1,0:T(8,128)(2,1)S(1)} collective-permute-done((bf16[1152,256]{1,0:T(8,128)(2,1)S(1)}, bf16[1152,256]{1,0:T(8,128)(2,1)S(1)}, u32[]{:S(2)}, u32[]{:S(2)}) %collective-permute-start.7) | collective-permute-done | bytes 589856 | tf_op jit(solution)/shard_map/ppermute | solution.py:98
  37.7 0.7 %shard_map.70 = (f32[16,384]{1,0:T(8,128)S(1)}, f32[16,144]{1,0:T(8,128)S(1)}, f32[16,528]{1,0:T(8,128)S(1)}, bf16[256,128]{1,0:T(8,128)(2,1)S(1)}) custom-call(bf16[400,1024]{1,0:T(8,128)(2,1)S(1)} %get-tuple-element.27.own.refs_0_, bf16[400,1024]{1,0:T(8,128)(2,1)S(1)} %collective-permute-done.refs_1_, ...), custom_call_target="tpu_custom_call" | custom-call | flops 553648128 | bytes 4933632 | tf_op jit(solution)/shard_map/pallas_call | solution.py:120
  38.4 1.6 %collective-permute-start.8 = (f32[16,528]{1,0:T(8,128)S(1)}, f32[16,528]{1,0:T(8,128)S(1)}, u32[]{:S(2)}, u32[]{:S(2)}) collective-permute-start(f32[16,528]{1,0:T(8,128)S(1)} %get-tuple-element.40), channel_id=1, source_target_pairs={{0,16},{1,17},{2,18},{3,19},{4,20},{5,21},{6,22},{7,23},{8,24},{9,... | collective-permute-start | bytes 101384 | tf_op jit(solution)/shard_map/ppermute | solution.py:98
  40.0 1.8 %collective-permute-start.14 = (bf16[256,128]{1,0:T(8,128)(2,1)S(1)}, bf16[256,128]{1,0:T(8,128)(2,1)S(1)}, u32[]{:S(2)}, u32[]{:S(2)}) collective-permute-start(bf16[256,128]{1,0:T(8,128)(2,1)S(1)} %get-tuple-element.48.last_up), channel_id=1, source_target_pairs={{0,4},{1,5},{2,6},{3,7},{4,0},{5,1},{6,2},{7,3},{8,12},{9,13},{10,... | collective-permute-start | bytes 196616 | tf_op jit(solution)/shard_map/ppermute | solution.py:98
  41.7 0.7 %collective-permute-done.8.near = f32[16,528]{1,0:T(8,128)S(1)} collective-permute-done((f32[16,528]{1,0:T(8,128)S(1)}, f32[16,528]{1,0:T(8,128)S(1)}, u32[]{:S(2)}, u32[]{:S(2)}) %collective-permute-start.8) | collective-permute-done | bytes 33824 | tf_op jit(solution)/shard_map/ppermute | solution.py:98
  42.5 2.5 %collective-permute-start.10 = (f32[16,512]{1,0:T(8,128)S(1)}, f32[16,512]{1,0:T(8,128)S(1)}, u32[]{:S(2)}, u32[]{:S(2)}) collective-permute-start(f32[16,512]{1,0:T(8,128)S(1)} %get-tuple-element.42), channel_id=1, source_target_pairs={{0,6},{1,7},{2,4},{3,5},{4,2},{5,3},{6,0},{7,1},{8,14},{9,15},{10,... | collective-permute-start | bytes 98312 | tf_op jit(solution)/shard_map/ppermute | solution.py:98
  44.9 0.5 %collective-permute-start.9 = (f32[16,384]{1,0:T(8,128)S(1)}, f32[16,384]{1,0:T(8,128)S(1)}, u32[]{:S(2)}, u32[]{:S(2)}) collective-permute-start(f32[16,384]{1,0:T(8,128)S(1)} %get-tuple-element.41.low), channel_id=1, source_target_pairs={{0,2},{1,3},{2,0},{3,1},{4,6},{5,7},{6,4},{7,5},{8,10},{9,11},{10,... | collective-permute-start | bytes 73736 | tf_op jit(solution)/shard_map/ppermute | solution.py:98
  45.5 0.5 %collective-permute-start.11 = (f32[16,144]{1,0:T(8,128)S(1)}, f32[16,144]{1,0:T(8,128)S(1)}, u32[]{:S(2)}, u32[]{:S(2)}) collective-permute-start(f32[16,144]{1,0:T(8,128)S(1)} %get-tuple-element.43), channel_id=1, source_target_pairs={{0,4},{1,5},{2,6},{3,7},{4,0},{5,1},{6,2},{7,3},{8,12},{9,13},{10,... | collective-permute-start | bytes 27656 | tf_op jit(solution)/shard_map/ppermute | solution.py:98
  46.0 3.2 %collective-permute-done.11.hop = f32[16,144]{1,0:T(8,128)S(1)} collective-permute-done((f32[16,144]{1,0:T(8,128)S(1)}, f32[16,144]{1,0:T(8,128)S(1)}, u32[]{:S(2)}, u32[]{:S(2)}) %collective-permute-start.11) | collective-permute-done | bytes 9248 | tf_op jit(solution)/shard_map/ppermute | solution.py:98
  49.2 0.0 collective-permute-done.9.far
  49.2 0.0 collective-permute-done.10.hop_far
  49.2 0.2 shard_map.72.near
  49.4 0.0 collective-permute-start.12
  49.4 0.0 collective-permute-done.13.got
  49.4 0.0 collective-permute-done.14.distant
  49.4 1.2 %collective-permute-done.12.far = f32[16,384]{1,0:T(8,128)S(1)} collective-permute-done((f32[16,384]{1,0:T(8,128)S(1)}, f32[16,384]{1,0:T(8,128)S(1)}, u32[]{:S(2)}, u32[]{:S(2)}) %collective-permute-start.12) | collective-permute-done | bytes 24608 | tf_op jit(solution)/shard_map/ppermute | solution.py:98
  50.6 1.2 %shard_map.73 = bf16[384,128]{1,0:T(8,128)(2,1)} custom-call(f32[16,384]{1,0:T(8,128)S(1)} %shard_map.72.near, f32[16,384]{1,0:T(8,128)S(1)} %collective-permute-done.12.far, f32[384,128]{1,0:T(8,128)S(1)} %get-tuple-element.44.keep, f32[384,128]{1,0:T(8,128)S(1)} %collective-permute-done.13.got, bf16[4,384,256]{2,1,0:T(8,128)(2,1)S(1)} %get-tuple-element.46.named_by, ...), custom_call_target="tpu_custom_call" | custom-call | bytes 1654784 | tf_op jit(solution)/shard_map/pallas_call | solution.py:120
  (1 shorter events, 0.0 us)
Async XLA Ops:
  1.1 7.5 %copy-start = (bf16[2048,512]{1,0:T(8,128)(2,1)S(1)}, bf16[2048,512]{1,0:T(8,128)(2,1)}, u32[]{:S(2)}) copy-start(bf16[2048,512]{1,0:T(8,128)(2,1)} %weights.1) | copy-start | bytes 6291460
  1.1 16.4 %collective-permute-start.1 = (bf16[1152,256]{1,0:T(8,128)(2,1)S(1)}, bf16[1152,256]{1,0:T(8,128)(2,1)S(1)}, u32[]{:S(2)}, u32[]{:S(2)}) collective-permute-start(bf16[1152,256]{1,0:T(8,128)(2,1)S(1)} %shard_map.64._.refs_2_), channel_id=1, source_target_pairs={{0,4},{1,5},{2,6},{3,7},{4,0},{5,1},{6,2},{7,3},{8,12},{9,13},{10,... | collective-permute-start | bytes 1769480 | tf_op jit(solution)/shard_map/ppermute | solution.py:98
  4.2 17.7 %collective-permute-start.4 = (bf16[1152,256]{1,0:T(8,128)(2,1)S(1)}, bf16[1152,256]{1,0:T(8,128)(2,1)S(1)}, u32[]{:S(2)}, u32[]{:S(2)}) collective-permute-start(bf16[1152,256]{1,0:T(8,128)(2,1)S(1)} %shard_map.64._.refs_2_), channel_id=1, source_target_pairs={{0,0},{1,1},{2,2},{3,3},{4,8},{5,9},{6,10},{7,11},{8,4},{9,5},{10,... | collective-permute-start | bytes 1769480 | tf_op jit(solution)/shard_map/ppermute | solution.py:98
  6.3 22.4 %collective-permute-start = (bf16[400,1024]{1,0:T(8,128)(2,1)S(1)}, bf16[400,1024]{1,0:T(8,128)(2,1)S(1)}, u32[]{:S(2)}, u32[]{:S(2)}) collective-permute-start(bf16[400,1024]{1,0:T(8,128)(2,1)S(1)} %get-tuple-element.28.away), channel_id=1, source_target_pairs={{0,16},{1,17},{2,18},{3,19},{4,20},{5,21},{6,22},{7,23},{8,24},{9,... | collective-permute-start | bytes 2457608 | tf_op jit(solution)/shard_map/ppermute | solution.py:98
  9.7 13.5 %collective-permute-start.5 = (f32[384,256]{1,0:T(8,128)S(1)}, f32[384,256]{1,0:T(8,128)S(1)}, u32[]{:S(2)}, u32[]{:S(2)}) collective-permute-start(f32[384,256]{1,0:T(8,128)S(1)} %get-tuple-element.34), channel_id=1, source_target_pairs={{0,2},{1,3},{2,0},{3,1},{4,6},{5,7},{6,4},{7,5},{8,10},{9,11},{10,... | collective-permute-start | bytes 1179656 | tf_op jit(solution)/shard_map/ppermute | solution.py:98
  17.5 13.0 %collective-permute-start.2 = (bf16[160,1024]{1,0:T(8,128)(2,1)S(1)}, bf16[160,1024]{1,0:T(8,128)(2,1)S(1)}, u32[]{:S(2)}, u32[]{:S(2)}) collective-permute-start(bf16[160,1024]{1,0:T(8,128)(2,1)S(1)} %get-tuple-element.30), channel_id=1, source_target_pairs={{0,4},{1,5},{2,6},{3,7},{12,8},{13,9},{14,10},{15,11},{16,20},{17,... | collective-permute-start | bytes 983048 | tf_op jit(solution)/shard_map/ppermute | solution.py:98
  21.2 13.1 %collective-permute-start.6 = (bf16[1152,256]{1,0:T(8,128)(2,1)S(1)}, bf16[1152,256]{1,0:T(8,128)(2,1)S(1)}, u32[]{:S(2)}, u32[]{:S(2)}) collective-permute-start(bf16[1152,256]{1,0:T(8,128)(2,1)S(1)} %collective-permute-done.1.refs_4_), channel_id=1, source_target_pairs={{0,0},{1,1},{2,2},{3,3},{4,8},{5,9},{6,10},{7,11},{8,4},{9,5},{10,... | collective-permute-start | bytes 1769480 | tf_op jit(solution)/shard_map/ppermute | solution.py:98
  21.9 15.8 %collective-permute-start.7 = (bf16[1152,256]{1,0:T(8,128)(2,1)S(1)}, bf16[1152,256]{1,0:T(8,128)(2,1)S(1)}, u32[]{:S(2)}, u32[]{:S(2)}) collective-permute-start(bf16[1152,256]{1,0:T(8,128)(2,1)S(1)} %collective-permute-done.4.refs_3_), channel_id=1, source_target_pairs={{4,0},{5,1},{6,2},{7,3},{8,12},{9,13},{10,14},{11,15},{20,16},{21,... | collective-permute-start | bytes 1769480 | tf_op jit(solution)/shard_map/ppermute | solution.py:98
  23.2 11.1 %collective-permute-start.3 = (bf16[160,1024]{1,0:T(8,128)(2,1)S(1)}, bf16[160,1024]{1,0:T(8,128)(2,1)S(1)}, u32[]{:S(2)}, u32[]{:S(2)}) collective-permute-start(bf16[160,1024]{1,0:T(8,128)(2,1)S(1)} %get-tuple-element.31), channel_id=1, source_target_pairs={{0,20},{1,21},{2,22},{3,23},{12,24},{13,25},{14,26},{15,27},{16,4}... | collective-permute-start | bytes 983048 | tf_op jit(solution)/shard_map/ppermute | solution.py:98
  30.4 19.0 %collective-permute-start.13 = (f32[384,128]{1,0:T(8,128)S(1)}, f32[384,128]{1,0:T(8,128)S(1)}, u32[]{:S(2)}, u32[]{:S(2)}) collective-permute-start(f32[384,128]{1,0:T(8,128)S(1)} %get-tuple-element.45), channel_id=1, source_target_pairs={{0,1},{1,0},{2,3},{3,2},{4,5},{5,4},{6,7},{7,6},{8,9},{9,8},{10,11... | collective-permute-start | bytes 589832 | tf_op jit(solution)/shard_map/ppermute | solution.py:98
  38.4 4.1 %collective-permute-start.8 = (f32[16,528]{1,0:T(8,128)S(1)}, f32[16,528]{1,0:T(8,128)S(1)}, u32[]{:S(2)}, u32[]{:S(2)}) collective-permute-start(f32[16,528]{1,0:T(8,128)S(1)} %get-tuple-element.40), channel_id=1, source_target_pairs={{0,16},{1,17},{2,18},{3,19},{4,20},{5,21},{6,22},{7,23},{8,24},{9,... | collective-permute-start | bytes 101384 | tf_op jit(solution)/shard_map/ppermute | solution.py:98
  40.0 9.5 %collective-permute-start.14 = (bf16[256,128]{1,0:T(8,128)(2,1)S(1)}, bf16[256,128]{1,0:T(8,128)(2,1)S(1)}, u32[]{:S(2)}, u32[]{:S(2)}) collective-permute-start(bf16[256,128]{1,0:T(8,128)(2,1)S(1)} %get-tuple-element.48.last_up), channel_id=1, source_target_pairs={{0,4},{1,5},{2,6},{3,7},{4,0},{5,1},{6,2},{7,3},{8,12},{9,13},{10,... | collective-permute-start | bytes 196616 | tf_op jit(solution)/shard_map/ppermute | solution.py:98
  42.5 6.8 %collective-permute-start.10 = (f32[16,512]{1,0:T(8,128)S(1)}, f32[16,512]{1,0:T(8,128)S(1)}, u32[]{:S(2)}, u32[]{:S(2)}) collective-permute-start(f32[16,512]{1,0:T(8,128)S(1)} %get-tuple-element.42), channel_id=1, source_target_pairs={{0,6},{1,7},{2,4},{3,5},{4,2},{5,3},{6,0},{7,1},{8,14},{9,15},{10,... | collective-permute-start | bytes 98312 | tf_op jit(solution)/shard_map/ppermute | solution.py:98
  44.9 4.3 %collective-permute-start.9 = (f32[16,384]{1,0:T(8,128)S(1)}, f32[16,384]{1,0:T(8,128)S(1)}, u32[]{:S(2)}, u32[]{:S(2)}) collective-permute-start(f32[16,384]{1,0:T(8,128)S(1)} %get-tuple-element.41.low), channel_id=1, source_target_pairs={{0,2},{1,3},{2,0},{3,1},{4,6},{5,7},{6,4},{7,5},{8,10},{9,11},{10,... | collective-permute-start | bytes 73736 | tf_op jit(solution)/shard_map/ppermute | solution.py:98
  45.5 3.7 %collective-permute-start.11 = (f32[16,144]{1,0:T(8,128)S(1)}, f32[16,144]{1,0:T(8,128)S(1)}, u32[]{:S(2)}, u32[]{:S(2)}) collective-permute-start(f32[16,144]{1,0:T(8,128)S(1)} %get-tuple-element.43), channel_id=1, source_target_pairs={{0,4},{1,5},{2,6},{3,7},{4,0},{5,1},{6,2},{7,3},{8,12},{9,13},{10,... | collective-permute-start | bytes 27656 | tf_op jit(solution)/shard_map/ppermute | solution.py:98
  49.4 1.2 %collective-permute-start.12 = (f32[16,384]{1,0:T(8,128)S(1)}, f32[16,384]{1,0:T(8,128)S(1)}, u32[]{:S(2)}, u32[]{:S(2)}) collective-permute-start(f32[16,384]{1,0:T(8,128)S(1)} %shard_map.72.near), channel_id=1, source_target_pairs={{0,1},{1,0},{2,3},{3,2},{4,5},{5,4},{6,7},{7,6},{8,9},{9,8},{10,11... | collective-permute-start | bytes 73736 | tf_op jit(solution)/shard_map/ppermute | solution.py:98

commit v25 on v24

--- a/solution.py
+++ b/solution.py
@@ -76,7 +76,7 @@
 
 AXES = ("groups", "adapter", "mp")
 ID_ROWS = 16
-HOP_URGENCY = (30 * 10**8, 0)
+HOP_URGENCY = (42 * 10**8, 0)
 OWNERS = 4
 LANES = 128
 NT = (((1,), (1,)), ((), ()))

time: 52.1 us -> 51.4 us (0.987)
  starting transfers between devices: 25.1 us -> 22.6 us
  waiting for transfers between devices: 18.3 us -> 20.1 us
    ppermute x15, starting transfers between devices: 25.1 us -> 22.6 us  [exchange(): return lax.ppermute(x, AXES, pairs)]
    ppermute x15, waiting for transfers between devices: 18.3 us -> 20.1 us  [exchange(): return lax.ppermute(x, AXES, pairs)]
  transfers between devices with their start and end apart: 15 -> 15, of which waited for: 6 -> 6; matrix products, arithmetic and copies ran while one was open for 0% -> 0% of each run, Pallas kernels for 11% -> 12%
where the time goes in v25:
time: 51.4 us; the launch traced here: 51.2 us
  starting transfers between devices  22.6 us (44%)
  waiting for transfers between devices  20.1 us (39%)
  Pallas kernels  8.22 us (16%)
    ppermute x15, starting transfers between devices, exchange(): return lax.ppermute(x, AXES, pairs)  22.6 us
    ppermute x15, waiting for transfers between devices, exchange(): return lax.ppermute(x, AXES, pairs)  20.1 us
    pallas_call x10, Pallas kernels, kernel(): pl.pallas_call(body, out_shape=outs, in_specs=specs or [inner] * len(oper...  8.22 us
  transfers between devices with their start and end apart: 15, of which 6 were waited for; matrix products, arithmetic and copies ran while one was open for 0% of the time, Pallas kernels for 12%

profile of v25, /device:TPU:0, one launch (start us, length us, event | category | flops | bytes accessed | tf_op | source)
XLA Modules:
  0.0 51.2 jit_solution(4167528898449340320)
XLA Ops:
  0.0 1.1 %shard_map.64._.refs_2_ = bf16[1152,256]{1,0:T(8,128)(2,1)S(1)} custom-call(bf16[2048,256]{1,0:T(8,128)(2,1)} %down.1, bf16[256,128]{1,0:T(8,128)(2,1)} %up.1), custom_call_target="tpu_custom_call" | custom-call | bytes 1703936 | tf_op jit(solution)/shard_map/pallas_call | solution.py:120
  1.1 0.0 copy-start
  1.1 3.1 %collective-permute-start.1 = (bf16[1152,256]{1,0:T(8,128)(2,1)S(1)}, bf16[1152,256]{1,0:T(8,128)(2,1)S(1)}, u32[]{:S(2)}, u32[]{:S(2)}) collective-permute-start(bf16[1152,256]{1,0:T(8,128)(2,1)S(1)} %shard_map.64._.refs_2_), channel_id=1, source_target_pairs={{0,4},{1,5},{2,6},{3,7},{4,0},{5,1},{6,2},{7,3},{8,12},{9,13},{10,... | collective-permute-start | bytes 1769480 | tf_op jit(solution)/shard_map/ppermute | solution.py:98
  4.2 1.4 %shard_map.65 = (bf16[400,1024]{1,0:T(8,128)(2,1)S(1)}, bf16[400,1024]{1,0:T(8,128)(2,1)S(1)}) custom-call(bf16[384,2048]{1,0:T(8,128)(2,1)} %tokens.1, s32[1,384]{1,0:T(1,128)} %bitcast.1, s32[384]{0:T(512)} %slot_in.1, bf16[1152,256]{1,0:T(8,128)(2,1)S(1)} %shard_map.64._.refs_2_), custom_call_target="tpu_custom_call" | custom-call | bytes 3804160 | tf_op jit(solution)/shard_map/pallas_call | solution.py:120
  5.6 1.6 %collective-permute-start = (bf16[400,1024]{1,0:T(8,128)(2,1)S(1)}, bf16[400,1024]{1,0:T(8,128)(2,1)S(1)}, u32[]{:S(2)}, u32[]{:S(2)}) collective-permute-start(bf16[400,1024]{1,0:T(8,128)(2,1)S(1)} %get-tuple-element.28.away), channel_id=1, source_target_pairs={{0,16},{1,17},{2,18},{3,19},{4,20},{5,21},{6,22},{7,23},{8,24},{9,... | collective-permute-start | bytes 2457608 | tf_op jit(solution)/shard_map/ppermute | solution.py:98
  7.2 0.7 %collective-permute-start.4 = (bf16[1152,256]{1,0:T(8,128)(2,1)S(1)}, bf16[1152,256]{1,0:T(8,128)(2,1)S(1)}, u32[]{:S(2)}, u32[]{:S(2)}) collective-permute-start(bf16[1152,256]{1,0:T(8,128)(2,1)S(1)} %shard_map.64._.refs_2_), channel_id=1, source_target_pairs={{0,0},{1,1},{2,2},{3,3},{4,8},{5,9},{6,10},{7,11},{8,4},{9,5},{10,... | collective-permute-start | bytes 1769480 | tf_op jit(solution)/shard_map/ppermute | solution.py:98
  7.9 0.7 %shard_map.66 = (bf16[160,1024]{1,0:T(8,128)(2,1)S(1)}, bf16[160,1024]{1,0:T(8,128)(2,1)S(1)}, bf16[144,384]{1,0:T(8,128)(2,1)S(1)}) custom-call(bf16[400,1024]{1,0:T(8,128)(2,1)S(1)} %get-tuple-element.27.own.refs_0_, bf16[400,1024]{1,0:T(8,128)(2,1)S(1)} %get-tuple-element.28.away), custom_call_target="tpu_custom_call" | custom-call | flops 226492416 | bytes 2404352 | tf_op jit(solution)/shard_map/pallas_call | solution.py:120
  8.6 0.0 copy-done
  8.6 1.1 %shard_map.67 = (f32[384,256]{1,0:T(8,128)S(1)}, f32[384,256]{1,0:T(8,128)S(1)}) custom-call(bf16[400,1024]{1,0:T(8,128)(2,1)S(1)} %get-tuple-element.27.own.refs_0_, bf16[400,1024]{1,0:T(8,128)(2,1)S(1)} %get-tuple-element.28.away, bf16[2048,512]{1,0:T(8,128)(2,1)S(1)} %copy-done, bf16[144,384]{1,0:T(8,128)(2,1)S(1)} %get-tuple-element.32._.places), custom_call_target="tpu_custom_call" | custom-call | flops 805306368 | bytes 4632576 | tf_op jit(solution)/shard_map/pallas_call | solution.py:120
  9.7 1.6 %collective-permute-start.5 = (f32[384,256]{1,0:T(8,128)S(1)}, f32[384,256]{1,0:T(8,128)S(1)}, u32[]{:S(2)}, u32[]{:S(2)}) collective-permute-start(f32[384,256]{1,0:T(8,128)S(1)} %get-tuple-element.34), channel_id=1, source_target_pairs={{0,2},{1,3},{2,0},{3,1},{4,6},{5,7},{6,4},{7,5},{8,10},{9,11},{10,... | collective-permute-start | bytes 1179656 | tf_op jit(solution)/shard_map/ppermute | solution.py:98
  11.2 6.3 %collective-permute-done.1.refs_4_ = bf16[1152,256]{1,0:T(8,128)(2,1)S(1)} collective-permute-done((bf16[1152,256]{1,0:T(8,128)(2,1)S(1)}, bf16[1152,256]{1,0:T(8,128)(2,1)S(1)}, u32[]{:S(2)}, u32[]{:S(2)}) %collective-permute-start.1) | collective-permute-done | bytes 589856 | tf_op jit(solution)/shard_map/ppermute | solution.py:98
  17.5 3.7 %collective-permute-start.2 = (bf16[160,1024]{1,0:T(8,128)(2,1)S(1)}, bf16[160,1024]{1,0:T(8,128)(2,1)S(1)}, u32[]{:S(2)}, u32[]{:S(2)}) collective-permute-start(bf16[160,1024]{1,0:T(8,128)(2,1)S(1)} %get-tuple-element.30), channel_id=1, source_target_pairs={{0,4},{1,5},{2,6},{3,7},{12,8},{13,9},{14,10},{15,11},{16,20},{17,... | collective-permute-start | bytes 983048 | tf_op jit(solution)/shard_map/ppermute | solution.py:98
  21.2 0.7 %collective-permute-start.6 = (bf16[1152,256]{1,0:T(8,128)(2,1)S(1)}, bf16[1152,256]{1,0:T(8,128)(2,1)S(1)}, u32[]{:S(2)}, u32[]{:S(2)}) collective-permute-start(bf16[1152,256]{1,0:T(8,128)(2,1)S(1)} %collective-permute-done.1.refs_4_), channel_id=1, source_target_pairs={{0,0},{1,1},{2,2},{3,3},{4,8},{5,9},{6,10},{7,11},{8,4},{9,5},{10,... | collective-permute-start | bytes 1769480 | tf_op jit(solution)/shard_map/ppermute | solution.py:98
  21.9 0.0 collective-permute-done.4.refs_3_
  21.9 1.3 %collective-permute-start.7 = (bf16[1152,256]{1,0:T(8,128)(2,1)S(1)}, bf16[1152,256]{1,0:T(8,128)(2,1)S(1)}, u32[]{:S(2)}, u32[]{:S(2)}) collective-permute-start(bf16[1152,256]{1,0:T(8,128)(2,1)S(1)} %collective-permute-done.4.refs_3_), channel_id=1, source_target_pairs={{4,0},{5,1},{6,2},{7,3},{8,12},{9,13},{10,14},{11,15},{20,16},{21,... | collective-permute-start | bytes 1769480 | tf_op jit(solution)/shard_map/ppermute | solution.py:98
  23.2 0.0 collective-permute-done.5.refs_6_
  23.2 5.6 %collective-permute-start.3 = (bf16[160,1024]{1,0:T(8,128)(2,1)S(1)}, bf16[160,1024]{1,0:T(8,128)(2,1)S(1)}, u32[]{:S(2)}, u32[]{:S(2)}) collective-permute-start(bf16[160,1024]{1,0:T(8,128)(2,1)S(1)} %get-tuple-element.31), channel_id=1, source_target_pairs={{0,20},{1,21},{2,22},{3,23},{12,24},{13,25},{14,26},{15,27},{16,4}... | collective-permute-start | bytes 983048 | tf_op jit(solution)/shard_map/ppermute | solution.py:98
  28.8 0.0 collective-permute-done.refs_1_
  28.8 1.6 %shard_map.68 = (f32[2,384,128]{2,1,0:T(8,128)S(1)}, f32[2,384,256]{2,1,0:T(8,128)S(1)}, bf16[4,384,256]{2,1,0:T(8,128)(2,1)S(1)}, bf16[3,256,128]{2,1,0:T(8,128...) custom-call(bf16[400,1024]{1,0:T(8,128)(2,1)S(1)} %get-tuple-element.27.own.refs_0_, ...), custom_call_target="tpu_custom_call" | custom-call | tf_op jit(solution)/shard_map/pallas_call | solution.py:120
  30.4 0.1 collective-permute-start.13
  30.5 0.0 collective-permute-done.2.hop.refs_2_
  30.5 0.3 shard_map.69.refs_4_
  30.7 3.5 %collective-permute-done.3.refs_3_ = bf16[160,1024]{1,0:T(8,128)(2,1)S(1)} collective-permute-done((bf16[160,1024]{1,0:T(8,128)(2,1)S(1)}, bf16[160,1024]{1,0:T(8,128)(2,1)S(1)}, u32[]{:S(2)}, u32[]{:S(2)}) %collective-permute-start.3) | collective-permute-done | bytes 327712 | tf_op jit(solution)/shard_map/ppermute | solution.py:98
  34.3 0.0 collective-permute-done.6.refs_7_
  34.3 4.2 %collective-permute-done.7.refs_8_ = bf16[1152,256]{1,0:T(8,128)(2,1)S(1)} collective-permute-done((bf16[1152,256]{1,0:T(8,128)(2,1)S(1)}, bf16[1152,256]{1,0:T(8,128)(2,1)S(1)}, u32[]{:S(2)}, u32[]{:S(2)}) %collective-permute-start.7) | collective-permute-done | bytes 589856 | tf_op jit(solution)/shard_map/ppermute | solution.py:98
  38.4 0.7 %shard_map.70 = (f32[16,384]{1,0:T(8,128)S(1)}, f32[16,144]{1,0:T(8,128)S(1)}, f32[16,528]{1,0:T(8,128)S(1)}, bf16[256,128]{1,0:T(8,128)(2,1)S(1)}) custom-call(bf16[400,1024]{1,0:T(8,128)(2,1)S(1)} %get-tuple-element.27.own.refs_0_, bf16[400,1024]{1,0:T(8,128)(2,1)S(1)} %collective-permute-done.refs_1_, ...), custom_call_target="tpu_custom_call" | custom-call | flops 553648128 | bytes 4933632 | tf_op jit(solution)/shard_map/pallas_call | solution.py:120
  39.1 0.9 %collective-permute-start.8 = (f32[16,528]{1,0:T(8,128)S(1)}, f32[16,528]{1,0:T(8,128)S(1)}, u32[]{:S(2)}, u32[]{:S(2)}) collective-permute-start(f32[16,528]{1,0:T(8,128)S(1)} %get-tuple-element.40), channel_id=1, source_target_pairs={{0,16},{1,17},{2,18},{3,19},{4,20},{5,21},{6,22},{7,23},{8,24},{9,... | collective-permute-start | bytes 101384 | tf_op jit(solution)/shard_map/ppermute | solution.py:98
  40.0 0.0 collective-permute-start.14
  40.0 3.2 %collective-permute-done.8.near = f32[16,528]{1,0:T(8,128)S(1)} collective-permute-done((f32[16,528]{1,0:T(8,128)S(1)}, f32[16,528]{1,0:T(8,128)S(1)}, u32[]{:S(2)}, u32[]{:S(2)}) %collective-permute-start.8) | collective-permute-done | bytes 33824 | tf_op jit(solution)/shard_map/ppermute | solution.py:98
  43.2 0.8 %collective-permute-start.10 = (f32[16,512]{1,0:T(8,128)S(1)}, f32[16,512]{1,0:T(8,128)S(1)}, u32[]{:S(2)}, u32[]{:S(2)}) collective-permute-start(f32[16,512]{1,0:T(8,128)S(1)} %get-tuple-element.42), channel_id=1, source_target_pairs={{0,6},{1,7},{2,4},{3,5},{4,2},{5,3},{6,0},{7,1},{8,14},{9,15},{10,... | collective-permute-start | bytes 98312 | tf_op jit(solution)/shard_map/ppermute | solution.py:98
  44.0 0.9 %collective-permute-start.9 = (f32[16,384]{1,0:T(8,128)S(1)}, f32[16,384]{1,0:T(8,128)S(1)}, u32[]{:S(2)}, u32[]{:S(2)}) collective-permute-start(f32[16,384]{1,0:T(8,128)S(1)} %get-tuple-element.41.low), channel_id=1, source_target_pairs={{0,2},{1,3},{2,0},{3,1},{4,6},{5,7},{6,4},{7,5},{8,10},{9,11},{10,... | collective-permute-start | bytes 73736 | tf_op jit(solution)/shard_map/ppermute | solution.py:98
  44.8 1.9 %collective-permute-start.11 = (f32[16,144]{1,0:T(8,128)S(1)}, f32[16,144]{1,0:T(8,128)S(1)}, u32[]{:S(2)}, u32[]{:S(2)}) collective-permute-start(f32[16,144]{1,0:T(8,128)S(1)} %get-tuple-element.43), channel_id=1, source_target_pairs={{0,4},{1,5},{2,6},{3,7},{4,0},{5,1},{6,2},{7,3},{8,12},{9,13},{10,... | collective-permute-start | bytes 27656 | tf_op jit(solution)/shard_map/ppermute | solution.py:98
  46.7 1.8 %collective-permute-done.11.hop = f32[16,144]{1,0:T(8,128)S(1)} collective-permute-done((f32[16,144]{1,0:T(8,128)S(1)}, f32[16,144]{1,0:T(8,128)S(1)}, u32[]{:S(2)}, u32[]{:S(2)}) %collective-permute-start.11) | collective-permute-done | bytes 9248 | tf_op jit(solution)/shard_map/ppermute | solution.py:98
  48.5 0.0 collective-permute-done.9.far
  48.6 0.0 collective-permute-done.10.hop_far
  48.6 0.2 shard_map.72.near
  48.7 0.0 collective-permute-start.12
  48.7 0.0 collective-permute-done.13.got
  48.8 0.0 collective-permute-done.14.distant
  48.8 1.2 %collective-permute-done.12.far = f32[16,384]{1,0:T(8,128)S(1)} collective-permute-done((f32[16,384]{1,0:T(8,128)S(1)}, f32[16,384]{1,0:T(8,128)S(1)}, u32[]{:S(2)}, u32[]{:S(2)}) %collective-permute-start.12) | collective-permute-done | bytes 24608 | tf_op jit(solution)/shard_map/ppermute | solution.py:98
  49.9 1.2 %shard_map.73 = bf16[384,128]{1,0:T(8,128)(2,1)} custom-call(f32[16,384]{1,0:T(8,128)S(1)} %shard_map.72.near, f32[16,384]{1,0:T(8,128)S(1)} %collective-permute-done.12.far, f32[384,128]{1,0:T(8,128)S(1)} %get-tuple-element.44.keep, f32[384,128]{1,0:T(8,128)S(1)} %collective-permute-done.13.got, bf16[4,384,256]{2,1,0:T(8,128)(2,1)S(1)} %get-tuple-element.46.named_by, ...), custom_call_target="tpu_custom_call" | custom-call | bytes 1654784 | tf_op jit(solution)/shard_map/pallas_call | solution.py:120
  (1 shorter events, 0.0 us)
Async XLA Ops:
  1.1 7.5 %copy-start = (bf16[2048,512]{1,0:T(8,128)(2,1)S(1)}, bf16[2048,512]{1,0:T(8,128)(2,1)}, u32[]{:S(2)}) copy-start(bf16[2048,512]{1,0:T(8,128)(2,1)} %weights.1) | copy-start | bytes 6291460
  1.1 16.4 %collective-permute-start.1 = (bf16[1152,256]{1,0:T(8,128)(2,1)S(1)}, bf16[1152,256]{1,0:T(8,128)(2,1)S(1)}, u32[]{:S(2)}, u32[]{:S(2)}) collective-permute-start(bf16[1152,256]{1,0:T(8,128)(2,1)S(1)} %shard_map.64._.refs_2_), channel_id=1, source_target_pairs={{0,4},{1,5},{2,6},{3,7},{4,0},{5,1},{6,2},{7,3},{8,12},{9,13},{10,... | collective-permute-start | bytes 1769480 | tf_op jit(solution)/shard_map/ppermute | solution.py:98
  5.6 23.1 %collective-permute-start = (bf16[400,1024]{1,0:T(8,128)(2,1)S(1)}, bf16[400,1024]{1,0:T(8,128)(2,1)S(1)}, u32[]{:S(2)}, u32[]{:S(2)}) collective-permute-start(bf16[400,1024]{1,0:T(8,128)(2,1)S(1)} %get-tuple-element.28.away), channel_id=1, source_target_pairs={{0,16},{1,17},{2,18},{3,19},{4,20},{5,21},{6,22},{7,23},{8,24},{9,... | collective-permute-start | bytes 2457608 | tf_op jit(solution)/shard_map/ppermute | solution.py:98
  7.2 14.7 %collective-permute-start.4 = (bf16[1152,256]{1,0:T(8,128)(2,1)S(1)}, bf16[1152,256]{1,0:T(8,128)(2,1)S(1)}, u32[]{:S(2)}, u32[]{:S(2)}) collective-permute-start(bf16[1152,256]{1,0:T(8,128)(2,1)S(1)} %shard_map.64._.refs_2_), channel_id=1, source_target_pairs={{0,0},{1,1},{2,2},{3,3},{4,8},{5,9},{6,10},{7,11},{8,4},{9,5},{10,... | collective-permute-start | bytes 1769480 | tf_op jit(solution)/shard_map/ppermute | solution.py:98
  9.7 13.5 %collective-permute-start.5 = (f32[384,256]{1,0:T(8,128)S(1)}, f32[384,256]{1,0:T(8,128)S(1)}, u32[]{:S(2)}, u32[]{:S(2)}) collective-permute-start(f32[384,256]{1,0:T(8,128)S(1)} %get-tuple-element.34), channel_id=1, source_target_pairs={{0,2},{1,3},{2,0},{3,1},{4,6},{5,7},{6,4},{7,5},{8,10},{9,11},{10,... | collective-permute-start | bytes 1179656 | tf_op jit(solution)/shard_map/ppermute | solution.py:98
  17.5 13.0 %collective-permute-start.2 = (bf16[160,1024]{1,0:T(8,128)(2,1)S(1)}, bf16[160,1024]{1,0:T(8,128)(2,1)S(1)}, u32[]{:S(2)}, u32[]{:S(2)}) collective-permute-start(bf16[160,1024]{1,0:T(8,128)(2,1)S(1)} %get-tuple-element.30), channel_id=1, source_target_pairs={{0,4},{1,5},{2,6},{3,7},{12,8},{13,9},{14,10},{15,11},{16,20},{17,... | collective-permute-start | bytes 983048 | tf_op jit(solution)/shard_map/ppermute | solution.py:98
  21.2 13.1 %collective-permute-start.6 = (bf16[1152,256]{1,0:T(8,128)(2,1)S(1)}, bf16[1152,256]{1,0:T(8,128)(2,1)S(1)}, u32[]{:S(2)}, u32[]{:S(2)}) collective-permute-start(bf16[1152,256]{1,0:T(8,128)(2,1)S(1)} %collective-permute-done.1.refs_4_), channel_id=1, source_target_pairs={{0,0},{1,1},{2,2},{3,3},{4,8},{5,9},{6,10},{7,11},{8,4},{9,5},{10,... | collective-permute-start | bytes 1769480 | tf_op jit(solution)/shard_map/ppermute | solution.py:98
  21.9 16.5 %collective-permute-start.7 = (bf16[1152,256]{1,0:T(8,128)(2,1)S(1)}, bf16[1152,256]{1,0:T(8,128)(2,1)S(1)}, u32[]{:S(2)}, u32[]{:S(2)}) collective-permute-start(bf16[1152,256]{1,0:T(8,128)(2,1)S(1)} %collective-permute-done.4.refs_3_), channel_id=1, source_target_pairs={{4,0},{5,1},{6,2},{7,3},{8,12},{9,13},{10,14},{11,15},{20,16},{21,... | collective-permute-start | bytes 1769480 | tf_op jit(solution)/shard_map/ppermute | solution.py:98
  23.2 11.1 %collective-permute-start.3 = (bf16[160,1024]{1,0:T(8,128)(2,1)S(1)}, bf16[160,1024]{1,0:T(8,128)(2,1)S(1)}, u32[]{:S(2)}, u32[]{:S(2)}) collective-permute-start(bf16[160,1024]{1,0:T(8,128)(2,1)S(1)} %get-tuple-element.31), channel_id=1, source_target_pairs={{0,20},{1,21},{2,22},{3,23},{12,24},{13,25},{14,26},{15,27},{16,4}... | collective-permute-start | bytes 983048 | tf_op jit(solution)/shard_map/ppermute | solution.py:98
  30.4 18.4 %collective-permute-start.13 = (f32[384,128]{1,0:T(8,128)S(1)}, f32[384,128]{1,0:T(8,128)S(1)}, u32[]{:S(2)}, u32[]{:S(2)}) collective-permute-start(f32[384,128]{1,0:T(8,128)S(1)} %get-tuple-element.45), channel_id=1, source_target_pairs={{0,1},{1,0},{2,3},{3,2},{4,5},{5,4},{6,7},{7,6},{8,9},{9,8},{10,11... | collective-permute-start | bytes 589832 | tf_op jit(solution)/shard_map/ppermute | solution.py:98
  39.1 4.1 %collective-permute-start.8 = (f32[16,528]{1,0:T(8,128)S(1)}, f32[16,528]{1,0:T(8,128)S(1)}, u32[]{:S(2)}, u32[]{:S(2)}) collective-permute-start(f32[16,528]{1,0:T(8,128)S(1)} %get-tuple-element.40), channel_id=1, source_target_pairs={{0,16},{1,17},{2,18},{3,19},{4,20},{5,21},{6,22},{7,23},{8,24},{9,... | collective-permute-start | bytes 101384 | tf_op jit(solution)/shard_map/ppermute | solution.py:98
  40.0 8.8 %collective-permute-start.14 = (bf16[256,128]{1,0:T(8,128)(2,1)S(1)}, bf16[256,128]{1,0:T(8,128)(2,1)S(1)}, u32[]{:S(2)}, u32[]{:S(2)}) collective-permute-start(bf16[256,128]{1,0:T(8,128)(2,1)S(1)} %get-tuple-element.48.last_up), channel_id=1, source_target_pairs={{0,4},{1,5},{2,6},{3,7},{4,0},{5,1},{6,2},{7,3},{8,12},{9,13},{10,... | collective-permute-start | bytes 196616 | tf_op jit(solution)/shard_map/ppermute | solution.py:98
  43.2 5.4 %collective-permute-start.10 = (f32[16,512]{1,0:T(8,128)S(1)}, f32[16,512]{1,0:T(8,128)S(1)}, u32[]{:S(2)}, u32[]{:S(2)}) collective-permute-start(f32[16,512]{1,0:T(8,128)S(1)} %get-tuple-element.42), channel_id=1, source_target_pairs={{0,6},{1,7},{2,4},{3,5},{4,2},{5,3},{6,0},{7,1},{8,14},{9,15},{10,... | collective-permute-start | bytes 98312 | tf_op jit(solution)/shard_map/ppermute | solution.py:98
  44.0 4.6 %collective-permute-start.9 = (f32[16,384]{1,0:T(8,128)S(1)}, f32[16,384]{1,0:T(8,128)S(1)}, u32[]{:S(2)}, u32[]{:S(2)}) collective-permute-start(f32[16,384]{1,0:T(8,128)S(1)} %get-tuple-element.41.low), channel_id=1, source_target_pairs={{0,2},{1,3},{2,0},{3,1},{4,6},{5,7},{6,4},{7,5},{8,10},{9,11},{10,... | collective-permute-start | bytes 73736 | tf_op jit(solution)/shard_map/ppermute | solution.py:98
  44.8 3.7 %collective-permute-start.11 = (f32[16,144]{1,0:T(8,128)S(1)}, f32[16,144]{1,0:T(8,128)S(1)}, u32[]{:S(2)}, u32[]{:S(2)}) collective-permute-start(f32[16,144]{1,0:T(8,128)S(1)} %get-tuple-element.43), channel_id=1, source_target_pairs={{0,4},{1,5},{2,6},{3,7},{4,0},{5,1},{6,2},{7,3},{8,12},{9,13},{10,... | collective-permute-start | bytes 27656 | tf_op jit(solution)/shard_map/ppermute | solution.py:98
  48.7 1.2 %collective-permute-start.12 = (f32[16,384]{1,0:T(8,128)S(1)}, f32[16,384]{1,0:T(8,128)S(1)}, u32[]{:S(2)}, u32[]{:S(2)}) collective-permute-start(f32[16,384]{1,0:T(8,128)S(1)} %shard_map.72.near), channel_id=1, source_target_pairs={{0,1},{1,0},{2,3},{3,2},{4,5},{5,4},{6,7},{7,6},{8,9},{9,8},{10,11... | collective-permute-start | bytes 73736 | tf_op jit(solution)/shard_map/ppermute | solution.py:98
